TPU v7x, 32 devices: a whole 2x2x4 slice. The times are simulated.
32 devices in a mesh: groups: 2 (over y), tensor: 4 (over z), dp: 4 (over x, core).
Axes of the slice: x: 2, y: 2, z: 4, core: 2. Of those that a mesh axis runs over, the one named last changes fastest.
Arguments:
- attention_result: bfloat16 [4096, 8192], P(('groups', 'dp'), 'tensor'), parts along dimension 0, may hold values from -6 to 6
- output_weight: bfloat16 [8192, 8192], P(None, 'tensor'), may hold values from -0.0625 to 0.0625
- adapter_down_weight: bfloat16 [16, 128, 8192], P('dp', 'tensor'), may hold values from -0.0625 to 0.0625
- adapter_up_weight: bfloat16 [16, 128, 8192], P('dp', None, 'tensor'), may hold values from -0.5 to 0.5
- adapter_page_row: int32 [32], P('groups'), parts along dimension 0, may hold values from 0 to 15, as said below
- requests: int32 [8, 6], P(('groups', 'dp')), parts along dimension 0, may hold values from 0 to 15, as said below
- row_request_entry: int32 [4096], P(('groups', 'dp')), parts along dimension 0, may hold values from 0 to 5
- ranks: int32 [16], replicated, may hold values from 16 to 128, as said below
Outputs:
- projected: bfloat16 [4096, 8192], P(('groups', 'dp'), 'tensor'), parts along dimension 0
There are 2 independent parts, one for each index of `groups`. A program takes and returns all parts, laid end to end along the dimension named above; an argument that names none is the same for every part. Nothing has to cross between parts.
Inputs may be any that keep to these rules, and one draw needn't show every extreme that they name: `adapter_page_row`: A permutation of the page rows. `requests`: each list holds 6 different adapters; among them at most 2 have their page with one holder, the holder of adapter a being adapter_page_row[a] // 4, and every list reaches 2 with some holder. `ranks`: some adapter has rank 128.
All inputs are finite; a program needn't handle non-finite values.
Results may differ from a plain program's by a relative error of at most 0.0037.
Values may be sent and summed in bfloat16 or wider, within the bound.
No kernel may reach another device: no remote copies, remote signals or barrier semaphores. Data moves between devices by JAX's collectives and lax.ppermute only.
A program may use at most 192 MiB of HBM per device.

v0:
```python
import jax
import jax.numpy as jnp
from jax import lax
from jax.sharding import PartitionSpec as P

CAP = 2


def slot_of(request_rows, adapter_page_row, holder_length):
    holders = adapter_page_row[request_rows] // holder_length
    req_len = request_rows.shape[-1]
    same_home = holders[..., :, None] == holders[..., None, :]
    earlier = jnp.arange(req_len)[:, None] > jnp.arange(req_len)[None, :]
    position = jnp.sum((same_home & earlier).astype(jnp.int32), axis=-1)
    return (holders * CAP + position, holders, position)


def local(
    attention_result,
    output_weight,
    adapter_down_weight,
    adapter_up_weight,
    adapter_page_row,
    requests,
    row_request_entry,
    ranks,
):
    row_count = attention_result.shape[0]
    n_dp = lax.axis_size("dp")
    holder_length = adapter_down_weight.shape[0]
    rank_per_holder = adapter_down_weight.shape[1]
    feature_length = adapter_down_weight.shape[2]
    rank_complete = adapter_up_weight.shape[1]
    output_columns = adapter_up_weight.shape[2]
    slot_count = n_dp * CAP
    own_list = requests[0]
    own_slots, _, _ = slot_of(own_list, adapter_page_row, holder_length)
    slot_hit = own_slots[None, :] == jnp.arange(slot_count)[:, None]
    needed = jnp.sum(jnp.where(slot_hit, adapter_page_row[own_list][None, :], 0), axis=1)
    needed = jnp.where(jnp.any(slot_hit, axis=1), needed, -1)
    fragment = (
        lax.all_gather(adapter_down_weight, "dp", axis=0, tiled=True),
        lax.all_gather(adapter_up_weight, "dp", axis=0, tiled=True),
    )
    piece_len = fragment[0].shape[0]
    picker = (needed[:, None] == jnp.arange(piece_len)[None, :]).astype(jnp.bfloat16)
    new_down = jnp.einsum("sp,pkd->skd", picker, fragment[0], preferred_element_type=jnp.float32)
    new_up = jnp.einsum("sp,pkd->skd", picker, fragment[1], preferred_element_type=jnp.float32)
    down_slots = new_down.astype(jnp.bfloat16)
    up_slots = new_up.astype(jnp.bfloat16)
    row_slots = own_slots[row_request_entry]
    one_hot = row_slots[:, None] == jnp.arange(slot_count)[None, :]
    row_rank = ranks[own_list][row_request_entry]
    flat_down = down_slots.reshape(slot_count * rank_per_holder, feature_length)
    fragment = lax.all_gather(attention_result, "tensor", axis=1, tiled=True)
    base_add = jnp.dot(fragment, output_weight, preferred_element_type=jnp.float32)
    low_add = lax.dot_general(
        fragment, flat_down, (((1,), (1,)), ((), ())), preferred_element_type=jnp.float32
    )
    low_mine = jnp.sum(
        low_add.reshape(row_count, slot_count, rank_per_holder)
        * one_hot[:, :, None].astype(jnp.float32),
        axis=1,
    ).astype(jnp.bfloat16)
    low_full = lax.all_gather(low_mine, "tensor", axis=1, tiled=True)
    live_mask = jnp.arange(rank_complete)[None, :] < row_rank[:, None]
    masked = jnp.where(live_mask, low_full, jnp.zeros_like(low_full))
    spread = (one_hot[:, :, None].astype(jnp.bfloat16) * masked[:, None, :]).reshape(
        row_count, slot_count * rank_complete
    )
    low_term = jnp.dot(
        spread,
        up_slots.reshape(slot_count * rank_complete, output_columns),
        preferred_element_type=jnp.float32,
    )
    return (base_add + low_term).astype(jnp.bfloat16)


def solution(mesh):
    in_specs = (
        P(("groups", "dp"), "tensor"),
        P(None, "tensor"),
        P("dp", "tensor", None),
        P("dp", None, "tensor"),
        P("groups"),
        P(("groups", "dp"), None),
        P(("groups", "dp")),
        P(),
    )
    out_specs = P(("groups", "dp"), "tensor")
    return jax.shard_map(local, mesh=mesh, in_specs=in_specs, out_specs=out_specs, check_vma=False)
```

profile of v0, /device:TPU:0, one launch (start us, length us, event | category | flops | bytes accessed | tf_op | source)
XLA Modules:
  0.0 326.3 jit_solution(15545446799693851461)
XLA Ops:
  6.5 0.0 copy-start
  6.5 0.0 all-gather.6.cloned.1.call-start
  6.5 0.7 all-gather.6.cloned.1.call-update
  7.3 0.0 all-gather.4.cloned.1.call-start
  7.3 0.7 all-gather.4.cloned.1.call-update
  8.0 0.0 all-gather.8.cloned.1.call-start
  8.1 0.7 all-gather.8.cloned.1.call-update
  8.7 0.7 fusion.22
  9.4 0.0 copy-done
  9.4 0.6 gather_fusion
  10.1 1.3 gather_fusion.1
  11.4 0.2 convert_reduce_fusion
  11.6 0.1 fusion.15
  11.7 0.1 select_reduce_fusion
  11.8 0.7 fusion.23
  12.5 0.7 fusion.24
  13.2 4.3 %select_select_fusion = (s32[512]{0:T(512)S(1)}, pred[512]{0:T(512)(128)(4,1)S(1)}, pred[512]{0:T(512)(128)(4,1)S(1)}, pred[512]{0:T(512)(128)(4,1)S(1)}, pred[5...) fusion(s32[]{:T(128)} %bitcast.8, s32[]{:T(128)} %bitcast.9, s32[]{:T(128)} %bitcast.10, s32[]{:T(128)} %bitcast.11, ...), kind=kLoop, calls=%fused_computation.31 | loop fusion | flops 6656 | bytes 6680 | tf_op jit(solution)/shard_map/gather | solution.py:53
  17.4 3.9 %select_select_fusion.1 = s32[512]{0:T(512)S(1)} fusion(pred[512]{0:T(512)(128)(4,1)S(1)} %get-tuple-element.10, pred[512]{0:T(512)(128)(4,1)S(1)} %get-tuple-element.9, pred[512]{0:T(512)(128)(4,1)S(1)} %get-tuple-element.8, pred[512]{0:T(512)(128)(4,1)S(1)} %get-tuple-element.7, pred[512]{0:T(512)(128)(4,1)S(1)} %get-tuple-element.6, s32[]{:T(128)} %bitcast.2, ...), kind=kLoop, calls=%fused_computation.32 | loop fusion | flops 2560 | bytes 4632 | tf_op jit(solution)/shard_map/gather | solution.py:51
  21.3 48.6 %all-gather.6.cloned.1.call-done = bf16[16,32,8192]{2,1,0:T(8,128)(2,1)} async-done(((bf16[4,32,8192]{2,1,0:T(8,128)(2,1)}), bf16[16,32,8192]{2,1,0:T(8,128)(2,1)}) %all-gather.6.cloned.1.call-update) | async-done | bytes 8388624 | tf_op jit(solution)/shard_map/all_gather | solution.py:42
  69.9 12.5 %convolution_convert_fusion = bf16[8,32,8192]{2,0,1:T(8,128)(2,1)S(1)} fusion(bf16[16,32,8192]{2,1,0:T(8,128)(2,1)} %all-gather.6.cloned.1.call-done, s32[8]{0:T(128)S(1)} %broadcast_select_fusion), kind=kOutput, calls=%fused_computation.2 | convolution fusion | flops 69206144 | bytes 12582944 | tf_op jit(solution)/shard_map/sp,pkd->skd/dot_general | solution.py:47
  82.4 4.4 %copy.18 = bf16[8,32,8192]{2,1,0:T(8,128)(2,1)} copy(bf16[8,32,8192]{2,0,1:T(8,128)(2,1)S(1)} %convolution_convert_fusion) | data formatting | bytes 8388608 | tf_op jit(solution)/shard_map/convert_element_type | solution.py:49
  86.8 134.3 %all-gather.4.cloned.1.call-done = bf16[512,8192]{1,0:T(8,128)(2,1)} async-done(((bf16[512,2048]{1,0:T(8,128)(2,1)}), bf16[512,8192]{1,0:T(8,128)(2,1)}) %all-gather.4.cloned.1.call-update) | async-done | bytes 8388624 | tf_op jit(solution)/shard_map/all_gather | solution.py:55
  221.2 7.0 %fusion.25 = f32[256,512]{1,0:T(8,128)S(1)} fusion(bf16[256,8192]{1,0:T(8,128)(2,1)} %bitcast.32, bf16[512,8192]{1,0:T(8,128)(2,1)} %all-gather.4.cloned.1.call-done), kind=kOutput, calls=%fused_computation.49 | convolution fusion | flops 2147483648 | bytes 13107200 | tf_op jit(solution)/shard_map/dot_general | solution.py:57
  228.2 0.1 multiply_reduce_fusion
  228.3 13.5 %all_gather.14 = bf16[512,128]{0,1:T(8,128)(2,1)S(1)} all-gather(bf16[512,32]{0,1:T(8,128)(2,1)S(1)} %multiply_reduce_fusion), channel_id=1, replica_groups=mesh['groups'=2,'tensor'=4,'dp'=4] {'tensor'}, dimensions={1}, use_global_device_ids=true | all-gather | bytes 163840 | tf_op jit(solution)/shard_map/all_gather | solution.py:65
  241.8 0.1 copy.19
  242.0 37.3 %all-gather.8.cloned.1.call-done = bf16[16,128,2048]{2,1,0:T(8,128)(2,1)} async-done(((bf16[4,128,2048]{2,1,0:T(8,128)(2,1)}), bf16[16,128,2048]{2,1,0:T(8,128)(2,1)}) %all-gather.8.cloned.1.call-update) | async-done | bytes 8388624 | tf_op jit(solution)/shard_map/all_gather | solution.py:43
  279.3 0.0 slice-start
  279.3 12.6 %fusion.6 = bf16[8,128,2048]{2,0,1:T(8,128)(2,1)S(1)} fusion(bf16[16,128,2048]{2,1,0:T(8,128)(2,1)} %all-gather.8.cloned.1.call-done, s32[8]{0:T(128)S(1)} %broadcast_select_fusion), kind=kOutput, calls=%fused_computation.10 | convolution fusion | flops 69206144 | bytes 12582944 | tf_op jit(solution)/shard_map/sp,pkd->skd/dot_general | solution.py:48
  291.9 0.0 slice-start.1
  291.9 5.7 %fusion.4 = f32[512,2048,1]{1,0,2:T(8,128)S(1)} fusion(bf16[8,128,2048]{2,0,1:T(8,128)(2,1)S(1)} %fusion.6, bf16[512,128]{1,0:T(8,128)(2,1)S(1)} %copy.19, bf16[512,8]{0,1:T(8,128)(2,1)S(1)} %get-tuple-element.11), kind=kOutput, calls=%fused_computation.8 | convolution fusion | flops 2148007936 | bytes 8527872 | tf_op jit(solution)/shard_map/dot_general | solution.py:71
  297.6 0.0 slice-done
  297.6 0.0 slice-done.1
  297.6 0.0 copy-start.1
  297.6 22.2 %fusion.3 = bf16[512,2048]{1,0:T(8,128)(2,1)} fusion(f32[512,2048,1]{1,0,2:T(8,128)S(1)} %fusion.4, bf16[512,8192]{1,0:T(8,128)(2,1)S(1)} %bitcast.35, bf16[8192,2048]{1,0:T(8,128)(2,1)} %param.9), kind=kOutput, calls=%fused_computation.7 | convolution fusion | flops 17181966336 | bytes 48234496 | tf_op jit(solution)/shard_map/dot_general | solution.py:56
  319.8 0.0 copy-done.1
  (7 shorter events, 0.1 us)
Async XLA Ops:
  6.5 2.9 copy-start
  6.5 63.4 %all-gather.6.cloned.1.call-start = ((), (), s32[]{:S(2)}) async-start(), calls=%async_computation.1 | async-start | bytes 10485760 | tf_op jit(solution)/shard_map/all_gather | solution.py:42
  7.3 213.9 %all-gather.4.cloned.1.call-start = ((), (), s32[]{:S(2)}) async-start(), calls=%async_computation | async-start | bytes 10485760 | tf_op jit(solution)/shard_map/all_gather | solution.py:55
  8.0 271.2 %all-gather.8.cloned.1.call-start = ((), (), s32[]{:S(2)}) async-start(), calls=%async_computation.2 | async-start | bytes 10485760 | tf_op jit(solution)/shard_map/all_gather | solution.py:43
  279.3 18.3 %slice-start = ((s8[8388608]{0:T(1024)(128)(4,1)}), s8[4194304]{0:T(1024)(128)(4,1)S(1)}, s32[]{:S(2)}) async-start(s8[8388608]{0:T(1024)(128)(4,1)} %bitcast.34), calls=%async_computation.3 | async-start | bytes 8388608
  291.9 5.7 %slice-start.1 = ((s8[8388608]{0:T(1024)(128)(4,1)}), s8[4194304]{0:T(1024)(128)(4,1)S(1)}, s32[]{:S(2)}) async-start(s8[8388608]{0:T(1024)(128)(4,1)} %bitcast.34), calls=%async_computation.4 | async-start | bytes 8388608
  297.6 22.2 %copy-start.1 = (s32[16]{0:T(128)S(1)}, s32[16]{0:T(128)}, u32[]{:S(2)}) copy-start(s32[16]{0:T(128)} %param.12) | copy-start | bytes 196
Sparse Core Ops, SparseCore 0:
  8.9 60.9 all-gather.5
  71.5 149.6 all-gather.3
  222.7 56.4 all-gather.7
where the time goes:
time: 327 us; the launch traced here: 326 us
  waiting for transfers between devices  222 us (68%)
  matrix products  60 us (18%)
  blocking collectives  13.5 us (4%)
  between operations  13.2 us (4%)
  other arithmetic  9.38 us (3%)
  local copies, waits for them, and re-layouts  7.83 us (2%)
    all_gather x1, waiting for transfers between devices, local(): fragment = lax.all_gather(attention_result, 'tensor', axis=1, tiled=True)  134 us
    all_gather x1, waiting for transfers between devices, local(): lax.all_gather(adapter_down_weight, 'dp', axis=0, tiled=True)  48.6 us
    all_gather x1, waiting for transfers between devices, local(): lax.all_gather(adapter_up_weight, 'dp', axis=0, tiled=True)  37.3 us
    dot_general x1, matrix products, local(): jnp.dot(fragment, output_weight, preferred_element_type=jnp.float32)  22.2 us
    all_gather x1, blocking collectives, local(): low_full = lax.all_gather(low_mine, 'tensor', axis=1, tiled=True)  13.5 us
    dot_general x1, matrix products, local(): jnp.einsum('sp,pkd->skd', picker, fragment[1], preferred_element_type=jnp...  12.6 us
    dot_general x1, matrix products, local(): jnp.einsum('sp,pkd->skd', picker, fragment[0], preferred_element_type=jnp...  12.5 us
    dot_general x1, matrix products, local(): lax.dot_general(fragment, flat_down, (((1,), (1,)), ((), ())), preferred_...  7.02 us
  transfers between devices with their start and end apart: 3, of which 3 were waited for; matrix products, arithmetic and copies ran while one was open for 11% of the time, Pallas kernels for 0%

commit v1 on v0

v1 whole, which is shorter than its diff:
```python
import jax
import jax.numpy as jnp
from jax import lax
from jax.sharding import PartitionSpec as P

ROW_CHUNKS = 2


def gather_pages(block, n_dp):
    held = block[None]
    step = n_dp // 2
    while step:
        pairs = [(i, i ^ step) for i in range(n_dp)]
        held = jnp.stack([held, lax.ppermute(held, "dp", pairs)], axis=1)
        held = held.reshape((-1,) + block.shape)
        step //= 2
    return held


def local(
    attention_result,
    output_weight,
    adapter_down_weight,
    adapter_up_weight,
    adapter_page_row,
    requests,
    row_request_entry,
    ranks,
):
    n_dp = lax.axis_size("dp")
    n_tensor = lax.axis_size("tensor")
    dp = lax.axis_index("dp")
    me = lax.axis_index("tensor")
    row_count, width = attention_result.shape
    holder_length, rank_part, _ = adapter_down_weight.shape
    rank_complete, output_columns = adapter_up_weight.shape[1:]
    own_list = requests[0]
    entries = own_list.shape[0]
    chunk_rows = row_count // ROW_CHUNKS

    pages = adapter_page_row[own_list]
    places = ((pages // holder_length) ^ dp) * holder_length + pages % holder_length

    def requested(block):
        every = gather_pages(block, n_dp).reshape((-1,) + block.shape[1:])
        return jnp.concatenate(
            [lax.dynamic_slice_in_dim(every, places[e], 1, 0) for e in range(entries)], axis=0
        )

    down = requested(adapter_down_weight).reshape(entries * rank_part, -1)
    up = requested(adapter_up_weight).reshape(entries * rank_complete, output_columns)

    base = [jnp.zeros((chunk_rows, output_columns), jnp.float32)] * ROW_CHUNKS
    low = [jnp.zeros((chunk_rows, entries * rank_part), jnp.float32)] * ROW_CHUNKS

    def add(c, features, source):
        start = jnp.clip(source, 0, n_tensor - 1) * width
        weight = lax.dynamic_slice_in_dim(output_weight, start, width, 0)
        down_part = lax.dynamic_slice_in_dim(down, start, width, 1)
        base[c] = base[c] + jnp.dot(features, weight, preferred_element_type=jnp.float32)
        low[c] = low[c] + lax.dot_general(
            features, down_part, (((1,), (1,)), ((), ())), preferred_element_type=jnp.float32
        )

    own = [attention_result[c * chunk_rows:(c + 1) * chunk_rows] for c in range(ROW_CHUNKS)]
    from_left, from_right = list(own), list(own)
    for c in range(ROW_CHUNKS):
        add(c, own[c], me)
    for s in range(1, n_tensor):
        right = [(i, i + 1) for i in range(s - 1, n_tensor - 1)]
        left = [(i, i - 1) for i in range(1, n_tensor - s + 1)]
        for c in range(ROW_CHUNKS):
            if s > n_tensor // 2:
                merged = jnp.where(me >= s - 1, from_left[c], from_right[c])
                merged = lax.ppermute(merged, "tensor", right + left)
                from_left[c] = from_right[c] = merged
                add(c, merged, jnp.where(me >= s, me - s, me + s))
            else:
                from_left[c] = lax.ppermute(from_left[c], "tensor", right)
                from_right[c] = lax.ppermute(from_right[c], "tensor", left)
                add(c, from_left[c], me - s)
                add(c, from_right[c], me + s)

    outs = []
    for c in range(ROW_CHUNKS):
        entry = row_request_entry[c * chunk_rows:(c + 1) * chunk_rows]
        one_hot = entry[:, None] == jnp.arange(entries)[None, :]
        row_rank = jnp.sum(jnp.where(one_hot, ranks[own_list][None, :], 0), axis=1)
        low_mine = jnp.sum(
            jnp.where(one_hot[:, :, None], low[c].reshape(chunk_rows, entries, rank_part), 0.0), axis=1
        ).astype(jnp.bfloat16)
        low_full = lax.all_gather(low_mine, "tensor", axis=1, tiled=True)
        live = jnp.arange(rank_complete)[None, :] < row_rank[:, None]
        masked = jnp.where(live, low_full, jnp.zeros_like(low_full))
        spread = jnp.where(one_hot[:, :, None], masked[:, None, :], jnp.zeros((), jnp.bfloat16))
        low_term = jnp.dot(
            spread.reshape(chunk_rows, entries * rank_complete), up, preferred_element_type=jnp.float32
        )
        outs.append((base[c] + low_term).astype(jnp.bfloat16))
    return jnp.concatenate(outs, axis=0)


def solution(mesh):
    in_specs = (
        P(("groups", "dp"), "tensor"),
        P(None, "tensor"),
        P("dp", "tensor", None),
        P("dp", None, "tensor"),
        P("groups"),
        P(("groups", "dp"), None),
        P(("groups", "dp")),
        P(),
    )
    out_specs = P(("groups", "dp"), "tensor")
    return jax.shard_map(local, mesh=mesh, in_specs=in_specs, out_specs=out_specs, check_vma=False)
```

time: 327 us -> 281 us (0.86)
  waiting for transfers between devices: 222 us -> 64.8 us
  matrix products: 60 us -> 93.3 us
  starting transfers between devices: 0.08 us -> 23.9 us
  local copies, waits for them, and re-layouts: 7.83 us -> 30.6 us
  blocking collectives: 13.5 us -> 32.9 us
  other arithmetic: 9.38 us -> 22.3 us
    all_gather x3 -> x0, waiting for transfers between devices: 220 us -> none  [the longest x1 134 us: local(): fragment = lax.all_gather(attention_result, 'tensor', axis=1, tiled=True)]
    ppermute x0 -> x14, waiting for transfers between devices: none -> 64.8 us  [the longest x2 27.3 us: local(): merged = lax.ppermute(merged, 'tensor', right + left)]
    dot_general x5 -> x26, matrix products: 60 us -> 93.3 us  [the longest x12 79.8 us: add(): jnp.dot(features, weight, preferred_element_type=jnp.float32)]
    ppermute x0 -> x14, starting transfers between devices: none -> 23.9 us  [the longest x4 13.1 us: local(): from_left[c] = lax.ppermute(from_left[c], 'tensor', right)]
    another operation x0 -> x4, other arithmetic: none -> 19.8 us  [gather_pages(): held = jnp.stack([held, lax.ppermute(held, 'dp', pairs)], axis=1)]
    all_gather x1 -> x2, blocking collectives: 13.5 us -> 32.9 us  [local(): low_full = lax.all_gather(low_mine, 'tensor', axis=1, tiled=True)]
    unnamed x8 -> x68, local copies, waits for them, and re-layouts: 0.02 us -> 14.7 us
    another operation x0 -> x1, local copies, waits for them, and re-layouts: none -> 8.29 us  [gather_pages(): held = jnp.stack([held, lax.ppermute(held, 'dp', pairs)], axis=1)]
  transfers between devices with their start and end apart: 3 -> 14, of which waited for: 3 -> 5; matrix products, arithmetic and copies ran while one was open for 11% -> 32% of each run, Pallas kernels for 0% -> 0%
where the time goes in v1:
time: 281 us; the launch traced here: 280 us
  matrix products  93.3 us (33%)
  waiting for transfers between devices  64.8 us (23%)
  blocking collectives  32.9 us (12%)
  local copies, waits for them, and re-layouts  30.6 us (11%)
  starting transfers between devices  23.9 us (9%)
  other arithmetic  22.3 us (8%)
  between operations  12 us (4%)
    dot_general x12, matrix products, add(): jnp.dot(features, weight, preferred_element_type=jnp.float32)  79.8 us
    all_gather x2, blocking collectives, local(): low_full = lax.all_gather(low_mine, 'tensor', axis=1, tiled=True)  32.9 us
    ppermute x2, waiting for transfers between devices, local(): merged = lax.ppermute(merged, 'tensor', right + left)  27.3 us
    ppermute x4, waiting for transfers between devices, gather_pages(): held = jnp.stack([held, lax.ppermute(held, 'dp', pairs)], axis=1)  25 us
    another operation x4, other arithmetic, gather_pages(): held = jnp.stack([held, lax.ppermute(held, 'dp', pairs)], axis=1)  19.8 us
    unnamed x68, local copies, waits for them, and re-layouts  14.7 us
    ppermute x4, starting transfers between devices, local(): from_left[c] = lax.ppermute(from_left[c], 'tensor', right)  13.1 us
    dot_general x12, matrix products, add(): lax.dot_general(features, down_part, (((1,), (1,)), ((), ())), preferred_...  11.4 us
  transfers between devices with their start and end apart: 14, of which 5 were waited for; matrix products, arithmetic and copies ran while one was open for 32% of the time, Pallas kernels for 0%

profile of v1, /device:TPU:0, one launch (start us, length us, event | category | flops | bytes accessed | tf_op | source)
XLA Modules:
  0.0 279.8 jit_solution(10288568574118968720)
XLA Ops:
  0.0 3.3 %fusion.142 = (bf16[256,2048]{1,0:T(8,128)(2,1)}, bf16[256,2048]{1,0:T(8,128)(2,1)}) fusion(bf16[512,2048]{1,0:T(8,128)(2,1)} %param.8), kind=kLoop, calls=%fused_computation.154 | loop fusion | bytes 4194304 | tf_op jit(solution)/shard_map/slice | solution.py:65
  3.3 5.9 %collective-permute-start = (bf16[256,2048]{1,0:T(8,128)(2,1)}, bf16[256,2048]{1,0:T(8,128)(2,1)}, u32[]{:S(2)}, u32[]{:S(2)}) collective-permute-start(bf16[256,2048]{1,0:T(8,128)(2,1)} %get-tuple-element.11), channel_id=1, source_target_pairs={{0,4},{4,8},{8,12},{1,5},{5,9},{9,13},{2,6},{6,10},{10,14},{3,7},{... | collective-permute-start | bytes 3145736 | tf_op jit(solution)/shard_map/ppermute | solution.py:79
  9.2 1.3 collective-permute-start.1
  10.5 5.5 %collective-permute-start.9 = (bf16[256,2048]{1,0:T(8,128)(2,1)}, bf16[256,2048]{1,0:T(8,128)(2,1)}, u32[]{:S(2)}, u32[]{:S(2)}) collective-permute-start(bf16[256,2048]{1,0:T(8,128)(2,1)} %get-tuple-element.12), channel_id=1, source_target_pairs={{0,4},{4,8},{8,12},{1,5},{5,9},{9,13},{2,6},{6,10},{10,14},{3,7},{... | collective-permute-start | bytes 3145736 | tf_op jit(solution)/shard_map/ppermute | solution.py:79
  16.0 1.3 collective-permute-start.10
  17.3 1.6 collective-permute-start.5
  32.9 5.7 %fusion.22 = f32[2048,256]{0,1:T(8,128)S(1)} fusion(bf16[8192,2048]{1,0:T(8,128)(2,1)} %param.9, s32[]{:T(128)S(6)} %select_n.128, bf16[512,2048]{1,0:T(8,128)(2,1)S(1)} %copy-done.14), kind=kOutput, calls=%fused_computation.26 | convolution fusion | flops 2147483648 | bytes 11534340 | tf_op jit(solution)/shard_map/dot_general | solution.py:60
  38.7 5.9 %fusion.20 = f32[2048,256]{0,1:T(8,128)S(1)} fusion(bf16[8192,2048]{1,0:T(8,128)(2,1)} %param.9, s32[]{:T(128)S(6)} %select_n.128, bf16[512,2048]{1,0:T(8,128)(2,1)S(1)} %copy-done.14), kind=kOutput, calls=%fused_computation.24 | convolution fusion | flops 2147483648 | bytes 11534340 | tf_op jit(solution)/shard_map/dot_general | solution.py:60
  44.6 8.8 %collective-permute-done.9 = bf16[256,2048]{1,0:T(8,128)(2,1)} collective-permute-done((bf16[256,2048]{1,0:T(8,128)(2,1)}, bf16[256,2048]{1,0:T(8,128)(2,1)}, u32[]{:S(2)}, u32[]{:S(2)}) %collective-permute-start.9) | collective-permute-done | bytes 1048608 | tf_op jit(solution)/shard_map/ppermute | solution.py:79
  53.4 1.5 collective-permute-start.7
  54.9 3.6 %collective-permute-done.10 = bf16[256,2048]{1,0:T(8,128)(2,1)} collective-permute-done((bf16[256,2048]{1,0:T(8,128)(2,1)}, bf16[256,2048]{1,0:T(8,128)(2,1)}, u32[]{:S(2)}, u32[]{:S(2)}) %collective-permute-start.10) | collective-permute-done | bytes 1048608 | tf_op jit(solution)/shard_map/ppermute | solution.py:80
  59.2 6.1 %fusion.14 = f32[2048,256]{0,1:T(8,128)S(1)} fusion(bf16[256,2048]{1,0:T(8,128)(2,1)} %collective-permute-done.10, bf16[8192,2048]{1,0:T(8,128)(2,1)} %param.9, s32[]{:T(128)S(6)} %select_n.130), kind=kOutput, calls=%fused_computation.18 | convolution fusion | flops 2147483648 | bytes 11534340 | tf_op jit(solution)/shard_map/dot_general | solution.py:60
  65.3 7.5 %fusion.67 = f32[2048,256]{0,1:T(8,128)} fusion(f32[2048,256]{0,1:T(8,128)S(1)} %fusion.14, f32[2048,256]{0,1:T(8,128)S(1)} %fusion.22, bf16[256,2048]{1,0:T(8,128)(2,1)} %collective-permute-done.9, bf16[8192,2048]{1,0:T(8,128)(2,1)} %param.9, s32[]{:T(128)S(6)} %select_n.129), kind=kOutput, calls=%fused_computation.49 | convolution fusion | flops 2148532224 | bytes 15728644 | tf_op jit(solution)/shard_map/dot_general | solution.py:60
  72.8 1.3 collective-permute-start.12
  74.1 2.5 fusion.27
  76.7 6.1 %fusion.12 = f32[2048,256]{0,1:T(8,128)S(1)} fusion(bf16[256,2048]{1,0:T(8,128)(2,1)} %collective-permute-done.1, bf16[8192,2048]{1,0:T(8,128)(2,1)} %param.9, s32[]{:T(128)S(6)} %select_n.130), kind=kOutput, calls=%fused_computation.16 | convolution fusion | flops 2147483648 | bytes 11534340 | tf_op jit(solution)/shard_map/dot_general | solution.py:60
  82.8 1.3 collective-permute-start.3
  84.1 25.0 %collective-permute-done.7 = bf16[1,4,128,2048]{3,2,1,0:T(8,128)(2,1)S(1)} collective-permute-done((bf16[1,4,128,2048]{3,2,1,0:T(8,128)(2,1)S(1)}, bf16[1,4,128,2048]{3,2,1,0:T(8,128)(2,1)S(1)}, u32[]{:S(2)}, u32[]{:S(2)}) %collective-permute-start.7) | collective-permute-done | bytes 2097184 | tf_op jit(solution)/shard_map/ppermute | solution.py:14
  110.0 7.6 %fusion.64 = f32[2048,256]{0,1:T(8,128)} fusion(f32[2048,256]{0,1:T(8,128)S(1)} %fusion.12, f32[2048,256]{0,1:T(8,128)S(1)} %fusion.20, bf16[256,2048]{1,0:T(8,128)(2,1)} %collective-permute-done, bf16[8192,2048]{1,0:T(8,128)(2,1)} %param.9, s32[]{:T(128)S(6)} %select_n.129), kind=kOutput, calls=%fused_computation.48 | convolution fusion | flops 2148532224 | bytes 15728644 | tf_op jit(solution)/shard_map/dot_general | solution.py:60
  117.5 3.6 %fusion.25 = (bf16[2,1,4,128,2048]{4,3,2,0,1:T(8,128)(2,1)}, bf16[2,4,128,2048]{3,2,1,0:T(8,128)(2,1)}) fusion(bf16[1,1,4,128,2048]{4,3,2,1,0:T(8,128)(2,1)S(1)} %bitcast.110, bf16[1,1,4,128,2048]{4,3,2,1,0:T(8,128)(2,1)S(1)} %bitcast.109), kind=kLoop, calls=%fused_computation.33 | loop fusion | flops 2097152 | bytes 12582912 | tf_op jit(solution)/shard_map/stack;reshape | solution.py:14
  121.2 1.3 collective-permute-start.13
  122.7 1.3 collective-permute-start.4
  124.0 7.1 %fusion.6 = f32[2048,256]{0,1:T(8,128)} fusion(bf16[256,2048]{1,0:T(8,128)(2,1)S(1)} %collective-permute-done.12, bf16[8192,2048]{1,0:T(8,128)(2,1)} %param.9, s32[]{:T(128)S(6)} %select_n.132), kind=kOutput, calls=%fused_computation.10 | convolution fusion | flops 2147483648 | bytes 11534340 | tf_op jit(solution)/shard_map/dot_general | solution.py:60
  131.1 7.0 %fusion.4 = f32[2048,256]{0,1:T(8,128)} fusion(bf16[256,2048]{1,0:T(8,128)(2,1)S(1)} %collective-permute-done.3, bf16[8192,2048]{1,0:T(8,128)(2,1)} %param.9, s32[]{:T(128)S(6)} %select_n.132), kind=kOutput, calls=%fused_computation.8 | convolution fusion | flops 2147483648 | bytes 11534340 | tf_op jit(solution)/shard_map/dot_general | solution.py:60
  138.1 12.5 %collective-permute-done.13 = bf16[256,2048]{1,0:T(8,128)(2,1)S(1)} collective-permute-done((bf16[256,2048]{1,0:T(8,128)(2,1)S(1)}, bf16[256,2048]{1,0:T(8,128)(2,1)S(1)}, u32[]{:S(2)}, u32[]{:S(2)}) %collective-permute-start.13) | collective-permute-done | bytes 1048608 | tf_op jit(solution)/shard_map/ppermute | solution.py:75
  150.6 7.4 %fusion = f32[256,2048]{1,0:T(8,128)} fusion(bf16[256,2048]{1,0:T(8,128)(2,1)S(1)} %collective-permute-done.13, bf16[8192,2048]{1,0:T(8,128)(2,1)} %param.9, s32[]{:T(128)S(6)} %select_n.136), kind=kOutput, calls=%fused_computation.4 | convolution fusion | flops 2147483648 | bytes 11534340 | tf_op jit(solution)/shard_map/dot_general | solution.py:60
  158.0 14.8 %collective-permute-done.4 = bf16[256,2048]{1,0:T(8,128)(2,1)S(1)} collective-permute-done((bf16[256,2048]{1,0:T(8,128)(2,1)S(1)}, bf16[256,2048]{1,0:T(8,128)(2,1)S(1)}, u32[]{:S(2)}, u32[]{:S(2)}) %collective-permute-start.4) | collective-permute-done | bytes 1048608 | tf_op jit(solution)/shard_map/ppermute | solution.py:75
  172.9 7.4 %fusion.2 = f32[256,2048]{1,0:T(8,128)} fusion(bf16[256,2048]{1,0:T(8,128)(2,1)S(1)} %collective-permute-done.4, bf16[8192,2048]{1,0:T(8,128)(2,1)} %param.9, s32[]{:T(128)S(6)} %select_n.136), kind=kOutput, calls=%fused_computation.6 | convolution fusion | flops 2147483648 | bytes 11534340 | tf_op jit(solution)/shard_map/dot_general | solution.py:60
  180.3 2.0 copy-done.13
  182.3 6.2 %pad_maximum_fusion = bf16[2,2,4,32,8192]{4,3,2,1,0:T(8,128)(2,1)} fusion(bf16[2,1,4,32,8192]{4,3,2,1,0:T(8,128)(2,1)} %bitcast.107, bf16[2,1,4,32,8192]{4,3,2,1,0:T(8,128)(2,1)S(1)} %get-tuple-element.7), kind=kLoop, calls=%fused_computation.2 | loop fusion | flops 4194304 | bytes 16777216 | tf_op jit(solution)/shard_map/stack | solution.py:14
  189.6 1.1 dynamic-slice_dynamic-update-slice_fusion.10
  191.8 1.1 dynamic-slice_dynamic-update-slice_fusion.8
  193.9 1.1 dynamic-slice_dynamic-update-slice_fusion.6
  196.0 7.5 %pad_maximum_fusion.1 = bf16[2,2,4,128,2048]{4,3,2,0,1:T(8,128)(2,1)} fusion(bf16[2,1,4,128,2048]{4,3,2,0,1:T(8,128)(2,1)} %bitcast.25, bf16[2,1,4,128,2048]{4,3,2,0,1:T(8,128)(2,1)} %get-tuple-element.9), kind=kLoop, calls=%fused_computation.3 | loop fusion | flops 4194304 | bytes 16777216 | tf_op jit(solution)/shard_map/stack | solution.py:14
  203.6 8.3 %copy.14 = bf16[2,2,4,128,2048]{4,3,2,1,0:T(8,128)(2,1)} copy(bf16[2,2,4,128,2048]{4,3,2,0,1:T(8,128)(2,1)} %pad_maximum_fusion.1) | data formatting | bytes 16777216 | tf_op jit(solution)/shard_map/stack | solution.py:14
  211.8 1.2 dynamic-slice_dynamic-update-slice_fusion.5
  213.0 1.1 dynamic-slice_dynamic-update-slice_fusion.4
  214.1 1.2 dynamic-slice_dynamic-update-slice_fusion.3
  215.3 1.1 dynamic-slice_dynamic-update-slice_fusion.2
  219.6 1.8 convolution_add_fusion.5
  221.4 2.0 convolution_add_fusion.4
  224.0 19.7 %all_gather.6 = bf16[256,128]{0,1:T(8,128)(2,1)S(1)} all-gather(bf16[256,32]{0,1:T(8,128)(2,1)S(1)} %select_reduce_fusion.1), channel_id=1, replica_groups=mesh['groups'=2,'tensor'=4,'dp'=4] {'tensor'}, dimensions={1}, use_global_device_ids=true | all-gather | bytes 81920 | tf_op jit(solution)/shard_map/all_gather | solution.py:92
  244.8 1.7 convolution_add_fusion.2
  246.6 1.7 convolution_add_fusion.1
  248.9 13.2 %all_gather.7 = bf16[256,128]{0,1:T(8,128)(2,1)S(1)} all-gather(bf16[256,32]{0,1:T(8,128)(2,1)S(1)} %select_reduce_fusion), channel_id=1, replica_groups=mesh['groups'=2,'tensor'=4,'dp'=4] {'tensor'}, dimensions={1}, use_global_device_ids=true | all-gather | bytes 81920 | tf_op jit(solution)/shard_map/all_gather | solution.py:92
  266.1 6.1 %fusion.70 = bf16[256,2048]{1,0:T(8,128)(2,1)S(1)} fusion(f32[256,2048]{1,0:T(8,128)S(1)} %convolution_bitcast_fusion, f32[256,2048]{1,0:T(8,128)S(1)} %copy-done.26, f32[2048,256]{0,1:T(8,128)S(1)} %copy-done.24, f32[2048,256]{0,1:T(8,128)S(1)} %copy-done.27, bf16[256,2048]{1,0:T(8,128)(2,1)S(1)} %copy-done.5, bf16[8192,2048]{1,0:T(8,128)(2,1)} %param.9, ...), kind=kOutput, calls=%fused_computation.50 | convolution fusion | flops 2150105088 | bytes 18874372 | tf_op jit(solution)/shard_map/dot_general | solution.py:60
  272.2 6.0 %fusion.73 = bf16[256,2048]{1,0:T(8,128)(2,1)S(1)} fusion(f32[256,2048]{1,0:T(8,128)S(1)} %convolution_bitcast_fusion.1, f32[256,2048]{1,0:T(8,128)S(1)} %copy-done.25, f32[2048,256]{0,1:T(8,128)S(1)} %copy-done.23, f32[2048,256]{0,1:T(8,128)S(1)} %copy-done.28, bf16[256,2048]{1,0:T(8,128)(2,1)S(1)} %copy-done.8, bf16[8192,2048]{1,0:T(8,128)(2,1)} %param.9, ...), kind=kOutput, calls=%fused_computation.51 | convolution fusion | flops 2150105088 | bytes 18874372 | tf_op jit(solution)/shard_map/dot_general | solution.py:60
  278.2 1.6 pad_maximum_fusion.4
  (102 shorter events, 18.1 us)
Async XLA Ops:
  0.0 18.9 %copy-start = (s32[16]{0:T(128)S(1)}, s32[16]{0:T(128)}, u32[]{:S(2)}) copy-start(s32[16]{0:T(128)} %param.12) | copy-start | bytes 196
  0.0 32.9 %copy-start.14 = (bf16[512,2048]{1,0:T(8,128)(2,1)S(1)}, bf16[512,2048]{1,0:T(8,128)(2,1)}, u32[]{:S(2)}) copy-start(bf16[512,2048]{1,0:T(8,128)(2,1)} %param.8) | copy-start | bytes 6291460
  0.0 18.9 %copy-start.22 = (s32[1,6]{1,0:T(1,128)S(1)}, s32[1,6]{1,0:T(1,128)}, u32[]{:S(2)}) copy-start(s32[1,6]{1,0:T(1,128)} %param.13) | copy-start | bytes 76
  0.0 18.9 %copy-start.21 = (s32[512]{0:T(512)S(1)}, s32[512]{0:T(512)}, u32[]{:S(2)}) copy-start(s32[512]{0:T(512)} %param.14) | copy-start | bytes 6148
  0.0 19.6 %copy-start.2 = (s32[16]{0:T(128)S(1)}, s32[16]{0:T(128)}, u32[]{:S(2)}) copy-start(s32[16]{0:T(128)} %param.15) | copy-start | bytes 196
  3.3 79.5 %collective-permute-start = (bf16[256,2048]{1,0:T(8,128)(2,1)}, bf16[256,2048]{1,0:T(8,128)(2,1)}, u32[]{:S(2)}, u32[]{:S(2)}) collective-permute-start(bf16[256,2048]{1,0:T(8,128)(2,1)} %get-tuple-element.11), channel_id=1, source_target_pairs={{0,4},{4,8},{8,12},{1,5},{5,9},{9,13},{2,6},{6,10},{10,14},{3,7},{... | collective-permute-start | bytes 3145736 | tf_op jit(solution)/shard_map/ppermute | solution.py:79
  9.2 67.4 %collective-permute-start.1 = (bf16[256,2048]{1,0:T(8,128)(2,1)}, bf16[256,2048]{1,0:T(8,128)(2,1)}, u32[]{:S(2)}, u32[]{:S(2)}) collective-permute-start(bf16[256,2048]{1,0:T(8,128)(2,1)} %get-tuple-element.11), channel_id=1, source_target_pairs={{4,0},{8,4},{12,8},{5,1},{9,5},{13,9},{6,2},{10,6},{14,10},{7,3},{... | collective-permute-start | bytes 3145736 | tf_op jit(solution)/shard_map/ppermute | solution.py:80
  10.5 42.9 %collective-permute-start.9 = (bf16[256,2048]{1,0:T(8,128)(2,1)}, bf16[256,2048]{1,0:T(8,128)(2,1)}, u32[]{:S(2)}, u32[]{:S(2)}) collective-permute-start(bf16[256,2048]{1,0:T(8,128)(2,1)} %get-tuple-element.12), channel_id=1, source_target_pairs={{0,4},{4,8},{8,12},{1,5},{5,9},{9,13},{2,6},{6,10},{10,14},{3,7},{... | collective-permute-start | bytes 3145736 | tf_op jit(solution)/shard_map/ppermute | solution.py:79
  16.0 42.5 %collective-permute-start.10 = (bf16[256,2048]{1,0:T(8,128)(2,1)}, bf16[256,2048]{1,0:T(8,128)(2,1)}, u32[]{:S(2)}, u32[]{:S(2)}) collective-permute-start(bf16[256,2048]{1,0:T(8,128)(2,1)} %get-tuple-element.12), channel_id=1, source_target_pairs={{4,0},{8,4},{12,8},{5,1},{9,5},{13,9},{6,2},{10,6},{14,10},{7,3},{... | collective-permute-start | bytes 3145736 | tf_op jit(solution)/shard_map/ppermute | solution.py:80
  17.3 55.5 %collective-permute-start.5 = (bf16[1,4,32,8192]{3,2,1,0:T(8,128)(2,1)}, bf16[1,4,32,8192]{3,2,1,0:T(8,128)(2,1)}, u32[]{:S(2)}, u32[]{:S(2)}) collective-permute-start(bf16[1,4,32,8192]{3,2,1,0:T(8,128)(2,1)} %bitcast.4), channel_id=1, source_target_pairs={{0,2},{1,3},{2,0},{3,1},{4,6},{5,7},{6,4},{7,5},{8,10},{9,11},{10,... | collective-permute-start | bytes 6291464 | tf_op jit(solution)/shard_map/ppermute | solution.py:14
  38.7 14.7 %copy-start.15 = (bf16[4,128,2048]{2,1,0:T(8,128)(2,1)S(1)}, bf16[4,128,2048]{2,1,0:T(8,128)(2,1)}, u32[]{:S(2)}) copy-start(bf16[4,128,2048]{2,1,0:T(8,128)(2,1)} %param.11) | copy-start | bytes 6291460
  53.4 55.6 %collective-permute-start.7 = (bf16[1,4,128,2048]{3,2,1,0:T(8,128)(2,1)S(1)}, bf16[1,4,128,2048]{3,2,1,0:T(8,128)(2,1)S(1)}, u32[]{:S(2)}, u32[]{:S(2)}) collective-permute-start(bf16[1,4,128,2048]{3,2,1,0:T(8,128)(2,1)S(1)} %bitcast.108), channel_id=1, source_target_pairs={{0,2},{1,3},{2,0},{3,1},{4,6},{5,7},{6,4},{7,5},{8,10},{9,11},{10,... | collective-permute-start | bytes 6291464 | tf_op jit(solution)/shard_map/ppermute | solution.py:14
  58.5 62.6 %collective-permute-start.11 = (bf16[256,2048]{1,0:T(8,128)(2,1)}, bf16[256,2048]{1,0:T(8,128)(2,1)S(1)}, u32[]{:S(2)}, u32[]{:S(2)}) collective-permute-start(bf16[256,2048]{1,0:T(8,128)(2,1)} %collective-permute-done.9), channel_id=1, source_target_pairs={{4,8},{8,12},{5,9},{9,13},{6,10},{10,14},{7,11},{11,15},{20,24},{2... | collective-permute-start | bytes 3145736 | tf_op jit(solution)/shard_map/ppermute | solution.py:79
  72.8 48.3 %collective-permute-start.12 = (bf16[256,2048]{1,0:T(8,128)(2,1)}, bf16[256,2048]{1,0:T(8,128)(2,1)S(1)}, u32[]{:S(2)}, u32[]{:S(2)}) collective-permute-start(bf16[256,2048]{1,0:T(8,128)(2,1)} %collective-permute-done.10), channel_id=1, source_target_pairs={{4,0},{8,4},{5,1},{9,5},{6,2},{10,6},{7,3},{11,7},{20,16},{24,20},... | collective-permute-start | bytes 3145736 | tf_op jit(solution)/shard_map/ppermute | solution.py:80
  76.6 103.7 %collective-permute-start.6 = (bf16[2,4,32,8192]{3,2,1,0:T(8,128)(2,1)S(1)}, bf16[2,4,32,8192]{3,2,1,0:T(8,128)(2,1)S(1)}, u32[]{:S(2)}, u32[]{:S(2)}) collective-permute-start(bf16[2,4,32,8192]{3,2,1,0:T(8,128)(2,1)S(1)} %get-tuple-element.8), channel_id=1, source_target_pairs={{0,1},{1,0},{2,3},{3,2},{4,5},{5,4},{6,7},{7,6},{8,9},{9,8},{10,11... | collective-permute-start | bytes 12582920 | tf_op jit(solution)/shard_map/ppermute | solution.py:14
  82.8 39.8 %collective-permute-start.3 = (bf16[256,2048]{1,0:T(8,128)(2,1)}, bf16[256,2048]{1,0:T(8,128)(2,1)S(1)}, u32[]{:S(2)}, u32[]{:S(2)}) collective-permute-start(bf16[256,2048]{1,0:T(8,128)(2,1)} %collective-permute-done.1), channel_id=1, source_target_pairs={{4,0},{8,4},{5,1},{9,5},{6,2},{10,6},{7,3},{11,7},{20,16},{24,20},... | collective-permute-start | bytes 3145736 | tf_op jit(solution)/shard_map/ppermute | solution.py:80
  109.1 13.5 %collective-permute-start.2 = (bf16[256,2048]{1,0:T(8,128)(2,1)}, bf16[256,2048]{1,0:T(8,128)(2,1)S(1)}, u32[]{:S(2)}, u32[]{:S(2)}) collective-permute-start(bf16[256,2048]{1,0:T(8,128)(2,1)} %collective-permute-done), channel_id=1, source_target_pairs={{4,8},{8,12},{5,9},{9,13},{6,10},{10,14},{7,11},{11,15},{20,24},{2... | collective-permute-start | bytes 3145736 | tf_op jit(solution)/shard_map/ppermute | solution.py:79
  121.1 1.6 copy-start.3
  121.1 74.9 %collective-permute-start.8 = (bf16[2,4,128,2048]{3,2,1,0:T(8,128)(2,1)}, bf16[2,4,128,2048]{3,2,1,0:T(8,128)(2,1)}, u32[]{:S(2)}, u32[]{:S(2)}) collective-permute-start(bf16[2,4,128,2048]{3,2,1,0:T(8,128)(2,1)} %get-tuple-element.10), channel_id=1, source_target_pairs={{0,1},{1,0},{2,3},{3,2},{4,5},{5,4},{6,7},{7,6},{8,9},{9,8},{10,11... | collective-permute-start | bytes 12582920 | tf_op jit(solution)/shard_map/ppermute | solution.py:14
  121.1 2.9 %copy-start.9 = (bf16[256,2048]{1,0:T(8,128)(2,1)}, bf16[256,2048]{1,0:T(8,128)(2,1)S(1)}, u32[]{:S(2)}) copy-start(bf16[256,2048]{1,0:T(8,128)(2,1)S(1)} %collective-permute-done.12) | copy-start | bytes 3145732
  121.2 29.4 %collective-permute-start.13 = (bf16[256,2048]{1,0:T(8,128)(2,1)S(1)}, bf16[256,2048]{1,0:T(8,128)(2,1)S(1)}, u32[]{:S(2)}, u32[]{:S(2)}) collective-permute-start(bf16[256,2048]{1,0:T(8,128)(2,1)S(1)} %broadcast_select_fusion), channel_id=1, source_target_pairs={{8,12},{4,0},{9,13},{5,1},{10,14},{6,2},{11,15},{7,3},{24,28},{20,... | collective-permute-start | bytes 3145736 | tf_op jit(solution)/shard_map/ppermute | solution.py:75
  122.6 8.5 %copy-start.6 = (bf16[256,2048]{1,0:T(8,128)(2,1)}, bf16[256,2048]{1,0:T(8,128)(2,1)S(1)}, u32[]{:S(2)}) copy-start(bf16[256,2048]{1,0:T(8,128)(2,1)S(1)} %collective-permute-done.2) | copy-start | bytes 3145732
  122.6 8.5 %copy-start.11 = (bf16[256,2048]{1,0:T(8,128)(2,1)}, bf16[256,2048]{1,0:T(8,128)(2,1)S(1)}, u32[]{:S(2)}) copy-start(bf16[256,2048]{1,0:T(8,128)(2,1)S(1)} %collective-permute-done.3) | copy-start | bytes 3145732
  122.7 50.1 %collective-permute-start.4 = (bf16[256,2048]{1,0:T(8,128)(2,1)S(1)}, bf16[256,2048]{1,0:T(8,128)(2,1)S(1)}, u32[]{:S(2)}, u32[]{:S(2)}) collective-permute-start(bf16[256,2048]{1,0:T(8,128)(2,1)S(1)} %broadcast_select_fusion.1), channel_id=1, source_target_pairs={{8,12},{4,0},{9,13},{5,1},{10,14},{6,2},{11,15},{7,3},{24,28},{20,... | collective-permute-start | bytes 3145736 | tf_op jit(solution)/shard_map/ppermute | solution.py:75
  150.6 7.4 %copy-start.16 = (bf16[256,2048]{1,0:T(8,128)(2,1)}, bf16[256,2048]{1,0:T(8,128)(2,1)S(1)}, u32[]{:S(2)}) copy-start(bf16[256,2048]{1,0:T(8,128)(2,1)S(1)} %collective-permute-done.13) | copy-start | bytes 3145732
  172.9 7.4 %copy-start.18 = (bf16[256,2048]{1,0:T(8,128)(2,1)}, bf16[256,2048]{1,0:T(8,128)(2,1)S(1)}, u32[]{:S(2)}) copy-start(bf16[256,2048]{1,0:T(8,128)(2,1)S(1)} %collective-permute-done.4) | copy-start | bytes 3145732
  180.3 2.0 copy-start.13
  211.8 6.7 %copy-start.19 = (bf16[256,2048]{1,0:T(8,128)(2,1)S(1)}, bf16[256,2048]{1,0:T(8,128)(2,1)}, u32[]{:S(2)}) copy-start(bf16[256,2048]{1,0:T(8,128)(2,1)} %copy-done.18) | copy-start | bytes 3145732
  214.1 5.0 %copy-start.12 = (bf16[256,2048]{1,0:T(8,128)(2,1)S(1)}, bf16[256,2048]{1,0:T(8,128)(2,1)}, u32[]{:S(2)}) copy-start(bf16[256,2048]{1,0:T(8,128)(2,1)} %copy-done.11) | copy-start | bytes 3145732
  219.1 4.4 %copy-start.7 = (bf16[256,2048]{1,0:T(8,128)(2,1)S(1)}, bf16[256,2048]{1,0:T(8,128)(2,1)}, u32[]{:S(2)}) copy-start(bf16[256,2048]{1,0:T(8,128)(2,1)} %copy-done.6) | copy-start | bytes 3145732
  219.6 24.2 %copy-start.17 = (bf16[256,2048]{1,0:T(8,128)(2,1)S(1)}, bf16[256,2048]{1,0:T(8,128)(2,1)}, u32[]{:S(2)}) copy-start(bf16[256,2048]{1,0:T(8,128)(2,1)} %copy-done.16) | copy-start | bytes 3145732
  221.4 22.9 %copy-start.10 = (bf16[256,2048]{1,0:T(8,128)(2,1)S(1)}, bf16[256,2048]{1,0:T(8,128)(2,1)}, u32[]{:S(2)}) copy-start(bf16[256,2048]{1,0:T(8,128)(2,1)} %copy-done.9) | copy-start | bytes 3145732
  244.3 4.0 %copy-start.4 = (bf16[256,2048]{1,0:T(8,128)(2,1)S(1)}, bf16[256,2048]{1,0:T(8,128)(2,1)}, u32[]{:S(2)}) copy-start(bf16[256,2048]{1,0:T(8,128)(2,1)} %copy-done.3) | copy-start | bytes 3145732
  244.8 17.2 %copy-start.20 = (s32[256]{0:T(256)S(1)}, s32[256]{0:T(256)}, u32[]{:S(2)}) copy-start(s32[256]{0:T(256)} %get-tuple-element.6) | copy-start | bytes 3076
  262.3 2.2 copy-start.27
  263.4 1.4 copy-start.5
  263.4 2.0 copy-start.24
  263.4 2.6 copy-start.26
  266.0 6.1 %copy-start.8 = (bf16[256,2048]{1,0:T(8,128)(2,1)S(1)}, bf16[256,2048]{1,0:T(8,128)(2,1)}, u32[]{:S(2)}) copy-start(bf16[256,2048]{1,0:T(8,128)(2,1)} %copy-done.6) | copy-start | bytes 3145732
  266.0 6.2 %copy-start.23 = (f32[2048,256]{0,1:T(8,128)S(1)}, f32[2048,256]{0,1:T(8,128)}, u32[]{:S(2)}) copy-start(f32[2048,256]{0,1:T(8,128)} %fusion.4) | copy-start | bytes 6291460
  266.0 6.2 %copy-start.25 = (f32[256,2048]{1,0:T(8,128)S(1)}, f32[256,2048]{1,0:T(8,128)}, u32[]{:S(2)}) copy-start(f32[256,2048]{1,0:T(8,128)} %fusion.2) | copy-start | bytes 6291460
  266.0 6.2 %copy-start.28 = (f32[2048,256]{0,1:T(8,128)S(1)}, f32[2048,256]{0,1:T(8,128)}, u32[]{:S(2)}) copy-start(f32[2048,256]{0,1:T(8,128)} %fusion.64) | copy-start | bytes 6291460
  272.2 7.6 %copy-start.1 = (s32[16]{0:T(128)S(1)}, s32[16]{0:T(128)}, u32[]{:S(2)}) copy-start(s32[16]{0:T(128)} %param.12) | copy-start | bytes 196

commit v2 on v1

v2 whole, which is shorter than its diff:
```python
import functools

import jax
import jax.numpy as jnp
from jax import lax
from jax.experimental import pallas as pl
from jax.experimental.pallas import tpu as pltpu
from jax.sharding import PartitionSpec as P

PARAMS = pltpu.CompilerParams(vmem_limit_bytes=40 * 2**20)
F32 = jnp.float32
BF16 = jnp.bfloat16


def gather_pages(block, n_dp):
    held = {0: block}
    step = n_dp // 2
    while step:
        pairs = [(i, i ^ step) for i in range(n_dp)]
        held.update({j | step: lax.ppermute(b, "dp", pairs) for j, b in held.items()})
        step //= 2
    return [held[j] for j in range(n_dp)]


def pick_kernel(length, places, *refs):
    *blocks, out, sems = refs
    entries = out.shape[0]
    for e in range(entries):
        for j, block in enumerate(blocks):

            @pl.when(places[e] // length == j)
            def _():
                pltpu.make_async_copy(block.at[places[e] % length], out.at[e], sems.at[e]).start()

    for e in range(entries):
        pltpu.make_async_copy(blocks[0].at[0], out.at[e], sems.at[e]).wait()


def pick_pages(places, blocks):
    entries = places.shape[0]
    length, rows, columns = blocks[0].shape
    return pl.pallas_call(
        functools.partial(pick_kernel, length),
        out_shape=jax.ShapeDtypeStruct((entries, rows, columns), BF16),
        in_specs=[pl.BlockSpec(memory_space=pltpu.SMEM)] + [pl.BlockSpec(memory_space=pl.ANY)] * len(blocks),
        out_specs=pl.BlockSpec(memory_space=pl.ANY),
        scratch_shapes=[pltpu.SemaphoreType.DMA((entries,))],
        cost_estimate=pl.CostEstimate(flops=0, bytes_accessed=4 * entries * rows * columns, transcendentals=0),
    )(places, *blocks)


def base_kernel(has_total, x, weight, *refs):
    out = refs[-1]
    columns = out.shape[1]
    part = min(columns, 512)

    @pl.when(pl.program_id(0) == 0)
    def _():
        out[...] = refs[0][...] if has_total else jnp.zeros_like(out)

    for n in range(0, columns, part):
        out[:, n:n + part] += jnp.dot(x[0], weight[0, :, n:n + part], preferred_element_type=F32)


def add_base(total, x, weight, k):
    shards, rows, features = x.shape
    columns = weight.shape[-1]
    held = [] if total is None else [total]
    whole = pl.BlockSpec((rows, columns), lambda t: (0, 0))
    return pl.pallas_call(
        functools.partial(base_kernel, bool(held)),
        grid=(shards,),
        out_shape=jax.ShapeDtypeStruct((rows, columns), F32),
        in_specs=[
            pl.BlockSpec((1, rows, features), lambda t: (t, 0, 0)),
            pl.BlockSpec((1, features, columns), lambda t: (t, k, 0)),
        ] + [whole] * len(held),
        out_specs=whole,
        compiler_params=PARAMS,
        cost_estimate=pl.CostEstimate(
            flops=2 * shards * rows * features * columns,
            bytes_accessed=2 * shards * features * (rows + columns) + 8 * rows * columns,
            transcendentals=0,
        ),
    )(x, weight, *held)


def low_kernel(has_total, last, rank_part, x, down, *refs):
    refs = list(refs)
    total = refs.pop(0) if has_total else None
    step = pl.program_id(0)
    out = refs[-1]
    acc = out if not last else refs.pop()
    if last:
        out = refs[-1]

    @pl.when(step == 0)
    def _():
        acc[...] = total[...] if has_total else jnp.zeros_like(acc)

    acc[...] += lax.dot_general(x[0], down[...], (((1,), (1,)), ((), ())), preferred_element_type=F32)
    if last:
        entry, live = refs[0], refs[1]

        @pl.when(step == pl.num_programs(0) - 1)
        def _():
            mine = jnp.zeros((acc.shape[0], rank_part), F32)
            for e in range(acc.shape[1] // rank_part):
                mine += jnp.where(entry[...] == e, acc[:, e * rank_part:(e + 1) * rank_part], 0.0)
            k = lax.broadcasted_iota(jnp.int32, mine.shape, 1)
            out[...] = jnp.where(k < live[...], mine.astype(BF16).astype(F32), 0.0).astype(BF16)


def add_low(total, x, down, k, chunks, rank_part, entry=None, live=None):
    shards, rows, features = x.shape
    ranks = down.shape[0]
    last = entry is not None
    held = [] if total is None else [total]
    whole = pl.BlockSpec((rows, ranks), lambda t: (0, 0))
    column = pl.BlockSpec((rows, 1), lambda t: (0, 0))
    return pl.pallas_call(
        functools.partial(low_kernel, bool(held), last, rank_part),
        grid=(shards,),
        out_shape=jax.ShapeDtypeStruct((rows, rank_part), BF16) if last else jax.ShapeDtypeStruct((rows, ranks), F32),
        in_specs=[
            pl.BlockSpec((1, rows, features), lambda t: (t, 0, 0)),
            pl.BlockSpec((ranks, features), lambda t: (0, t * chunks + k)),
        ] + [whole] * len(held) + ([column, column] if last else []),
        out_specs=pl.BlockSpec((rows, rank_part), lambda t: (0, 0)) if last else whole,
        scratch_shapes=[pltpu.VMEM((rows, ranks), F32)] if last else [],
        compiler_params=PARAMS,
        cost_estimate=pl.CostEstimate(
            flops=2 * shards * rows * features * ranks,
            bytes_accessed=2 * shards * features * (rows + ranks) + 8 * rows * ranks,
            transcendentals=0,
        ),
    )(x, down, *held, *([entry, live] if last else []))


def finish_kernel(parts, me, entry, total, up, *refs):
    lows, (out, spread) = refs[:parts], refs[parts:]
    rank_part = lows[0].shape[1]
    rank = parts * rank_part

    @pl.when(pl.program_id(0) == 0)
    def _():
        low = jnp.concatenate([part[...].astype(F32) for part in lows], axis=1)
        low = pltpu.roll(low, me[0] * rank_part, 1)
        for e in range(up.shape[0] // rank):
            spread[:, e * rank:(e + 1) * rank] = jnp.where(entry[...] == e, low, 0.0).astype(BF16)

    term = jnp.dot(spread[...], up[...], preferred_element_type=F32)
    out[...] = (total[...] + term).astype(BF16)


def finish(me, entry, total, up, lows):
    rows, columns = total.shape
    depth = up.shape[0]
    rank_part = lows[0].shape[1]
    part = min(columns, 512)
    return pl.pallas_call(
        functools.partial(finish_kernel, len(lows)),
        grid=(columns // part,),
        out_shape=jax.ShapeDtypeStruct((rows, columns), BF16),
        in_specs=[
            pl.BlockSpec(memory_space=pltpu.SMEM),
            pl.BlockSpec((rows, 1), lambda n: (0, 0)),
            pl.BlockSpec((rows, part), lambda n: (0, n)),
            pl.BlockSpec((depth, part), lambda n: (0, n)),
        ] + [pl.BlockSpec((rows, rank_part), lambda n: (0, 0))] * len(lows),
        out_specs=pl.BlockSpec((rows, part), lambda n: (0, n)),
        scratch_shapes=[pltpu.VMEM((rows, depth), BF16)],
        compiler_params=PARAMS,
        cost_estimate=pl.CostEstimate(
            flops=2 * rows * depth * columns,
            bytes_accessed=6 * rows * columns + 2 * depth * columns,
            transcendentals=0,
        ),
    )(me, entry, total, up, *lows)


def local(
    attention_result,
    output_weight,
    adapter_down_weight,
    adapter_up_weight,
    adapter_page_row,
    requests,
    row_request_entry,
    ranks,
):
    n_dp = lax.axis_size("dp")
    n_tensor = lax.axis_size("tensor")
    dp = lax.axis_index("dp")
    me = lax.axis_index("tensor")
    rows, width = attention_result.shape
    holder_length, rank_part, _ = adapter_down_weight.shape
    rank, columns = adapter_up_weight.shape[1:]
    own_list = requests[0]
    entries = own_list.shape[0]
    pages = adapter_page_row[own_list]
    places = ((pages // holder_length) ^ dp) * holder_length + pages % holder_length
    one_hot = row_request_entry[:, None] == jnp.arange(entries)[None, :]
    row_rank = jnp.sum(jnp.where(one_hot, ranks[own_list][None, :], 0), axis=1)

    if width % 512 or rank_part % 16:
        return plain(
            attention_result, output_weight, adapter_down_weight, adapter_up_weight, places, one_hot, row_rank
        )

    chunks = 4
    features = width // chunks
    gathered = [
        lax.all_gather(attention_result[:, k * features:(k + 1) * features], "tensor", axis=0)
        for k in range(chunks)
    ]
    weight = output_weight.reshape(n_tensor, width, columns)
    down_blocks = gather_pages(adapter_down_weight, n_dp)
    up_own = lax.optimization_barrier((adapter_up_weight, down_blocks[n_dp // 2]))[0]
    up_blocks = gather_pages(up_own, n_dp)
    down = pick_pages(places, down_blocks).reshape(entries * rank_part, -1)
    up = pick_pages(places, up_blocks).reshape(entries * rank, columns)

    entry = row_request_entry[:, None]
    live = row_rank[:, None] - me * rank_part
    base = low = None
    for k in range(chunks):
        ends = dict(entry=entry, live=live) if k == chunks - 1 else {}
        low = add_low(low, gathered[k], down, k, chunks, rank_part, **ends)
        base = add_base(base, gathered[k], weight, k)
    lows = [low] + [
        lax.ppermute(low, "tensor", [(i, (i - j) % n_tensor) for i in range(n_tensor)])
        for j in range(1, n_tensor)
    ]
    return finish(me[None], entry, base, up, lows)


def plain(attention_result, output_weight, adapter_down_weight, adapter_up_weight, places, one_hot, row_rank):
    n_dp = lax.axis_size("dp")
    rows = attention_result.shape[0]
    rank, columns = adapter_up_weight.shape[1:]
    entries = one_hot.shape[1]

    def requested(block):
        every = jnp.concatenate(gather_pages(block, n_dp), axis=0)
        return jnp.concatenate(
            [lax.dynamic_slice_in_dim(every, places[e], 1, 0) for e in range(entries)], axis=0
        )

    down, up = requested(adapter_down_weight), requested(adapter_up_weight)
    x = lax.all_gather(attention_result, "tensor", axis=1, tiled=True)
    base = jnp.dot(x, output_weight, preferred_element_type=F32)
    low = jnp.einsum("rd,ekd->rek", x, down, preferred_element_type=F32)
    low = jnp.sum(jnp.where(one_hot[:, :, None], low, 0.0), axis=1).astype(BF16)
    low = lax.all_gather(low, "tensor", axis=1, tiled=True)
    low = jnp.where(jnp.arange(rank)[None, :] < row_rank[:, None], low, jnp.zeros_like(low))
    spread = jnp.where(one_hot[:, :, None], low[:, None, :], jnp.zeros((), BF16))
    term = jnp.dot(
        spread.reshape(rows, entries * rank), up.reshape(entries * rank, columns), preferred_element_type=F32
    )
    return (base + term).astype(BF16)


def solution(mesh):
    in_specs = (
        P(("groups", "dp"), "tensor"),
        P(None, "tensor"),
        P("dp", "tensor", None),
        P("dp", None, "tensor"),
        P("groups"),
        P(("groups", "dp"), None),
        P(("groups", "dp")),
        P(),
    )
    out_specs = P(("groups", "dp"), "tensor")
    return jax.shard_map(local, mesh=mesh, in_specs=in_specs, out_specs=out_specs, check_vma=False)
```

time: 281 us -> 400 us (1.42)
  Pallas kernels: 0 us -> 235 us
  matrix products: 93.3 us -> 0 us
  waiting for transfers between devices: 64.8 us -> 109 us
  blocking collectives: 32.9 us -> 0 us
  other arithmetic: 22.3 us -> 0.63 us
  starting transfers between devices: 23.9 us -> 8.63 us
    pallas_call x0 -> x11, Pallas kernels: none -> 235 us  [the longest x2 194 us: pick_pages(): pl.pallas_call(functools.partial(pick_kernel, length), out_shape=jax.Shap...]
    dot_general x26 -> x0, matrix products: 93.3 us -> none  [the longest x12 79.8 us: add(): jnp.dot(features, weight, preferred_element_type=jnp.float32)]
    all_gather x2 -> x0, blocking collectives: 32.9 us -> none  [local(): low_full = lax.all_gather(low_mine, 'tensor', axis=1, tiled=True)]
    ppermute x14 -> x9, waiting for transfers between devices: 64.8 us -> 89.9 us  [the longest x6 89.9 us: gather_pages(): lax.ppermute(b, 'dp', pairs)]
    another operation x4 -> x0, other arithmetic: 19.8 us -> none  [gather_pages(): held = jnp.stack([held, lax.ppermute(held, 'dp', pairs)], axis=1)]
    all_gather x0 -> x4, waiting for transfers between devices: none -> 17.3 us  [local(): lax.all_gather(attention_result[:, k * features:(k + 1) * features], 'ten...]
    ppermute x14 -> x9, starting transfers between devices: 23.9 us -> 8.51 us  [the longest x6 5.39 us: gather_pages(): lax.ppermute(b, 'dp', pairs)]
    unnamed x68 -> x54, local copies, waits for them, and re-layouts: 14.7 us -> 27.7 us
  transfers between devices with their start and end apart: 14 -> 13, of which waited for: 5 -> 3; matrix products, arithmetic and copies ran while one was open for 32% -> 1% of each run, Pallas kernels for 0% -> 58%
where the time goes in v2:
time: 400 us; the launch traced here: 399 us
  Pallas kernels  235 us (59%)
  waiting for transfers between devices  109 us (27%)
  local copies, waits for them, and re-layouts  32.9 us (8%)
  between operations  13.4 us (3%)
  starting transfers between devices  8.63 us (2%)
    pallas_call x2, Pallas kernels, pick_pages(): pl.pallas_call(functools.partial(pick_kernel, length), out_shape=jax.Shap...  194 us
    ppermute x6, waiting for transfers between devices, gather_pages(): lax.ppermute(b, 'dp', pairs)  89.9 us
    pallas_call x4, Pallas kernels, add_base(): pl.pallas_call(functools.partial(base_kernel, bool(held)), grid=(shards,)...  29.7 us
    unnamed x54, local copies, waits for them, and re-layouts  27.7 us
    all_gather x4, waiting for transfers between devices, local(): lax.all_gather(attention_result[:, k * features:(k + 1) * features], 'ten...  17.3 us
  transfers between devices with their start and end apart: 13, of which 3 were waited for; matrix products, arithmetic and copies ran while one was open for 1% of the time, Pallas kernels for 58%

profile of v2, /device:TPU:0, one launch (start us, length us, event | category | flops | bytes accessed | tf_op | source)
XLA Modules:
  0.0 399.2 jit_solution(9511795605039332458)
XLA Ops:
  6.5 2.9 fusion.2
  9.5 0.7 all-gather.13.cloned.1.call-update
  10.3 0.7 all-gather.11.cloned.1.call-update
  11.0 3.0 collective-permute-start
  14.0 45.9 %collective-permute-done.refs_2_ = bf16[4,32,8192]{2,1,0:T(8,128)(2,1)} collective-permute-done((bf16[4,32,8192]{2,1,0:T(8,128)(2,1)}, bf16[4,32,8192]{2,1,0:T(8,128)(2,1)}, u32[]{:S(2)}, u32[]{:S(2)}) %collective-permute-start) | collective-permute-done | bytes 2097184 | tf_op jit(solution)/shard_map/ppermute | solution.py:20
  60.0 1.7 collective-permute-start.2
  61.8 0.5 collective-permute-start.5
  62.3 0.6 gather_fusion.1
  63.0 0.1 select_reduce_fusion
  63.1 0.1 collective-permute-start.1
  63.2 43.9 %collective-permute-done.2.refs_2_ = bf16[4,128,2048]{2,1,0:T(8,128)(2,1)} collective-permute-done((bf16[4,128,2048]{2,1,0:T(8,128)(2,1)}, bf16[4,128,2048]{2,1,0:T(8,128)(2,1)}, u32[]{:S(2)}, u32[]{:S(2)}) %collective-permute-start.2) | collective-permute-done | bytes 2097184 | tf_op jit(solution)/shard_map/ppermute | solution.py:20
  107.1 0.6 gather_fusion
  107.8 0.9 copy.13.refs_2_
  108.6 0.1 copy.14.refs_1_.entry
  108.8 0.5 fusion.places
  109.3 1.6 copy-done.13
  110.9 7.5 %shard_map.82.refs_0_ = f32[512,2048]{1,0:T(8,128)S(1)} custom-call(bf16[4,512,512]{2,1,0:T(8,128)(2,1)S(1)} %bitcast.19, bf16[4,2048,2048]{2,1,0:T(8,128)(2,1)} %bitcast.27), custom_call_target="tpu_custom_call" | custom-call | flops 4294967296 | bytes 18874368 | tf_op jit(solution)/shard_map/pallas_call | solution.py:70
  118.4 1.9 copy-done.6
  120.4 2.2 copy-done.7
  122.6 1.6 copy-done.15
  124.2 7.4 %shard_map.83.refs_0_ = f32[512,2048]{1,0:T(8,128)S(1)} custom-call(bf16[4,512,512]{2,1,0:T(8,128)(2,1)S(1)} %bitcast.21, bf16[4,2048,2048]{2,1,0:T(8,128)(2,1)} %bitcast.28, f32[512,2048]{1,0:T(8,128)S(1)} %copy-done.7), custom_call_target="tpu_custom_call" | custom-call | flops 4294967296 | bytes 18874368 | tf_op jit(solution)/shard_map/pallas_call | solution.py:70
  131.6 1.9 copy-done.10
  133.5 17.3 %all-gather.11.cloned.1.call-done = bf16[2048,512]{1,0:T(8,128)(2,1)} async-done(((bf16[512,512]{1,0:T(8,128)(2,1)}), bf16[2048,512]{1,0:T(8,128)(2,1)}) %all-gather.11.cloned.1.call-update) | async-done | bytes 2097168 | tf_op jit(solution)/shard_map/all_gather | solution.py:214
  150.8 2.2 copy-done.11
  153.0 1.6 copy-done.19
  154.6 7.5 %shard_map.84.refs_0_ = f32[512,2048]{1,0:T(8,128)S(1)} custom-call(bf16[4,512,512]{2,1,0:T(8,128)(2,1)S(1)} %bitcast.25, bf16[4,2048,2048]{2,1,0:T(8,128)(2,1)} %bitcast.29, f32[512,2048]{1,0:T(8,128)S(1)} %copy-done.11), custom_call_target="tpu_custom_call" | custom-call | flops 4294967296 | bytes 18874368 | tf_op jit(solution)/shard_map/pallas_call | solution.py:70
  162.1 1.9 copy-done.8
  164.1 97.3 %shard_map.87 = bf16[6,32,8192]{2,1,0:T(8,128)(2,1)} custom-call(s32[6]{0:T(128)} %fusion.places, bf16[4,32,8192]{2,1,0:T(8,128)(2,1)} %refs_0_.2, bf16[4,32,8192]{2,1,0:T(8,128)(2,1)} %collective-permute-done.4.refs_1_, bf16[4,32,8192]{2,1,0:T(8,128)(2,1)} %collective-permute-done.refs_2_, bf16[4,32,8192]{2,1,0:T(8,128)(2,1)} %collective-permute-done.5.refs_3_), custom_call_target="tpu_custom_call" | custom-call | bytes 6291456 | tf_op jit(solution)/shard_map/pallas_call | solution.py:42
  261.4 1.9 copy-done.2
  263.3 1.4 shard_map.88.refs_0_
  264.7 0.2 copy-done.16
  264.9 1.4 shard_map.89.refs_0_
  266.3 0.2 copy-done.20
  266.4 1.4 shard_map.90.refs_0_
  267.9 0.8 copy-done.21
  268.7 1.6 copy-done.17
  270.3 1.0 copy-done.22
  271.3 0.9 copy-done.23
  272.3 2.3 shard_map.91.refs_0_
  274.5 1.1 collective-permute-start.6
  275.7 0.2 collective-permute-start.7
  275.9 1.8 collective-permute-start.8
  277.7 7.3 %shard_map.85.total = f32[512,2048]{1,0:T(8,128)S(1)} custom-call(bf16[4,512,512]{2,1,0:T(8,128)(2,1)S(1)} %bitcast.24, bf16[4,2048,2048]{2,1,0:T(8,128)(2,1)} %bitcast.30, f32[512,2048]{1,0:T(8,128)S(1)} %copy-done.9), custom_call_target="tpu_custom_call" | custom-call | flops 4294967296 | bytes 18874368 | tf_op jit(solution)/shard_map/pallas_call | solution.py:70
  285.0 1.9 copy-done.4
  287.0 97.2 %shard_map.86 = bf16[6,128,2048]{2,1,0:T(8,128)(2,1)} custom-call(s32[6]{0:T(128)} %fusion.places, bf16[4,128,2048]{2,1,0:T(8,128)(2,1)} %refs_0_.1, bf16[4,128,2048]{2,1,0:T(8,128)(2,1)} %collective-permute-done.1.refs_1_, bf16[4,128,2048]{2,1,0:T(8,128)(2,1)} %collective-permute-done.2.refs_2_, bf16[4,128,2048]{2,1,0:T(8,128)(2,1)} %collective-permute-done.3.refs_3_), custom_call_target="tpu_custom_call" | custom-call | bytes 6291456 | tf_op jit(solution)/shard_map/pallas_call | solution.py:42
  384.2 2.2 copy-done.5
  386.4 1.9 copy-done.12
  388.3 4.4 %shard_map.92 = bf16[512,2048]{1,0:T(8,128)(2,1)} custom-call(s32[1]{0:T(128)} %bitcast.me, s32[512,1]{1,0:T(8,128)S(1)} %copy.14.refs_1_.entry, f32[512,2048]{1,0:T(8,128)S(1)} %copy-done.5, bf16[768,2048]{1,0:T(8,128)(2,1)S(1)} %bitcast.18, bf16[512,32]{1,0:T(8,128)(2,1)S(1)} %shard_map.91.refs_0_, bf16[512,32]{1,0:T(8,128)(2,1)S(1)} %collective-permute-done.6.refs_1_, ...), custom_call_target="tpu_custom_call" | custom-call | flops 1610612736 | bytes 9437184 | tf_op jit(solution)/shard_map/pallas_call | solution.py:161
  (57 shorter events, 0.3 us)
Async XLA Ops:
  6.5 55.8 %copy-start = (s32[16]{0:T(128)S(1)}, s32[16]{0:T(128)}, u32[]{:S(2)}) copy-start(s32[16]{0:T(128)} %param.15) | copy-start | bytes 196
  6.5 102.8 %all-gather.15.cloned.1.call-start = ((), (), s32[]{:S(2)}) async-start(), calls=%async_computation.3 | async-start | bytes 2621440 | tf_op jit(solution)/shard_map/all_gather | solution.py:214
  9.5 52.9 %copy-start.26 = (s32[1,6]{1,0:T(1,128)S(1)}, s32[1,6]{1,0:T(1,128)}, u32[]{:S(2)}) copy-start(s32[1,6]{1,0:T(1,128)} %param.13) | copy-start | bytes 76
  9.5 53.5 %copy-start.25 = (s32[512]{0:T(512)S(1)}, s32[512]{0:T(512)}, u32[]{:S(2)}) copy-start(s32[512]{0:T(512)} %param.14) | copy-start | bytes 6148
  9.5 97.7 %copy-start.24 = (s32[16]{0:T(128)S(1)}, s32[16]{0:T(128)}, u32[]{:S(2)}) copy-start(s32[16]{0:T(128)} %param.12) | copy-start | bytes 196
  9.5 110.9 %all-gather.13.cloned.1.call-start = ((), (), s32[]{:S(2)}) async-start(), calls=%async_computation.2 | async-start | bytes 2621440 | tf_op jit(solution)/shard_map/all_gather | solution.py:214
  10.2 140.6 %all-gather.11.cloned.1.call-start = ((), (), s32[]{:S(2)}) async-start(), calls=%async_computation.1 | async-start | bytes 2621440 | tf_op jit(solution)/shard_map/all_gather | solution.py:214
  11.0 257.7 %all-gather.9.cloned.1.call-start = ((), (), s32[]{:S(2)}) async-start(), calls=%async_computation | async-start | bytes 2621440 | tf_op jit(solution)/shard_map/all_gather | solution.py:214
  11.0 49.0 %collective-permute-start = (bf16[4,32,8192]{2,1,0:T(8,128)(2,1)}, bf16[4,32,8192]{2,1,0:T(8,128)(2,1)}, u32[]{:S(2)}, u32[]{:S(2)}) collective-permute-start(bf16[4,32,8192]{2,1,0:T(8,128)(2,1)} %refs_0_.2), channel_id=1, source_target_pairs={{0,2},{1,3},{2,0},{3,1},{4,6},{5,7},{6,4},{7,5},{8,10},{9,11},{10,... | collective-permute-start | bytes 6291464 | tf_op jit(solution)/shard_map/ppermute | solution.py:20
  60.0 47.1 %collective-permute-start.2 = (bf16[4,128,2048]{2,1,0:T(8,128)(2,1)}, bf16[4,128,2048]{2,1,0:T(8,128)(2,1)}, u32[]{:S(2)}, u32[]{:S(2)}) collective-permute-start(bf16[4,128,2048]{2,1,0:T(8,128)(2,1)} %refs_0_.1), channel_id=1, source_target_pairs={{0,2},{1,3},{2,0},{3,1},{4,6},{5,7},{6,4},{7,5},{8,10},{9,11},{10,... | collective-permute-start | bytes 6291464 | tf_op jit(solution)/shard_map/ppermute | solution.py:20
  61.7 102.3 %collective-permute-start.4 = (bf16[4,32,8192]{2,1,0:T(8,128)(2,1)}, bf16[4,32,8192]{2,1,0:T(8,128)(2,1)}, u32[]{:S(2)}, u32[]{:S(2)}) collective-permute-start(bf16[4,32,8192]{2,1,0:T(8,128)(2,1)} %refs_0_.2), channel_id=1, source_target_pairs={{0,1},{1,0},{2,3},{3,2},{4,5},{5,4},{6,7},{7,6},{8,9},{9,8},{10,11... | collective-permute-start | bytes 6291464 | tf_op jit(solution)/shard_map/ppermute | solution.py:20
  61.8 102.2 %collective-permute-start.5 = (bf16[4,32,8192]{2,1,0:T(8,128)(2,1)}, bf16[4,32,8192]{2,1,0:T(8,128)(2,1)}, u32[]{:S(2)}, u32[]{:S(2)}) collective-permute-start(bf16[4,32,8192]{2,1,0:T(8,128)(2,1)} %collective-permute-done.refs_2_), channel_id=1, source_target_pairs={{0,1},{1,0},{2,3},{3,2},{4,5},{5,4},{6,7},{7,6},{8,9},{9,8},{10,11... | collective-permute-start | bytes 6291464 | tf_op jit(solution)/shard_map/ppermute | solution.py:20
  63.1 223.9 %collective-permute-start.1 = (bf16[4,128,2048]{2,1,0:T(8,128)(2,1)}, bf16[4,128,2048]{2,1,0:T(8,128)(2,1)}, u32[]{:S(2)}, u32[]{:S(2)}) collective-permute-start(bf16[4,128,2048]{2,1,0:T(8,128)(2,1)} %refs_0_.1), channel_id=1, source_target_pairs={{0,1},{1,0},{2,3},{3,2},{4,5},{5,4},{6,7},{7,6},{8,9},{9,8},{10,11... | collective-permute-start | bytes 6291464 | tf_op jit(solution)/shard_map/ppermute | solution.py:20
  107.1 179.9 %collective-permute-start.3 = (bf16[4,128,2048]{2,1,0:T(8,128)(2,1)}, bf16[4,128,2048]{2,1,0:T(8,128)(2,1)}, u32[]{:S(2)}, u32[]{:S(2)}) collective-permute-start(bf16[4,128,2048]{2,1,0:T(8,128)(2,1)} %collective-permute-done.2.refs_2_), channel_id=1, source_target_pairs={{0,1},{1,0},{2,3},{3,2},{4,5},{5,4},{6,7},{7,6},{8,9},{9,8},{10,11... | collective-permute-start | bytes 6291464 | tf_op jit(solution)/shard_map/ppermute | solution.py:20
  109.3 1.6 copy-start.13
  118.4 2.0 copy-start.6
  120.4 2.2 copy-start.7
  122.6 1.6 copy-start.15
  131.6 2.0 copy-start.10
  150.8 2.2 copy-start.11
  153.0 1.6 copy-start.19
  162.1 2.0 copy-start.8
  164.1 97.3 %copy-start.14 = (bf16[2048,512]{1,0:T(8,128)(2,1)S(1)}, bf16[2048,512]{1,0:T(8,128)(2,1)}, u32[]{:S(2)}) copy-start(bf16[2048,512]{1,0:T(8,128)(2,1)} %all-gather.15.cloned.1.call-done) | copy-start | bytes 6291460
  261.4 1.9 copy-start.2
  263.3 1.6 copy-start.16
  264.9 1.6 copy-start.20
  266.4 2.2 copy-start.3
  267.9 0.8 copy-start.21
  268.7 1.6 copy-start.17
  270.3 1.0 copy-start.22
  271.3 0.9 copy-start.23
  272.3 5.4 %copy-start.9 = (f32[512,2048]{1,0:T(8,128)S(1)}, f32[512,2048]{1,0:T(8,128)}, u32[]{:S(2)}) copy-start(f32[512,2048]{1,0:T(8,128)} %copy-done.8) | copy-start | bytes 12582916
  272.3 5.4 %copy-start.18 = (bf16[2048,512]{1,0:T(8,128)(2,1)S(1)}, bf16[2048,512]{1,0:T(8,128)(2,1)}, u32[]{:S(2)}) copy-start(bf16[2048,512]{1,0:T(8,128)(2,1)} %all-gather.9.cloned.1.call-done) | copy-start | bytes 6291460
  274.5 109.6 %collective-permute-start.6 = (bf16[512,32]{1,0:T(8,128)(2,1)S(1)}, bf16[512,32]{1,0:T(8,128)(2,1)S(1)}, u32[]{:S(2)}, u32[]{:S(2)}) collective-permute-start(bf16[512,32]{1,0:T(8,128)(2,1)S(1)} %shard_map.91.refs_0_), channel_id=1, source_target_pairs={{0,12},{4,0},{8,4},{12,8},{1,13},{5,1},{9,5},{13,9},{2,14},{6,2},{... | collective-permute-start | bytes 98312 | tf_op jit(solution)/shard_map/ppermute | solution.py:232
  275.7 108.5 %collective-permute-start.7 = (bf16[512,32]{1,0:T(8,128)(2,1)S(1)}, bf16[512,32]{1,0:T(8,128)(2,1)S(1)}, u32[]{:S(2)}, u32[]{:S(2)}) collective-permute-start(bf16[512,32]{1,0:T(8,128)(2,1)S(1)} %shard_map.91.refs_0_), channel_id=1, source_target_pairs={{0,8},{4,12},{8,0},{12,4},{1,9},{5,13},{9,1},{13,5},{2,10},{6,14},... | collective-permute-start | bytes 98312 | tf_op jit(solution)/shard_map/ppermute | solution.py:232
  275.9 108.3 %collective-permute-start.8 = (bf16[512,32]{1,0:T(8,128)(2,1)S(1)}, bf16[512,32]{1,0:T(8,128)(2,1)S(1)}, u32[]{:S(2)}, u32[]{:S(2)}) collective-permute-start(bf16[512,32]{1,0:T(8,128)(2,1)S(1)} %shard_map.91.refs_0_), channel_id=1, source_target_pairs={{0,4},{4,8},{8,12},{12,0},{1,5},{5,9},{9,13},{13,1},{2,6},{6,10},{... | collective-permute-start | bytes 98312 | tf_op jit(solution)/shard_map/ppermute | solution.py:232
  285.0 2.0 copy-start.4
  384.2 2.2 copy-start.5
  386.4 1.9 copy-start.12
  388.2 4.4 %copy-start.1 = (s32[16]{0:T(128)S(1)}, s32[16]{0:T(128)}, u32[]{:S(2)}) copy-start(s32[16]{0:T(128)} %param.15) | copy-start | bytes 196
Sparse Core Ops, SparseCore 0:
  9.6 48.6 all-gather.14
  59.9 44.6 all-gather.12
  106.1 44.6 all-gather.10
  152.2 44.5 all-gather.8

commit v3 on v2

v3 whole, which is shorter than its diff:
```python
import functools

import jax
import jax.numpy as jnp
from jax import lax
from jax.experimental import pallas as pl
from jax.experimental.pallas import tpu as pltpu
from jax.sharding import PartitionSpec as P

CAP = 2
UNIT = 256
LINE = 512
GATHERED = (768, 768)
PARAMS = pltpu.CompilerParams(vmem_limit_bytes=60 * 2**20)
F32 = jnp.float32
BF16 = jnp.bfloat16


def pick_kernel(places, down, up, down_out, up_out):
    down_out[...] = down[...]
    up_out[...] = up[...]


def pick_pages(places, down, up):
    count = places.shape[0]
    blocks = [(1,) + a.shape[1:] for a in (down, up)]
    return pl.pallas_call(
        pick_kernel,
        out_shape=[jax.ShapeDtypeStruct((count,) + a.shape[1:], BF16) for a in (down, up)],
        grid_spec=pltpu.PrefetchScalarGridSpec(
            num_scalar_prefetch=1,
            grid=(count,),
            in_specs=[pl.BlockSpec(b, lambda i, places: (places[i], 0, 0)) for b in blocks],
            out_specs=[pl.BlockSpec(b, lambda i, places: (i, 0, 0)) for b in blocks],
        ),
        compiler_params=PARAMS,
    )(places, down, up)


def steps_of(xs):
    return sum(x.shape[0] for x in xs)


def x_specs(xs):
    specs, first = [], 0
    for x in xs:
        units = x.shape[2] // UNIT

        def index(s, j, *_, first=first, count=x.shape[0], units=units):
            shard = jnp.clip(s - first, 0, count - 1)
            return shard, 0, jnp.where(s < first, 0, jnp.where(s >= first + count, units - 1, j))

        specs.append(pl.BlockSpec((1, x.shape[1], UNIT), index))
        first += x.shape[0]
    return specs


def for_block(xs, counts, valid, body):
    s, first = pl.program_id(0), 0
    for x, count in zip(xs, counts):

        @pl.when((s >= first) & (s < first + count) & (valid[s] != 0))
        def _():
            body(x[0])

        first += count


def start_total(out, total):
    @pl.when((pl.program_id(0) == 0) & (pl.program_id(1) == 0))
    def _():
        out[...] = jnp.zeros_like(out) if total is None else total[...]


def base_kernel(counts, has_total, source, valid, *refs):
    xs, weight, out = refs[:len(counts)], refs[len(counts)], refs[-1]
    start_total(out, refs[-2] if has_total else None)
    columns = out.shape[1]
    part = min(columns, 512)

    def body(x):
        for n in range(0, columns, part):
            out[:, n:n + part] += jnp.dot(x, weight[0, :, n:n + part], preferred_element_type=F32)

    for_block(xs, counts, valid, body)


def add_base(total, xs, source, valid, offset, weight):
    rows, features = xs[0].shape[1:]
    columns = weight.shape[-1]
    held = [] if total is None else [total]
    whole = pl.BlockSpec((rows, columns), lambda s, j, *_: (0, 0))
    steps = steps_of(xs)
    return pl.pallas_call(
        functools.partial(base_kernel, [x.shape[0] for x in xs], bool(held)),
        out_shape=jax.ShapeDtypeStruct((rows, columns), F32),
        grid_spec=pltpu.PrefetchScalarGridSpec(
            num_scalar_prefetch=2,
            grid=(steps, features // UNIT),
            in_specs=x_specs(xs) + [
                pl.BlockSpec((1, UNIT, columns), lambda s, j, source, valid: (source[s], offset // UNIT + j, 0))
            ] + [whole] * len(held),
            out_specs=whole,
        ),
        compiler_params=PARAMS,
        cost_estimate=pl.CostEstimate(
            flops=2 * steps * rows * features * columns,
            bytes_accessed=2 * steps * features * (rows + columns) + 8 * rows * columns,
            transcendentals=0,
        ),
    )(source, valid, *xs, weight, *held)


def low_kernel(counts, parts, has_total, last, rank_part, source, valid, *refs):
    refs = list(refs)
    xs = [refs.pop(0) for _ in counts]
    downs = [refs.pop(0) for _ in range(parts)]
    total = refs.pop(0) if has_total else None
    acc = refs.pop()
    start_total(acc, total)

    def body(x):
        down = jnp.concatenate([d[...] for d in downs], axis=0)
        acc[...] += lax.dot_general(x, down, (((1,), (1,)), ((), ())), preferred_element_type=F32)

    for_block(xs, counts, valid, body)
    if last:
        slot, live, out = refs

        @pl.when((pl.program_id(0) == pl.num_programs(0) - 1) & (pl.program_id(1) == pl.num_programs(1) - 1))
        def _():
            mine = jnp.zeros((acc.shape[0], rank_part), F32)
            for e in range(acc.shape[1] // rank_part):
                mine += jnp.where(slot[...] == e, acc[:, e * rank_part:(e + 1) * rank_part], 0.0)
            k = lax.broadcasted_iota(jnp.int32, mine.shape, 1)
            out[...] = jnp.where(k < live[...], mine, 0.0).astype(BF16)


def add_low(total, xs, source, valid, offset, downs, rank_part, ends=()):
    rows, features = xs[0].shape[1:]
    shard_units = downs[0].shape[1] // lax.axis_size("tensor") // UNIT
    depth = downs[0].shape[0]
    ranks = depth * len(downs)
    held = [] if total is None else [total]
    whole = pl.BlockSpec((rows, ranks), lambda s, j, *_: (0, 0))
    column = pl.BlockSpec((rows, 1), lambda s, j, *_: (0, 0))
    steps = steps_of(xs)
    down_spec = pl.BlockSpec(
        (depth, UNIT), lambda s, j, source, valid: (0, source[s] * shard_units + offset // UNIT + j)
    )
    return pl.pallas_call(
        functools.partial(low_kernel, [x.shape[0] for x in xs], len(downs), bool(held), bool(ends), rank_part),
        out_shape=jax.ShapeDtypeStruct((rows, rank_part), BF16) if ends else jax.ShapeDtypeStruct((rows, ranks), F32),
        grid_spec=pltpu.PrefetchScalarGridSpec(
            num_scalar_prefetch=2,
            grid=(steps, features // UNIT),
            in_specs=x_specs(xs) + [down_spec] * len(downs) + [whole] * len(held) + [column] * len(ends),
            out_specs=pl.BlockSpec((rows, rank_part), lambda s, j, *_: (0, 0)) if ends else whole,
            scratch_shapes=[pltpu.VMEM((rows, ranks), F32)] if ends else [],
        ),
        compiler_params=PARAMS,
        cost_estimate=pl.CostEstimate(
            flops=2 * steps * rows * features * ranks,
            bytes_accessed=2 * steps * features * (rows + ranks) + 8 * rows * ranks,
            transcendentals=0,
        ),
    )(source, valid, *xs, *downs, *held, *ends)


def finish_kernel(parts, holders, me, slot, total, *refs):
    lows, ups, (out, spread) = refs[:parts], refs[parts:parts + holders], refs[parts + holders:]
    rank_part = lows[0].shape[1]
    rank = parts * rank_part
    depth = ups[0].shape[0]

    @pl.when(pl.program_id(0) == 0)
    def _():
        low = jnp.concatenate([part[...].astype(F32) for part in lows], axis=1)
        low = pltpu.roll(low, me[0] * rank_part, 1)
        for e in range(spread.shape[1] // rank):
            spread[:, e * rank:(e + 1) * rank] = jnp.where(slot[...] == e, low, 0.0).astype(BF16)

    term = total[...]
    for j, up in enumerate(ups):
        term += jnp.dot(spread[:, j * depth:(j + 1) * depth], up[...], preferred_element_type=F32)
    out[...] = term.astype(BF16)


def finish(me, slot, total, ups, lows):
    rows, columns = total.shape
    depth = ups[0].shape[0]
    rank_part = lows[0].shape[1]
    part = min(columns, 512)
    return pl.pallas_call(
        functools.partial(finish_kernel, len(lows), len(ups)),
        grid=(columns // part,),
        out_shape=jax.ShapeDtypeStruct((rows, columns), BF16),
        in_specs=[
            pl.BlockSpec(memory_space=pltpu.SMEM),
            pl.BlockSpec((rows, 1), lambda n: (0, 0)),
            pl.BlockSpec((rows, part), lambda n: (0, n)),
        ] + [pl.BlockSpec((rows, rank_part), lambda n: (0, 0))] * len(lows)
        + [pl.BlockSpec((depth, part), lambda n: (0, n))] * len(ups),
        out_specs=pl.BlockSpec((rows, part), lambda n: (0, n)),
        scratch_shapes=[pltpu.VMEM((rows, depth * len(ups)), BF16)],
        compiler_params=PARAMS,
        cost_estimate=pl.CostEstimate(
            flops=2 * rows * depth * len(ups) * columns,
            bytes_accessed=6 * rows * columns + 2 * depth * len(ups) * columns,
            transcendentals=0,
        ),
    )(me, slot, total, *lows, *ups)


def after(value, *earlier):
    return lax.optimization_barrier((value,) + earlier)[0]


def asked_pages(requests, adapter_page_row, holder_length):
    n_dp = lax.axis_size("dp")
    dp = lax.axis_index("dp")
    count = adapter_page_row.shape[0]

    def pages_of(wanted):
        hit = wanted[:, None] == jnp.arange(count)[None, :]
        return jnp.sum(jnp.where(hit, adapter_page_row[None, :], 0), axis=1)

    def order_in(holders):
        same = holders[:, None] == holders[None, :]
        n = holders.shape[0]
        earlier = jnp.arange(n)[:, None] > jnp.arange(n)[None, :]
        return jnp.sum((same & earlier).astype(jnp.int32), axis=1)

    own = pages_of(requests[0])
    holders = own // holder_length
    slots = (holders ^ dp) * CAP + order_in(holders)
    places = []
    for j in range(n_dp):
        wanted = requests if j == 0 else lax.ppermute(requests, "dp", [(i, i ^ j) for i in range(n_dp)])
        pages = pages_of(wanted[0])
        holder = pages // holder_length
        order = jnp.where(holder == dp, order_in(holder), -1)
        hit = order[None, :] == jnp.arange(CAP)[:, None]
        places.append(jnp.sum(jnp.where(hit, (pages % holder_length)[None, :], 0), axis=1))
    return slots, places


def local(
    attention_result,
    output_weight,
    adapter_down_weight,
    adapter_up_weight,
    adapter_page_row,
    requests,
    row_request_entry,
    ranks,
):
    n_dp = lax.axis_size("dp")
    n_tensor = lax.axis_size("tensor")
    me = lax.axis_index("tensor")
    rows, width = attention_result.shape
    holder_length, rank_part, _ = adapter_down_weight.shape
    rank, columns = adapter_up_weight.shape[1:]
    own_list = requests[0]
    entries = own_list.shape[0]
    one_hot = row_request_entry[:, None] == jnp.arange(entries)[None, :]
    row_rank = jnp.sum(jnp.where(one_hot, ranks[own_list][None, :], 0), axis=1)
    if n_tensor != 4 or width != LINE + sum(GATHERED) or rank_part % 16:
        return plain(
            attention_result, output_weight, adapter_down_weight, adapter_up_weight, adapter_page_row,
            own_list, one_hot, row_rank,
        )

    weight = output_weight.reshape(n_tensor, width, columns)
    every = jnp.arange(n_tensor, dtype=jnp.int32)
    ones = jnp.ones((n_tensor,), jnp.int32)

    gathered, offsets, offset = [], [], LINE
    for features in GATHERED:
        gathered.append(lax.all_gather(attention_result[:, offset:offset + features], "tensor", axis=0))
        offsets.append(offset)
        offset += features

    line = attention_result[None, :, :LINE]
    right = [(i, i + 1) for i in range(n_tensor - 1)]
    left = [(i + 1, i) for i in range(n_tensor - 1)]
    right_1 = lax.ppermute(line, "tensor", right)
    left_1 = lax.ppermute(line, "tensor", left)

    slots, places = asked_pages(requests, adapter_page_row, holder_length)
    downs, ups = [], []
    for j in range(n_dp):
        down, up = pick_pages(places[j], adapter_down_weight, adapter_up_weight)
        if j:
            pairs = [(i, i ^ j) for i in range(n_dp)]
            down, up = lax.ppermute(down, "dp", pairs), lax.ppermute(up, "dp", pairs)
        downs.append(down.reshape(CAP * rank_part, -1))
        ups.append(up.reshape(CAP * rank, columns))

    right_2 = lax.ppermute(right_1, "tensor", right[1:])
    left_2 = lax.ppermute(left_1, "tensor", left[:-1])
    upper = me >= n_tensor // 2
    second = jnp.where(upper, right_2, left_2)
    third = lax.ppermute(second, "tensor", right[-1:] + left[:1])

    near = jnp.stack([me, me - 1, me + 1])
    far = jnp.where(upper, jnp.stack([me - 2, me - 3]), jnp.stack([me + 2, me + 3]))
    xs = [
        ([line, right_1, left_1], near, 0),
        ([second, third], far, 0),
        ([gathered[0]], every, offsets[0]),
        ([gathered[1]], every, offsets[1]),
    ]
    base = low = None
    slot = jnp.sum(jnp.where(one_hot, slots[None, :], 0), axis=1)[:, None]
    live = row_rank[:, None] - me * rank_part
    for i, (blocks, source, start) in enumerate(xs):
        valid = ((source >= 0) & (source < n_tensor)).astype(jnp.int32)
        source = jnp.clip(source, 0, n_tensor - 1).astype(jnp.int32)
        ends = (slot, live) if i == len(xs) - 1 else ()
        if ends:
            blocks = [after(blocks[0], base, low)]
        low = add_low(low, blocks, source, valid, start, downs, rank_part, ends)
        base = add_base(base, blocks, source, valid, start, weight)
    lows = [low] + [
        lax.ppermute(low, "tensor", [(i, (i - j) % n_tensor) for i in range(n_tensor)])
        for j in range(1, n_tensor)
    ]
    return finish(me[None], slot, base, ups, lows)


def gather_pages(block, n_dp):
    return [block] + [
        lax.ppermute(block, "dp", [(i, i ^ j) for i in range(n_dp)]) for j in range(1, n_dp)
    ]


def plain(x, output_weight, down_weight, up_weight, adapter_page_row, own_list, one_hot, row_rank):
    n_dp = lax.axis_size("dp")
    dp = lax.axis_index("dp")
    rows = x.shape[0]
    holder_length = down_weight.shape[0]
    rank, columns = up_weight.shape[1:]
    entries = one_hot.shape[1]
    pages = adapter_page_row[own_list]
    places = ((pages // holder_length) ^ dp) * holder_length + pages % holder_length

    def requested(block):
        blocks = jnp.concatenate(gather_pages(block, n_dp), axis=0)
        return jnp.concatenate(
            [lax.dynamic_slice_in_dim(blocks, places[e], 1, 0) for e in range(entries)], axis=0
        )

    down, up = requested(down_weight), requested(up_weight)
    x = lax.all_gather(x, "tensor", axis=1, tiled=True)
    base = jnp.dot(x, output_weight, preferred_element_type=F32)
    low = jnp.einsum("rd,ekd->rek", x, down, preferred_element_type=F32)
    low = jnp.sum(jnp.where(one_hot[:, :, None], low, 0.0), axis=1).astype(BF16)
    low = lax.all_gather(low, "tensor", axis=1, tiled=True)
    low = jnp.where(jnp.arange(rank)[None, :] < row_rank[:, None], low, jnp.zeros_like(low))
    spread = jnp.where(one_hot[:, :, None], low[:, None, :], jnp.zeros((), BF16))
    term = jnp.dot(
        spread.reshape(rows, entries * rank), up.reshape(entries * rank, columns), preferred_element_type=F32
    )
    return (base + term).astype(BF16)


def solution(mesh):
    in_specs = (
        P(("groups", "dp"), "tensor"),
        P(None, "tensor"),
        P("dp", "tensor", None),
        P("dp", None, "tensor"),
        P("groups"),
        P(("groups", "dp"), None),
        P(("groups", "dp")),
        P(),
    )
    out_specs = P(("groups", "dp"), "tensor")
    return jax.shard_map(local, mesh=mesh, in_specs=in_specs, out_specs=out_specs, check_vma=False)
```

time: 400 us -> 214 us (0.54)
  Pallas kernels: 235 us -> 107 us
  waiting for transfers between devices: 109 us -> 55 us
  local copies, waits for them, and re-layouts: 32.9 us -> 8.61 us
  starting transfers between devices: 8.63 us -> 18.5 us
  other arithmetic: 0.63 us -> 9.08 us
    pallas_call x11 -> x13, Pallas kernels: 235 us -> 107 us  [the longest x4 54.6 us: add_base(): pl.pallas_call(functools.partial(base_kernel, [x.shape[0] for x in xs], b...]
    ppermute x6 -> x14, waiting for transfers between devices: 89.9 us -> 55 us  [the longest x1 30.4 us: local(): left_2 = lax.ppermute(left_1, 'tensor', left[:-1])]
    unnamed x54 -> x22, local copies, waits for them, and re-layouts: 27.7 us -> 1.72 us
    all_gather x4 -> x2, waiting for transfers between devices: 17.3 us -> 0.01 us  [local(): lax.all_gather(attention_result[:, offset:offset + features], 'tensor', a...]
    ppermute x6 -> x14, starting transfers between devices: 5.39 us -> 16.5 us  [the longest x1 4.51 us: local(): right_1 = lax.ppermute(line, 'tensor', right)]
  transfers between devices with their start and end apart: 13 -> 19, of which waited for: 3 -> 4; matrix products, arithmetic and copies ran while one was open for 1% -> 6% of each run, Pallas kernels for 58% -> 47%
where the time goes in v3:
time: 214 us; the launch traced here: 212 us
  Pallas kernels  107 us (50%)
  waiting for transfers between devices  55 us (26%)
  starting transfers between devices  18.5 us (9%)
  between operations  13.6 us (6%)
  other arithmetic  9.08 us (4%)
  local copies, waits for them, and re-layouts  8.61 us (4%)
    pallas_call x4, Pallas kernels, add_base(): pl.pallas_call(functools.partial(base_kernel, [x.shape[0] for x in xs], b...  54.6 us
    pallas_call x4, Pallas kernels, add_low(): pl.pallas_call(functools.partial(low_kernel, [x.shape[0] for x in xs], le...  31.8 us
    ppermute x1, waiting for transfers between devices, local(): left_2 = lax.ppermute(left_1, 'tensor', left[:-1])  30.4 us
    ppermute x1, waiting for transfers between devices, local(): left_1 = lax.ppermute(line, 'tensor', left)  17.4 us
    pallas_call x4, Pallas kernels, pick_pages(): pl.pallas_call(pick_kernel, out_shape=[jax.ShapeDtypeStruct((count,) + a....  13.3 us
    pallas_call x1, Pallas kernels, finish(): pl.pallas_call(functools.partial(finish_kernel, len(lows), len(ups)), gri...  7.61 us
    ppermute x1, waiting for transfers between devices, local(): third = lax.ppermute(second, 'tensor', right[-1:] + left[:1])  6.47 us
    ppermute x1, starting transfers between devices, local(): right_1 = lax.ppermute(line, 'tensor', right)  4.51 us
  transfers between devices with their start and end apart: 19, of which 4 were waited for; matrix products, arithmetic and copies ran while one was open for 6% of the time, Pallas kernels for 47%

profile of v3, /device:TPU:0, one launch (start us, length us, event | category | flops | bytes accessed | tf_op | source)
XLA Modules:
  0.0 212.1 jit_solution(5837294351563048728)
XLA Ops:
  6.5 2.6 %fusion.9 = (bf16[512,768]{1,0:T(8,128)(2,1)}, bf16[512,768]{1,0:T(8,128)(2,1)}) fusion(bf16[512,2048]{1,0:T(8,128)(2,1)} %param.8), kind=kLoop, calls=%fused_computation.68 | loop fusion | bytes 3145728 | tf_op jit(solution)/shard_map/slice | solution.py:280
  9.2 0.5 collective-permute-start.5
  9.8 2.6 %collective-permute-start.7 = (s32[1,6]{1,0:T(1,128)S(1)}, s32[1,6]{1,0:T(1,128)S(1)}, u32[]{:S(2)}, u32[]{:S(2)}) collective-permute-start(s32[1,6]{1,0:T(1,128)S(1)} %copy-done.9), channel_id=1, source_target_pairs={{0,2},{1,3},{2,0},{3,1},{4,6},{5,7},{6,4},{7,5},{8,10},{9,11},{10,... | collective-permute-start | bytes 80 | tf_op jit(solution)/shard_map/ppermute | solution.py:239
  12.4 1.9 slice_bitcast_fusion.refs_0_
  14.3 4.5 %collective-permute-start = (bf16[1,512,512]{2,1,0:T(8,128)(2,1)}, bf16[1,512,512]{2,1,0:T(8,128)(2,1)}, u32[]{:S(2)}, u32[]{:S(2)}) collective-permute-start(bf16[1,512,512]{2,1,0:T(8,128)(2,1)} %slice_bitcast_fusion.refs_0_), channel_id=1, source_target_pairs={{0,4},{4,8},{8,12},{1,5},{5,9},{9,13},{2,6},{6,10},{10,14},{3,7},{... | collective-permute-start | bytes 1572872 | tf_op jit(solution)/shard_map/ppermute | solution.py:287
  18.8 1.3 collective-permute-start.2
  20.1 0.6 compare_convert_fusion.valid
  20.7 0.6 and_convert_fusion
  21.3 0.6 and_convert_fusion.1
  22.0 0.6 iota_clamp_fusion.source
  22.5 0.6 gather_fusion
  23.2 0.6 broadcast_clamp_fusion.source
  23.7 0.5 broadcast_clamp_fusion.1.source
  24.7 0.6 fusion.6.places
  25.3 3.3 %shard_map.87 = (bf16[2,32,8192]{2,1,0:T(8,128)(2,1)}, bf16[2,128,2048]{2,1,0:T(8,128)(2,1)}) custom-call(s32[2]{0:T(128)} %fusion.6.places, bf16[4,32,8192]{2,1,0:T(8,128)(2,1)} %down.7, bf16[4,128,2048]{2,1,0:T(8,128)(2,1)} %up.7), custom_call_target="tpu_custom_call" | custom-call | tf_op jit(solution)/shard_map/pallas_call | solution.py:27
  28.6 1.5 collective-permute-start.8
  30.3 0.6 fusion.7.places
  30.9 3.3 %shard_map.88 = (bf16[2,32,8192]{2,1,0:T(8,128)(2,1)}, bf16[2,128,2048]{2,1,0:T(8,128)(2,1)}) custom-call(s32[2]{0:T(128)} %fusion.7.places, bf16[4,32,8192]{2,1,0:T(8,128)(2,1)} %down.7, bf16[4,128,2048]{2,1,0:T(8,128)(2,1)} %up.7), custom_call_target="tpu_custom_call" | custom-call | tf_op jit(solution)/shard_map/pallas_call | solution.py:27
  34.5 0.6 fusion.5.places
  35.1 3.3 %shard_map.86 = (bf16[2,32,8192]{2,1,0:T(8,128)(2,1)}, bf16[2,128,2048]{2,1,0:T(8,128)(2,1)}) custom-call(s32[2]{0:T(128)} %fusion.5.places, bf16[4,32,8192]{2,1,0:T(8,128)(2,1)} %down.7, bf16[4,128,2048]{2,1,0:T(8,128)(2,1)} %up.7), custom_call_target="tpu_custom_call" | custom-call | tf_op jit(solution)/shard_map/pallas_call | solution.py:27
  38.4 0.6 collective-permute-start.6
  39.1 0.8 collective-permute-done.refs_1_
  39.8 0.7 collective-permute-start.1
  40.5 17.4 %collective-permute-done.2.refs_2_ = bf16[1,512,512]{2,1,0:T(8,128)(2,1)} collective-permute-done((bf16[1,512,512]{2,1,0:T(8,128)(2,1)}, bf16[1,512,512]{2,1,0:T(8,128)(2,1)}, u32[]{:S(2)}, u32[]{:S(2)}) %collective-permute-start.2) | collective-permute-done | bytes 524320 | tf_op jit(solution)/shard_map/ppermute | solution.py:288
  57.9 1.3 collective-permute-start.3
  59.4 0.7 fusion.4.places
  60.1 3.3 %shard_map.85 = (bf16[2,32,8192]{2,1,0:T(8,128)(2,1)}, bf16[2,128,2048]{2,1,0:T(8,128)(2,1)}) custom-call(s32[2]{0:T(128)} %fusion.4.places, bf16[4,32,8192]{2,1,0:T(8,128)(2,1)} %down.7, bf16[4,128,2048]{2,1,0:T(8,128)(2,1)} %up.7), custom_call_target="tpu_custom_call" | custom-call | tf_op jit(solution)/shard_map/pallas_call | solution.py:27
  63.5 30.4 %collective-permute-done.3 = bf16[1,512,512]{2,1,0:T(8,128)(2,1)} collective-permute-done((bf16[1,512,512]{2,1,0:T(8,128)(2,1)}, bf16[1,512,512]{2,1,0:T(8,128)(2,1)}, u32[]{:S(2)}, u32[]{:S(2)}) %collective-permute-start.3) | collective-permute-done | bytes 524320 | tf_op jit(solution)/shard_map/ppermute | solution.py:301
  93.9 1.9 broadcast_select_fusion.refs_0_
  95.8 1.3 collective-permute-start.4
  97.1 0.9 copy.13.refs_7_
  97.9 0.9 copy.14.refs_6_.slot
  98.8 1.5 collective-permute-start.15
  100.3 9.7 %shard_map.82.refs_3_ = f32[512,2048]{1,0:T(8,128)} custom-call(s32[3]{0:T(128)} %broadcast_clamp_fusion.source, s32[3]{0:T(128)} %get-tuple-element.29.valid, bf16[1,512,512]{2,1,0:T(8,128)(2,1)} %slice_bitcast_fusion.refs_0_, bf16[1,512,512]{2,1,0:T(8,128)(2,1)} %collective-permute-done.refs_1_, bf16[1,512,512]{2,1,0:T(8,128)(2,1)} %collective-permute-done.2.refs_2_, ...), custom_call_target="tpu_custom_call" | custom-call | flops 3221225472 | bytes 16252928 | tf_op jit(solution)/shard_map/pallas_call | solution.py:94
  110.1 0.6 collective-permute-start.14
  111.0 0.4 copy-done.3
  111.4 0.3 copy-done.4
  111.7 5.7 %shard_map.89.refs_6_ = f32[512,256]{1,0:T(8,128)} custom-call(s32[3]{0:T(128)} %broadcast_clamp_fusion.source, s32[3]{0:T(128)} %get-tuple-element.29.valid, bf16[1,512,512]{2,1,0:T(8,128)(2,1)} %slice_bitcast_fusion.refs_0_, bf16[1,512,512]{2,1,0:T(8,128)(2,1)} %collective-permute-done.refs_1_, bf16[1,512,512]{2,1,0:T(8,128)(2,1)} %collective-permute-done.2.refs_2_, ...), custom_call_target="tpu_custom_call" | custom-call | flops 402653184 | bytes 3407872 | tf_op jit(solution)/shard_map/pallas_call | solution.py:151
  117.5 6.5 %collective-permute-done.4.refs_1_ = bf16[1,512,512]{2,1,0:T(8,128)(2,1)} collective-permute-done((bf16[1,512,512]{2,1,0:T(8,128)(2,1)}, bf16[1,512,512]{2,1,0:T(8,128)(2,1)}, u32[]{:S(2)}, u32[]{:S(2)}) %collective-permute-start.4) | collective-permute-done | bytes 524320 | tf_op jit(solution)/shard_map/ppermute | solution.py:304
  123.9 4.8 %shard_map.90.refs_5_ = f32[512,256]{1,0:T(8,128)} custom-call(s32[2]{0:T(128)} %broadcast_clamp_fusion.1.source, s32[2]{0:T(128)} %get-tuple-element.31.valid, bf16[1,512,512]{2,1,0:T(8,128)(2,1)} %broadcast_select_fusion.refs_0_, bf16[1,512,512]{2,1,0:T(8,128)(2,1)} %collective-permute-done.4.refs_1_, bf16[64,8192]{1,0:T(8,128)(2,1)} %bitcast.47, ...), custom_call_target="tpu_custom_call" | custom-call | flops 268435456 | bytes 2621440 | tf_op jit(solution)/shard_map/pallas_call | solution.py:151
  128.7 9.3 %shard_map.83.refs_2_ = f32[512,2048]{1,0:T(8,128)} custom-call(s32[2]{0:T(128)} %broadcast_clamp_fusion.1.source, s32[2]{0:T(128)} %get-tuple-element.31.valid, bf16[1,512,512]{2,1,0:T(8,128)(2,1)} %broadcast_select_fusion.refs_0_, bf16[1,512,512]{2,1,0:T(8,128)(2,1)} %collective-permute-done.4.refs_1_, bf16[4,2048,2048]{2,1,0:T(8,128)(2,1)} %bitcast.31, ...), custom_call_target="tpu_custom_call" | custom-call | flops 2147483648 | bytes 13631488 | tf_op jit(solution)/shard_map/pallas_call | solution.py:94
  138.0 10.1 %shard_map.91.refs_5_ = f32[512,256]{1,0:T(8,128)} custom-call(s32[4]{0:T(128)} %iota_clamp_fusion.source, s32[4]{0:T(128)} %compare_convert_fusion.valid, bf16[4,512,768]{2,1,0:T(8,128)(2,1)} %bitcast.50, bf16[64,8192]{1,0:T(8,128)(2,1)} %bitcast.48, bf16[64,8192]{1,0:T(8,128)(2,1)} %bitcast.44, bf16[64,8192]{1,0:T(8,128)(2,1)} %bitcast.36, ...), custom_call_target="tpu_custom_call" | custom-call | flops 805306368 | bytes 5767168 | tf_op jit(solution)/shard_map/pallas_call | solution.py:151
  148.1 17.8 %shard_map.84.refs_2_ = f32[512,2048]{1,0:T(8,128)} custom-call(s32[4]{0:T(128)} %iota_clamp_fusion.source, s32[4]{0:T(128)} %compare_convert_fusion.valid, bf16[4,512,768]{2,1,0:T(8,128)(2,1)} %bitcast.51, bf16[4,2048,2048]{2,1,0:T(8,128)(2,1)} %bitcast.32, f32[512,2048]{1,0:T(8,128)} %shard_map.83.refs_2_), custom_call_target="tpu_custom_call" | custom-call | flops 6442450944 | bytes 24117248 | tf_op jit(solution)/shard_map/pallas_call | solution.py:94
  165.9 11.2 %shard_map.93.refs_0_ = bf16[512,32]{1,0:T(8,128)(2,1)} custom-call(s32[4]{0:T(128)} %iota_clamp_fusion.source, s32[4]{0:T(128)} %compare_convert_fusion.valid, bf16[4,512,768]{2,1,0:T(8,128)(2,1)} %bitcast.52, bf16[64,8192]{1,0:T(8,128)(2,1)} %bitcast.49, bf16[64,8192]{1,0:T(8,128)(2,1)} %bitcast.45, bf16[64,8192]{1,0:T(8,128)(2,1)} %bitcast.37, ...), custom_call_target="tpu_custom_call" | custom-call | flops 805306368 | bytes 5767168 | tf_op jit(solution)/shard_map/pallas_call | solution.py:151
  177.1 2.0 collective-permute-start.13
  179.1 17.7 %shard_map.92.total = f32[512,2048]{1,0:T(8,128)} custom-call(s32[4]{0:T(128)} %iota_clamp_fusion.source, s32[4]{0:T(128)} %compare_convert_fusion.valid, bf16[4,512,768]{2,1,0:T(8,128)(2,1)} %bitcast.53, bf16[4,2048,2048]{2,1,0:T(8,128)(2,1)} %bitcast.33, f32[512,2048]{1,0:T(8,128)} %shard_map.84.refs_2_), custom_call_target="tpu_custom_call" | custom-call | flops 6442450944 | bytes 24117248 | tf_op jit(solution)/shard_map/pallas_call | solution.py:94
  197.0 0.6 copy-done.5
  197.6 7.6 %shard_map.94 = bf16[512,2048]{1,0:T(8,128)(2,1)} custom-call(s32[1]{0:T(128)} %bitcast.me, s32[512,1]{1,0:T(8,128)} %copy.14.refs_6_.slot, f32[512,2048]{1,0:T(8,128)} %shard_map.92.total, bf16[512,32]{1,0:T(8,128)(2,1)} %shard_map.93.refs_0_, bf16[512,32]{1,0:T(8,128)(2,1)} %copy-done.5, bf16[512,32]{1,0:T(8,128)(2,1)} %copy-done.6, ...), custom_call_target="tpu_custom_call" | custom-call | flops 2147483648 | bytes 10485760 | tf_op jit(solution)/shard_map/pallas_call | solution.py:194
  (58 shorter events, 1.8 us)
Async XLA Ops:
  6.5 16.0 %copy-start = (s32[16]{0:T(128)S(1)}, s32[16]{0:T(128)}, u32[]{:S(2)}) copy-start(s32[16]{0:T(128)} %param.15) | copy-start | bytes 196
  6.5 2.7 %copy-start.9 = (s32[1,6]{1,0:T(1,128)S(1)}, s32[1,6]{1,0:T(1,128)}, u32[]{:S(2)}) copy-start(s32[1,6]{1,0:T(1,128)} %param.13) | copy-start | bytes 76
  6.5 17.7 %copy-start.10 = (s32[16]{0:T(128)S(1)}, s32[16]{0:T(128)}, u32[]{:S(2)}) copy-start(s32[16]{0:T(128)} %param.12) | copy-start | bytes 196
  6.5 131.5 %all-gather.7.cloned.1.call-start = ((), (), s32[]{:S(2)}) async-start(), calls=%async_computation.1 | async-start | bytes 3932160 | tf_op jit(solution)/shard_map/all_gather | solution.py:280
  9.2 156.7 %all-gather.5.cloned.1.call-start = ((), (), s32[]{:S(2)}) async-start(), calls=%async_computation | async-start | bytes 3932160 | tf_op jit(solution)/shard_map/all_gather | solution.py:280
  9.2 15.0 %collective-permute-start.5 = (s32[1,6]{1,0:T(1,128)S(1)}, s32[1,6]{1,0:T(1,128)S(1)}, u32[]{:S(2)}, u32[]{:S(2)}) collective-permute-start(s32[1,6]{1,0:T(1,128)S(1)} %copy-done.9), channel_id=1, source_target_pairs={{0,1},{1,0},{2,3},{3,2},{4,5},{5,4},{6,7},{7,6},{8,9},{9,8},{10,11... | collective-permute-start | bytes 80 | tf_op jit(solution)/shard_map/ppermute | solution.py:239
  9.8 14.5 %collective-permute-start.7 = (s32[1,6]{1,0:T(1,128)S(1)}, s32[1,6]{1,0:T(1,128)S(1)}, u32[]{:S(2)}, u32[]{:S(2)}) collective-permute-start(s32[1,6]{1,0:T(1,128)S(1)} %copy-done.9), channel_id=1, source_target_pairs={{0,2},{1,3},{2,0},{3,1},{4,6},{5,7},{6,4},{7,5},{8,10},{9,11},{10,... | collective-permute-start | bytes 80 | tf_op jit(solution)/shard_map/ppermute | solution.py:239
  12.3 11.9 %collective-permute-start.9 = (s32[1,6]{1,0:T(1,128)S(1)}, s32[1,6]{1,0:T(1,128)S(1)}, u32[]{:S(2)}, u32[]{:S(2)}) collective-permute-start(s32[1,6]{1,0:T(1,128)S(1)} %copy-done.9), channel_id=1, source_target_pairs={{0,3},{1,2},{2,1},{3,0},{4,7},{5,6},{6,5},{7,4},{8,11},{9,10},{10,... | collective-permute-start | bytes 80 | tf_op jit(solution)/shard_map/ppermute | solution.py:239
  14.3 25.5 %collective-permute-start = (bf16[1,512,512]{2,1,0:T(8,128)(2,1)}, bf16[1,512,512]{2,1,0:T(8,128)(2,1)}, u32[]{:S(2)}, u32[]{:S(2)}) collective-permute-start(bf16[1,512,512]{2,1,0:T(8,128)(2,1)} %slice_bitcast_fusion.refs_0_), channel_id=1, source_target_pairs={{0,4},{4,8},{8,12},{1,5},{5,9},{9,13},{2,6},{6,10},{10,14},{3,7},{... | collective-permute-start | bytes 1572872 | tf_op jit(solution)/shard_map/ppermute | solution.py:287
  18.8 39.1 %collective-permute-start.2 = (bf16[1,512,512]{2,1,0:T(8,128)(2,1)}, bf16[1,512,512]{2,1,0:T(8,128)(2,1)}, u32[]{:S(2)}, u32[]{:S(2)}) collective-permute-start(bf16[1,512,512]{2,1,0:T(8,128)(2,1)} %slice_bitcast_fusion.refs_0_), channel_id=1, source_target_pairs={{4,0},{8,4},{12,8},{5,1},{9,5},{13,9},{6,2},{10,6},{14,10},{7,3},{... | collective-permute-start | bytes 1572872 | tf_op jit(solution)/shard_map/ppermute | solution.py:288
  28.6 81.4 %collective-permute-start.8 = (bf16[2,32,8192]{2,1,0:T(8,128)(2,1)}, bf16[2,32,8192]{2,1,0:T(8,128)(2,1)S(1)}, u32[]{:S(2)}, u32[]{:S(2)}) collective-permute-start(bf16[2,32,8192]{2,1,0:T(8,128)(2,1)} %get-tuple-element.16), channel_id=1, source_target_pairs={{0,2},{1,3},{2,0},{3,1},{4,6},{5,7},{6,4},{7,5},{8,10},{9,11},{10,... | collective-permute-start | bytes 3145736 | tf_op jit(solution)/shard_map/ppermute | solution.py:296
  34.3 75.9 %collective-permute-start.10 = (bf16[2,32,8192]{2,1,0:T(8,128)(2,1)}, bf16[2,32,8192]{2,1,0:T(8,128)(2,1)S(1)}, u32[]{:S(2)}, u32[]{:S(2)}) collective-permute-start(bf16[2,32,8192]{2,1,0:T(8,128)(2,1)} %get-tuple-element.17), channel_id=1, source_target_pairs={{0,3},{1,2},{2,1},{3,0},{4,7},{5,6},{6,5},{7,4},{8,11},{9,10},{10,... | collective-permute-start | bytes 3145736 | tf_op jit(solution)/shard_map/ppermute | solution.py:296
  38.4 25.0 %copy-start.8 = (s32[512]{0:T(512)S(1)}, s32[512]{0:T(512)}, u32[]{:S(2)}) copy-start(s32[512]{0:T(512)} %param.14) | copy-start | bytes 6148
  38.4 72.3 %collective-permute-start.6 = (bf16[2,32,8192]{2,1,0:T(8,128)(2,1)}, bf16[2,32,8192]{2,1,0:T(8,128)(2,1)S(1)}, u32[]{:S(2)}, u32[]{:S(2)}) collective-permute-start(bf16[2,32,8192]{2,1,0:T(8,128)(2,1)} %get-tuple-element.15), channel_id=1, source_target_pairs={{0,1},{1,0},{2,3},{3,2},{4,5},{5,4},{6,7},{7,6},{8,9},{9,8},{10,11... | collective-permute-start | bytes 3145736 | tf_op jit(solution)/shard_map/ppermute | solution.py:296
  39.8 23.7 %collective-permute-start.1 = (bf16[1,512,512]{2,1,0:T(8,128)(2,1)}, bf16[1,512,512]{2,1,0:T(8,128)(2,1)S(1)}, u32[]{:S(2)}, u32[]{:S(2)}) collective-permute-start(bf16[1,512,512]{2,1,0:T(8,128)(2,1)} %collective-permute-done.refs_1_), channel_id=1, source_target_pairs={{4,8},{8,12},{5,9},{9,13},{6,10},{10,14},{7,11},{11,15},{20,24},{2... | collective-permute-start | bytes 1572872 | tf_op jit(solution)/shard_map/ppermute | solution.py:300
  57.9 36.0 %collective-permute-start.3 = (bf16[1,512,512]{2,1,0:T(8,128)(2,1)}, bf16[1,512,512]{2,1,0:T(8,128)(2,1)}, u32[]{:S(2)}, u32[]{:S(2)}) collective-permute-start(bf16[1,512,512]{2,1,0:T(8,128)(2,1)} %collective-permute-done.2.refs_2_), channel_id=1, source_target_pairs={{4,0},{8,4},{5,1},{9,5},{6,2},{10,6},{7,3},{11,7},{20,16},{24,20},... | collective-permute-start | bytes 1572872 | tf_op jit(solution)/shard_map/ppermute | solution.py:301
  95.8 28.2 %collective-permute-start.4 = (bf16[1,512,512]{2,1,0:T(8,128)(2,1)}, bf16[1,512,512]{2,1,0:T(8,128)(2,1)}, u32[]{:S(2)}, u32[]{:S(2)}) collective-permute-start(bf16[1,512,512]{2,1,0:T(8,128)(2,1)} %broadcast_select_fusion.refs_0_), channel_id=1, source_target_pairs={{8,12},{4,0},{9,13},{5,1},{10,14},{6,2},{11,15},{7,3},{24,28},{20,... | collective-permute-start | bytes 1572872 | tf_op jit(solution)/shard_map/ppermute | solution.py:304
  98.8 78.3 %collective-permute-start.15 = (bf16[2,128,2048]{2,1,0:T(8,128)(2,1)}, bf16[2,128,2048]{2,1,0:T(8,128)(2,1)}, u32[]{:S(2)}, u32[]{:S(2)}) collective-permute-start(bf16[2,128,2048]{2,1,0:T(8,128)(2,1)} %get-tuple-element.21), channel_id=1, source_target_pairs={{0,2},{1,3},{2,0},{3,1},{4,6},{5,7},{6,4},{7,5},{8,10},{9,11},{10,... | collective-permute-start | bytes 3145736 | tf_op jit(solution)/shard_map/ppermute | solution.py:296
  110.0 1.0 copy-start.2
  110.0 86.8 %collective-permute-start.16 = (bf16[2,128,2048]{2,1,0:T(8,128)(2,1)}, bf16[2,128,2048]{2,1,0:T(8,128)(2,1)}, u32[]{:S(2)}, u32[]{:S(2)}) collective-permute-start(bf16[2,128,2048]{2,1,0:T(8,128)(2,1)} %get-tuple-element.22), channel_id=1, source_target_pairs={{0,3},{1,2},{2,1},{3,0},{4,7},{5,6},{6,5},{7,4},{8,11},{9,10},{10,... | collective-permute-start | bytes 3145736 | tf_op jit(solution)/shard_map/ppermute | solution.py:296
  110.1 1.3 copy-start.3
  110.1 86.7 %collective-permute-start.14 = (bf16[2,128,2048]{2,1,0:T(8,128)(2,1)}, bf16[2,128,2048]{2,1,0:T(8,128)(2,1)}, u32[]{:S(2)}, u32[]{:S(2)}) collective-permute-start(bf16[2,128,2048]{2,1,0:T(8,128)(2,1)} %get-tuple-element.20), channel_id=1, source_target_pairs={{0,1},{1,0},{2,3},{3,2},{4,5},{5,4},{6,7},{7,6},{8,9},{9,8},{10,11... | collective-permute-start | bytes 3145736 | tf_op jit(solution)/shard_map/ppermute | solution.py:296
  110.7 1.0 copy-start.4
  177.1 19.8 %collective-permute-start.11 = (bf16[512,32]{1,0:T(8,128)(2,1)}, bf16[512,32]{1,0:T(8,128)(2,1)S(1)}, u32[]{:S(2)}, u32[]{:S(2)}) collective-permute-start(bf16[512,32]{1,0:T(8,128)(2,1)} %shard_map.93.refs_0_), channel_id=1, source_target_pairs={{0,12},{4,0},{8,4},{12,8},{1,13},{5,1},{9,5},{13,9},{2,14},{6,2},{... | collective-permute-start | bytes 98312 | tf_op jit(solution)/shard_map/ppermute | solution.py:326
  177.1 19.8 %collective-permute-start.12 = (bf16[512,32]{1,0:T(8,128)(2,1)}, bf16[512,32]{1,0:T(8,128)(2,1)S(1)}, u32[]{:S(2)}, u32[]{:S(2)}) collective-permute-start(bf16[512,32]{1,0:T(8,128)(2,1)} %shard_map.93.refs_0_), channel_id=1, source_target_pairs={{0,8},{4,12},{8,0},{12,4},{1,9},{5,13},{9,1},{13,5},{2,10},{6,14},... | collective-permute-start | bytes 98312 | tf_op jit(solution)/shard_map/ppermute | solution.py:326
  177.1 19.8 %collective-permute-start.13 = (bf16[512,32]{1,0:T(8,128)(2,1)}, bf16[512,32]{1,0:T(8,128)(2,1)S(1)}, u32[]{:S(2)}, u32[]{:S(2)}) collective-permute-start(bf16[512,32]{1,0:T(8,128)(2,1)} %shard_map.93.refs_0_), channel_id=1, source_target_pairs={{0,4},{4,8},{8,12},{12,0},{1,5},{5,9},{9,13},{13,1},{2,6},{6,10},{... | collective-permute-start | bytes 98312 | tf_op jit(solution)/shard_map/ppermute | solution.py:326
  196.9 0.6 copy-start.5
  196.9 0.7 copy-start.6
  196.9 0.7 copy-start.7
  196.9 8.3 %copy-start.1 = (s32[16]{0:T(128)S(1)}, s32[16]{0:T(128)}, u32[]{:S(2)}) copy-start(s32[16]{0:T(128)} %param.15) | copy-start | bytes 196
Sparse Core Ops, SparseCore 0:
  9.3 87.8 all-gather.6
  98.8 63.8 all-gather.4

commit v4 on v3

--- a/solution.py
+++ b/solution.py
@@ -8,126 +8,112 @@
 from jax.sharding import PartitionSpec as P
 
 CAP = 2
-UNIT = 256
-LINE = 512
-GATHERED = (768, 768)
+LINE = 768
+GATHERED = (768, 512)
 PARAMS = pltpu.CompilerParams(vmem_limit_bytes=60 * 2**20)
 F32 = jnp.float32
 BF16 = jnp.bfloat16
 
 
 def pick_kernel(places, down, up, down_out, up_out):
-    down_out[...] = down[...]
+    shards, _, width = down_out.shape[1:]
+    for t in range(shards):
+        down_out[0, t] = down[0, :, t * width:(t + 1) * width]
     up_out[...] = up[...]
 
 
-def pick_pages(places, down, up):
+def pick_pages(places, down, up, shards):
     count = places.shape[0]
-    blocks = [(1,) + a.shape[1:] for a in (down, up)]
+    _, rank_part, features = down.shape
+    shapes = [(shards, rank_part, features // shards), up.shape[1:]]
     return pl.pallas_call(
         pick_kernel,
-        out_shape=[jax.ShapeDtypeStruct((count,) + a.shape[1:], BF16) for a in (down, up)],
+        out_shape=[jax.ShapeDtypeStruct((count,) + shape, BF16) for shape in shapes],
         grid_spec=pltpu.PrefetchScalarGridSpec(
             num_scalar_prefetch=1,
             grid=(count,),
-            in_specs=[pl.BlockSpec(b, lambda i, places: (places[i], 0, 0)) for b in blocks],
-            out_specs=[pl.BlockSpec(b, lambda i, places: (i, 0, 0)) for b in blocks],
+            in_specs=[pl.BlockSpec((1,) + a.shape[1:], lambda i, places: (places[i], 0, 0)) for a in (down, up)],
+            out_specs=[
+                pl.BlockSpec((1,) + shapes[0], lambda i, places: (i, 0, 0, 0)),
+                pl.BlockSpec((1,) + shapes[1], lambda i, places: (i, 0, 0)),
+            ],
         ),
         compiler_params=PARAMS,
     )(places, down, up)
 
 
-def steps_of(xs):
-    return sum(x.shape[0] for x in xs)
-
-
-def x_specs(xs):
-    specs, first = [], 0
-    for x in xs:
-        units = x.shape[2] // UNIT
-
-        def index(s, j, *_, first=first, count=x.shape[0], units=units):
-            shard = jnp.clip(s - first, 0, count - 1)
-            return shard, 0, jnp.where(s < first, 0, jnp.where(s >= first + count, units - 1, j))
-
-        specs.append(pl.BlockSpec((1, x.shape[1], UNIT), index))
-        first += x.shape[0]
-    return specs
-
-
-def for_block(xs, counts, valid, body):
-    s, first = pl.program_id(0), 0
-    for x, count in zip(xs, counts):
-
-        @pl.when((s >= first) & (s < first + count) & (valid[s] != 0))
+def base_kernel(count, has_total, source, valid, *refs):
+    xs, weights, out = refs[:count], refs[count:2 * count], refs[-1]
+    shards = xs[0].shape[0]
+
+    def product(x, weight):
+        return sum(jnp.dot(x[t], weight[t], preferred_element_type=F32) for t in range(shards))
+
+    first = product(xs[0], weights[0])
+    out[...] = refs[-2][...] + first if has_total else first
+    for i in range(1, count):
+
+        @pl.when(valid[i] != 0)
         def _():
-            body(x[0])
-
-        first += count
-
-
-def start_total(out, total):
-    @pl.when((pl.program_id(0) == 0) & (pl.program_id(1) == 0))
-    def _():
-        out[...] = jnp.zeros_like(out) if total is None else total[...]
-
-
-def base_kernel(counts, has_total, source, valid, *refs):
-    xs, weight, out = refs[:len(counts)], refs[len(counts)], refs[-1]
-    start_total(out, refs[-2] if has_total else None)
-    columns = out.shape[1]
+            out[...] += product(xs[i], weights[i])
+
+
+def add_base(total, xs, source, valid, offset, weight):
+    shards, rows, features = xs[0].shape
+    columns = weight.shape[-1]
     part = min(columns, 512)
-
-    def body(x):
-        for n in range(0, columns, part):
-            out[:, n:n + part] += jnp.dot(x, weight[0, :, n:n + part], preferred_element_type=F32)
-
-    for_block(xs, counts, valid, body)
-
-
-def add_base(total, xs, source, valid, offset, weight):
-    rows, features = xs[0].shape[1:]
-    columns = weight.shape[-1]
     held = [] if total is None else [total]
-    whole = pl.BlockSpec((rows, columns), lambda s, j, *_: (0, 0))
-    steps = steps_of(xs)
+    tile = pl.BlockSpec((rows, part), lambda n, *_: (0, n))
+    depth = len(xs) * shards * features
+
+    def weight_spec(i):
+        def index(n, source, valid):
+            return 0 if shards > 1 else source[i], offset // features, n
+
+        return pl.BlockSpec((shards, features, part), index)
+
     return pl.pallas_call(
-        functools.partial(base_kernel, [x.shape[0] for x in xs], bool(held)),
+        functools.partial(base_kernel, len(xs), bool(held)),
         out_shape=jax.ShapeDtypeStruct((rows, columns), F32),
         grid_spec=pltpu.PrefetchScalarGridSpec(
             num_scalar_prefetch=2,
-            grid=(steps, features // UNIT),
-            in_specs=x_specs(xs) + [
-                pl.BlockSpec((1, UNIT, columns), lambda s, j, source, valid: (source[s], offset // UNIT + j, 0))
-            ] + [whole] * len(held),
-            out_specs=whole,
+            grid=(columns // part,),
+            in_specs=[pl.BlockSpec(x.shape, lambda n, *_: (0, 0, 0)) for x in xs]
+            + [weight_spec(i) for i in range(len(xs))] + [tile] * len(held),
+            out_specs=tile,
         ),
         compiler_params=PARAMS,
         cost_estimate=pl.CostEstimate(
-            flops=2 * steps * rows * features * columns,
-            bytes_accessed=2 * steps * features * (rows + columns) + 8 * rows * columns,
+            flops=2 * depth * rows * columns,
+            bytes_accessed=2 * depth * (rows + columns) + 8 * rows * columns,
             transcendentals=0,
         ),
-    )(source, valid, *xs, weight, *held)
-
-
-def low_kernel(counts, parts, has_total, last, rank_part, source, valid, *refs):
+    )(source, valid, *xs, *[weight] * len(xs), *held)
+
+
+def low_kernel(count, shards, parts, has_total, last, rank_part, source, valid, *refs):
     refs = list(refs)
-    xs = [refs.pop(0) for _ in counts]
+    xs = [refs.pop(0) for _ in range(count)]
     downs = [refs.pop(0) for _ in range(parts)]
     total = refs.pop(0) if has_total else None
     acc = refs.pop()
-    start_total(acc, total)
-
-    def body(x):
-        down = jnp.concatenate([d[...] for d in downs], axis=0)
-        acc[...] += lax.dot_general(x, down, (((1,), (1,)), ((), ())), preferred_element_type=F32)
-
-    for_block(xs, counts, valid, body)
+    step = pl.program_id(0)
+
+    @pl.when(step == 0)
+    def _():
+        acc[...] = total[...] if has_total else jnp.zeros_like(acc)
+
+    for i, x in enumerate(xs):
+
+        @pl.when((step >= i * shards) & (step < (i + 1) * shards) & (valid[step] != 0))
+        def _():
+            down = jnp.concatenate([d[c, 0] for d in downs for c in range(CAP)], axis=0)
+            acc[...] += lax.dot_general(x[0], down, (((1,), (1,)), ((), ())), preferred_element_type=F32)
+
     if last:
         slot, live, out = refs
 
-        @pl.when((pl.program_id(0) == pl.num_programs(0) - 1) & (pl.program_id(1) == pl.num_programs(1) - 1))
+        @pl.when(step == pl.num_programs(0) - 1)
         def _():
             mine = jnp.zeros((acc.shape[0], rank_part), F32)
             for e in range(acc.shape[1] // rank_part):
@@ -136,26 +122,29 @@
             out[...] = jnp.where(k < live[...], mine, 0.0).astype(BF16)
 
 
-def add_low(total, xs, source, valid, offset, downs, rank_part, ends=()):
-    rows, features = xs[0].shape[1:]
-    shard_units = downs[0].shape[1] // lax.axis_size("tensor") // UNIT
-    depth = downs[0].shape[0]
-    ranks = depth * len(downs)
+def add_low(total, xs, source, valid, offset, downs, ends=()):
+    shards, rows, features = xs[0].shape
+    rank_part = downs[0].shape[2]
+    ranks = CAP * rank_part * len(downs)
     held = [] if total is None else [total]
-    whole = pl.BlockSpec((rows, ranks), lambda s, j, *_: (0, 0))
-    column = pl.BlockSpec((rows, 1), lambda s, j, *_: (0, 0))
-    steps = steps_of(xs)
+    steps = len(xs) * shards
+    whole = pl.BlockSpec((rows, ranks), lambda s, *_: (0, 0))
+    column = pl.BlockSpec((rows, 1), lambda s, *_: (0, 0))
+    x_specs = [
+        pl.BlockSpec((1, rows, features), lambda s, *_, i=i: (jnp.clip(s - i * shards, 0, shards - 1), 0, 0))
+        for i in range(len(xs))
+    ]
     down_spec = pl.BlockSpec(
-        (depth, UNIT), lambda s, j, source, valid: (0, source[s] * shard_units + offset // UNIT + j)
+        (CAP, 1, rank_part, features), lambda s, source, valid: (0, source[s], 0, offset // features)
     )
     return pl.pallas_call(
-        functools.partial(low_kernel, [x.shape[0] for x in xs], len(downs), bool(held), bool(ends), rank_part),
+        functools.partial(low_kernel, len(xs), shards, len(downs), bool(held), bool(ends), rank_part),
         out_shape=jax.ShapeDtypeStruct((rows, rank_part), BF16) if ends else jax.ShapeDtypeStruct((rows, ranks), F32),
         grid_spec=pltpu.PrefetchScalarGridSpec(
             num_scalar_prefetch=2,
-            grid=(steps, features // UNIT),
-            in_specs=x_specs(xs) + [down_spec] * len(downs) + [whole] * len(held) + [column] * len(ends),
-            out_specs=pl.BlockSpec((rows, rank_part), lambda s, j, *_: (0, 0)) if ends else whole,
+            grid=(steps,),
+            in_specs=x_specs + [down_spec] * len(downs) + [whole] * len(held) + [column] * len(ends),
+            out_specs=pl.BlockSpec((rows, rank_part), lambda s, *_: (0, 0)) if ends else whole,
             scratch_shapes=[pltpu.VMEM((rows, ranks), F32)] if ends else [],
         ),
         compiler_params=PARAMS,
@@ -276,12 +265,15 @@
     ones = jnp.ones((n_tensor,), jnp.int32)
 
     gathered, offsets, offset = [], [], LINE
+    x = attention_result
     for features in GATHERED:
-        gathered.append(lax.all_gather(attention_result[:, offset:offset + features], "tensor", axis=0))
+        piece = x[:, offset:offset + features]
+        gathered.append(lax.all_gather(piece, "tensor", axis=0))
+        x = after(x, piece)
         offsets.append(offset)
         offset += features
 
-    line = attention_result[None, :, :LINE]
+    line = x[None, :, :LINE]
     right = [(i, i + 1) for i in range(n_tensor - 1)]
     left = [(i + 1, i) for i in range(n_tensor - 1)]
     right_1 = lax.ppermute(line, "tensor", right)
@@ -290,11 +282,11 @@
     slots, places = asked_pages(requests, adapter_page_row, holder_length)
     downs, ups = [], []
     for j in range(n_dp):
-        down, up = pick_pages(places[j], adapter_down_weight, adapter_up_weight)
+        down, up = pick_pages(places[j], adapter_down_weight, adapter_up_weight, n_tensor)
         if j:
             pairs = [(i, i ^ j) for i in range(n_dp)]
             down, up = lax.ppermute(down, "dp", pairs), lax.ppermute(up, "dp", pairs)
-        downs.append(down.reshape(CAP * rank_part, -1))
+        downs.append(down)
         ups.append(up.reshape(CAP * rank, columns))
 
     right_2 = lax.ppermute(right_1, "tensor", right[1:])
@@ -320,7 +312,7 @@
         ends = (slot, live) if i == len(xs) - 1 else ()
         if ends:
             blocks = [after(blocks[0], base, low)]
-        low = add_low(low, blocks, source, valid, start, downs, rank_part, ends)
+        low = add_low(low, blocks, source, valid, start, downs, ends)
         base = add_base(base, blocks, source, valid, start, weight)
     lows = [low] + [
         lax.ppermute(low, "tensor", [(i, (i - j) % n_tensor) for i in range(n_tensor)])

time: 214 us -> 228 us (1.065)
  waiting for transfers between devices: 55 us -> 89.3 us
  Pallas kernels: 107 us -> 85.8 us
    pallas_call x12, Pallas kernels: 99.6 us -> 78.2 us  [the longest x4 43.7 us: add_base(): pl.pallas_call(functools.partial(base_kernel, len(xs), bool(held)), out_s...]
    ppermute x1, waiting for transfers between devices: 6.47 us -> 25 us  [local(): third = lax.ppermute(second, 'tensor', right[-1:] + left[:1])]
    ppermute x1, waiting for transfers between devices: 0.75 us -> 16.7 us  [local(): right_1 = lax.ppermute(line, 'tensor', right)]
    ppermute x1, waiting for transfers between devices: 30.4 us -> 25.5 us  [local(): left_2 = lax.ppermute(left_1, 'tensor', left[:-1])]
    ppermute x1, waiting for transfers between devices: 17.4 us -> 21.7 us  [local(): left_1 = lax.ppermute(line, 'tensor', left)]
  transfers between devices with their start and end apart: 19 -> 19, of which waited for: 4 -> 5; matrix products, arithmetic and copies ran while one was open for 6% -> 6% of each run, Pallas kernels for 47% -> 34%
where the time goes in v4:
time: 228 us; the launch traced here: 227 us
  waiting for transfers between devices  89.3 us (39%)
  Pallas kernels  85.8 us (38%)
  starting transfers between devices  20.2 us (9%)
  between operations  13.6 us (6%)
  other arithmetic  9.29 us (4%)
  local copies, waits for them, and re-layouts  9.22 us (4%)
    pallas_call x4, Pallas kernels, add_base(): pl.pallas_call(functools.partial(base_kernel, len(xs), bool(held)), out_s...  43.7 us
    ppermute x1, waiting for transfers between devices, local(): left_2 = lax.ppermute(left_1, 'tensor', left[:-1])  25.5 us
    ppermute x1, waiting for transfers between devices, local(): third = lax.ppermute(second, 'tensor', right[-1:] + left[:1])  25 us
    ppermute x1, waiting for transfers between devices, local(): left_1 = lax.ppermute(line, 'tensor', left)  21.7 us
    pallas_call x4, Pallas kernels, add_low(): pl.pallas_call(functools.partial(low_kernel, len(xs), shards, len(downs),...  21.2 us
    ppermute x1, waiting for transfers between devices, local(): right_1 = lax.ppermute(line, 'tensor', right)  16.7 us
    pallas_call x4, Pallas kernels, pick_pages(): pl.pallas_call(pick_kernel, out_shape=[jax.ShapeDtypeStruct((count,) + sh...  13.3 us
    pallas_call x1, Pallas kernels, finish(): pl.pallas_call(functools.partial(finish_kernel, len(lows), len(ups)), gri...  7.61 us
  transfers between devices with their start and end apart: 19, of which 5 were waited for; matrix products, arithmetic and copies ran while one was open for 6% of the time, Pallas kernels for 34%

profile of v4, /device:TPU:0, one launch (start us, length us, event | category | flops | bytes accessed | tf_op | source)
XLA Modules:
  0.0 227.4 jit_solution(11591748564418070681)
XLA Ops:
  6.5 2.1 slice.9
  8.7 0.5 collective-permute-start.5
  9.2 2.6 %collective-permute-start.7 = (s32[1,6]{1,0:T(1,128)}, s32[1,6]{1,0:T(1,128)S(1)}, u32[]{:S(2)}, u32[]{:S(2)}) collective-permute-start(s32[1,6]{1,0:T(1,128)} %param.13), channel_id=1, source_target_pairs={{0,2},{1,3},{2,0},{3,1},{4,6},{5,7},{6,4},{7,5},{8,10},{9,11},{10,... | collective-permute-start | bytes 80 | tf_op jit(solution)/shard_map/ppermute | solution.py:228
  11.9 1.9 slice.10
  13.7 1.2 slice_bitcast_fusion.refs_0_
  14.9 4.6 %collective-permute-start = (bf16[1,512,768]{2,1,0:T(8,128)(2,1)S(1)}, bf16[1,512,768]{2,1,0:T(8,128)(2,1)}, u32[]{:S(2)}, u32[]{:S(2)}) collective-permute-start(bf16[1,512,768]{2,1,0:T(8,128)(2,1)S(1)} %slice_bitcast_fusion.refs_0_), channel_id=1, source_target_pairs={{0,4},{4,8},{8,12},{1,5},{5,9},{9,13},{2,6},{6,10},{10,14},{3,7},{... | collective-permute-start | bytes 2359304 | tf_op jit(solution)/shard_map/ppermute | solution.py:279
  19.6 1.3 collective-permute-start.2
  20.9 0.6 compare_convert_fusion.valid
  21.5 0.5 iota_clamp_fusion.source
  22.0 0.7 and_convert_fusion
  22.6 0.6 broadcast_clamp_fusion.source
  23.2 0.7 and_convert_fusion.1
  23.9 0.6 broadcast_clamp_fusion.1.source
  24.5 0.6 gather_fusion
  25.6 0.6 fusion.7.places
  26.2 3.4 %shard_map.88 = (bf16[2,4,32,2048]{3,2,1,0:T(8,128)(2,1)}, bf16[2,128,2048]{2,1,0:T(8,128)(2,1)}) custom-call(s32[2]{0:T(128)} %fusion.7.places, bf16[4,32,8192]{2,1,0:T(8,128)(2,1)} %down.7, bf16[4,128,2048]{2,1,0:T(8,128)(2,1)} %up.7), custom_call_target="tpu_custom_call" | custom-call | tf_op jit(solution)/shard_map/pallas_call | solution.py:29
  29.6 1.2 collective-permute-start.10
  30.9 0.6 fusion.6.places
  31.5 3.3 %shard_map.87 = (bf16[2,4,32,2048]{3,2,1,0:T(8,128)(2,1)}, bf16[2,128,2048]{2,1,0:T(8,128)(2,1)}) custom-call(s32[2]{0:T(128)} %fusion.6.places, bf16[4,32,8192]{2,1,0:T(8,128)(2,1)} %down.7, bf16[4,128,2048]{2,1,0:T(8,128)(2,1)} %up.7), custom_call_target="tpu_custom_call" | custom-call | tf_op jit(solution)/shard_map/pallas_call | solution.py:29
  34.8 0.6 collective-permute-start.8
  35.6 16.7 %collective-permute-done.refs_1_ = bf16[1,512,768]{2,1,0:T(8,128)(2,1)} collective-permute-done((bf16[1,512,768]{2,1,0:T(8,128)(2,1)S(1)}, bf16[1,512,768]{2,1,0:T(8,128)(2,1)}, u32[]{:S(2)}, u32[]{:S(2)}) %collective-permute-start) | collective-permute-done | bytes 786464 | tf_op jit(solution)/shard_map/ppermute | solution.py:279
  52.3 1.6 collective-permute-start.1
  53.9 21.7 %collective-permute-done.2.refs_2_ = bf16[1,512,768]{2,1,0:T(8,128)(2,1)} collective-permute-done((bf16[1,512,768]{2,1,0:T(8,128)(2,1)S(1)}, bf16[1,512,768]{2,1,0:T(8,128)(2,1)}, u32[]{:S(2)}, u32[]{:S(2)}) %collective-permute-start.2) | collective-permute-done | bytes 786464 | tf_op jit(solution)/shard_map/ppermute | solution.py:280
  75.6 1.3 collective-permute-start.3
  76.9 0.6 fusion.5.places
  77.6 3.4 %shard_map.86 = (bf16[2,4,32,2048]{3,2,1,0:T(8,128)(2,1)}, bf16[2,128,2048]{2,1,0:T(8,128)(2,1)}) custom-call(s32[2]{0:T(128)} %fusion.5.places, bf16[4,32,8192]{2,1,0:T(8,128)(2,1)} %down.7, bf16[4,128,2048]{2,1,0:T(8,128)(2,1)} %up.7), custom_call_target="tpu_custom_call" | custom-call | tf_op jit(solution)/shard_map/pallas_call | solution.py:29
  81.3 25.5 %collective-permute-done.3 = bf16[1,512,768]{2,1,0:T(8,128)(2,1)} collective-permute-done((bf16[1,512,768]{2,1,0:T(8,128)(2,1)}, bf16[1,512,768]{2,1,0:T(8,128)(2,1)}, u32[]{:S(2)}, u32[]{:S(2)}) %collective-permute-start.3) | collective-permute-done | bytes 786464 | tf_op jit(solution)/shard_map/ppermute | solution.py:293
  106.7 2.1 broadcast_select_fusion.refs_0_
  108.9 1.3 collective-permute-start.4
  110.2 0.6 fusion.4.places
  110.8 3.3 %shard_map.85 = (bf16[2,4,32,2048]{3,2,1,0:T(8,128)(2,1)}, bf16[2,128,2048]{2,1,0:T(8,128)(2,1)}) custom-call(s32[2]{0:T(128)} %fusion.4.places, bf16[4,32,8192]{2,1,0:T(8,128)(2,1)} %down.7, bf16[4,128,2048]{2,1,0:T(8,128)(2,1)} %up.7), custom_call_target="tpu_custom_call" | custom-call | tf_op jit(solution)/shard_map/pallas_call | solution.py:29
  114.0 0.9 copy.13.refs_7_
  114.9 0.8 copy.14.refs_6_.slot
  115.7 1.5 collective-permute-start.15
  117.3 10.1 %shard_map.82.refs_4_ = f32[512,2048]{1,0:T(8,128)} custom-call(s32[3]{0:T(128)} %broadcast_clamp_fusion.source, s32[3]{0:T(128)} %get-tuple-element.33.valid, bf16[1,512,768]{2,1,0:T(8,128)(2,1)} %copy-done.5, bf16[1,512,768]{2,1,0:T(8,128)(2,1)} %collective-permute-done.refs_1_, bf16[1,512,768]{2,1,0:T(8,128)(2,1)} %collective-permute-done.2.refs_2_, ...), custom_call_target="tpu_custom_call" | custom-call | flops 4831838208 | bytes 20185088 | tf_op jit(solution)/shard_map/pallas_call | solution.py:75
  127.5 0.6 collective-permute-start.14
  129.1 5.2 %shard_map.89.refs_6_ = f32[512,256]{1,0:T(8,128)} custom-call(s32[3]{0:T(128)} %broadcast_clamp_fusion.source, s32[3]{0:T(128)} %get-tuple-element.33.valid, bf16[1,512,768]{2,1,0:T(8,128)(2,1)} %copy-done.5, bf16[1,512,768]{2,1,0:T(8,128)(2,1)} %collective-permute-done.refs_1_, bf16[1,512,768]{2,1,0:T(8,128)(2,1)} %collective-permute-done.2.refs_2_, ...), custom_call_target="tpu_custom_call" | custom-call | flops 603979776 | bytes 4587520 | tf_op jit(solution)/shard_map/pallas_call | solution.py:140
  134.2 25.0 %collective-permute-done.4.refs_1_ = bf16[1,512,768]{2,1,0:T(8,128)(2,1)} collective-permute-done((bf16[1,512,768]{2,1,0:T(8,128)(2,1)}, bf16[1,512,768]{2,1,0:T(8,128)(2,1)}, u32[]{:S(2)}, u32[]{:S(2)}) %collective-permute-start.4) | collective-permute-done | bytes 786464 | tf_op jit(solution)/shard_map/ppermute | solution.py:296
  159.2 4.1 %shard_map.90.refs_5_ = f32[512,256]{1,0:T(8,128)} custom-call(s32[2]{0:T(128)} %broadcast_clamp_fusion.1.source, s32[2]{0:T(128)} %get-tuple-element.35.valid, bf16[1,512,768]{2,1,0:T(8,128)(2,1)} %broadcast_select_fusion.refs_0_, bf16[1,512,768]{2,1,0:T(8,128)(2,1)} %collective-permute-done.4.refs_1_, ...), custom_call_target="tpu_custom_call" | custom-call | flops 402653184 | bytes 3407872 | tf_op jit(solution)/shard_map/pallas_call | solution.py:140
  163.3 9.9 %shard_map.83.refs_2_ = f32[512,2048]{1,0:T(8,128)} custom-call(s32[2]{0:T(128)} %broadcast_clamp_fusion.1.source, s32[2]{0:T(128)} %get-tuple-element.35.valid, bf16[1,512,768]{2,1,0:T(8,128)(2,1)} %broadcast_select_fusion.refs_0_, bf16[1,512,768]{2,1,0:T(8,128)(2,1)} %collective-permute-done.4.refs_1_, bf16[4,2048,2048]{2,1,0:T(8,128)(2,1)} %bitcast.29, ...), custom_call_target="tpu_custom_call" | custom-call | flops 3221225472 | bytes 16252928 | tf_op jit(solution)/shard_map/pallas_call | solution.py:75
  173.2 5.7 %shard_map.91.refs_5_ = f32[512,256]{1,0:T(8,128)} custom-call(s32[4]{0:T(128)} %iota_clamp_fusion.source, s32[4]{0:T(128)} %compare_convert_fusion.valid, bf16[4,512,768]{2,1,0:T(8,128)(2,1)} %bitcast.33, bf16[2,4,32,2048]{3,2,1,0:T(8,128)(2,1)} %get-tuple-element.18.refs_3_.refs_2_.refs_1_, bf16[2,4,32,2048]{3,2,1,0:T(8,128)(2,1)} %copy-done.4, ...), custom_call_target="tpu_custom_call" | custom-call | flops 805306368 | bytes 5767168 | tf_op jit(solution)/shard_map/pallas_call | solution.py:140
  178.9 13.1 %shard_map.84.refs_2_ = f32[512,2048]{1,0:T(8,128)} custom-call(s32[4]{0:T(128)} %iota_clamp_fusion.source, s32[4]{0:T(128)} %compare_convert_fusion.valid, bf16[4,512,768]{2,1,0:T(8,128)(2,1)} %bitcast.34, bf16[4,2048,2048]{2,1,0:T(8,128)(2,1)} %bitcast.31, f32[512,2048]{1,0:T(8,128)} %shard_map.83.refs_2_), custom_call_target="tpu_custom_call" | custom-call | flops 6442450944 | bytes 24117248 | tf_op jit(solution)/shard_map/pallas_call | solution.py:75
  192.0 6.2 %shard_map.93.refs_0_ = bf16[512,32]{1,0:T(8,128)(2,1)} custom-call(s32[4]{0:T(128)} %iota_clamp_fusion.source, s32[4]{0:T(128)} %compare_convert_fusion.valid, bf16[4,512,512]{2,1,0:T(8,128)(2,1)} %bitcast.35, bf16[2,4,32,2048]{3,2,1,0:T(8,128)(2,1)} %get-tuple-element.18.refs_3_.refs_2_.refs_1_, bf16[2,4,32,2048]{3,2,1,0:T(8,128)(2,1)} %copy-done.4, ...), custom_call_target="tpu_custom_call" | custom-call | flops 536870912 | bytes 4194304 | tf_op jit(solution)/shard_map/pallas_call | solution.py:140
  198.2 2.4 %collective-permute-start.11 = (bf16[512,32]{1,0:T(8,128)(2,1)}, bf16[512,32]{1,0:T(8,128)(2,1)S(1)}, u32[]{:S(2)}, u32[]{:S(2)}) collective-permute-start(bf16[512,32]{1,0:T(8,128)(2,1)} %shard_map.93.refs_0_), channel_id=1, source_target_pairs={{0,12},{4,0},{8,4},{12,8},{1,13},{5,1},{9,5},{13,9},{2,14},{6,2},{... | collective-permute-start | bytes 98312 | tf_op jit(solution)/shard_map/ppermute | solution.py:318
  200.6 0.6 collective-permute-start.13
  201.2 10.6 %shard_map.92.total = f32[512,2048]{1,0:T(8,128)} custom-call(s32[4]{0:T(128)} %iota_clamp_fusion.source, s32[4]{0:T(128)} %compare_convert_fusion.valid, bf16[4,512,512]{2,1,0:T(8,128)(2,1)} %bitcast.36, bf16[4,2048,2048]{2,1,0:T(8,128)(2,1)} %bitcast.32, f32[512,2048]{1,0:T(8,128)} %shard_map.84.refs_2_), custom_call_target="tpu_custom_call" | custom-call | flops 4294967296 | bytes 18874368 | tf_op jit(solution)/shard_map/pallas_call | solution.py:75
  212.4 0.5 copy-done.7
  212.9 7.6 %shard_map.94 = bf16[512,2048]{1,0:T(8,128)(2,1)} custom-call(s32[1]{0:T(128)} %bitcast.me, s32[512,1]{1,0:T(8,128)} %copy.14.refs_6_.slot, f32[512,2048]{1,0:T(8,128)} %shard_map.92.total, bf16[512,32]{1,0:T(8,128)(2,1)} %shard_map.93.refs_0_, bf16[512,32]{1,0:T(8,128)(2,1)} %copy-done.6, bf16[512,32]{1,0:T(8,128)(2,1)} %copy-done.7, ...), custom_call_target="tpu_custom_call" | custom-call | flops 2147483648 | bytes 10485760 | tf_op jit(solution)/shard_map/pallas_call | solution.py:183
  (61 shorter events, 3.1 us)
Async XLA Ops:
  6.5 17.9 %copy-start = (s32[16]{0:T(128)S(1)}, s32[16]{0:T(128)}, u32[]{:S(2)}) copy-start(s32[16]{0:T(128)} %param.15) | copy-start | bytes 196
  6.5 15.4 %copy-start.10 = (s32[1,6]{1,0:T(1,128)S(1)}, s32[1,6]{1,0:T(1,128)}, u32[]{:S(2)}) copy-start(s32[1,6]{1,0:T(1,128)} %param.13) | copy-start | bytes 76
  6.5 18.6 %copy-start.11 = (s32[16]{0:T(128)S(1)}, s32[16]{0:T(128)}, u32[]{:S(2)}) copy-start(s32[16]{0:T(128)} %param.12) | copy-start | bytes 196
  6.5 166.7 %all-gather.7.cloned.1.call-start = ((), (), s32[]{:S(2)}) async-start(), calls=%async_computation.1 | async-start | bytes 3932160 | tf_op jit(solution)/shard_map/all_gather | solution.py:271
  8.7 183.3 %all-gather.5.cloned.1.call-start = ((), (), s32[]{:S(2)}) async-start(), calls=%async_computation | async-start | bytes 2621440 | tf_op jit(solution)/shard_map/all_gather | solution.py:271
  8.7 16.4 %collective-permute-start.5 = (s32[1,6]{1,0:T(1,128)}, s32[1,6]{1,0:T(1,128)S(1)}, u32[]{:S(2)}, u32[]{:S(2)}) collective-permute-start(s32[1,6]{1,0:T(1,128)} %param.13), channel_id=1, source_target_pairs={{0,1},{1,0},{2,3},{3,2},{4,5},{5,4},{6,7},{7,6},{8,9},{9,8},{10,11... | collective-permute-start | bytes 80 | tf_op jit(solution)/shard_map/ppermute | solution.py:228
  9.2 15.9 %collective-permute-start.7 = (s32[1,6]{1,0:T(1,128)}, s32[1,6]{1,0:T(1,128)S(1)}, u32[]{:S(2)}, u32[]{:S(2)}) collective-permute-start(s32[1,6]{1,0:T(1,128)} %param.13), channel_id=1, source_target_pairs={{0,2},{1,3},{2,0},{3,1},{4,6},{5,7},{6,4},{7,5},{8,10},{9,11},{10,... | collective-permute-start | bytes 80 | tf_op jit(solution)/shard_map/ppermute | solution.py:228
  11.8 13.3 %collective-permute-start.9 = (s32[1,6]{1,0:T(1,128)}, s32[1,6]{1,0:T(1,128)S(1)}, u32[]{:S(2)}, u32[]{:S(2)}) collective-permute-start(s32[1,6]{1,0:T(1,128)} %param.13), channel_id=1, source_target_pairs={{0,3},{1,2},{2,1},{3,0},{4,7},{5,6},{6,5},{7,4},{8,11},{9,10},{10,... | collective-permute-start | bytes 80 | tf_op jit(solution)/shard_map/ppermute | solution.py:228
  14.9 19.9 %copy-start.5 = (bf16[1,512,768]{2,1,0:T(8,128)(2,1)}, bf16[1,512,768]{2,1,0:T(8,128)(2,1)S(1)}, u32[]{:S(2)}) copy-start(bf16[1,512,768]{2,1,0:T(8,128)(2,1)S(1)} %slice_bitcast_fusion.refs_0_) | copy-start | bytes 2359300
  14.9 37.4 %collective-permute-start = (bf16[1,512,768]{2,1,0:T(8,128)(2,1)S(1)}, bf16[1,512,768]{2,1,0:T(8,128)(2,1)}, u32[]{:S(2)}, u32[]{:S(2)}) collective-permute-start(bf16[1,512,768]{2,1,0:T(8,128)(2,1)S(1)} %slice_bitcast_fusion.refs_0_), channel_id=1, source_target_pairs={{0,4},{4,8},{8,12},{1,5},{5,9},{9,13},{2,6},{6,10},{10,14},{3,7},{... | collective-permute-start | bytes 2359304 | tf_op jit(solution)/shard_map/ppermute | solution.py:279
  19.6 56.1 %collective-permute-start.2 = (bf16[1,512,768]{2,1,0:T(8,128)(2,1)S(1)}, bf16[1,512,768]{2,1,0:T(8,128)(2,1)}, u32[]{:S(2)}, u32[]{:S(2)}) collective-permute-start(bf16[1,512,768]{2,1,0:T(8,128)(2,1)S(1)} %slice_bitcast_fusion.refs_0_), channel_id=1, source_target_pairs={{4,0},{8,4},{12,8},{5,1},{9,5},{13,9},{6,2},{10,6},{14,10},{7,3},{... | collective-permute-start | bytes 2359304 | tf_op jit(solution)/shard_map/ppermute | solution.py:280
  29.6 97.8 %collective-permute-start.10 = (bf16[2,4,32,2048]{3,2,1,0:T(8,128)(2,1)}, bf16[2,4,32,2048]{3,2,1,0:T(8,128)(2,1)S(1)}, u32[]{:S(2)}, u32[]{:S(2)}) collective-permute-start(bf16[2,4,32,2048]{3,2,1,0:T(8,128)(2,1)} %get-tuple-element.21), channel_id=1, source_target_pairs={{0,3},{1,2},{2,1},{3,0},{4,7},{5,6},{6,5},{7,4},{8,11},{9,10},{10,... | collective-permute-start | bytes 3145736 | tf_op jit(solution)/shard_map/ppermute | solution.py:288
  34.8 46.3 %copy-start.9 = (s32[512]{0:T(512)S(1)}, s32[512]{0:T(512)}, u32[]{:S(2)}) copy-start(s32[512]{0:T(512)} %param.14) | copy-start | bytes 6148
  34.8 92.6 %collective-permute-start.8 = (bf16[2,4,32,2048]{3,2,1,0:T(8,128)(2,1)}, bf16[2,4,32,2048]{3,2,1,0:T(8,128)(2,1)S(1)}, u32[]{:S(2)}, u32[]{:S(2)}) collective-permute-start(bf16[2,4,32,2048]{3,2,1,0:T(8,128)(2,1)} %get-tuple-element.20), channel_id=1, source_target_pairs={{0,2},{1,3},{2,0},{3,1},{4,6},{5,7},{6,4},{7,5},{8,10},{9,11},{10,... | collective-permute-start | bytes 3145736 | tf_op jit(solution)/shard_map/ppermute | solution.py:288
  52.3 29.0 %collective-permute-start.1 = (bf16[1,512,768]{2,1,0:T(8,128)(2,1)}, bf16[1,512,768]{2,1,0:T(8,128)(2,1)}, u32[]{:S(2)}, u32[]{:S(2)}) collective-permute-start(bf16[1,512,768]{2,1,0:T(8,128)(2,1)} %collective-permute-done.refs_1_), channel_id=1, source_target_pairs={{4,8},{8,12},{5,9},{9,13},{6,10},{10,14},{7,11},{11,15},{20,24},{2... | collective-permute-start | bytes 2359304 | tf_op jit(solution)/shard_map/ppermute | solution.py:292
  75.6 31.1 %collective-permute-start.3 = (bf16[1,512,768]{2,1,0:T(8,128)(2,1)}, bf16[1,512,768]{2,1,0:T(8,128)(2,1)}, u32[]{:S(2)}, u32[]{:S(2)}) collective-permute-start(bf16[1,512,768]{2,1,0:T(8,128)(2,1)} %collective-permute-done.2.refs_2_), channel_id=1, source_target_pairs={{4,0},{8,4},{5,1},{9,5},{6,2},{10,6},{7,3},{11,7},{20,16},{24,20},... | collective-permute-start | bytes 2359304 | tf_op jit(solution)/shard_map/ppermute | solution.py:293
  81.0 47.1 %collective-permute-start.6 = (bf16[2,4,32,2048]{3,2,1,0:T(8,128)(2,1)}, bf16[2,4,32,2048]{3,2,1,0:T(8,128)(2,1)S(1)}, u32[]{:S(2)}, u32[]{:S(2)}) collective-permute-start(bf16[2,4,32,2048]{3,2,1,0:T(8,128)(2,1)} %get-tuple-element.19), channel_id=1, source_target_pairs={{0,1},{1,0},{2,3},{3,2},{4,5},{5,4},{6,7},{7,6},{8,9},{9,8},{10,11... | collective-permute-start | bytes 3145736 | tf_op jit(solution)/shard_map/ppermute | solution.py:288
  108.9 50.3 %collective-permute-start.4 = (bf16[1,512,768]{2,1,0:T(8,128)(2,1)}, bf16[1,512,768]{2,1,0:T(8,128)(2,1)}, u32[]{:S(2)}, u32[]{:S(2)}) collective-permute-start(bf16[1,512,768]{2,1,0:T(8,128)(2,1)} %broadcast_select_fusion.refs_0_), channel_id=1, source_target_pairs={{8,12},{4,0},{9,13},{5,1},{10,14},{6,2},{11,15},{7,3},{24,28},{20,... | collective-permute-start | bytes 2359304 | tf_op jit(solution)/shard_map/ppermute | solution.py:296
  115.7 84.8 %collective-permute-start.15 = (bf16[2,128,2048]{2,1,0:T(8,128)(2,1)}, bf16[2,128,2048]{2,1,0:T(8,128)(2,1)}, u32[]{:S(2)}, u32[]{:S(2)}) collective-permute-start(bf16[2,128,2048]{2,1,0:T(8,128)(2,1)} %get-tuple-element.25), channel_id=1, source_target_pairs={{0,2},{1,3},{2,0},{3,1},{4,6},{5,7},{6,4},{7,5},{8,10},{9,11},{10,... | collective-permute-start | bytes 3145736 | tf_op jit(solution)/shard_map/ppermute | solution.py:288
  127.4 1.0 copy-start.2
  127.4 84.3 %collective-permute-start.16 = (bf16[2,128,2048]{2,1,0:T(8,128)(2,1)}, bf16[2,128,2048]{2,1,0:T(8,128)(2,1)}, u32[]{:S(2)}, u32[]{:S(2)}) collective-permute-start(bf16[2,128,2048]{2,1,0:T(8,128)(2,1)} %get-tuple-element.26), channel_id=1, source_target_pairs={{0,3},{1,2},{2,1},{3,0},{4,7},{5,6},{6,5},{7,4},{8,11},{9,10},{10,... | collective-permute-start | bytes 3145736 | tf_op jit(solution)/shard_map/ppermute | solution.py:288
  127.5 1.2 copy-start.3
  127.5 84.2 %collective-permute-start.14 = (bf16[2,128,2048]{2,1,0:T(8,128)(2,1)}, bf16[2,128,2048]{2,1,0:T(8,128)(2,1)}, u32[]{:S(2)}, u32[]{:S(2)}) collective-permute-start(bf16[2,128,2048]{2,1,0:T(8,128)(2,1)} %get-tuple-element.24), channel_id=1, source_target_pairs={{0,1},{1,0},{2,3},{3,2},{4,5},{5,4},{6,7},{7,6},{8,9},{9,8},{10,11... | collective-permute-start | bytes 3145736 | tf_op jit(solution)/shard_map/ppermute | solution.py:288
  128.1 1.0 copy-start.4
  198.2 13.5 %collective-permute-start.11 = (bf16[512,32]{1,0:T(8,128)(2,1)}, bf16[512,32]{1,0:T(8,128)(2,1)S(1)}, u32[]{:S(2)}, u32[]{:S(2)}) collective-permute-start(bf16[512,32]{1,0:T(8,128)(2,1)} %shard_map.93.refs_0_), channel_id=1, source_target_pairs={{0,12},{4,0},{8,4},{12,8},{1,13},{5,1},{9,5},{13,9},{2,14},{6,2},{... | collective-permute-start | bytes 98312 | tf_op jit(solution)/shard_map/ppermute | solution.py:318
  200.6 11.6 %collective-permute-start.12 = (bf16[512,32]{1,0:T(8,128)(2,1)}, bf16[512,32]{1,0:T(8,128)(2,1)S(1)}, u32[]{:S(2)}, u32[]{:S(2)}) collective-permute-start(bf16[512,32]{1,0:T(8,128)(2,1)} %shard_map.93.refs_0_), channel_id=1, source_target_pairs={{0,8},{4,12},{8,0},{12,4},{1,9},{5,13},{9,1},{13,5},{2,10},{6,14},... | collective-permute-start | bytes 98312 | tf_op jit(solution)/shard_map/ppermute | solution.py:318
  200.6 11.6 %collective-permute-start.13 = (bf16[512,32]{1,0:T(8,128)(2,1)}, bf16[512,32]{1,0:T(8,128)(2,1)S(1)}, u32[]{:S(2)}, u32[]{:S(2)}) collective-permute-start(bf16[512,32]{1,0:T(8,128)(2,1)} %shard_map.93.refs_0_), channel_id=1, source_target_pairs={{0,4},{4,8},{8,12},{12,0},{1,5},{5,9},{9,13},{13,1},{2,6},{6,10},{... | collective-permute-start | bytes 98312 | tf_op jit(solution)/shard_map/ppermute | solution.py:318
  211.7 0.7 copy-start.6
  212.2 0.6 copy-start.7
  212.2 0.7 copy-start.8
  212.2 8.3 %copy-start.1 = (s32[16]{0:T(128)S(1)}, s32[16]{0:T(128)}, u32[]{:S(2)}) copy-start(s32[16]{0:T(128)} %param.15) | copy-start | bytes 196
Sparse Core Ops, SparseCore 0:
  8.9 88.4 all-gather.6
  99.0 57.5 all-gather.4

commit v5 on v4

v5 whole, which is shorter than its diff:
```python
import functools

import jax
import jax.numpy as jnp
from jax import lax
from jax.experimental import pallas as pl
from jax.experimental.pallas import tpu as pltpu
from jax.sharding import PartitionSpec as P

CAP = 2
LINE = 512
GATHERED = (1024, 512)
PARAMS = pltpu.CompilerParams(vmem_limit_bytes=60 * 2**20)
F32 = jnp.float32
BF16 = jnp.bfloat16


def pick_kernel(places, down, up, down_out, up_out):
    shards, _, width = down_out.shape[1:]
    for t in range(shards):
        down_out[0, t] = down[0, :, t * width:(t + 1) * width]
    up_out[...] = up[...]


def pick_pages(places, down, up, shards):
    count = places.shape[0]
    _, rank_part, features = down.shape
    shapes = [(shards, rank_part, features // shards), up.shape[1:]]
    return pl.pallas_call(
        pick_kernel,
        out_shape=[jax.ShapeDtypeStruct((count,) + shape, BF16) for shape in shapes],
        grid_spec=pltpu.PrefetchScalarGridSpec(
            num_scalar_prefetch=1,
            grid=(count,),
            in_specs=[pl.BlockSpec((1,) + a.shape[1:], lambda i, places: (places[i], 0, 0)) for a in (down, up)],
            out_specs=[
                pl.BlockSpec((1,) + shapes[0], lambda i, places: (i, 0, 0, 0)),
                pl.BlockSpec((1,) + shapes[1], lambda i, places: (i, 0, 0)),
            ],
        ),
        compiler_params=PARAMS,
    )(places, down, up)


def join_kernel(by_shard, *refs):
    *pages, out = refs
    if by_shard:
        out[0] = jnp.concatenate([p[c, 0] for p in pages for c in range(CAP)], axis=0)
        return
    for j, p in enumerate(pages):

        @pl.when(pl.program_id(0) == j)
        def _():
            out[...] = p[...]


def join_downs(downs):
    _, shards, rank_part, features = downs[0].shape
    slots = CAP * rank_part * len(downs)
    return pl.pallas_call(
        functools.partial(join_kernel, True),
        out_shape=jax.ShapeDtypeStruct((shards, slots, features), BF16),
        grid=(shards,),
        in_specs=[pl.BlockSpec((CAP, 1, rank_part, features), lambda t: (0, t, 0, 0))] * len(downs),
        out_specs=pl.BlockSpec((1, slots, features), lambda t: (t, 0, 0)),
        compiler_params=PARAMS,
    )(*downs)


def join_ups(ups):
    count, rank, columns = ups[0].shape
    return pl.pallas_call(
        functools.partial(join_kernel, False),
        out_shape=jax.ShapeDtypeStruct((count * len(ups), rank, columns), BF16),
        grid=(len(ups),),
        in_specs=[pl.BlockSpec(up.shape, lambda j: (0, 0, 0)) for up in ups],
        out_specs=pl.BlockSpec(ups[0].shape, lambda j: (j, 0, 0)),
        compiler_params=PARAMS,
    )(*ups).reshape(-1, columns)


def depth_of(weight):
    return weight[...].reshape(-1, weight.shape[-1])


def chunk_kernel(spans, has_total, source, valid, *refs):
    refs = list(refs)
    count = len(spans)
    xs, weights, downs = (refs[i * count:(i + 1) * count] for i in range(3))
    totals, (base, low) = refs[3 * count:-2], refs[-2:]

    def base_of(i):
        return jnp.dot(xs[i][...], depth_of(weights[i]), preferred_element_type=F32)

    def low_of(i):
        f = downs[i].shape[-1]
        return sum(
            lax.dot_general(
                xs[i][:, t * f:(t + 1) * f], downs[i][t], (((1,), (1,)), ((), ())), preferred_element_type=F32
            )
            for t in range(spans[i])
        )

    start = pl.program_id(0) == 0
    base[...] = totals[0][...] + base_of(0) if has_total else base_of(0)

    @pl.when(start)
    def _():
        low[...] = totals[1][...] + low_of(0) if has_total else low_of(0)

    for i in range(1, count):

        @pl.when(valid[i] != 0)
        def _():
            base[...] += base_of(i)

        @pl.when((valid[i] != 0) & start)
        def _():
            low[...] += low_of(i)


def add_chunk(totals, blocks, source, weight, down):
    n_tensor, _, columns = weight.shape
    slots = down.shape[1]
    rows = blocks[0][0].shape[0]
    part = min(columns, 512)
    valid = ((source >= 0) & (source < n_tensor)).astype(jnp.int32)
    source = jnp.clip(source, 0, n_tensor - 1).astype(jnp.int32)
    x_specs, weight_specs, down_specs, depth = [], [], [], 0
    for i, (x, span, first) in enumerate(blocks):
        f = x.shape[1] // span

        def place(source, i=i, span=span, at=first // f):
            return (0 if span > 1 else source[i]), at

        x_specs.append(pl.BlockSpec(x.shape, lambda n, *_: (0, 0)))
        weight_specs.append(
            pl.BlockSpec((span, f, part), lambda n, source, valid, place=place: place(source) + (n,))
        )
        down_specs.append(
            pl.BlockSpec(
                (span, slots, f),
                lambda n, source, valid, place=place: (place(source)[0], 0, place(source)[1]),
            )
        )
        depth += x.shape[1]
    tile = pl.BlockSpec((rows, part), lambda n, *_: (0, n))
    whole = pl.BlockSpec((rows, slots), lambda n, *_: (0, 0))
    return pl.pallas_call(
        functools.partial(chunk_kernel, [span for _, span, _ in blocks], bool(totals)),
        out_shape=[jax.ShapeDtypeStruct((rows, columns), F32), jax.ShapeDtypeStruct((rows, slots), F32)],
        grid_spec=pltpu.PrefetchScalarGridSpec(
            num_scalar_prefetch=2,
            grid=(columns // part,),
            in_specs=x_specs + weight_specs + down_specs + ([tile, whole] if totals else []),
            out_specs=[tile, whole],
        ),
        compiler_params=PARAMS,
        cost_estimate=pl.CostEstimate(
            flops=2 * depth * rows * (columns + slots),
            bytes_accessed=2 * depth * (rows + columns + slots) + 8 * rows * (columns + slots),
            transcendentals=0,
        ),
    )(source, valid, *[x for x, _, _ in blocks], *[weight] * len(blocks), *[down] * len(blocks), *totals)


def base_kernel(x, weight, total, out):
    out[...] = total[...] + jnp.dot(x[...], depth_of(weight), preferred_element_type=F32)


def add_base(total, x, first, weight):
    shards, _, columns = weight.shape
    rows, depth = x.shape
    features = depth // shards
    part = min(columns, 512)
    tile = pl.BlockSpec((rows, part), lambda n: (0, n))
    return pl.pallas_call(
        base_kernel,
        out_shape=jax.ShapeDtypeStruct((rows, columns), F32),
        grid=(columns // part,),
        in_specs=[
            pl.BlockSpec((rows, depth), lambda n: (0, 0)),
            pl.BlockSpec((shards, features, part), lambda n: (0, first // features, n)),
            tile,
        ],
        out_specs=tile,
        compiler_params=PARAMS,
        cost_estimate=pl.CostEstimate(
            flops=2 * depth * rows * columns,
            bytes_accessed=2 * depth * (rows + columns) + 8 * rows * columns,
            transcendentals=0,
        ),
    )(x, weight, total)


def low_kernel(x, down, total, slot, live, out, acc):
    step = pl.program_id(0)
    rank_part = out.shape[1]

    @pl.when(step == 0)
    def _():
        acc[...] = total[...]

    acc[...] += lax.dot_general(x[...], down[0], (((1,), (1,)), ((), ())), preferred_element_type=F32)

    @pl.when(step == pl.num_programs(0) - 1)
    def _():
        mine = jnp.zeros(out.shape, F32)
        for e in range(acc.shape[1] // rank_part):
            mine += jnp.where(slot[...] == e, acc[:, e * rank_part:(e + 1) * rank_part], 0.0)
        k = lax.broadcasted_iota(jnp.int32, mine.shape, 1)
        out[...] = jnp.where(k < live[...], mine, 0.0).astype(BF16)


def finish_low(total, x, first, down, slot, live, rank_part):
    shards, slots, _ = down.shape
    rows, depth = x.shape
    features = depth // shards
    column = pl.BlockSpec((rows, 1), lambda t: (0, 0))
    return pl.pallas_call(
        low_kernel,
        out_shape=jax.ShapeDtypeStruct((rows, rank_part), BF16),
        grid=(shards,),
        in_specs=[
            pl.BlockSpec((rows, features), lambda t: (0, t)),
            pl.BlockSpec((1, slots, features), lambda t: (t, 0, first // features)),
            pl.BlockSpec((rows, slots), lambda t: (0, 0)),
            column,
            column,
        ],
        out_specs=pl.BlockSpec((rows, rank_part), lambda t: (0, 0)),
        scratch_shapes=[pltpu.VMEM((rows, slots), F32)],
        compiler_params=PARAMS,
        cost_estimate=pl.CostEstimate(
            flops=2 * depth * rows * slots,
            bytes_accessed=2 * depth * (rows + slots) + 4 * rows * slots,
            transcendentals=0,
        ),
    )(x, down, total, slot, live)


def finish_kernel(parts, me, slot, total, up, *refs):
    lows, (out, spread) = refs[:parts], refs[parts:]
    rank_part = lows[0].shape[1]
    rank = parts * rank_part

    @pl.when(pl.program_id(0) == 0)
    def _():
        low = jnp.concatenate([part[...].astype(F32) for part in lows], axis=1)
        low = pltpu.roll(low, me[0] * rank_part, 1)
        for e in range(spread.shape[1] // rank):
            spread[:, e * rank:(e + 1) * rank] = jnp.where(slot[...] == e, low, 0.0).astype(BF16)

    out[...] = (total[...] + jnp.dot(spread[...], up[...], preferred_element_type=F32)).astype(BF16)


def finish(me, slot, total, up, lows):
    rows, columns = total.shape
    depth = up.shape[0]
    rank_part = lows[0].shape[1]
    part = min(columns, 512)
    return pl.pallas_call(
        functools.partial(finish_kernel, len(lows)),
        grid=(columns // part,),
        out_shape=jax.ShapeDtypeStruct((rows, columns), BF16),
        in_specs=[
            pl.BlockSpec(memory_space=pltpu.SMEM),
            pl.BlockSpec((rows, 1), lambda n: (0, 0)),
            pl.BlockSpec((rows, part), lambda n: (0, n)),
            pl.BlockSpec((depth, part), lambda n: (0, n)),
        ] + [pl.BlockSpec((rows, rank_part), lambda n: (0, 0))] * len(lows),
        out_specs=pl.BlockSpec((rows, part), lambda n: (0, n)),
        scratch_shapes=[pltpu.VMEM((rows, depth), BF16)],
        compiler_params=PARAMS,
        cost_estimate=pl.CostEstimate(
            flops=2 * rows * depth * columns,
            bytes_accessed=6 * rows * columns + 2 * depth * columns,
            transcendentals=0,
        ),
    )(me, slot, total, up, *lows)


def after(value, *earlier):
    return lax.optimization_barrier((value,) + earlier)[0]


def asked_pages(requests, adapter_page_row, holder_length):
    n_dp = lax.axis_size("dp")
    dp = lax.axis_index("dp")
    count = adapter_page_row.shape[0]

    def pages_of(wanted):
        hit = wanted[:, None] == jnp.arange(count)[None, :]
        return jnp.sum(jnp.where(hit, adapter_page_row[None, :], 0), axis=1)

    def order_in(holders):
        same = holders[:, None] == holders[None, :]
        n = holders.shape[0]
        earlier = jnp.arange(n)[:, None] > jnp.arange(n)[None, :]
        return jnp.sum((same & earlier).astype(jnp.int32), axis=1)

    own = pages_of(requests[0])
    holders = own // holder_length
    slots = (holders ^ dp) * CAP + order_in(holders)
    places = []
    for j in range(n_dp):
        wanted = requests if j == 0 else lax.ppermute(requests, "dp", [(i, i ^ j) for i in range(n_dp)])
        pages = pages_of(wanted[0])
        holder = pages // holder_length
        order = jnp.where(holder == dp, order_in(holder), -1)
        hit = order[None, :] == jnp.arange(CAP)[:, None]
        places.append(jnp.sum(jnp.where(hit, (pages % holder_length)[None, :], 0), axis=1))
    return slots, places


def local(
    attention_result,
    output_weight,
    adapter_down_weight,
    adapter_up_weight,
    adapter_page_row,
    requests,
    row_request_entry,
    ranks,
):
    n_dp = lax.axis_size("dp")
    n_tensor = lax.axis_size("tensor")
    me = lax.axis_index("tensor")
    rows, width = attention_result.shape
    holder_length, rank_part, _ = adapter_down_weight.shape
    rank, columns = adapter_up_weight.shape[1:]
    own_list = requests[0]
    entries = own_list.shape[0]
    one_hot = row_request_entry[:, None] == jnp.arange(entries)[None, :]
    row_rank = jnp.sum(jnp.where(one_hot, ranks[own_list][None, :], 0), axis=1)
    if n_tensor != 4 or width != LINE + sum(GATHERED) or rank_part % 16:
        return plain(
            attention_result, output_weight, adapter_down_weight, adapter_up_weight, adapter_page_row,
            own_list, one_hot, row_rank,
        )

    weight = output_weight.reshape(n_tensor, width, columns)
    gathered, x, first = [], attention_result, 0
    for features in GATHERED:
        piece = x[:, first:first + features]
        gathered.append(lax.all_gather(piece, "tensor", axis=1, tiled=True))
        x = after(x, piece)
        first += features + LINE

    middle = GATHERED[0]
    last = middle + LINE
    line = x[:, middle:last]
    right = [(i, i + 1) for i in range(n_tensor - 1)]
    left = [(i + 1, i) for i in range(n_tensor - 1)]
    right_1 = lax.ppermute(line, "tensor", right)
    left_1 = lax.ppermute(line, "tensor", left)

    slots, places = asked_pages(requests, adapter_page_row, holder_length)
    downs, ups = [], []
    for j in range(n_dp):
        down, up = pick_pages(places[j], adapter_down_weight, adapter_up_weight, n_tensor)
        if j:
            pairs = [(i, i ^ j) for i in range(n_dp)]
            down, up = lax.ppermute(down, "dp", pairs), lax.ppermute(up, "dp", pairs)
        downs.append(down)
        ups.append(up)

    right_2 = lax.ppermute(right_1, "tensor", right[1:])
    left_2 = lax.ppermute(left_1, "tensor", left[:-1])
    upper = me >= n_tensor // 2
    second = jnp.where(upper, right_2, left_2)
    third = lax.ppermute(second, "tensor", right[-1:] + left[:1])

    down = join_downs(after(tuple(downs), third))
    up = join_ups(ups)

    slot = jnp.sum(jnp.where(one_hot, slots[None, :], 0), axis=1)[:, None]
    live = row_rank[:, None] - me * rank_part
    near = jnp.stack([me, me - 1, me + 1])
    totals = add_chunk((), [(line, 1, middle), (right_1, 1, middle), (left_1, 1, middle)], near, weight, down)
    far = jnp.where(upper, jnp.stack([me - 2, me - 3, me]), jnp.stack([me + 2, me + 3, me]))
    totals = add_chunk(
        totals, [(second, 1, middle), (third, 1, middle), (gathered[0], n_tensor, 0)], far, weight, down
    )
    x = after(gathered[1], *totals, up)
    low = finish_low(totals[1], x, last, down, slot, live, rank_part)
    base = add_base(totals[0], x, last, weight)
    lows = [low] + [
        lax.ppermute(low, "tensor", [(i, (i - j) % n_tensor) for i in range(n_tensor)])
        for j in range(1, n_tensor)
    ]
    return finish(me[None], slot, base, up, lows)


def gather_pages(block, n_dp):
    return [block] + [
        lax.ppermute(block, "dp", [(i, i ^ j) for i in range(n_dp)]) for j in range(1, n_dp)
    ]


def plain(x, output_weight, down_weight, up_weight, adapter_page_row, own_list, one_hot, row_rank):
    n_dp = lax.axis_size("dp")
    dp = lax.axis_index("dp")
    rows = x.shape[0]
    holder_length = down_weight.shape[0]
    rank, columns = up_weight.shape[1:]
    entries = one_hot.shape[1]
    pages = adapter_page_row[own_list]
    places = ((pages // holder_length) ^ dp) * holder_length + pages % holder_length

    def requested(block):
        blocks = jnp.concatenate(gather_pages(block, n_dp), axis=0)
        return jnp.concatenate(
            [lax.dynamic_slice_in_dim(blocks, places[e], 1, 0) for e in range(entries)], axis=0
        )

    down, up = requested(down_weight), requested(up_weight)
    x = lax.all_gather(x, "tensor", axis=1, tiled=True)
    base = jnp.dot(x, output_weight, preferred_element_type=F32)
    low = jnp.einsum("rd,ekd->rek", x, down, preferred_element_type=F32)
    low = jnp.sum(jnp.where(one_hot[:, :, None], low, 0.0), axis=1).astype(BF16)
    low = lax.all_gather(low, "tensor", axis=1, tiled=True)
    low = jnp.where(jnp.arange(rank)[None, :] < row_rank[:, None], low, jnp.zeros_like(low))
    spread = jnp.where(one_hot[:, :, None], low[:, None, :], jnp.zeros((), BF16))
    term = jnp.dot(
        spread.reshape(rows, entries * rank), up.reshape(entries * rank, columns), preferred_element_type=F32
    )
    return (base + term).astype(BF16)


def solution(mesh):
    in_specs = (
        P(("groups", "dp"), "tensor"),
        P(None, "tensor"),
        P("dp", "tensor", None),
        P("dp", None, "tensor"),
        P("groups"),
        P(("groups", "dp"), None),
        P(("groups", "dp")),
        P(),
    )
    out_specs = P(("groups", "dp"), "tensor")
    return jax.shard_map(local, mesh=mesh, in_specs=in_specs, out_specs=out_specs, check_vma=False)
```

time: 228 us -> 197 us (0.86)
  waiting for transfers between devices: 89.3 us -> 69.9 us
  Pallas kernels: 85.8 us -> 77.4 us
  other arithmetic: 9.29 us -> 6.98 us
    ppermute x1, waiting for transfers between devices: 25 us -> 5.84 us  [local(): third = lax.ppermute(second, 'tensor', right[-1:] + left[:1])]
    ppermute x6, waiting for transfers between devices: 0.02 us -> 13.2 us  [local(): down, up = (lax.ppermute(down, 'dp', pairs), lax.ppermute(up, 'dp', pairs))]
    ppermute x1, waiting for transfers between devices: 16.7 us -> 5.83 us  [local(): right_1 = lax.ppermute(line, 'tensor', right)]
    pallas_call x9 -> x7, Pallas kernels: 72.4 us -> 64 us  [the longest x2 31.7 us: add_chunk(): pl.pallas_call(functools.partial(chunk_kernel, [span for _, span, _ in bl...]
    ppermute x1, waiting for transfers between devices: 21.7 us -> 15.6 us  [local(): left_1 = lax.ppermute(line, 'tensor', left)]
    ppermute x1, waiting for transfers between devices: 25.5 us -> 28.6 us  [local(): left_2 = lax.ppermute(left_1, 'tensor', left[:-1])]
    slice x2 -> x3, local copies, waits for them, and re-layouts: 3.97 us -> 5.24 us  [the longest x2 4.16 us: local(): piece = x[:, first:first + features]]
  transfers between devices with their start and end apart: 19 -> 19, of which waited for: 5 -> 7; matrix products, arithmetic and copies ran while one was open for 6% -> 6% of each run, Pallas kernels for 34% -> 33%
where the time goes in v5:
time: 197 us; the launch traced here: 196 us
  Pallas kernels  77.4 us (39%)
  waiting for transfers between devices  69.9 us (35%)
  starting transfers between devices  18.9 us (10%)
  between operations  13.6 us (7%)
  local copies, waits for them, and re-layouts  9.22 us (5%)
  other arithmetic  6.98 us (4%)
    pallas_call x2, Pallas kernels, add_chunk(): pl.pallas_call(functools.partial(chunk_kernel, [span for _, span, _ in bl...  31.7 us
    ppermute x1, waiting for transfers between devices, local(): left_2 = lax.ppermute(left_1, 'tensor', left[:-1])  28.6 us
    ppermute x1, waiting for transfers between devices, local(): left_1 = lax.ppermute(line, 'tensor', left)  15.6 us
    pallas_call x4, Pallas kernels, pick_pages(): pl.pallas_call(pick_kernel, out_shape=[jax.ShapeDtypeStruct((count,) + sh...  13.4 us
    ppermute x6, waiting for transfers between devices, local(): down, up = (lax.ppermute(down, 'dp', pairs), lax.ppermute(up, 'dp', pairs))  13.2 us
    pallas_call x1, Pallas kernels, add_base(): pl.pallas_call(base_kernel, out_shape=jax.ShapeDtypeStruct((rows, columns...  9.9 us
    pallas_call x1, Pallas kernels, finish(): pl.pallas_call(functools.partial(finish_kernel, len(lows)), grid=(columns...  7.46 us
    ppermute x1, waiting for transfers between devices, local(): third = lax.ppermute(second, 'tensor', right[-1:] + left[:1])  5.84 us
  transfers between devices with their start and end apart: 19, of which 7 were waited for; matrix products, arithmetic and copies ran while one was open for 6% of the time, Pallas kernels for 33%

profile of v5, /device:TPU:0, one launch (start us, length us, event | category | flops | bytes accessed | tf_op | source)
XLA Modules:
  0.0 196.0 jit_solution(7984950474095625292)
XLA Ops:
  6.5 2.3 %slice.9 = bf16[512,1024]{1,0:T(8,128)(2,1)} slice(bf16[512,2048]{1,0:T(8,128)(2,1)} %param.8), slice={[0:512], [0:1024]} | slice | bytes 2097152 | tf_op jit(solution)/shard_map/slice | solution.py:345
  8.9 2.4 %collective-permute-start.9 = (s32[1,6]{1,0:T(1,128)}, s32[1,6]{1,0:T(1,128)S(1)}, u32[]{:S(2)}, u32[]{:S(2)}) collective-permute-start(s32[1,6]{1,0:T(1,128)} %param.13), channel_id=1, source_target_pairs={{0,3},{1,2},{2,1},{3,0},{4,7},{5,6},{6,5},{7,4},{8,11},{9,10},{10,... | collective-permute-start | bytes 80 | tf_op jit(solution)/shard_map/ppermute | solution.py:307
  11.3 0.7 collective-permute-start.5
  12.1 1.9 slice.10
  13.9 1.1 slice.11.refs_0_
  15.0 4.0 %collective-permute-start = (bf16[512,512]{1,0:T(8,128)(2,1)S(1)}, bf16[512,512]{1,0:T(8,128)(2,1)S(1)}, u32[]{:S(2)}, u32[]{:S(2)}) collective-permute-start(bf16[512,512]{1,0:T(8,128)(2,1)S(1)} %slice.11.refs_0_), channel_id=1, source_target_pairs={{0,4},{4,8},{8,12},{1,5},{5,9},{9,13},{2,6},{6,10},{10,14},{3,7},{... | collective-permute-start | bytes 1572872 | tf_op jit(solution)/shard_map/ppermute | solution.py:355
  19.0 1.3 collective-permute-start.2
  20.4 0.6 and_convert_fusion
  21.0 0.5 broadcast_clamp_fusion.source
  21.5 0.6 and_convert_fusion.1
  22.1 0.5 broadcast_clamp_fusion.1.source
  22.6 0.6 gather_fusion
  23.7 0.6 fusion.6.places
  24.3 3.3 %shard_map.84 = (bf16[2,4,32,2048]{3,2,1,0:T(8,128)(2,1)}, bf16[2,128,2048]{2,1,0:T(8,128)(2,1)}) custom-call(s32[2]{0:T(128)} %fusion.6.places, bf16[4,32,8192]{2,1,0:T(8,128)(2,1)} %down.7, bf16[4,128,2048]{2,1,0:T(8,128)(2,1)} %up.7), custom_call_target="tpu_custom_call" | custom-call | tf_op jit(solution)/shard_map/pallas_call | solution.py:29
  27.6 1.5 collective-permute-start.12
  29.3 0.6 fusion.7.places
  30.0 3.4 %shard_map.85 = (bf16[2,4,32,2048]{3,2,1,0:T(8,128)(2,1)}, bf16[2,128,2048]{2,1,0:T(8,128)(2,1)}) custom-call(s32[2]{0:T(128)} %fusion.7.places, bf16[4,32,8192]{2,1,0:T(8,128)(2,1)} %down.7, bf16[4,128,2048]{2,1,0:T(8,128)(2,1)} %up.7), custom_call_target="tpu_custom_call" | custom-call | tf_op jit(solution)/shard_map/pallas_call | solution.py:29
  33.3 1.7 collective-permute-start.13
  35.1 5.8 %collective-permute-done.refs_1_ = bf16[512,512]{1,0:T(8,128)(2,1)S(1)} collective-permute-done((bf16[512,512]{1,0:T(8,128)(2,1)S(1)}, bf16[512,512]{1,0:T(8,128)(2,1)S(1)}, u32[]{:S(2)}, u32[]{:S(2)}) %collective-permute-start) | collective-permute-done | bytes 524320 | tf_op jit(solution)/shard_map/ppermute | solution.py:355
  40.9 0.7 collective-permute-start.1
  41.6 15.6 %collective-permute-done.2.refs_2_ = bf16[512,512]{1,0:T(8,128)(2,1)} collective-permute-done((bf16[512,512]{1,0:T(8,128)(2,1)S(1)}, bf16[512,512]{1,0:T(8,128)(2,1)}, u32[]{:S(2)}, u32[]{:S(2)}) %collective-permute-start.2) | collective-permute-done | bytes 524320 | tf_op jit(solution)/shard_map/ppermute | solution.py:356
  57.2 1.3 collective-permute-start.3
  58.7 0.6 fusion.5.places
  59.3 3.5 %shard_map.83 = (bf16[2,4,32,2048]{3,2,1,0:T(8,128)(2,1)}, bf16[2,128,2048]{2,1,0:T(8,128)(2,1)}) custom-call(s32[2]{0:T(128)} %fusion.5.places, bf16[4,32,8192]{2,1,0:T(8,128)(2,1)} %down.7, bf16[4,128,2048]{2,1,0:T(8,128)(2,1)} %up.7), custom_call_target="tpu_custom_call" | custom-call | tf_op jit(solution)/shard_map/pallas_call | solution.py:29
  62.8 1.3 collective-permute-start.8
  64.1 28.6 %collective-permute-done.3 = bf16[512,512]{1,0:T(8,128)(2,1)S(1)} collective-permute-done((bf16[512,512]{1,0:T(8,128)(2,1)}, bf16[512,512]{1,0:T(8,128)(2,1)S(1)}, u32[]{:S(2)}, u32[]{:S(2)}) %collective-permute-start.3) | collective-permute-done | bytes 524320 | tf_op jit(solution)/shard_map/ppermute | solution.py:369
  92.8 0.5 collective-permute-start.11
  93.7 1.1 broadcast_select_fusion.refs_0_
  94.8 3.2 %collective-permute-done.13.refs_3_ = bf16[2,128,2048]{2,1,0:T(8,128)(2,1)} collective-permute-done((bf16[2,128,2048]{2,1,0:T(8,128)(2,1)}, bf16[2,128,2048]{2,1,0:T(8,128)(2,1)}, u32[]{:S(2)}, u32[]{:S(2)}) %collective-permute-start.13) | collective-permute-done | bytes 1048608 | tf_op jit(solution)/shard_map/ppermute | solution.py:364
  98.0 1.3 collective-permute-start.4
  99.3 0.7 fusion.4.places
  100.0 3.3 %shard_map.82 = (bf16[2,4,32,2048]{3,2,1,0:T(8,128)(2,1)}, bf16[2,128,2048]{2,1,0:T(8,128)(2,1)}) custom-call(s32[2]{0:T(128)} %fusion.4.places, bf16[4,32,8192]{2,1,0:T(8,128)(2,1)} %down.7, bf16[4,128,2048]{2,1,0:T(8,128)(2,1)} %up.7), custom_call_target="tpu_custom_call" | custom-call | tf_op jit(solution)/shard_map/pallas_call | solution.py:29
  103.4 0.9 copy.13.live
  104.3 0.9 copy.14.slot
  105.2 4.7 %shard_map.89 = bf16[8,128,2048]{2,1,0:T(8,128)(2,1)} custom-call(bf16[2,128,2048]{2,1,0:T(8,128)(2,1)} %get-tuple-element.38.refs_0_, bf16[2,128,2048]{2,1,0:T(8,128)(2,1)} %collective-permute-done.11.refs_1_, bf16[2,128,2048]{2,1,0:T(8,128)(2,1)} %copy-done.5, bf16[2,128,2048]{2,1,0:T(8,128)(2,1)} %collective-permute-done.13.refs_3_), custom_call_target="tpu_custom_call" | custom-call | tf_op jit(solution)/shard_map/pallas_call | solution.py:72
  109.9 10.0 %collective-permute-done.8.refs_2_ = bf16[2,4,32,2048]{3,2,1,0:T(8,128)(2,1)} collective-permute-done((bf16[2,4,32,2048]{3,2,1,0:T(8,128)(2,1)}, bf16[2,4,32,2048]{3,2,1,0:T(8,128)(2,1)}, u32[]{:S(2)}, u32[]{:S(2)}) %collective-permute-start.8) | collective-permute-done | bytes 1048608 | tf_op jit(solution)/shard_map/ppermute | solution.py:364
  119.9 5.8 %collective-permute-done.4.refs_1_ = bf16[512,512]{1,0:T(8,128)(2,1)} collective-permute-done((bf16[512,512]{1,0:T(8,128)(2,1)S(1)}, bf16[512,512]{1,0:T(8,128)(2,1)}, u32[]{:S(2)}, u32[]{:S(2)}) %collective-permute-start.4) | collective-permute-done | bytes 524320 | tf_op jit(solution)/shard_map/ppermute | solution.py:372
  125.7 4.7 %shard_map.86.refs_6_.refs_7_.refs_8_.down = bf16[4,256,2048]{2,1,0:T(8,128)(2,1)} custom-call(bf16[2,4,32,2048]{3,2,1,0:T(8,128)(2,1)} %get-tuple-element.30.refs_0_, bf16[2,4,32,2048]{3,2,1,0:T(8,128)(2,1)} %collective-permute-done.6.refs_1_, bf16[2,4,32,2048]{3,2,1,0:T(8,128)(2,1)} %collective-permute-done.8.refs_2_, bf16[2,4,32,2048]{3,2,1,0:T(8,128)(2,1)} %copy-done.4), custom_call_target="tpu_custom_call" | custom-call | tf_op jit(solution)/shard_map/pallas_call | solution.py:60
  130.4 9.5 %shard_map.87 = (f32[512,2048]{1,0:T(8,128)}, f32[512,256]{1,0:T(8,128)}) custom-call(s32[3]{0:T(128)} %broadcast_clamp_fusion.source, s32[3]{0:T(128)} %get-tuple-element.49.valid, bf16[512,512]{1,0:T(8,128)(2,1)} %copy-done.2, bf16[512,512]{1,0:T(8,128)(2,1)} %copy-done.6, bf16[512,512]{1,0:T(8,128)(2,1)} %collective-permute-done.2.refs_2_, ...), custom_call_target="tpu_custom_call" | custom-call | flops 3623878656 | bytes 18087936 | tf_op jit(solution)/shard_map/pallas_call | solution.py:149
  140.0 22.2 %shard_map.88 = (f32[512,2048]{1,0:T(8,128)}, f32[512,256]{1,0:T(8,128)}) custom-call(s32[3]{0:T(128)} %broadcast_clamp_fusion.1.source, s32[3]{0:T(128)} %get-tuple-element.51.valid, bf16[512,512]{1,0:T(8,128)(2,1)} %copy-done.3, bf16[512,512]{1,0:T(8,128)(2,1)} %collective-permute-done.4.refs_1_, bf16[512,4096]{1,0:T(8,128)(2,1)} %all-gather.5.cloned.1.call-done.refs_2_, ...), custom_call_target="tpu_custom_call" | custom-call | flops 12079595520 | bytes 38273024 | tf_op jit(solution)/shard_map/pallas_call | solution.py:149
  162.2 5.5 %shard_map.91.refs_0_ = bf16[512,32]{1,0:T(8,128)(2,1)} custom-call(bf16[512,2048]{1,0:T(8,128)(2,1)} %all-gather.3.cloned.1.call-done.x, bf16[4,256,2048]{2,1,0:T(8,128)(2,1)} %shard_map.86.refs_6_.refs_7_.refs_8_.down, f32[512,256]{1,0:T(8,128)} %get-tuple-element.37.total, s32[512,1]{1,0:T(8,128)} %copy.14.slot, s32[512,1]{1,0:T(8,128)} %copy.13.live), custom_call_target="tpu_custom_call" | custom-call | flops 536870912 | bytes 3670016 | tf_op jit(solution)/shard_map/pallas_call | solution.py:220
  167.7 0.6 collective-permute-start.15
  168.3 1.4 collective-permute-start.16
  169.8 9.9 %shard_map.90.total = f32[512,2048]{1,0:T(8,128)} custom-call(bf16[512,2048]{1,0:T(8,128)(2,1)} %all-gather.3.cloned.1.call-done.x, bf16[4,2048,2048]{2,1,0:T(8,128)(2,1)} %bitcast.25, f32[512,2048]{1,0:T(8,128)} %get-tuple-element.36.total), custom_call_target="tpu_custom_call" | custom-call | flops 4294967296 | bytes 18874368 | tf_op jit(solution)/shard_map/pallas_call | solution.py:177
  179.7 0.7 collective-permute-done.15.refs_2_
  180.4 0.6 copy-done.9
  181.0 0.7 copy-done.10
  181.7 7.5 %shard_map.92 = bf16[512,2048]{1,0:T(8,128)(2,1)} custom-call(s32[1]{0:T(128)} %bitcast.me, s32[512,1]{1,0:T(8,128)} %copy.14.slot, f32[512,2048]{1,0:T(8,128)} %shard_map.90.total, bf16[1024,2048]{1,0:T(8,128)(2,1)} %bitcast.26, bf16[512,32]{1,0:T(8,128)(2,1)} %shard_map.91.refs_0_, bf16[512,32]{1,0:T(8,128)(2,1)} %copy-done.8, bf16[512,32]{1,0:T(8,128)(2,1)} %copy-done.9, ...), custom_call_target="tpu_custom_call" | custom-call | flops 2147483648 | bytes 10485760 | tf_op jit(solution)/shard_map/pallas_call | solution.py:262
  (61 shorter events, 1.6 us)
Async XLA Ops:
  6.5 16.1 %copy-start = (s32[16]{0:T(128)S(1)}, s32[16]{0:T(128)}, u32[]{:S(2)}) copy-start(s32[16]{0:T(128)} %param.15) | copy-start | bytes 196
  6.5 13.8 %copy-start.12 = (s32[1,6]{1,0:T(1,128)S(1)}, s32[1,6]{1,0:T(1,128)}, u32[]{:S(2)}) copy-start(s32[1,6]{1,0:T(1,128)} %param.13) | copy-start | bytes 76
  6.5 16.7 %copy-start.13 = (s32[16]{0:T(128)S(1)}, s32[16]{0:T(128)}, u32[]{:S(2)}) copy-start(s32[16]{0:T(128)} %param.12) | copy-start | bytes 196
  6.5 133.4 %all-gather.5.cloned.1.call-start = ((), (), s32[]{:S(2)}) async-start(), calls=%async_computation.1 | async-start | bytes 5242880 | tf_op jit(solution)/shard_map/all_gather | solution.py:346
  8.9 153.3 %all-gather.3.cloned.1.call-start = ((), (), s32[]{:S(2)}) async-start(), calls=%async_computation | async-start | bytes 2621440 | tf_op jit(solution)/shard_map/all_gather | solution.py:346
  8.9 14.4 %collective-permute-start.9 = (s32[1,6]{1,0:T(1,128)}, s32[1,6]{1,0:T(1,128)S(1)}, u32[]{:S(2)}, u32[]{:S(2)}) collective-permute-start(s32[1,6]{1,0:T(1,128)} %param.13), channel_id=1, source_target_pairs={{0,3},{1,2},{2,1},{3,0},{4,7},{5,6},{6,5},{7,4},{8,11},{9,10},{10,... | collective-permute-start | bytes 80 | tf_op jit(solution)/shard_map/ppermute | solution.py:307
  11.3 11.9 %collective-permute-start.5 = (s32[1,6]{1,0:T(1,128)}, s32[1,6]{1,0:T(1,128)S(1)}, u32[]{:S(2)}, u32[]{:S(2)}) collective-permute-start(s32[1,6]{1,0:T(1,128)} %param.13), channel_id=1, source_target_pairs={{0,1},{1,0},{2,3},{3,2},{4,5},{5,4},{6,7},{7,6},{8,9},{9,8},{10,11... | collective-permute-start | bytes 80 | tf_op jit(solution)/shard_map/ppermute | solution.py:307
  12.0 11.2 %collective-permute-start.7 = (s32[1,6]{1,0:T(1,128)}, s32[1,6]{1,0:T(1,128)S(1)}, u32[]{:S(2)}, u32[]{:S(2)}) collective-permute-start(s32[1,6]{1,0:T(1,128)} %param.13), channel_id=1, source_target_pairs={{0,2},{1,3},{2,0},{3,1},{4,6},{5,7},{6,4},{7,5},{8,10},{9,11},{10,... | collective-permute-start | bytes 80 | tf_op jit(solution)/shard_map/ppermute | solution.py:307
  15.0 18.3 %copy-start.2 = (bf16[512,512]{1,0:T(8,128)(2,1)}, bf16[512,512]{1,0:T(8,128)(2,1)S(1)}, u32[]{:S(2)}) copy-start(bf16[512,512]{1,0:T(8,128)(2,1)S(1)} %slice.11.refs_0_) | copy-start | bytes 1572868
  15.0 25.9 %collective-permute-start = (bf16[512,512]{1,0:T(8,128)(2,1)S(1)}, bf16[512,512]{1,0:T(8,128)(2,1)S(1)}, u32[]{:S(2)}, u32[]{:S(2)}) collective-permute-start(bf16[512,512]{1,0:T(8,128)(2,1)S(1)} %slice.11.refs_0_), channel_id=1, source_target_pairs={{0,4},{4,8},{8,12},{1,5},{5,9},{9,13},{2,6},{6,10},{10,14},{3,7},{... | collective-permute-start | bytes 1572872 | tf_op jit(solution)/shard_map/ppermute | solution.py:355
  19.0 38.2 %collective-permute-start.2 = (bf16[512,512]{1,0:T(8,128)(2,1)S(1)}, bf16[512,512]{1,0:T(8,128)(2,1)}, u32[]{:S(2)}, u32[]{:S(2)}) collective-permute-start(bf16[512,512]{1,0:T(8,128)(2,1)S(1)} %slice.11.refs_0_), channel_id=1, source_target_pairs={{4,0},{8,4},{12,8},{5,1},{9,5},{13,9},{6,2},{10,6},{14,10},{7,3},{... | collective-permute-start | bytes 1572872 | tf_op jit(solution)/shard_map/ppermute | solution.py:356
  27.6 65.1 %collective-permute-start.12 = (bf16[2,128,2048]{2,1,0:T(8,128)(2,1)}, bf16[2,128,2048]{2,1,0:T(8,128)(2,1)S(1)}, u32[]{:S(2)}, u32[]{:S(2)}) collective-permute-start(bf16[2,128,2048]{2,1,0:T(8,128)(2,1)} %get-tuple-element.40), channel_id=1, source_target_pairs={{0,2},{1,3},{2,0},{3,1},{4,6},{5,7},{6,4},{7,5},{8,10},{9,11},{10,... | collective-permute-start | bytes 3145736 | tf_op jit(solution)/shard_map/ppermute | solution.py:364
  33.3 76.5 %collective-permute-start.10 = (bf16[2,4,32,2048]{3,2,1,0:T(8,128)(2,1)}, bf16[2,4,32,2048]{3,2,1,0:T(8,128)(2,1)S(1)}, u32[]{:S(2)}, u32[]{:S(2)}) collective-permute-start(bf16[2,4,32,2048]{3,2,1,0:T(8,128)(2,1)} %get-tuple-element.29), channel_id=1, source_target_pairs={{0,3},{1,2},{2,1},{3,0},{4,7},{5,6},{6,5},{7,4},{8,11},{9,10},{10,... | collective-permute-start | bytes 3145736 | tf_op jit(solution)/shard_map/ppermute | solution.py:364
  33.3 64.7 %collective-permute-start.13 = (bf16[2,128,2048]{2,1,0:T(8,128)(2,1)}, bf16[2,128,2048]{2,1,0:T(8,128)(2,1)}, u32[]{:S(2)}, u32[]{:S(2)}) collective-permute-start(bf16[2,128,2048]{2,1,0:T(8,128)(2,1)} %get-tuple-element.41), channel_id=1, source_target_pairs={{0,3},{1,2},{2,1},{3,0},{4,7},{5,6},{6,5},{7,4},{8,11},{9,10},{10,... | collective-permute-start | bytes 3145736 | tf_op jit(solution)/shard_map/ppermute | solution.py:364
  40.9 62.4 %copy-start.6 = (bf16[512,512]{1,0:T(8,128)(2,1)}, bf16[512,512]{1,0:T(8,128)(2,1)S(1)}, u32[]{:S(2)}) copy-start(bf16[512,512]{1,0:T(8,128)(2,1)S(1)} %collective-permute-done.refs_1_) | copy-start | bytes 1572868
  40.9 21.9 %collective-permute-start.1 = (bf16[512,512]{1,0:T(8,128)(2,1)S(1)}, bf16[512,512]{1,0:T(8,128)(2,1)S(1)}, u32[]{:S(2)}, u32[]{:S(2)}) collective-permute-start(bf16[512,512]{1,0:T(8,128)(2,1)S(1)} %collective-permute-done.refs_1_), channel_id=1, source_target_pairs={{4,8},{8,12},{5,9},{9,13},{6,10},{10,14},{7,11},{11,15},{20,24},{2... | collective-permute-start | bytes 1572872 | tf_op jit(solution)/shard_map/ppermute | solution.py:368
  57.2 35.6 %collective-permute-start.3 = (bf16[512,512]{1,0:T(8,128)(2,1)}, bf16[512,512]{1,0:T(8,128)(2,1)S(1)}, u32[]{:S(2)}, u32[]{:S(2)}) collective-permute-start(bf16[512,512]{1,0:T(8,128)(2,1)} %collective-permute-done.2.refs_2_), channel_id=1, source_target_pairs={{4,0},{8,4},{5,1},{9,5},{6,2},{10,6},{7,3},{11,7},{20,16},{24,20},... | collective-permute-start | bytes 1572872 | tf_op jit(solution)/shard_map/ppermute | solution.py:369
  59.3 44.0 %copy-start.11 = (s32[512]{0:T(512)S(1)}, s32[512]{0:T(512)}, u32[]{:S(2)}) copy-start(s32[512]{0:T(512)} %param.14) | copy-start | bytes 6148
  62.8 57.1 %collective-permute-start.8 = (bf16[2,4,32,2048]{3,2,1,0:T(8,128)(2,1)}, bf16[2,4,32,2048]{3,2,1,0:T(8,128)(2,1)}, u32[]{:S(2)}, u32[]{:S(2)}) collective-permute-start(bf16[2,4,32,2048]{3,2,1,0:T(8,128)(2,1)} %get-tuple-element.28), channel_id=1, source_target_pairs={{0,2},{1,3},{2,0},{3,1},{4,6},{5,7},{6,4},{7,5},{8,10},{9,11},{10,... | collective-permute-start | bytes 3145736 | tf_op jit(solution)/shard_map/ppermute | solution.py:364
  92.8 0.8 copy-start.7
  92.8 27.1 %collective-permute-start.6 = (bf16[2,4,32,2048]{3,2,1,0:T(8,128)(2,1)}, bf16[2,4,32,2048]{3,2,1,0:T(8,128)(2,1)}, u32[]{:S(2)}, u32[]{:S(2)}) collective-permute-start(bf16[2,4,32,2048]{3,2,1,0:T(8,128)(2,1)} %get-tuple-element.27), channel_id=1, source_target_pairs={{0,1},{1,0},{2,3},{3,2},{4,5},{5,4},{6,7},{7,6},{8,9},{9,8},{10,11... | collective-permute-start | bytes 3145736 | tf_op jit(solution)/shard_map/ppermute | solution.py:364
  92.8 12.4 %copy-start.5 = (bf16[2,128,2048]{2,1,0:T(8,128)(2,1)}, bf16[2,128,2048]{2,1,0:T(8,128)(2,1)S(1)}, u32[]{:S(2)}) copy-start(bf16[2,128,2048]{2,1,0:T(8,128)(2,1)S(1)} %collective-permute-done.12.refs_2_) | copy-start | bytes 3145732
  92.8 12.4 %collective-permute-start.11 = (bf16[2,128,2048]{2,1,0:T(8,128)(2,1)}, bf16[2,128,2048]{2,1,0:T(8,128)(2,1)}, u32[]{:S(2)}, u32[]{:S(2)}) collective-permute-start(bf16[2,128,2048]{2,1,0:T(8,128)(2,1)} %get-tuple-element.39), channel_id=1, source_target_pairs={{0,1},{1,0},{2,3},{3,2},{4,5},{5,4},{6,7},{7,6},{8,9},{9,8},{10,11... | collective-permute-start | bytes 3145736 | tf_op jit(solution)/shard_map/ppermute | solution.py:364
  94.8 15.0 %copy-start.3 = (bf16[512,512]{1,0:T(8,128)(2,1)}, bf16[512,512]{1,0:T(8,128)(2,1)S(1)}, u32[]{:S(2)}) copy-start(bf16[512,512]{1,0:T(8,128)(2,1)S(1)} %broadcast_select_fusion.refs_0_) | copy-start | bytes 1572868
  98.0 27.7 %collective-permute-start.4 = (bf16[512,512]{1,0:T(8,128)(2,1)S(1)}, bf16[512,512]{1,0:T(8,128)(2,1)}, u32[]{:S(2)}, u32[]{:S(2)}) collective-permute-start(bf16[512,512]{1,0:T(8,128)(2,1)S(1)} %broadcast_select_fusion.refs_0_), channel_id=1, source_target_pairs={{8,12},{4,0},{9,13},{5,1},{10,14},{6,2},{11,15},{7,3},{24,28},{20,... | collective-permute-start | bytes 1572872 | tf_op jit(solution)/shard_map/ppermute | solution.py:372
  109.8 15.9 %copy-start.4 = (bf16[2,4,32,2048]{3,2,1,0:T(8,128)(2,1)}, bf16[2,4,32,2048]{3,2,1,0:T(8,128)(2,1)S(1)}, u32[]{:S(2)}) copy-start(bf16[2,4,32,2048]{3,2,1,0:T(8,128)(2,1)S(1)} %collective-permute-done.10.refs_3_) | copy-start | bytes 3145732
  167.7 11.9 %collective-permute-start.14 = (bf16[512,32]{1,0:T(8,128)(2,1)}, bf16[512,32]{1,0:T(8,128)(2,1)S(1)}, u32[]{:S(2)}, u32[]{:S(2)}) collective-permute-start(bf16[512,32]{1,0:T(8,128)(2,1)} %shard_map.91.refs_0_), channel_id=1, source_target_pairs={{0,12},{4,0},{8,4},{12,8},{1,13},{5,1},{9,5},{13,9},{2,14},{6,2},{... | collective-permute-start | bytes 98312 | tf_op jit(solution)/shard_map/ppermute | solution.py:389
  167.7 12.6 %collective-permute-start.15 = (bf16[512,32]{1,0:T(8,128)(2,1)}, bf16[512,32]{1,0:T(8,128)(2,1)S(1)}, u32[]{:S(2)}, u32[]{:S(2)}) collective-permute-start(bf16[512,32]{1,0:T(8,128)(2,1)} %shard_map.91.refs_0_), channel_id=1, source_target_pairs={{0,8},{4,12},{8,0},{12,4},{1,9},{5,13},{9,1},{13,5},{2,10},{6,14},... | collective-permute-start | bytes 98312 | tf_op jit(solution)/shard_map/ppermute | solution.py:389
  168.3 12.0 %collective-permute-start.16 = (bf16[512,32]{1,0:T(8,128)(2,1)}, bf16[512,32]{1,0:T(8,128)(2,1)S(1)}, u32[]{:S(2)}, u32[]{:S(2)}) collective-permute-start(bf16[512,32]{1,0:T(8,128)(2,1)} %shard_map.91.refs_0_), channel_id=1, source_target_pairs={{0,4},{4,8},{8,12},{12,0},{1,5},{5,9},{9,13},{13,1},{2,6},{6,10},{... | collective-permute-start | bytes 98312 | tf_op jit(solution)/shard_map/ppermute | solution.py:389
  169.8 19.4 %copy-start.1 = (s32[16]{0:T(128)S(1)}, s32[16]{0:T(128)}, u32[]{:S(2)}) copy-start(s32[16]{0:T(128)} %param.15) | copy-start | bytes 196
  179.7 0.7 copy-start.8
  180.4 0.7 copy-start.9
  181.0 0.7 copy-start.10
Sparse Core Ops, SparseCore 0:
  9.0 105.2 all-gather.4
  115.8 44.1 all-gather.2

commit v6 on v4

v6 whole, which is shorter than its diff:
```python
import functools

import jax
import jax.numpy as jnp
from jax import lax
from jax.experimental import pallas as pl
from jax.experimental.pallas import tpu as pltpu
from jax.sharding import PartitionSpec as P

CAP = 2
UNIT = 512
LINE = 512
GATHERED = (1024, 512)
PARAMS = pltpu.CompilerParams(vmem_limit_bytes=48 * 2**20)
F32 = jnp.float32
BF16 = jnp.bfloat16


def pick_kernel(places, down, up, down_out, up_out):
    shards, _, width = down_out.shape[1:]
    for t in range(shards):
        down_out[0, t] = down[0, :, t * width:(t + 1) * width]
    up_out[...] = up[...]


def pick_pages(places, down, up, shards):
    count = places.shape[0]
    _, rank_part, features = down.shape
    shapes = [(shards, rank_part, features // shards), up.shape[1:]]
    return pl.pallas_call(
        pick_kernel,
        out_shape=[jax.ShapeDtypeStruct((count,) + shape, BF16) for shape in shapes],
        grid_spec=pltpu.PrefetchScalarGridSpec(
            num_scalar_prefetch=1,
            grid=(count,),
            in_specs=[pl.BlockSpec((1,) + a.shape[1:], lambda i, places: (places[i], 0, 0)) for a in (down, up)],
            out_specs=[
                pl.BlockSpec((1,) + shapes[0], lambda i, places: (i, 0, 0, 0)),
                pl.BlockSpec((1,) + shapes[1], lambda i, places: (i, 0, 0)),
            ],
        ),
        compiler_params=PARAMS,
    )(places, down, up)


def join_downs_kernel(*refs):
    *pages, out = refs
    units = out.shape[0]
    for u in range(units):
        out[u] = jnp.concatenate(
            [p[c, 0, :, u * UNIT:(u + 1) * UNIT] for p in pages for c in range(CAP)], axis=0
        )


def join_downs(downs):
    _, shards, rank_part, features = downs[0].shape
    slots = CAP * rank_part * len(downs)
    units = features // UNIT
    return pl.pallas_call(
        join_downs_kernel,
        out_shape=jax.ShapeDtypeStruct((shards * units, slots, UNIT), BF16),
        grid=(shards,),
        in_specs=[pl.BlockSpec((CAP, 1, rank_part, features), lambda t: (0, t, 0, 0))] * len(downs),
        out_specs=pl.BlockSpec((units, slots, UNIT), lambda t: (t, 0, 0)),
        compiler_params=PARAMS,
    )(*downs)


def join_ups_kernel(*refs):
    *pages, out = refs
    for j, p in enumerate(pages):

        @pl.when(pl.program_id(0) == j)
        def _():
            out[...] = p[...]


def join_ups(ups):
    count, rank, columns = ups[0].shape
    return pl.pallas_call(
        join_ups_kernel,
        out_shape=jax.ShapeDtypeStruct((count * len(ups), rank, columns), BF16),
        grid=(len(ups),),
        in_specs=[pl.BlockSpec(up.shape, lambda j: (0, 0, 0)) for up in ups],
        out_specs=pl.BlockSpec(ups[0].shape, lambda j: (j, 0, 0)),
        compiler_params=PARAMS,
    )(*ups).reshape(-1, columns)


RESIDENT = pl.BlockSpec(memory_space=pltpu.VMEM)


def unit_steps(x):
    return x.shape[0] * (x.shape[2] // UNIT)


def x_specs(xs):
    specs, first = [], 0
    for x in xs:
        units = x.shape[2] // UNIT

        def index(s, *_, first=first, units=units, last=x.shape[0] - 1):
            return jnp.clip((s - first) // units, 0, last), 0, 0

        specs.append(pl.BlockSpec((1,) + x.shape[1:], index))
        first += unit_steps(x)
    return specs


def for_unit(xs, counts, valid, body):
    s, first = pl.program_id(0), 0
    for x, count in zip(xs, counts):
        units = x.shape[2] // UNIT

        @pl.when((s >= first) & (s < first + count) & (valid[s] != 0))
        def _():
            if units == 1:
                body(x[0])
            else:
                at = pl.multiple_of(lax.rem(s - first, units) * UNIT, UNIT)
                body(x[0, :, pl.ds(at, UNIT)])

        first += count


def chunk_kernel(counts, held, with_base, with_low, rank_part, unit, valid, *refs):
    refs = list(refs)
    xs = [refs.pop(0) for _ in counts]
    weight = refs.pop(0) if with_base else None
    down = refs.pop(0) if with_low else None
    ends = [refs.pop(0) for _ in range(2)] if rank_part else None
    totals = [refs.pop(0) for _ in range(held)]
    base = refs.pop(0) if with_base else None
    low = refs.pop(0) if with_low and not rank_part else None
    if rank_part:
        out, low = refs

    @pl.when(pl.program_id(0) == 0)
    def _():
        if rank_part:
            low[...] = totals[0][...]
        elif not held:
            base[...] = jnp.zeros_like(base)
            low[...] = jnp.zeros_like(low)

    def body(x):
        if with_base:
            part = min(base.shape[1], 512)
            for n in range(0, base.shape[1], part):
                base[:, n:n + part] += jnp.dot(x, weight[0, :, n:n + part], preferred_element_type=F32)
        if with_low:
            low[...] += lax.dot_general(x, down[0], (((1,), (1,)), ((), ())), preferred_element_type=F32)

    for_unit(xs, counts, valid, body)
    if rank_part:
        slot, live = ends

        @pl.when(pl.program_id(0) == pl.num_programs(0) - 1)
        def _():
            mine = jnp.zeros(out.shape, F32)
            for e in range(low.shape[1] // rank_part):
                mine += jnp.where(slot[...] == e, low[:, e * rank_part:(e + 1) * rank_part], 0.0)
            k = lax.broadcasted_iota(jnp.int32, mine.shape, 1)
            out[...] = jnp.where(k < live[...], mine, 0.0).astype(BF16)


def add_chunk(totals, xs, unit, valid, weight=None, down=None, ends=(), rank_part=0):
    rows = xs[0].shape[1]
    columns = 0 if weight is None else weight.shape[-1]
    slots = 0 if down is None else down.shape[1]
    steps = sum(unit_steps(x) for x in xs)
    walked = [a for a in (weight, down) if a is not None]
    out_shape, aliases = [], {}
    if rank_part:
        out_shape = [jax.ShapeDtypeStruct((rows, rank_part), BF16)]
    else:
        out_shape = [pltpu.VMEM((rows, a), F32) for a in (columns, slots) if a]
        first = 2 + len(xs) + len(walked) + len(ends)
        aliases = {first + i: i for i in range(len(totals))}
    outs = pl.pallas_call(
        functools.partial(
            chunk_kernel, [unit_steps(x) for x in xs], len(totals), weight is not None, down is not None, rank_part
        ),
        out_shape=out_shape,
        grid_spec=pltpu.PrefetchScalarGridSpec(
            num_scalar_prefetch=2,
            grid=(steps,),
            in_specs=x_specs(xs)
            + [pl.BlockSpec((1,) + a.shape[1:], lambda s, unit, valid: (unit[s], 0, 0)) for a in walked]
            + [pl.BlockSpec((rows, 1), lambda s, *_: (0, 0))] * len(ends)
            + [RESIDENT] * len(totals),
            out_specs=[RESIDENT if not rank_part else pl.BlockSpec((rows, rank_part), lambda s, *_: (0, 0))]
            * len(out_shape),
            scratch_shapes=[pltpu.VMEM((rows, slots), F32)] if rank_part else [],
        ),
        input_output_aliases=aliases,
        compiler_params=PARAMS,
        cost_estimate=pl.CostEstimate(
            flops=2 * steps * UNIT * rows * (columns + slots),
            bytes_accessed=2 * steps * UNIT * (rows + columns + slots),
            transcendentals=0,
        ),
    )(unit, valid, *xs, *walked, *ends, *totals)
    return outs


def finish_kernel(parts, me, slot, total, up, *refs):
    lows, (out, acc, spread) = refs[:parts], refs[parts:]
    rank_part = lows[0].shape[1]
    rank = parts * rank_part
    step = pl.program_id(0)
    depth = up.shape[0]

    @pl.when(step == 0)
    def _():
        low = jnp.concatenate([part[...].astype(F32) for part in lows], axis=1)
        low = pltpu.roll(low, me[0] * rank_part, 1)
        for e in range(spread.shape[0] * depth // rank):
            own = jnp.where(slot[...] == e, low, 0.0).astype(BF16)
            spread[e * rank // depth, :, e * rank % depth:e * rank % depth + rank] = own

    last = pl.num_programs(0) - 1
    part = min(out.shape[1], 512)
    for n in range(0, out.shape[1], part):
        cut = slice(n, n + part)
        term = jnp.dot(spread[step], up[:, cut], preferred_element_type=F32)

        @pl.when(step == 0)
        def _():
            acc[:, cut] = total[:, cut] + term

        @pl.when((step > 0) & (step < last))
        def _():
            acc[:, cut] += term

        @pl.when(step == last)
        def _():
            out[:, cut] = (acc[:, cut] + term).astype(BF16)


def finish(me, slot, total, up, lows):
    rows, columns = total.shape
    rank_part = lows[0].shape[1]
    depth = 2 * len(lows) * rank_part
    steps = up.shape[0] // depth
    return pl.pallas_call(
        functools.partial(finish_kernel, len(lows)),
        grid=(steps,),
        out_shape=jax.ShapeDtypeStruct((rows, columns), BF16),
        in_specs=[
            pl.BlockSpec(memory_space=pltpu.SMEM),
            pl.BlockSpec((rows, 1), lambda s: (0, 0)),
            RESIDENT,
            pl.BlockSpec((depth, columns), lambda s: (s, 0)),
        ] + [pl.BlockSpec((rows, rank_part), lambda s: (0, 0))] * len(lows),
        out_specs=pl.BlockSpec((rows, columns), lambda s: (0, 0)),
        scratch_shapes=[pltpu.VMEM((rows, columns), F32), pltpu.VMEM((steps, rows, depth), BF16)],
        compiler_params=PARAMS,
        cost_estimate=pl.CostEstimate(
            flops=2 * rows * up.shape[0] * columns,
            bytes_accessed=2 * (rows + up.shape[0]) * columns,
            transcendentals=0,
        ),
    )(me, slot, total, up, *lows)


def after(value, *earlier):
    return lax.optimization_barrier((value,) + earlier)[0]


def asked_pages(requests, adapter_page_row, holder_length):
    n_dp = lax.axis_size("dp")
    dp = lax.axis_index("dp")
    count = adapter_page_row.shape[0]

    def pages_of(wanted):
        hit = wanted[:, None] == jnp.arange(count)[None, :]
        return jnp.sum(jnp.where(hit, adapter_page_row[None, :], 0), axis=1)

    def order_in(holders):
        same = holders[:, None] == holders[None, :]
        n = holders.shape[0]
        earlier = jnp.arange(n)[:, None] > jnp.arange(n)[None, :]
        return jnp.sum((same & earlier).astype(jnp.int32), axis=1)

    own = pages_of(requests[0])
    holders = own // holder_length
    slots = (holders ^ dp) * CAP + order_in(holders)
    places = []
    for j in range(n_dp):
        wanted = requests if j == 0 else lax.ppermute(requests, "dp", [(i, i ^ j) for i in range(n_dp)])
        pages = pages_of(wanted[0])
        holder = pages // holder_length
        order = jnp.where(holder == dp, order_in(holder), -1)
        hit = order[None, :] == jnp.arange(CAP)[:, None]
        places.append(jnp.sum(jnp.where(hit, (pages % holder_length)[None, :], 0), axis=1))
    return slots, places


def local(
    attention_result,
    output_weight,
    adapter_down_weight,
    adapter_up_weight,
    adapter_page_row,
    requests,
    row_request_entry,
    ranks,
):
    n_dp = lax.axis_size("dp")
    n_tensor = lax.axis_size("tensor")
    me = lax.axis_index("tensor")
    rows, width = attention_result.shape
    holder_length, rank_part, _ = adapter_down_weight.shape
    rank, columns = adapter_up_weight.shape[1:]
    own_list = requests[0]
    entries = own_list.shape[0]
    one_hot = row_request_entry[:, None] == jnp.arange(entries)[None, :]
    row_rank = jnp.sum(jnp.where(one_hot, ranks[own_list][None, :], 0), axis=1)
    if n_tensor != 4 or width != LINE + sum(GATHERED) or rank_part % 16:
        return plain(
            attention_result, output_weight, adapter_down_weight, adapter_up_weight, adapter_page_row,
            own_list, one_hot, row_rank,
        )

    units = width // UNIT
    weight = output_weight.reshape(n_tensor * units, UNIT, columns)
    gathered, x, first = [], attention_result, 0
    for features in GATHERED:
        piece = x[:, first:first + features]
        gathered.append(lax.all_gather(piece, "tensor", axis=0))
        x = after(x, piece)
        first += features + LINE

    middle = GATHERED[0]
    last = middle + LINE
    line = x[None, :, middle:last]
    right = [(i, i + 1) for i in range(n_tensor - 1)]
    left = [(i + 1, i) for i in range(n_tensor - 1)]
    right_1 = lax.ppermute(line, "tensor", right)
    left_1 = lax.ppermute(line, "tensor", left)

    slots, places = asked_pages(requests, adapter_page_row, holder_length)
    downs, ups = [], []
    for j in range(n_dp):
        down, up = pick_pages(places[j], adapter_down_weight, adapter_up_weight, n_tensor)
        if j:
            pairs = [(i, i ^ j) for i in range(n_dp)]
            down, up = lax.ppermute(down, "dp", pairs), lax.ppermute(up, "dp", pairs)
        downs.append(down)
        ups.append(up)

    right_2 = lax.ppermute(right_1, "tensor", right[1:])
    left_2 = lax.ppermute(left_1, "tensor", left[:-1])
    upper = me >= n_tensor // 2
    second = jnp.where(upper, right_2, left_2)
    third = lax.ppermute(second, "tensor", right[-1:] + left[:1])
    down = join_downs(after(tuple(downs), third))
    up = join_ups(ups)

    slot = jnp.sum(jnp.where(one_hot, slots[None, :], 0), axis=1)[:, None]
    live = row_rank[:, None] - me * rank_part
    every = jnp.arange(n_tensor)

    def places_of(*spans):
        unit, valid = [], []
        for source, first, length in spans:
            source = jnp.atleast_1d(source)
            there = (source >= 0) & (source < n_tensor)
            source = jnp.clip(source, 0, n_tensor - 1)
            ids = source[:, None] * units + first // UNIT + jnp.arange(length // UNIT)[None, :]
            unit.append(ids.reshape(-1))
            valid.append(jnp.broadcast_to(there[:, None], ids.shape).reshape(-1))
        return jnp.concatenate(unit).astype(jnp.int32), jnp.concatenate(valid).astype(jnp.int32)

    near = places_of(*[(me + o, middle, LINE) for o in (0, -1, 1)])
    totals = add_chunk((), [line, right_1, left_1], *near, weight, down)
    toward = jnp.where(upper, -1, 1)
    far = places_of((me + 2 * toward, middle, LINE), (me + 3 * toward, middle, LINE), (every, 0, GATHERED[0]))
    totals = add_chunk(totals, [second, third, gathered[0]], *far, weight, down)
    x = pltpu.with_memory_space_constraint(after(gathered[1], *totals, up), pltpu.HBM)
    at = places_of((every, last, GATHERED[1]))
    low, = add_chunk(totals[1:], [x], *at, None, down, (slot, live), rank_part)
    base, = add_chunk(totals[:1], [x], *at, weight)
    lows = [low] + [
        lax.ppermute(low, "tensor", [(i, (i - j) % n_tensor) for i in range(n_tensor)])
        for j in range(1, n_tensor)
    ]
    return finish(me[None], slot, base, up, lows)


def gather_pages(block, n_dp):
    return [block] + [
        lax.ppermute(block, "dp", [(i, i ^ j) for i in range(n_dp)]) for j in range(1, n_dp)
    ]


def plain(x, output_weight, down_weight, up_weight, adapter_page_row, own_list, one_hot, row_rank):
    n_dp = lax.axis_size("dp")
    dp = lax.axis_index("dp")
    rows = x.shape[0]
    holder_length = down_weight.shape[0]
    rank, columns = up_weight.shape[1:]
    entries = one_hot.shape[1]
    pages = adapter_page_row[own_list]
    places = ((pages // holder_length) ^ dp) * holder_length + pages % holder_length

    def requested(block):
        blocks = jnp.concatenate(gather_pages(block, n_dp), axis=0)
        return jnp.concatenate(
            [lax.dynamic_slice_in_dim(blocks, places[e], 1, 0) for e in range(entries)], axis=0
        )

    down, up = requested(down_weight), requested(up_weight)
    x = lax.all_gather(x, "tensor", axis=1, tiled=True)
    base = jnp.dot(x, output_weight, preferred_element_type=F32)
    low = jnp.einsum("rd,ekd->rek", x, down, preferred_element_type=F32)
    low = jnp.sum(jnp.where(one_hot[:, :, None], low, 0.0), axis=1).astype(BF16)
    low = lax.all_gather(low, "tensor", axis=1, tiled=True)
    low = jnp.where(jnp.arange(rank)[None, :] < row_rank[:, None], low, jnp.zeros_like(low))
    spread = jnp.where(one_hot[:, :, None], low[:, None, :], jnp.zeros((), BF16))
    term = jnp.dot(
        spread.reshape(rows, entries * rank), up.reshape(entries * rank, columns), preferred_element_type=F32
    )
    return (base + term).astype(BF16)


def solution(mesh):
    in_specs = (
        P(("groups", "dp"), "tensor"),
        P(None, "tensor"),
        P("dp", "tensor", None),
        P("dp", None, "tensor"),
        P("groups"),
        P(("groups", "dp"), None),
        P(("groups", "dp")),
        P(),
    )
    out_specs = P(("groups", "dp"), "tensor")
    return jax.shard_map(local, mesh=mesh, in_specs=in_specs, out_specs=out_specs, check_vma=False)
```

time: 228 us -> 201 us (0.88)
  Pallas kernels: 85.8 us -> 67.8 us
  waiting for transfers between devices: 89.3 us -> 76.3 us
  local copies, waits for them, and re-layouts: 9.22 us -> 20.9 us
  other arithmetic: 9.29 us -> 2.02 us
    ppermute x1, waiting for transfers between devices: 25 us -> 8.68 us  [local(): third = lax.ppermute(second, 'tensor', right[-1:] + left[:1])]
    pallas_call x9 -> x7, Pallas kernels: 72.4 us -> 57.5 us  [the longest x4 39.4 us: add_chunk(): pl.pallas_call(functools.partial(chunk_kernel, [unit_steps(x) for x in xs...]
    unnamed x24 -> x42, local copies, waits for them, and re-layouts: 1.72 us -> 14.4 us
    ppermute x6, waiting for transfers between devices: 0.02 us -> 9.67 us  [local(): down, up = (lax.ppermute(down, 'dp', pairs), lax.ppermute(up, 'dp', pairs))]
    ppermute x1, waiting for transfers between devices: 16.7 us -> 9.95 us  [local(): right_1 = lax.ppermute(line, 'tensor', right)]
    ppermute x1, waiting for transfers between devices: 21.7 us -> 15.2 us  [local(): left_1 = lax.ppermute(line, 'tensor', left)]
    ppermute x1, waiting for transfers between devices: 25.5 us -> 30.2 us  [local(): left_2 = lax.ppermute(left_1, 'tensor', left[:-1])]
    pallas_call x4, Pallas kernels: 13.3 us -> 10.2 us  [pick_pages(): pl.pallas_call(pick_kernel, out_shape=[jax.ShapeDtypeStruct((count,) + sh...]
  transfers between devices with their start and end apart: 19 -> 19, of which waited for: 5 -> 7; matrix products, arithmetic and copies ran while one was open for 6% -> 3% of each run, Pallas kernels for 34% -> 26%
where the time goes in v6:
time: 201 us; the launch traced here: 200 us
  waiting for transfers between devices  76.3 us (38%)
  Pallas kernels  67.8 us (34%)
  local copies, waits for them, and re-layouts  20.9 us (10%)
  starting transfers between devices  19 us (9%)
  between operations  13.8 us (7%)
  other arithmetic  2.02 us (1%)
    pallas_call x4, Pallas kernels, add_chunk(): pl.pallas_call(functools.partial(chunk_kernel, [unit_steps(x) for x in xs...  39.4 us
    ppermute x1, waiting for transfers between devices, local(): left_2 = lax.ppermute(left_1, 'tensor', left[:-1])  30.2 us
    ppermute x1, waiting for transfers between devices, local(): left_1 = lax.ppermute(line, 'tensor', left)  15.2 us
    unnamed x42, local copies, waits for them, and re-layouts  14.4 us
    pallas_call x4, Pallas kernels, pick_pages(): pl.pallas_call(pick_kernel, out_shape=[jax.ShapeDtypeStruct((count,) + sh...  10.2 us
    ppermute x1, waiting for transfers between devices, local(): right_1 = lax.ppermute(line, 'tensor', right)  9.95 us
    pallas_call x1, Pallas kernels, finish(): pl.pallas_call(functools.partial(finish_kernel, len(lows)), grid=(steps,)...  9.69 us
    ppermute x6, waiting for transfers between devices, local(): down, up = (lax.ppermute(down, 'dp', pairs), lax.ppermute(up, 'dp', pairs))  9.67 us
  transfers between devices with their start and end apart: 19, of which 7 were waited for; matrix products, arithmetic and copies ran while one was open for 3% of the time, Pallas kernels for 26%

profile of v6, /device:TPU:0, one launch (start us, length us, event | category | flops | bytes accessed | tf_op | source)
XLA Modules:
  0.0 199.9 jit_solution(10537297144965065992)
XLA Ops:
  6.6 2.4 %slice.9 = bf16[512,1024]{1,0:T(8,128)(2,1)} slice(bf16[512,2048]{1,0:T(8,128)(2,1)} %param.8), slice={[0:512], [0:1024]} | slice | bytes 2097152 | tf_op jit(solution)/shard_map/slice | solution.py:330
  9.1 0.5 collective-permute-start.5
  9.6 2.6 %collective-permute-start.7 = (s32[1,6]{1,0:T(1,128)}, s32[1,6]{1,0:T(1,128)S(1)}, u32[]{:S(2)}, u32[]{:S(2)}) collective-permute-start(s32[1,6]{1,0:T(1,128)} %param.13), channel_id=1, source_target_pairs={{0,2},{1,3},{2,0},{3,1},{4,6},{5,7},{6,4},{7,5},{8,10},{9,11},{10,... | collective-permute-start | bytes 80 | tf_op jit(solution)/shard_map/ppermute | solution.py:291
  12.2 1.9 slice.10
  14.1 1.1 slice_bitcast_fusion.refs_0_
  15.2 3.7 %collective-permute-start = (bf16[1,512,512]{2,1,0:T(8,128)(2,1)S(1)}, bf16[1,512,512]{2,1,0:T(8,128)(2,1)S(1)}, u32[]{:S(2)}, u32[]{:S(2)}) collective-permute-start(bf16[1,512,512]{2,1,0:T(8,128)(2,1)S(1)} %slice_bitcast_fusion.refs_0_), channel_id=1, source_target_pairs={{0,4},{4,8},{8,12},{1,5},{5,9},{9,13},{2,6},{6,10},{10,14},{3,7},{... | collective-permute-start | bytes 1572872 | tf_op jit(solution)/shard_map/ppermute | solution.py:340
  18.9 1.3 collective-permute-start.2
  20.7 0.6 gather_fusion
  21.7 0.2 select_reduce_fusion.2
  22.0 0.2 convert_reduce_fusion.1
  22.3 2.7 %shard_map.84 = (bf16[2,4,32,2048]{3,2,1,0:T(8,128)(2,1)}, bf16[2,128,2048]{2,1,0:T(8,128)(2,1)S(1)}) custom-call(s32[2]{0:T(128)S(1)} %fusion.6.places, bf16[4,32,8192]{2,1,0:T(8,128)(2,1)S(1)} %copy-done.7, bf16[4,128,2048]{2,1,0:T(8,128)(2,1)} %up.7), custom_call_target="tpu_custom_call" | custom-call | tf_op jit(solution)/shard_map/pallas_call | solution.py:30
  24.9 1.5 collective-permute-start.12
  26.7 2.7 %shard_map.85 = (bf16[2,4,32,2048]{3,2,1,0:T(8,128)(2,1)}, bf16[2,128,2048]{2,1,0:T(8,128)(2,1)S(1)}) custom-call(s32[2]{0:T(128)S(1)} %fusion.7.places, bf16[4,32,8192]{2,1,0:T(8,128)(2,1)S(1)} %copy-done.7, bf16[4,128,2048]{2,1,0:T(8,128)(2,1)} %up.7), custom_call_target="tpu_custom_call" | custom-call | tf_op jit(solution)/shard_map/pallas_call | solution.py:30
  29.5 1.7 collective-permute-start.13
  31.2 9.9 %collective-permute-done.refs_1_ = bf16[1,512,512]{2,1,0:T(8,128)(2,1)S(1)} collective-permute-done((bf16[1,512,512]{2,1,0:T(8,128)(2,1)S(1)}, bf16[1,512,512]{2,1,0:T(8,128)(2,1)S(1)}, u32[]{:S(2)}, u32[]{:S(2)}) %collective-permute-start) | collective-permute-done | bytes 524320 | tf_op jit(solution)/shard_map/ppermute | solution.py:340
  41.2 0.7 collective-permute-start.1
  41.9 15.2 %collective-permute-done.2.refs_2_ = bf16[1,512,512]{2,1,0:T(8,128)(2,1)} collective-permute-done((bf16[1,512,512]{2,1,0:T(8,128)(2,1)S(1)}, bf16[1,512,512]{2,1,0:T(8,128)(2,1)}, u32[]{:S(2)}, u32[]{:S(2)}) %collective-permute-start.2) | collective-permute-done | bytes 524320 | tf_op jit(solution)/shard_map/ppermute | solution.py:341
  57.0 1.3 collective-permute-start.3
  58.6 3.0 %shard_map.83 = (bf16[2,4,32,2048]{3,2,1,0:T(8,128)(2,1)}, bf16[2,128,2048]{2,1,0:T(8,128)(2,1)}) custom-call(s32[2]{0:T(128)S(1)} %fusion.5.places, bf16[4,32,8192]{2,1,0:T(8,128)(2,1)S(1)} %copy-done.7, bf16[4,128,2048]{2,1,0:T(8,128)(2,1)} %up.7), custom_call_target="tpu_custom_call" | custom-call | tf_op jit(solution)/shard_map/pallas_call | solution.py:30
  61.6 1.5 collective-permute-start.8
  63.2 30.2 %collective-permute-done.3 = bf16[1,512,512]{2,1,0:T(8,128)(2,1)S(1)} collective-permute-done((bf16[1,512,512]{2,1,0:T(8,128)(2,1)}, bf16[1,512,512]{2,1,0:T(8,128)(2,1)S(1)}, u32[]{:S(2)}, u32[]{:S(2)}) %collective-permute-start.3) | collective-permute-done | bytes 524320 | tf_op jit(solution)/shard_map/ppermute | solution.py:354
  93.4 0.2 collective-permute-start.6
  93.6 0.3 collective-permute-start.11
  94.1 0.4 copy-done.8
  94.5 0.3 collective-permute-done.13.refs_3_
  94.9 1.5 collective-permute-start.4
  96.5 1.8 shard_map.82
  98.3 1.0 copy-done.12
  99.3 1.0 copy-done.14
  100.8 1.2 copy-done.9
  102.0 1.2 copy-done.11
  103.2 1.2 copy-done.15
  104.4 3.8 %shard_map.89 = bf16[8,128,2048]{2,1,0:T(8,128)(2,1)} custom-call(bf16[2,128,2048]{2,1,0:T(8,128)(2,1)S(1)} %copy-done.15, bf16[2,128,2048]{2,1,0:T(8,128)(2,1)} %collective-permute-done.11.refs_1_, bf16[2,128,2048]{2,1,0:T(8,128)(2,1)S(1)} %copy-done.9, bf16[2,128,2048]{2,1,0:T(8,128)(2,1)S(1)} %copy-done.11), custom_call_target="tpu_custom_call" | custom-call | tf_op jit(solution)/shard_map/pallas_call | solution.py:80
  108.2 9.3 %collective-permute-done.8.refs_2_ = bf16[2,4,32,2048]{3,2,1,0:T(8,128)(2,1)} collective-permute-done((bf16[2,4,32,2048]{3,2,1,0:T(8,128)(2,1)}, bf16[2,4,32,2048]{3,2,1,0:T(8,128)(2,1)}, u32[]{:S(2)}, u32[]{:S(2)}) %collective-permute-start.8) | collective-permute-done | bytes 1048608 | tf_op jit(solution)/shard_map/ppermute | solution.py:349
  117.6 8.7 %collective-permute-done.4.refs_1_ = bf16[1,512,512]{2,1,0:T(8,128)(2,1)} collective-permute-done((bf16[1,512,512]{2,1,0:T(8,128)(2,1)S(1)}, bf16[1,512,512]{2,1,0:T(8,128)(2,1)}, u32[]{:S(2)}, u32[]{:S(2)}) %collective-permute-start.4) | collective-permute-done | bytes 524320 | tf_op jit(solution)/shard_map/ppermute | solution.py:357
  126.3 4.6 %shard_map.86.refs_4_.refs_1_ = bf16[16,256,512]{2,1,0:T(8,128)(2,1)} custom-call(bf16[2,4,32,2048]{3,2,1,0:T(8,128)(2,1)S(1)} %copy-done.13, bf16[2,4,32,2048]{3,2,1,0:T(8,128)(2,1)} %collective-permute-done.6.refs_1_, bf16[2,4,32,2048]{3,2,1,0:T(8,128)(2,1)} %collective-permute-done.8.refs_2_, bf16[2,4,32,2048]{3,2,1,0:T(8,128)(2,1)} %collective-permute-done.10.refs_3_), custom_call_target="tpu_custom_call" | custom-call | tf_op jit(solution)/shard_map/pallas_call | solution.py:59
  130.9 7.2 %shard_map.87 = (f32[512,2048]{1,0:T(8,128)S(1)}, f32[512,256]{1,0:T(8,128)S(1)}) custom-call(s32[3]{0:T(128)S(1)} %pad_add_fusion.1.unit, s32[3]{0:T(128)S(1)} %add_convert_fusion.1.valid, bf16[1,512,512]{2,1,0:T(8,128)(2,1)S(1)} %slice_bitcast_fusion.refs_0_, bf16[1,512,512]{2,1,0:T(8,128)(2,1)S(1)} %copy-done.17, ...), custom_call_target="tpu_custom_call" | custom-call | flops 3623878656 | bytes 8650752 | tf_op jit(solution)/shard_map/pallas_call | solution.py:180
  138.1 1.9 copy-done.3
  140.0 2.2 %copy-done.4 = f32[512,2048]{1,0:T(8,128)S(1)} copy-done((f32[512,2048]{1,0:T(8,128)S(1)}, f32[512,2048]{1,0:T(8,128)}, u32[]{:S(2)}) %copy-start.4) | copy-done | bytes 4194328
  142.2 18.9 %shard_map.88 = (f32[512,2048]{1,0:T(8,128)S(1)}, f32[512,256]{1,0:T(8,128)S(1)}) custom-call(s32[10]{0:T(128)S(1)} %pad_add_fusion.unit, s32[10]{0:T(128)S(1)} %add_convert_fusion.valid, bf16[1,512,512]{2,1,0:T(8,128)(2,1)S(1)} %broadcast_select_fusion.refs_0_, ...), custom_call_target="tpu_custom_call", output_to_operand_aliasing={{0}: (7, {}), {1}: (8, {})} | custom-call | flops 12079595520 | bytes 28835840 | tf_op jit(solution)/shard_map/pallas_call | solution.py:180
  161.2 1.9 copy-done.5
  163.1 2.2 %copy-done.2 = bf16[16,256,512]{2,1,0:T(8,128)(2,1)S(1)} copy-done((bf16[16,256,512]{2,1,0:T(8,128)(2,1)S(1)}, bf16[16,256,512]{2,1,0:T(8,128)(2,1)}, u32[]{:S(2)}) %copy-start.2) | copy-done | bytes 4194328
  165.3 5.2 %shard_map.91.refs_0_ = bf16[512,32]{1,0:T(8,128)(2,1)S(1)} custom-call(s32[4]{0:T(128)S(1)} %broadcast_add_fusion.unit, s32[4]{0:T(128)S(1)} %fusion.9.valid, bf16[4,512,512]{2,1,0:T(8,128)(2,1)} %bitcast.29, bf16[16,256,512]{2,1,0:T(8,128)(2,1)S(1)} %copy-done.2, s32[512,1]{1,0:T(8,128)S(1)} %copy.17.refs_2_.slot, s32[512,1]{1,0:T(8,128)S(1)} %copy.16.refs_3_, ...), custom_call_target="tpu_custom_call" | custom-call | flops 536870912 | bytes 3145728 | tf_op jit(solution)/shard_map/pallas_call | solution.py:180
  170.5 0.9 collective-permute-start.15
  171.4 1.2 collective-permute-start.16
  172.5 8.1 %shard_map.90.total = f32[512,2048]{1,0:T(8,128)S(1)} custom-call(s32[4]{0:T(128)S(1)} %broadcast_add_fusion.unit, s32[4]{0:T(128)S(1)} %fusion.9.valid, bf16[4,512,512]{2,1,0:T(8,128)(2,1)} %bitcast.30, bf16[16,512,2048]{2,1,0:T(8,128)(2,1)} %bitcast.27, f32[512,2048]{1,0:T(8,128)S(1)} %copy-done.6), custom_call_target="tpu_custom_call", output_to_operand_aliasing={{}: (4, {})} | custom-call | flops 4294967296 | bytes 10485760 | tf_op jit(solution)/shard_map/pallas_call | solution.py:180
  180.7 2.6 %collective-permute-done.15.refs_2_ = bf16[512,32]{1,0:T(8,128)(2,1)S(1)} collective-permute-done((bf16[512,32]{1,0:T(8,128)(2,1)S(1)}, bf16[512,32]{1,0:T(8,128)(2,1)S(1)}, u32[]{:S(2)}, u32[]{:S(2)}) %collective-permute-start.15) | collective-permute-done | bytes 32800 | tf_op jit(solution)/shard_map/ppermute | solution.py:386
  183.3 9.7 %shard_map.92 = bf16[512,2048]{1,0:T(8,128)(2,1)} custom-call(s32[1]{0:T(128)} %bitcast.me, s32[512,1]{1,0:T(8,128)S(1)} %copy.17.refs_2_.slot, f32[512,2048]{1,0:T(8,128)S(1)} %shard_map.90.total, bf16[1024,2048]{1,0:T(8,128)(2,1)} %bitcast.28, bf16[512,32]{1,0:T(8,128)(2,1)S(1)} %shard_map.91.refs_0_, bf16[512,32]{1,0:T(8,128)(2,1)S(1)} %collective-permute-done.14.refs_1_, ...), custom_call_target="tpu_custom_call" | custom-call | flops 2147483648 | bytes 6291456 | tf_op jit(solution)/shard_map/pallas_call | solution.py:246
  (83 shorter events, 2.5 us)
Async XLA Ops:
  6.5 14.2 %copy-start = (s32[16]{0:T(128)S(1)}, s32[16]{0:T(128)}, u32[]{:S(2)}) copy-start(s32[16]{0:T(128)} %param.15) | copy-start | bytes 196
  6.5 13.8 %copy-start.19 = (s32[1,6]{1,0:T(1,128)S(1)}, s32[1,6]{1,0:T(1,128)}, u32[]{:S(2)}) copy-start(s32[1,6]{1,0:T(1,128)} %param.13) | copy-start | bytes 76
  6.5 15.2 %copy-start.20 = (s32[16]{0:T(128)S(1)}, s32[16]{0:T(128)}, u32[]{:S(2)}) copy-start(s32[16]{0:T(128)} %param.12) | copy-start | bytes 196
  6.5 15.7 %copy-start.7 = (bf16[4,32,8192]{2,1,0:T(8,128)(2,1)S(1)}, bf16[4,32,8192]{2,1,0:T(8,128)(2,1)}, u32[]{:S(2)}) copy-start(bf16[4,32,8192]{2,1,0:T(8,128)(2,1)} %down.7) | copy-start | bytes 6291460
  6.5 133.5 %all-gather.7.cloned.1.call-start = ((), (), s32[]{:S(2)}) async-start(), calls=%async_computation.1 | async-start | bytes 5242880 | tf_op jit(solution)/shard_map/all_gather | solution.py:331
  9.0 154.1 %all-gather.5.cloned.1.call-start = ((), (), s32[]{:S(2)}) async-start(), calls=%async_computation | async-start | bytes 2621440 | tf_op jit(solution)/shard_map/all_gather | solution.py:331
  9.1 12.6 %collective-permute-start.5 = (s32[1,6]{1,0:T(1,128)}, s32[1,6]{1,0:T(1,128)S(1)}, u32[]{:S(2)}, u32[]{:S(2)}) collective-permute-start(s32[1,6]{1,0:T(1,128)} %param.13), channel_id=1, source_target_pairs={{0,1},{1,0},{2,3},{3,2},{4,5},{5,4},{6,7},{7,6},{8,9},{9,8},{10,11... | collective-permute-start | bytes 80 | tf_op jit(solution)/shard_map/ppermute | solution.py:291
  9.6 12.1 %collective-permute-start.7 = (s32[1,6]{1,0:T(1,128)}, s32[1,6]{1,0:T(1,128)S(1)}, u32[]{:S(2)}, u32[]{:S(2)}) collective-permute-start(s32[1,6]{1,0:T(1,128)} %param.13), channel_id=1, source_target_pairs={{0,2},{1,3},{2,0},{3,1},{4,6},{5,7},{6,4},{7,5},{8,10},{9,11},{10,... | collective-permute-start | bytes 80 | tf_op jit(solution)/shard_map/ppermute | solution.py:291
  12.2 9.5 %collective-permute-start.9 = (s32[1,6]{1,0:T(1,128)}, s32[1,6]{1,0:T(1,128)S(1)}, u32[]{:S(2)}, u32[]{:S(2)}) collective-permute-start(s32[1,6]{1,0:T(1,128)} %param.13), channel_id=1, source_target_pairs={{0,3},{1,2},{2,1},{3,0},{4,7},{5,6},{6,5},{7,4},{8,11},{9,10},{10,... | collective-permute-start | bytes 80 | tf_op jit(solution)/shard_map/ppermute | solution.py:291
  15.2 26.0 %collective-permute-start = (bf16[1,512,512]{2,1,0:T(8,128)(2,1)S(1)}, bf16[1,512,512]{2,1,0:T(8,128)(2,1)S(1)}, u32[]{:S(2)}, u32[]{:S(2)}) collective-permute-start(bf16[1,512,512]{2,1,0:T(8,128)(2,1)S(1)} %slice_bitcast_fusion.refs_0_), channel_id=1, source_target_pairs={{0,4},{4,8},{8,12},{1,5},{5,9},{9,13},{2,6},{6,10},{10,14},{3,7},{... | collective-permute-start | bytes 1572872 | tf_op jit(solution)/shard_map/ppermute | solution.py:340
  18.9 38.1 %collective-permute-start.2 = (bf16[1,512,512]{2,1,0:T(8,128)(2,1)S(1)}, bf16[1,512,512]{2,1,0:T(8,128)(2,1)}, u32[]{:S(2)}, u32[]{:S(2)}) collective-permute-start(bf16[1,512,512]{2,1,0:T(8,128)(2,1)S(1)} %slice_bitcast_fusion.refs_0_), channel_id=1, source_target_pairs={{4,0},{8,4},{12,8},{5,1},{9,5},{13,9},{6,2},{10,6},{14,10},{7,3},{... | collective-permute-start | bytes 1572872 | tf_op jit(solution)/shard_map/ppermute | solution.py:341
  24.9 68.7 %collective-permute-start.12 = (bf16[2,128,2048]{2,1,0:T(8,128)(2,1)S(1)}, bf16[2,128,2048]{2,1,0:T(8,128)(2,1)S(1)}, u32[]{:S(2)}, u32[]{:S(2)}) collective-permute-start(bf16[2,128,2048]{2,1,0:T(8,128)(2,1)S(1)} %get-tuple-element.40), channel_id=1, source_target_pairs={{0,2},{1,3},{2,0},{3,1},{4,6},{5,7},{6,4},{7,5},{8,10},{9,11},{10,... | collective-permute-start | bytes 3145736 | tf_op jit(solution)/shard_map/ppermute | solution.py:349
  29.5 78.8 %collective-permute-start.10 = (bf16[2,4,32,2048]{3,2,1,0:T(8,128)(2,1)}, bf16[2,4,32,2048]{3,2,1,0:T(8,128)(2,1)}, u32[]{:S(2)}, u32[]{:S(2)}) collective-permute-start(bf16[2,4,32,2048]{3,2,1,0:T(8,128)(2,1)} %get-tuple-element.29), channel_id=1, source_target_pairs={{0,3},{1,2},{2,1},{3,0},{4,7},{5,6},{6,5},{7,4},{8,11},{9,10},{10,... | collective-permute-start | bytes 3145736 | tf_op jit(solution)/shard_map/ppermute | solution.py:349
  29.5 65.4 %collective-permute-start.13 = (bf16[2,128,2048]{2,1,0:T(8,128)(2,1)S(1)}, bf16[2,128,2048]{2,1,0:T(8,128)(2,1)S(1)}, u32[]{:S(2)}, u32[]{:S(2)}) collective-permute-start(bf16[2,128,2048]{2,1,0:T(8,128)(2,1)S(1)} %get-tuple-element.41), channel_id=1, source_target_pairs={{0,3},{1,2},{2,1},{3,0},{4,7},{5,6},{6,5},{7,4},{8,11},{9,10},{10,... | collective-permute-start | bytes 3145736 | tf_op jit(solution)/shard_map/ppermute | solution.py:349
  41.2 52.7 %copy-start.16 = (bf16[1,512,512]{2,1,0:T(8,128)(2,1)}, bf16[1,512,512]{2,1,0:T(8,128)(2,1)S(1)}, u32[]{:S(2)}) copy-start(bf16[1,512,512]{2,1,0:T(8,128)(2,1)S(1)} %collective-permute-done.refs_1_) | copy-start | bytes 1572868
  41.2 20.5 %collective-permute-start.1 = (bf16[1,512,512]{2,1,0:T(8,128)(2,1)S(1)}, bf16[1,512,512]{2,1,0:T(8,128)(2,1)S(1)}, u32[]{:S(2)}, u32[]{:S(2)}) collective-permute-start(bf16[1,512,512]{2,1,0:T(8,128)(2,1)S(1)} %collective-permute-done.refs_1_), channel_id=1, source_target_pairs={{4,8},{8,12},{5,9},{9,13},{6,10},{10,14},{7,11},{11,15},{20,24},{2... | collective-permute-start | bytes 1572872 | tf_op jit(solution)/shard_map/ppermute | solution.py:353
  57.0 36.3 %collective-permute-start.3 = (bf16[1,512,512]{2,1,0:T(8,128)(2,1)}, bf16[1,512,512]{2,1,0:T(8,128)(2,1)S(1)}, u32[]{:S(2)}, u32[]{:S(2)}) collective-permute-start(bf16[1,512,512]{2,1,0:T(8,128)(2,1)} %collective-permute-done.2.refs_2_), channel_id=1, source_target_pairs={{4,0},{8,4},{5,1},{9,5},{6,2},{10,6},{7,3},{11,7},{20,16},{24,20},... | collective-permute-start | bytes 1572872 | tf_op jit(solution)/shard_map/ppermute | solution.py:354
  58.6 41.7 %copy-start.18 = (s32[512]{0:T(512)S(1)}, s32[512]{0:T(512)}, u32[]{:S(2)}) copy-start(s32[512]{0:T(512)} %param.14) | copy-start | bytes 6148
  61.6 55.9 %collective-permute-start.8 = (bf16[2,4,32,2048]{3,2,1,0:T(8,128)(2,1)}, bf16[2,4,32,2048]{3,2,1,0:T(8,128)(2,1)}, u32[]{:S(2)}, u32[]{:S(2)}) collective-permute-start(bf16[2,4,32,2048]{3,2,1,0:T(8,128)(2,1)} %get-tuple-element.28), channel_id=1, source_target_pairs={{0,2},{1,3},{2,0},{3,1},{4,6},{5,7},{6,4},{7,5},{8,10},{9,11},{10,... | collective-permute-start | bytes 3145736 | tf_op jit(solution)/shard_map/ppermute | solution.py:349
  93.4 24.2 %collective-permute-start.6 = (bf16[2,4,32,2048]{3,2,1,0:T(8,128)(2,1)}, bf16[2,4,32,2048]{3,2,1,0:T(8,128)(2,1)}, u32[]{:S(2)}, u32[]{:S(2)}) collective-permute-start(bf16[2,4,32,2048]{3,2,1,0:T(8,128)(2,1)} %get-tuple-element.27), channel_id=1, source_target_pairs={{0,1},{1,0},{2,3},{3,2},{4,5},{5,4},{6,7},{7,6},{8,9},{9,8},{10,11... | collective-permute-start | bytes 3145736 | tf_op jit(solution)/shard_map/ppermute | solution.py:349
  93.6 1.0 copy-start.8
  93.6 7.2 %collective-permute-start.11 = (bf16[2,128,2048]{2,1,0:T(8,128)(2,1)}, bf16[2,128,2048]{2,1,0:T(8,128)(2,1)}, u32[]{:S(2)}, u32[]{:S(2)}) collective-permute-start(bf16[2,128,2048]{2,1,0:T(8,128)(2,1)} %get-tuple-element.39), channel_id=1, source_target_pairs={{0,1},{1,0},{2,3},{3,2},{4,5},{5,4},{6,7},{7,6},{8,9},{9,8},{10,11... | collective-permute-start | bytes 3145736 | tf_op jit(solution)/shard_map/ppermute | solution.py:349
  94.9 5.6 %copy-start.10 = (bf16[2,128,2048]{2,1,0:T(8,128)(2,1)}, bf16[2,128,2048]{2,1,0:T(8,128)(2,1)S(1)}, u32[]{:S(2)}) copy-start(bf16[2,128,2048]{2,1,0:T(8,128)(2,1)S(1)} %collective-permute-done.13.refs_3_) | copy-start | bytes 3145732
  94.9 31.4 %collective-permute-start.4 = (bf16[1,512,512]{2,1,0:T(8,128)(2,1)S(1)}, bf16[1,512,512]{2,1,0:T(8,128)(2,1)}, u32[]{:S(2)}, u32[]{:S(2)}) collective-permute-start(bf16[1,512,512]{2,1,0:T(8,128)(2,1)S(1)} %broadcast_select_fusion.refs_0_), channel_id=1, source_target_pairs={{8,12},{4,0},{9,13},{5,1},{10,14},{6,2},{11,15},{7,3},{24,28},{20,... | collective-permute-start | bytes 1572872 | tf_op jit(solution)/shard_map/ppermute | solution.py:357
  98.3 1.0 copy-start.12
  99.3 1.0 copy-start.14
  100.8 1.2 copy-start.9
  102.0 1.2 copy-start.11
  103.2 1.2 copy-start.15
  104.4 21.8 %copy-start.13 = (bf16[2,4,32,2048]{3,2,1,0:T(8,128)(2,1)S(1)}, bf16[2,4,32,2048]{3,2,1,0:T(8,128)(2,1)}, u32[]{:S(2)}) copy-start(bf16[2,4,32,2048]{3,2,1,0:T(8,128)(2,1)} %copy-done.12) | copy-start | bytes 3145732
  126.3 4.6 %copy-start.17 = (bf16[1,512,512]{2,1,0:T(8,128)(2,1)S(1)}, bf16[1,512,512]{2,1,0:T(8,128)(2,1)}, u32[]{:S(2)}) copy-start(bf16[1,512,512]{2,1,0:T(8,128)(2,1)} %copy-done.16) | copy-start | bytes 1572868
  138.1 1.9 copy-start.3
  140.0 2.2 %copy-start.4 = (f32[512,2048]{1,0:T(8,128)S(1)}, f32[512,2048]{1,0:T(8,128)}, u32[]{:S(2)}) copy-start(f32[512,2048]{1,0:T(8,128)} %copy-done.3) | copy-start | bytes 12582916
  161.2 1.9 copy-start.5
  163.1 2.2 %copy-start.2 = (bf16[16,256,512]{2,1,0:T(8,128)(2,1)S(1)}, bf16[16,256,512]{2,1,0:T(8,128)(2,1)}, u32[]{:S(2)}) copy-start(bf16[16,256,512]{2,1,0:T(8,128)(2,1)} %shard_map.86.refs_4_.refs_1_) | copy-start | bytes 12582916
  165.3 7.3 %copy-start.6 = (f32[512,2048]{1,0:T(8,128)S(1)}, f32[512,2048]{1,0:T(8,128)}, u32[]{:S(2)}) copy-start(f32[512,2048]{1,0:T(8,128)} %copy-done.5) | copy-start | bytes 12582916
  170.5 10.2 %collective-permute-start.14 = (bf16[512,32]{1,0:T(8,128)(2,1)S(1)}, bf16[512,32]{1,0:T(8,128)(2,1)S(1)}, u32[]{:S(2)}, u32[]{:S(2)}) collective-permute-start(bf16[512,32]{1,0:T(8,128)(2,1)S(1)} %shard_map.91.refs_0_), channel_id=1, source_target_pairs={{0,12},{4,0},{8,4},{12,8},{1,13},{5,1},{9,5},{13,9},{2,14},{6,2},{... | collective-permute-start | bytes 98312 | tf_op jit(solution)/shard_map/ppermute | solution.py:386
  170.5 12.8 %collective-permute-start.15 = (bf16[512,32]{1,0:T(8,128)(2,1)S(1)}, bf16[512,32]{1,0:T(8,128)(2,1)S(1)}, u32[]{:S(2)}, u32[]{:S(2)}) collective-permute-start(bf16[512,32]{1,0:T(8,128)(2,1)S(1)} %shard_map.91.refs_0_), channel_id=1, source_target_pairs={{0,8},{4,12},{8,0},{12,4},{1,9},{5,13},{9,1},{13,5},{2,10},{6,14},... | collective-permute-start | bytes 98312 | tf_op jit(solution)/shard_map/ppermute | solution.py:386
  171.4 11.9 %collective-permute-start.16 = (bf16[512,32]{1,0:T(8,128)(2,1)S(1)}, bf16[512,32]{1,0:T(8,128)(2,1)S(1)}, u32[]{:S(2)}, u32[]{:S(2)}) collective-permute-start(bf16[512,32]{1,0:T(8,128)(2,1)S(1)} %shard_map.91.refs_0_), channel_id=1, source_target_pairs={{0,4},{4,8},{8,12},{12,0},{1,5},{5,9},{9,13},{13,1},{2,6},{6,10},{... | collective-permute-start | bytes 98312 | tf_op jit(solution)/shard_map/ppermute | solution.py:386
  172.5 20.5 %copy-start.1 = (s32[16]{0:T(128)S(1)}, s32[16]{0:T(128)}, u32[]{:S(2)}) copy-start(s32[16]{0:T(128)} %param.15) | copy-start | bytes 196
Sparse Core Ops, SparseCore 0:
  9.1 105.5 all-gather.6
  116.3 44.0 all-gather.4

commit v7 on v5

v7 whole, which is shorter than its diff:
```python
import functools

import jax
import jax.numpy as jnp
from jax import lax
from jax.experimental import pallas as pl
from jax.experimental.pallas import tpu as pltpu
from jax.sharding import PartitionSpec as P

CAP = 2
ALIGN = 256
LINE = 512
GATHERED = (1280, 256)
PARAMS = pltpu.CompilerParams(vmem_limit_bytes=48 * 2**20)
TAIL_PARAMS = pltpu.CompilerParams(vmem_limit_bytes=24 * 2**20)
F32 = jnp.float32
BF16 = jnp.bfloat16


def pick_kernel(places, down, up, down_out, up_out):
    shards, _, width = down_out.shape[1:]
    for t in range(shards):
        down_out[0, t] = down[0, :, t * width:(t + 1) * width]
    up_out[...] = up[...]


def pick_pages(places, down, up, shards):
    count = places.shape[0]
    _, rank_part, features = down.shape
    shapes = [(shards, rank_part, features // shards), up.shape[1:]]
    return pl.pallas_call(
        pick_kernel,
        out_shape=[jax.ShapeDtypeStruct((count,) + shape, BF16) for shape in shapes],
        grid_spec=pltpu.PrefetchScalarGridSpec(
            num_scalar_prefetch=1,
            grid=(count,),
            in_specs=[pl.BlockSpec((1,) + a.shape[1:], lambda i, places: (places[i], 0, 0)) for a in (down, up)],
            out_specs=[
                pl.BlockSpec((1,) + shapes[0], lambda i, places: (i, 0, 0, 0)),
                pl.BlockSpec((1,) + shapes[1], lambda i, places: (i, 0, 0)),
            ],
        ),
        compiler_params=PARAMS,
    )(places, down, up)


def join_downs_kernel(*refs):
    *pages, out = refs
    joined = jnp.concatenate([p[c, 0] for p in pages for c in range(CAP)], axis=0)
    out[...] = joined.T


def join_downs(downs):
    _, shards, rank_part, features = downs[0].shape
    slots = CAP * rank_part * len(downs)
    return pl.pallas_call(
        join_downs_kernel,
        out_shape=jax.ShapeDtypeStruct((shards * features, slots), BF16),
        grid=(shards,),
        in_specs=[pl.BlockSpec((CAP, 1, rank_part, features), lambda t: (0, t, 0, 0))] * len(downs),
        out_specs=pl.BlockSpec((features, slots), lambda t: (t, 0)),
        compiler_params=PARAMS,
    )(*downs)


def join_ups_kernel(*refs):
    *pages, out = refs
    for j, p in enumerate(pages):

        @pl.when(pl.program_id(0) == j)
        def _():
            out[...] = p[...]


def join_ups(ups):
    count, rank, columns = ups[0].shape
    return pl.pallas_call(
        join_ups_kernel,
        out_shape=jax.ShapeDtypeStruct((count * len(ups), rank, columns), BF16),
        grid=(len(ups),),
        in_specs=[pl.BlockSpec(up.shape, lambda j: (0, 0, 0)) for up in ups],
        out_specs=pl.BlockSpec(ups[0].shape, lambda j: (j, 0, 0)),
        compiler_params=PARAMS,
    )(*ups).reshape(-1, columns)


RESIDENT = pl.BlockSpec(memory_space=pltpu.VMEM)
IN_HBM = pl.BlockSpec(memory_space=pltpu.HBM)


def chunk_kernel(counts, held, start, valid, *refs):
    refs = list(refs)
    xs = [refs.pop(0) for _ in counts]
    weight, down = refs.pop(0), refs.pop(0)
    totals, (base, low) = refs[:-2], refs[-2:]
    step = pl.program_id(0)

    @pl.when(step == 0)
    def _():
        base[...] = totals[0][...] if held else jnp.zeros_like(base)
        low[...] = totals[1][...] if held else jnp.zeros_like(low)

    first = 0
    for x, count in zip(xs, counts):

        @pl.when((step >= first) & (step < first + count) & (valid[step] != 0))
        def _():
            part = min(base.shape[1], 512)
            for n in range(0, base.shape[1], part):
                base[:, n:n + part] += jnp.dot(x[0], weight[:, n:n + part], preferred_element_type=F32)
            low[...] += jnp.dot(x[0], down[...], preferred_element_type=F32)

        first += count


def add_chunk(totals, xs, source, first, weight, down):
    rows, features = xs[0].shape[1:]
    columns, slots = weight.shape[1], down.shape[1]
    counts = [x.shape[0] for x in xs]
    steps = sum(counts)
    n_tensor = lax.axis_size("tensor")
    valid = ((source >= 0) & (source < n_tensor)).astype(jnp.int32)
    start = (jnp.clip(source, 0, n_tensor - 1) * (weight.shape[0] // n_tensor) + first) // ALIGN
    start = start.astype(jnp.int32)
    x_specs, begin = [], 0
    for count in counts:
        x_specs.append(
            pl.BlockSpec(
                (1, rows, features),
                lambda s, *_, begin=begin, count=count: (jnp.clip(s - begin, 0, count - 1), 0, 0),
            )
        )
        begin += count
    walked = [
        pl.BlockSpec((pl.Element(features), pl.Element(a)), lambda s, start, valid: (start[s] * ALIGN, 0))
        for a in (columns, slots)
    ]
    whole = [pl.BlockSpec((rows, a), lambda s, *_: (0, 0)) for a in (columns, slots)]
    return pl.pallas_call(
        functools.partial(chunk_kernel, counts, bool(totals)),
        out_shape=[jax.ShapeDtypeStruct((rows, a), F32) for a in (columns, slots)],
        grid_spec=pltpu.PrefetchScalarGridSpec(
            num_scalar_prefetch=2,
            grid=(steps,),
            in_specs=x_specs + walked + (whole if totals else []),
            out_specs=whole,
        ),
        compiler_params=PARAMS,
        cost_estimate=pl.CostEstimate(
            flops=2 * steps * features * rows * (columns + slots),
            bytes_accessed=2 * steps * features * (rows + columns + slots) + 8 * rows * (columns + slots),
            transcendentals=0,
        ),
    )(start, valid, *xs, weight, down, *totals)


def low_kernel(first, x_hbm, down, total, slot, live, out, x, rows_of, sems):
    shards, _, features = x.shape
    width = down.shape[0] // shards
    rank_part = out.shape[1]
    copies = [
        pltpu.make_async_copy(down.at[pl.ds(t * width + first, features)], rows_of.at[t], sems.at[t])
        for t in range(shards)
    ]
    copies += [pltpu.make_async_copy(x_hbm.at[t], x.at[t], sems.at[shards + t]) for t in range(shards)]
    for copy in copies:
        copy.start()
    low = total[...]
    for t in range(shards):
        copies[t].wait()
        copies[shards + t].wait()
        low += jnp.dot(x[t], rows_of[t], preferred_element_type=F32)
    lane = lax.broadcasted_iota(jnp.int32, low.shape, 1)
    own = jnp.where(lane // rank_part == slot[...], low, 0.0).astype(BF16)
    fold = (
        lax.rem(lax.broadcasted_iota(jnp.int32, (low.shape[1], rank_part), 0), rank_part)
        == lax.broadcasted_iota(jnp.int32, (low.shape[1], rank_part), 1)
    ).astype(BF16)
    mine = jnp.dot(own, fold, preferred_element_type=F32)
    k = lax.broadcasted_iota(jnp.int32, mine.shape, 1)
    out[...] = jnp.where(k < live[...], mine, 0.0).astype(BF16)


def finish_low(total, x, first, down, slot, live, rank_part):
    shards, rows, features = x.shape
    slots = down.shape[1]
    return pl.pallas_call(
        functools.partial(low_kernel, first),
        out_shape=jax.ShapeDtypeStruct((rows, rank_part), BF16),
        in_specs=[IN_HBM, IN_HBM, RESIDENT, RESIDENT, RESIDENT],
        out_specs=RESIDENT,
        scratch_shapes=[
            pltpu.VMEM(x.shape, BF16),
            pltpu.VMEM((shards, features, slots), BF16),
            pltpu.SemaphoreType.DMA((2 * shards,)),
        ],
        compiler_params=TAIL_PARAMS,
        cost_estimate=pl.CostEstimate(
            flops=2 * shards * features * rows * slots,
            bytes_accessed=2 * shards * features * (rows + slots) + 4 * rows * slots,
            transcendentals=0,
        ),
    )(x, down, total, slot, live)


def base_kernel(first, x, weight, total, up, out, up_out, xs, ws, ts, sems, up_sem):
    shards, rows, features = x.shape
    columns = out.shape[1]
    parts, _, _, part = ws.shape
    width = weight.shape[0] // shards
    for t in range(shards):
        pltpu.make_async_copy(x.at[t], xs.at[t], sems.at[parts, t]).start()

    def copies(n):
        cut = pl.ds(n * part, part)
        return [
            pltpu.make_async_copy(
                weight.at[pl.ds(t * width + first, features), cut], ws.at[n, t], sems.at[n, t]
            )
            for t in range(shards)
        ] + [pltpu.make_async_copy(total.at[:, cut], ts.at[n], sems.at[n, shards])]

    for n in range(parts):
        for copy in copies(n):
            copy.start()
    pltpu.make_async_copy(up, up_out, up_sem).start()
    for t in range(shards):
        pltpu.make_async_copy(x.at[t], xs.at[t], sems.at[parts, t]).wait()
    joined = jnp.concatenate([xs[t] for t in range(shards)], axis=1)
    for n in range(parts):
        for copy in copies(n):
            copy.wait()
        w = ws[n].reshape(shards * features, part)
        out[:, n * part:(n + 1) * part] = ts[n] + jnp.dot(joined, w, preferred_element_type=F32)
    pltpu.make_async_copy(up, up_out, up_sem).wait()


def add_last(total, x, first, weight, up):
    shards, rows, features = x.shape
    columns = weight.shape[1]
    part = min(columns, 512)
    parts = columns // part
    return pl.pallas_call(
        functools.partial(base_kernel, first),
        out_shape=[pltpu.VMEM((rows, columns), F32), pltpu.VMEM(up.shape, BF16)],
        in_specs=[IN_HBM] * 4,
        out_specs=[RESIDENT] * 2,
        scratch_shapes=[
            pltpu.VMEM((shards, rows, features), BF16),
            pltpu.VMEM((parts, shards, features, part), BF16),
            pltpu.VMEM((parts, rows, part), F32),
            pltpu.SemaphoreType.DMA((parts + 1, shards + 1)),
            pltpu.SemaphoreType.DMA,
        ],
        compiler_params=TAIL_PARAMS,
        cost_estimate=pl.CostEstimate(
            flops=2 * shards * features * rows * columns,
            bytes_accessed=2 * shards * features * (rows + columns) + 4 * rows * columns,
            transcendentals=0,
        ),
    )(x, weight, total, up)


def finish_kernel(parts, me, slot, total, up, *refs):
    lows, (out, spread) = refs[:parts], refs[parts:]
    rank_part = lows[0].shape[1]
    rank = parts * rank_part
    part = out.shape[1]

    @pl.when(pl.program_id(0) == 0)
    def _():
        low = jnp.concatenate([part[...].astype(F32) for part in lows], axis=1)
        low = pltpu.roll(low, me[0] * rank_part, 1)
        for e in range(spread.shape[1] // rank):
            spread[:, e * rank:(e + 1) * rank] = jnp.where(slot[...] == e, low, 0.0).astype(BF16)

    cut = pl.ds(pl.multiple_of(pl.program_id(0) * part, part), part)
    out[...] = (total[:, cut] + jnp.dot(spread[...], up[:, cut], preferred_element_type=F32)).astype(BF16)


def finish(me, slot, total, up, lows):
    rows, columns = total.shape
    depth = up.shape[0]
    part = min(columns, 512)
    return pl.pallas_call(
        functools.partial(finish_kernel, len(lows)),
        grid=(columns // part,),
        out_shape=jax.ShapeDtypeStruct((rows, columns), BF16),
        in_specs=[pl.BlockSpec(memory_space=pltpu.SMEM)] + [RESIDENT] * (3 + len(lows)),
        out_specs=pl.BlockSpec((rows, part), lambda n: (0, n)),
        scratch_shapes=[pltpu.VMEM((rows, depth), BF16)],
        compiler_params=TAIL_PARAMS,
        cost_estimate=pl.CostEstimate(
            flops=2 * rows * depth * columns,
            bytes_accessed=2 * rows * columns,
            transcendentals=0,
        ),
    )(me, slot, total, up, *lows)


def after(value, *earlier):
    return lax.optimization_barrier((value,) + earlier)[0]


def asked_pages(requests, adapter_page_row, holder_length):
    n_dp = lax.axis_size("dp")
    dp = lax.axis_index("dp")
    count = adapter_page_row.shape[0]

    def pages_of(wanted):
        hit = wanted[:, None] == jnp.arange(count)[None, :]
        return jnp.sum(jnp.where(hit, adapter_page_row[None, :], 0), axis=1)

    def order_in(holders):
        same = holders[:, None] == holders[None, :]
        n = holders.shape[0]
        earlier = jnp.arange(n)[:, None] > jnp.arange(n)[None, :]
        return jnp.sum((same & earlier).astype(jnp.int32), axis=1)

    own = pages_of(requests[0])
    holders = own // holder_length
    slots = (holders ^ dp) * CAP + order_in(holders)
    places = []
    for j in range(n_dp):
        wanted = requests if j == 0 else lax.ppermute(requests, "dp", [(i, i ^ j) for i in range(n_dp)])
        pages = pages_of(wanted[0])
        holder = pages // holder_length
        order = jnp.where(holder == dp, order_in(holder), -1)
        hit = order[None, :] == jnp.arange(CAP)[:, None]
        places.append(jnp.sum(jnp.where(hit, (pages % holder_length)[None, :], 0), axis=1))
    return slots, places


def local(
    attention_result,
    output_weight,
    adapter_down_weight,
    adapter_up_weight,
    adapter_page_row,
    requests,
    row_request_entry,
    ranks,
):
    n_dp = lax.axis_size("dp")
    n_tensor = lax.axis_size("tensor")
    me = lax.axis_index("tensor")
    rows, width = attention_result.shape
    holder_length, rank_part, _ = adapter_down_weight.shape
    rank, columns = adapter_up_weight.shape[1:]
    own_list = requests[0]
    entries = own_list.shape[0]
    one_hot = row_request_entry[:, None] == jnp.arange(entries)[None, :]
    row_rank = jnp.sum(jnp.where(one_hot, ranks[own_list][None, :], 0), axis=1)
    if n_tensor != 4 or width != LINE + sum(GATHERED) or rank_part % 16:
        return plain(
            attention_result, output_weight, adapter_down_weight, adapter_up_weight, adapter_page_row,
            own_list, one_hot, row_rank,
        )

    gathered, x, first = [], attention_result, 0
    for features in GATHERED:
        piece = x[:, first:first + features]
        gathered.append(lax.all_gather(piece, "tensor", axis=0))
        x = after(x, piece)
        first += features + LINE

    middle = GATHERED[0]
    last = middle + LINE
    line = x[None, :, middle:last]
    right = [(i, i + 1) for i in range(n_tensor - 1)]
    left = [(i + 1, i) for i in range(n_tensor - 1)]
    right_1 = lax.ppermute(line, "tensor", right)
    left_1 = lax.ppermute(line, "tensor", left)

    slots, places = asked_pages(requests, adapter_page_row, holder_length)
    downs, ups = [], []
    for j in range(n_dp):
        down, up = pick_pages(places[j], adapter_down_weight, adapter_up_weight, n_tensor)
        if j:
            pairs = [(i, i ^ j) for i in range(n_dp)]
            down, up = lax.ppermute(down, "dp", pairs), lax.ppermute(up, "dp", pairs)
        downs.append(down)
        ups.append(up)

    right_2 = lax.ppermute(right_1, "tensor", right[1:])
    left_2 = lax.ppermute(left_1, "tensor", left[:-1])
    upper = me >= n_tensor // 2
    second = jnp.where(upper, right_2, left_2)
    third = lax.ppermute(second, "tensor", right[-1:] + left[:1])
    down = join_downs(after(tuple(downs), third))
    up = join_ups(ups)

    slot = jnp.sum(jnp.where(one_hot, slots[None, :], 0), axis=1)[:, None]
    live = row_rank[:, None] - me * rank_part
    toward = jnp.where(upper, -1, 1)
    source = me + jnp.stack([jnp.zeros_like(me), -jnp.ones_like(me), jnp.ones_like(me), 2 * toward, 3 * toward])
    blocks = [line, right_1, left_1, second, third]
    totals = add_chunk((), blocks, source, middle, output_weight, down)
    totals = add_chunk(totals, gathered[:1], jnp.arange(n_tensor), 0, output_weight, down)
    x = pltpu.with_memory_space_constraint(after(gathered[1], *totals, up), pltpu.HBM)
    low = finish_low(totals[1], x, last, down, slot, live, rank_part)
    base, up = add_last(totals[0], x, last, output_weight, up)
    lows = [low] + [
        lax.ppermute(low, "tensor", [(i, (i - j) % n_tensor) for i in range(n_tensor)])
        for j in range(1, n_tensor)
    ]
    return finish(me[None], slot, base, up, lows)


def gather_pages(block, n_dp):
    return [block] + [
        lax.ppermute(block, "dp", [(i, i ^ j) for i in range(n_dp)]) for j in range(1, n_dp)
    ]


def plain(x, output_weight, down_weight, up_weight, adapter_page_row, own_list, one_hot, row_rank):
    n_dp = lax.axis_size("dp")
    dp = lax.axis_index("dp")
    rows = x.shape[0]
    holder_length = down_weight.shape[0]
    rank, columns = up_weight.shape[1:]
    entries = one_hot.shape[1]
    pages = adapter_page_row[own_list]
    places = ((pages // holder_length) ^ dp) * holder_length + pages % holder_length

    def requested(block):
        blocks = jnp.concatenate(gather_pages(block, n_dp), axis=0)
        return jnp.concatenate(
            [lax.dynamic_slice_in_dim(blocks, places[e], 1, 0) for e in range(entries)], axis=0
        )

    down, up = requested(down_weight), requested(up_weight)
    x = lax.all_gather(x, "tensor", axis=1, tiled=True)
    base = jnp.dot(x, output_weight, preferred_element_type=F32)
    low = jnp.einsum("rd,ekd->rek", x, down, preferred_element_type=F32)
    low = jnp.sum(jnp.where(one_hot[:, :, None], low, 0.0), axis=1).astype(BF16)
    low = lax.all_gather(low, "tensor", axis=1, tiled=True)
    low = jnp.where(jnp.arange(rank)[None, :] < row_rank[:, None], low, jnp.zeros_like(low))
    spread = jnp.where(one_hot[:, :, None], low[:, None, :], jnp.zeros((), BF16))
    term = jnp.dot(
        spread.reshape(rows, entries * rank), up.reshape(entries * rank, columns), preferred_element_type=F32
    )
    return (base + term).astype(BF16)


def solution(mesh):
    in_specs = (
        P(("groups", "dp"), "tensor"),
        P(None, "tensor"),
        P("dp", "tensor", None),
        P("dp", None, "tensor"),
        P("groups"),
        P(("groups", "dp"), None),
        P(("groups", "dp")),
        P(),
    )
    out_specs = P(("groups", "dp"), "tensor")
    return jax.shard_map(local, mesh=mesh, in_specs=in_specs, out_specs=out_specs, check_vma=False)
```

time: 197 us -> 210 us (1.066)
  waiting for transfers between devices: 69.9 us -> 95.2 us
  Pallas kernels: 77.4 us -> 62.7 us
  local copies, waits for them, and re-layouts: 9.22 us -> 18.7 us
  other arithmetic: 6.98 us -> 1.66 us
    ppermute x1, waiting for transfers between devices: 5.84 us -> 25 us  [local(): third = lax.ppermute(second, 'tensor', right[-1:] + left[:1])]
    unnamed x28 -> x40, local copies, waits for them, and re-layouts: 1.61 us -> 12.3 us
    pallas_call x6, Pallas kernels: 56.5 us -> 47.8 us  [the longest x2 31.3 us: add_chunk(): pl.pallas_call(functools.partial(chunk_kernel, counts, bool(totals)), out...]
    ppermute x1, waiting for transfers between devices: 5.83 us -> 10.5 us  [local(): right_1 = lax.ppermute(line, 'tensor', right)]
    ppermute x6, waiting for transfers between devices: 13.2 us -> 9.02 us  [local(): down, up = (lax.ppermute(down, 'dp', pairs), lax.ppermute(up, 'dp', pairs))]
    pallas_call x4, Pallas kernels: 13.4 us -> 10.3 us  [pick_pages(): pl.pallas_call(pick_kernel, out_shape=[jax.ShapeDtypeStruct((count,) + sh...]
    pallas_call x1, Pallas kernels: 7.46 us -> 4.58 us  [finish(): pl.pallas_call(functools.partial(finish_kernel, len(lows)), grid=(columns...]
    ppermute x3, waiting for transfers between devices: 0.72 us -> 3.56 us  [local(): lax.ppermute(low, 'tensor', [(i, (i - j) % n_tensor) for i in range(n_ten...]
  transfers between devices with their start and end apart: 19 -> 19, of which waited for: 7 -> 7; matrix products, arithmetic and copies ran while one was open for 6% -> 3% of each run, Pallas kernels for 33% -> 26%
where the time goes in v7:
time: 210 us; the launch traced here: 209 us
  waiting for transfers between devices  95.2 us (45%)
  Pallas kernels  62.7 us (30%)
  local copies, waits for them, and re-layouts  18.7 us (9%)
  starting transfers between devices  16.9 us (8%)
  between operations  13.7 us (7%)
    pallas_call x2, Pallas kernels, add_chunk(): pl.pallas_call(functools.partial(chunk_kernel, counts, bool(totals)), out...  31.3 us
    ppermute x1, waiting for transfers between devices, local(): left_2 = lax.ppermute(left_1, 'tensor', left[:-1])  30.9 us
    ppermute x1, waiting for transfers between devices, local(): third = lax.ppermute(second, 'tensor', right[-1:] + left[:1])  25 us
    ppermute x1, waiting for transfers between devices, local(): left_1 = lax.ppermute(line, 'tensor', left)  16.2 us
    unnamed x40, local copies, waits for them, and re-layouts  12.3 us
    ppermute x1, waiting for transfers between devices, local(): right_1 = lax.ppermute(line, 'tensor', right)  10.5 us
    pallas_call x4, Pallas kernels, pick_pages(): pl.pallas_call(pick_kernel, out_shape=[jax.ShapeDtypeStruct((count,) + sh...  10.3 us
    ppermute x6, waiting for transfers between devices, local(): down, up = (lax.ppermute(down, 'dp', pairs), lax.ppermute(up, 'dp', pairs))  9.02 us
  transfers between devices with their start and end apart: 19, of which 7 were waited for; matrix products, arithmetic and copies ran while one was open for 3% of the time, Pallas kernels for 26%

profile of v7, /device:TPU:0, one launch (start us, length us, event | category | flops | bytes accessed | tf_op | source)
XLA Modules:
  0.0 208.8 jit_solution(18342825304685866735)
XLA Ops:
  6.6 2.6 %slice.9 = bf16[512,1280]{1,0:T(8,128)(2,1)} slice(bf16[512,2048]{1,0:T(8,128)(2,1)} %param.8), slice={[0:512], [0:1280]} | slice | bytes 2621440 | tf_op jit(solution)/shard_map/slice | solution.py:362
  9.3 0.5 collective-permute-start
  9.8 2.6 %collective-permute-start.2 = (s32[1,6]{1,0:T(1,128)}, s32[1,6]{1,0:T(1,128)S(1)}, u32[]{:S(2)}, u32[]{:S(2)}) collective-permute-start(s32[1,6]{1,0:T(1,128)} %param.13), channel_id=1, source_target_pairs={{0,2},{1,3},{2,0},{3,1},{4,6},{5,7},{6,4},{7,5},{8,10},{9,11},{10,... | collective-permute-start | bytes 80 | tf_op jit(solution)/shard_map/ppermute | solution.py:325
  12.4 1.7 slice.10
  14.1 1.1 slice_bitcast_fusion.refs_0_
  15.2 3.7 %collective-permute-start.6 = (bf16[1,512,512]{2,1,0:T(8,128)(2,1)S(1)}, bf16[1,512,512]{2,1,0:T(8,128)(2,1)S(1)}, u32[]{:S(2)}, u32[]{:S(2)}) collective-permute-start(bf16[1,512,512]{2,1,0:T(8,128)(2,1)S(1)} %slice_bitcast_fusion.refs_0_), channel_id=1, source_target_pairs={{0,4},{4,8},{8,12},{1,5},{5,9},{9,13},{2,6},{6,10},{10,14},{3,7},{... | collective-permute-start | bytes 1572872 | tf_op jit(solution)/shard_map/ppermute | solution.py:372
  18.9 1.3 collective-permute-start.8
  20.5 0.6 gather_fusion
  21.1 0.2 select_reduce_fusion.2
  21.4 0.2 convert_reduce_fusion.1
  21.7 2.7 %shard_map.84 = (bf16[2,4,32,2048]{3,2,1,0:T(8,128)(2,1)}, bf16[2,128,2048]{2,1,0:T(8,128)(2,1)S(1)}) custom-call(s32[2]{0:T(128)S(1)} %fusion.6.places, bf16[4,32,8192]{2,1,0:T(8,128)(2,1)S(1)} %copy-done.3, bf16[4,128,2048]{2,1,0:T(8,128)(2,1)} %up.7), custom_call_target="tpu_custom_call" | custom-call | tf_op jit(solution)/shard_map/pallas_call | solution.py:31
  24.4 1.5 collective-permute-start.3
  25.9 0.5 collective-permute-start.12
  26.5 0.2 convert_reduce_fusion
  26.8 2.7 %shard_map.85 = (bf16[2,4,32,2048]{3,2,1,0:T(8,128)(2,1)}, bf16[2,128,2048]{2,1,0:T(8,128)(2,1)S(1)}) custom-call(s32[2]{0:T(128)S(1)} %fusion.7.places, bf16[4,32,8192]{2,1,0:T(8,128)(2,1)S(1)} %copy-done.3, bf16[4,128,2048]{2,1,0:T(8,128)(2,1)} %up.7), custom_call_target="tpu_custom_call" | custom-call | tf_op jit(solution)/shard_map/pallas_call | solution.py:31
  29.4 0.6 collective-permute-start.13
  30.1 10.5 %collective-permute-done.6.refs_1_ = bf16[1,512,512]{2,1,0:T(8,128)(2,1)S(1)} collective-permute-done((bf16[1,512,512]{2,1,0:T(8,128)(2,1)S(1)}, bf16[1,512,512]{2,1,0:T(8,128)(2,1)S(1)}, u32[]{:S(2)}, u32[]{:S(2)}) %collective-permute-start.6) | collective-permute-done | bytes 524320 | tf_op jit(solution)/shard_map/ppermute | solution.py:372
  40.5 0.7 collective-permute-start.7
  41.2 16.2 %collective-permute-done.8.refs_2_ = bf16[1,512,512]{2,1,0:T(8,128)(2,1)} collective-permute-done((bf16[1,512,512]{2,1,0:T(8,128)(2,1)S(1)}, bf16[1,512,512]{2,1,0:T(8,128)(2,1)}, u32[]{:S(2)}, u32[]{:S(2)}) %collective-permute-start.8) | collective-permute-done | bytes 524320 | tf_op jit(solution)/shard_map/ppermute | solution.py:373
  57.4 1.3 collective-permute-start.9
  58.8 0.2 convert_reduce_fusion.2
  59.1 3.1 %shard_map.83 = (bf16[2,4,32,2048]{3,2,1,0:T(8,128)(2,1)}, bf16[2,128,2048]{2,1,0:T(8,128)(2,1)}) custom-call(s32[2]{0:T(128)S(1)} %fusion.5.places, bf16[4,32,8192]{2,1,0:T(8,128)(2,1)S(1)} %copy-done.3, bf16[4,128,2048]{2,1,0:T(8,128)(2,1)} %up.7), custom_call_target="tpu_custom_call" | custom-call | tf_op jit(solution)/shard_map/pallas_call | solution.py:31
  62.1 30.9 %collective-permute-done.9 = bf16[1,512,512]{2,1,0:T(8,128)(2,1)S(1)} collective-permute-done((bf16[1,512,512]{2,1,0:T(8,128)(2,1)}, bf16[1,512,512]{2,1,0:T(8,128)(2,1)S(1)}, u32[]{:S(2)}, u32[]{:S(2)}) %collective-permute-start.9) | collective-permute-done | bytes 524320 | tf_op jit(solution)/shard_map/ppermute | solution.py:386
  93.0 0.5 collective-permute-start.11
  93.8 0.2 copy-done.7
  94.0 0.6 collective-permute-done.13.refs_3_
  94.6 1.5 collective-permute-start.10
  96.2 1.8 shard_map.82
  98.1 1.0 copy-done.11
  99.1 1.0 copy-done.13
  100.5 1.2 copy-done.8
  101.7 1.2 copy-done.10
  103.0 1.2 copy-done.14
  104.2 3.9 %shard_map.89 = bf16[8,128,2048]{2,1,0:T(8,128)(2,1)} custom-call(bf16[2,128,2048]{2,1,0:T(8,128)(2,1)S(1)} %copy-done.14, bf16[2,128,2048]{2,1,0:T(8,128)(2,1)} %collective-permute-done.11.refs_1_, bf16[2,128,2048]{2,1,0:T(8,128)(2,1)S(1)} %copy-done.8, bf16[2,128,2048]{2,1,0:T(8,128)(2,1)S(1)} %copy-done.10), custom_call_target="tpu_custom_call" | custom-call | tf_op jit(solution)/shard_map/pallas_call | solution.py:77
  108.1 8.4 %collective-permute-done.5.refs_3_ = bf16[2,4,32,2048]{3,2,1,0:T(8,128)(2,1)} collective-permute-done((bf16[2,4,32,2048]{3,2,1,0:T(8,128)(2,1)}, bf16[2,4,32,2048]{3,2,1,0:T(8,128)(2,1)}, u32[]{:S(2)}, u32[]{:S(2)}) %collective-permute-start.5) | collective-permute-done | bytes 1048608 | tf_op jit(solution)/shard_map/ppermute | solution.py:381
  116.4 25.0 %collective-permute-done.10.refs_4_ = bf16[1,512,512]{2,1,0:T(8,128)(2,1)} collective-permute-done((bf16[1,512,512]{2,1,0:T(8,128)(2,1)S(1)}, bf16[1,512,512]{2,1,0:T(8,128)(2,1)}, u32[]{:S(2)}, u32[]{:S(2)}) %collective-permute-start.10) | collective-permute-done | bytes 524320 | tf_op jit(solution)/shard_map/ppermute | solution.py:389
  141.4 5.0 %shard_map.86.refs_6_.refs_2_.down = bf16[8192,256]{1,0:T(8,128)(2,1)} custom-call(bf16[2,4,32,2048]{3,2,1,0:T(8,128)(2,1)S(1)} %copy-done.12, bf16[2,4,32,2048]{3,2,1,0:T(8,128)(2,1)} %collective-permute-done.1.refs_1_, bf16[2,4,32,2048]{3,2,1,0:T(8,128)(2,1)} %collective-permute-done.3.refs_2_, bf16[2,4,32,2048]{3,2,1,0:T(8,128)(2,1)} %collective-permute-done.5.refs_3_), custom_call_target="tpu_custom_call" | custom-call | tf_op jit(solution)/shard_map/pallas_call | solution.py:56
  146.5 12.6 %shard_map.87 = (f32[512,2048]{1,0:T(8,128)}, f32[512,256]{1,0:T(8,128)S(1)}) custom-call(s32[5]{0:T(128)S(1)} %and_select_fusion.start, s32[5]{0:T(128)S(1)} %and_convert_fusion.valid, bf16[1,512,512]{2,1,0:T(8,128)(2,1)S(1)} %slice_bitcast_fusion.refs_0_, bf16[1,512,512]{2,1,0:T(8,128)(2,1)S(1)} %copy-done.16, ...), custom_call_target="tpu_custom_call" | custom-call | flops 6039797760 | bytes 23855104 | tf_op jit(solution)/shard_map/pallas_call | solution.py:139
  159.1 18.7 %shard_map.88 = (f32[512,2048]{1,0:T(8,128)S(1)}, f32[512,256]{1,0:T(8,128)S(1)}) custom-call(s32[4]{0:T(128)S(1)} %and_select_fusion.8.start, s32[4]{0:T(128)S(1)} %compare_convert_fusion.valid, bf16[4,512,1280]{2,1,0:T(8,128)(2,1)} %bitcast.19, bf16[8192,2048]{1,0:T(8,128)(2,1)} %weight.1, bf16[8192,256]{1,0:T(8,128)(2,1)} %shard_map.86.refs_6_.refs_2_.down, ...), custom_call_target="tpu_custom_call" | custom-call | flops 12079595520 | bytes 38273024 | tf_op jit(solution)/shard_map/pallas_call | solution.py:139
  177.8 2.0 copy-done.5
  179.8 2.2 %copy-done.2 = bf16[8192,256]{1,0:T(8,128)(2,1)S(1)} copy-done((bf16[8192,256]{1,0:T(8,128)(2,1)S(1)}, bf16[8192,256]{1,0:T(8,128)(2,1)}, u32[]{:S(2)}) %copy-start.2) | copy-done | bytes 4194328
  181.9 3.0 %shard_map.91.refs_0_ = bf16[512,32]{1,0:T(8,128)(2,1)S(1)} custom-call(bf16[4,512,256]{2,1,0:T(8,128)(2,1)} %bitcast.20, bf16[8192,256]{1,0:T(8,128)(2,1)S(1)} %copy-done.2, f32[512,256]{1,0:T(8,128)S(1)} %get-tuple-element.39.total, s32[512,1]{1,0:T(8,128)S(1)} %copy.14.slot, s32[512,1]{1,0:T(8,128)S(1)} %copy.13.live), custom_call_target="tpu_custom_call" | custom-call | flops 268435456 | bytes 2097152 | tf_op jit(solution)/shard_map/pallas_call | solution.py:187
  185.0 0.6 collective-permute-start.14
  185.6 1.4 collective-permute-start.16
  187.1 2.2 %copy-done.6 = f32[512,2048]{1,0:T(8,128)S(1)} copy-done((f32[512,2048]{1,0:T(8,128)S(1)}, f32[512,2048]{1,0:T(8,128)}, u32[]{:S(2)}) %copy-start.6) | copy-done | bytes 4194328
  189.2 4.6 %shard_map.90 = (f32[512,2048]{1,0:T(8,128)S(1)}, bf16[1024,2048]{1,0:T(8,128)(2,1)S(1)}) custom-call(bf16[4,512,256]{2,1,0:T(8,128)(2,1)} %bitcast.21, bf16[8192,2048]{1,0:T(8,128)(2,1)} %weight.1, f32[512,2048]{1,0:T(8,128)S(1)} %copy-done.6, bf16[1024,2048]{1,0:T(8,128)(2,1)S(1)} %bitcast.18), custom_call_target="tpu_custom_call" | custom-call | flops 2147483648 | bytes 9437184 | tf_op jit(solution)/shard_map/pallas_call | solution.py:243
  193.8 3.5 %collective-permute-done.15.refs_2_ = bf16[512,32]{1,0:T(8,128)(2,1)S(1)} collective-permute-done((bf16[512,32]{1,0:T(8,128)(2,1)S(1)}, bf16[512,32]{1,0:T(8,128)(2,1)S(1)}, u32[]{:S(2)}, u32[]{:S(2)}) %collective-permute-start.15) | collective-permute-done | bytes 32800 | tf_op jit(solution)/shard_map/ppermute | solution.py:404
  197.4 4.6 %shard_map.92 = bf16[512,2048]{1,0:T(8,128)(2,1)} custom-call(s32[1]{0:T(128)} %bitcast.me, s32[512,1]{1,0:T(8,128)S(1)} %copy.14.slot, f32[512,2048]{1,0:T(8,128)S(1)} %get-tuple-element.45.total, bf16[1024,2048]{1,0:T(8,128)(2,1)S(1)} %get-tuple-element.46.up, bf16[512,32]{1,0:T(8,128)(2,1)S(1)} %shard_map.91.refs_0_, ...), custom_call_target="tpu_custom_call" | custom-call | flops 2147483648 | bytes 2097152 | tf_op jit(solution)/shard_map/pallas_call | solution.py:285
  (74 shorter events, 1.6 us)
Async XLA Ops:
  6.5 13.9 %copy-start = (s32[16]{0:T(128)S(1)}, s32[16]{0:T(128)}, u32[]{:S(2)}) copy-start(s32[16]{0:T(128)} %param.15) | copy-start | bytes 196
  6.5 13.9 %copy-start.18 = (s32[1,6]{1,0:T(1,128)S(1)}, s32[1,6]{1,0:T(1,128)}, u32[]{:S(2)}) copy-start(s32[1,6]{1,0:T(1,128)} %param.13) | copy-start | bytes 76
  6.5 14.6 %copy-start.19 = (s32[16]{0:T(128)S(1)}, s32[16]{0:T(128)}, u32[]{:S(2)}) copy-start(s32[16]{0:T(128)} %param.12) | copy-start | bytes 196
  6.5 15.2 %copy-start.3 = (bf16[4,32,8192]{2,1,0:T(8,128)(2,1)S(1)}, bf16[4,32,8192]{2,1,0:T(8,128)(2,1)}, u32[]{:S(2)}) copy-start(bf16[4,32,8192]{2,1,0:T(8,128)(2,1)} %down.7) | copy-start | bytes 6291460
  6.5 152.5 %all-gather.7.cloned.1.call-start = ((), (), s32[]{:S(2)}) async-start(), calls=%async_computation.1 | async-start | bytes 6553600 | tf_op jit(solution)/shard_map/all_gather | solution.py:363
  9.2 170.5 %all-gather.5.cloned.1.call-start = ((), (), s32[]{:S(2)}) async-start(), calls=%async_computation | async-start | bytes 1310720 | tf_op jit(solution)/shard_map/all_gather | solution.py:363
  9.3 11.8 %collective-permute-start = (s32[1,6]{1,0:T(1,128)}, s32[1,6]{1,0:T(1,128)S(1)}, u32[]{:S(2)}, u32[]{:S(2)}) collective-permute-start(s32[1,6]{1,0:T(1,128)} %param.13), channel_id=1, source_target_pairs={{0,1},{1,0},{2,3},{3,2},{4,5},{5,4},{6,7},{7,6},{8,9},{9,8},{10,11... | collective-permute-start | bytes 80 | tf_op jit(solution)/shard_map/ppermute | solution.py:325
  9.8 11.3 %collective-permute-start.2 = (s32[1,6]{1,0:T(1,128)}, s32[1,6]{1,0:T(1,128)S(1)}, u32[]{:S(2)}, u32[]{:S(2)}) collective-permute-start(s32[1,6]{1,0:T(1,128)} %param.13), channel_id=1, source_target_pairs={{0,2},{1,3},{2,0},{3,1},{4,6},{5,7},{6,4},{7,5},{8,10},{9,11},{10,... | collective-permute-start | bytes 80 | tf_op jit(solution)/shard_map/ppermute | solution.py:325
  12.4 8.8 %collective-permute-start.4 = (s32[1,6]{1,0:T(1,128)}, s32[1,6]{1,0:T(1,128)S(1)}, u32[]{:S(2)}, u32[]{:S(2)}) collective-permute-start(s32[1,6]{1,0:T(1,128)} %param.13), channel_id=1, source_target_pairs={{0,3},{1,2},{2,1},{3,0},{4,7},{5,6},{6,5},{7,4},{8,11},{9,10},{10,... | collective-permute-start | bytes 80 | tf_op jit(solution)/shard_map/ppermute | solution.py:325
  15.2 25.3 %collective-permute-start.6 = (bf16[1,512,512]{2,1,0:T(8,128)(2,1)S(1)}, bf16[1,512,512]{2,1,0:T(8,128)(2,1)S(1)}, u32[]{:S(2)}, u32[]{:S(2)}) collective-permute-start(bf16[1,512,512]{2,1,0:T(8,128)(2,1)S(1)} %slice_bitcast_fusion.refs_0_), channel_id=1, source_target_pairs={{0,4},{4,8},{8,12},{1,5},{5,9},{9,13},{2,6},{6,10},{10,14},{3,7},{... | collective-permute-start | bytes 1572872 | tf_op jit(solution)/shard_map/ppermute | solution.py:372
  18.9 38.5 %collective-permute-start.8 = (bf16[1,512,512]{2,1,0:T(8,128)(2,1)S(1)}, bf16[1,512,512]{2,1,0:T(8,128)(2,1)}, u32[]{:S(2)}, u32[]{:S(2)}) collective-permute-start(bf16[1,512,512]{2,1,0:T(8,128)(2,1)S(1)} %slice_bitcast_fusion.refs_0_), channel_id=1, source_target_pairs={{4,0},{8,4},{12,8},{5,1},{9,5},{13,9},{6,2},{10,6},{14,10},{7,3},{... | collective-permute-start | bytes 1572872 | tf_op jit(solution)/shard_map/ppermute | solution.py:373
  24.4 83.6 %collective-permute-start.3 = (bf16[2,4,32,2048]{3,2,1,0:T(8,128)(2,1)}, bf16[2,4,32,2048]{3,2,1,0:T(8,128)(2,1)}, u32[]{:S(2)}, u32[]{:S(2)}) collective-permute-start(bf16[2,4,32,2048]{3,2,1,0:T(8,128)(2,1)} %get-tuple-element.29), channel_id=1, source_target_pairs={{0,2},{1,3},{2,0},{3,1},{4,6},{5,7},{6,4},{7,5},{8,10},{9,11},{10,... | collective-permute-start | bytes 3145736 | tf_op jit(solution)/shard_map/ppermute | solution.py:381
  25.9 67.1 %collective-permute-start.12 = (bf16[2,128,2048]{2,1,0:T(8,128)(2,1)S(1)}, bf16[2,128,2048]{2,1,0:T(8,128)(2,1)S(1)}, u32[]{:S(2)}, u32[]{:S(2)}) collective-permute-start(bf16[2,128,2048]{2,1,0:T(8,128)(2,1)S(1)} %get-tuple-element.42), channel_id=1, source_target_pairs={{0,2},{1,3},{2,0},{3,1},{4,6},{5,7},{6,4},{7,5},{8,10},{9,11},{10,... | collective-permute-start | bytes 3145736 | tf_op jit(solution)/shard_map/ppermute | solution.py:381
  29.4 65.2 %collective-permute-start.13 = (bf16[2,128,2048]{2,1,0:T(8,128)(2,1)S(1)}, bf16[2,128,2048]{2,1,0:T(8,128)(2,1)S(1)}, u32[]{:S(2)}, u32[]{:S(2)}) collective-permute-start(bf16[2,128,2048]{2,1,0:T(8,128)(2,1)S(1)} %get-tuple-element.43), channel_id=1, source_target_pairs={{0,3},{1,2},{2,1},{3,0},{4,7},{5,6},{6,5},{7,4},{8,11},{9,10},{10,... | collective-permute-start | bytes 3145736 | tf_op jit(solution)/shard_map/ppermute | solution.py:381
  40.5 53.0 %copy-start.15 = (bf16[1,512,512]{2,1,0:T(8,128)(2,1)}, bf16[1,512,512]{2,1,0:T(8,128)(2,1)S(1)}, u32[]{:S(2)}) copy-start(bf16[1,512,512]{2,1,0:T(8,128)(2,1)S(1)} %collective-permute-done.6.refs_1_) | copy-start | bytes 1572868
  40.5 21.6 %collective-permute-start.7 = (bf16[1,512,512]{2,1,0:T(8,128)(2,1)S(1)}, bf16[1,512,512]{2,1,0:T(8,128)(2,1)S(1)}, u32[]{:S(2)}, u32[]{:S(2)}) collective-permute-start(bf16[1,512,512]{2,1,0:T(8,128)(2,1)S(1)} %collective-permute-done.6.refs_1_), channel_id=1, source_target_pairs={{4,8},{8,12},{5,9},{9,13},{6,10},{10,14},{7,11},{11,15},{20,24},{2... | collective-permute-start | bytes 1572872 | tf_op jit(solution)/shard_map/ppermute | solution.py:385
  57.4 35.6 %collective-permute-start.9 = (bf16[1,512,512]{2,1,0:T(8,128)(2,1)}, bf16[1,512,512]{2,1,0:T(8,128)(2,1)S(1)}, u32[]{:S(2)}, u32[]{:S(2)}) collective-permute-start(bf16[1,512,512]{2,1,0:T(8,128)(2,1)} %collective-permute-done.8.refs_2_), channel_id=1, source_target_pairs={{4,0},{8,4},{5,1},{9,5},{6,2},{10,6},{7,3},{11,7},{20,16},{24,20},... | collective-permute-start | bytes 1572872 | tf_op jit(solution)/shard_map/ppermute | solution.py:386
  59.1 41.0 %copy-start.17 = (s32[512]{0:T(512)S(1)}, s32[512]{0:T(512)}, u32[]{:S(2)}) copy-start(s32[512]{0:T(512)} %param.14) | copy-start | bytes 6148
  62.1 54.3 %collective-permute-start.5 = (bf16[2,4,32,2048]{3,2,1,0:T(8,128)(2,1)}, bf16[2,4,32,2048]{3,2,1,0:T(8,128)(2,1)}, u32[]{:S(2)}, u32[]{:S(2)}) collective-permute-start(bf16[2,4,32,2048]{3,2,1,0:T(8,128)(2,1)} %get-tuple-element.30), channel_id=1, source_target_pairs={{0,3},{1,2},{2,1},{3,0},{4,7},{5,6},{6,5},{7,4},{8,11},{9,10},{10,... | collective-permute-start | bytes 3145736 | tf_op jit(solution)/shard_map/ppermute | solution.py:381
  93.0 23.4 %collective-permute-start.1 = (bf16[2,4,32,2048]{3,2,1,0:T(8,128)(2,1)}, bf16[2,4,32,2048]{3,2,1,0:T(8,128)(2,1)}, u32[]{:S(2)}, u32[]{:S(2)}) collective-permute-start(bf16[2,4,32,2048]{3,2,1,0:T(8,128)(2,1)} %get-tuple-element.28), channel_id=1, source_target_pairs={{0,1},{1,0},{2,3},{3,2},{4,5},{5,4},{6,7},{7,6},{8,9},{9,8},{10,11... | collective-permute-start | bytes 3145736 | tf_op jit(solution)/shard_map/ppermute | solution.py:381
  93.0 1.0 copy-start.7
  93.0 7.5 %collective-permute-start.11 = (bf16[2,128,2048]{2,1,0:T(8,128)(2,1)}, bf16[2,128,2048]{2,1,0:T(8,128)(2,1)}, u32[]{:S(2)}, u32[]{:S(2)}) collective-permute-start(bf16[2,128,2048]{2,1,0:T(8,128)(2,1)} %get-tuple-element.41), channel_id=1, source_target_pairs={{0,1},{1,0},{2,3},{3,2},{4,5},{5,4},{6,7},{7,6},{8,9},{9,8},{10,11... | collective-permute-start | bytes 3145736 | tf_op jit(solution)/shard_map/ppermute | solution.py:381
  94.6 5.6 %copy-start.9 = (bf16[2,128,2048]{2,1,0:T(8,128)(2,1)}, bf16[2,128,2048]{2,1,0:T(8,128)(2,1)S(1)}, u32[]{:S(2)}) copy-start(bf16[2,128,2048]{2,1,0:T(8,128)(2,1)S(1)} %collective-permute-done.13.refs_3_) | copy-start | bytes 3145732
  94.6 46.8 %collective-permute-start.10 = (bf16[1,512,512]{2,1,0:T(8,128)(2,1)S(1)}, bf16[1,512,512]{2,1,0:T(8,128)(2,1)}, u32[]{:S(2)}, u32[]{:S(2)}) collective-permute-start(bf16[1,512,512]{2,1,0:T(8,128)(2,1)S(1)} %broadcast_select_fusion.refs_3_), channel_id=1, source_target_pairs={{8,12},{4,0},{9,13},{5,1},{10,14},{6,2},{11,15},{7,3},{24,28},{20,... | collective-permute-start | bytes 1572872 | tf_op jit(solution)/shard_map/ppermute | solution.py:389
  98.1 1.0 copy-start.11
  99.1 1.0 copy-start.13
  100.5 1.2 copy-start.8
  101.7 1.2 copy-start.10
  103.0 1.2 copy-start.14
  104.2 37.2 %copy-start.12 = (bf16[2,4,32,2048]{3,2,1,0:T(8,128)(2,1)S(1)}, bf16[2,4,32,2048]{3,2,1,0:T(8,128)(2,1)}, u32[]{:S(2)}) copy-start(bf16[2,4,32,2048]{3,2,1,0:T(8,128)(2,1)} %copy-done.11) | copy-start | bytes 3145732
  141.4 5.0 %copy-start.16 = (bf16[1,512,512]{2,1,0:T(8,128)(2,1)S(1)}, bf16[1,512,512]{2,1,0:T(8,128)(2,1)}, u32[]{:S(2)}) copy-start(bf16[1,512,512]{2,1,0:T(8,128)(2,1)} %copy-done.15) | copy-start | bytes 1572868
  177.7 2.0 copy-start.5
  179.8 2.2 %copy-start.2 = (bf16[8192,256]{1,0:T(8,128)(2,1)S(1)}, bf16[8192,256]{1,0:T(8,128)(2,1)}, u32[]{:S(2)}) copy-start(bf16[8192,256]{1,0:T(8,128)(2,1)} %shard_map.86.refs_6_.refs_2_.down) | copy-start | bytes 12582916
  181.9 5.1 %copy-start.4 = (bf16[8,128,2048]{2,1,0:T(8,128)(2,1)S(1)}, bf16[8,128,2048]{2,1,0:T(8,128)(2,1)}, u32[]{:S(2)}) copy-start(bf16[8,128,2048]{2,1,0:T(8,128)(2,1)} %shard_map.89) | copy-start | bytes 12582916
  185.0 8.9 %collective-permute-start.14 = (bf16[512,32]{1,0:T(8,128)(2,1)S(1)}, bf16[512,32]{1,0:T(8,128)(2,1)S(1)}, u32[]{:S(2)}, u32[]{:S(2)}) collective-permute-start(bf16[512,32]{1,0:T(8,128)(2,1)S(1)} %shard_map.91.refs_0_), channel_id=1, source_target_pairs={{0,12},{4,0},{8,4},{12,8},{1,13},{5,1},{9,5},{13,9},{2,14},{6,2},{... | collective-permute-start | bytes 98312 | tf_op jit(solution)/shard_map/ppermute | solution.py:404
  185.6 11.8 %collective-permute-start.15 = (bf16[512,32]{1,0:T(8,128)(2,1)S(1)}, bf16[512,32]{1,0:T(8,128)(2,1)S(1)}, u32[]{:S(2)}, u32[]{:S(2)}) collective-permute-start(bf16[512,32]{1,0:T(8,128)(2,1)S(1)} %shard_map.91.refs_0_), channel_id=1, source_target_pairs={{0,8},{4,12},{8,0},{12,4},{1,9},{5,13},{9,1},{13,5},{2,10},{6,14},... | collective-permute-start | bytes 98312 | tf_op jit(solution)/shard_map/ppermute | solution.py:404
  185.6 11.8 %collective-permute-start.16 = (bf16[512,32]{1,0:T(8,128)(2,1)S(1)}, bf16[512,32]{1,0:T(8,128)(2,1)S(1)}, u32[]{:S(2)}, u32[]{:S(2)}) collective-permute-start(bf16[512,32]{1,0:T(8,128)(2,1)S(1)} %shard_map.91.refs_0_), channel_id=1, source_target_pairs={{0,4},{4,8},{8,12},{12,0},{1,5},{5,9},{9,13},{13,1},{2,6},{6,10},{... | collective-permute-start | bytes 98312 | tf_op jit(solution)/shard_map/ppermute | solution.py:404
  187.1 2.2 %copy-start.6 = (f32[512,2048]{1,0:T(8,128)S(1)}, f32[512,2048]{1,0:T(8,128)}, u32[]{:S(2)}) copy-start(f32[512,2048]{1,0:T(8,128)} %copy-done.5) | copy-start | bytes 12582916
  197.4 4.6 %copy-start.1 = (s32[16]{0:T(128)S(1)}, s32[16]{0:T(128)}, u32[]{:S(2)}) copy-start(s32[16]{0:T(128)} %param.15) | copy-start | bytes 196
Sparse Core Ops, SparseCore 0:
  9.3 123.7 all-gather.6
  134.7 26.9 all-gather.4

commit v8 on v7

--- a/solution.py
+++ b/solution.py
@@ -8,9 +8,7 @@
 from jax.sharding import PartitionSpec as P
 
 CAP = 2
-ALIGN = 256
-LINE = 512
-GATHERED = (1280, 256)
+HALF = 1024
 PARAMS = pltpu.CompilerParams(vmem_limit_bytes=48 * 2**20)
 TAIL_PARAMS = pltpu.CompilerParams(vmem_limit_bytes=24 * 2**20)
 F32 = jnp.float32
@@ -88,88 +86,113 @@
 IN_HBM = pl.BlockSpec(memory_space=pltpu.HBM)
 
 
-def chunk_kernel(counts, held, start, valid, *refs):
+def chunk_kernel(count, halves, held, with_base, with_low, start, valid, *refs):
     refs = list(refs)
-    xs = [refs.pop(0) for _ in counts]
-    weight, down = refs.pop(0), refs.pop(0)
-    totals, (base, low) = refs[:-2], refs[-2:]
+    xs = [refs.pop(0) for _ in range(count)]
+    weight = refs.pop(0) if with_base else None
+    down = refs.pop(0) if with_low else None
+    outs = [refs.pop() for _ in range(with_base + with_low)][::-1]
     step = pl.program_id(0)
 
     @pl.when(step == 0)
     def _():
-        base[...] = totals[0][...] if held else jnp.zeros_like(base)
-        low[...] = totals[1][...] if held else jnp.zeros_like(low)
-
-    first = 0
-    for x, count in zip(xs, counts):
-
-        @pl.when((step >= first) & (step < first + count) & (valid[step] != 0))
+        for i, out in enumerate(outs):
+            out[...] = refs[i][...] if held else jnp.zeros_like(out)
+
+    for i, x in enumerate(xs):
+
+        @pl.when((step >= i * halves) & (step < (i + 1) * halves) & (valid[step] != 0))
         def _():
-            part = min(base.shape[1], 512)
-            for n in range(0, base.shape[1], part):
-                base[:, n:n + part] += jnp.dot(x[0], weight[:, n:n + part], preferred_element_type=F32)
-            low[...] += jnp.dot(x[0], down[...], preferred_element_type=F32)
-
-        first += count
-
-
-def add_chunk(totals, xs, source, first, weight, down):
-    rows, features = xs[0].shape[1:]
-    columns, slots = weight.shape[1], down.shape[1]
-    counts = [x.shape[0] for x in xs]
-    steps = sum(counts)
-    n_tensor = lax.axis_size("tensor")
-    valid = ((source >= 0) & (source < n_tensor)).astype(jnp.int32)
-    start = (jnp.clip(source, 0, n_tensor - 1) * (weight.shape[0] // n_tensor) + first) // ALIGN
-    start = start.astype(jnp.int32)
-    x_specs, begin = [], 0
-    for count in counts:
-        x_specs.append(
-            pl.BlockSpec(
-                (1, rows, features),
-                lambda s, *_, begin=begin, count=count: (jnp.clip(s - begin, 0, count - 1), 0, 0),
-            )
-        )
-        begin += count
-    walked = [
-        pl.BlockSpec((pl.Element(features), pl.Element(a)), lambda s, start, valid: (start[s] * ALIGN, 0))
-        for a in (columns, slots)
-    ]
-    whole = [pl.BlockSpec((rows, a), lambda s, *_: (0, 0)) for a in (columns, slots)]
-    return pl.pallas_call(
-        functools.partial(chunk_kernel, counts, bool(totals)),
-        out_shape=[jax.ShapeDtypeStruct((rows, a), F32) for a in (columns, slots)],
+            if with_base:
+                base = outs[0]
+                part = min(base.shape[1], 512)
+                for n in range(0, base.shape[1], part):
+                    base[:, n:n + part] += jnp.dot(x[...], weight[:, n:n + part], preferred_element_type=F32)
+            if with_low:
+                outs[-1][...] += jnp.dot(x[...], down[...], preferred_element_type=F32)
+
+
+def add_chunk(totals, xs, source, weight, down):
+    rows, width = xs[0].shape
+    walked = [a for a in (weight, down) if a is not None]
+    n_tensor = walked[0].shape[0] // width
+    halves = width // HALF
+    steps = len(xs) * halves
+    valid = jnp.repeat(((source >= 0) & (source < n_tensor)).astype(jnp.int32), halves)
+    start = jnp.clip(source, 0, n_tensor - 1)[:, None] * halves + jnp.arange(halves)[None, :]
+    start = start.reshape(-1).astype(jnp.int32)
+    whole = [pl.BlockSpec((rows, a.shape[1]), lambda s, *_: (0, 0)) for a in walked]
+    columns = sum(a.shape[1] for a in walked)
+    return pl.pallas_call(
+        functools.partial(chunk_kernel, len(xs), halves, bool(totals), weight is not None, down is not None),
+        out_shape=[jax.ShapeDtypeStruct((rows, a.shape[1]), F32) for a in walked],
         grid_spec=pltpu.PrefetchScalarGridSpec(
             num_scalar_prefetch=2,
             grid=(steps,),
-            in_specs=x_specs + walked + (whole if totals else []),
+            in_specs=[
+                pl.BlockSpec((rows, HALF), lambda s, *_, i=i: (0, jnp.clip(s - i * halves, 0, halves - 1)))
+                for i in range(len(xs))
+            ]
+            + [pl.BlockSpec((HALF, a.shape[1]), lambda s, start, valid: (start[s], 0)) for a in walked]
+            + (whole if totals else []),
             out_specs=whole,
         ),
         compiler_params=PARAMS,
         cost_estimate=pl.CostEstimate(
-            flops=2 * steps * features * rows * (columns + slots),
-            bytes_accessed=2 * steps * features * (rows + columns + slots) + 8 * rows * (columns + slots),
+            flops=2 * len(xs) * width * rows * columns,
+            bytes_accessed=2 * len(xs) * width * (rows + columns) + 8 * rows * columns,
             transcendentals=0,
         ),
-    )(start, valid, *xs, weight, down, *totals)
-
-
-def low_kernel(first, x_hbm, down, total, slot, live, out, x, rows_of, sems):
-    shards, _, features = x.shape
-    width = down.shape[0] // shards
-    rank_part = out.shape[1]
-    copies = [
-        pltpu.make_async_copy(down.at[pl.ds(t * width + first, features)], rows_of.at[t], sems.at[t])
-        for t in range(shards)
+    )(start, valid, *xs, *walked, *totals)
+
+
+def pin_kernel(source, weight, down, base, low, up, weight_out, down_out, base_out, low_out, up_out, sems):
+    width = weight_out.shape[0]
+    rows = pl.ds(pl.multiple_of(source[0] * width, width), width)
+    pairs = [
+        (weight.at[rows], weight_out), (down.at[rows], down_out), (base, base_out), (low, low_out), (up, up_out)
     ]
-    copies += [pltpu.make_async_copy(x_hbm.at[t], x.at[t], sems.at[shards + t]) for t in range(shards)]
+    copies = [pltpu.make_async_copy(a, b, sems.at[i]) for i, (a, b) in enumerate(pairs)]
     for copy in copies:
         copy.start()
-    low = total[...]
-    for t in range(shards):
-        copies[t].wait()
-        copies[shards + t].wait()
-        low += jnp.dot(x[t], rows_of[t], preferred_element_type=F32)
+    for copy in copies:
+        copy.wait()
+
+
+def pin(source, width, weight, down, base, low, up):
+    shapes = [((width,) + a.shape[1:], a.dtype) for a in (weight, down)]
+    shapes += [(a.shape, a.dtype) for a in (base, low, up)]
+    return pl.pallas_call(
+        pin_kernel,
+        out_shape=[pltpu.VMEM(*a) for a in shapes],
+        in_specs=[pl.BlockSpec(memory_space=pltpu.SMEM)] + [IN_HBM] * 5,
+        out_specs=[RESIDENT] * 5,
+        scratch_shapes=[pltpu.SemaphoreType.DMA((5,))],
+        compiler_params=TAIL_PARAMS,
+        cost_estimate=pl.CostEstimate(
+            flops=0, bytes_accessed=sum(a[0] * a[1] for a, _ in shapes) * 3, transcendentals=0
+        ),
+    )(source, weight, down, base, low, up)
+
+
+def low_kernel(rank_part, which, from_left, from_right, down, total, slot, live, out, x, sem):
+    @pl.when(which[0] > 0)
+    def _():
+        pltpu.make_async_copy(from_left, x, sem).start()
+
+    @pl.when(which[0] < 0)
+    def _():
+        pltpu.make_async_copy(from_right, x, sem).start()
+
+    @pl.when(which[0] != 0)
+    def _():
+        pltpu.make_async_copy(from_left, x, sem).wait()
+
+    @pl.when(which[0] == 0)
+    def _():
+        x[...] = jnp.zeros_like(x)
+
+    low = total[...] + jnp.dot(x[...], down[...], preferred_element_type=F32)
     lane = lax.broadcasted_iota(jnp.int32, low.shape, 1)
     own = jnp.where(lane // rank_part == slot[...], low, 0.0).astype(BF16)
     fold = (
@@ -181,84 +204,44 @@
     out[...] = jnp.where(k < live[...], mine, 0.0).astype(BF16)
 
 
-def finish_low(total, x, first, down, slot, live, rank_part):
-    shards, rows, features = x.shape
+def finish_low(which, from_left, from_right, down, total, slot, live, rank_part):
+    rows, width = from_left.shape
     slots = down.shape[1]
     return pl.pallas_call(
-        functools.partial(low_kernel, first),
-        out_shape=jax.ShapeDtypeStruct((rows, rank_part), BF16),
-        in_specs=[IN_HBM, IN_HBM, RESIDENT, RESIDENT, RESIDENT],
-        out_specs=RESIDENT,
-        scratch_shapes=[
-            pltpu.VMEM(x.shape, BF16),
-            pltpu.VMEM((shards, features, slots), BF16),
-            pltpu.SemaphoreType.DMA((2 * shards,)),
-        ],
+        functools.partial(low_kernel, rank_part),
+        out_shape=[pltpu.VMEM((rows, rank_part), BF16), pltpu.VMEM((rows, width), BF16)],
+        in_specs=[pl.BlockSpec(memory_space=pltpu.SMEM), IN_HBM, IN_HBM] + [RESIDENT] * 4,
+        out_specs=[RESIDENT] * 2,
+        scratch_shapes=[pltpu.SemaphoreType.DMA],
         compiler_params=TAIL_PARAMS,
         cost_estimate=pl.CostEstimate(
-            flops=2 * shards * features * rows * slots,
-            bytes_accessed=2 * shards * features * (rows + slots) + 4 * rows * slots,
-            transcendentals=0,
-        ),
-    )(x, down, total, slot, live)
-
-
-def base_kernel(first, x, weight, total, up, out, up_out, xs, ws, ts, sems, up_sem):
-    shards, rows, features = x.shape
-    columns = out.shape[1]
-    parts, _, _, part = ws.shape
-    width = weight.shape[0] // shards
-    for t in range(shards):
-        pltpu.make_async_copy(x.at[t], xs.at[t], sems.at[parts, t]).start()
-
-    def copies(n):
-        cut = pl.ds(n * part, part)
-        return [
-            pltpu.make_async_copy(
-                weight.at[pl.ds(t * width + first, features), cut], ws.at[n, t], sems.at[n, t]
+            flops=2 * width * rows * slots, bytes_accessed=2 * width * rows, transcendentals=0
+        ),
+    )(which, from_left, from_right, down, total, slot, live)
+
+
+def base_kernel(which, x, weight, total, out):
+    @pl.when(which[0] != 0)
+    def _():
+        part = min(out.shape[1], 512)
+        for n in range(0, out.shape[1], part):
+            out[:, n:n + part] = total[:, n:n + part] + jnp.dot(
+                x[...], weight[:, n:n + part], preferred_element_type=F32
             )
-            for t in range(shards)
-        ] + [pltpu.make_async_copy(total.at[:, cut], ts.at[n], sems.at[n, shards])]
-
-    for n in range(parts):
-        for copy in copies(n):
-            copy.start()
-    pltpu.make_async_copy(up, up_out, up_sem).start()
-    for t in range(shards):
-        pltpu.make_async_copy(x.at[t], xs.at[t], sems.at[parts, t]).wait()
-    joined = jnp.concatenate([xs[t] for t in range(shards)], axis=1)
-    for n in range(parts):
-        for copy in copies(n):
-            copy.wait()
-        w = ws[n].reshape(shards * features, part)
-        out[:, n * part:(n + 1) * part] = ts[n] + jnp.dot(joined, w, preferred_element_type=F32)
-    pltpu.make_async_copy(up, up_out, up_sem).wait()
-
-
-def add_last(total, x, first, weight, up):
-    shards, rows, features = x.shape
+
+
+def add_last(which, x, weight, total):
+    rows, width = x.shape
     columns = weight.shape[1]
-    part = min(columns, 512)
-    parts = columns // part
-    return pl.pallas_call(
-        functools.partial(base_kernel, first),
-        out_shape=[pltpu.VMEM((rows, columns), F32), pltpu.VMEM(up.shape, BF16)],
-        in_specs=[IN_HBM] * 4,
-        out_specs=[RESIDENT] * 2,
-        scratch_shapes=[
-            pltpu.VMEM((shards, rows, features), BF16),
-            pltpu.VMEM((parts, shards, features, part), BF16),
-            pltpu.VMEM((parts, rows, part), F32),
-            pltpu.SemaphoreType.DMA((parts + 1, shards + 1)),
-            pltpu.SemaphoreType.DMA,
-        ],
+    return pl.pallas_call(
+        base_kernel,
+        out_shape=pltpu.VMEM((rows, columns), F32),
+        in_specs=[pl.BlockSpec(memory_space=pltpu.SMEM)] + [RESIDENT] * 3,
+        out_specs=RESIDENT,
+        input_output_aliases={3: 0},
         compiler_params=TAIL_PARAMS,
-        cost_estimate=pl.CostEstimate(
-            flops=2 * shards * features * rows * columns,
-            bytes_accessed=2 * shards * features * (rows + columns) + 4 * rows * columns,
-            transcendentals=0,
-        ),
-    )(x, weight, total, up)
+        cost_estimate=pl.CostEstimate(flops=2 * width * rows * columns, bytes_accessed=0, transcendentals=0),
+    )(which, x, weight, total)
 
 
 def finish_kernel(parts, me, slot, total, up, *refs):
@@ -351,26 +334,17 @@
     entries = own_list.shape[0]
     one_hot = row_request_entry[:, None] == jnp.arange(entries)[None, :]
     row_rank = jnp.sum(jnp.where(one_hot, ranks[own_list][None, :], 0), axis=1)
-    if n_tensor != 4 or width != LINE + sum(GATHERED) or rank_part % 16:
+    if n_tensor != 4 or width % HALF or rank_part % 16:
         return plain(
             attention_result, output_weight, adapter_down_weight, adapter_up_weight, adapter_page_row,
             own_list, one_hot, row_rank,
         )
 
-    gathered, x, first = [], attention_result, 0
-    for features in GATHERED:
-        piece = x[:, first:first + features]
-        gathered.append(lax.all_gather(piece, "tensor", axis=0))
-        x = after(x, piece)
-        first += features + LINE
-
-    middle = GATHERED[0]
-    last = middle + LINE
-    line = x[None, :, middle:last]
     right = [(i, i + 1) for i in range(n_tensor - 1)]
     left = [(i + 1, i) for i in range(n_tensor - 1)]
-    right_1 = lax.ppermute(line, "tensor", right)
-    left_1 = lax.ppermute(line, "tensor", left)
+    own = attention_result
+    right_1 = lax.ppermute(own, "tensor", right)
+    left_1 = lax.ppermute(own, "tensor", left)
 
     slots, places = asked_pages(requests, adapter_page_row, holder_length)
     downs, ups = [], []
@@ -378,28 +352,34 @@
         down, up = pick_pages(places[j], adapter_down_weight, adapter_up_weight, n_tensor)
         if j:
             pairs = [(i, i ^ j) for i in range(n_dp)]
-            down, up = lax.ppermute(down, "dp", pairs), lax.ppermute(up, "dp", pairs)
+            down = lax.ppermute(down, "dp", pairs)
+            up = lax.ppermute(after(up, right_1, left_1), "dp", pairs)
         downs.append(down)
         ups.append(up)
 
     right_2 = lax.ppermute(right_1, "tensor", right[1:])
     left_2 = lax.ppermute(left_1, "tensor", left[:-1])
-    upper = me >= n_tensor // 2
-    second = jnp.where(upper, right_2, left_2)
-    third = lax.ppermute(second, "tensor", right[-1:] + left[:1])
-    down = join_downs(after(tuple(downs), third))
-    up = join_ups(ups)
-
+    near = me + jnp.array([0, -1, 1], jnp.int32)
+    base, = add_chunk((), [own, right_1, left_1], near, output_weight, None)
+    base, right_2, left_2 = lax.optimization_barrier((base, right_2, left_2))
+    right_3 = lax.ppermute(right_2, "tensor", right[2:])
+    left_3 = lax.ppermute(left_2, "tensor", left[:-2])
+
+    down = join_downs(after(tuple(downs), base))
+    low, = add_chunk((), [own, right_1, left_1], near, None, down)
+    far = me + jnp.array([-2, 2], jnp.int32)
+    base, low = add_chunk((base, low), [right_2, left_2], far, output_weight, down)
+    up = join_ups(after(tuple(ups), base))
+    which = jnp.where(me == n_tensor - 1, 1, jnp.where(me == 0, -1, 0)).astype(jnp.int32)
+    source = jnp.where(me == 0, n_tensor - 1, 0).astype(jnp.int32)
     slot = jnp.sum(jnp.where(one_hot, slots[None, :], 0), axis=1)[:, None]
     live = row_rank[:, None] - me * rank_part
-    toward = jnp.where(upper, -1, 1)
-    source = me + jnp.stack([jnp.zeros_like(me), -jnp.ones_like(me), jnp.ones_like(me), 2 * toward, 3 * toward])
-    blocks = [line, right_1, left_1, second, third]
-    totals = add_chunk((), blocks, source, middle, output_weight, down)
-    totals = add_chunk(totals, gathered[:1], jnp.arange(n_tensor), 0, output_weight, down)
-    x = pltpu.with_memory_space_constraint(after(gathered[1], *totals, up), pltpu.HBM)
-    low = finish_low(totals[1], x, last, down, slot, live, rank_part)
-    base, up = add_last(totals[0], x, last, output_weight, up)
+    rest = (which[None], slot, live)
+    pinned = pin(after(source[None], rest), width, output_weight, down, base, low, up)
+    weight, down, base, low, up, right_3, left_3 = lax.optimization_barrier((*pinned, right_3, left_3))
+    which, slot, live = rest
+    low, x = finish_low(which, right_3, left_3, down, low, slot, live, rank_part)
+    base = add_last(which, x, weight, base)
     lows = [low] + [
         lax.ppermute(low, "tensor", [(i, (i - j) % n_tensor) for i in range(n_tensor)])
         for j in range(1, n_tensor)

time: 210 us -> 200 us (0.952)
  waiting for transfers between devices: 95.2 us -> 69.9 us
  between operations: 13.7 us -> 0.28 us
  Pallas kernels: 62.7 us -> 74.8 us
  starting transfers between devices: 16.9 us -> 25.5 us
  local copies, waits for them, and re-layouts: 18.7 us -> 23.9 us
  other arithmetic: 1.66 us -> 5.03 us
    ppermute x9 -> x10, waiting for transfers between devices: 60.7 us -> 46.1 us  [the longest x1 28.9 us: local(): right_1 = lax.ppermute(own, 'tensor', right)]
    pallas_call x4 -> x6, Pallas kernels: 38.9 us -> 53 us  [the longest x3 40.9 us: add_chunk(): pl.pallas_call(functools.partial(chunk_kernel, len(xs), halves, bool(tota...]
    ppermute x1, waiting for transfers between devices: 30.9 us -> 19.6 us  [local(): left_2 = lax.ppermute(left_1, 'tensor', left[:-1])]
    unnamed x40 -> x50, local copies, waits for them, and re-layouts: 12.3 us -> 22.5 us
    ppermute x9 -> x10, starting transfers between devices: 9.65 us -> 16.5 us  [the longest x1 6.42 us: local(): right_1 = lax.ppermute(own, 'tensor', right)]
    slice x2 -> x0, local copies, waits for them, and re-layouts: 4.3 us -> none  [local(): piece = x[:, first:first + features]]
  transfers between devices with their start and end apart: 19 -> 18, of which waited for: 7 -> 5; matrix products, arithmetic and copies ran while one was open for 3% -> 3% of each run, Pallas kernels for 26% -> 34%
where the time goes in v8:
time: 200 us; the launch traced here: 199 us
  Pallas kernels  74.8 us (37%)
  waiting for transfers between devices  69.9 us (35%)
  starting transfers between devices  25.5 us (13%)
  local copies, waits for them, and re-layouts  23.9 us (12%)
  other arithmetic  5.03 us (3%)
    pallas_call x3, Pallas kernels, add_chunk(): pl.pallas_call(functools.partial(chunk_kernel, len(xs), halves, bool(tota...  40.9 us
    ppermute x1, waiting for transfers between devices, local(): right_1 = lax.ppermute(own, 'tensor', right)  28.9 us
    unnamed x50, local copies, waits for them, and re-layouts  22.5 us
    ppermute x1, waiting for transfers between devices, local(): left_2 = lax.ppermute(left_1, 'tensor', left[:-1])  19.6 us
    ppermute x3, waiting for transfers between devices, local(): up = lax.ppermute(after(up, right_1, left_1), 'dp', pairs)  13.7 us
    pallas_call x4, Pallas kernels, pick_pages(): pl.pallas_call(pick_kernel, out_shape=[jax.ShapeDtypeStruct((count,) + sh...  9.87 us
    ppermute x1, starting transfers between devices, local(): right_1 = lax.ppermute(own, 'tensor', right)  6.42 us
    pallas_call x1, Pallas kernels, join_downs(): pl.pallas_call(join_downs_kernel, out_shape=jax.ShapeDtypeStruct((shards...  4.9 us
  transfers between devices with their start and end apart: 18, of which 5 were waited for; matrix products, arithmetic and copies ran while one was open for 3% of the time, Pallas kernels for 34%

profile of v8, /device:TPU:0, one launch (start us, length us, event | category | flops | bytes accessed | tf_op | source)
XLA Modules:
  0.0 199.4 jit_solution(11280655309101214193)
XLA Ops:
  0.0 6.4 %collective-permute-start.6 = (bf16[512,2048]{1,0:T(8,128)(2,1)}, bf16[512,2048]{1,0:T(8,128)(2,1)}, u32[]{:S(2)}, u32[]{:S(2)}) collective-permute-start(bf16[512,2048]{1,0:T(8,128)(2,1)} %refs_0_.3), channel_id=1, source_target_pairs={{0,4},{4,8},{8,12},{1,5},{5,9},{9,13},{2,6},{6,10},{10,14},{3,7},{... | collective-permute-start | bytes 6291464 | tf_op jit(solution)/shard_map/ppermute | solution.py:346
  6.4 1.3 collective-permute-start.7
  7.7 0.7 collective-permute-start.4
  8.4 1.0 collective-permute-start
  11.6 0.7 fusion.9
  13.2 0.9 select_reduce_fusion.2
  14.4 1.6 copy-done.3
  16.0 2.6 %shard_map.102 = (bf16[2,4,32,2048]{3,2,1,0:T(8,128)(2,1)}, bf16[2,128,2048]{2,1,0:T(8,128)(2,1)S(1)}) custom-call(s32[2]{0:T(128)S(1)} %fusion.6.places, bf16[4,32,8192]{2,1,0:T(8,128)(2,1)S(1)} %copy-done.3, bf16[4,128,2048]{2,1,0:T(8,128)(2,1)} %up.7), custom_call_target="tpu_custom_call" | custom-call | tf_op jit(solution)/shard_map/pallas_call | solution.py:29
  18.7 1.0 copy-done.20
  19.6 1.5 collective-permute-start.3
  21.3 28.9 %collective-permute-done.6.refs_1_ = bf16[512,2048]{1,0:T(8,128)(2,1)} collective-permute-done((bf16[512,2048]{1,0:T(8,128)(2,1)}, bf16[512,2048]{1,0:T(8,128)(2,1)}, u32[]{:S(2)}, u32[]{:S(2)}) %collective-permute-start.6) | collective-permute-done | bytes 2097184 | tf_op jit(solution)/shard_map/ppermute | solution.py:346
  50.2 2.0 collective-permute-start.8
  52.2 3.5 %collective-permute-done.7.refs_2_ = bf16[512,2048]{1,0:T(8,128)(2,1)} collective-permute-done((bf16[512,2048]{1,0:T(8,128)(2,1)}, bf16[512,2048]{1,0:T(8,128)(2,1)}, u32[]{:S(2)}, u32[]{:S(2)}) %collective-permute-start.7) | collective-permute-done | bytes 2097184 | tf_op jit(solution)/shard_map/ppermute | solution.py:347
  55.7 1.3 collective-permute-start.9
  57.1 2.7 %shard_map.103 = (bf16[2,4,32,2048]{3,2,1,0:T(8,128)(2,1)}, bf16[2,128,2048]{2,1,0:T(8,128)(2,1)S(1)}) custom-call(s32[2]{0:T(128)S(1)} %fusion.7.places, bf16[4,32,8192]{2,1,0:T(8,128)(2,1)S(1)} %copy-done.3, bf16[4,128,2048]{2,1,0:T(8,128)(2,1)} %up.7), custom_call_target="tpu_custom_call" | custom-call | tf_op jit(solution)/shard_map/pallas_call | solution.py:29
  59.8 1.0 copy-done.21
  61.1 2.7 %shard_map.101 = (bf16[2,4,32,2048]{3,2,1,0:T(8,128)(2,1)}, bf16[2,128,2048]{2,1,0:T(8,128)(2,1)S(1)}) custom-call(s32[2]{0:T(128)S(1)} %fusion.5.places, bf16[4,32,8192]{2,1,0:T(8,128)(2,1)S(1)} %copy-done.3, bf16[4,128,2048]{2,1,0:T(8,128)(2,1)} %up.7), custom_call_target="tpu_custom_call" | custom-call | tf_op jit(solution)/shard_map/pallas_call | solution.py:29
  63.9 1.7 collective-permute-start.1
  65.5 19.1 %shard_map.104.refs_4_ = f32[512,2048]{1,0:T(8,128)} custom-call(s32[6]{0:T(128)S(1)} %add.166.start, s32[6]{0:T(128)S(1)} %reshape.287.valid, bf16[512,2048]{1,0:T(8,128)(2,1)S(1)} %copy-done.8, bf16[512,2048]{1,0:T(8,128)(2,1)} %collective-permute-done.6.refs_1_, bf16[512,2048]{1,0:T(8,128)(2,1)} %collective-permute-done.7.refs_2_, bf16[8192,2048]{1,0:T(8,128)(2,1)} %weight.1), custom_call_target="tpu_custom_call" | custom-call | flops 12884901888 | bytes 39845888 | tf_op jit(solution)/shard_map/pallas_call | solution.py:126
  84.6 19.6 %collective-permute-done.9.refs_1_ = bf16[512,2048]{1,0:T(8,128)(2,1)} collective-permute-done((bf16[512,2048]{1,0:T(8,128)(2,1)}, bf16[512,2048]{1,0:T(8,128)(2,1)}, u32[]{:S(2)}, u32[]{:S(2)}) %collective-permute-start.9) | collective-permute-done | bytes 2097184 | tf_op jit(solution)/shard_map/ppermute | solution.py:361
  104.2 2.0 collective-permute-start.13
  106.2 1.5 collective-permute-start.14
  108.7 1.8 shard_map.100
  110.6 1.0 copy-done.10
  111.6 1.0 copy-done.12
  113.0 1.6 collective-permute-start.11
  115.2 1.2 copy-done.13
  116.4 4.9 %shard_map.105.refs_3_.down = bf16[8192,256]{1,0:T(8,128)(2,1)} custom-call(bf16[2,4,32,2048]{3,2,1,0:T(8,128)(2,1)S(1)} %copy-done.13, bf16[2,4,32,2048]{3,2,1,0:T(8,128)(2,1)} %collective-permute-done.1.refs_1_, bf16[2,4,32,2048]{3,2,1,0:T(8,128)(2,1)S(1)} %collective-permute-done.3.refs_2_, bf16[2,4,32,2048]{3,2,1,0:T(8,128)(2,1)} %collective-permute-done.5.refs_3_), custom_call_target="tpu_custom_call" | custom-call | tf_op jit(solution)/shard_map/pallas_call | solution.py:54
  121.3 6.6 %shard_map.106.refs_5_ = f32[512,256]{1,0:T(8,128)S(1)} custom-call(s32[6]{0:T(128)S(1)} %add.166.start, s32[6]{0:T(128)S(1)} %reshape.287.valid, bf16[512,2048]{1,0:T(8,128)(2,1)S(1)} %copy-done.9, bf16[512,2048]{1,0:T(8,128)(2,1)} %collective-permute-done.6.refs_1_, bf16[512,2048]{1,0:T(8,128)(2,1)} %collective-permute-done.7.refs_2_, ...), custom_call_target="tpu_custom_call" | custom-call | flops 1610612736 | bytes 10485760 | tf_op jit(solution)/shard_map/pallas_call | solution.py:126
  128.0 15.1 %shard_map.107 = (f32[512,2048]{1,0:T(8,128)}, f32[512,256]{1,0:T(8,128)S(1)}) custom-call(s32[4]{0:T(128)S(1)} %add.172.start, s32[4]{0:T(128)S(1)} %reshape.288.valid, bf16[512,2048]{1,0:T(8,128)(2,1)} %collective-permute-done.8.refs_0_, bf16[512,2048]{1,0:T(8,128)(2,1)} %collective-permute-done.9.refs_1_, bf16[8192,2048]{1,0:T(8,128)(2,1)} %weight.1, ...), custom_call_target="tpu_custom_call" | custom-call | flops 9663676416 | bytes 32505856 | tf_op jit(solution)/shard_map/pallas_call | solution.py:126
  143.1 1.0 copy-done.14
  144.1 13.7 %collective-permute-done.12.refs_3_ = bf16[2,128,2048]{2,1,0:T(8,128)(2,1)S(1)} collective-permute-done((bf16[2,128,2048]{2,1,0:T(8,128)(2,1)}, bf16[2,128,2048]{2,1,0:T(8,128)(2,1)S(1)}, u32[]{:S(2)}, u32[]{:S(2)}) %collective-permute-start.12) | collective-permute-done | bytes 1048608 | tf_op jit(solution)/shard_map/ppermute | solution.py:356
  157.7 1.0 copy-done.16
  158.7 1.0 copy-done.18
  159.7 1.2 copy-done.15
  160.9 1.2 copy-done.17
  162.2 1.2 copy-done.19
  163.4 2.5 %shard_map.108 = bf16[8,128,2048]{2,1,0:T(8,128)(2,1)} custom-call(bf16[2,128,2048]{2,1,0:T(8,128)(2,1)S(1)} %copy-done.11, bf16[2,128,2048]{2,1,0:T(8,128)(2,1)S(1)} %copy-done.19, bf16[2,128,2048]{2,1,0:T(8,128)(2,1)S(1)} %copy-done.15, bf16[2,128,2048]{2,1,0:T(8,128)(2,1)S(1)} %copy-done.17), custom_call_target="tpu_custom_call" | custom-call | tf_op jit(solution)/shard_map/pallas_call | solution.py:75
  165.9 1.2 copy-done.2
  167.1 1.3 copy-done.7
  168.4 4.7 %shard_map.109 = (bf16[2048,2048]{1,0:T(8,128)(2,1)S(1)}, bf16[2048,256]{1,0:T(8,128)(2,1)S(1)}, f32[512,2048]{1,0:T(8,128)S(1)}, f32[512,256]{1,0:T(8,128)S(1)}, bf16[1024,2048]{1,0:T(8,128)(2,1)S(1)}) custom-call(s32[1]{0:T(128)} %bitcast.4.source, bf16[8192,2048]{1,0:T(8,128)(2,1)} %weight.1, bf16[8192,256]{1,0:T(8,128)(2,1)S(1)} %copy-done.2, ...), custom_call_target="tpu_custom_call" | custom-call | bytes 23986176 | tf_op jit(solution)/shard_map/pallas_call | solution.py:165
  173.1 3.2 %copy-done.5 = bf16[2048,2048]{1,0:T(8,128)(2,1)} copy-done((bf16[2048,2048]{1,0:T(8,128)(2,1)}, bf16[2048,2048]{1,0:T(8,128)(2,1)S(1)}, u32[]{:S(2)}) %copy-start.5) | copy-done | bytes 8388632
  176.3 2.5 %shard_map.110 = (bf16[512,32]{1,0:T(8,128)(2,1)S(1)}, bf16[512,2048]{1,0:T(8,128)(2,1)S(1)}) custom-call(s32[1]{0:T(128)} %bitcast.3.which, bf16[512,2048]{1,0:T(8,128)(2,1)} %collective-permute-done.13.from_left, bf16[512,2048]{1,0:T(8,128)(2,1)} %collective-permute-done.14.from_right, bf16[2048,256]{1,0:T(8,128)(2,1)S(1)} %get-tuple-element.76.down, ...), custom_call_target="tpu_custom_call" | custom-call | flops 536870912 | bytes 2097152 | tf_op jit(solution)/shard_map/pallas_call | solution.py:210
  178.9 3.5 %collective-permute-start.16 = (bf16[512,32]{1,0:T(8,128)(2,1)S(1)}, bf16[512,32]{1,0:T(8,128)(2,1)S(1)}, u32[]{:S(2)}, u32[]{:S(2)}) collective-permute-start(bf16[512,32]{1,0:T(8,128)(2,1)S(1)} %get-tuple-element.82.refs_0_), channel_id=1, source_target_pairs={{0,8},{4,12},{8,0},{12,4},{1,9},{5,13},{9,1},{13,5},{2,10},{6,14},... | collective-permute-start | bytes 98312 | tf_op jit(solution)/shard_map/ppermute | solution.py:384
  182.4 3.4 %copy-done.6 = bf16[2048,2048]{1,0:T(8,128)(2,1)S(1)} copy-done((bf16[2048,2048]{1,0:T(8,128)(2,1)S(1)}, bf16[2048,2048]{1,0:T(8,128)(2,1)}, u32[]{:S(2)}) %copy-start.6) | copy-done | bytes 8388632
  185.8 4.9 %shard_map.111.total = f32[512,2048]{1,0:T(8,128)S(1)} custom-call(s32[1]{0:T(128)} %bitcast.3.which, bf16[512,2048]{1,0:T(8,128)(2,1)S(1)} %get-tuple-element.78.x, bf16[2048,2048]{1,0:T(8,128)(2,1)S(1)} %copy-done.6, f32[512,2048]{1,0:T(8,128)S(1)} %get-tuple-element.80.total), custom_call_target="tpu_custom_call", output_to_operand_aliasing={{}: (3, {})} | custom-call | flops 4294967296 | tf_op jit(solution)/shard_map/pallas_call | solution.py:236
  190.7 4.1 %collective-permute-done.16.refs_2_ = bf16[512,32]{1,0:T(8,128)(2,1)S(1)} collective-permute-done((bf16[512,32]{1,0:T(8,128)(2,1)S(1)}, bf16[512,32]{1,0:T(8,128)(2,1)S(1)}, u32[]{:S(2)}, u32[]{:S(2)}) %collective-permute-start.16) | collective-permute-done | bytes 32800 | tf_op jit(solution)/shard_map/ppermute | solution.py:384
  194.8 4.6 %shard_map.112 = bf16[512,2048]{1,0:T(8,128)(2,1)} custom-call(s32[1]{0:T(128)} %bitcast.me, s32[512,1]{1,0:T(8,128)S(1)} %copy.17.slot, f32[512,2048]{1,0:T(8,128)S(1)} %shard_map.111.total, bf16[1024,2048]{1,0:T(8,128)(2,1)S(1)} %get-tuple-element.81.up, bf16[512,32]{1,0:T(8,128)(2,1)S(1)} %get-tuple-element.82.refs_0_, ...), custom_call_target="tpu_custom_call" | custom-call | flops 2147483648 | bytes 2097152 | tf_op jit(solution)/shard_map/pallas_call | solution.py:268
  (85 shorter events, 6.2 us)
Async XLA Ops:
  0.0 107.7 %copy-start = (s32[16]{0:T(128)S(1)}, s32[16]{0:T(128)}, u32[]{:S(2)}) copy-start(s32[16]{0:T(128)} %param.17) | copy-start | bytes 196
  0.0 50.2 %collective-permute-start.6 = (bf16[512,2048]{1,0:T(8,128)(2,1)}, bf16[512,2048]{1,0:T(8,128)(2,1)}, u32[]{:S(2)}, u32[]{:S(2)}) collective-permute-start(bf16[512,2048]{1,0:T(8,128)(2,1)} %refs_0_.3), channel_id=1, source_target_pairs={{0,4},{4,8},{8,12},{1,5},{5,9},{9,13},{2,6},{6,10},{10,14},{3,7},{... | collective-permute-start | bytes 6291464 | tf_op jit(solution)/shard_map/ppermute | solution.py:346
  6.4 49.3 %collective-permute-start.7 = (bf16[512,2048]{1,0:T(8,128)(2,1)}, bf16[512,2048]{1,0:T(8,128)(2,1)}, u32[]{:S(2)}, u32[]{:S(2)}) collective-permute-start(bf16[512,2048]{1,0:T(8,128)(2,1)} %refs_0_.3), channel_id=1, source_target_pairs={{4,0},{8,4},{12,8},{5,1},{9,5},{13,9},{6,2},{10,6},{14,10},{7,3},{... | collective-permute-start | bytes 6291464 | tf_op jit(solution)/shard_map/ppermute | solution.py:347
  7.7 5.5 %collective-permute-start.4 = (s32[1,6]{1,0:T(1,128)}, s32[1,6]{1,0:T(1,128)S(1)}, u32[]{:S(2)}, u32[]{:S(2)}) collective-permute-start(s32[1,6]{1,0:T(1,128)} %param.15), channel_id=1, source_target_pairs={{0,3},{1,2},{2,1},{3,0},{4,7},{5,6},{6,5},{7,4},{8,11},{9,10},{10,... | collective-permute-start | bytes 80 | tf_op jit(solution)/shard_map/ppermute | solution.py:308
  8.4 4.8 %collective-permute-start = (s32[1,6]{1,0:T(1,128)}, s32[1,6]{1,0:T(1,128)S(1)}, u32[]{:S(2)}, u32[]{:S(2)}) collective-permute-start(s32[1,6]{1,0:T(1,128)} %param.15), channel_id=1, source_target_pairs={{0,1},{1,0},{2,3},{3,2},{4,5},{5,4},{6,7},{7,6},{8,9},{9,8},{10,11... | collective-permute-start | bytes 80 | tf_op jit(solution)/shard_map/ppermute | solution.py:308
  9.4 3.8 %collective-permute-start.2 = (s32[1,6]{1,0:T(1,128)}, s32[1,6]{1,0:T(1,128)S(1)}, u32[]{:S(2)}, u32[]{:S(2)}) collective-permute-start(s32[1,6]{1,0:T(1,128)} %param.15), channel_id=1, source_target_pairs={{0,2},{1,3},{2,0},{3,1},{4,6},{5,7},{6,4},{7,5},{8,10},{9,11},{10,... | collective-permute-start | bytes 80 | tf_op jit(solution)/shard_map/ppermute | solution.py:308
  14.4 1.6 copy-start.3
  18.7 1.0 copy-start.20
  19.6 93.3 %collective-permute-start.3 = (bf16[2,4,32,2048]{3,2,1,0:T(8,128)(2,1)}, bf16[2,4,32,2048]{3,2,1,0:T(8,128)(2,1)S(1)}, u32[]{:S(2)}, u32[]{:S(2)}) collective-permute-start(bf16[2,4,32,2048]{3,2,1,0:T(8,128)(2,1)} %get-tuple-element.47), channel_id=1, source_target_pairs={{0,2},{1,3},{2,0},{3,1},{4,6},{5,7},{6,4},{7,5},{8,10},{9,11},{10,... | collective-permute-start | bytes 3145736 | tf_op jit(solution)/shard_map/ppermute | solution.py:355
  50.2 34.4 %collective-permute-start.8 = (bf16[512,2048]{1,0:T(8,128)(2,1)}, bf16[512,2048]{1,0:T(8,128)(2,1)}, u32[]{:S(2)}, u32[]{:S(2)}) collective-permute-start(bf16[512,2048]{1,0:T(8,128)(2,1)} %collective-permute-done.6.refs_1_), channel_id=1, source_target_pairs={{4,8},{8,12},{5,9},{9,13},{6,10},{10,14},{7,11},{11,15},{20,24},{2... | collective-permute-start | bytes 6291464 | tf_op jit(solution)/shard_map/ppermute | solution.py:360
  55.7 48.5 %collective-permute-start.9 = (bf16[512,2048]{1,0:T(8,128)(2,1)}, bf16[512,2048]{1,0:T(8,128)(2,1)}, u32[]{:S(2)}, u32[]{:S(2)}) collective-permute-start(bf16[512,2048]{1,0:T(8,128)(2,1)} %collective-permute-done.7.refs_2_), channel_id=1, source_target_pairs={{4,0},{8,4},{5,1},{9,5},{6,2},{10,6},{7,3},{11,7},{20,16},{24,20},... | collective-permute-start | bytes 6291464 | tf_op jit(solution)/shard_map/ppermute | solution.py:361
  59.8 1.0 copy-start.21
  60.8 53.7 %collective-permute-start.5 = (bf16[2,4,32,2048]{3,2,1,0:T(8,128)(2,1)}, bf16[2,4,32,2048]{3,2,1,0:T(8,128)(2,1)}, u32[]{:S(2)}, u32[]{:S(2)}) collective-permute-start(bf16[2,4,32,2048]{3,2,1,0:T(8,128)(2,1)} %get-tuple-element.48), channel_id=1, source_target_pairs={{0,3},{1,2},{2,1},{3,0},{4,7},{5,6},{6,5},{7,4},{8,11},{9,10},{10,... | collective-permute-start | bytes 3145736 | tf_op jit(solution)/shard_map/ppermute | solution.py:355
  61.1 4.4 %copy-start.8 = (bf16[512,2048]{1,0:T(8,128)(2,1)S(1)}, bf16[512,2048]{1,0:T(8,128)(2,1)}, u32[]{:S(2)}) copy-start(bf16[512,2048]{1,0:T(8,128)(2,1)} %refs_0_.3) | copy-start | bytes 6291460
  63.9 20.8 %copy-start.22 = (bf16[2,128,2048]{2,1,0:T(8,128)(2,1)}, bf16[2,128,2048]{2,1,0:T(8,128)(2,1)S(1)}, u32[]{:S(2)}) copy-start(bf16[2,128,2048]{2,1,0:T(8,128)(2,1)S(1)} %get-tuple-element.60) | copy-start | bytes 3145732
  63.9 43.8 %copy-start.24 = (s32[1,6]{1,0:T(1,128)S(1)}, s32[1,6]{1,0:T(1,128)}, u32[]{:S(2)}) copy-start(s32[1,6]{1,0:T(1,128)} %param.15) | copy-start | bytes 76
  63.9 44.8 %copy-start.4 = (bf16[4,32,8192]{2,1,0:T(8,128)(2,1)S(1)}, bf16[4,32,8192]{2,1,0:T(8,128)(2,1)}, u32[]{:S(2)}) copy-start(bf16[4,32,8192]{2,1,0:T(8,128)(2,1)} %down.7) | copy-start | bytes 6291460
  63.9 50.7 %collective-permute-start.1 = (bf16[2,4,32,2048]{3,2,1,0:T(8,128)(2,1)}, bf16[2,4,32,2048]{3,2,1,0:T(8,128)(2,1)}, u32[]{:S(2)}, u32[]{:S(2)}) collective-permute-start(bf16[2,4,32,2048]{3,2,1,0:T(8,128)(2,1)} %get-tuple-element.46), channel_id=1, source_target_pairs={{0,1},{1,0},{2,3},{3,2},{4,5},{5,4},{6,7},{7,6},{8,9},{9,8},{10,11... | collective-permute-start | bytes 3145736 | tf_op jit(solution)/shard_map/ppermute | solution.py:355
  104.2 72.1 %collective-permute-start.13 = (bf16[512,2048]{1,0:T(8,128)(2,1)}, bf16[512,2048]{1,0:T(8,128)(2,1)}, u32[]{:S(2)}, u32[]{:S(2)}) collective-permute-start(bf16[512,2048]{1,0:T(8,128)(2,1)} %collective-permute-done.8.refs_0_), channel_id=1, source_target_pairs={{8,12},{9,13},{10,14},{11,15},{24,28},{25,29},{26,30},{27,31}} | collective-permute-start | bytes 6291464 | tf_op jit(solution)/shard_map/ppermute | solution.py:365
  106.2 70.1 %collective-permute-start.14 = (bf16[512,2048]{1,0:T(8,128)(2,1)}, bf16[512,2048]{1,0:T(8,128)(2,1)}, u32[]{:S(2)}, u32[]{:S(2)}) collective-permute-start(bf16[512,2048]{1,0:T(8,128)(2,1)} %collective-permute-done.9.refs_1_), channel_id=1, source_target_pairs={{4,0},{5,1},{6,2},{7,3},{20,16},{21,17},{22,18},{23,19}} | collective-permute-start | bytes 6291464 | tf_op jit(solution)/shard_map/ppermute | solution.py:366
  108.7 3.8 %copy-start.23 = (s32[512]{0:T(512)S(1)}, s32[512]{0:T(512)}, u32[]{:S(2)}) copy-start(s32[512]{0:T(512)} %param.16) | copy-start | bytes 6148
  110.6 1.0 copy-start.10
  111.6 1.0 copy-start.12
  113.0 30.1 %collective-permute-start.11 = (bf16[2,128,2048]{2,1,0:T(8,128)(2,1)}, bf16[2,128,2048]{2,1,0:T(8,128)(2,1)S(1)}, u32[]{:S(2)}, u32[]{:S(2)}) collective-permute-start(bf16[2,128,2048]{2,1,0:T(8,128)(2,1)} %copy-done.20), channel_id=1, source_target_pairs={{0,2},{1,3},{2,0},{3,1},{4,6},{5,7},{6,4},{7,5},{8,10},{9,11},{10,... | collective-permute-start | bytes 3145736 | tf_op jit(solution)/shard_map/ppermute | solution.py:356
  114.5 43.2 %collective-permute-start.12 = (bf16[2,128,2048]{2,1,0:T(8,128)(2,1)}, bf16[2,128,2048]{2,1,0:T(8,128)(2,1)S(1)}, u32[]{:S(2)}, u32[]{:S(2)}) collective-permute-start(bf16[2,128,2048]{2,1,0:T(8,128)(2,1)} %copy-done.21), channel_id=1, source_target_pairs={{0,3},{1,2},{2,1},{3,0},{4,7},{5,6},{6,5},{7,4},{8,11},{9,10},{10,... | collective-permute-start | bytes 3145736 | tf_op jit(solution)/shard_map/ppermute | solution.py:356
  114.5 44.2 %collective-permute-start.10 = (bf16[2,128,2048]{2,1,0:T(8,128)(2,1)}, bf16[2,128,2048]{2,1,0:T(8,128)(2,1)S(1)}, u32[]{:S(2)}, u32[]{:S(2)}) collective-permute-start(bf16[2,128,2048]{2,1,0:T(8,128)(2,1)} %copy-done.22), channel_id=1, source_target_pairs={{0,1},{1,0},{2,3},{3,2},{4,5},{5,4},{6,7},{7,6},{8,9},{9,8},{10,11... | collective-permute-start | bytes 3145736 | tf_op jit(solution)/shard_map/ppermute | solution.py:356
  115.2 1.2 copy-start.13
  116.4 4.9 %copy-start.9 = (bf16[512,2048]{1,0:T(8,128)(2,1)S(1)}, bf16[512,2048]{1,0:T(8,128)(2,1)}, u32[]{:S(2)}) copy-start(bf16[512,2048]{1,0:T(8,128)(2,1)} %refs_0_.3) | copy-start | bytes 6291460
  128.0 31.8 %copy-start.11 = (bf16[2,128,2048]{2,1,0:T(8,128)(2,1)S(1)}, bf16[2,128,2048]{2,1,0:T(8,128)(2,1)}, u32[]{:S(2)}) copy-start(bf16[2,128,2048]{2,1,0:T(8,128)(2,1)} %copy-done.10) | copy-start | bytes 3145732
  143.1 1.0 copy-start.14
  157.7 1.0 copy-start.16
  158.7 1.0 copy-start.18
  159.7 1.2 copy-start.15
  160.9 1.2 copy-start.17
  162.2 1.2 copy-start.19
  163.4 3.7 %copy-start.2 = (bf16[8192,256]{1,0:T(8,128)(2,1)S(1)}, bf16[8192,256]{1,0:T(8,128)(2,1)}, u32[]{:S(2)}) copy-start(bf16[8192,256]{1,0:T(8,128)(2,1)} %shard_map.105.refs_3_.down) | copy-start | bytes 12582916
  163.4 5.0 %copy-start.7 = (f32[512,2048]{1,0:T(8,128)S(1)}, f32[512,2048]{1,0:T(8,128)}, u32[]{:S(2)}) copy-start(f32[512,2048]{1,0:T(8,128)} %get-tuple-element.56.base) | copy-start | bytes 12582916
  173.1 3.2 %copy-start.5 = (bf16[2048,2048]{1,0:T(8,128)(2,1)}, bf16[2048,2048]{1,0:T(8,128)(2,1)S(1)}, u32[]{:S(2)}) copy-start(bf16[2048,2048]{1,0:T(8,128)(2,1)S(1)} %get-tuple-element.79.weight) | copy-start | bytes 25165828
  178.8 11.8 %collective-permute-start.15 = (bf16[512,32]{1,0:T(8,128)(2,1)S(1)}, bf16[512,32]{1,0:T(8,128)(2,1)S(1)}, u32[]{:S(2)}, u32[]{:S(2)}) collective-permute-start(bf16[512,32]{1,0:T(8,128)(2,1)S(1)} %get-tuple-element.82.refs_0_), channel_id=1, source_target_pairs={{0,12},{4,0},{8,4},{12,8},{1,13},{5,1},{9,5},{13,9},{2,14},{6,2},{... | collective-permute-start | bytes 98312 | tf_op jit(solution)/shard_map/ppermute | solution.py:384
  178.9 15.9 %collective-permute-start.16 = (bf16[512,32]{1,0:T(8,128)(2,1)S(1)}, bf16[512,32]{1,0:T(8,128)(2,1)S(1)}, u32[]{:S(2)}, u32[]{:S(2)}) collective-permute-start(bf16[512,32]{1,0:T(8,128)(2,1)S(1)} %get-tuple-element.82.refs_0_), channel_id=1, source_target_pairs={{0,8},{4,12},{8,0},{12,4},{1,9},{5,13},{9,1},{13,5},{2,10},{6,14},... | collective-permute-start | bytes 98312 | tf_op jit(solution)/shard_map/ppermute | solution.py:384
  182.4 12.4 %collective-permute-start.17 = (bf16[512,32]{1,0:T(8,128)(2,1)S(1)}, bf16[512,32]{1,0:T(8,128)(2,1)S(1)}, u32[]{:S(2)}, u32[]{:S(2)}) collective-permute-start(bf16[512,32]{1,0:T(8,128)(2,1)S(1)} %get-tuple-element.82.refs_0_), channel_id=1, source_target_pairs={{0,4},{4,8},{8,12},{12,0},{1,5},{5,9},{9,13},{13,1},{2,6},{6,10},{... | collective-permute-start | bytes 98312 | tf_op jit(solution)/shard_map/ppermute | solution.py:384
  182.4 3.4 %copy-start.6 = (bf16[2048,2048]{1,0:T(8,128)(2,1)S(1)}, bf16[2048,2048]{1,0:T(8,128)(2,1)}, u32[]{:S(2)}) copy-start(bf16[2048,2048]{1,0:T(8,128)(2,1)} %copy-done.5) | copy-start | bytes 25165828
  194.8 4.6 %copy-start.1 = (s32[16]{0:T(128)S(1)}, s32[16]{0:T(128)}, u32[]{:S(2)}) copy-start(s32[16]{0:T(128)} %param.17) | copy-start | bytes 196

commit v9 on v8

--- a/solution.py
+++ b/solution.py
@@ -15,50 +15,50 @@
 BF16 = jnp.bfloat16
 
 
-def pick_kernel(places, down, up, down_out, up_out):
-    shards, _, width = down_out.shape[1:]
-    for t in range(shards):
-        down_out[0, t] = down[0, :, t * width:(t + 1) * width]
-    up_out[...] = up[...]
-
-
-def pick_pages(places, down, up, shards):
-    count = places.shape[0]
-    _, rank_part, features = down.shape
-    shapes = [(shards, rank_part, features // shards), up.shape[1:]]
+def pick_kernel(places, down, up, first, rest):
+    rank_part, width = down.shape[1], first.shape[2]
+    step = pl.program_id(0)
+    for c, out in enumerate((first, rest)):
+
+        @pl.when(step == c)
+        def _():
+            for t in range(down.shape[2] // width):
+                out[0, t * rank_part:(t + 1) * rank_part] = down[0, :, t * width:(t + 1) * width]
+            rest[1 + c] = up[0]
+
+
+def pick_pages(places, down, up):
+    block = up.shape[1:]
     return pl.pallas_call(
         pick_kernel,
-        out_shape=[jax.ShapeDtypeStruct((count,) + shape, BF16) for shape in shapes],
+        out_shape=[jax.ShapeDtypeStruct((count,) + block, BF16) for count in (1, 3)],
         grid_spec=pltpu.PrefetchScalarGridSpec(
             num_scalar_prefetch=1,
-            grid=(count,),
+            grid=(CAP,),
             in_specs=[pl.BlockSpec((1,) + a.shape[1:], lambda i, places: (places[i], 0, 0)) for a in (down, up)],
-            out_specs=[
-                pl.BlockSpec((1,) + shapes[0], lambda i, places: (i, 0, 0, 0)),
-                pl.BlockSpec((1,) + shapes[1], lambda i, places: (i, 0, 0)),
-            ],
-        ),
-        compiler_params=PARAMS,
+            out_specs=[pl.BlockSpec((count,) + block, lambda i, places: (0, 0, 0)) for count in (1, 3)],
+        ),
+        compiler_params=TAIL_PARAMS,
     )(places, down, up)
 
 
 def join_downs_kernel(*refs):
     *pages, out = refs
-    joined = jnp.concatenate([p[c, 0] for p in pages for c in range(CAP)], axis=0)
-    out[...] = joined.T
-
-
-def join_downs(downs):
-    _, shards, rank_part, features = downs[0].shape
-    slots = CAP * rank_part * len(downs)
+    out[...] = jnp.concatenate([p[0] for p in pages], axis=0).T
+
+
+def join_downs(pages, shards):
+    _, rank, columns = pages[0].shape
+    rank_part = rank // shards
+    slots = rank_part * len(pages)
     return pl.pallas_call(
         join_downs_kernel,
-        out_shape=jax.ShapeDtypeStruct((shards * features, slots), BF16),
+        out_shape=jax.ShapeDtypeStruct((shards * columns, slots), BF16),
         grid=(shards,),
-        in_specs=[pl.BlockSpec((CAP, 1, rank_part, features), lambda t: (0, t, 0, 0))] * len(downs),
-        out_specs=pl.BlockSpec((features, slots), lambda t: (t, 0)),
+        in_specs=[pl.BlockSpec((1, rank_part, columns), lambda t: (0, t, 0))] * len(pages),
+        out_specs=pl.BlockSpec((columns, slots), lambda t: (t, 0)),
         compiler_params=PARAMS,
-    )(*downs)
+    )(*pages)
 
 
 def join_ups_kernel(*refs):
@@ -67,19 +67,19 @@
 
         @pl.when(pl.program_id(0) == j)
         def _():
-            out[...] = p[...]
-
-
-def join_ups(ups):
-    count, rank, columns = ups[0].shape
+            out[...] = p[1:]
+
+
+def join_ups(pages):
+    _, rank, columns = pages[0].shape
     return pl.pallas_call(
         join_ups_kernel,
-        out_shape=jax.ShapeDtypeStruct((count * len(ups), rank, columns), BF16),
-        grid=(len(ups),),
-        in_specs=[pl.BlockSpec(up.shape, lambda j: (0, 0, 0)) for up in ups],
-        out_specs=pl.BlockSpec(ups[0].shape, lambda j: (j, 0, 0)),
+        out_shape=jax.ShapeDtypeStruct((CAP * len(pages), rank, columns), BF16),
+        grid=(len(pages),),
+        in_specs=[pl.BlockSpec(p.shape, lambda j: (0, 0, 0)) for p in pages],
+        out_specs=pl.BlockSpec((CAP, rank, columns), lambda j: (j, 0, 0)),
         compiler_params=PARAMS,
-    )(*ups).reshape(-1, columns)
+    )(*pages).reshape(-1, columns)
 
 
 RESIDENT = pl.BlockSpec(memory_space=pltpu.VMEM)
@@ -120,6 +120,9 @@
     steps = len(xs) * halves
     valid = jnp.repeat(((source >= 0) & (source < n_tensor)).astype(jnp.int32), halves)
     start = jnp.clip(source, 0, n_tensor - 1)[:, None] * halves + jnp.arange(halves)[None, :]
+    if len(xs) > 1:
+        idle = jnp.concatenate([start[1:2, :1], start[:-1, -1:]], axis=0)
+        start = jnp.where(((source >= 0) & (source < n_tensor))[:, None], start, idle)
     start = start.reshape(-1).astype(jnp.int32)
     whole = [pl.BlockSpec((rows, a.shape[1]), lambda s, *_: (0, 0)) for a in walked]
     columns = sum(a.shape[1] for a in walked)
@@ -147,10 +150,14 @@
 
 
 def pin_kernel(source, weight, down, base, low, up, weight_out, down_out, base_out, low_out, up_out, sems):
-    width = weight_out.shape[0]
+    width, columns = weight_out.shape
     rows = pl.ds(pl.multiple_of(source[0] * width, width), width)
     pairs = [
-        (weight.at[rows], weight_out), (down.at[rows], down_out), (base, base_out), (low, low_out), (up, up_out)
+        (weight.at[rows, pl.ds(0, columns)], weight_out),
+        (down.at[rows], down_out),
+        (base, base_out),
+        (low, low_out),
+        (up, up_out),
     ]
     copies = [pltpu.make_async_copy(a, b, sems.at[i]) for i, (a, b) in enumerate(pairs)]
     for copy in copies:
@@ -160,7 +167,7 @@
 
 
 def pin(source, width, weight, down, base, low, up):
-    shapes = [((width,) + a.shape[1:], a.dtype) for a in (weight, down)]
+    shapes = [((width, weight.shape[1] // 2), BF16), ((width, down.shape[1]), BF16)]
     shapes += [(a.shape, a.dtype) for a in (base, low, up)]
     return pl.pallas_call(
         pin_kernel,
@@ -220,28 +227,45 @@
     )(which, from_left, from_right, down, total, slot, live)
 
 
-def base_kernel(which, x, weight, total, out):
+def base_kernel(which, source, x, near, weight, total, out, rest, sems):
+    width, columns = near.shape
+    parts, _, part = rest.shape
+    rows = pl.ds(pl.multiple_of(source[0] * width, width), width)
+
     @pl.when(which[0] != 0)
     def _():
-        part = min(out.shape[1], 512)
-        for n in range(0, out.shape[1], part):
-            out[:, n:n + part] = total[:, n:n + part] + jnp.dot(
-                x[...], weight[:, n:n + part], preferred_element_type=F32
-            )
-
-
-def add_last(which, x, weight, total):
+        copies = [
+            pltpu.make_async_copy(weight.at[rows, pl.ds(columns + n * part, part)], rest.at[n], sems.at[n])
+            for n in range(parts)
+        ]
+        for copy in copies:
+            copy.start()
+        for n in range(2 * parts):
+            cut = slice(n * part, (n + 1) * part)
+            if n < parts:
+                rows_of = near[:, cut]
+            else:
+                copies[n - parts].wait()
+                rows_of = rest[n - parts]
+            out[:, cut] = total[:, cut] + jnp.dot(x[...], rows_of, preferred_element_type=F32)
+
+
+def add_last(which, source, x, near, weight, total):
     rows, width = x.shape
     columns = weight.shape[1]
+    part = columns // 4
     return pl.pallas_call(
         base_kernel,
         out_shape=pltpu.VMEM((rows, columns), F32),
-        in_specs=[pl.BlockSpec(memory_space=pltpu.SMEM)] + [RESIDENT] * 3,
+        in_specs=[pl.BlockSpec(memory_space=pltpu.SMEM)] * 2 + [RESIDENT, RESIDENT, IN_HBM, RESIDENT],
         out_specs=RESIDENT,
-        input_output_aliases={3: 0},
+        scratch_shapes=[pltpu.VMEM((2, width, part), BF16), pltpu.SemaphoreType.DMA((2,))],
+        input_output_aliases={5: 0},
         compiler_params=TAIL_PARAMS,
-        cost_estimate=pl.CostEstimate(flops=2 * width * rows * columns, bytes_accessed=0, transcendentals=0),
-    )(which, x, weight, total)
+        cost_estimate=pl.CostEstimate(
+            flops=2 * width * rows * columns, bytes_accessed=width * columns, transcendentals=0
+        ),
+    )(which, source, x, near, weight, total)
 
 
 def finish_kernel(parts, me, slot, total, up, *refs):
@@ -334,7 +358,7 @@
     entries = own_list.shape[0]
     one_hot = row_request_entry[:, None] == jnp.arange(entries)[None, :]
     row_rank = jnp.sum(jnp.where(one_hot, ranks[own_list][None, :], 0), axis=1)
-    if n_tensor != 4 or width % HALF or rank_part % 16:
+    if n_tensor != 4 or width % HALF or rank_part % 16 or width != columns:
         return plain(
             attention_result, output_weight, adapter_down_weight, adapter_up_weight, adapter_page_row,
             own_list, one_hot, row_rank,
@@ -347,39 +371,41 @@
     left_1 = lax.ppermute(own, "tensor", left)
 
     slots, places = asked_pages(requests, adapter_page_row, holder_length)
-    downs, ups = [], []
-    for j in range(n_dp):
-        down, up = pick_pages(places[j], adapter_down_weight, adapter_up_weight, n_tensor)
-        if j:
-            pairs = [(i, i ^ j) for i in range(n_dp)]
-            down = lax.ppermute(down, "dp", pairs)
-            up = lax.ppermute(after(up, right_1, left_1), "dp", pairs)
-        downs.append(down)
-        ups.append(up)
-
+    firsts, rests = zip(*[pick_pages(places[j], adapter_down_weight, adapter_up_weight) for j in range(n_dp)])
+
+    def send(pages):
+        return (pages[0],) + tuple(
+            lax.ppermute(pages[j], "dp", [(i, i ^ j) for i in range(n_dp)]) for j in range(1, n_dp)
+        )
+
+    firsts = send(firsts)
+    right_1, left_1 = lax.optimization_barrier((right_1, left_1, *firsts))[:2]
+    rests = send(rests)
     right_2 = lax.ppermute(right_1, "tensor", right[1:])
     left_2 = lax.ppermute(left_1, "tensor", left[:-1])
     near = me + jnp.array([0, -1, 1], jnp.int32)
+    far = me + jnp.array([-2, 2], jnp.int32)
     base, = add_chunk((), [own, right_1, left_1], near, output_weight, None)
     base, right_2, left_2 = lax.optimization_barrier((base, right_2, left_2))
     right_3 = lax.ppermute(right_2, "tensor", right[2:])
     left_3 = lax.ppermute(left_2, "tensor", left[:-2])
 
-    down = join_downs(after(tuple(downs), base))
-    low, = add_chunk((), [own, right_1, left_1], near, None, down)
-    far = me + jnp.array([-2, 2], jnp.int32)
-    base, low = add_chunk((base, low), [right_2, left_2], far, output_weight, down)
-    up = join_ups(after(tuple(ups), base))
+    base, = add_chunk((base,), [right_2, left_2], far, output_weight, None)
+    rests = after(rests, base)
+    down = join_downs([p for pair in zip(firsts, rests) for p in pair], n_tensor)
+    up = join_ups(rests)
+    blocks = [own, right_1, left_1, right_2, left_2]
+    low, = add_chunk((), blocks, jnp.concatenate([near, far]), None, down)
+
     which = jnp.where(me == n_tensor - 1, 1, jnp.where(me == 0, -1, 0)).astype(jnp.int32)
     source = jnp.where(me == 0, n_tensor - 1, 0).astype(jnp.int32)
     slot = jnp.sum(jnp.where(one_hot, slots[None, :], 0), axis=1)[:, None]
     live = row_rank[:, None] - me * rank_part
-    rest = (which[None], slot, live)
-    pinned = pin(after(source[None], rest), width, output_weight, down, base, low, up)
-    weight, down, base, low, up, right_3, left_3 = lax.optimization_barrier((*pinned, right_3, left_3))
-    which, slot, live = rest
+    source, which, slot, live = lax.optimization_barrier((source[None], which[None], slot, live, low))[:4]
+    pinned = pin(source, width, output_weight, down, base, low, up)
+    part, down, base, low, up, right_3, left_3 = lax.optimization_barrier((*pinned, right_3, left_3))
     low, x = finish_low(which, right_3, left_3, down, low, slot, live, rank_part)
-    base = add_last(which, x, weight, base)
+    base = add_last(which, source, x, part, output_weight, base)
     lows = [low] + [
         lax.ppermute(low, "tensor", [(i, (i - j) % n_tensor) for i in range(n_tensor)])
         for j in range(1, n_tensor)

time: 200 us -> 233 us (1.17)
  waiting for transfers between devices: 69.9 us -> 113 us
  Pallas kernels: 74.8 us -> 69.2 us
  local copies, waits for them, and re-layouts: 23.9 us -> 19.4 us
  starting transfers between devices: 25.5 us -> 23.1 us
    ppermute x6, waiting for transfers between devices: 13.7 us -> 66.1 us  [send(): lax.ppermute(pages[j], 'dp', [(i, i ^ j) for i in range(n_dp)])]
    ppermute x1, waiting for transfers between devices: 28.9 us -> 9.72 us  [local(): right_1 = lax.ppermute(own, 'tensor', right)]
    unnamed x50 -> x46, local copies, waits for them, and re-layouts: 22.5 us -> 15.8 us
    ppermute x1, waiting for transfers between devices: 19.6 us -> 25.8 us  [local(): left_2 = lax.ppermute(left_1, 'tensor', left[:-1])]
    ppermute x3, waiting for transfers between devices: 4.14 us -> 7.56 us  [local(): lax.ppermute(low, 'tensor', [(i, (i - j) % n_tensor) for i in range(n_ten...]
    pallas_call x1, Pallas kernels: 4.71 us -> 2.24 us  [pin(): pl.pallas_call(pin_kernel, out_shape=[pltpu.VMEM(*a) for a in shapes], in...]
    pallas_call x3, Pallas kernels: 40.9 us -> 38.4 us  [add_chunk(): pl.pallas_call(functools.partial(chunk_kernel, len(xs), halves, bool(tota...]
    ppermute x1, starting transfers between devices: 6.42 us -> 4.07 us  [local(): right_1 = lax.ppermute(own, 'tensor', right)]
  transfers between devices with their start and end apart: 18 -> 18, of which waited for: 5 -> 8; matrix products, arithmetic and copies ran while one was open for 3% -> 5% of each run, Pallas kernels for 34% -> 27%
where the time goes in v9:
time: 233 us
  waiting for transfers between devices  113 us (48%)
  Pallas kernels  69.2 us (30%)
  starting transfers between devices  23.1 us (10%)
  local copies, waits for them, and re-layouts  19.4 us (8%)
  other arithmetic  7.3 us (3%)
    ppermute x6, waiting for transfers between devices, send(): lax.ppermute(pages[j], 'dp', [(i, i ^ j) for i in range(n_dp)])  66.1 us
    pallas_call x3, Pallas kernels, add_chunk(): pl.pallas_call(functools.partial(chunk_kernel, len(xs), halves, bool(tota...  38.4 us
    ppermute x1, waiting for transfers between devices, local(): left_2 = lax.ppermute(left_1, 'tensor', left[:-1])  25.8 us
    unnamed x46, local copies, waits for them, and re-layouts  15.8 us
    ppermute x1, waiting for transfers between devices, local(): right_1 = lax.ppermute(own, 'tensor', right)  9.72 us
    ppermute x3, waiting for transfers between devices, local(): lax.ppermute(low, 'tensor', [(i, (i - j) % n_tensor) for i in range(n_ten...  7.56 us
    pallas_call x4, Pallas kernels, pick_pages(): pl.pallas_call(pick_kernel, out_shape=[jax.ShapeDtypeStruct((count,) + bl...  6.44 us
    pallas_call x1, Pallas kernels, add_last(): pl.pallas_call(base_kernel, out_shape=pltpu.VMEM((rows, columns), F32), i...  5.04 us
  transfers between devices with their start and end apart: 18, of which 8 were waited for; matrix products, arithmetic and copies ran while one was open for 5% of the time, Pallas kernels for 27%

profile of v9, /device:TPU:0, one launch (start us, length us, event | category | flops | bytes accessed | tf_op | source)
XLA Modules:
  0.0 232.7 jit_solution(1728800948937162646)
XLA Ops:
  0.0 2.9 %collective-permute-start.4 = (s32[1,6]{1,0:T(1,128)}, s32[1,6]{1,0:T(1,128)S(1)}, u32[]{:S(2)}, u32[]{:S(2)}) collective-permute-start(s32[1,6]{1,0:T(1,128)} %param.15), channel_id=1, source_target_pairs={{0,2},{1,3},{2,0},{3,1},{4,6},{5,7},{6,4},{7,5},{8,10},{9,11},{10,... | collective-permute-start | bytes 80 | tf_op jit(solution)/shard_map/ppermute | solution.py:332
  3.1 4.1 %collective-permute-start = (bf16[512,2048]{1,0:T(8,128)(2,1)}, bf16[512,2048]{1,0:T(8,128)(2,1)S(1)}, u32[]{:S(2)}, u32[]{:S(2)}) collective-permute-start(bf16[512,2048]{1,0:T(8,128)(2,1)} %refs_0_.3), channel_id=1, source_target_pairs={{0,4},{4,8},{8,12},{1,5},{5,9},{9,13},{2,6},{6,10},{10,14},{3,7},{... | collective-permute-start | bytes 6291464 | tf_op jit(solution)/shard_map/ppermute | solution.py:370
  7.2 1.3 collective-permute-start.1
  8.5 0.7 clamp_multiply_fusion.1
  9.8 0.7 fusion.10
  10.4 0.7 clamp_multiply_fusion
  11.1 0.7 add_bitcast_fusion.1
  11.8 0.9 select_reduce_fusion.2
  13.1 1.6 copy-done.3
  14.7 1.6 copy-done.5
  16.2 1.9 shard_map.102
  18.1 1.5 collective-permute-start.5
  19.9 2.0 shard_map.103
  22.2 1.9 shard_map.101
  25.1 0.7 shard_map.100
  25.9 1.2 copy-done.9
  27.1 0.8 copy-done.18
  27.9 5.1 %collective-permute-done.5.refs_4_ = bf16[1,128,2048]{2,1,0:T(8,128)(2,1)S(1)} collective-permute-done((bf16[1,128,2048]{2,1,0:T(8,128)(2,1)S(1)}, bf16[1,128,2048]{2,1,0:T(8,128)(2,1)S(1)}, u32[]{:S(2)}, u32[]{:S(2)}) %collective-permute-start.5) | collective-permute-done | bytes 524320 | tf_op jit(solution)/shard_map/ppermute | solution.py:378
  32.9 9.0 %collective-permute-done.7.refs_6_ = bf16[1,128,2048]{2,1,0:T(8,128)(2,1)S(1)} collective-permute-done((bf16[1,128,2048]{2,1,0:T(8,128)(2,1)S(1)}, bf16[1,128,2048]{2,1,0:T(8,128)(2,1)S(1)}, u32[]{:S(2)}, u32[]{:S(2)}) %collective-permute-start.7) | collective-permute-done | bytes 524320 | tf_op jit(solution)/shard_map/ppermute | solution.py:378
  41.9 0.8 copy-done.16
  42.7 9.7 %collective-permute-done.refs_1_ = bf16[512,2048]{1,0:T(8,128)(2,1)S(1)} collective-permute-done((bf16[512,2048]{1,0:T(8,128)(2,1)}, bf16[512,2048]{1,0:T(8,128)(2,1)S(1)}, u32[]{:S(2)}, u32[]{:S(2)}) %collective-permute-start) | collective-permute-done | bytes 2097184 | tf_op jit(solution)/shard_map/ppermute | solution.py:370
  52.4 4.2 %collective-permute-done.1.refs_2_ = bf16[512,2048]{1,0:T(8,128)(2,1)} collective-permute-done((bf16[512,2048]{1,0:T(8,128)(2,1)}, bf16[512,2048]{1,0:T(8,128)(2,1)}, u32[]{:S(2)}, u32[]{:S(2)}) %collective-permute-start.1) | collective-permute-done | bytes 2097184 | tf_op jit(solution)/shard_map/ppermute | solution.py:371
  56.7 0.8 collective-permute-start.8
  57.5 1.3 collective-permute-start.9
  60.4 1.4 add_reduce_fusion
  61.9 1.6 copy-done.11
  63.5 1.6 copy-done.14
  65.1 17.4 %shard_map.104.refs_3_ = f32[512,2048]{1,0:T(8,128)} custom-call(s32[6]{0:T(128)S(1)} %select_n.234.start, s32[6]{0:T(128)S(1)} %reshape.350.valid, bf16[512,2048]{1,0:T(8,128)(2,1)S(1)} %copy-done.11, bf16[512,2048]{1,0:T(8,128)(2,1)S(1)} %copy-done.14, bf16[512,2048]{1,0:T(8,128)(2,1)} %collective-permute-done.1.refs_2_, bf16[8192,2048]{1,0:T(8,128)(2,1)} %weight.3), custom_call_target="tpu_custom_call" | custom-call | flops 12884901888 | bytes 39845888 | tf_op jit(solution)/shard_map/pallas_call | solution.py:129
  82.5 25.8 %collective-permute-done.9.refs_1_.refs_4_ = bf16[512,2048]{1,0:T(8,128)(2,1)} collective-permute-done((bf16[512,2048]{1,0:T(8,128)(2,1)}, bf16[512,2048]{1,0:T(8,128)(2,1)}, u32[]{:S(2)}, u32[]{:S(2)}) %collective-permute-start.9) | collective-permute-done | bytes 2097184 | tf_op jit(solution)/shard_map/ppermute | solution.py:385
  108.3 2.0 collective-permute-start.13
  110.3 1.5 collective-permute-start.14
  112.5 1.5 collective-permute-start.11
  114.0 0.6 collective-permute-start.10
  116.0 11.6 %shard_map.105.base = f32[512,2048]{1,0:T(8,128)} custom-call(s32[4]{0:T(128)S(1)} %select_n.236.start, s32[4]{0:T(128)S(1)} %reshape.351.valid, bf16[512,2048]{1,0:T(8,128)(2,1)S(1)} %collective-permute-done.8.refs_0_.refs_3_, bf16[512,2048]{1,0:T(8,128)(2,1)} %collective-permute-done.9.refs_1_.refs_4_, bf16[8192,2048]{1,0:T(8,128)(2,1)} %weight.3, ...), custom_call_target="tpu_custom_call" | custom-call | flops 8589934592 | bytes 29360128 | tf_op jit(solution)/shard_map/pallas_call | solution.py:129
  127.6 22.5 %collective-permute-done.11.refs_5_.refs_2_ = bf16[3,128,2048]{2,1,0:T(8,128)(2,1)} collective-permute-done((bf16[3,128,2048]{2,1,0:T(8,128)(2,1)}, bf16[3,128,2048]{2,1,0:T(8,128)(2,1)}, u32[]{:S(2)}, u32[]{:S(2)}) %collective-permute-start.11) | collective-permute-done | bytes 1572896 | tf_op jit(solution)/shard_map/ppermute | solution.py:378
  150.1 29.6 %collective-permute-done.12.refs_7_.refs_3_ = bf16[3,128,2048]{2,1,0:T(8,128)(2,1)} collective-permute-done((bf16[3,128,2048]{2,1,0:T(8,128)(2,1)}, bf16[3,128,2048]{2,1,0:T(8,128)(2,1)}, u32[]{:S(2)}, u32[]{:S(2)}) %collective-permute-start.12) | collective-permute-done | bytes 1572896 | tf_op jit(solution)/shard_map/ppermute | solution.py:378
  179.7 5.0 %shard_map.108 = bf16[8,128,2048]{2,1,0:T(8,128)(2,1)} custom-call(bf16[3,128,2048]{2,1,0:T(8,128)(2,1)S(1)} %copy-done.10, bf16[3,128,2048]{2,1,0:T(8,128)(2,1)} %collective-permute-done.10.refs_3_.refs_1_, bf16[3,128,2048]{2,1,0:T(8,128)(2,1)} %collective-permute-done.11.refs_5_.refs_2_, bf16[3,128,2048]{2,1,0:T(8,128)(2,1)} %collective-permute-done.12.refs_7_.refs_3_), custom_call_target="tpu_custom_call" | custom-call | tf_op jit(solution)/shard_map/pallas_call | solution.py:75
  184.7 5.0 %shard_map.106.refs_5_.down = bf16[8192,256]{1,0:T(8,128)(2,1)} custom-call(bf16[1,128,2048]{2,1,0:T(8,128)(2,1)S(1)} %copy-done.19, bf16[3,128,2048]{2,1,0:T(8,128)(2,1)S(1)} %copy-done.10, bf16[1,128,2048]{2,1,0:T(8,128)(2,1)S(1)} %copy-done.17, bf16[3,128,2048]{2,1,0:T(8,128)(2,1)} %collective-permute-done.10.refs_3_.refs_1_, ...), custom_call_target="tpu_custom_call" | custom-call | tf_op jit(solution)/shard_map/pallas_call | solution.py:54
  189.7 9.3 %shard_map.107.low = f32[512,256]{1,0:T(8,128)S(1)} custom-call(s32[10]{0:T(128)S(1)} %select_n.214.start, s32[10]{0:T(128)S(1)} %reshape.349.valid, bf16[512,2048]{1,0:T(8,128)(2,1)S(1)} %copy-done.12, bf16[512,2048]{1,0:T(8,128)(2,1)S(1)} %copy-done.15, bf16[512,2048]{1,0:T(8,128)(2,1)} %collective-permute-done.1.refs_2_, bf16[512,2048]{1,0:T(8,128)(2,1)} %copy-done.8, ...), custom_call_target="tpu_custom_call" | custom-call | flops 2684354560 | bytes 16777216 | tf_op jit(solution)/shard_map/pallas_call | solution.py:129
  199.3 2.2 copy-done.2
  201.5 2.2 copy-done.6
  203.7 2.2 copy-done.7
  205.9 2.2 shard_map.109
  208.2 2.5 %shard_map.110 = (bf16[512,32]{1,0:T(8,128)(2,1)S(1)}, bf16[512,2048]{1,0:T(8,128)(2,1)S(1)}) custom-call(s32[1]{0:T(128)} %bitcast.2.which, bf16[512,2048]{1,0:T(8,128)(2,1)} %collective-permute-done.13.from_left, bf16[512,2048]{1,0:T(8,128)(2,1)} %collective-permute-done.14.from_right, bf16[2048,256]{1,0:T(8,128)(2,1)S(1)} %get-tuple-element.67.down, ...), custom_call_target="tpu_custom_call" | custom-call | flops 536870912 | bytes 2097152 | tf_op jit(solution)/shard_map/pallas_call | solution.py:217
  210.8 4.7 %collective-permute-start.16 = (bf16[512,32]{1,0:T(8,128)(2,1)S(1)}, bf16[512,32]{1,0:T(8,128)(2,1)S(1)}, u32[]{:S(2)}, u32[]{:S(2)}) collective-permute-start(bf16[512,32]{1,0:T(8,128)(2,1)S(1)} %get-tuple-element.74.refs_0_), channel_id=1, source_target_pairs={{0,8},{4,12},{8,0},{12,4},{1,9},{5,13},{9,1},{13,5},{2,10},{6,14},... | collective-permute-start | bytes 98312 | tf_op jit(solution)/shard_map/ppermute | solution.py:410
  215.5 5.0 %shard_map.111.total = f32[512,2048]{1,0:T(8,128)S(1)} custom-call(s32[1]{0:T(128)} %bitcast.2.which, s32[1]{0:T(128)} %bitcast.1.source, bf16[512,2048]{1,0:T(8,128)(2,1)S(1)} %get-tuple-element.70.x, bf16[2048,1024]{1,0:T(8,128)(2,1)S(1)} %get-tuple-element.71.near, bf16[8192,2048]{1,0:T(8,128)(2,1)} %weight.3, ...), custom_call_target="tpu_custom_call", output_to_operand_aliasing={{}: (5, {})} | custom-call | flops 4294967296 | bytes 4194304 | tf_op jit(solution)/shard_map/pallas_call | solution.py:257
  220.6 7.6 %collective-permute-done.16.refs_2_ = bf16[512,32]{1,0:T(8,128)(2,1)S(1)} collective-permute-done((bf16[512,32]{1,0:T(8,128)(2,1)S(1)}, bf16[512,32]{1,0:T(8,128)(2,1)S(1)}, u32[]{:S(2)}, u32[]{:S(2)}) %collective-permute-start.16) | collective-permute-done | bytes 32800 | tf_op jit(solution)/shard_map/ppermute | solution.py:410
  228.1 4.6 %shard_map.112 = bf16[512,2048]{1,0:T(8,128)(2,1)} custom-call(s32[1]{0:T(128)} %bitcast.me, s32[512,1]{1,0:T(8,128)S(1)} %copy.24.slot, f32[512,2048]{1,0:T(8,128)S(1)} %shard_map.111.total, bf16[1024,2048]{1,0:T(8,128)(2,1)S(1)} %get-tuple-element.73.up, bf16[512,32]{1,0:T(8,128)(2,1)S(1)} %get-tuple-element.74.refs_0_, ...), custom_call_target="tpu_custom_call" | custom-call | flops 2147483648 | bytes 2097152 | tf_op jit(solution)/shard_map/pallas_call | solution.py:292
  (100 shorter events, 7.0 us)
Async XLA Ops:
  0.0 115.2 %copy-start = (s32[16]{0:T(128)S(1)}, s32[16]{0:T(128)}, u32[]{:S(2)}) copy-start(s32[16]{0:T(128)} %param.17) | copy-start | bytes 196
  0.0 11.8 %collective-permute-start.4 = (s32[1,6]{1,0:T(1,128)}, s32[1,6]{1,0:T(1,128)S(1)}, u32[]{:S(2)}, u32[]{:S(2)}) collective-permute-start(s32[1,6]{1,0:T(1,128)} %param.15), channel_id=1, source_target_pairs={{0,2},{1,3},{2,0},{3,1},{4,6},{5,7},{6,4},{7,5},{8,10},{9,11},{10,... | collective-permute-start | bytes 80 | tf_op jit(solution)/shard_map/ppermute | solution.py:332
  2.9 8.9 %collective-permute-start.6 = (s32[1,6]{1,0:T(1,128)}, s32[1,6]{1,0:T(1,128)S(1)}, u32[]{:S(2)}, u32[]{:S(2)}) collective-permute-start(s32[1,6]{1,0:T(1,128)} %param.15), channel_id=1, source_target_pairs={{0,3},{1,2},{2,1},{3,0},{4,7},{5,6},{6,5},{7,4},{8,11},{9,10},{10,... | collective-permute-start | bytes 80 | tf_op jit(solution)/shard_map/ppermute | solution.py:332
  2.9 8.9 %collective-permute-start.2 = (s32[1,6]{1,0:T(1,128)}, s32[1,6]{1,0:T(1,128)S(1)}, u32[]{:S(2)}, u32[]{:S(2)}) collective-permute-start(s32[1,6]{1,0:T(1,128)} %param.15), channel_id=1, source_target_pairs={{0,1},{1,0},{2,3},{3,2},{4,5},{5,4},{6,7},{7,6},{8,9},{9,8},{10,11... | collective-permute-start | bytes 80 | tf_op jit(solution)/shard_map/ppermute | solution.py:332
  3.1 49.3 %collective-permute-start = (bf16[512,2048]{1,0:T(8,128)(2,1)}, bf16[512,2048]{1,0:T(8,128)(2,1)S(1)}, u32[]{:S(2)}, u32[]{:S(2)}) collective-permute-start(bf16[512,2048]{1,0:T(8,128)(2,1)} %refs_0_.3), channel_id=1, source_target_pairs={{0,4},{4,8},{8,12},{1,5},{5,9},{9,13},{2,6},{6,10},{10,14},{3,7},{... | collective-permute-start | bytes 6291464 | tf_op jit(solution)/shard_map/ppermute | solution.py:370
  7.2 49.5 %collective-permute-start.1 = (bf16[512,2048]{1,0:T(8,128)(2,1)}, bf16[512,2048]{1,0:T(8,128)(2,1)}, u32[]{:S(2)}, u32[]{:S(2)}) collective-permute-start(bf16[512,2048]{1,0:T(8,128)(2,1)} %refs_0_.3), channel_id=1, source_target_pairs={{4,0},{8,4},{12,8},{5,1},{9,5},{13,9},{6,2},{10,6},{14,10},{7,3},{... | collective-permute-start | bytes 6291464 | tf_op jit(solution)/shard_map/ppermute | solution.py:371
  13.1 1.6 copy-start.3
  14.7 1.6 copy-start.5
  18.1 14.8 %collective-permute-start.5 = (bf16[1,128,2048]{2,1,0:T(8,128)(2,1)S(1)}, bf16[1,128,2048]{2,1,0:T(8,128)(2,1)S(1)}, u32[]{:S(2)}, u32[]{:S(2)}) collective-permute-start(bf16[1,128,2048]{2,1,0:T(8,128)(2,1)S(1)} %get-tuple-element.42), channel_id=1, source_target_pairs={{0,2},{1,3},{2,0},{3,1},{4,6},{5,7},{6,4},{7,5},{8,10},{9,11},{10,... | collective-permute-start | bytes 1572872 | tf_op jit(solution)/shard_map/ppermute | solution.py:378
  21.9 20.0 %collective-permute-start.7 = (bf16[1,128,2048]{2,1,0:T(8,128)(2,1)S(1)}, bf16[1,128,2048]{2,1,0:T(8,128)(2,1)S(1)}, u32[]{:S(2)}, u32[]{:S(2)}) collective-permute-start(bf16[1,128,2048]{2,1,0:T(8,128)(2,1)S(1)} %get-tuple-element.43), channel_id=1, source_target_pairs={{0,3},{1,2},{2,1},{3,0},{4,7},{5,6},{6,5},{7,4},{8,11},{9,10},{10,... | collective-permute-start | bytes 1572872 | tf_op jit(solution)/shard_map/ppermute | solution.py:378
  22.2 2.9 %copy-start.4 = (bf16[4,32,8192]{2,1,0:T(8,128)(2,1)S(1)}, bf16[4,32,8192]{2,1,0:T(8,128)(2,1)}, u32[]{:S(2)}) copy-start(bf16[4,32,8192]{2,1,0:T(8,128)(2,1)} %down.7) | copy-start | bytes 6291460
  24.1 17.8 %collective-permute-start.3 = (bf16[1,128,2048]{2,1,0:T(8,128)(2,1)S(1)}, bf16[1,128,2048]{2,1,0:T(8,128)(2,1)S(1)}, u32[]{:S(2)}, u32[]{:S(2)}) collective-permute-start(bf16[1,128,2048]{2,1,0:T(8,128)(2,1)S(1)} %get-tuple-element.41), channel_id=1, source_target_pairs={{0,1},{1,0},{2,3},{3,2},{4,5},{5,4},{6,7},{7,6},{8,9},{9,8},{10,11... | collective-permute-start | bytes 1572872 | tf_op jit(solution)/shard_map/ppermute | solution.py:378
  25.1 36.7 %copy-start.21 = (s32[2]{0:T(128)S(1)}, s32[2]{0:T(128)}, u32[]{:S(2)}) copy-start(s32[2]{0:T(128)} %constant.97.clone) | copy-start | bytes 28
  25.9 1.2 copy-start.9
  27.1 0.8 copy-start.18
  41.9 0.8 copy-start.16
  52.4 4.3 %copy-start.13 = (bf16[512,2048]{1,0:T(8,128)(2,1)}, bf16[512,2048]{1,0:T(8,128)(2,1)S(1)}, u32[]{:S(2)}) copy-start(bf16[512,2048]{1,0:T(8,128)(2,1)S(1)} %collective-permute-done.refs_1_) | copy-start | bytes 6291460
  56.7 25.8 %collective-permute-start.8 = (bf16[512,2048]{1,0:T(8,128)(2,1)}, bf16[512,2048]{1,0:T(8,128)(2,1)S(1)}, u32[]{:S(2)}, u32[]{:S(2)}) collective-permute-start(bf16[512,2048]{1,0:T(8,128)(2,1)} %copy-done.13), channel_id=1, source_target_pairs={{4,8},{8,12},{5,9},{9,13},{6,10},{10,14},{7,11},{11,15},{20,24},{2... | collective-permute-start | bytes 6291464 | tf_op jit(solution)/shard_map/ppermute | solution.py:384
  57.5 50.8 %collective-permute-start.9 = (bf16[512,2048]{1,0:T(8,128)(2,1)}, bf16[512,2048]{1,0:T(8,128)(2,1)}, u32[]{:S(2)}, u32[]{:S(2)}) collective-permute-start(bf16[512,2048]{1,0:T(8,128)(2,1)} %collective-permute-done.1.refs_2_), channel_id=1, source_target_pairs={{4,0},{8,4},{5,1},{9,5},{6,2},{10,6},{7,3},{11,7},{20,16},{24,20},... | collective-permute-start | bytes 6291464 | tf_op jit(solution)/shard_map/ppermute | solution.py:385
  61.9 1.6 copy-start.11
  63.5 1.6 copy-start.14
  65.1 50.1 %copy-start.22 = (s32[1,6]{1,0:T(1,128)S(1)}, s32[1,6]{1,0:T(1,128)}, u32[]{:S(2)}) copy-start(s32[1,6]{1,0:T(1,128)} %param.15) | copy-start | bytes 76
  65.1 50.8 %copy-start.20 = (s32[512]{0:T(512)S(1)}, s32[512]{0:T(512)}, u32[]{:S(2)}) copy-start(s32[512]{0:T(512)} %param.16) | copy-start | bytes 6148
  82.5 45.1 %copy-start.8 = (bf16[512,2048]{1,0:T(8,128)(2,1)}, bf16[512,2048]{1,0:T(8,128)(2,1)S(1)}, u32[]{:S(2)}) copy-start(bf16[512,2048]{1,0:T(8,128)(2,1)S(1)} %collective-permute-done.8.refs_0_.refs_3_) | copy-start | bytes 6291460
  108.3 99.9 %collective-permute-start.13 = (bf16[512,2048]{1,0:T(8,128)(2,1)S(1)}, bf16[512,2048]{1,0:T(8,128)(2,1)}, u32[]{:S(2)}, u32[]{:S(2)}) collective-permute-start(bf16[512,2048]{1,0:T(8,128)(2,1)S(1)} %collective-permute-done.8.refs_0_.refs_3_), channel_id=1, source_target_pairs={{8,12},{9,13},{10,14},{11,15},{24,28},{25,29},{26,30},{27,31}} | collective-permute-start | bytes 6291464 | tf_op jit(solution)/shard_map/ppermute | solution.py:390
  110.3 97.9 %collective-permute-start.14 = (bf16[512,2048]{1,0:T(8,128)(2,1)}, bf16[512,2048]{1,0:T(8,128)(2,1)}, u32[]{:S(2)}, u32[]{:S(2)}) collective-permute-start(bf16[512,2048]{1,0:T(8,128)(2,1)} %collective-permute-done.9.refs_1_.refs_4_), channel_id=1, source_target_pairs={{4,0},{5,1},{6,2},{7,3},{20,16},{21,17},{22,18},{23,19}} | collective-permute-start | bytes 6291464 | tf_op jit(solution)/shard_map/ppermute | solution.py:391
  112.5 37.6 %collective-permute-start.11 = (bf16[3,128,2048]{2,1,0:T(8,128)(2,1)}, bf16[3,128,2048]{2,1,0:T(8,128)(2,1)}, u32[]{:S(2)}, u32[]{:S(2)}) collective-permute-start(bf16[3,128,2048]{2,1,0:T(8,128)(2,1)} %get-tuple-element.50), channel_id=1, source_target_pairs={{0,2},{1,3},{2,0},{3,1},{4,6},{5,7},{6,4},{7,5},{8,10},{9,11},{10,... | collective-permute-start | bytes 4718600 | tf_op jit(solution)/shard_map/ppermute | solution.py:378
  114.0 65.8 %collective-permute-start.12 = (bf16[3,128,2048]{2,1,0:T(8,128)(2,1)}, bf16[3,128,2048]{2,1,0:T(8,128)(2,1)}, u32[]{:S(2)}, u32[]{:S(2)}) collective-permute-start(bf16[3,128,2048]{2,1,0:T(8,128)(2,1)} %get-tuple-element.51), channel_id=1, source_target_pairs={{0,3},{1,2},{2,1},{3,0},{4,7},{5,6},{6,5},{7,4},{8,11},{9,10},{10,... | collective-permute-start | bytes 4718600 | tf_op jit(solution)/shard_map/ppermute | solution.py:378
  114.0 65.8 %collective-permute-start.10 = (bf16[3,128,2048]{2,1,0:T(8,128)(2,1)}, bf16[3,128,2048]{2,1,0:T(8,128)(2,1)}, u32[]{:S(2)}, u32[]{:S(2)}) collective-permute-start(bf16[3,128,2048]{2,1,0:T(8,128)(2,1)} %get-tuple-element.49), channel_id=1, source_target_pairs={{0,1},{1,0},{2,3},{3,2},{4,5},{5,4},{6,7},{7,6},{8,9},{9,8},{10,11... | collective-permute-start | bytes 4718600 | tf_op jit(solution)/shard_map/ppermute | solution.py:378
  116.0 63.8 %copy-start.10 = (bf16[3,128,2048]{2,1,0:T(8,128)(2,1)S(1)}, bf16[3,128,2048]{2,1,0:T(8,128)(2,1)}, u32[]{:S(2)}) copy-start(bf16[3,128,2048]{2,1,0:T(8,128)(2,1)} %copy-done.9) | copy-start | bytes 4718596
  179.7 5.0 %copy-start.17 = (bf16[1,128,2048]{2,1,0:T(8,128)(2,1)S(1)}, bf16[1,128,2048]{2,1,0:T(8,128)(2,1)}, u32[]{:S(2)}) copy-start(bf16[1,128,2048]{2,1,0:T(8,128)(2,1)} %copy-done.16) | copy-start | bytes 1572868
  179.7 5.0 %copy-start.19 = (bf16[1,128,2048]{2,1,0:T(8,128)(2,1)S(1)}, bf16[1,128,2048]{2,1,0:T(8,128)(2,1)}, u32[]{:S(2)}) copy-start(bf16[1,128,2048]{2,1,0:T(8,128)(2,1)} %copy-done.18) | copy-start | bytes 1572868
  184.7 5.0 %copy-start.12 = (bf16[512,2048]{1,0:T(8,128)(2,1)S(1)}, bf16[512,2048]{1,0:T(8,128)(2,1)}, u32[]{:S(2)}) copy-start(bf16[512,2048]{1,0:T(8,128)(2,1)} %refs_0_.3) | copy-start | bytes 6291460
  184.7 5.0 %copy-start.15 = (bf16[512,2048]{1,0:T(8,128)(2,1)S(1)}, bf16[512,2048]{1,0:T(8,128)(2,1)}, u32[]{:S(2)}) copy-start(bf16[512,2048]{1,0:T(8,128)(2,1)} %copy-done.13) | copy-start | bytes 6291460
  199.3 2.2 copy-start.2
  201.5 2.2 copy-start.6
  203.7 2.2 copy-start.7
  210.7 9.8 %collective-permute-start.15 = (bf16[512,32]{1,0:T(8,128)(2,1)S(1)}, bf16[512,32]{1,0:T(8,128)(2,1)S(1)}, u32[]{:S(2)}, u32[]{:S(2)}) collective-permute-start(bf16[512,32]{1,0:T(8,128)(2,1)S(1)} %get-tuple-element.74.refs_0_), channel_id=1, source_target_pairs={{0,12},{4,0},{8,4},{12,8},{1,13},{5,1},{9,5},{13,9},{2,14},{6,2},{... | collective-permute-start | bytes 98312 | tf_op jit(solution)/shard_map/ppermute | solution.py:410
  210.8 17.3 %collective-permute-start.16 = (bf16[512,32]{1,0:T(8,128)(2,1)S(1)}, bf16[512,32]{1,0:T(8,128)(2,1)S(1)}, u32[]{:S(2)}, u32[]{:S(2)}) collective-permute-start(bf16[512,32]{1,0:T(8,128)(2,1)S(1)} %get-tuple-element.74.refs_0_), channel_id=1, source_target_pairs={{0,8},{4,12},{8,0},{12,4},{1,9},{5,13},{9,1},{13,5},{2,10},{6,14},... | collective-permute-start | bytes 98312 | tf_op jit(solution)/shard_map/ppermute | solution.py:410
  215.5 12.6 %collective-permute-start.17 = (bf16[512,32]{1,0:T(8,128)(2,1)S(1)}, bf16[512,32]{1,0:T(8,128)(2,1)S(1)}, u32[]{:S(2)}, u32[]{:S(2)}) collective-permute-start(bf16[512,32]{1,0:T(8,128)(2,1)S(1)} %get-tuple-element.74.refs_0_), channel_id=1, source_target_pairs={{0,4},{4,8},{8,12},{12,0},{1,5},{5,9},{9,13},{13,1},{2,6},{6,10},{... | collective-permute-start | bytes 98312 | tf_op jit(solution)/shard_map/ppermute | solution.py:410
  228.1 4.6 %copy-start.1 = (s32[16]{0:T(128)S(1)}, s32[16]{0:T(128)}, u32[]{:S(2)}) copy-start(s32[16]{0:T(128)} %param.17) | copy-start | bytes 196

commit v10 on v8

v10 whole, which is shorter than its diff:
```python
import functools

import jax
import jax.numpy as jnp
from jax import lax
from jax.experimental import pallas as pl
from jax.experimental.pallas import tpu as pltpu
from jax.sharding import PartitionSpec as P

PARAMS = pltpu.CompilerParams(vmem_limit_bytes=48 * 2**20)
TAIL_PARAMS = pltpu.CompilerParams(vmem_limit_bytes=24 * 2**20)
F32 = jnp.float32
BF16 = jnp.bfloat16


def start_pages(places, blocks, length, targets, sems, rows_of):
    for e, target in enumerate(targets):
        for j, block in enumerate(blocks):

            @pl.when(places[e] // length == j)
            def _():
                pltpu.make_async_copy(rows_of(block.at[lax.rem(places[e], length)]), target, sems[e]).start()


def join_downs_kernel(places, *refs):
    *blocks, out, held, sems = refs
    length, rank_part, _ = blocks[0].shape
    shards, slots, width = held.shape
    step = pl.program_id(0)

    def targets(t):
        return [held.at[t, pl.ds(e * rank_part, rank_part)] for e in range(slots // rank_part)]

    @pl.when(step == 0)
    def _():
        for t in range(shards):
            semaphores = [sems.at[t, e] for e in range(slots // rank_part)]
            start_pages(
                places, blocks, length, targets(t), semaphores, lambda page: page.at[:, pl.ds(t * width, width)]
            )

    for t in range(shards):

        @pl.when(step == t)
        def _():
            for e, target in enumerate(targets(t)):
                source = blocks[0].at[0, :, pl.ds(t * width, width)]
                pltpu.make_async_copy(source, target, sems.at[t, e]).wait()
            out[...] = held[t].T


def join_downs(places, blocks, shards):
    entries = places.shape[0]
    _, rank_part, features = blocks[0].shape
    width, slots = features // shards, entries * rank_part
    return pl.pallas_call(
        join_downs_kernel,
        out_shape=jax.ShapeDtypeStruct((features, slots), BF16),
        grid=(shards,),
        in_specs=[pl.BlockSpec(memory_space=pltpu.SMEM)] + [pl.BlockSpec(memory_space=pltpu.HBM)] * len(blocks),
        out_specs=pl.BlockSpec((width, slots), lambda t: (t, 0)),
        scratch_shapes=[pltpu.VMEM((shards, slots, width), BF16), pltpu.SemaphoreType.DMA((shards, entries))],
        compiler_params=TAIL_PARAMS,
        cost_estimate=pl.CostEstimate(flops=0, bytes_accessed=4 * features * slots, transcendentals=0),
    )(places, *blocks)


RESIDENT = pl.BlockSpec(memory_space=pltpu.VMEM)
IN_HBM = pl.BlockSpec(memory_space=pltpu.HBM)


def chunk_kernel(held, with_base, with_low, start, valid, *refs):
    refs = list(refs)
    xs = [refs.pop(0) for _ in range(valid.shape[0])]
    weight = refs.pop(0) if with_base else None
    down = refs.pop(0) if with_low else None
    outs = [refs.pop() for _ in range(with_base + with_low)][::-1]
    step = pl.program_id(0)

    @pl.when(step == 0)
    def _():
        for i, out in enumerate(outs):
            out[...] = refs[i][...] if held else jnp.zeros_like(out)

    for i, x in enumerate(xs):

        @pl.when((step == i) & (valid[step] != 0))
        def _():
            if with_base:
                base = outs[0]
                part = min(base.shape[1], 512)
                for n in range(0, base.shape[1], part):
                    base[:, n:n + part] += jnp.dot(x[...], weight[:, n:n + part], preferred_element_type=F32)
            if with_low:
                outs[-1][...] += jnp.dot(x[...], down[...], preferred_element_type=F32)


def add_chunk(totals, xs, source, half, weight, down):
    rows, width = xs[0].shape
    walked = [a for a in (weight, down) if a is not None]
    n_tensor = walked[0].shape[0] // (2 * width)
    steps = len(xs)
    there = (source >= 0) & (source < n_tensor)
    start = 2 * jnp.clip(source, 0, n_tensor - 1) + jnp.array(half, jnp.int32)
    start = jnp.where(there, start, jnp.concatenate([start[1:2], start[:-1]])).astype(jnp.int32)
    valid = there.astype(jnp.int32)
    whole = [pl.BlockSpec((rows, a.shape[1]), lambda s, *_: (0, 0)) for a in walked]
    columns = sum(a.shape[1] for a in walked)
    return pl.pallas_call(
        functools.partial(chunk_kernel, bool(totals), weight is not None, down is not None),
        out_shape=[jax.ShapeDtypeStruct((rows, a.shape[1]), F32) for a in walked],
        grid_spec=pltpu.PrefetchScalarGridSpec(
            num_scalar_prefetch=2,
            grid=(steps,),
            in_specs=[pl.BlockSpec((rows, width), lambda s, *_: (0, 0))] * steps
            + [pl.BlockSpec((width, a.shape[1]), lambda s, start, valid: (start[s], 0)) for a in walked]
            + (whole if totals else []),
            out_specs=whole,
        ),
        compiler_params=PARAMS,
        cost_estimate=pl.CostEstimate(
            flops=2 * steps * width * rows * columns,
            bytes_accessed=2 * steps * width * (rows + columns) + 8 * rows * columns,
            transcendentals=0,
        ),
    )(start, valid, *xs, *walked, *totals)


def pin_kernel(start, places, weight, down, base, low, *refs):
    *blocks, weight_out, down_out, base_out, low_out, up_out, sems = refs
    width = weight_out.shape[0]
    length, rank, _ = blocks[0].shape
    rows = pl.ds(pl.multiple_of(start[0] * width, width), width)
    pairs = [(weight.at[rows], weight_out), (down.at[rows], down_out), (base, base_out), (low, low_out)]
    copies = [pltpu.make_async_copy(a, b, sems.at[i]) for i, (a, b) in enumerate(pairs)]
    pages = [up_out.at[pl.ds(e * rank, rank)] for e in range(up_out.shape[0] // rank)]
    for copy in copies:
        copy.start()
    page_sems = [sems.at[len(copies) + e] for e in range(len(pages))]
    start_pages(places, blocks, length, pages, page_sems, lambda page: page)
    for copy in copies:
        copy.wait()
    for page, sem in zip(pages, page_sems):
        pltpu.make_async_copy(blocks[0].at[0], page, sem).wait()


def pin(start, places, width, weight, down, base, low, blocks):
    entries = places.shape[0]
    rank, columns = blocks[0].shape[1:]
    shapes = [((width, a.shape[1]), BF16) for a in (weight, down)] + [(a.shape, a.dtype) for a in (base, low)]
    shapes += [((entries * rank, columns), BF16)]
    return pl.pallas_call(
        pin_kernel,
        out_shape=[pltpu.VMEM(*a) for a in shapes],
        in_specs=[pl.BlockSpec(memory_space=pltpu.SMEM)] * 2 + [IN_HBM] * (4 + len(blocks)),
        out_specs=[RESIDENT] * 5,
        scratch_shapes=[pltpu.SemaphoreType.DMA((4 + entries,))],
        compiler_params=TAIL_PARAMS,
        cost_estimate=pl.CostEstimate(
            flops=0, bytes_accessed=sum(a[0] * a[1] for a, _ in shapes) * 3, transcendentals=0
        ),
    )(start, places, weight, down, base, low, *blocks)


def low_kernel(rank_part, which, from_left, from_right, down, total, slot, live, out, x, sem):
    @pl.when(which[0] > 0)
    def _():
        pltpu.make_async_copy(from_left, x, sem).start()

    @pl.when(which[0] < 0)
    def _():
        pltpu.make_async_copy(from_right, x, sem).start()

    @pl.when(which[0] != 0)
    def _():
        pltpu.make_async_copy(from_left, x, sem).wait()

    @pl.when(which[0] == 0)
    def _():
        x[...] = jnp.zeros_like(x)

    low = total[...] + jnp.dot(x[...], down[...], preferred_element_type=F32)
    lane = lax.broadcasted_iota(jnp.int32, low.shape, 1)
    own = jnp.where(lane // rank_part == slot[...], low, 0.0).astype(BF16)
    fold = (
        lax.rem(lax.broadcasted_iota(jnp.int32, (low.shape[1], rank_part), 0), rank_part)
        == lax.broadcasted_iota(jnp.int32, (low.shape[1], rank_part), 1)
    ).astype(BF16)
    mine = jnp.dot(own, fold, preferred_element_type=F32)
    k = lax.broadcasted_iota(jnp.int32, mine.shape, 1)
    out[...] = jnp.where(k < live[...], mine, 0.0).astype(BF16)


def finish_low(which, from_left, from_right, down, total, slot, live, rank_part):
    rows, width = from_left.shape
    slots = down.shape[1]
    return pl.pallas_call(
        functools.partial(low_kernel, rank_part),
        out_shape=[pltpu.VMEM((rows, rank_part), BF16), pltpu.VMEM((rows, width), BF16)],
        in_specs=[pl.BlockSpec(memory_space=pltpu.SMEM), IN_HBM, IN_HBM] + [RESIDENT] * 4,
        out_specs=[RESIDENT] * 2,
        scratch_shapes=[pltpu.SemaphoreType.DMA],
        compiler_params=TAIL_PARAMS,
        cost_estimate=pl.CostEstimate(
            flops=2 * width * rows * slots, bytes_accessed=2 * width * rows, transcendentals=0
        ),
    )(which, from_left, from_right, down, total, slot, live)


def base_kernel(which, x, weight, total, out):
    @pl.when(which[0] != 0)
    def _():
        part = min(out.shape[1], 512)
        for n in range(0, out.shape[1], part):
            cut = slice(n, n + part)
            out[:, cut] = total[:, cut] + jnp.dot(x[...], weight[:, cut], preferred_element_type=F32)


def add_last(which, x, weight, total):
    rows, width = x.shape
    columns = weight.shape[1]
    return pl.pallas_call(
        base_kernel,
        out_shape=pltpu.VMEM((rows, columns), F32),
        in_specs=[pl.BlockSpec(memory_space=pltpu.SMEM)] + [RESIDENT] * 3,
        out_specs=RESIDENT,
        input_output_aliases={3: 0},
        compiler_params=TAIL_PARAMS,
        cost_estimate=pl.CostEstimate(flops=2 * width * rows * columns, bytes_accessed=0, transcendentals=0),
    )(which, x, weight, total)


def finish_kernel(parts, me, slot, total, up, *refs):
    lows, (out, spread) = refs[:parts], refs[parts:]
    rank_part = lows[0].shape[1]
    rank = parts * rank_part
    part = out.shape[1]

    @pl.when(pl.program_id(0) == 0)
    def _():
        low = jnp.concatenate([part[...].astype(F32) for part in lows], axis=1)
        low = pltpu.roll(low, me[0] * rank_part, 1)
        for e in range(spread.shape[1] // rank):
            spread[:, e * rank:(e + 1) * rank] = jnp.where(slot[...] == e, low, 0.0).astype(BF16)

    cut = pl.ds(pl.multiple_of(pl.program_id(0) * part, part), part)
    out[...] = (total[:, cut] + jnp.dot(spread[...], up[:, cut], preferred_element_type=F32)).astype(BF16)


def finish(me, slot, total, up, lows):
    rows, columns = total.shape
    depth = up.shape[0]
    part = min(columns, 512)
    return pl.pallas_call(
        functools.partial(finish_kernel, len(lows)),
        grid=(columns // part,),
        out_shape=jax.ShapeDtypeStruct((rows, columns), BF16),
        in_specs=[pl.BlockSpec(memory_space=pltpu.SMEM)] + [RESIDENT] * (3 + len(lows)),
        out_specs=pl.BlockSpec((rows, part), lambda n: (0, n)),
        scratch_shapes=[pltpu.VMEM((rows, depth), BF16)],
        compiler_params=TAIL_PARAMS,
        cost_estimate=pl.CostEstimate(
            flops=2 * rows * depth * columns,
            bytes_accessed=2 * rows * columns,
            transcendentals=0,
        ),
    )(me, slot, total, up, *lows)


def after(value, *earlier):
    return lax.optimization_barrier((value,) + earlier)[0]


def looked_up(table, ids):
    hit = ids[:, None] == jnp.arange(table.shape[0])[None, :]
    return jnp.sum(jnp.where(hit, table[None, :], 0), axis=1)


def local(
    attention_result,
    output_weight,
    adapter_down_weight,
    adapter_up_weight,
    adapter_page_row,
    requests,
    row_request_entry,
    ranks,
):
    n_dp = lax.axis_size("dp")
    n_tensor = lax.axis_size("tensor")
    me = lax.axis_index("tensor")
    rows, width = attention_result.shape
    holder_length, rank_part, _ = adapter_down_weight.shape
    rank, columns = adapter_up_weight.shape[1:]
    own_list = requests[0]
    entries = own_list.shape[0]
    one_hot = row_request_entry[:, None] == jnp.arange(entries)[None, :]
    row_rank = jnp.sum(jnp.where(one_hot, looked_up(ranks, own_list)[None, :], 0), axis=1)
    pages = looked_up(adapter_page_row, own_list)
    apart = (pages // holder_length) ^ lax.axis_index("dp")
    places = apart * holder_length + pages % holder_length
    if n_tensor != 4 or n_dp != 4 or width % 256 or rank_part % 16 or entries * rank_part > 256:
        return plain(
            attention_result, output_weight, adapter_down_weight, adapter_up_weight, places, one_hot, row_rank
        )

    places = (apart % 2 * 2 + apart // 2) * holder_length + pages % holder_length

    def across(x, distance):
        return lax.ppermute(x, "dp", [(i, i ^ distance) for i in range(n_dp)])

    right = [(i, i + 1) for i in range(n_tensor - 1)]
    left = [(i + 1, i) for i in range(n_tensor - 1)]

    def onward(from_left, from_right, step):
        return (
            lax.ppermute(from_left, "tensor", right[step:]),
            lax.ppermute(from_right, "tensor", left[:len(left) - step]),
        )

    first = attention_result[:, :width // 2]
    second = after(attention_result, first)[:, width // 2:]
    first_1 = onward(first, first, 0)
    second_1 = onward(second, second, 0)
    far_down = across(adapter_down_weight, 2)
    far_up = across(after(adapter_up_weight, far_down), 2)

    first_2 = onward(*first_1, 1)
    second_1 = lax.optimization_barrier((*first_1, *second_1))[2:]
    second_2 = onward(*second_1, 1)
    downs = jnp.concatenate([adapter_down_weight, after(far_down, *second_1)], axis=0)
    downs = (downs, across(downs, 1))
    near = me + jnp.array([0, 0, -1, 1, -1, 1], jnp.int32)
    far = me + jnp.array([-2, 2, -2, 2], jnp.int32)
    last = me + jnp.array([-3, 3], jnp.int32)
    near_xs = [first, second, *first_1, *second_1]
    far_xs = [*first_2, *second_2]
    near_half, far_half = (0, 1, 0, 0, 1, 1), (0, 0, 1, 1)
    base, = add_chunk((), near_xs, near, near_half, output_weight, None)
    first_2 = lax.optimization_barrier((base, *first_2))[1:]
    first_3 = onward(*first_2, 2)
    second_2 = lax.optimization_barrier((*first_2, *second_2))[2:]
    second_3 = onward(*second_2, 2)
    ups = jnp.concatenate([adapter_up_weight, after(far_up, *second_2)], axis=0)
    ups = (ups, across(ups, 1))

    base, = add_chunk((base,), far_xs, far, far_half, output_weight, None)
    down = join_downs(places, after(downs, base), n_tensor)
    low, = add_chunk((), near_xs + far_xs, jnp.concatenate([near, far]), near_half + far_half, None, down)
    base, low = add_chunk((base, low), list(first_3), last, (0, 0), output_weight, down)

    which = jnp.where(me == n_tensor - 1, 1, jnp.where(me == 0, -1, 0)).astype(jnp.int32)[None]
    start = jnp.where(me == 0, 2 * n_tensor - 1, 1).astype(jnp.int32)[None]
    slot = row_request_entry[:, None]
    live = row_rank[:, None] - me * rank_part
    start, which, slot, live = lax.optimization_barrier((start, which, slot, live, low))[:4]
    pinned = pin(start, places, width // 2, output_weight, down, base, low, ups)
    weight, down, base, low, up, *second_3 = lax.optimization_barrier((*pinned, *second_3))
    low, x = finish_low(which, *second_3, down, low, slot, live, rank_part)
    base = add_last(which, x, weight, base)
    lows = [low] + [
        lax.ppermute(low, "tensor", [(i, (i - j) % n_tensor) for i in range(n_tensor)])
        for j in range(1, n_tensor)
    ]
    return finish(me[None], slot, base, up, lows)


def gather_pages(block, n_dp):
    return [block] + [
        lax.ppermute(block, "dp", [(i, i ^ j) for i in range(n_dp)]) for j in range(1, n_dp)
    ]


def plain(x, output_weight, down_weight, up_weight, places, one_hot, row_rank):
    n_dp = lax.axis_size("dp")
    rows = x.shape[0]
    rank, columns = up_weight.shape[1:]
    entries = one_hot.shape[1]

    def requested(block):
        blocks = jnp.concatenate(gather_pages(block, n_dp), axis=0)
        return jnp.concatenate(
            [lax.dynamic_slice_in_dim(blocks, places[e], 1, 0) for e in range(entries)], axis=0
        )

    down, up = requested(down_weight), requested(up_weight)
    x = lax.all_gather(x, "tensor", axis=1, tiled=True)
    base = jnp.dot(x, output_weight, preferred_element_type=F32)
    low = jnp.einsum("rd,ekd->rek", x, down, preferred_element_type=F32)
    low = jnp.sum(jnp.where(one_hot[:, :, None], low, 0.0), axis=1).astype(BF16)
    low = lax.all_gather(low, "tensor", axis=1, tiled=True)
    low = jnp.where(jnp.arange(rank)[None, :] < row_rank[:, None], low, jnp.zeros_like(low))
    spread = jnp.where(one_hot[:, :, None], low[:, None, :], jnp.zeros((), BF16))
    term = jnp.dot(
        spread.reshape(rows, entries * rank), up.reshape(entries * rank, columns), preferred_element_type=F32
    )
    return (base + term).astype(BF16)


def solution(mesh):
    in_specs = (
        P(("groups", "dp"), "tensor"),
        P(None, "tensor"),
        P("dp", "tensor", None),
        P("dp", None, "tensor"),
        P("groups"),
        P(("groups", "dp"), None),
        P(("groups", "dp")),
        P(),
    )
    out_specs = P(("groups", "dp"), "tensor")
    return jax.shard_map(local, mesh=mesh, in_specs=in_specs, out_specs=out_specs, check_vma=False)
```

time: 200 us -> 193 us (0.965)
  waiting for transfers between devices: 69.9 us -> 63.1 us
  starting transfers between devices: 25.5 us -> 30.6 us
  Pallas kernels: 74.8 us -> 70.8 us
    ppermute x15 -> x16, waiting for transfers between devices: 65.7 us -> 54.9 us  [the longest x6 32.4 us: onward(): lax.ppermute(from_right, 'tensor', left[:len(left) - step])]
    unnamed x50 -> x54, local copies, waits for them, and re-layouts: 22.5 us -> 13.5 us
    slice x0 -> x6, local copies, waits for them, and re-layouts: none -> 4.98 us  [the longest x4 2.39 us: add_chunk(): start[1:2]]
    concatenate x0 -> x2, local copies, waits for them, and re-layouts: none -> 4.73 us  [the longest x1 3.18 us: local(): jnp.concatenate([adapter_down_weight, after(far_down, *second_1)], axis=0)]
    ppermute x15 -> x16, starting transfers between devices: 22 us -> 26.3 us  [the longest x6 14.8 us: onward(): lax.ppermute(from_left, 'tensor', right[step:])]
    ppermute x3, waiting for transfers between devices: 4.14 us -> 8.19 us  [local(): lax.ppermute(low, 'tensor', [(i, (i - j) % n_tensor) for i in range(n_ten...]
    pallas_call x1, Pallas kernels: 4.89 us -> 2.73 us  [add_last(): pl.pallas_call(base_kernel, out_shape=pltpu.VMEM((rows, columns), F32), i...]
    pallas_call x9 -> x5, Pallas kernels: 58.1 us -> 58.4 us  [the longest x4 54.8 us: add_chunk(): pl.pallas_call(functools.partial(chunk_kernel, bool(totals), weight is no...]
  transfers between devices with their start and end apart: 18 -> 19, of which waited for: 5 -> 6; matrix products, arithmetic and copies ran while one was open for 3% -> 10% of each run, Pallas kernels for 34% -> 34%
where the time goes in v10:
time: 193 us; the launch traced here: 192 us
  Pallas kernels  70.8 us (37%)
  waiting for transfers between devices  63.1 us (33%)
  starting transfers between devices  30.6 us (16%)
  local copies, waits for them, and re-layouts  23.5 us (12%)
  other arithmetic  3.89 us (2%)
    pallas_call x4, Pallas kernels, add_chunk(): pl.pallas_call(functools.partial(chunk_kernel, bool(totals), weight is no...  54.8 us
    ppermute x6, waiting for transfers between devices, onward(): lax.ppermute(from_right, 'tensor', left[:len(left) - step])  32.4 us
    ppermute x6, waiting for transfers between devices, onward(): lax.ppermute(from_left, 'tensor', right[step:])  22.5 us
    ppermute x6, starting transfers between devices, onward(): lax.ppermute(from_left, 'tensor', right[step:])  14.8 us
    unnamed x54, local copies, waits for them, and re-layouts  13.5 us
    ppermute x3, waiting for transfers between devices, local(): lax.ppermute(low, 'tensor', [(i, (i - j) % n_tensor) for i in range(n_ten...  8.19 us
    ppermute x6, starting transfers between devices, onward(): lax.ppermute(from_right, 'tensor', left[:len(left) - step])  7.89 us
    ppermute x3, starting transfers between devices, local(): lax.ppermute(low, 'tensor', [(i, (i - j) % n_tensor) for i in range(n_ten...  4.32 us
  transfers between devices with their start and end apart: 19, of which 6 were waited for; matrix products, arithmetic and copies ran while one was open for 10% of the time, Pallas kernels for 34%

profile of v10, /device:TPU:0, one launch (start us, length us, event | category | flops | bytes accessed | tf_op | source)
XLA Modules:
  0.0 192.4 jit_solution(18409206820355625640)
XLA Ops:
  0.0 2.9 %collective-permute-start.8 = (bf16[4,32,8192]{2,1,0:T(8,128)(2,1)}, bf16[4,32,8192]{2,1,0:T(8,128)(2,1)}, u32[]{:S(2)}, u32[]{:S(2)}) collective-permute-start(bf16[4,32,8192]{2,1,0:T(8,128)(2,1)} %param.17), channel_id=1, source_target_pairs={{0,2},{1,3},{2,0},{3,1},{4,6},{5,7},{6,4},{7,5},{8,10},{9,11},{10,... | collective-permute-start | bytes 6291464 | tf_op jit(solution)/shard_map/ppermute | solution.py:310
  2.9 1.3 slice.34.refs_0_
  4.2 4.5 %collective-permute-start = (bf16[512,1024]{1,0:T(8,128)(2,1)S(1)}, bf16[512,1024]{1,0:T(8,128)(2,1)}, u32[]{:S(2)}, u32[]{:S(2)}) collective-permute-start(bf16[512,1024]{1,0:T(8,128)(2,1)S(1)} %slice.34.refs_0_), channel_id=1, source_target_pairs={{0,4},{4,8},{8,12},{1,5},{5,9},{9,13},{2,6},{6,10},{10,14},{3,7},{... | collective-permute-start | bytes 3145736 | tf_op jit(solution)/shard_map/ppermute | solution.py:317
  8.7 1.3 collective-permute-start.1
  10.0 1.3 slice.35.refs_1_
  11.3 5.5 %collective-permute-start.2 = (bf16[512,1024]{1,0:T(8,128)(2,1)S(1)}, bf16[512,1024]{1,0:T(8,128)(2,1)}, u32[]{:S(2)}, u32[]{:S(2)}) collective-permute-start(bf16[512,1024]{1,0:T(8,128)(2,1)S(1)} %slice.35.refs_1_), channel_id=1, source_target_pairs={{0,4},{4,8},{8,12},{1,5},{5,9},{9,13},{2,6},{6,10},{10,14},{3,7},{... | collective-permute-start | bytes 3145736 | tf_op jit(solution)/shard_map/ppermute | solution.py:317
  16.8 1.3 collective-permute-start.3
  18.8 3.3 %constant_dynamic-update-slice_fusion.3 = bf16[8,128,2048]{2,1,0:T(8,128)(2,1)} fusion(bf16[4,128,2048]{2,1,0:T(8,128)(2,1)} %param.18), kind=kLoop, calls=%fused_computation.5 | loop fusion | bytes 4194304
  22.1 0.7 broadcast_add_fusion.1
  22.8 1.5 constant_dynamic-update-slice_fusion.1
  24.4 7.0 %collective-permute-done.refs_2_ = bf16[512,1024]{1,0:T(8,128)(2,1)} collective-permute-done((bf16[512,1024]{1,0:T(8,128)(2,1)S(1)}, bf16[512,1024]{1,0:T(8,128)(2,1)}, u32[]{:S(2)}, u32[]{:S(2)}) %collective-permute-start) | collective-permute-done | bytes 1048608 | tf_op jit(solution)/shard_map/ppermute | solution.py:317
  31.3 0.8 collective-permute-start.4
  32.2 4.6 %collective-permute-done.1.refs_3_ = bf16[512,1024]{1,0:T(8,128)(2,1)} collective-permute-done((bf16[512,1024]{1,0:T(8,128)(2,1)S(1)}, bf16[512,1024]{1,0:T(8,128)(2,1)}, u32[]{:S(2)}, u32[]{:S(2)}) %collective-permute-start.1) | collective-permute-done | bytes 1048608 | tf_op jit(solution)/shard_map/ppermute | solution.py:318
  36.8 15.5 %collective-permute-done.2.refs_4_ = bf16[512,1024]{1,0:T(8,128)(2,1)} collective-permute-done((bf16[512,1024]{1,0:T(8,128)(2,1)S(1)}, bf16[512,1024]{1,0:T(8,128)(2,1)}, u32[]{:S(2)}, u32[]{:S(2)}) %collective-permute-start.2) | collective-permute-done | bytes 1048608 | tf_op jit(solution)/shard_map/ppermute | solution.py:317
  52.3 5.2 %collective-permute-done.3.refs_5_ = bf16[512,1024]{1,0:T(8,128)(2,1)} collective-permute-done((bf16[512,1024]{1,0:T(8,128)(2,1)S(1)}, bf16[512,1024]{1,0:T(8,128)(2,1)}, u32[]{:S(2)}, u32[]{:S(2)}) %collective-permute-start.3) | collective-permute-done | bytes 1048608 | tf_op jit(solution)/shard_map/ppermute | solution.py:318
  57.5 0.7 collective-permute-start.10
  58.2 1.3 collective-permute-start.11
  59.5 1.3 collective-permute-start.5
  60.9 0.6 collective-permute-start.12
  61.5 3.2 %constant_dynamic-update-slice_fusion.refs_0_ = bf16[8,32,8192]{2,1,0:T(8,128)(2,1)} fusion(bf16[8,32,8192]{2,1,0:T(8,128)(2,1)} %constant_dynamic-update-slice_fusion.1, bf16[4,32,8192]{2,1,0:T(8,128)(2,1)} %collective-permute-done.8), kind=kLoop, calls=%fused_computation.2 | loop fusion | bytes 4194304 | tf_op jit(solution)/shard_map/concatenate | solution.py:331
  64.7 20.3 %shard_map.145.refs_5_ = f32[512,2048]{1,0:T(8,128)} custom-call(s32[6]{0:T(128)S(1)} %get-tuple-element.72.start, s32[6]{0:T(128)S(1)} %fusion.5.valid, bf16[512,1024]{1,0:T(8,128)(2,1)S(1)} %copy-done.9, bf16[512,1024]{1,0:T(8,128)(2,1)S(1)} %copy-done.12, bf16[512,1024]{1,0:T(8,128)(2,1)} %collective-permute-done.refs_2_, ...), custom_call_target="tpu_custom_call" | custom-call | flops 12884901888 | bytes 39845888 | tf_op jit(solution)/shard_map/pallas_call | solution.py:109
  85.0 22.6 %collective-permute-done.5.refs_1_.refs_7_ = bf16[512,1024]{1,0:T(8,128)(2,1)S(1)} collective-permute-done((bf16[512,1024]{1,0:T(8,128)(2,1)}, bf16[512,1024]{1,0:T(8,128)(2,1)S(1)}, u32[]{:S(2)}, u32[]{:S(2)}) %collective-permute-start.5) | collective-permute-done | bytes 1048608 | tf_op jit(solution)/shard_map/ppermute | solution.py:318
  107.7 1.0 copy-done.6
  108.6 1.6 constant_dynamic-update-slice_fusion.2.refs_0_
  110.2 0.6 slice.36
  110.8 0.7 broadcast_add_fusion
  111.6 0.6 slice.38
  113.1 1.3 add_select_fusion.start
  114.4 0.7 add_select_fusion.3.start
  115.1 1.6 collective-permute-start.6
  116.8 1.3 collective-permute-start.7
  118.1 1.6 collective-permute-start.14
  119.8 1.5 collective-permute-start.15
  121.2 1.2 copy-done.7
  122.5 13.2 %shard_map.146.refs_4_ = f32[512,2048]{1,0:T(8,128)} custom-call(s32[4]{0:T(128)S(1)} %get-tuple-element.74.start, s32[4]{0:T(128)S(1)} %fusion.6.valid, bf16[512,1024]{1,0:T(8,128)(2,1)S(1)} %collective-permute-done.4.refs_0_.refs_6_, bf16[512,1024]{1,0:T(8,128)(2,1)S(1)} %copy-done.7, bf16[512,1024]{1,0:T(8,128)(2,1)S(1)} %collective-permute-done.10.refs_2_.refs_8_, ...), custom_call_target="tpu_custom_call" | custom-call | flops 8589934592 | bytes 29360128 | tf_op jit(solution)/shard_map/pallas_call | solution.py:109
  135.7 3.6 %shard_map.147.refs_10_.refs_3_.down = bf16[8192,192]{1,0:T(8,128)(2,1)S(1)} custom-call(s32[6]{0:T(128)S(1)} %fusion.1.places, bf16[8,32,8192]{2,1,0:T(8,128)(2,1)} %constant_dynamic-update-slice_fusion.refs_0_, bf16[8,32,8192]{2,1,0:T(8,128)(2,1)} %collective-permute-done.9.refs_1_), custom_call_target="tpu_custom_call" | custom-call | bytes 6291456 | tf_op jit(solution)/shard_map/pallas_call | solution.py:56
  139.2 2.0 %copy-done = bf16[8192,192]{1,0:T(8,128)(2,1)} copy-done((bf16[8192,192]{1,0:T(8,128)(2,1)}, bf16[8192,192]{1,0:T(8,128)(2,1)S(1)}, u32[]{:S(2)}) %copy-start) | copy-done | bytes 3145752
  141.3 11.4 %shard_map.148.refs_5_ = f32[512,192]{1,0:T(8,128)S(1)} custom-call(s32[10]{0:T(128)S(1)} %add_select_fusion.3.start, s32[10]{0:T(128)S(1)} %fusion.7.valid, bf16[512,1024]{1,0:T(8,128)(2,1)S(1)} %copy-done.10, bf16[512,1024]{1,0:T(8,128)(2,1)S(1)} %copy-done.13, bf16[512,1024]{1,0:T(8,128)(2,1)} %collective-permute-done.refs_2_, ...), custom_call_target="tpu_custom_call" | custom-call | flops 2013265920 | bytes 15204352 | tf_op jit(solution)/shard_map/pallas_call | solution.py:109
  152.7 10.0 %shard_map.149 = (f32[512,2048]{1,0:T(8,128)}, f32[512,192]{1,0:T(8,128)S(1)}) custom-call(s32[2]{0:T(128)S(1)} %add_select_fusion.start, s32[2]{0:T(128)S(1)} %fusion.4.valid, bf16[512,1024]{1,0:T(8,128)(2,1)} %collective-permute-done.6.refs_0_, bf16[512,1024]{1,0:T(8,128)(2,1)} %collective-permute-done.7.refs_1_, bf16[8192,2048]{1,0:T(8,128)(2,1)} %weight.1, ...), custom_call_target="tpu_custom_call" | custom-call | flops 4697620480 | bytes 20447232 | tf_op jit(solution)/shard_map/pallas_call | solution.py:109
  163.0 2.2 %copy-done.1 = bf16[8192,192]{1,0:T(8,128)(2,1)S(1)} copy-done((bf16[8192,192]{1,0:T(8,128)(2,1)S(1)}, bf16[8192,192]{1,0:T(8,128)(2,1)}, u32[]{:S(2)}) %copy-start.1) | copy-done | bytes 3145752
  165.2 2.2 %copy-done.2 = f32[512,2048]{1,0:T(8,128)S(1)} copy-done((f32[512,2048]{1,0:T(8,128)S(1)}, f32[512,2048]{1,0:T(8,128)}, u32[]{:S(2)}) %copy-start.2) | copy-done | bytes 4194328
  167.4 3.8 %shard_map.150 = (bf16[1024,2048]{1,0:T(8,128)(2,1)S(1)}, bf16[1024,192]{1,0:T(8,128)(2,1)S(1)}, f32[512,2048]{1,0:T(8,128)S(1)}, f32[512,192]{1,0:T(8,128)S(1)}, bf16[768,2048]{1,0:T(8,128)(2,1)S(1)}) custom-call(s32[1]{0:T(128)} %bitcast.1.start, s32[6]{0:T(128)S(1)} %fusion.1.places, bf16[8192,2048]{1,0:T(8,128)(2,1)} %weight.1, ...), custom_call_target="tpu_custom_call" | custom-call | bytes 15040512 | tf_op jit(solution)/shard_map/pallas_call | solution.py:152
  171.2 1.9 shard_map.151
  173.2 3.0 %collective-permute-start.17 = (bf16[512,32]{1,0:T(8,128)(2,1)S(1)}, bf16[512,32]{1,0:T(8,128)(2,1)S(1)}, u32[]{:S(2)}, u32[]{:S(2)}) collective-permute-start(bf16[512,32]{1,0:T(8,128)(2,1)S(1)} %get-tuple-element.68.refs_0_), channel_id=1, source_target_pairs={{0,8},{4,12},{8,0},{12,4},{1,9},{5,13},{9,1},{13,5},{2,10},{6,14},... | collective-permute-start | bytes 98312 | tf_op jit(solution)/shard_map/ppermute | solution.py:362
  176.2 1.2 collective-permute-start.18
  177.4 2.7 %shard_map.152.total = f32[512,2048]{1,0:T(8,128)S(1)} custom-call(s32[1]{0:T(128)} %bitcast.2.which, bf16[512,1024]{1,0:T(8,128)(2,1)S(1)} %get-tuple-element.64.x, bf16[1024,2048]{1,0:T(8,128)(2,1)S(1)} %get-tuple-element.65.weight, f32[512,2048]{1,0:T(8,128)S(1)} %get-tuple-element.66.total), custom_call_target="tpu_custom_call", output_to_operand_aliasing={{}: (3, {})} | custom-call | flops 2147483648 | tf_op jit(solution)/shard_map/pallas_call | solution.py:222
  180.2 8.2 %collective-permute-done.17.refs_2_ = bf16[512,32]{1,0:T(8,128)(2,1)S(1)} collective-permute-done((bf16[512,32]{1,0:T(8,128)(2,1)S(1)}, bf16[512,32]{1,0:T(8,128)(2,1)S(1)}, u32[]{:S(2)}, u32[]{:S(2)}) %collective-permute-start.17) | collective-permute-done | bytes 32800 | tf_op jit(solution)/shard_map/ppermute | solution.py:362
  188.4 4.0 %shard_map.153 = bf16[512,2048]{1,0:T(8,128)(2,1)} custom-call(s32[1]{0:T(128)} %bitcast.me, s32[512,1]{1,0:T(8,128)S(1)} %copy.22.slot, f32[512,2048]{1,0:T(8,128)S(1)} %shard_map.152.total, bf16[768,2048]{1,0:T(8,128)(2,1)S(1)} %get-tuple-element.67.up, bf16[512,32]{1,0:T(8,128)(2,1)S(1)} %get-tuple-element.68.refs_0_, ...), custom_call_target="tpu_custom_call" | custom-call | flops 1610612736 | bytes 2097152 | tf_op jit(solution)/shard_map/pallas_call | solution.py:254
  (79 shorter events, 2.2 us)
Async XLA Ops:
  0.0 18.1 %copy-start.19 = (s32[6]{0:T(128)S(1)}, s32[6]{0:T(128)}, u32[]{:S(2)}) copy-start(s32[6]{0:T(128)} %constant.86.clone) | copy-start | bytes 76
  0.0 18.1 %copy-start.20 = (s32[6]{0:T(128)S(1)}, s32[6]{0:T(128)}, u32[]{:S(2)}) copy-start(s32[6]{0:T(128)} %constant.89.clone) | copy-start | bytes 76
  0.0 60.8 %collective-permute-start.8 = (bf16[4,32,8192]{2,1,0:T(8,128)(2,1)}, bf16[4,32,8192]{2,1,0:T(8,128)(2,1)}, u32[]{:S(2)}, u32[]{:S(2)}) collective-permute-start(bf16[4,32,8192]{2,1,0:T(8,128)(2,1)} %param.17), channel_id=1, source_target_pairs={{0,2},{1,3},{2,0},{3,1},{4,6},{5,7},{6,4},{7,5},{8,10},{9,11},{10,... | collective-permute-start | bytes 6291464 | tf_op jit(solution)/shard_map/ppermute | solution.py:310
  4.2 20.1 %copy-start.8 = (bf16[512,1024]{1,0:T(8,128)(2,1)}, bf16[512,1024]{1,0:T(8,128)(2,1)S(1)}, u32[]{:S(2)}) copy-start(bf16[512,1024]{1,0:T(8,128)(2,1)S(1)} %slice.34.refs_0_) | copy-start | bytes 3145732
  4.2 27.1 %collective-permute-start = (bf16[512,1024]{1,0:T(8,128)(2,1)S(1)}, bf16[512,1024]{1,0:T(8,128)(2,1)}, u32[]{:S(2)}, u32[]{:S(2)}) collective-permute-start(bf16[512,1024]{1,0:T(8,128)(2,1)S(1)} %slice.34.refs_0_), channel_id=1, source_target_pairs={{0,4},{4,8},{8,12},{1,5},{5,9},{9,13},{2,6},{6,10},{10,14},{3,7},{... | collective-permute-start | bytes 3145736 | tf_op jit(solution)/shard_map/ppermute | solution.py:317
  8.7 28.1 %collective-permute-start.1 = (bf16[512,1024]{1,0:T(8,128)(2,1)S(1)}, bf16[512,1024]{1,0:T(8,128)(2,1)}, u32[]{:S(2)}, u32[]{:S(2)}) collective-permute-start(bf16[512,1024]{1,0:T(8,128)(2,1)S(1)} %slice.34.refs_0_), channel_id=1, source_target_pairs={{4,0},{8,4},{12,8},{5,1},{9,5},{13,9},{6,2},{10,6},{14,10},{7,3},{... | collective-permute-start | bytes 3145736 | tf_op jit(solution)/shard_map/ppermute | solution.py:318
  11.3 13.1 %copy-start.11 = (bf16[512,1024]{1,0:T(8,128)(2,1)}, bf16[512,1024]{1,0:T(8,128)(2,1)S(1)}, u32[]{:S(2)}) copy-start(bf16[512,1024]{1,0:T(8,128)(2,1)S(1)} %slice.35.refs_1_) | copy-start | bytes 3145732
  11.3 41.0 %collective-permute-start.2 = (bf16[512,1024]{1,0:T(8,128)(2,1)S(1)}, bf16[512,1024]{1,0:T(8,128)(2,1)}, u32[]{:S(2)}, u32[]{:S(2)}) collective-permute-start(bf16[512,1024]{1,0:T(8,128)(2,1)S(1)} %slice.35.refs_1_), channel_id=1, source_target_pairs={{0,4},{4,8},{8,12},{1,5},{5,9},{9,13},{2,6},{6,10},{10,14},{3,7},{... | collective-permute-start | bytes 3145736 | tf_op jit(solution)/shard_map/ppermute | solution.py:317
  16.8 40.7 %collective-permute-start.3 = (bf16[512,1024]{1,0:T(8,128)(2,1)S(1)}, bf16[512,1024]{1,0:T(8,128)(2,1)}, u32[]{:S(2)}, u32[]{:S(2)}) collective-permute-start(bf16[512,1024]{1,0:T(8,128)(2,1)S(1)} %slice.35.refs_1_), channel_id=1, source_target_pairs={{4,0},{8,4},{12,8},{5,1},{9,5},{13,9},{6,2},{10,6},{14,10},{7,3},{... | collective-permute-start | bytes 3145736 | tf_op jit(solution)/shard_map/ppermute | solution.py:318
  18.1 4.7 %copy-start.14 = (bf16[4,32,8192]{2,1,0:T(8,128)(2,1)S(1)}, bf16[4,32,8192]{2,1,0:T(8,128)(2,1)}, u32[]{:S(2)}) copy-start(bf16[4,32,8192]{2,1,0:T(8,128)(2,1)} %param.17) | copy-start | bytes 6291460
  18.8 42.1 %copy-start.15 = (bf16[4,128,2048]{2,1,0:T(8,128)(2,1)S(1)}, bf16[4,128,2048]{2,1,0:T(8,128)(2,1)}, u32[]{:S(2)}) copy-start(bf16[4,128,2048]{2,1,0:T(8,128)(2,1)} %param.18) | copy-start | bytes 6291460
  31.3 33.3 %copy-start.9 = (bf16[512,1024]{1,0:T(8,128)(2,1)S(1)}, bf16[512,1024]{1,0:T(8,128)(2,1)}, u32[]{:S(2)}) copy-start(bf16[512,1024]{1,0:T(8,128)(2,1)} %copy-done.8) | copy-start | bytes 3145732
  31.3 33.3 %copy-start.12 = (bf16[512,1024]{1,0:T(8,128)(2,1)S(1)}, bf16[512,1024]{1,0:T(8,128)(2,1)}, u32[]{:S(2)}) copy-start(bf16[512,1024]{1,0:T(8,128)(2,1)} %copy-done.11) | copy-start | bytes 3145732
  31.3 33.3 %collective-permute-start.4 = (bf16[512,1024]{1,0:T(8,128)(2,1)}, bf16[512,1024]{1,0:T(8,128)(2,1)S(1)}, u32[]{:S(2)}, u32[]{:S(2)}) collective-permute-start(bf16[512,1024]{1,0:T(8,128)(2,1)} %collective-permute-done.refs_2_), channel_id=1, source_target_pairs={{4,8},{8,12},{5,9},{9,13},{6,10},{10,14},{7,11},{11,15},{20,24},{2... | collective-permute-start | bytes 3145736 | tf_op jit(solution)/shard_map/ppermute | solution.py:317
  57.5 50.1 %collective-permute-start.10 = (bf16[512,1024]{1,0:T(8,128)(2,1)}, bf16[512,1024]{1,0:T(8,128)(2,1)S(1)}, u32[]{:S(2)}, u32[]{:S(2)}) collective-permute-start(bf16[512,1024]{1,0:T(8,128)(2,1)} %collective-permute-done.2.refs_4_), channel_id=1, source_target_pairs={{4,8},{8,12},{5,9},{9,13},{6,10},{10,14},{7,11},{11,15},{20,24},{2... | collective-permute-start | bytes 3145736 | tf_op jit(solution)/shard_map/ppermute | solution.py:317
  58.2 49.4 %collective-permute-start.11 = (bf16[512,1024]{1,0:T(8,128)(2,1)}, bf16[512,1024]{1,0:T(8,128)(2,1)S(1)}, u32[]{:S(2)}, u32[]{:S(2)}) collective-permute-start(bf16[512,1024]{1,0:T(8,128)(2,1)} %collective-permute-done.3.refs_5_), channel_id=1, source_target_pairs={{4,0},{8,4},{5,1},{9,5},{6,2},{10,6},{7,3},{11,7},{20,16},{24,20},... | collective-permute-start | bytes 3145736 | tf_op jit(solution)/shard_map/ppermute | solution.py:318
  59.5 48.1 %collective-permute-start.5 = (bf16[512,1024]{1,0:T(8,128)(2,1)}, bf16[512,1024]{1,0:T(8,128)(2,1)S(1)}, u32[]{:S(2)}, u32[]{:S(2)}) collective-permute-start(bf16[512,1024]{1,0:T(8,128)(2,1)} %collective-permute-done.1.refs_3_), channel_id=1, source_target_pairs={{4,0},{8,4},{5,1},{9,5},{6,2},{10,6},{7,3},{11,7},{20,16},{24,20},... | collective-permute-start | bytes 3145736 | tf_op jit(solution)/shard_map/ppermute | solution.py:318
  60.9 47.8 %collective-permute-start.12 = (bf16[4,128,2048]{2,1,0:T(8,128)(2,1)S(1)}, bf16[4,128,2048]{2,1,0:T(8,128)(2,1)S(1)}, u32[]{:S(2)}, u32[]{:S(2)}) collective-permute-start(bf16[4,128,2048]{2,1,0:T(8,128)(2,1)S(1)} %copy-done.15), channel_id=1, source_target_pairs={{0,2},{1,3},{2,0},{3,1},{4,6},{5,7},{6,4},{7,5},{8,10},{9,11},{10,... | collective-permute-start | bytes 6291464 | tf_op jit(solution)/shard_map/ppermute | solution.py:310
  64.6 56.6 %copy-start.5 = (bf16[512,1024]{1,0:T(8,128)(2,1)}, bf16[512,1024]{1,0:T(8,128)(2,1)S(1)}, u32[]{:S(2)}) copy-start(bf16[512,1024]{1,0:T(8,128)(2,1)S(1)} %collective-permute-done.4.refs_0_.refs_6_) | copy-start | bytes 3145732
  64.6 55.1 %collective-permute-start.9 = (bf16[8,32,8192]{2,1,0:T(8,128)(2,1)}, bf16[8,32,8192]{2,1,0:T(8,128)(2,1)}, u32[]{:S(2)}, u32[]{:S(2)}) collective-permute-start(bf16[8,32,8192]{2,1,0:T(8,128)(2,1)} %constant_dynamic-update-slice_fusion.refs_0_), channel_id=1, source_target_pairs={{0,1},{1,0},{2,3},{3,2},{4,5},{5,4},{6,7},{7,6},{8,9},{9,8},{10,11... | collective-permute-start | bytes 12582920 | tf_op jit(solution)/shard_map/ppermute | solution.py:310
  84.9 25.2 %copy-start.17 = (s32[4]{0:T(128)S(1)}, s32[4]{0:T(128)}, u32[]{:S(2)}) copy-start(s32[4]{0:T(128)} %constant.87.clone) | copy-start | bytes 52
  84.9 25.3 %copy-start.18 = (s32[4]{0:T(128)S(1)}, s32[4]{0:T(128)}, u32[]{:S(2)}) copy-start(s32[4]{0:T(128)} %constant.90.clone) | copy-start | bytes 52
  84.9 26.6 %copy-start.25 = (s32[10]{0:T(128)S(1)}, s32[10]{0:T(128)}, u32[]{:S(2)}) copy-start(s32[10]{0:T(128)} %constant.91.clone) | copy-start | bytes 124
  84.9 27.3 %copy-start.24 = (s32[2]{0:T(128)S(1)}, s32[2]{0:T(128)}, u32[]{:S(2)}) copy-start(s32[2]{0:T(128)} %constant.88.clone) | copy-start | bytes 28
  85.0 27.9 %copy-start.21 = (s32[16]{0:T(128)S(1)}, s32[16]{0:T(128)}, u32[]{:S(2)}) copy-start(s32[16]{0:T(128)} %param.19) | copy-start | bytes 196
  85.0 27.9 %copy-start.22 = (s32[1,6]{1,0:T(1,128)S(1)}, s32[1,6]{1,0:T(1,128)}, u32[]{:S(2)}) copy-start(s32[1,6]{1,0:T(1,128)} %param.20) | copy-start | bytes 76
  85.0 27.8 %copy-start.23 = (s32[16]{0:T(128)S(1)}, s32[16]{0:T(128)}, u32[]{:S(2)}) copy-start(s32[16]{0:T(128)} %param.22) | copy-start | bytes 196
  85.0 28.0 %copy-start.16 = (s32[512]{0:T(512)S(1)}, s32[512]{0:T(512)}, u32[]{:S(2)}) copy-start(s32[512]{0:T(512)} %param.21) | copy-start | bytes 6148
  107.6 1.0 copy-start.6
  107.7 28.0 %copy-start.3 = (bf16[512,1024]{1,0:T(8,128)(2,1)}, bf16[512,1024]{1,0:T(8,128)(2,1)S(1)}, u32[]{:S(2)}) copy-start(bf16[512,1024]{1,0:T(8,128)(2,1)S(1)} %collective-permute-done.10.refs_2_.refs_8_) | copy-start | bytes 3145732
  108.6 27.0 %copy-start.4 = (bf16[512,1024]{1,0:T(8,128)(2,1)}, bf16[512,1024]{1,0:T(8,128)(2,1)S(1)}, u32[]{:S(2)}) copy-start(bf16[512,1024]{1,0:T(8,128)(2,1)S(1)} %collective-permute-done.11.refs_3_.refs_9_) | copy-start | bytes 3145732
  110.2 52.8 %collective-permute-start.13 = (bf16[8,128,2048]{2,1,0:T(8,128)(2,1)}, bf16[8,128,2048]{2,1,0:T(8,128)(2,1)}, u32[]{:S(2)}, u32[]{:S(2)}) collective-permute-start(bf16[8,128,2048]{2,1,0:T(8,128)(2,1)} %constant_dynamic-update-slice_fusion.2.refs_0_), channel_id=1, source_target_pairs={{0,1},{1,0},{2,3},{3,2},{4,5},{5,4},{6,7},{7,6},{8,9},{9,8},{10,11... | collective-permute-start | bytes 12582920 | tf_op jit(solution)/shard_map/ppermute | solution.py:310
  115.1 37.5 %collective-permute-start.6 = (bf16[512,1024]{1,0:T(8,128)(2,1)S(1)}, bf16[512,1024]{1,0:T(8,128)(2,1)}, u32[]{:S(2)}, u32[]{:S(2)}) collective-permute-start(bf16[512,1024]{1,0:T(8,128)(2,1)S(1)} %collective-permute-done.4.refs_0_.refs_6_), channel_id=1, source_target_pairs={{8,12},{9,13},{10,14},{11,15},{24,28},{25,29},{26,30},{27,31}} | collective-permute-start | bytes 3145736 | tf_op jit(solution)/shard_map/ppermute | solution.py:317
  116.8 35.9 %collective-permute-start.7 = (bf16[512,1024]{1,0:T(8,128)(2,1)}, bf16[512,1024]{1,0:T(8,128)(2,1)}, u32[]{:S(2)}, u32[]{:S(2)}) collective-permute-start(bf16[512,1024]{1,0:T(8,128)(2,1)} %copy-done.6), channel_id=1, source_target_pairs={{4,0},{5,1},{6,2},{7,3},{20,16},{21,17},{22,18},{23,19}} | collective-permute-start | bytes 3145736 | tf_op jit(solution)/shard_map/ppermute | solution.py:318
  118.1 53.1 %collective-permute-start.14 = (bf16[512,1024]{1,0:T(8,128)(2,1)S(1)}, bf16[512,1024]{1,0:T(8,128)(2,1)}, u32[]{:S(2)}, u32[]{:S(2)}) collective-permute-start(bf16[512,1024]{1,0:T(8,128)(2,1)S(1)} %collective-permute-done.10.refs_2_.refs_8_), channel_id=1, source_target_pairs={{8,12},{9,13},{10,14},{11,15},{24,28},{25,29},{26,30},{27,31}} | collective-permute-start | bytes 3145736 | tf_op jit(solution)/shard_map/ppermute | solution.py:317
  119.8 51.4 %collective-permute-start.15 = (bf16[512,1024]{1,0:T(8,128)(2,1)S(1)}, bf16[512,1024]{1,0:T(8,128)(2,1)}, u32[]{:S(2)}, u32[]{:S(2)}) collective-permute-start(bf16[512,1024]{1,0:T(8,128)(2,1)S(1)} %collective-permute-done.11.refs_3_.refs_9_), channel_id=1, source_target_pairs={{4,0},{5,1},{6,2},{7,3},{20,16},{21,17},{22,18},{23,19}} | collective-permute-start | bytes 3145736 | tf_op jit(solution)/shard_map/ppermute | solution.py:318
  121.2 1.2 copy-start.7
  135.7 5.6 %copy-start.10 = (bf16[512,1024]{1,0:T(8,128)(2,1)S(1)}, bf16[512,1024]{1,0:T(8,128)(2,1)}, u32[]{:S(2)}) copy-start(bf16[512,1024]{1,0:T(8,128)(2,1)} %copy-done.8) | copy-start | bytes 3145732
  135.7 5.6 %copy-start.13 = (bf16[512,1024]{1,0:T(8,128)(2,1)S(1)}, bf16[512,1024]{1,0:T(8,128)(2,1)}, u32[]{:S(2)}) copy-start(bf16[512,1024]{1,0:T(8,128)(2,1)} %copy-done.11) | copy-start | bytes 3145732
  139.2 2.0 %copy-start = (bf16[8192,192]{1,0:T(8,128)(2,1)}, bf16[8192,192]{1,0:T(8,128)(2,1)S(1)}, u32[]{:S(2)}) copy-start(bf16[8192,192]{1,0:T(8,128)(2,1)S(1)} %shard_map.147.refs_10_.refs_3_.down) | copy-start | bytes 9437188
  163.0 2.2 %copy-start.1 = (bf16[8192,192]{1,0:T(8,128)(2,1)S(1)}, bf16[8192,192]{1,0:T(8,128)(2,1)}, u32[]{:S(2)}) copy-start(bf16[8192,192]{1,0:T(8,128)(2,1)} %copy-done) | copy-start | bytes 9437188
  165.2 2.2 %copy-start.2 = (f32[512,2048]{1,0:T(8,128)S(1)}, f32[512,2048]{1,0:T(8,128)}, u32[]{:S(2)}) copy-start(f32[512,2048]{1,0:T(8,128)} %get-tuple-element.49.base) | copy-start | bytes 12582916
  173.1 7.1 %collective-permute-start.16 = (bf16[512,32]{1,0:T(8,128)(2,1)S(1)}, bf16[512,32]{1,0:T(8,128)(2,1)S(1)}, u32[]{:S(2)}, u32[]{:S(2)}) collective-permute-start(bf16[512,32]{1,0:T(8,128)(2,1)S(1)} %get-tuple-element.68.refs_0_), channel_id=1, source_target_pairs={{0,12},{4,0},{8,4},{12,8},{1,13},{5,1},{9,5},{13,9},{2,14},{6,2},{... | collective-permute-start | bytes 98312 | tf_op jit(solution)/shard_map/ppermute | solution.py:362
  173.2 15.2 %collective-permute-start.17 = (bf16[512,32]{1,0:T(8,128)(2,1)S(1)}, bf16[512,32]{1,0:T(8,128)(2,1)S(1)}, u32[]{:S(2)}, u32[]{:S(2)}) collective-permute-start(bf16[512,32]{1,0:T(8,128)(2,1)S(1)} %get-tuple-element.68.refs_0_), channel_id=1, source_target_pairs={{0,8},{4,12},{8,0},{12,4},{1,9},{5,13},{9,1},{13,5},{2,10},{6,14},... | collective-permute-start | bytes 98312 | tf_op jit(solution)/shard_map/ppermute | solution.py:362
  176.2 12.2 %collective-permute-start.18 = (bf16[512,32]{1,0:T(8,128)(2,1)S(1)}, bf16[512,32]{1,0:T(8,128)(2,1)S(1)}, u32[]{:S(2)}, u32[]{:S(2)}) collective-permute-start(bf16[512,32]{1,0:T(8,128)(2,1)S(1)} %get-tuple-element.68.refs_0_), channel_id=1, source_target_pairs={{0,4},{4,8},{8,12},{12,0},{1,5},{5,9},{9,13},{13,1},{2,6},{6,10},{... | collective-permute-start | bytes 98312 | tf_op jit(solution)/shard_map/ppermute | solution.py:362

commit v11 on v10

v11 whole, which is shorter than its diff:
```python
import functools

import jax
import jax.numpy as jnp
from jax import lax
from jax.experimental import pallas as pl
from jax.experimental.pallas import tpu as pltpu
from jax.sharding import PartitionSpec as P

PARAMS = pltpu.CompilerParams(vmem_limit_bytes=48 * 2**20)
TAIL_PARAMS = pltpu.CompilerParams(vmem_limit_bytes=24 * 2**20)
F32 = jnp.float32
BF16 = jnp.bfloat16


def start_pages(places, blocks, length, targets, sems, rows_of):
    for e, target in enumerate(targets):
        for j, block in enumerate(blocks):

            @pl.when(places[e] // length == j)
            def _():
                pltpu.make_async_copy(rows_of(block.at[lax.rem(places[e], length)]), target, sems[e]).start()


def join_downs_kernel(places, *refs):
    *blocks, out, held, sems = refs
    length, rank_part, _ = blocks[0].shape
    shards, slots, width = held.shape
    step = pl.program_id(0)

    def targets(t):
        return [held.at[t, pl.ds(e * rank_part, rank_part)] for e in range(slots // rank_part)]

    @pl.when(step == 0)
    def _():
        for t in range(shards):
            semaphores = [sems.at[t, e] for e in range(slots // rank_part)]
            start_pages(
                places, blocks, length, targets(t), semaphores, lambda page: page.at[:, pl.ds(t * width, width)]
            )

    for t in range(shards):

        @pl.when(step == t)
        def _():
            for e, target in enumerate(targets(t)):
                source = blocks[0].at[0, :, pl.ds(t * width, width)]
                pltpu.make_async_copy(source, target, sems.at[t, e]).wait()
            out[...] = held[t].T


def join_downs(places, blocks, shards):
    entries = places.shape[0]
    _, rank_part, features = blocks[0].shape
    width, slots = features // shards, entries * rank_part
    return pl.pallas_call(
        join_downs_kernel,
        out_shape=jax.ShapeDtypeStruct((features, slots), BF16),
        grid=(shards,),
        in_specs=[pl.BlockSpec(memory_space=pltpu.SMEM)] + [pl.BlockSpec(memory_space=pltpu.HBM)] * len(blocks),
        out_specs=pl.BlockSpec((width, slots), lambda t: (t, 0)),
        scratch_shapes=[pltpu.VMEM((shards, slots, width), BF16), pltpu.SemaphoreType.DMA((shards, entries))],
        compiler_params=TAIL_PARAMS,
        cost_estimate=pl.CostEstimate(flops=0, bytes_accessed=4 * features * slots, transcendentals=0),
    )(places, *blocks)


RESIDENT = pl.BlockSpec(memory_space=pltpu.VMEM)
IN_HBM = pl.BlockSpec(memory_space=pltpu.HBM)


def near_kernel(start, valid, *refs):
    *xs, weight, down, base, low = refs
    step = pl.program_id(0)

    @pl.when(step == 0)
    def _():
        base[...] = jnp.zeros_like(base)
        low[...] = jnp.zeros_like(low)

    for i, x in enumerate(xs):

        @pl.when((step // 2 == i) & (valid[i] != 0))
        def _():
            part = min(base.shape[1], 512)
            for n in range(0, base.shape[1], part):
                base[:, n:n + part] += jnp.dot(x[...], weight[:, n:n + part], preferred_element_type=F32)
            low[...] += jnp.dot(x[...], down[...], preferred_element_type=F32)


def near_products(xs, source, weight, down):
    rows, width = xs[0].shape
    half = width // 2
    n_tensor = weight.shape[0] // width
    there = (source >= 0) & (source < n_tensor)
    start = 2 * jnp.clip(source, 0, n_tensor - 1)[:, None] + jnp.arange(2)[None, :]
    before = jnp.broadcast_to(jnp.roll(start[:, 1:], 1, axis=0), start.shape)
    start = jnp.where(there[:, None], start, before).reshape(-1).astype(jnp.int32)
    columns, slots = weight.shape[1], down.shape[1]
    whole = [pl.BlockSpec((rows, a), lambda s, *_: (0, 0)) for a in (columns, slots)]
    steps = 2 * len(xs)
    return pl.pallas_call(
        near_kernel,
        out_shape=[jax.ShapeDtypeStruct((rows, a), F32) for a in (columns, slots)],
        grid_spec=pltpu.PrefetchScalarGridSpec(
            num_scalar_prefetch=2,
            grid=(steps,),
            in_specs=[
                pl.BlockSpec((rows, half), lambda s, *_, i=i: (0, jnp.clip(s - 2 * i, 0, 1)))
                for i in range(len(xs))
            ]
            + [pl.BlockSpec((half, a), lambda s, start, valid: (start[s], 0)) for a in (columns, slots)],
            out_specs=whole,
        ),
        compiler_params=PARAMS,
        cost_estimate=pl.CostEstimate(
            flops=2 * steps * half * rows * (columns + slots),
            bytes_accessed=2 * steps * half * (rows + columns + slots) + 4 * rows * (columns + slots),
            transcendentals=0,
        ),
    )(start, there.astype(jnp.int32), *xs, weight, down)


def fold_entry(low, slot, rank_part):
    lane = lax.broadcasted_iota(jnp.int32, low.shape, 1)
    own = jnp.where(lane // rank_part == slot, low, 0.0)
    shape = (low.shape[1], rank_part)
    fold = lax.rem(lax.broadcasted_iota(jnp.int32, shape, 0), rank_part) == lax.broadcasted_iota(jnp.int32, shape, 1)
    return jnp.dot(own, fold.astype(F32), precision=lax.Precision.HIGHEST, preferred_element_type=F32)


def far_kernel(start, first, second, weight, down, other_down, slot, base_in, low_in, base, low, other, acc, other_acc):
    step = pl.program_id(0)
    rank_part = low.shape[1]

    @pl.when(step == 0)
    def _():
        base[...] = base_in[...]
        acc[...] = low_in[...]
        other_acc[...] = jnp.zeros_like(other_acc)

    for i, x in enumerate((first, second)):

        @pl.when(step == i)
        def _():
            part = min(base.shape[1], 512)
            for n in range(0, base.shape[1], part):
                base[:, n:n + part] += jnp.dot(x[...], weight[:, n:n + part], preferred_element_type=F32)
            acc[...] += jnp.dot(x[...], down[...], preferred_element_type=F32)
            other_acc[...] += jnp.dot(x[...], other_down[...], preferred_element_type=F32)

    @pl.when(step == 1)
    def _():
        low[...] = fold_entry(acc[...], slot[...], rank_part)
        other[...] = fold_entry(other_acc[...], slot[...], rank_part)


def add_far(base, low, first, second, source, weight, down, other_down, slot, rank_part):
    rows, width = first.shape
    columns, slots = weight.shape[1], down.shape[1]
    start = (2 * source + jnp.arange(2)).astype(jnp.int32)

    def whole(a):
        return pl.BlockSpec((rows, a), lambda s, start: (0, 0))

    return pl.pallas_call(
        far_kernel,
        out_shape=[jax.ShapeDtypeStruct((rows, a), F32) for a in (columns, rank_part, rank_part)],
        grid_spec=pltpu.PrefetchScalarGridSpec(
            num_scalar_prefetch=1,
            grid=(2,),
            in_specs=[
                whole(width),
                whole(width),
                pl.BlockSpec((width, columns), lambda s, start: (start[s], 0)),
                pl.BlockSpec((width, slots), lambda s, start: (start[s], 0)),
                pl.BlockSpec((width, slots), lambda s, start: (s, 0)),
                whole(1),
                whole(columns),
                whole(slots),
            ],
            out_specs=[whole(columns), whole(rank_part), whole(rank_part)],
            scratch_shapes=[pltpu.VMEM((rows, slots), F32)] * 2,
        ),
        compiler_params=PARAMS,
        cost_estimate=pl.CostEstimate(
            flops=4 * width * rows * (columns + 2 * slots),
            bytes_accessed=4 * width * (rows + columns + 2 * slots) + 8 * rows * columns,
            transcendentals=0,
        ),
    )(start, first, second, weight, down, other_down, slot, base, low)


def prepare_kernel(facts, places, base, third, weight, *refs):
    *refs, total, last_rows, x, rows_of, up, spread, sems = refs
    *lows, slot = refs[2:]
    blocks = refs[:2]
    width = x.shape[1]
    length, rank, _ = blocks[0].shape
    rank_part = lows[0].shape[1]
    count = up.shape[0] // rank
    me, which, start = facts[0], facts[1], facts[2]
    part = min(total.shape[1], 512)

    def rows_at(half):
        return weight.at[pl.ds(pl.multiple_of((start + half) * width, width), width)]

    to_total = pltpu.make_async_copy(base, total, sems.at[0])
    to_x = pltpu.make_async_copy(third, x, sems.at[1])
    to_rows = pltpu.make_async_copy(rows_at(0), rows_of, sems.at[2])
    to_last = pltpu.make_async_copy(rows_at(1), last_rows, sems.at[3])
    pages = [up.at[pl.ds(e * rank, rank)] for e in range(count)]
    page_sems = [sems.at[4 + e] for e in range(count)]
    start_pages(places, blocks, length, pages, page_sems, lambda page: page)
    to_total.start()

    @pl.when(which != 0)
    def _():
        to_x.start()
        to_rows.start()
        to_last.start()

    low = jnp.concatenate([part_of[...].astype(F32) for part_of in lows], axis=1)
    low = pltpu.roll(low, me * rank_part, 1)
    for e in range(count):
        spread[:, e * rank:(e + 1) * rank] = jnp.where(slot[...] == e, low, 0.0).astype(BF16)
    for page, sem in zip(pages, page_sems):
        pltpu.make_async_copy(blocks[0].at[0], page, sem).wait()
    to_total.wait()
    for n in range(0, total.shape[1], part):
        cut = slice(n, n + part)
        total[:, cut] += jnp.dot(spread[...], up[:, cut], preferred_element_type=F32)

    @pl.when(which != 0)
    def _():
        to_x.wait()
        to_rows.wait()
        for n in range(0, total.shape[1], part):
            cut = slice(n, n + part)
            total[:, cut] += jnp.dot(x[...], rows_of[:, cut], preferred_element_type=F32)
        to_last.wait()


def prepare(facts, places, base, third, weight, blocks, lows, slot):
    rows, columns = base.shape
    width = third.shape[1]
    rank = blocks[0].shape[1]
    entries = places.shape[0]
    return pl.pallas_call(
        prepare_kernel,
        out_shape=[pltpu.VMEM((rows, columns), F32), pltpu.VMEM((width, columns), BF16)],
        in_specs=[pl.BlockSpec(memory_space=pltpu.SMEM)] * 2 + [IN_HBM] * 5 + [RESIDENT] * (len(lows) + 1),
        out_specs=[RESIDENT] * 2,
        scratch_shapes=[
            pltpu.VMEM((rows, width), BF16),
            pltpu.VMEM((width, columns), BF16),
            pltpu.VMEM((entries * rank, columns), BF16),
            pltpu.VMEM((rows, entries * rank), BF16),
            pltpu.SemaphoreType.DMA((4 + entries,)),
        ],
        compiler_params=TAIL_PARAMS,
        cost_estimate=pl.CostEstimate(
            flops=2 * (width + entries * rank) * rows * columns,
            bytes_accessed=2 * (2 * width + entries * rank + 2 * rows) * columns,
            transcendentals=0,
        ),
    )(facts, places, base, third, weight, *blocks, *lows, slot)


def last_kernel(facts, total, weight, x, out):
    part = out.shape[1]
    cut = pl.ds(pl.multiple_of(pl.program_id(0) * part, part), part)

    @pl.when(facts[1] != 0)
    def _():
        out[...] = (total[:, cut] + jnp.dot(x[...], weight[:, cut], preferred_element_type=F32)).astype(BF16)

    @pl.when(facts[1] == 0)
    def _():
        out[...] = total[:, cut].astype(BF16)


def add_last(facts, total, weight, x):
    rows, columns = total.shape
    part = min(columns, 512)
    return pl.pallas_call(
        last_kernel,
        out_shape=jax.ShapeDtypeStruct((rows, columns), BF16),
        grid=(columns // part,),
        in_specs=[pl.BlockSpec(memory_space=pltpu.SMEM), RESIDENT, RESIDENT, pl.BlockSpec(x.shape, lambda n: (0, 0))],
        out_specs=pl.BlockSpec((rows, part), lambda n: (0, n)),
        compiler_params=TAIL_PARAMS,
        cost_estimate=pl.CostEstimate(
            flops=2 * x.shape[1] * rows * columns, bytes_accessed=2 * rows * columns, transcendentals=0
        ),
    )(facts, total, weight, x)


def after(value, *earlier):
    return lax.optimization_barrier((value,) + earlier)[0]


def looked_up(table, ids):
    hit = ids[:, None] == jnp.arange(table.shape[0])[None, :]
    return jnp.sum(jnp.where(hit, table[None, :], 0), axis=1)


def local(
    attention_result,
    output_weight,
    adapter_down_weight,
    adapter_up_weight,
    adapter_page_row,
    requests,
    row_request_entry,
    ranks,
):
    n_dp = lax.axis_size("dp")
    n_tensor = lax.axis_size("tensor")
    me = lax.axis_index("tensor")
    rows, width = attention_result.shape
    holder_length, rank_part, _ = adapter_down_weight.shape
    rank, columns = adapter_up_weight.shape[1:]
    own_list = requests[0]
    entries = own_list.shape[0]
    one_hot = row_request_entry[:, None] == jnp.arange(entries)[None, :]
    row_rank = jnp.sum(jnp.where(one_hot, looked_up(ranks, own_list)[None, :], 0), axis=1)
    pages = looked_up(adapter_page_row, own_list)
    apart = (pages // holder_length) ^ lax.axis_index("dp")
    places = apart * holder_length + pages % holder_length
    if n_tensor != 4 or n_dp != 4 or width % 256 or rank_part % 16 or entries * rank_part > 256:
        return plain(
            attention_result, output_weight, adapter_down_weight, adapter_up_weight, places, one_hot, row_rank
        )

    places = (apart % 2 * 2 + apart // 2) * holder_length + pages % holder_length

    def across(x, distance):
        return lax.ppermute(x, "dp", [(i, i ^ distance) for i in range(n_dp)])

    right = [(i, i + 1) for i in range(n_tensor - 1)]
    left = [(i + 1, i) for i in range(n_tensor - 1)]
    upper = me >= n_tensor // 2
    ends = me * (n_tensor - 1 - me) == 0
    slot = row_request_entry[:, None]

    right_1 = lax.ppermute(attention_result, "tensor", right)
    left_1 = lax.ppermute(attention_result, "tensor", left)
    far_down = across(adapter_down_weight, 2)
    far_up = across(adapter_up_weight, 2)

    right_2 = lax.ppermute(right_1, "tensor", right[1:])
    left_2 = lax.ppermute(left_1, "tensor", left[:-1])
    downs = jnp.concatenate([adapter_down_weight, after(far_down, right_1, left_1)], axis=0)
    downs = (downs, across(downs, 1))
    down = join_downs(places, downs, n_tensor)
    farthest = jnp.where(upper, 0, n_tensor - 1)
    other_down = lax.dynamic_slice_in_dim(down, farthest * width, width, 0)
    other_down = lax.ppermute(other_down, "tensor", [(0, 1), (3, 2)])

    near = me + jnp.array([0, -1, 1], jnp.int32)
    base, low = near_products([attention_result, right_1, left_1], near, output_weight, down)

    right_2, left_2 = lax.optimization_barrier((base, right_2, left_2))[1:]
    half = width // 2
    first_2 = jnp.where(upper, right_2[:, :half], left_2[:, :half])
    first_3 = lax.ppermute(first_2, "tensor", right[-1:] + left[:1])
    second_2 = jnp.where(upper, right_2[:, half:], left_2[:, half:])
    second_3 = lax.ppermute(second_2, "tensor", right[-1:] + left[:1])

    ups = jnp.concatenate([adapter_up_weight, after(far_up, second_2)], axis=0)
    ups = (ups, across(ups, 1))
    source = jnp.where(upper, me - 2, me + 2)
    base, low, other = add_far(base, low, first_2, second_2, source, output_weight, down, other_down, slot, rank_part)
    low = low + lax.ppermute(other, "tensor", [(1, 0), (2, 3)])
    live = row_rank[:, None] - me * rank_part
    low = jnp.where(jnp.arange(rank_part)[None, :] < live, low, 0.0).astype(BF16)
    lows = [low] + [
        lax.ppermute(low, "tensor", [(i, (i - j) % n_tensor) for i in range(n_tensor)])
        for j in range(1, n_tensor)
    ]
    facts = jnp.stack([me, ends.astype(jnp.int32), 2 * farthest]).astype(jnp.int32)
    total, rows_of = prepare(facts, places, base, first_3, output_weight, ups, lows, slot)
    total, rows_of, second_3 = lax.optimization_barrier((total, rows_of, second_3))
    return add_last(facts, total, rows_of, second_3)


def gather_pages(block, n_dp):
    return [block] + [
        lax.ppermute(block, "dp", [(i, i ^ j) for i in range(n_dp)]) for j in range(1, n_dp)
    ]


def plain(x, output_weight, down_weight, up_weight, places, one_hot, row_rank):
    n_dp = lax.axis_size("dp")
    rows = x.shape[0]
    rank, columns = up_weight.shape[1:]
    entries = one_hot.shape[1]

    def requested(block):
        blocks = jnp.concatenate(gather_pages(block, n_dp), axis=0)
        return jnp.concatenate(
            [lax.dynamic_slice_in_dim(blocks, places[e], 1, 0) for e in range(entries)], axis=0
        )

    down, up = requested(down_weight), requested(up_weight)
    x = lax.all_gather(x, "tensor", axis=1, tiled=True)
    base = jnp.dot(x, output_weight, preferred_element_type=F32)
    low = jnp.einsum("rd,ekd->rek", x, down, preferred_element_type=F32)
    low = jnp.sum(jnp.where(one_hot[:, :, None], low, 0.0), axis=1).astype(BF16)
    low = lax.all_gather(low, "tensor", axis=1, tiled=True)
    low = jnp.where(jnp.arange(rank)[None, :] < row_rank[:, None], low, jnp.zeros_like(low))
    spread = jnp.where(one_hot[:, :, None], low[:, None, :], jnp.zeros((), BF16))
    term = jnp.dot(
        spread.reshape(rows, entries * rank), up.reshape(entries * rank, columns), preferred_element_type=F32
    )
    return (base + term).astype(BF16)


def solution(mesh):
    in_specs = (
        P(("groups", "dp"), "tensor"),
        P(None, "tensor"),
        P("dp", "tensor", None),
        P("dp", None, "tensor"),
        P("groups"),
        P(("groups", "dp"), None),
        P(("groups", "dp")),
        P(),
    )
    out_specs = P(("groups", "dp"), "tensor")
    return jax.shard_map(local, mesh=mesh, in_specs=in_specs, out_specs=out_specs, check_vma=False)
```

time: 193 us -> 209 us (1.083)
  waiting for transfers between devices: 63.1 us -> 110 us
  Pallas kernels: 70.8 us -> 47.2 us
  starting transfers between devices: 30.6 us -> 25.3 us
    ppermute x12 -> x8, waiting for transfers between devices: 54.9 us -> 102 us  [the longest x1 39 us: local(): right_1 = lax.ppermute(attention_result, 'tensor', right)]
    pallas_call x8 -> x4, Pallas kernels: 67.2 us -> 43.6 us  [the longest x1 18.8 us: near_products(): pl.pallas_call(near_kernel, out_shape=[jax.ShapeDtypeStruct((rows, a), F3...]
    ppermute x12 -> x8, starting transfers between devices: 22.7 us -> 18.3 us  [the longest x1 5.21 us: local(): right_1 = lax.ppermute(attention_result, 'tensor', right)]
    slice x6 -> x2, local copies, waits for them, and re-layouts: 4.98 us -> 0.59 us  [near_products(): before = jnp.broadcast_to(jnp.roll(start[:, 1:], 1, axis=0), start.shape)]
    dynamic_slice x0 -> x2, local copies, waits for them, and re-layouts: none -> 2.53 us  [local(): other_down = lax.dynamic_slice_in_dim(down, farthest * width, width, 0)]
    unnamed x54 -> x24, local copies, waits for them, and re-layouts: 13.5 us -> 11.9 us
  transfers between devices with their start and end apart: 19 -> 15, of which waited for: 6 -> 7; matrix products, arithmetic and copies ran while one was open for 10% -> 7% of each run, Pallas kernels for 34% -> 20%
where the time goes in v11:
time: 209 us; the launch traced here: 208 us
  waiting for transfers between devices  110 us (53%)
  Pallas kernels  47.2 us (23%)
  starting transfers between devices  25.3 us (12%)
  local copies, waits for them, and re-layouts  21.5 us (10%)
  other arithmetic  3.55 us (2%)
    ppermute x1, waiting for transfers between devices, local(): right_1 = lax.ppermute(attention_result, 'tensor', right)  39 us
    ppermute x1, waiting for transfers between devices, local(): left_2 = lax.ppermute(left_1, 'tensor', left[:-1])  23 us
    ppermute x1, waiting for transfers between devices, local(): low = low + lax.ppermute(other, 'tensor', [(1, 0), (2, 3)])  21.8 us
    pallas_call x1, Pallas kernels, near_products(): pl.pallas_call(near_kernel, out_shape=[jax.ShapeDtypeStruct((rows, a), F3...  18.8 us
    ppermute x1, waiting for transfers between devices, local(): other_down = lax.ppermute(other_down, 'tensor', [(0, 1), (3, 2)])  13.9 us
    pallas_call x1, Pallas kernels, add_far(): pl.pallas_call(far_kernel, out_shape=[jax.ShapeDtypeStruct((rows, a), F32...  13 us
    unnamed x24, local copies, waits for them, and re-layouts  11.9 us
    ppermute x3, waiting for transfers between devices, local(): lax.ppermute(low, 'tensor', [(i, (i - j) % n_tensor) for i in range(n_ten...  8.43 us
  transfers between devices with their start and end apart: 15, of which 7 were waited for; matrix products, arithmetic and copies ran while one was open for 7% of the time, Pallas kernels for 20%

profile of v11, /device:TPU:0, one launch (start us, length us, event | category | flops | bytes accessed | tf_op | source)
XLA Modules:
  0.0 208.1 jit_solution(5294217794469963491)
XLA Ops:
  0.0 5.2 %collective-permute-start = (bf16[512,2048]{1,0:T(8,128)(2,1)}, bf16[512,2048]{1,0:T(8,128)(2,1)S(1)}, u32[]{:S(2)}, u32[]{:S(2)}) collective-permute-start(bf16[512,2048]{1,0:T(8,128)(2,1)} %refs_0_.1), channel_id=1, source_target_pairs={{0,4},{4,8},{8,12},{1,5},{5,9},{9,13},{2,6},{6,10},{10,14},{3,7},{... | collective-permute-start | bytes 6291464 | tf_op jit(solution)/shard_map/ppermute | solution.py:347
  5.2 1.3 collective-permute-start.1
  6.5 1.6 collective-permute-start.2
  8.1 3.1 %constant_dynamic-update-slice_fusion.1 = bf16[8,32,8192]{2,1,0:T(8,128)(2,1)} fusion(bf16[4,32,8192]{2,1,0:T(8,128)(2,1)} %param.11), kind=kLoop, calls=%fused_computation.7 | loop fusion | bytes 4194304
  11.2 39.0 %collective-permute-done.refs_1_ = bf16[512,2048]{1,0:T(8,128)(2,1)S(1)} collective-permute-done((bf16[512,2048]{1,0:T(8,128)(2,1)}, bf16[512,2048]{1,0:T(8,128)(2,1)S(1)}, u32[]{:S(2)}, u32[]{:S(2)}) %collective-permute-start) | collective-permute-done | bytes 2097184 | tf_op jit(solution)/shard_map/ppermute | solution.py:347
  50.3 4.1 %collective-permute-done.1.refs_2_ = bf16[512,2048]{1,0:T(8,128)(2,1)S(1)} collective-permute-done((bf16[512,2048]{1,0:T(8,128)(2,1)}, bf16[512,2048]{1,0:T(8,128)(2,1)S(1)}, u32[]{:S(2)}, u32[]{:S(2)}) %collective-permute-start.1) | collective-permute-done | bytes 2097184 | tf_op jit(solution)/shard_map/ppermute | solution.py:348
  54.4 1.6 constant_dynamic-update-slice_fusion.refs_0_
  56.0 0.4 copy-done.10
  56.4 1.5 collective-permute-start.8
  57.9 0.6 slice.23
  58.5 0.6 add_bitcast_fusion
  59.2 2.0 collective-permute-start.4
  61.2 1.3 collective-permute-start.5
  62.5 0.1 copy.17
  62.5 0.1 select_n.73.start
  62.6 0.2 select_reduce_fusion.1
  62.9 3.2 %constant_dynamic-update-slice_fusion.3 = bf16[8,128,2048]{2,1,0:T(8,128)(2,1)} fusion(bf16[4,128,2048]{2,1,0:T(8,128)(2,1)} %param.12), kind=kLoop, calls=%fused_computation.9 | loop fusion | bytes 4194304
  66.0 0.0 collective-permute-done.3.refs_1_
  66.0 3.6 %shard_map.91.refs_4_.down = bf16[8192,192]{1,0:T(8,128)(2,1)S(1)} custom-call(s32[6]{0:T(128)S(1)} %fusion.1.places, bf16[8,32,8192]{2,1,0:T(8,128)(2,1)} %constant_dynamic-update-slice_fusion.refs_0_, bf16[8,32,8192]{2,1,0:T(8,128)(2,1)} %collective-permute-done.3.refs_1_), custom_call_target="tpu_custom_call" | custom-call | bytes 6291456 | tf_op jit(solution)/shard_map/pallas_call | solution.py:56
  69.6 1.9 copy-done
  71.5 18.8 %shard_map.92 = (f32[512,2048]{1,0:T(8,128)}, f32[512,192]{1,0:T(8,128)S(1)}) custom-call(s32[6]{0:T(128)S(1)} %select_n.73.start, s32[3]{0:T(128)S(1)} %get-tuple-element.35.valid, bf16[512,2048]{1,0:T(8,128)(2,1)S(1)} %copy-done.4, bf16[512,2048]{1,0:T(8,128)(2,1)S(1)} %collective-permute-done.refs_1_, bf16[512,2048]{1,0:T(8,128)(2,1)} %copy-done.10, ...), custom_call_target="tpu_custom_call" | custom-call | flops 14092861440 | bytes 38404096 | tf_op jit(solution)/shard_map/pallas_call | solution.py:102
  90.4 23.0 %collective-permute-done.5 = bf16[512,2048]{1,0:T(8,128)(2,1)} collective-permute-done((bf16[512,2048]{1,0:T(8,128)(2,1)}, bf16[512,2048]{1,0:T(8,128)(2,1)}, u32[]{:S(2)}, u32[]{:S(2)}) %collective-permute-start.5) | collective-permute-done | bytes 2097184 | tf_op jit(solution)/shard_map/ppermute | solution.py:353
  113.4 2.4 %slice_select_fusion = (bf16[512,1024]{1,0:T(8,128)(2,1)S(1)}, bf16[512,1024]{1,0:T(8,128)(2,1)S(1)}) fusion(bf16[512,2048]{1,0:T(8,128)(2,1)} %collective-permute-done.5, bf16[512,2048]{1,0:T(8,128)(2,1)} %collective-permute-done.4, pred[]{:T(512)S(6)} %ge.6), kind=kLoop, calls=%fused_computation | loop fusion | flops 1048576 | bytes 6291457 | tf_op jit(solution)/shard_map/jit(_where)/select_n | solution.py:368
  115.8 0.0 copy-start.5
  115.8 3.2 %constant_dynamic-update-slice_fusion.2.refs_0_ = bf16[8,128,2048]{2,1,0:T(8,128)(2,1)} fusion(bf16[8,128,2048]{2,1,0:T(8,128)(2,1)} %constant_dynamic-update-slice_fusion.3, bf16[4,128,2048]{2,1,0:T(8,128)(2,1)} %collective-permute-done.8), kind=kLoop, calls=%fused_computation.8 | loop fusion | bytes 4194304 | tf_op jit(solution)/shard_map/concatenate | solution.py:371
  119.0 1.3 constant_dynamic-slice_fusion
  120.3 1.2 copy.18
  121.5 4.5 %collective-permute-start.6 = (bf16[2048,192]{0,1:T(8,128)(2,1)}, bf16[2048,192]{0,1:T(8,128)(2,1)}, u32[]{:S(2)}, u32[]{:S(2)}) collective-permute-start(bf16[2048,192]{0,1:T(8,128)(2,1)} %copy.18), channel_id=1, source_target_pairs={{0,4},{12,8},{1,5},{13,9},{2,6},{14,10},{3,7},{15,11},{16,20},{28,... | collective-permute-start | bytes 2359304 | tf_op jit(solution)/shard_map/ppermute | solution.py:359
  126.1 0.1 copy.20.slot.refs_6_
  126.2 0.1 select_reduce_fusion
  126.3 1.3 collective-permute-start.14
  127.6 1.5 collective-permute-start.7
  129.1 13.9 %collective-permute-done.6 = bf16[2048,192]{0,1:T(8,128)(2,1)} collective-permute-done((bf16[2048,192]{0,1:T(8,128)(2,1)}, bf16[2048,192]{0,1:T(8,128)(2,1)}, u32[]{:S(2)}, u32[]{:S(2)}) %collective-permute-start.6) | collective-permute-done | bytes 786464 | tf_op jit(solution)/shard_map/ppermute | solution.py:359
  142.9 1.4 copy.19.other_down
  144.4 1.0 copy-done.3
  145.4 13.0 %shard_map.93 = (f32[512,2048]{1,0:T(8,128)}, f32[512,32]{1,0:T(8,128)S(1)}, f32[512,32]{1,0:T(8,128)S(1)}) custom-call(s32[2]{0:T(128)S(1)} %iota_add_fusion.1.start, bf16[512,1024]{1,0:T(8,128)(2,1)S(1)} %get-tuple-element.38.first, bf16[512,1024]{1,0:T(8,128)(2,1)S(1)} %get-tuple-element.37.second, bf16[8192,2048]{1,0:T(8,128)(2,1)} %weight.3, ...), custom_call_target="tpu_custom_call" | custom-call | flops 5100273664 | bytes 20447232 | tf_op jit(solution)/shard_map/pallas_call | solution.py:166
  158.4 1.3 collective-permute-start.10
  159.7 21.8 %collective-permute-done.10 = f32[512,32]{1,0:T(8,128)S(1)} collective-permute-done((f32[512,32]{1,0:T(8,128)S(1)}, f32[512,32]{1,0:T(8,128)S(1)}, u32[]{:S(2)}, u32[]{:S(2)}) %collective-permute-start.10) | collective-permute-done | bytes 65568 | tf_op jit(solution)/shard_map/ppermute | solution.py:375
  181.6 0.1 select_convert_fusion.refs_2_
  181.7 0.5 collective-permute-start.11
  182.2 0.6 collective-permute-start.12
  182.8 4.4 %collective-permute-done.11.refs_3_ = bf16[512,32]{1,0:T(8,128)(2,1)S(1)} collective-permute-done((bf16[512,32]{1,0:T(8,128)(2,1)S(1)}, bf16[512,32]{1,0:T(8,128)(2,1)S(1)}, u32[]{:S(2)}, u32[]{:S(2)}) %collective-permute-start.11) | collective-permute-done | bytes 32800 | tf_op jit(solution)/shard_map/ppermute | solution.py:379
  187.2 2.9 %collective-permute-start.13 = (bf16[512,32]{1,0:T(8,128)(2,1)S(1)}, bf16[512,32]{1,0:T(8,128)(2,1)S(1)}, u32[]{:S(2)}, u32[]{:S(2)}) collective-permute-start(bf16[512,32]{1,0:T(8,128)(2,1)S(1)} %select_convert_fusion.refs_2_), channel_id=1, source_target_pairs={{0,4},{4,8},{8,12},{12,0},{1,5},{5,9},{9,13},{13,1},{2,6},{6,10},{... | collective-permute-start | bytes 98312 | tf_op jit(solution)/shard_map/ppermute | solution.py:379
  190.0 0.1 pad_add_fusion.facts
  190.1 4.0 %collective-permute-done.12.refs_4_ = bf16[512,32]{1,0:T(8,128)(2,1)S(1)} collective-permute-done((bf16[512,32]{1,0:T(8,128)(2,1)S(1)}, bf16[512,32]{1,0:T(8,128)(2,1)S(1)}, u32[]{:S(2)}, u32[]{:S(2)}) %collective-permute-start.12) | collective-permute-done | bytes 32800 | tf_op jit(solution)/shard_map/ppermute | solution.py:379
  194.2 2.2 %copy-done.1 = f32[512,2048]{1,0:T(8,128)S(1)} copy-done((f32[512,2048]{1,0:T(8,128)S(1)}, f32[512,2048]{1,0:T(8,128)}, u32[]{:S(2)}) %copy-start.1) | copy-done | bytes 4194328
  196.3 6.7 %shard_map.94 = (f32[512,2048]{1,0:T(8,128)S(1)}, bf16[1024,2048]{1,0:T(8,128)(2,1)S(1)}) custom-call(s32[3]{0:T(128)S(1)} %pad_add_fusion.facts, s32[6]{0:T(128)S(1)} %fusion.1.places, f32[512,2048]{1,0:T(8,128)S(1)} %copy-done.1, bf16[512,1024]{1,0:T(8,128)(2,1)} %collective-permute-done.7.third, bf16[8192,2048]{1,0:T(8,128)(2,1)} %weight.3, ...), custom_call_target="tpu_custom_call" | custom-call | flops 3758096384 | bytes 15728640 | tf_op jit(solution)/shard_map/pallas_call | solution.py:249
  203.1 5.1 %shard_map.95 = bf16[512,2048]{1,0:T(8,128)(2,1)} custom-call(s32[3]{0:T(128)S(1)} %pad_add_fusion.facts, f32[512,2048]{1,0:T(8,128)S(1)} %get-tuple-element.30.total, bf16[1024,2048]{1,0:T(8,128)(2,1)S(1)} %get-tuple-element.31.weight, bf16[512,1024]{1,0:T(8,128)(2,1)} %collective-permute-done.14.x), custom_call_target="tpu_custom_call" | custom-call | flops 2147483648 | bytes 2097152 | tf_op jit(solution)/shard_map/pallas_call | solution.py:286
  (34 shorter events, 0.1 us)
Async XLA Ops:
  0.0 57.9 %copy-start.9 = (s32[3]{0:T(128)S(1)}, s32[3]{0:T(128)}, u32[]{:S(2)}) copy-start(s32[3]{0:T(128)} %constant.71.clone) | copy-start | bytes 40
  0.0 62.6 %copy-start.7 = (s32[1,6]{1,0:T(1,128)S(1)}, s32[1,6]{1,0:T(1,128)}, u32[]{:S(2)}) copy-start(s32[1,6]{1,0:T(1,128)} %param.14) | copy-start | bytes 76
  0.0 62.6 %copy-start.8 = (s32[16]{0:T(128)S(1)}, s32[16]{0:T(128)}, u32[]{:S(2)}) copy-start(s32[16]{0:T(128)} %param.13) | copy-start | bytes 196
  0.0 62.6 %copy-start.6 = (s32[16]{0:T(128)S(1)}, s32[16]{0:T(128)}, u32[]{:S(2)}) copy-start(s32[16]{0:T(128)} %param.16) | copy-start | bytes 196
  0.0 50.3 %collective-permute-start = (bf16[512,2048]{1,0:T(8,128)(2,1)}, bf16[512,2048]{1,0:T(8,128)(2,1)S(1)}, u32[]{:S(2)}, u32[]{:S(2)}) collective-permute-start(bf16[512,2048]{1,0:T(8,128)(2,1)} %refs_0_.1), channel_id=1, source_target_pairs={{0,4},{4,8},{8,12},{1,5},{5,9},{9,13},{2,6},{6,10},{10,14},{3,7},{... | collective-permute-start | bytes 6291464 | tf_op jit(solution)/shard_map/ppermute | solution.py:347
  5.2 49.2 %collective-permute-start.1 = (bf16[512,2048]{1,0:T(8,128)(2,1)}, bf16[512,2048]{1,0:T(8,128)(2,1)S(1)}, u32[]{:S(2)}, u32[]{:S(2)}) collective-permute-start(bf16[512,2048]{1,0:T(8,128)(2,1)} %refs_0_.1), channel_id=1, source_target_pairs={{4,0},{8,4},{12,8},{5,1},{9,5},{13,9},{6,2},{10,6},{14,10},{7,3},{... | collective-permute-start | bytes 6291464 | tf_op jit(solution)/shard_map/ppermute | solution.py:348
  6.5 47.9 %collective-permute-start.2 = (bf16[4,32,8192]{2,1,0:T(8,128)(2,1)}, bf16[4,32,8192]{2,1,0:T(8,128)(2,1)S(1)}, u32[]{:S(2)}, u32[]{:S(2)}) collective-permute-start(bf16[4,32,8192]{2,1,0:T(8,128)(2,1)} %param.11), channel_id=1, source_target_pairs={{0,2},{1,3},{2,0},{3,1},{4,6},{5,7},{6,4},{7,5},{8,10},{9,11},{10,... | collective-permute-start | bytes 6291464 | tf_op jit(solution)/shard_map/ppermute | solution.py:339
  54.4 2.0 copy-start.10
  56.4 9.6 %collective-permute-start.3 = (bf16[8,32,8192]{2,1,0:T(8,128)(2,1)}, bf16[8,32,8192]{2,1,0:T(8,128)(2,1)}, u32[]{:S(2)}, u32[]{:S(2)}) collective-permute-start(bf16[8,32,8192]{2,1,0:T(8,128)(2,1)} %constant_dynamic-update-slice_fusion.refs_0_), channel_id=1, source_target_pairs={{0,1},{1,0},{2,3},{3,2},{4,5},{5,4},{6,7},{7,6},{8,9},{9,8},{10,11... | collective-permute-start | bytes 12582920 | tf_op jit(solution)/shard_map/ppermute | solution.py:339
  56.4 59.4 %collective-permute-start.8 = (bf16[4,128,2048]{2,1,0:T(8,128)(2,1)}, bf16[4,128,2048]{2,1,0:T(8,128)(2,1)}, u32[]{:S(2)}, u32[]{:S(2)}) collective-permute-start(bf16[4,128,2048]{2,1,0:T(8,128)(2,1)} %param.12), channel_id=1, source_target_pairs={{0,2},{1,3},{2,0},{3,1},{4,6},{5,7},{6,4},{7,5},{8,10},{9,11},{10,... | collective-permute-start | bytes 6291464 | tf_op jit(solution)/shard_map/ppermute | solution.py:339
  59.2 31.2 %collective-permute-start.4 = (bf16[512,2048]{1,0:T(8,128)(2,1)S(1)}, bf16[512,2048]{1,0:T(8,128)(2,1)}, u32[]{:S(2)}, u32[]{:S(2)}) collective-permute-start(bf16[512,2048]{1,0:T(8,128)(2,1)S(1)} %collective-permute-done.refs_1_), channel_id=1, source_target_pairs={{4,8},{8,12},{5,9},{9,13},{6,10},{10,14},{7,11},{11,15},{20,24},{2... | collective-permute-start | bytes 6291464 | tf_op jit(solution)/shard_map/ppermute | solution.py:352
  61.2 52.3 %collective-permute-start.5 = (bf16[512,2048]{1,0:T(8,128)(2,1)}, bf16[512,2048]{1,0:T(8,128)(2,1)}, u32[]{:S(2)}, u32[]{:S(2)}) collective-permute-start(bf16[512,2048]{1,0:T(8,128)(2,1)} %copy-done.10), channel_id=1, source_target_pairs={{4,0},{8,4},{5,1},{9,5},{6,2},{10,6},{7,3},{11,7},{20,16},{24,20},... | collective-permute-start | bytes 6291464 | tf_op jit(solution)/shard_map/ppermute | solution.py:353
  66.0 5.5 %copy-start.4 = (bf16[512,2048]{1,0:T(8,128)(2,1)S(1)}, bf16[512,2048]{1,0:T(8,128)(2,1)}, u32[]{:S(2)}) copy-start(bf16[512,2048]{1,0:T(8,128)(2,1)} %refs_0_.1) | copy-start | bytes 6291460
  69.6 1.9 copy-start
  90.4 28.6 %copy-start.2 = (f32[512,192]{1,0:T(8,128)}, f32[512,192]{1,0:T(8,128)S(1)}, u32[]{:S(2)}) copy-start(f32[512,192]{1,0:T(8,128)S(1)} %get-tuple-element.23.low_in) | copy-start | bytes 1179652
  115.8 10.2 %copy-start.5 = (s32[512]{0:T(512)S(1)}, s32[512]{0:T(512)}, u32[]{:S(2)}) copy-start(s32[512]{0:T(512)} %param.15) | copy-start | bytes 6148
  119.0 75.1 %collective-permute-start.9 = (bf16[8,128,2048]{2,1,0:T(8,128)(2,1)}, bf16[8,128,2048]{2,1,0:T(8,128)(2,1)}, u32[]{:S(2)}, u32[]{:S(2)}) collective-permute-start(bf16[8,128,2048]{2,1,0:T(8,128)(2,1)} %constant_dynamic-update-slice_fusion.2.refs_0_), channel_id=1, source_target_pairs={{0,1},{1,0},{2,3},{3,2},{4,5},{5,4},{6,7},{7,6},{8,9},{9,8},{10,11... | collective-permute-start | bytes 12582920 | tf_op jit(solution)/shard_map/ppermute | solution.py:339
  121.5 21.4 %collective-permute-start.6 = (bf16[2048,192]{0,1:T(8,128)(2,1)}, bf16[2048,192]{0,1:T(8,128)(2,1)}, u32[]{:S(2)}, u32[]{:S(2)}) collective-permute-start(bf16[2048,192]{0,1:T(8,128)(2,1)} %copy.18), channel_id=1, source_target_pairs={{0,4},{12,8},{1,5},{13,9},{2,6},{14,10},{3,7},{15,11},{16,20},{28,... | collective-permute-start | bytes 2359304 | tf_op jit(solution)/shard_map/ppermute | solution.py:359
  126.3 76.7 %collective-permute-start.14 = (bf16[512,1024]{1,0:T(8,128)(2,1)S(1)}, bf16[512,1024]{1,0:T(8,128)(2,1)}, u32[]{:S(2)}, u32[]{:S(2)}) collective-permute-start(bf16[512,1024]{1,0:T(8,128)(2,1)S(1)} %get-tuple-element.37.second), channel_id=1, source_target_pairs={{8,12},{4,0},{9,13},{5,1},{10,14},{6,2},{11,15},{7,3},{24,28},{20,... | collective-permute-start | bytes 3145736 | tf_op jit(solution)/shard_map/ppermute | solution.py:369
  127.6 66.5 %collective-permute-start.7 = (bf16[512,1024]{1,0:T(8,128)(2,1)S(1)}, bf16[512,1024]{1,0:T(8,128)(2,1)}, u32[]{:S(2)}, u32[]{:S(2)}) collective-permute-start(bf16[512,1024]{1,0:T(8,128)(2,1)S(1)} %get-tuple-element.38.first), channel_id=1, source_target_pairs={{8,12},{4,0},{9,13},{5,1},{10,14},{6,2},{11,15},{7,3},{24,28},{20,... | collective-permute-start | bytes 3145736 | tf_op jit(solution)/shard_map/ppermute | solution.py:367
  144.4 1.0 copy-start.3
  158.4 23.1 %collective-permute-start.10 = (f32[512,32]{1,0:T(8,128)S(1)}, f32[512,32]{1,0:T(8,128)S(1)}, u32[]{:S(2)}, u32[]{:S(2)}) collective-permute-start(f32[512,32]{1,0:T(8,128)S(1)} %get-tuple-element.27), channel_id=1, source_target_pairs={{4,0},{8,12},{5,1},{9,13},{6,2},{10,14},{7,3},{11,15},{20,16},{24,... | collective-permute-start | bytes 196616 | tf_op jit(solution)/shard_map/ppermute | solution.py:375
  181.7 5.5 %collective-permute-start.11 = (bf16[512,32]{1,0:T(8,128)(2,1)S(1)}, bf16[512,32]{1,0:T(8,128)(2,1)S(1)}, u32[]{:S(2)}, u32[]{:S(2)}) collective-permute-start(bf16[512,32]{1,0:T(8,128)(2,1)S(1)} %select_convert_fusion.refs_2_), channel_id=1, source_target_pairs={{0,12},{4,0},{8,4},{12,8},{1,13},{5,1},{9,5},{13,9},{2,14},{6,2},{... | collective-permute-start | bytes 98312 | tf_op jit(solution)/shard_map/ppermute | solution.py:379
  182.2 11.9 %collective-permute-start.12 = (bf16[512,32]{1,0:T(8,128)(2,1)S(1)}, bf16[512,32]{1,0:T(8,128)(2,1)S(1)}, u32[]{:S(2)}, u32[]{:S(2)}) collective-permute-start(bf16[512,32]{1,0:T(8,128)(2,1)S(1)} %select_convert_fusion.refs_2_), channel_id=1, source_target_pairs={{0,8},{4,12},{8,0},{12,4},{1,9},{5,13},{9,1},{13,5},{2,10},{6,14},... | collective-permute-start | bytes 98312 | tf_op jit(solution)/shard_map/ppermute | solution.py:379
  187.2 7.0 %collective-permute-start.13 = (bf16[512,32]{1,0:T(8,128)(2,1)S(1)}, bf16[512,32]{1,0:T(8,128)(2,1)S(1)}, u32[]{:S(2)}, u32[]{:S(2)}) collective-permute-start(bf16[512,32]{1,0:T(8,128)(2,1)S(1)} %select_convert_fusion.refs_2_), channel_id=1, source_target_pairs={{0,4},{4,8},{8,12},{12,0},{1,5},{5,9},{9,13},{13,1},{2,6},{6,10},{... | collective-permute-start | bytes 98312 | tf_op jit(solution)/shard_map/ppermute | solution.py:379
  194.2 2.2 %copy-start.1 = (f32[512,2048]{1,0:T(8,128)S(1)}, f32[512,2048]{1,0:T(8,128)}, u32[]{:S(2)}) copy-start(f32[512,2048]{1,0:T(8,128)} %get-tuple-element.24.base) | copy-start | bytes 12582916

commit v12 on v11

v12 whole, which is shorter than its diff:
```python
import functools

import jax
import jax.numpy as jnp
from jax import lax
from jax.experimental import pallas as pl
from jax.experimental.pallas import tpu as pltpu
from jax.sharding import PartitionSpec as P

PARAMS = pltpu.CompilerParams(vmem_limit_bytes=48 * 2**20)
TAIL_PARAMS = pltpu.CompilerParams(vmem_limit_bytes=24 * 2**20)
F32 = jnp.float32
BF16 = jnp.bfloat16


def start_pages(places, blocks, length, targets, sems, rows_of):
    for e, target in enumerate(targets):
        for j, block in enumerate(blocks):

            @pl.when(places[e] // length == j)
            def _():
                pltpu.make_async_copy(rows_of(block.at[lax.rem(places[e], length)]), target, sems[e]).start()


def join_downs_kernel(places, *refs):
    *blocks, out, held, sems = refs
    length, rank_part, _ = blocks[0].shape
    shards, slots, width = held.shape
    step = pl.program_id(0)

    def targets(t):
        return [held.at[t, pl.ds(e * rank_part, rank_part)] for e in range(slots // rank_part)]

    @pl.when(step == 0)
    def _():
        for t in range(shards):
            semaphores = [sems.at[t, e] for e in range(slots // rank_part)]
            start_pages(
                places, blocks, length, targets(t), semaphores, lambda page: page.at[:, pl.ds(t * width, width)]
            )

    for t in range(shards):

        @pl.when(step == t)
        def _():
            for e, target in enumerate(targets(t)):
                source = blocks[0].at[0, :, pl.ds(t * width, width)]
                pltpu.make_async_copy(source, target, sems.at[t, e]).wait()
            out[...] = held[t].T


def join_downs(places, blocks, shards):
    entries = places.shape[0]
    _, rank_part, features = blocks[0].shape
    width, slots = features // shards, entries * rank_part
    return pl.pallas_call(
        join_downs_kernel,
        out_shape=jax.ShapeDtypeStruct((features, slots), BF16),
        grid=(shards,),
        in_specs=[pl.BlockSpec(memory_space=pltpu.SMEM)] + [pl.BlockSpec(memory_space=pltpu.HBM)] * len(blocks),
        out_specs=pl.BlockSpec((width, slots), lambda t: (t, 0)),
        scratch_shapes=[pltpu.VMEM((shards, slots, width), BF16), pltpu.SemaphoreType.DMA((shards, entries))],
        compiler_params=TAIL_PARAMS,
        cost_estimate=pl.CostEstimate(flops=0, bytes_accessed=4 * features * slots, transcendentals=0),
    )(places, *blocks)


RESIDENT = pl.BlockSpec(memory_space=pltpu.VMEM)
IN_HBM = pl.BlockSpec(memory_space=pltpu.HBM)


def fold_entry(low, slot, rank_part):
    lane = lax.broadcasted_iota(jnp.int32, low.shape, 1)
    own = jnp.where(lane // rank_part == slot, low, 0.0)
    shape = (low.shape[1], rank_part)
    fold = lax.rem(lax.broadcasted_iota(jnp.int32, shape, 0), rank_part) == lax.broadcasted_iota(jnp.int32, shape, 1)
    return jnp.dot(own, fold.astype(F32), precision=lax.Precision.HIGHEST, preferred_element_type=F32)


def shards_kernel(with_low, start, valid, *refs):
    refs = list(refs)
    xs = [refs.pop(0) for _ in range(valid.shape[0])]
    weight = refs.pop(0)
    if with_low:
        down, slot, base, low, acc = refs
    else:
        base_in, base = refs
    step = pl.program_id(0)

    @pl.when(step == 0)
    def _():
        base[...] = jnp.zeros_like(base) if with_low else base_in[...]
        if with_low:
            acc[...] = jnp.zeros_like(acc)

    for i, x in enumerate(xs):

        @pl.when((step // 2 == i) & (valid[i] != 0))
        def _():
            part = min(base.shape[1], 512)
            for n in range(0, base.shape[1], part):
                base[:, n:n + part] += jnp.dot(x[...], weight[:, n:n + part], preferred_element_type=F32)
            if with_low:
                acc[...] += jnp.dot(x[...], down[...], preferred_element_type=F32)

    if with_low:

        @pl.when(step == pl.num_programs(0) - 1)
        def _():
            low[...] = fold_entry(acc[...], slot[...], low.shape[1])


def add_shards(base, xs, source, weight, down=None, slot=None, rank_part=0):
    rows, width = xs[0].shape
    half = width // 2
    columns = weight.shape[1]
    n_tensor = weight.shape[0] // width
    there = (source >= 0) & (source < n_tensor)
    start = 2 * jnp.clip(source, 0, n_tensor - 1)[:, None] + jnp.arange(2)[None, :]
    idle = jnp.concatenate([start[1:2, :1], start[:-1, 1:]], axis=0)
    start = jnp.where(there[:, None], start, idle).reshape(-1).astype(jnp.int32)
    steps = 2 * len(xs)

    def whole(a):
        return pl.BlockSpec((rows, a), lambda s, *_: (0, 0))

    def walked(a):
        return pl.BlockSpec((half, a.shape[1]), lambda s, start, valid: (start[s], 0))

    in_specs = [
        pl.BlockSpec((rows, half), lambda s, *_, i=i: (0, jnp.clip(s - 2 * i, 0, 1))) for i in range(len(xs))
    ] + [walked(weight)]
    out_shape = [jax.ShapeDtypeStruct((rows, columns), F32)]
    scratch = []
    slots = 0
    if base is None:
        slots = down.shape[1]
        in_specs += [walked(down), whole(1)]
        out_shape += [jax.ShapeDtypeStruct((rows, rank_part), F32)]
        scratch = [pltpu.VMEM((rows, slots), F32)]
        rest = (down, slot)
    else:
        in_specs += [whole(columns)]
        rest = (base,)
    return pl.pallas_call(
        functools.partial(shards_kernel, base is None),
        out_shape=out_shape,
        grid_spec=pltpu.PrefetchScalarGridSpec(
            num_scalar_prefetch=2,
            grid=(steps,),
            in_specs=in_specs,
            out_specs=[whole(a.shape[1]) for a in out_shape],
            scratch_shapes=scratch,
        ),
        compiler_params=PARAMS,
        cost_estimate=pl.CostEstimate(
            flops=2 * steps * half * rows * (columns + slots),
            bytes_accessed=2 * steps * half * (rows + columns + slots) + 8 * rows * columns,
            transcendentals=0,
        ),
    )(start, there.astype(jnp.int32), *xs, weight, *rest)


def half_kernel(start, valid, x, weight, base_in, base):
    step = pl.program_id(0)

    @pl.when(step == 0)
    def _():
        base[...] = base_in[...]

    @pl.when(valid[0] != 0)
    def _():
        part = min(base.shape[1], 512)
        for n in range(0, base.shape[1], part):
            base[:, n:n + part] += jnp.dot(x[...], weight[:, n:n + part], preferred_element_type=F32)


def add_half(base, x, valid, source, weight):
    rows, half = x.shape
    columns = weight.shape[1]
    step = half // 2
    whole = pl.BlockSpec((rows, columns), lambda s, *_: (0, 0))
    return pl.pallas_call(
        half_kernel,
        out_shape=jax.ShapeDtypeStruct((rows, columns), F32),
        grid_spec=pltpu.PrefetchScalarGridSpec(
            num_scalar_prefetch=2,
            grid=(2,),
            in_specs=[
                pl.BlockSpec((rows, step), lambda s, *_: (0, s)),
                pl.BlockSpec((step, columns), lambda s, source, valid: (source[0] * 4 + s, 0)),
                whole,
            ],
            out_specs=whole,
        ),
        compiler_params=PARAMS,
        cost_estimate=pl.CostEstimate(
            flops=2 * half * rows * columns,
            bytes_accessed=2 * half * (rows + columns) + 8 * rows * columns,
            transcendentals=0,
        ),
    )(source[None], valid[None], x, weight, base)


def far_low_kernel(
    facts, left_1, left_2, right_1, right_2, down, other_down, slot, row_rank, low, other_low,
    out, near_x, far_x, rows_of, other_rows, sems
):
    me, end, source, upper = facts[0], facts[1], facts[2], facts[3]
    width = far_x.shape[1]
    rank_part = low.shape[1]
    start = pl.multiple_of(source * width, width)

    @pl.when(upper != 0)
    def _():
        pltpu.make_async_copy(left_2, far_x, sems.at[0]).start()
        pltpu.make_async_copy(left_1, near_x, sems.at[1]).start()

    @pl.when(upper == 0)
    def _():
        pltpu.make_async_copy(right_2, far_x, sems.at[0]).start()
        pltpu.make_async_copy(right_1, near_x, sems.at[1]).start()

    copies = [
        pltpu.make_async_copy(down.at[pl.ds(start, width)], rows_of, sems.at[2]),
        pltpu.make_async_copy(other_down, other_rows, sems.at[3]),
    ]
    for copy in copies:
        copy.start()
    pltpu.make_async_copy(left_2, far_x, sems.at[0]).wait()

    def finished(total, sums, place):
        sums = total[...] + fold_entry(sums, slot[...], rank_part)
        k = lax.broadcasted_iota(jnp.int32, sums.shape, 1) + place * rank_part
        return jnp.where(k < row_rank[...], sums, 0.0)

    copies[0].wait()
    own = finished(low, jnp.dot(far_x[...], rows_of[...], preferred_element_type=F32), me)
    pltpu.make_async_copy(left_1, near_x, sems.at[1]).wait()
    copies[1].wait()
    far_rows = other_rows[pl.ds(pl.multiple_of((1 - upper) * width, width), width)]
    near_rows = other_rows[pl.ds(pl.multiple_of(upper * width, width), width)]
    sums = jnp.dot(far_x[...], far_rows, preferred_element_type=F32)
    sums += jnp.dot(near_x[...], near_rows, preferred_element_type=F32)
    other = finished(other_low, sums, end)
    at_left = jnp.concatenate([other, own], axis=1)
    at_right = jnp.concatenate([own, other], axis=1)
    out[...] = jnp.where(upper != 0, at_right, at_left).astype(BF16)


def far_low(facts, left_1, left_2, right_1, right_2, down, other_down, slot, row_rank, low, other_low):
    rows, width = left_1.shape
    slots = down.shape[1]
    return pl.pallas_call(
        far_low_kernel,
        out_shape=jax.ShapeDtypeStruct((rows, 2 * low.shape[1]), BF16),
        in_specs=[pl.BlockSpec(memory_space=pltpu.SMEM)] + [IN_HBM] * 6 + [RESIDENT] * 4,
        out_specs=RESIDENT,
        scratch_shapes=[
            pltpu.VMEM((rows, width), BF16),
            pltpu.VMEM((rows, width), BF16),
            pltpu.VMEM((width, slots), BF16),
            pltpu.VMEM((2 * width, slots), BF16),
            pltpu.SemaphoreType.DMA((4,)),
        ],
        compiler_params=TAIL_PARAMS,
        cost_estimate=pl.CostEstimate(
            flops=6 * width * rows * slots, bytes_accessed=2 * width * (2 * rows + 3 * slots), transcendentals=0
        ),
    )(facts, left_1, left_2, right_1, right_2, down, other_down, slot, row_rank, low, other_low)


def prepare_kernel(facts, places, base, sent, received, weight, *refs):
    *blocks, slot, total, last_rows, mid, mid_rows, up, spread, sems = refs
    mid_width, last_width = mid_rows.shape[0], last_rows.shape[0]
    width = mid_width + last_width
    length, rank, _ = blocks[0].shape
    count = up.shape[0] // rank
    which, start = facts[0], facts[1] * 2 * width + width
    part = min(total.shape[1], 512)

    def rows_at(first, length):
        return weight.at[pl.ds(pl.multiple_of(start + first, length), length)]

    to_total = pltpu.make_async_copy(base, total, sems.at[0])
    to_mid_rows = pltpu.make_async_copy(rows_at(0, mid_width), mid_rows, sems.at[1])
    to_last = pltpu.make_async_copy(rows_at(mid_width, last_width), last_rows, sems.at[2])
    pages = [up.at[pl.ds(e * rank, rank)] for e in range(count)]
    page_sems = [sems.at[4 + e] for e in range(count)]

    @pl.when(which == 0)
    def _():
        pltpu.make_async_copy(sent, mid, sems.at[3]).start()

    @pl.when(which != 0)
    def _():
        pltpu.make_async_copy(received, mid, sems.at[3]).start()

    to_total.start()
    start_pages(places, blocks, length, pages, page_sems, lambda page: page)

    @pl.when(which != 0)
    def _():
        to_mid_rows.start()
        to_last.start()

    pltpu.make_async_copy(sent, mid, sems.at[3]).wait()
    for e in range(count):
        spread[:, e * rank:(e + 1) * rank] = jnp.where(
            slot[...] == e, mid[:, mid_width:].astype(F32), 0.0
        ).astype(BF16)
    for page, sem in zip(pages, page_sems):
        pltpu.make_async_copy(blocks[0].at[0], page, sem).wait()
    to_total.wait()
    for n in range(0, total.shape[1], part):
        cut = slice(n, n + part)
        total[:, cut] += jnp.dot(spread[...], up[:, cut], preferred_element_type=F32)

    @pl.when(which != 0)
    def _():
        to_mid_rows.wait()
        for n in range(0, total.shape[1], part):
            cut = slice(n, n + part)
            total[:, cut] += jnp.dot(mid[:, :mid_width], mid_rows[:, cut], preferred_element_type=F32)
        to_last.wait()


def prepare(facts, places, base, sent, received, weight, blocks, slot):
    rows, columns = base.shape
    rank = blocks[0].shape[1]
    entries = places.shape[0]
    mid_width = sent.shape[1] - rank
    last_width = mid_width
    return pl.pallas_call(
        prepare_kernel,
        out_shape=[pltpu.VMEM((rows, columns), F32), pltpu.VMEM((last_width, columns), BF16)],
        in_specs=[pl.BlockSpec(memory_space=pltpu.SMEM)] * 2 + [IN_HBM] * (4 + len(blocks)) + [RESIDENT],
        out_specs=[RESIDENT] * 2,
        scratch_shapes=[
            pltpu.VMEM(sent.shape, BF16),
            pltpu.VMEM((mid_width, columns), BF16),
            pltpu.VMEM((entries * rank, columns), BF16),
            pltpu.VMEM((rows, entries * rank), BF16),
            pltpu.SemaphoreType.DMA((4 + entries,)),
        ],
        compiler_params=TAIL_PARAMS,
        cost_estimate=pl.CostEstimate(
            flops=2 * (mid_width + entries * rank) * rows * columns,
            bytes_accessed=2 * (columns + entries * rank + 2 * rows) * columns,
            transcendentals=0,
        ),
    )(facts, places, base, sent, received, weight, *blocks, slot)


def last_kernel(facts, total, weight, x, out):
    part = out.shape[1]
    cut = pl.ds(pl.multiple_of(pl.program_id(0) * part, part), part)

    @pl.when(facts[0] != 0)
    def _():
        out[...] = (total[:, cut] + jnp.dot(x[...], weight[:, cut], preferred_element_type=F32)).astype(BF16)

    @pl.when(facts[0] == 0)
    def _():
        out[...] = total[:, cut].astype(BF16)


def add_last(facts, total, weight, x):
    rows, columns = total.shape
    part = min(columns, 512)
    return pl.pallas_call(
        last_kernel,
        out_shape=jax.ShapeDtypeStruct((rows, columns), BF16),
        grid=(columns // part,),
        in_specs=[pl.BlockSpec(memory_space=pltpu.SMEM), RESIDENT, RESIDENT, pl.BlockSpec(x.shape, lambda n: (0, 0))],
        out_specs=pl.BlockSpec((rows, part), lambda n: (0, n)),
        compiler_params=TAIL_PARAMS,
        cost_estimate=pl.CostEstimate(
            flops=2 * x.shape[1] * rows * columns, bytes_accessed=2 * rows * columns, transcendentals=0
        ),
    )(facts, total, weight, x)


def after(value, *earlier):
    return lax.optimization_barrier((value,) + earlier)[0]


def looked_up(table, ids):
    hit = ids[:, None] == jnp.arange(table.shape[0])[None, :]
    return jnp.sum(jnp.where(hit, table[None, :], 0), axis=1)


def local(
    attention_result,
    output_weight,
    adapter_down_weight,
    adapter_up_weight,
    adapter_page_row,
    requests,
    row_request_entry,
    ranks,
):
    n_dp = lax.axis_size("dp")
    n_tensor = lax.axis_size("tensor")
    me = lax.axis_index("tensor")
    rows, width = attention_result.shape
    holder_length, rank_part, _ = adapter_down_weight.shape
    rank, columns = adapter_up_weight.shape[1:]
    own_list = requests[0]
    entries = own_list.shape[0]
    one_hot = row_request_entry[:, None] == jnp.arange(entries)[None, :]
    row_rank = jnp.sum(jnp.where(one_hot, looked_up(ranks, own_list)[None, :], 0), axis=1)
    pages = looked_up(adapter_page_row, own_list)
    places = ((pages // holder_length) ^ lax.axis_index("dp")) * holder_length + pages % holder_length
    if n_tensor != 4 or n_dp != 4 or width % 512 or columns != width or rank_part % 16 or entries * rank_part > 256:
        return plain(
            attention_result, output_weight, adapter_down_weight, adapter_up_weight, places, one_hot, row_rank
        )


    def across(x, distance):
        return lax.ppermute(x, "dp", [(i, i ^ distance) for i in range(n_dp)])

    right = [(i, i + 1) for i in range(n_tensor - 1)]
    left = [(i + 1, i) for i in range(n_tensor - 1)]
    upper = me >= n_tensor // 2
    ends = me * (n_tensor - 1 - me) == 0
    slot = row_request_entry[:, None]

    right_1 = lax.ppermute(attention_result, "tensor", right)
    left_1 = lax.ppermute(attention_result, "tensor", left)
    far_down = across(adapter_down_weight, 2)
    far_up = across(adapter_up_weight, 2)
    near_down = across(adapter_down_weight, 1)

    right_2 = lax.ppermute(right_1, "tensor", right[1:])
    left_2 = lax.ppermute(left_1, "tensor", left[:-1])
    downs = (adapter_down_weight, near_down, far_down, across(after(far_down, right_1, left_1), 1))
    down = join_downs(places, downs, n_tensor)
    farthest = jnp.where(upper, 0, n_tensor - 1)
    other_down = lax.dynamic_slice_in_dim(down, jnp.where(upper, 0, 2 * width), 2 * width, 0)
    other_down = lax.ppermute(other_down, "tensor", [(0, 1), (3, 2)])

    near = me + jnp.array([0, -1, 1], jnp.int32)
    base, low = add_shards(
        None, [attention_result, right_1, left_1], near, output_weight, down, slot, rank_part
    )
    other_low = lax.ppermute(low, "tensor", [(0, 1), (3, 2)])

    right_2, left_2, other_down, other_low = lax.optimization_barrier((right_2, left_2, other_down, other_low))
    third = right[-1:] + left[:1]
    cuts = (0, width // 2, width // 4 * 3, width)

    def piece(i):
        cut = slice(cuts[i], cuts[i + 1])
        return jnp.where(upper, right_2[:, cut], left_2[:, cut])

    first_2 = piece(0)
    first_3 = lax.ppermute(first_2, "tensor", third)
    right_2, left_2 = lax.optimization_barrier((first_2, right_2, left_2))[1:]
    end = jnp.where(upper, n_tensor - 1, 0)
    source = jnp.where(upper, me - 2, me + 2)
    pair = far_low(
        jnp.stack([me, end, source, upper.astype(jnp.int32)]).astype(jnp.int32),
        right_1, right_2, left_1, left_2, down, other_down, slot, row_rank[:, None], low, other_low,
    )
    from_middle = lax.ppermute(pair, "tensor", [(1, 2), (2, 1)])
    far = me + jnp.array([-2, 2], jnp.int32)
    base, = add_shards(after(base, pair), [right_2, left_2], far, output_weight)
    low = jnp.where(upper, jnp.concatenate([from_middle, pair], axis=1), jnp.concatenate([pair, from_middle], axis=1))
    second_2 = jnp.concatenate([piece(1), low], axis=1)
    second_3 = lax.ppermute(second_2, "tensor", third)
    right_2, left_2 = lax.optimization_barrier((second_2, right_2, left_2))[1:]
    last_3 = lax.ppermute(piece(2), "tensor", third)
    ups = (adapter_up_weight, across(after(adapter_up_weight, far_down), 1), far_up, across(after(far_up, first_2), 1))
    facts = jnp.stack([ends.astype(jnp.int32), farthest]).astype(jnp.int32)
    base = add_half(base, first_3, facts[0], facts[1], output_weight)
    total, rows_of = prepare(facts, places, base, second_2, second_3, output_weight, ups, slot)
    total, rows_of, last_3 = lax.optimization_barrier((total, rows_of, last_3))
    return add_last(facts, total, rows_of, last_3)


def gather_pages(block, n_dp):
    return [block] + [
        lax.ppermute(block, "dp", [(i, i ^ j) for i in range(n_dp)]) for j in range(1, n_dp)
    ]


def plain(x, output_weight, down_weight, up_weight, places, one_hot, row_rank):
    n_dp = lax.axis_size("dp")
    rows = x.shape[0]
    rank, columns = up_weight.shape[1:]
    entries = one_hot.shape[1]

    def requested(block):
        blocks = jnp.concatenate(gather_pages(block, n_dp), axis=0)
        return jnp.concatenate(
            [lax.dynamic_slice_in_dim(blocks, places[e], 1, 0) for e in range(entries)], axis=0
        )

    down, up = requested(down_weight), requested(up_weight)
    x = lax.all_gather(x, "tensor", axis=1, tiled=True)
    base = jnp.dot(x, output_weight, preferred_element_type=F32)
    low = jnp.einsum("rd,ekd->rek", x, down, preferred_element_type=F32)
    low = jnp.sum(jnp.where(one_hot[:, :, None], low, 0.0), axis=1).astype(BF16)
    low = lax.all_gather(low, "tensor", axis=1, tiled=True)
    low = jnp.where(jnp.arange(rank)[None, :] < row_rank[:, None], low, jnp.zeros_like(low))
    spread = jnp.where(one_hot[:, :, None], low[:, None, :], jnp.zeros((), BF16))
    term = jnp.dot(
        spread.reshape(rows, entries * rank), up.reshape(entries * rank, columns), preferred_element_type=F32
    )
    return (base + term).astype(BF16)


def solution(mesh):
    in_specs = (
        P(("groups", "dp"), "tensor"),
        P(None, "tensor"),
        P("dp", "tensor", None),
        P("dp", None, "tensor"),
        P("groups"),
        P(("groups", "dp"), None),
        P(("groups", "dp")),
        P(),
    )
    out_specs = P(("groups", "dp"), "tensor")
    return jax.shard_map(local, mesh=mesh, in_specs=in_specs, out_specs=out_specs, check_vma=False)
```

time: 209 us -> 207 us (level)
  waiting for transfers between devices: 110 us -> 86.9 us
  Pallas kernels: 47.2 us -> 56.6 us
  other arithmetic: 3.55 us -> 10.8 us
  local copies, waits for them, and re-layouts: 21.5 us -> 23.8 us
  starting transfers between devices: 25.3 us -> 27.5 us
    ppermute x1, waiting for transfers between devices: 23 us -> 4.27 us  [local(): left_2 = lax.ppermute(left_1, 'tensor', left[:-1])]
    ppermute x1, waiting for transfers between devices: 13.9 us -> 0.01 us  [local(): other_down = lax.ppermute(other_down, 'tensor', [(0, 1), (3, 2)])]
    pallas_call x2 -> x4, Pallas kernels: 31.8 us -> 43.7 us  [the longest x2 31.1 us: add_shards(): pl.pallas_call(functools.partial(shards_kernel, base is None), out_shape=...]
    ppermute x6 -> x5, waiting for transfers between devices: 30.3 us -> 35.7 us  [the longest x1 14.6 us: local(): first_3 = lax.ppermute(first_2, 'tensor', third)]
    concatenate x2 -> x0, local copies, waits for them, and re-layouts: 4.79 us -> none  [the longest x1 3.17 us: local(): ups = jnp.concatenate([adapter_up_weight, after(far_up, second_2)], axis=0)]
    ppermute x1, starting transfers between devices: 4.52 us -> 9.08 us  [local(): other_down = lax.ppermute(other_down, 'tensor', [(0, 1), (3, 2)])]
    optimization_barrier x0 -> x1, local copies, waits for them, and re-layouts: none -> 3.84 us  [local(): lax.optimization_barrier((right_2, left_2, other_down, other_low))]
    dynamic_slice x2, local copies, waits for them, and re-layouts: 2.53 us -> 5.43 us  [local(): lax.dynamic_slice_in_dim(down, jnp.where(upper, 0, 2 * width), 2 * width, 0)]
  transfers between devices with their start and end apart: 15 -> 16, of which waited for: 7 -> 8; matrix products, arithmetic and copies ran while one was open for 7% -> 11% of each run, Pallas kernels for 20% -> 26%
where the time goes in v12:
time: 207 us; the launch traced here: 206 us
  waiting for transfers between devices  86.9 us (42%)
  Pallas kernels  56.6 us (27%)
  starting transfers between devices  27.5 us (13%)
  local copies, waits for them, and re-layouts  23.8 us (11%)
  other arithmetic  10.8 us (5%)
    ppermute x1, waiting for transfers between devices, local(): right_1 = lax.ppermute(attention_result, 'tensor', right)  41.7 us
    pallas_call x2, Pallas kernels, add_shards(): pl.pallas_call(functools.partial(shards_kernel, base is None), out_shape=...  31.1 us
    ppermute x1, waiting for transfers between devices, local(): first_3 = lax.ppermute(first_2, 'tensor', third)  14.6 us
    unnamed x20, local copies, waits for them, and re-layouts  12.1 us
    ppermute x1, starting transfers between devices, local(): other_down = lax.ppermute(other_down, 'tensor', [(0, 1), (3, 2)])  9.08 us
    ppermute x1, waiting for transfers between devices, local(): second_3 = lax.ppermute(second_2, 'tensor', third)  8.32 us
    ppermute x1, waiting for transfers between devices, local(): other_low = lax.ppermute(low, 'tensor', [(0, 1), (3, 2)])  7.85 us
    pallas_call x1, Pallas kernels, far_low(): pl.pallas_call(far_low_kernel, out_shape=jax.ShapeDtypeStruct((rows, 2 *...  6.92 us
  transfers between devices with their start and end apart: 16, of which 8 were waited for; matrix products, arithmetic and copies ran while one was open for 11% of the time, Pallas kernels for 26%

profile of v12, /device:TPU:0, one launch (start us, length us, event | category | flops | bytes accessed | tf_op | source)
XLA Modules:
  0.0 205.7 jit_solution(15337838401178089719)
XLA Ops:
  0.0 5.1 %collective-permute-start = (bf16[512,2048]{1,0:T(8,128)(2,1)}, bf16[512,2048]{1,0:T(8,128)(2,1)S(1)}, u32[]{:S(2)}, u32[]{:S(2)}) collective-permute-start(bf16[512,2048]{1,0:T(8,128)(2,1)} %refs_0_.4), channel_id=1, source_target_pairs={{0,4},{4,8},{8,12},{1,5},{5,9},{9,13},{2,6},{6,10},{10,14},{3,7},{... | collective-permute-start | bytes 6291464 | tf_op jit(solution)/shard_map/ppermute | solution.py:430
  5.1 1.3 collective-permute-start.2
  6.4 1.6 collective-permute-start.5
  8.5 41.7 %collective-permute-done.refs_1_.left_1 = bf16[512,2048]{1,0:T(8,128)(2,1)S(1)} collective-permute-done((bf16[512,2048]{1,0:T(8,128)(2,1)}, bf16[512,2048]{1,0:T(8,128)(2,1)S(1)}, u32[]{:S(2)}, u32[]{:S(2)}) %collective-permute-start) | collective-permute-done | bytes 2097184 | tf_op jit(solution)/shard_map/ppermute | solution.py:430
  50.1 4.2 %collective-permute-done.2.refs_2_.right_1 = bf16[512,2048]{1,0:T(8,128)(2,1)} collective-permute-done((bf16[512,2048]{1,0:T(8,128)(2,1)}, bf16[512,2048]{1,0:T(8,128)(2,1)}, u32[]{:S(2)}, u32[]{:S(2)}) %collective-permute-start.2) | collective-permute-done | bytes 2097184 | tf_op jit(solution)/shard_map/ppermute | solution.py:431
  54.4 0.9 collective-permute-done.5.refs_2_
  55.3 0.7 fusion
  56.0 0.6 slice.30
  56.6 0.7 add_bitcast_fusion
  57.3 0.7 fusion.4
  58.1 0.8 copy.24.refs_5_.slot.refs_4_
  59.0 0.7 fusion.1
  60.3 1.3 add_reduce_fusion
  61.6 0.9 select_reduce_fusion.1
  62.5 0.7 fusion.3
  63.2 0.8 collective-permute-start.1
  64.0 1.3 collective-permute-start.3
  65.3 1.6 copy-done.3
  66.9 3.5 %shard_map.100.refs_4_.down = bf16[8192,192]{1,0:T(8,128)(2,1)S(1)} custom-call(s32[6]{0:T(128)S(1)} %fusion.2.places, bf16[4,32,8192]{2,1,0:T(8,128)(2,1)S(1)} %copy-done.3, bf16[4,32,8192]{2,1,0:T(8,128)(2,1)} %collective-permute-done.4.refs_1_, bf16[4,32,8192]{2,1,0:T(8,128)(2,1)} %collective-permute-done.5.refs_2_, ...), custom_call_target="tpu_custom_call" | custom-call | bytes 6291456 | tf_op jit(solution)/shard_map/pallas_call | solution.py:56
  70.4 1.9 copy-done
  72.4 1.5 constant_dynamic-slice_fusion
  73.9 3.9 %copy.22 = bf16[4096,192]{0,1:T(8,128)(2,1)} copy(bf16[4096,192]{1,0:T(8,128)(2,1)} %constant_dynamic-slice_fusion) | data formatting | bytes 3145728 | tf_op jit(solution)/shard_map/dynamic_slice | solution.py:441
  77.8 9.1 %collective-permute-start.7 = (bf16[4096,192]{0,1:T(8,128)(2,1)}, bf16[4096,192]{0,1:T(8,128)(2,1)}, u32[]{:S(2)}, u32[]{:S(2)}) collective-permute-start(bf16[4096,192]{0,1:T(8,128)(2,1)} %copy.22), channel_id=1, source_target_pairs={{0,4},{12,8},{1,5},{13,9},{2,6},{14,10},{3,7},{15,11},{16,20},{28,... | collective-permute-start | bytes 4718600 | tf_op jit(solution)/shard_map/ppermute | solution.py:442
  87.0 1.6 copy-done.6
  88.5 1.6 copy-done.8
  90.1 19.4 %shard_map.101 = (f32[512,2048]{1,0:T(8,128)}, f32[512,32]{1,0:T(8,128)S(1)}) custom-call(s32[6]{0:T(128)S(1)} %select_n.88.start, s32[3]{0:T(128)S(1)} %get-tuple-element.47.valid, bf16[512,2048]{1,0:T(8,128)(2,1)S(1)} %copy-done.8, bf16[512,2048]{1,0:T(8,128)(2,1)S(1)} %copy-done.6, bf16[512,2048]{1,0:T(8,128)(2,1)} %collective-permute-done.2.refs_2_.right_1, ...), custom_call_target="tpu_custom_call" | custom-call | flops 14092861440 | bytes 42205184 | tf_op jit(solution)/shard_map/pallas_call | solution.py:145
  109.6 3.3 %collective-permute-start.8 = (f32[512,32]{1,0:T(8,128)S(1)}, f32[512,32]{1,0:T(8,128)S(1)}, u32[]{:S(2)}, u32[]{:S(2)}) collective-permute-start(f32[512,32]{1,0:T(8,128)S(1)} %get-tuple-element.25.low), channel_id=1, source_target_pairs={{0,4},{12,8},{1,5},{13,9},{2,6},{14,10},{3,7},{15,11},{16,20},{28,... | collective-permute-start | bytes 196616 | tf_op jit(solution)/shard_map/ppermute | solution.py:448
  113.3 4.3 %collective-permute-done.3.right_2.refs_1_ = bf16[512,2048]{1,0:T(8,128)(2,1)} collective-permute-done((bf16[512,2048]{1,0:T(8,128)(2,1)}, bf16[512,2048]{1,0:T(8,128)(2,1)}, u32[]{:S(2)}, u32[]{:S(2)}) %collective-permute-start.3) | collective-permute-done | bytes 2097184 | tf_op jit(solution)/shard_map/ppermute | solution.py:437
  117.6 7.9 %collective-permute-done.8.other_low = f32[512,32]{1,0:T(8,128)S(1)} collective-permute-done((f32[512,32]{1,0:T(8,128)S(1)}, f32[512,32]{1,0:T(8,128)S(1)}, u32[]{:S(2)}, u32[]{:S(2)}) %collective-permute-start.8) | collective-permute-done | bytes 65568 | tf_op jit(solution)/shard_map/ppermute | solution.py:448
  125.4 2.3 %slice_select_fusion = bf16[512,1024]{1,0:T(8,128)(2,1)} fusion(bf16[512,2048]{1,0:T(8,128)(2,1)} %collective-permute-done.3.right_2.refs_1_, bf16[512,2048]{1,0:T(8,128)(2,1)S(1)} %collective-permute-done.1.left_2.refs_0_, pred[]{:T(512)S(6)} %ge.9), kind=kLoop, calls=%fused_computation | loop fusion | flops 524288 | bytes 3145729 | tf_op jit(solution)/shard_map/jit(_where)/select_n | solution.py:456
  127.9 3.8 %copy.25.other_down = bf16[4096,192]{1,0:T(8,128)(2,1)} copy(bf16[4096,192]{0,1:T(8,128)(2,1)} %collective-permute-done.7) | data formatting | bytes 3145728 | tf_op jit(solution)/shard_map/optimization_barrier | solution.py:450
  131.8 2.2 %copy-done.1 = bf16[8192,192]{1,0:T(8,128)(2,1)S(1)} copy-done((bf16[8192,192]{1,0:T(8,128)(2,1)S(1)}, bf16[8192,192]{1,0:T(8,128)(2,1)}, u32[]{:S(2)}) %copy-start.1) | copy-done | bytes 3145752
  134.0 1.6 copy-done.2
  135.6 1.6 copy-done.7
  137.2 6.9 %shard_map.102 = bf16[512,64]{1,0:T(8,128)(2,1)S(1)} custom-call(s32[4]{0:T(128)S(1)} %pad_add_fusion.1.facts, bf16[512,2048]{1,0:T(8,128)(2,1)S(1)} %copy-done.7, bf16[512,2048]{1,0:T(8,128)(2,1)S(1)} %collective-permute-done.1.left_2.refs_0_, bf16[512,2048]{1,0:T(8,128)(2,1)} %collective-permute-done.2.refs_2_.right_1, ...), custom_call_target="tpu_custom_call" | custom-call | flops 1207959552 | bytes 6553600 | tf_op jit(solution)/shard_map/pallas_call | solution.py:254
  144.1 0.7 collective-permute-start.10
  144.8 1.1 slice_select_fusion.2
  145.9 1.3 collective-permute-start.9
  147.4 1.3 collective-permute-start.11
  148.7 1.1 slice_select_fusion.1
  149.8 1.3 collective-permute-start.15
  151.1 11.6 %shard_map.103.base_in = f32[512,2048]{1,0:T(8,128)} custom-call(s32[4]{0:T(128)S(1)} %select_n.91.start, s32[2]{0:T(128)S(1)} %get-tuple-element.45.valid, bf16[512,2048]{1,0:T(8,128)(2,1)S(1)} %collective-permute-done.1.left_2.refs_0_, bf16[512,2048]{1,0:T(8,128)(2,1)} %collective-permute-done.3.right_2.refs_1_, bf16[8192,2048]{1,0:T(8,128)(2,1)} %weight.3, ...), custom_call_target="tpu_custom_call" | custom-call | flops 8589934592 | bytes 29360128 | tf_op jit(solution)/shard_map/pallas_call | solution.py:145
  162.8 14.6 %collective-permute-done.9.x = bf16[512,1024]{1,0:T(8,128)(2,1)S(1)} collective-permute-done((bf16[512,1024]{1,0:T(8,128)(2,1)}, bf16[512,1024]{1,0:T(8,128)(2,1)S(1)}, u32[]{:S(2)}, u32[]{:S(2)}) %collective-permute-start.9) | collective-permute-done | bytes 1048608 | tf_op jit(solution)/shard_map/ppermute | solution.py:459
  177.3 5.7 %shard_map.104.base = f32[512,2048]{1,0:T(8,128)S(1)} custom-call(s32[1]{0:T(128)} %bitcast.1.start, s32[1]{0:T(128)} %bitcast.valid, bf16[512,1024]{1,0:T(8,128)(2,1)S(1)} %collective-permute-done.9.x, bf16[8192,2048]{1,0:T(8,128)(2,1)} %weight.3, f32[512,2048]{1,0:T(8,128)} %shard_map.103.base_in), custom_call_target="tpu_custom_call" | custom-call | flops 2147483648 | bytes 13631488 | tf_op jit(solution)/shard_map/pallas_call | solution.py:183
  183.1 8.3 %collective-permute-done.11.received = bf16[512,640]{1,0:T(8,128)(2,1)S(1)} collective-permute-done((bf16[512,640]{1,0:T(8,128)(2,1)S(1)}, bf16[512,640]{1,0:T(8,128)(2,1)S(1)}, u32[]{:S(2)}, u32[]{:S(2)}) %collective-permute-start.11) | collective-permute-done | bytes 655392 | tf_op jit(solution)/shard_map/ppermute | solution.py:472
  191.4 5.9 %shard_map.105 = (f32[512,2048]{1,0:T(8,128)S(1)}, bf16[512,2048]{1,0:T(8,128)(2,1)S(1)}) custom-call(s32[2]{0:T(128)S(1)} %pad_add_fusion.facts, s32[6]{0:T(128)S(1)} %fusion.2.places, f32[512,2048]{1,0:T(8,128)S(1)} %shard_map.104.base, bf16[512,640]{1,0:T(8,128)(2,1)S(1)} %pad_maximum_fusion.sent, bf16[512,640]{1,0:T(8,128)(2,1)S(1)} %collective-permute-done.11.received, ...), custom_call_target="tpu_custom_call" | custom-call | flops 2684354560 | bytes 15728640 | tf_op jit(solution)/shard_map/pallas_call | solution.py:334
  197.3 5.0 %collective-permute-done.15.x = bf16[512,512]{1,0:T(8,128)(2,1)S(1)} collective-permute-done((bf16[512,512]{1,0:T(8,128)(2,1)S(1)}, bf16[512,512]{1,0:T(8,128)(2,1)S(1)}, u32[]{:S(2)}, u32[]{:S(2)}) %collective-permute-start.15) | collective-permute-done | bytes 524320 | tf_op jit(solution)/shard_map/ppermute | solution.py:474
  202.2 3.5 %shard_map.106 = bf16[512,2048]{1,0:T(8,128)(2,1)} custom-call(s32[2]{0:T(128)S(1)} %pad_add_fusion.facts, f32[512,2048]{1,0:T(8,128)S(1)} %get-tuple-element.40.total, bf16[512,2048]{1,0:T(8,128)(2,1)S(1)} %get-tuple-element.41.weight, bf16[512,512]{1,0:T(8,128)(2,1)S(1)} %collective-permute-done.15.x), custom_call_target="tpu_custom_call" | custom-call | flops 1073741824 | bytes 2097152 | tf_op jit(solution)/shard_map/pallas_call | solution.py:371
  (42 shorter events, 2.2 us)
Async XLA Ops:
  0.0 50.1 %collective-permute-start = (bf16[512,2048]{1,0:T(8,128)(2,1)}, bf16[512,2048]{1,0:T(8,128)(2,1)S(1)}, u32[]{:S(2)}, u32[]{:S(2)}) collective-permute-start(bf16[512,2048]{1,0:T(8,128)(2,1)} %refs_0_.4), channel_id=1, source_target_pairs={{0,4},{4,8},{8,12},{1,5},{5,9},{9,13},{2,6},{6,10},{10,14},{3,7},{... | collective-permute-start | bytes 6291464 | tf_op jit(solution)/shard_map/ppermute | solution.py:430
  5.1 49.3 %collective-permute-start.2 = (bf16[512,2048]{1,0:T(8,128)(2,1)}, bf16[512,2048]{1,0:T(8,128)(2,1)}, u32[]{:S(2)}, u32[]{:S(2)}) collective-permute-start(bf16[512,2048]{1,0:T(8,128)(2,1)} %refs_0_.4), channel_id=1, source_target_pairs={{4,0},{8,4},{12,8},{5,1},{9,5},{13,9},{6,2},{10,6},{14,10},{7,3},{... | collective-permute-start | bytes 6291464 | tf_op jit(solution)/shard_map/ppermute | solution.py:431
  6.4 48.9 %collective-permute-start.5 = (bf16[4,32,8192]{2,1,0:T(8,128)(2,1)}, bf16[4,32,8192]{2,1,0:T(8,128)(2,1)}, u32[]{:S(2)}, u32[]{:S(2)}) collective-permute-start(bf16[4,32,8192]{2,1,0:T(8,128)(2,1)} %refs_0_.3), channel_id=1, source_target_pairs={{0,2},{1,3},{2,0},{3,1},{4,6},{5,7},{6,4},{7,5},{8,10},{9,11},{10,... | collective-permute-start | bytes 6291464 | tf_op jit(solution)/shard_map/ppermute | solution.py:422
  7.9 57.4 %collective-permute-start.4 = (bf16[4,32,8192]{2,1,0:T(8,128)(2,1)}, bf16[4,32,8192]{2,1,0:T(8,128)(2,1)}, u32[]{:S(2)}, u32[]{:S(2)}) collective-permute-start(bf16[4,32,8192]{2,1,0:T(8,128)(2,1)} %refs_0_.3), channel_id=1, source_target_pairs={{0,1},{1,0},{2,3},{3,2},{4,5},{5,4},{6,7},{7,6},{8,9},{9,8},{10,11... | collective-permute-start | bytes 6291464 | tf_op jit(solution)/shard_map/ppermute | solution.py:422
  7.9 119.9 %collective-permute-start.13 = (bf16[4,128,2048]{2,1,0:T(8,128)(2,1)}, bf16[4,128,2048]{2,1,0:T(8,128)(2,1)}, u32[]{:S(2)}, u32[]{:S(2)}) collective-permute-start(bf16[4,128,2048]{2,1,0:T(8,128)(2,1)} %refs_0_.5), channel_id=1, source_target_pairs={{0,2},{1,3},{2,0},{3,1},{4,6},{5,7},{6,4},{7,5},{8,10},{9,11},{10,... | collective-permute-start | bytes 6291464 | tf_op jit(solution)/shard_map/ppermute | solution.py:422
  50.1 12.4 %copy-start.5 = (bf16[512,2048]{1,0:T(8,128)(2,1)}, bf16[512,2048]{1,0:T(8,128)(2,1)S(1)}, u32[]{:S(2)}) copy-start(bf16[512,2048]{1,0:T(8,128)(2,1)S(1)} %collective-permute-done.refs_1_.left_1) | copy-start | bytes 6291460
  55.3 10.0 %collective-permute-start.6 = (bf16[4,32,8192]{2,1,0:T(8,128)(2,1)}, bf16[4,32,8192]{2,1,0:T(8,128)(2,1)}, u32[]{:S(2)}, u32[]{:S(2)}) collective-permute-start(bf16[4,32,8192]{2,1,0:T(8,128)(2,1)} %collective-permute-done.5.refs_2_), channel_id=1, source_target_pairs={{0,1},{1,0},{2,3},{3,2},{4,5},{5,4},{6,7},{7,6},{8,9},{9,8},{10,11... | collective-permute-start | bytes 6291464 | tf_op jit(solution)/shard_map/ppermute | solution.py:422
  63.2 50.1 %collective-permute-start.1 = (bf16[512,2048]{1,0:T(8,128)(2,1)}, bf16[512,2048]{1,0:T(8,128)(2,1)S(1)}, u32[]{:S(2)}, u32[]{:S(2)}) collective-permute-start(bf16[512,2048]{1,0:T(8,128)(2,1)} %copy-done.5), channel_id=1, source_target_pairs={{4,8},{8,12},{5,9},{9,13},{6,10},{10,14},{7,11},{11,15},{20,24},{2... | collective-permute-start | bytes 6291464 | tf_op jit(solution)/shard_map/ppermute | solution.py:436
  64.0 53.6 %collective-permute-start.3 = (bf16[512,2048]{1,0:T(8,128)(2,1)}, bf16[512,2048]{1,0:T(8,128)(2,1)}, u32[]{:S(2)}, u32[]{:S(2)}) collective-permute-start(bf16[512,2048]{1,0:T(8,128)(2,1)} %collective-permute-done.2.refs_2_.right_1), channel_id=1, source_target_pairs={{4,0},{8,4},{5,1},{9,5},{6,2},{10,6},{7,3},{11,7},{20,16},{24,20},... | collective-permute-start | bytes 6291464 | tf_op jit(solution)/shard_map/ppermute | solution.py:437
  65.3 1.6 copy-start.3
  70.4 1.9 copy-start
  77.8 47.6 %collective-permute-start.7 = (bf16[4096,192]{0,1:T(8,128)(2,1)}, bf16[4096,192]{0,1:T(8,128)(2,1)}, u32[]{:S(2)}, u32[]{:S(2)}) collective-permute-start(bf16[4096,192]{0,1:T(8,128)(2,1)} %copy.22), channel_id=1, source_target_pairs={{0,4},{12,8},{1,5},{13,9},{2,6},{14,10},{3,7},{15,11},{16,20},{28,... | collective-permute-start | bytes 4718600 | tf_op jit(solution)/shard_map/ppermute | solution.py:442
  87.0 1.6 copy-start.6
  88.5 1.6 copy-start.8
  90.1 22.8 %copy-start.9 = (s32[512]{0:T(512)S(1)}, s32[512]{0:T(512)}, u32[]{:S(2)}) copy-start(s32[512]{0:T(512)} %param.16) | copy-start | bytes 6148
  109.6 15.8 %collective-permute-start.8 = (f32[512,32]{1,0:T(8,128)S(1)}, f32[512,32]{1,0:T(8,128)S(1)}, u32[]{:S(2)}, u32[]{:S(2)}) collective-permute-start(f32[512,32]{1,0:T(8,128)S(1)} %get-tuple-element.25.low), channel_id=1, source_target_pairs={{0,4},{12,8},{1,5},{13,9},{2,6},{14,10},{3,7},{15,11},{16,20},{28,... | collective-permute-start | bytes 196616 | tf_op jit(solution)/shard_map/ppermute | solution.py:448
  113.3 69.8 %collective-permute-start.12 = (bf16[4,128,2048]{2,1,0:T(8,128)(2,1)}, bf16[4,128,2048]{2,1,0:T(8,128)(2,1)}, u32[]{:S(2)}, u32[]{:S(2)}) collective-permute-start(bf16[4,128,2048]{2,1,0:T(8,128)(2,1)} %refs_0_.5), channel_id=1, source_target_pairs={{0,1},{1,0},{2,3},{3,2},{4,5},{5,4},{6,7},{7,6},{8,9},{9,8},{10,11... | collective-permute-start | bytes 6291464 | tf_op jit(solution)/shard_map/ppermute | solution.py:422
  127.8 63.6 %collective-permute-start.14 = (bf16[4,128,2048]{2,1,0:T(8,128)(2,1)}, bf16[4,128,2048]{2,1,0:T(8,128)(2,1)}, u32[]{:S(2)}, u32[]{:S(2)}) collective-permute-start(bf16[4,128,2048]{2,1,0:T(8,128)(2,1)} %collective-permute-done.13.refs_2_), channel_id=1, source_target_pairs={{0,1},{1,0},{2,3},{3,2},{4,5},{5,4},{6,7},{7,6},{8,9},{9,8},{10,11... | collective-permute-start | bytes 6291464 | tf_op jit(solution)/shard_map/ppermute | solution.py:422
  131.8 2.2 %copy-start.1 = (bf16[8192,192]{1,0:T(8,128)(2,1)S(1)}, bf16[8192,192]{1,0:T(8,128)(2,1)}, u32[]{:S(2)}) copy-start(bf16[8192,192]{1,0:T(8,128)(2,1)} %copy-done) | copy-start | bytes 9437188
  134.0 1.6 copy-start.2
  135.6 1.6 copy-start.7
  144.1 3.1 %collective-permute-start.10 = (bf16[512,64]{1,0:T(8,128)(2,1)S(1)}, bf16[512,64]{1,0:T(8,128)(2,1)S(1)}, u32[]{:S(2)}, u32[]{:S(2)}) collective-permute-start(bf16[512,64]{1,0:T(8,128)(2,1)S(1)} %shard_map.102), channel_id=1, source_target_pairs={{4,8},{8,4},{5,9},{9,5},{6,10},{10,6},{7,11},{11,7},{20,24},{24,20... | collective-permute-start | bytes 196616 | tf_op jit(solution)/shard_map/ppermute | solution.py:467
  145.9 31.5 %collective-permute-start.9 = (bf16[512,1024]{1,0:T(8,128)(2,1)}, bf16[512,1024]{1,0:T(8,128)(2,1)S(1)}, u32[]{:S(2)}, u32[]{:S(2)}) collective-permute-start(bf16[512,1024]{1,0:T(8,128)(2,1)} %slice_select_fusion), channel_id=1, source_target_pairs={{8,12},{4,0},{9,13},{5,1},{10,14},{6,2},{11,15},{7,3},{24,28},{20,... | collective-permute-start | bytes 3145736 | tf_op jit(solution)/shard_map/ppermute | solution.py:459
  147.4 44.0 %collective-permute-start.11 = (bf16[512,640]{1,0:T(8,128)(2,1)S(1)}, bf16[512,640]{1,0:T(8,128)(2,1)S(1)}, u32[]{:S(2)}, u32[]{:S(2)}) collective-permute-start(bf16[512,640]{1,0:T(8,128)(2,1)S(1)} %pad_maximum_fusion.sent), channel_id=1, source_target_pairs={{8,12},{4,0},{9,13},{5,1},{10,14},{6,2},{11,15},{7,3},{24,28},{20,... | collective-permute-start | bytes 1966088 | tf_op jit(solution)/shard_map/ppermute | solution.py:472
  149.8 52.4 %collective-permute-start.15 = (bf16[512,512]{1,0:T(8,128)(2,1)S(1)}, bf16[512,512]{1,0:T(8,128)(2,1)S(1)}, u32[]{:S(2)}, u32[]{:S(2)}) collective-permute-start(bf16[512,512]{1,0:T(8,128)(2,1)S(1)} %slice_select_fusion.1), channel_id=1, source_target_pairs={{8,12},{4,0},{9,13},{5,1},{10,14},{6,2},{11,15},{7,3},{24,28},{20,... | collective-permute-start | bytes 1572872 | tf_op jit(solution)/shard_map/ppermute | solution.py:474
  162.8 28.6 %copy-start.4 = (bf16[4,128,2048]{2,1,0:T(8,128)(2,1)S(1)}, bf16[4,128,2048]{2,1,0:T(8,128)(2,1)}, u32[]{:S(2)}) copy-start(bf16[4,128,2048]{2,1,0:T(8,128)(2,1)} %refs_0_.5) | copy-start | bytes 6291460

commit v13 on v12

--- a/solution.py
+++ b/solution.py
@@ -22,22 +22,24 @@
                 pltpu.make_async_copy(rows_of(block.at[lax.rem(places[e], length)]), target, sems[e]).start()
 
 
-def join_downs_kernel(places, *refs):
-    *blocks, out, held, sems = refs
+def join_downs_kernel(places, upper, *refs):
+    *blocks, out, other, held, sems = refs
     length, rank_part, _ = blocks[0].shape
     shards, slots, width = held.shape
+    entries = places.shape[0]
     step = pl.program_id(0)
 
     def targets(t):
-        return [held.at[t, pl.ds(e * rank_part, rank_part)] for e in range(slots // rank_part)]
+        return [held.at[t, pl.ds(e * rank_part, rank_part)] for e in range(entries)]
 
     @pl.when(step == 0)
     def _():
         for t in range(shards):
-            semaphores = [sems.at[t, e] for e in range(slots // rank_part)]
+            semaphores = [sems.at[t, e] for e in range(entries)]
             start_pages(
                 places, blocks, length, targets(t), semaphores, lambda page: page.at[:, pl.ds(t * width, width)]
             )
+            held[t, entries * rank_part:] = jnp.zeros((slots - entries * rank_part, width), BF16)
 
     for t in range(shards):
 
@@ -46,23 +48,33 @@
             for e, target in enumerate(targets(t)):
                 source = blocks[0].at[0, :, pl.ds(t * width, width)]
                 pltpu.make_async_copy(source, target, sems.at[t, e]).wait()
-            out[...] = held[t].T
-
-
-def join_downs(places, blocks, shards):
+            joined = held[t].T
+            out[...] = joined
+            half = shards // 2
+
+            @pl.when((upper[0] != 0) == (t < half))
+            def _():
+                other[t % half * width:(t % half + 1) * width] = joined
+
+
+def join_downs(places, upper, blocks, shards):
     entries = places.shape[0]
     _, rank_part, features = blocks[0].shape
-    width, slots = features // shards, entries * rank_part
+    width, slots = features // shards, -(-entries * rank_part // 128) * 128
     return pl.pallas_call(
         join_downs_kernel,
-        out_shape=jax.ShapeDtypeStruct((features, slots), BF16),
+        out_shape=[jax.ShapeDtypeStruct((a, slots), BF16) for a in (features, features // 2)],
         grid=(shards,),
-        in_specs=[pl.BlockSpec(memory_space=pltpu.SMEM)] + [pl.BlockSpec(memory_space=pltpu.HBM)] * len(blocks),
-        out_specs=pl.BlockSpec((width, slots), lambda t: (t, 0)),
+        in_specs=[pl.BlockSpec(memory_space=pltpu.SMEM)] * 2
+        + [pl.BlockSpec(memory_space=pltpu.HBM)] * len(blocks),
+        out_specs=[
+            pl.BlockSpec((width, slots), lambda t: (t, 0)),
+            pl.BlockSpec((features // 2, slots), lambda t: (0, 0)),
+        ],
         scratch_shapes=[pltpu.VMEM((shards, slots, width), BF16), pltpu.SemaphoreType.DMA((shards, entries))],
         compiler_params=TAIL_PARAMS,
         cost_estimate=pl.CostEstimate(flops=0, bytes_accessed=4 * features * slots, transcendentals=0),
-    )(places, *blocks)
+    )(places, upper, *blocks)
 
 
 RESIDENT = pl.BlockSpec(memory_space=pltpu.VMEM)
@@ -110,15 +122,18 @@
             low[...] = fold_entry(acc[...], slot[...], low.shape[1])
 
 
-def add_shards(base, xs, source, weight, down=None, slot=None, rank_part=0):
-    rows, width = xs[0].shape
-    half = width // 2
-    columns = weight.shape[1]
-    n_tensor = weight.shape[0] // width
+def plan_shards(source, n_tensor):
     there = (source >= 0) & (source < n_tensor)
     start = 2 * jnp.clip(source, 0, n_tensor - 1)[:, None] + jnp.arange(2)[None, :]
     idle = jnp.concatenate([start[1:2, :1], start[:-1, 1:]], axis=0)
     start = jnp.where(there[:, None], start, idle).reshape(-1).astype(jnp.int32)
+    return start, there.astype(jnp.int32)
+
+
+def add_shards(base, xs, plan, weight, down=None, slot=None, rank_part=0):
+    rows, width = xs[0].shape
+    half = width // 2
+    columns = weight.shape[1]
     steps = 2 * len(xs)
 
     def whole(a):
@@ -158,7 +173,7 @@
             bytes_accessed=2 * steps * half * (rows + columns + slots) + 8 * rows * columns,
             transcendentals=0,
         ),
-    )(start, there.astype(jnp.int32), *xs, weight, *rest)
+    )(*plan, *xs, weight, *rest)
 
 
 def half_kernel(start, valid, x, weight, base_in, base):
@@ -426,6 +441,13 @@
     upper = me >= n_tensor // 2
     ends = me * (n_tensor - 1 - me) == 0
     slot = row_request_entry[:, None]
+    farthest = jnp.where(upper, 0, n_tensor - 1)
+    end = jnp.where(upper, n_tensor - 1, 0)
+    source = jnp.where(upper, me - 2, me + 2)
+    facts = jnp.stack([ends.astype(jnp.int32), farthest]).astype(jnp.int32)
+    far_facts = jnp.stack([me, end, source, upper.astype(jnp.int32)]).astype(jnp.int32)
+    near = plan_shards(me + jnp.array([0, -1, 1], jnp.int32), n_tensor)
+    far = plan_shards(me + jnp.array([-2, 2], jnp.int32), n_tensor)
 
     right_1 = lax.ppermute(attention_result, "tensor", right)
     left_1 = lax.ppermute(attention_result, "tensor", left)
@@ -433,21 +455,21 @@
     far_up = across(adapter_up_weight, 2)
     near_down = across(adapter_down_weight, 1)
 
+    right_1, left_1, places, slot, live, facts, far_facts, near, far = lax.optimization_barrier(
+        (right_1, left_1, places, slot, row_rank[:, None], facts, far_facts, near, far)
+    )
     right_2 = lax.ppermute(right_1, "tensor", right[1:])
     left_2 = lax.ppermute(left_1, "tensor", left[:-1])
     downs = (adapter_down_weight, near_down, far_down, across(after(far_down, right_1, left_1), 1))
-    down = join_downs(places, downs, n_tensor)
-    farthest = jnp.where(upper, 0, n_tensor - 1)
-    other_down = lax.dynamic_slice_in_dim(down, jnp.where(upper, 0, 2 * width), 2 * width, 0)
+    down, other_down = join_downs(places, far_facts[3:], downs, n_tensor)
     other_down = lax.ppermute(other_down, "tensor", [(0, 1), (3, 2)])
 
-    near = me + jnp.array([0, -1, 1], jnp.int32)
     base, low = add_shards(
         None, [attention_result, right_1, left_1], near, output_weight, down, slot, rank_part
     )
     other_low = lax.ppermute(low, "tensor", [(0, 1), (3, 2)])
 
-    right_2, left_2, other_down, other_low = lax.optimization_barrier((right_2, left_2, other_down, other_low))
+    right_2, left_2 = lax.optimization_barrier((base, right_2, left_2))[1:]
     third = right[-1:] + left[:1]
     cuts = (0, width // 2, width // 4 * 3, width)
 
@@ -457,15 +479,13 @@
 
     first_2 = piece(0)
     first_3 = lax.ppermute(first_2, "tensor", third)
-    right_2, left_2 = lax.optimization_barrier((first_2, right_2, left_2))[1:]
-    end = jnp.where(upper, n_tensor - 1, 0)
-    source = jnp.where(upper, me - 2, me + 2)
+    right_2, left_2, other_down, other_low = lax.optimization_barrier(
+        (first_2, right_2, left_2, other_down, other_low)
+    )[1:]
     pair = far_low(
-        jnp.stack([me, end, source, upper.astype(jnp.int32)]).astype(jnp.int32),
-        right_1, right_2, left_1, left_2, down, other_down, slot, row_rank[:, None], low, other_low,
+        far_facts, right_1, right_2, left_1, left_2, down, other_down, slot, live, low, other_low
     )
     from_middle = lax.ppermute(pair, "tensor", [(1, 2), (2, 1)])
-    far = me + jnp.array([-2, 2], jnp.int32)
     base, = add_shards(after(base, pair), [right_2, left_2], far, output_weight)
     low = jnp.where(upper, jnp.concatenate([from_middle, pair], axis=1), jnp.concatenate([pair, from_middle], axis=1))
     second_2 = jnp.concatenate([piece(1), low], axis=1)
@@ -473,7 +493,6 @@
     right_2, left_2 = lax.optimization_barrier((second_2, right_2, left_2))[1:]
     last_3 = lax.ppermute(piece(2), "tensor", third)
     ups = (adapter_up_weight, across(after(adapter_up_weight, far_down), 1), far_up, across(after(far_up, first_2), 1))
-    facts = jnp.stack([ends.astype(jnp.int32), farthest]).astype(jnp.int32)
     base = add_half(base, first_3, facts[0], facts[1], output_weight)
     total, rows_of = prepare(facts, places, base, second_2, second_3, output_weight, ups, slot)
     total, rows_of, last_3 = lax.optimization_barrier((total, rows_of, last_3))

time: 207 us -> 177 us (0.86)
  waiting for transfers between devices: 86.9 us -> 59.6 us
  local copies, waits for them, and re-layouts: 23.8 us -> 15.2 us
  Pallas kernels: 56.6 us -> 60.4 us
    ppermute x1, waiting for transfers between devices: 14.6 us -> 0.01 us  [local(): first_3 = lax.ppermute(first_2, 'tensor', third)]
    ppermute x1, waiting for transfers between devices: 41.7 us -> 33.9 us  [local(): right_1 = lax.ppermute(attention_result, 'tensor', right)]
    ppermute x1, waiting for transfers between devices: 8.32 us -> 2 us  [local(): second_3 = lax.ppermute(second_2, 'tensor', third)]
    dynamic_slice x2 -> x0, local copies, waits for them, and re-layouts: 5.43 us -> none  [local(): lax.dynamic_slice_in_dim(down, jnp.where(upper, 0, 2 * width), 2 * width, 0)]
    ppermute x1, waiting for transfers between devices: 4.27 us -> 8.61 us  [local(): left_2 = lax.ppermute(left_1, 'tensor', left[:-1])]
    ppermute x1, waiting for transfers between devices: 4.98 us -> 1.24 us  [local(): last_3 = lax.ppermute(piece(2), 'tensor', third)]
    optimization_barrier x1 -> x2, local copies, waits for them, and re-layouts: 3.84 us -> 0.29 us  [local(): lax.optimization_barrier((right_1, left_1, places, slot, row_rank[:, None...]
    pallas_call x1, Pallas kernels: 3.5 us -> 5.81 us  [join_downs(): pl.pallas_call(join_downs_kernel, out_shape=[jax.ShapeDtypeStruct((a, slo...]
  transfers between devices with their start and end apart: 16 -> 16, of which waited for: 8 -> 7; matrix products, arithmetic and copies ran while one was open for 11% -> 8% of each run, Pallas kernels for 26% -> 32%
where the time goes in v13:
time: 177 us; the launch traced here: 176 us
  Pallas kernels  60.4 us (34%)
  waiting for transfers between devices  59.6 us (34%)
  starting transfers between devices  28.8 us (16%)
  local copies, waits for them, and re-layouts  15.2 us (9%)
  other arithmetic  11.6 us (7%)
    ppermute x1, waiting for transfers between devices, local(): right_1 = lax.ppermute(attention_result, 'tensor', right)  33.9 us
    pallas_call x2, Pallas kernels, add_shards(): pl.pallas_call(functools.partial(shards_kernel, base is None), out_shape=...  31.1 us
    unnamed x18, local copies, waits for them, and re-layouts  12.1 us
    ppermute x1, waiting for transfers between devices, local(): other_low = lax.ppermute(low, 'tensor', [(0, 1), (3, 2)])  9.57 us
    ppermute x1, waiting for transfers between devices, local(): left_2 = lax.ppermute(left_1, 'tensor', left[:-1])  8.61 us
    ppermute x1, starting transfers between devices, local(): other_down = lax.ppermute(other_down, 'tensor', [(0, 1), (3, 2)])  8.33 us
    pallas_call x1, Pallas kernels, far_low(): pl.pallas_call(far_low_kernel, out_shape=jax.ShapeDtypeStruct((rows, 2 *...  7.15 us
    pallas_call x1, Pallas kernels, add_half(): pl.pallas_call(half_kernel, out_shape=jax.ShapeDtypeStruct((rows, columns...  6.97 us
  transfers between devices with their start and end apart: 16, of which 7 were waited for; matrix products, arithmetic and copies ran while one was open for 8% of the time, Pallas kernels for 32%

profile of v13, /device:TPU:0, one launch (start us, length us, event | category | flops | bytes accessed | tf_op | source)
XLA Modules:
  0.0 175.8 jit_solution(7579106730367045900)
XLA Ops:
  0.0 5.1 %collective-permute-start = (bf16[512,2048]{1,0:T(8,128)(2,1)}, bf16[512,2048]{1,0:T(8,128)(2,1)S(1)}, u32[]{:S(2)}, u32[]{:S(2)}) collective-permute-start(bf16[512,2048]{1,0:T(8,128)(2,1)} %refs_0_.4), channel_id=1, source_target_pairs={{0,4},{4,8},{8,12},{1,5},{5,9},{9,13},{2,6},{6,10},{10,14},{3,7},{... | collective-permute-start | bytes 6291464 | tf_op jit(solution)/shard_map/ppermute | solution.py:452
  5.1 1.3 collective-permute-start.1
  6.4 1.6 collective-permute-start.3
  7.9 0.7 fusion
  8.6 0.6 slice.39
  9.2 0.7 add_bitcast_fusion
  10.0 0.7 fusion.4
  10.8 0.7 fusion.1
  11.6 0.6 fusion.5
  12.2 1.4 add_reduce_fusion
  13.6 0.7 fusion.3
  14.6 0.9 select_reduce_fusion.1
  15.5 0.8 select_reduce_fusion
  16.2 33.9 %collective-permute-done.refs_1_.left_1 = bf16[512,2048]{1,0:T(8,128)(2,1)S(1)} collective-permute-done((bf16[512,2048]{1,0:T(8,128)(2,1)}, bf16[512,2048]{1,0:T(8,128)(2,1)S(1)}, u32[]{:S(2)}, u32[]{:S(2)}) %collective-permute-start) | collective-permute-done | bytes 2097184 | tf_op jit(solution)/shard_map/ppermute | solution.py:452
  50.1 4.2 %collective-permute-done.1.refs_2_.right_1 = bf16[512,2048]{1,0:T(8,128)(2,1)} collective-permute-done((bf16[512,2048]{1,0:T(8,128)(2,1)}, bf16[512,2048]{1,0:T(8,128)(2,1)}, u32[]{:S(2)}, u32[]{:S(2)}) %collective-permute-start.1) | collective-permute-done | bytes 2097184 | tf_op jit(solution)/shard_map/ppermute | solution.py:453
  54.4 0.8 collective-permute-start.5
  55.2 1.3 collective-permute-start.6
  56.5 1.6 collective-permute-start.13
  58.0 0.6 slice.45.upper
  58.7 1.6 copy-done.2
  60.3 5.8 %shard_map.100 = (bf16[8192,256]{1,0:T(8,128)(2,1)S(1)}, bf16[4096,256]{1,0:T(8,128)(2,1)}) custom-call(s32[6]{0:T(128)S(1)} %fusion.2.places, s32[1]{0:T(128)} %slice.45.upper, bf16[4,32,8192]{2,1,0:T(8,128)(2,1)S(1)} %copy-done.2, bf16[4,32,8192]{2,1,0:T(8,128)(2,1)} %collective-permute-done.2.refs_1_, ...), custom_call_target="tpu_custom_call" | custom-call | bytes 8388608 | tf_op jit(solution)/shard_map/pallas_call | solution.py:64
  66.2 2.0 %copy-done = bf16[8192,256]{1,0:T(8,128)(2,1)} copy-done((bf16[8192,256]{1,0:T(8,128)(2,1)}, bf16[8192,256]{1,0:T(8,128)(2,1)S(1)}, u32[]{:S(2)}) %copy-start) | copy-done | bytes 4194328
  68.1 8.3 %collective-permute-start.8 = (bf16[4096,256]{1,0:T(8,128)(2,1)}, bf16[4096,256]{1,0:T(8,128)(2,1)}, u32[]{:S(2)}, u32[]{:S(2)}) collective-permute-start(bf16[4096,256]{1,0:T(8,128)(2,1)} %get-tuple-element.52), channel_id=1, source_target_pairs={{0,4},{12,8},{1,5},{13,9},{2,6},{14,10},{3,7},{15,11},{16,20},{28,... | collective-permute-start | bytes 6291464 | tf_op jit(solution)/shard_map/ppermute | solution.py:465
  76.7 1.6 copy-done.5
  78.3 1.6 copy-done.7
  79.9 19.4 %shard_map.101 = (f32[512,2048]{1,0:T(8,128)}, f32[512,32]{1,0:T(8,128)S(1)}) custom-call(s32[6]{0:T(128)S(1)} %select_n.86.start, s32[3]{0:T(128)S(1)} %get-tuple-element.40.valid, bf16[512,2048]{1,0:T(8,128)(2,1)S(1)} %copy-done.7, bf16[512,2048]{1,0:T(8,128)(2,1)S(1)} %copy-done.5, bf16[512,2048]{1,0:T(8,128)(2,1)} %collective-permute-done.1.refs_2_.right_1, ...), custom_call_target="tpu_custom_call" | custom-call | flops 14495514624 | bytes 42991616 | tf_op jit(solution)/shard_map/pallas_call | solution.py:160
  99.3 8.6 %collective-permute-done.6.right_2.refs_1_ = bf16[512,2048]{1,0:T(8,128)(2,1)} collective-permute-done((bf16[512,2048]{1,0:T(8,128)(2,1)}, bf16[512,2048]{1,0:T(8,128)(2,1)}, u32[]{:S(2)}, u32[]{:S(2)}) %collective-permute-start.6) | collective-permute-done | bytes 2097184 | tf_op jit(solution)/shard_map/ppermute | solution.py:462
  107.9 2.3 %slice_select_fusion = bf16[512,1024]{1,0:T(8,128)(2,1)} fusion(bf16[512,2048]{1,0:T(8,128)(2,1)} %collective-permute-done.6.right_2.refs_1_, bf16[512,2048]{1,0:T(8,128)(2,1)S(1)} %collective-permute-done.5.left_2.refs_0_, pred[]{:T(512)S(6)} %ge.9), kind=kLoop, calls=%fused_computation | loop fusion | flops 524288 | bytes 3145729 | tf_op jit(solution)/shard_map/jit(_where)/select_n | solution.py:478
  110.4 4.1 %collective-permute-start.9 = (f32[512,32]{1,0:T(8,128)S(1)}, f32[512,32]{1,0:T(8,128)S(1)}, u32[]{:S(2)}, u32[]{:S(2)}) collective-permute-start(f32[512,32]{1,0:T(8,128)S(1)} %get-tuple-element.53.low), channel_id=1, source_target_pairs={{0,4},{12,8},{1,5},{13,9},{2,6},{14,10},{3,7},{15,11},{16,20},{28,... | collective-permute-start | bytes 196616 | tf_op jit(solution)/shard_map/ppermute | solution.py:470
  114.5 0.6 fusion.6
  115.1 1.3 collective-permute-start.7
  116.4 9.6 %collective-permute-done.9.other_low = f32[512,32]{1,0:T(8,128)S(1)} collective-permute-done((f32[512,32]{1,0:T(8,128)S(1)}, f32[512,32]{1,0:T(8,128)S(1)}, u32[]{:S(2)}, u32[]{:S(2)}) %collective-permute-start.9) | collective-permute-done | bytes 65568 | tf_op jit(solution)/shard_map/ppermute | solution.py:470
  125.9 2.2 %copy-done.1 = bf16[8192,256]{1,0:T(8,128)(2,1)S(1)} copy-done((bf16[8192,256]{1,0:T(8,128)(2,1)S(1)}, bf16[8192,256]{1,0:T(8,128)(2,1)}, u32[]{:S(2)}) %copy-start.1) | copy-done | bytes 4194328
  128.1 1.6 copy-done.6
  129.7 7.2 %shard_map.102 = bf16[512,64]{1,0:T(8,128)(2,1)S(1)} custom-call(s32[4]{0:T(128)S(1)} %pad_add_fusion.1.facts, bf16[512,2048]{1,0:T(8,128)(2,1)S(1)} %copy-done.6, bf16[512,2048]{1,0:T(8,128)(2,1)S(1)} %collective-permute-done.5.left_2.refs_0_, bf16[512,2048]{1,0:T(8,128)(2,1)} %collective-permute-done.1.refs_2_.right_1, ...), custom_call_target="tpu_custom_call" | custom-call | flops 1610612736 | bytes 7340032 | tf_op jit(solution)/shard_map/pallas_call | solution.py:269
  136.9 0.9 collective-permute-start.10
  137.8 1.1 slice_select_fusion.2
  138.9 0.1 maximum_select_fusion
  139.1 1.3 collective-permute-start.11
  140.4 1.1 slice_select_fusion.1
  141.6 1.3 collective-permute-start.15
  142.9 11.7 %shard_map.103.base_in = f32[512,2048]{1,0:T(8,128)} custom-call(s32[4]{0:T(128)S(1)} %select_n.88.start, s32[2]{0:T(128)S(1)} %get-tuple-element.51.valid, bf16[512,2048]{1,0:T(8,128)(2,1)S(1)} %collective-permute-done.5.left_2.refs_0_, bf16[512,2048]{1,0:T(8,128)(2,1)} %collective-permute-done.6.right_2.refs_1_, bf16[8192,2048]{1,0:T(8,128)(2,1)} %weight.3, ...), custom_call_target="tpu_custom_call" | custom-call | flops 8589934592 | bytes 29360128 | tf_op jit(solution)/shard_map/pallas_call | solution.py:160
  154.6 7.0 %shard_map.104.base = f32[512,2048]{1,0:T(8,128)S(1)} custom-call(s32[1]{0:T(128)} %get-tuple-element.78.start, s32[1]{0:T(128)} %get-tuple-element.77.valid, bf16[512,1024]{1,0:T(8,128)(2,1)S(1)} %collective-permute-done.7.x, bf16[8192,2048]{1,0:T(8,128)(2,1)} %weight.3, f32[512,2048]{1,0:T(8,128)} %shard_map.103.base_in), custom_call_target="tpu_custom_call" | custom-call | flops 2147483648 | bytes 13631488 | tf_op jit(solution)/shard_map/pallas_call | solution.py:198
  161.5 2.0 %collective-permute-done.11.received = bf16[512,640]{1,0:T(8,128)(2,1)S(1)} collective-permute-done((bf16[512,640]{1,0:T(8,128)(2,1)S(1)}, bf16[512,640]{1,0:T(8,128)(2,1)S(1)}, u32[]{:S(2)}, u32[]{:S(2)}) %collective-permute-start.11) | collective-permute-done | bytes 655392 | tf_op jit(solution)/shard_map/ppermute | solution.py:492
  163.5 1.6 copy-done.3
  165.1 5.9 %shard_map.105 = (f32[512,2048]{1,0:T(8,128)S(1)}, bf16[512,2048]{1,0:T(8,128)(2,1)S(1)}) custom-call(s32[2]{0:T(128)S(1)} %pad_add_fusion.facts, s32[6]{0:T(128)S(1)} %fusion.2.places, f32[512,2048]{1,0:T(8,128)S(1)} %shard_map.104.base, bf16[512,640]{1,0:T(8,128)(2,1)S(1)} %pad_maximum_fusion.sent, bf16[512,640]{1,0:T(8,128)(2,1)S(1)} %collective-permute-done.11.received, ...), custom_call_target="tpu_custom_call" | custom-call | flops 2684354560 | bytes 15728640 | tf_op jit(solution)/shard_map/pallas_call | solution.py:349
  171.0 1.2 collective-permute-done.15.x
  172.2 3.5 %shard_map.106 = bf16[512,2048]{1,0:T(8,128)(2,1)} custom-call(s32[2]{0:T(128)S(1)} %pad_add_fusion.facts, f32[512,2048]{1,0:T(8,128)S(1)} %get-tuple-element.66.total, bf16[512,2048]{1,0:T(8,128)(2,1)S(1)} %get-tuple-element.67.weight, bf16[512,512]{1,0:T(8,128)(2,1)S(1)} %collective-permute-done.15.x), custom_call_target="tpu_custom_call" | custom-call | flops 1073741824 | bytes 2097152 | tf_op jit(solution)/shard_map/pallas_call | solution.py:386
  (39 shorter events, 1.1 us)
Async XLA Ops:
  0.0 50.1 %collective-permute-start = (bf16[512,2048]{1,0:T(8,128)(2,1)}, bf16[512,2048]{1,0:T(8,128)(2,1)S(1)}, u32[]{:S(2)}, u32[]{:S(2)}) collective-permute-start(bf16[512,2048]{1,0:T(8,128)(2,1)} %refs_0_.4), channel_id=1, source_target_pairs={{0,4},{4,8},{8,12},{1,5},{5,9},{9,13},{2,6},{6,10},{10,14},{3,7},{... | collective-permute-start | bytes 6291464 | tf_op jit(solution)/shard_map/ppermute | solution.py:452
  5.1 49.3 %collective-permute-start.1 = (bf16[512,2048]{1,0:T(8,128)(2,1)}, bf16[512,2048]{1,0:T(8,128)(2,1)}, u32[]{:S(2)}, u32[]{:S(2)}) collective-permute-start(bf16[512,2048]{1,0:T(8,128)(2,1)} %refs_0_.4), channel_id=1, source_target_pairs={{4,0},{8,4},{12,8},{5,1},{9,5},{13,9},{6,2},{10,6},{14,10},{7,3},{... | collective-permute-start | bytes 6291464 | tf_op jit(solution)/shard_map/ppermute | solution.py:453
  6.4 48.0 %collective-permute-start.3 = (bf16[4,32,8192]{2,1,0:T(8,128)(2,1)}, bf16[4,32,8192]{2,1,0:T(8,128)(2,1)}, u32[]{:S(2)}, u32[]{:S(2)}) collective-permute-start(bf16[4,32,8192]{2,1,0:T(8,128)(2,1)} %refs_0_.3), channel_id=1, source_target_pairs={{0,2},{1,3},{2,0},{3,1},{4,6},{5,7},{6,4},{7,5},{8,10},{9,11},{10,... | collective-permute-start | bytes 6291464 | tf_op jit(solution)/shard_map/ppermute | solution.py:437
  7.9 50.8 %collective-permute-start.2 = (bf16[4,32,8192]{2,1,0:T(8,128)(2,1)}, bf16[4,32,8192]{2,1,0:T(8,128)(2,1)}, u32[]{:S(2)}, u32[]{:S(2)}) collective-permute-start(bf16[4,32,8192]{2,1,0:T(8,128)(2,1)} %refs_0_.3), channel_id=1, source_target_pairs={{0,1},{1,0},{2,3},{3,2},{4,5},{5,4},{6,7},{7,6},{8,9},{9,8},{10,11... | collective-permute-start | bytes 6291464 | tf_op jit(solution)/shard_map/ppermute | solution.py:437
  50.1 4.3 %copy-start.4 = (bf16[512,2048]{1,0:T(8,128)(2,1)}, bf16[512,2048]{1,0:T(8,128)(2,1)S(1)}, u32[]{:S(2)}) copy-start(bf16[512,2048]{1,0:T(8,128)(2,1)S(1)} %collective-permute-done.refs_1_.left_1) | copy-start | bytes 6291460
  54.4 4.4 %collective-permute-start.4 = (bf16[4,32,8192]{2,1,0:T(8,128)(2,1)}, bf16[4,32,8192]{2,1,0:T(8,128)(2,1)S(1)}, u32[]{:S(2)}, u32[]{:S(2)}) collective-permute-start(bf16[4,32,8192]{2,1,0:T(8,128)(2,1)} %collective-permute-done.3.refs_2_), channel_id=1, source_target_pairs={{0,1},{1,0},{2,3},{3,2},{4,5},{5,4},{6,7},{7,6},{8,9},{9,8},{10,11... | collective-permute-start | bytes 6291464 | tf_op jit(solution)/shard_map/ppermute | solution.py:437
  54.4 44.9 %collective-permute-start.5 = (bf16[512,2048]{1,0:T(8,128)(2,1)}, bf16[512,2048]{1,0:T(8,128)(2,1)S(1)}, u32[]{:S(2)}, u32[]{:S(2)}) collective-permute-start(bf16[512,2048]{1,0:T(8,128)(2,1)} %copy-done.4), channel_id=1, source_target_pairs={{4,8},{8,12},{5,9},{9,13},{6,10},{10,14},{7,11},{11,15},{20,24},{2... | collective-permute-start | bytes 6291464 | tf_op jit(solution)/shard_map/ppermute | solution.py:461
  55.2 52.7 %collective-permute-start.6 = (bf16[512,2048]{1,0:T(8,128)(2,1)}, bf16[512,2048]{1,0:T(8,128)(2,1)}, u32[]{:S(2)}, u32[]{:S(2)}) collective-permute-start(bf16[512,2048]{1,0:T(8,128)(2,1)} %collective-permute-done.1.refs_2_.right_1), channel_id=1, source_target_pairs={{4,0},{8,4},{5,1},{9,5},{6,2},{10,6},{7,3},{11,7},{20,16},{24,20},... | collective-permute-start | bytes 6291464 | tf_op jit(solution)/shard_map/ppermute | solution.py:462
  56.5 53.8 %collective-permute-start.13 = (bf16[4,128,2048]{2,1,0:T(8,128)(2,1)}, bf16[4,128,2048]{2,1,0:T(8,128)(2,1)}, u32[]{:S(2)}, u32[]{:S(2)}) collective-permute-start(bf16[4,128,2048]{2,1,0:T(8,128)(2,1)} %refs_0_.5), channel_id=1, source_target_pairs={{0,2},{1,3},{2,0},{3,1},{4,6},{5,7},{6,4},{7,5},{8,10},{9,11},{10,... | collective-permute-start | bytes 6291464 | tf_op jit(solution)/shard_map/ppermute | solution.py:437
  58.7 1.6 copy-start.2
  60.3 16.1 %copy-start.8 = (s32[512]{0:T(512)S(1)}, s32[512]{0:T(512)}, u32[]{:S(2)}) copy-start(s32[512]{0:T(512)} %param.16) | copy-start | bytes 6148
  66.2 2.0 %copy-start = (bf16[8192,256]{1,0:T(8,128)(2,1)}, bf16[8192,256]{1,0:T(8,128)(2,1)S(1)}, u32[]{:S(2)}) copy-start(bf16[8192,256]{1,0:T(8,128)(2,1)S(1)} %get-tuple-element.45.refs_4_.down) | copy-start | bytes 12582916
  68.1 57.8 %collective-permute-start.8 = (bf16[4096,256]{1,0:T(8,128)(2,1)}, bf16[4096,256]{1,0:T(8,128)(2,1)}, u32[]{:S(2)}, u32[]{:S(2)}) collective-permute-start(bf16[4096,256]{1,0:T(8,128)(2,1)} %get-tuple-element.52), channel_id=1, source_target_pairs={{0,4},{12,8},{1,5},{13,9},{2,6},{14,10},{3,7},{15,11},{16,20},{28,... | collective-permute-start | bytes 6291464 | tf_op jit(solution)/shard_map/ppermute | solution.py:465
  76.6 84.9 %collective-permute-start.12 = (bf16[4,128,2048]{2,1,0:T(8,128)(2,1)}, bf16[4,128,2048]{2,1,0:T(8,128)(2,1)}, u32[]{:S(2)}, u32[]{:S(2)}) collective-permute-start(bf16[4,128,2048]{2,1,0:T(8,128)(2,1)} %refs_0_.5), channel_id=1, source_target_pairs={{0,1},{1,0},{2,3},{3,2},{4,5},{5,4},{6,7},{7,6},{8,9},{9,8},{10,11... | collective-permute-start | bytes 6291464 | tf_op jit(solution)/shard_map/ppermute | solution.py:437
  76.7 1.6 copy-start.5
  78.3 1.6 copy-start.7
  110.3 51.3 %collective-permute-start.14 = (bf16[4,128,2048]{2,1,0:T(8,128)(2,1)}, bf16[4,128,2048]{2,1,0:T(8,128)(2,1)}, u32[]{:S(2)}, u32[]{:S(2)}) collective-permute-start(bf16[4,128,2048]{2,1,0:T(8,128)(2,1)} %collective-permute-done.13.refs_2_), channel_id=1, source_target_pairs={{0,1},{1,0},{2,3},{3,2},{4,5},{5,4},{6,7},{7,6},{8,9},{9,8},{10,11... | collective-permute-start | bytes 6291464 | tf_op jit(solution)/shard_map/ppermute | solution.py:437
  110.4 15.5 %collective-permute-start.9 = (f32[512,32]{1,0:T(8,128)S(1)}, f32[512,32]{1,0:T(8,128)S(1)}, u32[]{:S(2)}, u32[]{:S(2)}) collective-permute-start(f32[512,32]{1,0:T(8,128)S(1)} %get-tuple-element.53.low), channel_id=1, source_target_pairs={{0,4},{12,8},{1,5},{13,9},{2,6},{14,10},{3,7},{15,11},{16,20},{28,... | collective-permute-start | bytes 196616 | tf_op jit(solution)/shard_map/ppermute | solution.py:470
  115.1 39.5 %collective-permute-start.7 = (bf16[512,1024]{1,0:T(8,128)(2,1)}, bf16[512,1024]{1,0:T(8,128)(2,1)S(1)}, u32[]{:S(2)}, u32[]{:S(2)}) collective-permute-start(bf16[512,1024]{1,0:T(8,128)(2,1)} %slice_select_fusion), channel_id=1, source_target_pairs={{8,12},{4,0},{9,13},{5,1},{10,14},{6,2},{11,15},{7,3},{24,28},{20,... | collective-permute-start | bytes 3145736 | tf_op jit(solution)/shard_map/ppermute | solution.py:481
  125.9 2.2 %copy-start.1 = (bf16[8192,256]{1,0:T(8,128)(2,1)S(1)}, bf16[8192,256]{1,0:T(8,128)(2,1)}, u32[]{:S(2)}) copy-start(bf16[8192,256]{1,0:T(8,128)(2,1)} %copy-done) | copy-start | bytes 12582916
  128.1 1.6 copy-start.6
  136.9 2.0 %collective-permute-start.10 = (bf16[512,64]{1,0:T(8,128)(2,1)S(1)}, bf16[512,64]{1,0:T(8,128)(2,1)S(1)}, u32[]{:S(2)}, u32[]{:S(2)}) collective-permute-start(bf16[512,64]{1,0:T(8,128)(2,1)S(1)} %shard_map.102), channel_id=1, source_target_pairs={{4,8},{8,4},{5,9},{9,5},{6,10},{10,6},{7,11},{11,7},{20,24},{24,20... | collective-permute-start | bytes 196616 | tf_op jit(solution)/shard_map/ppermute | solution.py:488
  139.1 24.4 %collective-permute-start.11 = (bf16[512,640]{1,0:T(8,128)(2,1)S(1)}, bf16[512,640]{1,0:T(8,128)(2,1)S(1)}, u32[]{:S(2)}, u32[]{:S(2)}) collective-permute-start(bf16[512,640]{1,0:T(8,128)(2,1)S(1)} %pad_maximum_fusion.sent), channel_id=1, source_target_pairs={{8,12},{4,0},{9,13},{5,1},{10,14},{6,2},{11,15},{7,3},{24,28},{20,... | collective-permute-start | bytes 1966088 | tf_op jit(solution)/shard_map/ppermute | solution.py:492
  141.6 30.7 %collective-permute-start.15 = (bf16[512,512]{1,0:T(8,128)(2,1)S(1)}, bf16[512,512]{1,0:T(8,128)(2,1)S(1)}, u32[]{:S(2)}, u32[]{:S(2)}) collective-permute-start(bf16[512,512]{1,0:T(8,128)(2,1)S(1)} %slice_select_fusion.1), channel_id=1, source_target_pairs={{8,12},{4,0},{9,13},{5,1},{10,14},{6,2},{11,15},{7,3},{24,28},{20,... | collective-permute-start | bytes 1572872 | tf_op jit(solution)/shard_map/ppermute | solution.py:494
  163.5 1.6 copy-start.3

commit v14 on v13

--- a/solution.py
+++ b/solution.py
@@ -54,7 +54,7 @@
 
             @pl.when((upper[0] != 0) == (t < half))
             def _():
-                other[t % half * width:(t % half + 1) * width] = joined
+                other[:, t % half * width:(t % half + 1) * width] = held[t, :entries * rank_part]
 
 
 def join_downs(places, upper, blocks, shards):
@@ -63,13 +63,16 @@
     width, slots = features // shards, -(-entries * rank_part // 128) * 128
     return pl.pallas_call(
         join_downs_kernel,
-        out_shape=[jax.ShapeDtypeStruct((a, slots), BF16) for a in (features, features // 2)],
+        out_shape=[
+            jax.ShapeDtypeStruct((features, slots), BF16),
+            jax.ShapeDtypeStruct((entries * rank_part, features // 2), BF16),
+        ],
         grid=(shards,),
         in_specs=[pl.BlockSpec(memory_space=pltpu.SMEM)] * 2
         + [pl.BlockSpec(memory_space=pltpu.HBM)] * len(blocks),
         out_specs=[
             pl.BlockSpec((width, slots), lambda t: (t, 0)),
-            pl.BlockSpec((features // 2, slots), lambda t: (0, 0)),
+            pl.BlockSpec((entries * rank_part, features // 2), lambda t: (0, 0)),
         ],
         scratch_shapes=[pltpu.VMEM((shards, slots, width), BF16), pltpu.SemaphoreType.DMA((shards, entries))],
         compiler_params=TAIL_PARAMS,
@@ -78,6 +81,12 @@
 
 
 RESIDENT = pl.BlockSpec(memory_space=pltpu.VMEM)
+
+
+def in_hbm(a):
+    return pltpu.with_memory_space_constraint(a, pltpu.HBM)
+
+
 IN_HBM = pl.BlockSpec(memory_space=pltpu.HBM)
 
 
@@ -253,10 +262,10 @@
     own = finished(low, jnp.dot(far_x[...], rows_of[...], preferred_element_type=F32), me)
     pltpu.make_async_copy(left_1, near_x, sems.at[1]).wait()
     copies[1].wait()
-    far_rows = other_rows[pl.ds(pl.multiple_of((1 - upper) * width, width), width)]
-    near_rows = other_rows[pl.ds(pl.multiple_of(upper * width, width), width)]
-    sums = jnp.dot(far_x[...], far_rows, preferred_element_type=F32)
-    sums += jnp.dot(near_x[...], near_rows, preferred_element_type=F32)
+    sums = jnp.zeros((far_x.shape[0], other_rows.shape[0]), F32)
+    for x, place in ((far_x, 1 - upper), (near_x, upper)):
+        rows = other_rows[:, pl.ds(pl.multiple_of(place * width, width), width)]
+        sums += lax.dot_general(x[...], rows, (((1,), (1,)), ((), ())), preferred_element_type=F32)
     other = finished(other_low, sums, end)
     at_left = jnp.concatenate([other, own], axis=1)
     at_right = jnp.concatenate([own, other], axis=1)
@@ -275,14 +284,14 @@
             pltpu.VMEM((rows, width), BF16),
             pltpu.VMEM((rows, width), BF16),
             pltpu.VMEM((width, slots), BF16),
-            pltpu.VMEM((2 * width, slots), BF16),
+            pltpu.VMEM(other_down.shape, BF16),
             pltpu.SemaphoreType.DMA((4,)),
         ],
         compiler_params=TAIL_PARAMS,
         cost_estimate=pl.CostEstimate(
             flops=6 * width * rows * slots, bytes_accessed=2 * width * (2 * rows + 3 * slots), transcendentals=0
         ),
-    )(facts, left_1, left_2, right_1, right_2, down, other_down, slot, row_rank, low, other_low)
+    )(facts, left_1, left_2, right_1, right_2, in_hbm(down), other_down, slot, row_rank, low, other_low)
 
 
 def prepare_kernel(facts, places, base, sent, received, weight, *refs):
@@ -364,7 +373,7 @@
             bytes_accessed=2 * (columns + entries * rank + 2 * rows) * columns,
             transcendentals=0,
         ),
-    )(facts, places, base, sent, received, weight, *blocks, slot)
+    )(facts, places, base, sent, received, weight, in_hbm(blocks[0]), *blocks[1:], slot)
 
 
 def last_kernel(facts, total, weight, x, out):

time: 177 us -> 172 us (0.972)
  local copies, waits for them, and re-layouts: 15.2 us -> 8.96 us
    unnamed x18 -> x12, local copies, waits for them, and re-layouts: 12.1 us -> 5.17 us
    ppermute x1, waiting for transfers between devices: 9.57 us -> 4.28 us  [local(): other_low = lax.ppermute(low, 'tensor', [(0, 1), (3, 2)])]
    ppermute x1, waiting for transfers between devices: 1.24 us -> 4.49 us  [local(): last_3 = lax.ppermute(piece(2), 'tensor', third)]
    ppermute x1, waiting for transfers between devices: 8.61 us -> 11.7 us  [local(): left_2 = lax.ppermute(left_1, 'tensor', left[:-1])]
  transfers between devices with their start and end apart: 16 -> 16, of which waited for: 7 -> 6; matrix products, arithmetic and copies ran while one was open for 8% -> 9% of each run, Pallas kernels for 32% -> 34%
where the time goes in v14:
time: 172 us; the launch traced here: 171 us
  waiting for transfers between devices  61.1 us (36%)
  Pallas kernels  61 us (35%)
  starting transfers between devices  28.4 us (17%)
  other arithmetic  11.6 us (7%)
  local copies, waits for them, and re-layouts  8.96 us (5%)
    ppermute x1, waiting for transfers between devices, local(): right_1 = lax.ppermute(attention_result, 'tensor', right)  33.7 us
    pallas_call x2, Pallas kernels, add_shards(): pl.pallas_call(functools.partial(shards_kernel, base is None), out_shape=...  31.1 us
    ppermute x1, waiting for transfers between devices, local(): left_2 = lax.ppermute(left_1, 'tensor', left[:-1])  11.7 us
    pallas_call x1, Pallas kernels, far_low(): pl.pallas_call(far_low_kernel, out_shape=jax.ShapeDtypeStruct((rows, 2 *...  8.05 us
    ppermute x1, starting transfers between devices, local(): other_down = lax.ppermute(other_down, 'tensor', [(0, 1), (3, 2)])  8.01 us
    pallas_call x1, Pallas kernels, add_half(): pl.pallas_call(half_kernel, out_shape=jax.ShapeDtypeStruct((rows, columns...  6.9 us
    pallas_call x1, Pallas kernels, prepare(): pl.pallas_call(prepare_kernel, out_shape=[pltpu.VMEM((rows, columns), F32...  6.04 us
    pallas_call x1, Pallas kernels, join_downs(): pl.pallas_call(join_downs_kernel, out_shape=[jax.ShapeDtypeStruct((featur...  5.39 us
  transfers between devices with their start and end apart: 16, of which 6 were waited for; matrix products, arithmetic and copies ran while one was open for 9% of the time, Pallas kernels for 34%

profile of v14, /device:TPU:0, one launch (start us, length us, event | category | flops | bytes accessed | tf_op | source)
XLA Modules:
  0.0 171.3 jit_solution(5628801474083052563)
XLA Ops:
  0.0 5.1 %collective-permute-start = (bf16[512,2048]{1,0:T(8,128)(2,1)}, bf16[512,2048]{1,0:T(8,128)(2,1)S(1)}, u32[]{:S(2)}, u32[]{:S(2)}) collective-permute-start(bf16[512,2048]{1,0:T(8,128)(2,1)} %refs_0_.4), channel_id=1, source_target_pairs={{0,4},{4,8},{8,12},{1,5},{5,9},{9,13},{2,6},{6,10},{10,14},{3,7},{... | collective-permute-start | bytes 6291464 | tf_op jit(solution)/shard_map/ppermute | solution.py:461
  5.1 1.3 collective-permute-start.1
  6.4 1.6 collective-permute-start.3
  7.9 0.7 fusion
  8.6 0.6 slice.39
  9.2 0.7 add_bitcast_fusion
  10.0 0.7 fusion.4
  10.7 0.1 copy.20
  10.8 0.7 fusion.1
  11.6 0.7 fusion.5
  12.2 1.5 add_reduce_fusion
  13.7 0.7 fusion.3
  14.7 0.9 select_reduce_fusion.1
  15.6 0.8 select_reduce_fusion
  16.4 33.7 %collective-permute-done.refs_1_.left_1 = bf16[512,2048]{1,0:T(8,128)(2,1)S(1)} collective-permute-done((bf16[512,2048]{1,0:T(8,128)(2,1)}, bf16[512,2048]{1,0:T(8,128)(2,1)S(1)}, u32[]{:S(2)}, u32[]{:S(2)}) %collective-permute-start) | collective-permute-done | bytes 2097184 | tf_op jit(solution)/shard_map/ppermute | solution.py:461
  50.1 4.2 %collective-permute-done.1.refs_2_.right_1 = bf16[512,2048]{1,0:T(8,128)(2,1)} collective-permute-done((bf16[512,2048]{1,0:T(8,128)(2,1)}, bf16[512,2048]{1,0:T(8,128)(2,1)}, u32[]{:S(2)}, u32[]{:S(2)}) %collective-permute-start.1) | collective-permute-done | bytes 2097184 | tf_op jit(solution)/shard_map/ppermute | solution.py:462
  54.4 0.8 collective-permute-start.5
  55.2 1.3 collective-permute-start.6
  56.5 1.6 collective-permute-start.13
  58.0 0.6 slice.45.upper
  58.6 0.8 copy.21.refs_5_.slot.refs_4_
  59.5 0.3 collective-permute-start.12
  59.8 1.6 copy-done.1
  61.4 5.4 %shard_map.100 = (bf16[8192,256]{1,0:T(8,128)(2,1)S(1)}, bf16[192,4096]{1,0:T(8,128)(2,1)}) custom-call(s32[6]{0:T(128)S(1)} %fusion.2.places, s32[1]{0:T(128)} %slice.45.upper, bf16[4,32,8192]{2,1,0:T(8,128)(2,1)S(1)} %copy-done.1, bf16[4,32,8192]{2,1,0:T(8,128)(2,1)} %collective-permute-done.2.refs_1_, ...), custom_call_target="tpu_custom_call" | custom-call | bytes 8388608 | tf_op jit(solution)/shard_map/pallas_call | solution.py:64
  66.8 2.0 %copy-done = bf16[8192,256]{1,0:T(8,128)(2,1)} copy-done((bf16[8192,256]{1,0:T(8,128)(2,1)}, bf16[8192,256]{1,0:T(8,128)(2,1)S(1)}, u32[]{:S(2)}) %copy-start) | copy-done | bytes 4194328
  68.7 8.0 %collective-permute-start.8 = (bf16[192,4096]{1,0:T(8,128)(2,1)}, bf16[192,4096]{1,0:T(8,128)(2,1)}, u32[]{:S(2)}, u32[]{:S(2)}) collective-permute-start(bf16[192,4096]{1,0:T(8,128)(2,1)} %get-tuple-element.52), channel_id=1, source_target_pairs={{0,4},{12,8},{1,5},{13,9},{2,6},{14,10},{3,7},{15,11},{16,20},{28,... | collective-permute-start | bytes 4718600 | tf_op jit(solution)/shard_map/ppermute | solution.py:474
  76.8 19.4 %shard_map.101 = (f32[512,2048]{1,0:T(8,128)}, f32[512,32]{1,0:T(8,128)S(1)}) custom-call(s32[6]{0:T(128)S(1)} %select_n.86.start, s32[3]{0:T(128)S(1)} %get-tuple-element.40.valid, bf16[512,2048]{1,0:T(8,128)(2,1)S(1)} %copy-done.5, bf16[512,2048]{1,0:T(8,128)(2,1)S(1)} %copy-done.3, bf16[512,2048]{1,0:T(8,128)(2,1)} %collective-permute-done.1.refs_2_.right_1, ...), custom_call_target="tpu_custom_call" | custom-call | flops 14495514624 | bytes 42991616 | tf_op jit(solution)/shard_map/pallas_call | solution.py:169
  96.2 11.7 %collective-permute-done.6.right_2.refs_1_ = bf16[512,2048]{1,0:T(8,128)(2,1)} collective-permute-done((bf16[512,2048]{1,0:T(8,128)(2,1)}, bf16[512,2048]{1,0:T(8,128)(2,1)}, u32[]{:S(2)}, u32[]{:S(2)}) %collective-permute-start.6) | collective-permute-done | bytes 2097184 | tf_op jit(solution)/shard_map/ppermute | solution.py:471
  107.9 2.3 %slice_select_fusion = bf16[512,1024]{1,0:T(8,128)(2,1)} fusion(bf16[512,2048]{1,0:T(8,128)(2,1)} %collective-permute-done.6.right_2.refs_1_, bf16[512,2048]{1,0:T(8,128)(2,1)S(1)} %collective-permute-done.5.left_2.refs_0_, pred[]{:T(512)S(6)} %ge.9), kind=kLoop, calls=%fused_computation | loop fusion | flops 524288 | bytes 3145729 | tf_op jit(solution)/shard_map/jit(_where)/select_n | solution.py:487
  110.3 0.1 copy.23.row_rank
  110.4 4.1 %collective-permute-start.9 = (f32[512,32]{1,0:T(8,128)S(1)}, f32[512,32]{1,0:T(8,128)S(1)}, u32[]{:S(2)}, u32[]{:S(2)}) collective-permute-start(f32[512,32]{1,0:T(8,128)S(1)} %get-tuple-element.53.low), channel_id=1, source_target_pairs={{0,4},{12,8},{1,5},{13,9},{2,6},{14,10},{3,7},{15,11},{16,20},{28,... | collective-permute-start | bytes 196616 | tf_op jit(solution)/shard_map/ppermute | solution.py:479
  114.5 0.6 fusion.6
  115.1 1.3 collective-permute-start.7
  116.4 4.3 %collective-permute-done.9.other_low = f32[512,32]{1,0:T(8,128)S(1)} collective-permute-done((f32[512,32]{1,0:T(8,128)S(1)}, f32[512,32]{1,0:T(8,128)S(1)}, u32[]{:S(2)}, u32[]{:S(2)}) %collective-permute-start.9) | collective-permute-done | bytes 65568 | tf_op jit(solution)/shard_map/ppermute | solution.py:479
  120.7 1.6 copy-done.4
  122.3 8.0 %shard_map.102 = bf16[512,64]{1,0:T(8,128)(2,1)S(1)} custom-call(s32[4]{0:T(128)S(1)} %pad_add_fusion.1.facts, bf16[512,2048]{1,0:T(8,128)(2,1)S(1)} %copy-done.4, bf16[512,2048]{1,0:T(8,128)(2,1)S(1)} %collective-permute-done.5.left_2.refs_0_, bf16[512,2048]{1,0:T(8,128)(2,1)} %collective-permute-done.1.refs_2_.right_1, ...), custom_call_target="tpu_custom_call" | custom-call | flops 1610612736 | bytes 7340032 | tf_op jit(solution)/shard_map/pallas_call | solution.py:278
  130.4 0.7 collective-permute-start.10
  131.0 1.1 slice_select_fusion.2
  132.1 0.1 maximum_select_fusion
  132.4 1.3 collective-permute-start.11
  133.7 1.1 slice_select_fusion.1
  134.8 1.3 collective-permute-start.15
  136.1 11.7 %shard_map.103.base_in = f32[512,2048]{1,0:T(8,128)} custom-call(s32[4]{0:T(128)S(1)} %select_n.88.start, s32[2]{0:T(128)S(1)} %get-tuple-element.51.valid, bf16[512,2048]{1,0:T(8,128)(2,1)S(1)} %collective-permute-done.5.left_2.refs_0_, bf16[512,2048]{1,0:T(8,128)(2,1)} %collective-permute-done.6.right_2.refs_1_, bf16[8192,2048]{1,0:T(8,128)(2,1)} %weight.3, ...), custom_call_target="tpu_custom_call" | custom-call | flops 8589934592 | bytes 29360128 | tf_op jit(solution)/shard_map/pallas_call | solution.py:169
  147.7 6.9 %shard_map.104.base = f32[512,2048]{1,0:T(8,128)S(1)} custom-call(s32[1]{0:T(128)} %get-tuple-element.78.start, s32[1]{0:T(128)} %get-tuple-element.77.valid, bf16[512,1024]{1,0:T(8,128)(2,1)S(1)} %collective-permute-done.7.x, bf16[8192,2048]{1,0:T(8,128)(2,1)} %weight.3, f32[512,2048]{1,0:T(8,128)} %shard_map.103.base_in), custom_call_target="tpu_custom_call" | custom-call | flops 2147483648 | bytes 13631488 | tf_op jit(solution)/shard_map/pallas_call | solution.py:207
  154.7 2.6 %collective-permute-done.11.received = bf16[512,640]{1,0:T(8,128)(2,1)S(1)} collective-permute-done((bf16[512,640]{1,0:T(8,128)(2,1)S(1)}, bf16[512,640]{1,0:T(8,128)(2,1)S(1)}, u32[]{:S(2)}, u32[]{:S(2)}) %collective-permute-start.11) | collective-permute-done | bytes 655392 | tf_op jit(solution)/shard_map/ppermute | solution.py:501
  157.3 6.0 %shard_map.105 = (f32[512,2048]{1,0:T(8,128)S(1)}, bf16[512,2048]{1,0:T(8,128)(2,1)S(1)}) custom-call(s32[2]{0:T(128)S(1)} %pad_add_fusion.facts, s32[6]{0:T(128)S(1)} %fusion.2.places, f32[512,2048]{1,0:T(8,128)S(1)} %shard_map.104.base, bf16[512,640]{1,0:T(8,128)(2,1)S(1)} %pad_maximum_fusion.sent, bf16[512,640]{1,0:T(8,128)(2,1)S(1)} %collective-permute-done.11.received, ...), custom_call_target="tpu_custom_call" | custom-call | flops 2684354560 | bytes 15728640 | tf_op jit(solution)/shard_map/pallas_call | solution.py:358
  163.3 4.5 %collective-permute-done.15.x = bf16[512,512]{1,0:T(8,128)(2,1)S(1)} collective-permute-done((bf16[512,512]{1,0:T(8,128)(2,1)S(1)}, bf16[512,512]{1,0:T(8,128)(2,1)S(1)}, u32[]{:S(2)}, u32[]{:S(2)}) %collective-permute-start.15) | collective-permute-done | bytes 524320 | tf_op jit(solution)/shard_map/ppermute | solution.py:503
  167.8 3.5 %shard_map.106 = bf16[512,2048]{1,0:T(8,128)(2,1)} custom-call(s32[2]{0:T(128)S(1)} %pad_add_fusion.facts, f32[512,2048]{1,0:T(8,128)S(1)} %get-tuple-element.66.total, bf16[512,2048]{1,0:T(8,128)(2,1)S(1)} %get-tuple-element.67.weight, bf16[512,512]{1,0:T(8,128)(2,1)S(1)} %collective-permute-done.15.x), custom_call_target="tpu_custom_call" | custom-call | flops 1073741824 | bytes 2097152 | tf_op jit(solution)/shard_map/pallas_call | solution.py:395
  (33 shorter events, 0.6 us)
Async XLA Ops:
  0.0 50.1 %collective-permute-start = (bf16[512,2048]{1,0:T(8,128)(2,1)}, bf16[512,2048]{1,0:T(8,128)(2,1)S(1)}, u32[]{:S(2)}, u32[]{:S(2)}) collective-permute-start(bf16[512,2048]{1,0:T(8,128)(2,1)} %refs_0_.4), channel_id=1, source_target_pairs={{0,4},{4,8},{8,12},{1,5},{5,9},{9,13},{2,6},{6,10},{10,14},{3,7},{... | collective-permute-start | bytes 6291464 | tf_op jit(solution)/shard_map/ppermute | solution.py:461
  5.1 49.3 %collective-permute-start.1 = (bf16[512,2048]{1,0:T(8,128)(2,1)}, bf16[512,2048]{1,0:T(8,128)(2,1)}, u32[]{:S(2)}, u32[]{:S(2)}) collective-permute-start(bf16[512,2048]{1,0:T(8,128)(2,1)} %refs_0_.4), channel_id=1, source_target_pairs={{4,0},{8,4},{12,8},{5,1},{9,5},{13,9},{6,2},{10,6},{14,10},{7,3},{... | collective-permute-start | bytes 6291464 | tf_op jit(solution)/shard_map/ppermute | solution.py:462
  6.4 48.0 %collective-permute-start.3 = (bf16[4,32,8192]{2,1,0:T(8,128)(2,1)}, bf16[4,32,8192]{2,1,0:T(8,128)(2,1)}, u32[]{:S(2)}, u32[]{:S(2)}) collective-permute-start(bf16[4,32,8192]{2,1,0:T(8,128)(2,1)} %refs_0_.3), channel_id=1, source_target_pairs={{0,2},{1,3},{2,0},{3,1},{4,6},{5,7},{6,4},{7,5},{8,10},{9,11},{10,... | collective-permute-start | bytes 6291464 | tf_op jit(solution)/shard_map/ppermute | solution.py:446
  7.9 51.6 %collective-permute-start.2 = (bf16[4,32,8192]{2,1,0:T(8,128)(2,1)}, bf16[4,32,8192]{2,1,0:T(8,128)(2,1)}, u32[]{:S(2)}, u32[]{:S(2)}) collective-permute-start(bf16[4,32,8192]{2,1,0:T(8,128)(2,1)} %refs_0_.3), channel_id=1, source_target_pairs={{0,1},{1,0},{2,3},{3,2},{4,5},{5,4},{6,7},{7,6},{8,9},{9,8},{10,11... | collective-permute-start | bytes 6291464 | tf_op jit(solution)/shard_map/ppermute | solution.py:446
  50.1 4.3 %copy-start.2 = (bf16[512,2048]{1,0:T(8,128)(2,1)}, bf16[512,2048]{1,0:T(8,128)(2,1)S(1)}, u32[]{:S(2)}) copy-start(bf16[512,2048]{1,0:T(8,128)(2,1)S(1)} %collective-permute-done.refs_1_.left_1) | copy-start | bytes 6291460
  54.4 5.4 %collective-permute-start.4 = (bf16[4,32,8192]{2,1,0:T(8,128)(2,1)}, bf16[4,32,8192]{2,1,0:T(8,128)(2,1)}, u32[]{:S(2)}, u32[]{:S(2)}) collective-permute-start(bf16[4,32,8192]{2,1,0:T(8,128)(2,1)} %collective-permute-done.3.refs_2_), channel_id=1, source_target_pairs={{0,1},{1,0},{2,3},{3,2},{4,5},{5,4},{6,7},{7,6},{8,9},{9,8},{10,11... | collective-permute-start | bytes 6291464 | tf_op jit(solution)/shard_map/ppermute | solution.py:446
  54.4 41.8 %collective-permute-start.5 = (bf16[512,2048]{1,0:T(8,128)(2,1)}, bf16[512,2048]{1,0:T(8,128)(2,1)S(1)}, u32[]{:S(2)}, u32[]{:S(2)}) collective-permute-start(bf16[512,2048]{1,0:T(8,128)(2,1)} %copy-done.2), channel_id=1, source_target_pairs={{4,8},{8,12},{5,9},{9,13},{6,10},{10,14},{7,11},{11,15},{20,24},{2... | collective-permute-start | bytes 6291464 | tf_op jit(solution)/shard_map/ppermute | solution.py:470
  55.2 52.7 %collective-permute-start.6 = (bf16[512,2048]{1,0:T(8,128)(2,1)}, bf16[512,2048]{1,0:T(8,128)(2,1)}, u32[]{:S(2)}, u32[]{:S(2)}) collective-permute-start(bf16[512,2048]{1,0:T(8,128)(2,1)} %collective-permute-done.1.refs_2_.right_1), channel_id=1, source_target_pairs={{4,0},{8,4},{5,1},{9,5},{6,2},{10,6},{7,3},{11,7},{20,16},{24,20},... | collective-permute-start | bytes 6291464 | tf_op jit(solution)/shard_map/ppermute | solution.py:471
  56.5 53.8 %collective-permute-start.13 = (bf16[4,128,2048]{2,1,0:T(8,128)(2,1)}, bf16[4,128,2048]{2,1,0:T(8,128)(2,1)}, u32[]{:S(2)}, u32[]{:S(2)}) collective-permute-start(bf16[4,128,2048]{2,1,0:T(8,128)(2,1)} %refs_0_.5), channel_id=1, source_target_pairs={{0,2},{1,3},{2,0},{3,1},{4,6},{5,7},{6,4},{7,5},{8,10},{9,11},{10,... | collective-permute-start | bytes 6291464 | tf_op jit(solution)/shard_map/ppermute | solution.py:446
  59.5 95.2 %collective-permute-start.12 = (bf16[4,128,2048]{2,1,0:T(8,128)(2,1)}, bf16[4,128,2048]{2,1,0:T(8,128)(2,1)}, u32[]{:S(2)}, u32[]{:S(2)}) collective-permute-start(bf16[4,128,2048]{2,1,0:T(8,128)(2,1)} %refs_0_.5), channel_id=1, source_target_pairs={{0,1},{1,0},{2,3},{3,2},{4,5},{5,4},{6,7},{7,6},{8,9},{9,8},{10,11... | collective-permute-start | bytes 6291464 | tf_op jit(solution)/shard_map/ppermute | solution.py:446
  59.8 1.6 copy-start.1
  61.4 15.4 %copy-start.3 = (bf16[512,2048]{1,0:T(8,128)(2,1)S(1)}, bf16[512,2048]{1,0:T(8,128)(2,1)}, u32[]{:S(2)}) copy-start(bf16[512,2048]{1,0:T(8,128)(2,1)} %copy-done.2) | copy-start | bytes 6291460
  61.4 15.4 %copy-start.5 = (bf16[512,2048]{1,0:T(8,128)(2,1)S(1)}, bf16[512,2048]{1,0:T(8,128)(2,1)}, u32[]{:S(2)}) copy-start(bf16[512,2048]{1,0:T(8,128)(2,1)} %refs_0_.4) | copy-start | bytes 6291460
  66.8 2.0 %copy-start = (bf16[8192,256]{1,0:T(8,128)(2,1)}, bf16[8192,256]{1,0:T(8,128)(2,1)S(1)}, u32[]{:S(2)}) copy-start(bf16[8192,256]{1,0:T(8,128)(2,1)S(1)} %get-tuple-element.45.refs_4_.down) | copy-start | bytes 12582916
  68.7 52.0 %collective-permute-start.8 = (bf16[192,4096]{1,0:T(8,128)(2,1)}, bf16[192,4096]{1,0:T(8,128)(2,1)}, u32[]{:S(2)}, u32[]{:S(2)}) collective-permute-start(bf16[192,4096]{1,0:T(8,128)(2,1)} %get-tuple-element.52), channel_id=1, source_target_pairs={{0,4},{12,8},{1,5},{13,9},{2,6},{14,10},{3,7},{15,11},{16,20},{28,... | collective-permute-start | bytes 4718600 | tf_op jit(solution)/shard_map/ppermute | solution.py:474
  110.3 44.4 %collective-permute-start.14 = (bf16[4,128,2048]{2,1,0:T(8,128)(2,1)}, bf16[4,128,2048]{2,1,0:T(8,128)(2,1)}, u32[]{:S(2)}, u32[]{:S(2)}) collective-permute-start(bf16[4,128,2048]{2,1,0:T(8,128)(2,1)} %collective-permute-done.13.refs_2_), channel_id=1, source_target_pairs={{0,1},{1,0},{2,3},{3,2},{4,5},{5,4},{6,7},{7,6},{8,9},{9,8},{10,11... | collective-permute-start | bytes 6291464 | tf_op jit(solution)/shard_map/ppermute | solution.py:446
  110.4 10.3 %collective-permute-start.9 = (f32[512,32]{1,0:T(8,128)S(1)}, f32[512,32]{1,0:T(8,128)S(1)}, u32[]{:S(2)}, u32[]{:S(2)}) collective-permute-start(f32[512,32]{1,0:T(8,128)S(1)} %get-tuple-element.53.low), channel_id=1, source_target_pairs={{0,4},{12,8},{1,5},{13,9},{2,6},{14,10},{3,7},{15,11},{16,20},{28,... | collective-permute-start | bytes 196616 | tf_op jit(solution)/shard_map/ppermute | solution.py:479
  115.1 32.6 %collective-permute-start.7 = (bf16[512,1024]{1,0:T(8,128)(2,1)}, bf16[512,1024]{1,0:T(8,128)(2,1)S(1)}, u32[]{:S(2)}, u32[]{:S(2)}) collective-permute-start(bf16[512,1024]{1,0:T(8,128)(2,1)} %slice_select_fusion), channel_id=1, source_target_pairs={{8,12},{4,0},{9,13},{5,1},{10,14},{6,2},{11,15},{7,3},{24,28},{20,... | collective-permute-start | bytes 3145736 | tf_op jit(solution)/shard_map/ppermute | solution.py:490
  120.7 1.6 copy-start.4
  130.4 1.8 %collective-permute-start.10 = (bf16[512,64]{1,0:T(8,128)(2,1)S(1)}, bf16[512,64]{1,0:T(8,128)(2,1)S(1)}, u32[]{:S(2)}, u32[]{:S(2)}) collective-permute-start(bf16[512,64]{1,0:T(8,128)(2,1)S(1)} %shard_map.102), channel_id=1, source_target_pairs={{4,8},{8,4},{5,9},{9,5},{6,10},{10,6},{7,11},{11,7},{20,24},{24,20... | collective-permute-start | bytes 196616 | tf_op jit(solution)/shard_map/ppermute | solution.py:497
  132.4 24.9 %collective-permute-start.11 = (bf16[512,640]{1,0:T(8,128)(2,1)S(1)}, bf16[512,640]{1,0:T(8,128)(2,1)S(1)}, u32[]{:S(2)}, u32[]{:S(2)}) collective-permute-start(bf16[512,640]{1,0:T(8,128)(2,1)S(1)} %pad_maximum_fusion.sent), channel_id=1, source_target_pairs={{8,12},{4,0},{9,13},{5,1},{10,14},{6,2},{11,15},{7,3},{24,28},{20,... | collective-permute-start | bytes 1966088 | tf_op jit(solution)/shard_map/ppermute | solution.py:501
  134.8 33.0 %collective-permute-start.15 = (bf16[512,512]{1,0:T(8,128)(2,1)S(1)}, bf16[512,512]{1,0:T(8,128)(2,1)S(1)}, u32[]{:S(2)}, u32[]{:S(2)}) collective-permute-start(bf16[512,512]{1,0:T(8,128)(2,1)S(1)} %slice_select_fusion.1), channel_id=1, source_target_pairs={{8,12},{4,0},{9,13},{5,1},{10,14},{6,2},{11,15},{7,3},{24,28},{20,... | collective-permute-start | bytes 1572872 | tf_op jit(solution)/shard_map/ppermute | solution.py:503

commit v15 on v14

--- a/solution.py
+++ b/solution.py
@@ -223,7 +223,7 @@
             bytes_accessed=2 * half * (rows + columns) + 8 * rows * columns,
             transcendentals=0,
         ),
-    )(source[None], valid[None], x, weight, base)
+    )(source, valid, x, weight, base)
 
 
 def far_low_kernel(
@@ -459,18 +459,21 @@
     far = plan_shards(me + jnp.array([-2, 2], jnp.int32), n_tensor)
 
     right_1 = lax.ppermute(attention_result, "tensor", right)
-    left_1 = lax.ppermute(attention_result, "tensor", left)
+    left_1 = lax.ppermute(after(attention_result, facts), "tensor", left)
     far_down = across(adapter_down_weight, 2)
     far_up = across(adapter_up_weight, 2)
     near_down = across(adapter_down_weight, 1)
 
-    right_1, left_1, places, slot, live, facts, far_facts, near, far = lax.optimization_barrier(
-        (right_1, left_1, places, slot, row_rank[:, None], facts, far_facts, near, far)
+    right_1, left_1, places, slot, live, facts, far_facts, near, far, ended, started, is_upper = lax.optimization_barrier(
+        (
+            right_1, left_1, places, slot, row_rank[:, None], facts, far_facts, near, far,
+            ends.astype(jnp.int32)[None], farthest.astype(jnp.int32)[None], upper.astype(jnp.int32)[None],
+        )
     )
     right_2 = lax.ppermute(right_1, "tensor", right[1:])
     left_2 = lax.ppermute(left_1, "tensor", left[:-1])
     downs = (adapter_down_weight, near_down, far_down, across(after(far_down, right_1, left_1), 1))
-    down, other_down = join_downs(places, far_facts[3:], downs, n_tensor)
+    down, other_down = join_downs(places, is_upper, downs, n_tensor)
     other_down = lax.ppermute(other_down, "tensor", [(0, 1), (3, 2)])
 
     base, low = add_shards(
@@ -478,7 +481,8 @@
     )
     other_low = lax.ppermute(low, "tensor", [(0, 1), (3, 2)])
 
-    right_2, left_2 = lax.optimization_barrier((base, right_2, left_2))[1:]
+    near_up = across(after(adapter_up_weight, far_down), 1)
+    near_up, right_2, left_2 = lax.optimization_barrier((base, near_up, right_2, left_2))[1:]
     third = right[-1:] + left[:1]
     cuts = (0, width // 2, width // 4 * 3, width)
 
@@ -501,8 +505,8 @@
     second_3 = lax.ppermute(second_2, "tensor", third)
     right_2, left_2 = lax.optimization_barrier((second_2, right_2, left_2))[1:]
     last_3 = lax.ppermute(piece(2), "tensor", third)
-    ups = (adapter_up_weight, across(after(adapter_up_weight, far_down), 1), far_up, across(after(far_up, first_2), 1))
-    base = add_half(base, first_3, facts[0], facts[1], output_weight)
+    ups = (adapter_up_weight, near_up, far_up, across(after(far_up, first_2), 1))
+    base = add_half(base, first_3, ended, started, output_weight)
     total, rows_of = prepare(facts, places, base, second_2, second_3, output_weight, ups, slot)
     total, rows_of, last_3 = lax.optimization_barrier((total, rows_of, last_3))
     return add_last(facts, total, rows_of, last_3)

time: 172 us -> 175 us (1.017)
  waiting for transfers between devices: 61.1 us -> 65.7 us
  Pallas kernels: 61 us -> 59.2 us
  starting transfers between devices: 28.4 us -> 26.6 us
    ppermute x1, waiting for transfers between devices: 4.25 us -> 40.5 us  [local(): left_1 = lax.ppermute(after(attention_result, facts), 'tensor', left)]
    ppermute x1, waiting for transfers between devices: 33.7 us -> 0.01 us  [local(): right_1 = lax.ppermute(attention_result, 'tensor', right)]
    unnamed x12, local copies, waits for them, and re-layouts: 5.17 us -> 8.06 us
  transfers between devices with their start and end apart: 16 -> 16, of which waited for: 6 -> 6; matrix products, arithmetic and copies ran while one was open for 9% -> 8% of each run, Pallas kernels for 34% -> 32%
where the time goes in v15:
time: 175 us; the launch traced here: 174 us
  waiting for transfers between devices  65.7 us (38%)
  Pallas kernels  59.2 us (34%)
  starting transfers between devices  26.6 us (15%)
  other arithmetic  11.5 us (7%)
  local copies, waits for them, and re-layouts  10.5 us (6%)
    ppermute x1, waiting for transfers between devices, local(): left_1 = lax.ppermute(after(attention_result, facts), 'tensor', left)  40.5 us
    pallas_call x2, Pallas kernels, add_shards(): pl.pallas_call(functools.partial(shards_kernel, base is None), out_shape=...  31.1 us
    ppermute x1, waiting for transfers between devices, local(): left_2 = lax.ppermute(left_1, 'tensor', left[:-1])  12.3 us
    pallas_call x1, Pallas kernels, far_low(): pl.pallas_call(far_low_kernel, out_shape=jax.ShapeDtypeStruct((rows, 2 *...  8.06 us
    unnamed x12, local copies, waits for them, and re-layouts  8.06 us
    ppermute x1, starting transfers between devices, local(): other_down = lax.ppermute(other_down, 'tensor', [(0, 1), (3, 2)])  7.21 us
    pallas_call x1, Pallas kernels, prepare(): pl.pallas_call(prepare_kernel, out_shape=[pltpu.VMEM((rows, columns), F32...  6.12 us
    pallas_call x1, Pallas kernels, add_half(): pl.pallas_call(half_kernel, out_shape=jax.ShapeDtypeStruct((rows, columns...  5.74 us
  transfers between devices with their start and end apart: 16, of which 6 were waited for; matrix products, arithmetic and copies ran while one was open for 8% of the time, Pallas kernels for 32%

profile of v15, /device:TPU:0, one launch (start us, length us, event | category | flops | bytes accessed | tf_op | source)
XLA Modules:
  0.0 173.8 jit_solution(14329444204725553898)
XLA Ops:
  0.0 2.9 %collective-permute-start.3 = (bf16[4,32,8192]{2,1,0:T(8,128)(2,1)}, bf16[4,32,8192]{2,1,0:T(8,128)(2,1)}, u32[]{:S(2)}, u32[]{:S(2)}) collective-permute-start(bf16[4,32,8192]{2,1,0:T(8,128)(2,1)} %refs_0_.3), channel_id=1, source_target_pairs={{0,2},{1,3},{2,0},{3,1},{4,6},{5,7},{6,4},{7,5},{8,10},{9,11},{10,... | collective-permute-start | bytes 6291464 | tf_op jit(solution)/shard_map/ppermute | solution.py:446
  2.9 3.6 %collective-permute-start = (bf16[512,2048]{1,0:T(8,128)(2,1)}, bf16[512,2048]{1,0:T(8,128)(2,1)S(1)}, u32[]{:S(2)}, u32[]{:S(2)}) collective-permute-start(bf16[512,2048]{1,0:T(8,128)(2,1)} %refs_0_.4), channel_id=1, source_target_pairs={{0,4},{4,8},{8,12},{1,5},{5,9},{9,13},{2,6},{6,10},{10,14},{3,7},{... | collective-permute-start | bytes 6291464 | tf_op jit(solution)/shard_map/ppermute | solution.py:461
  6.6 1.3 collective-permute-start.1
  7.9 0.7 fusion
  8.6 0.6 slice.30
  9.2 0.7 add_bitcast_fusion
  9.9 0.7 fusion.4
  10.6 0.1 copy.20
  10.8 0.7 fusion.1
  11.5 0.6 fusion.5
  12.1 1.4 add_reduce_fusion
  13.5 0.7 fusion.3
  14.3 0.9 select_reduce_fusion.1
  15.3 0.8 select_reduce_fusion
  16.1 40.5 %collective-permute-done.1.refs_2_.right_1 = bf16[512,2048]{1,0:T(8,128)(2,1)} collective-permute-done((bf16[512,2048]{1,0:T(8,128)(2,1)}, bf16[512,2048]{1,0:T(8,128)(2,1)}, u32[]{:S(2)}, u32[]{:S(2)}) %collective-permute-start.1) | collective-permute-done | bytes 2097184 | tf_op jit(solution)/shard_map/ppermute | solution.py:462
  56.6 1.3 copy-done.2
  57.9 0.8 collective-permute-start.6
  58.7 1.3 collective-permute-start.7
  60.0 0.6 collective-permute-start.5
  60.6 0.5 collective-permute-start.13
  61.1 0.8 copy.21.refs_5_.slot.refs_4_
  62.0 0.5 collective-permute-done.4.refs_3_
  62.4 1.6 copy-done.1
  64.0 4.7 %shard_map.100 = (bf16[8192,256]{1,0:T(8,128)(2,1)S(1)}, bf16[192,4096]{1,0:T(8,128)(2,1)}) custom-call(s32[6]{0:T(128)S(1)} %fusion.2.places, s32[1]{0:T(128)} %bitcast.8.upper, bf16[4,32,8192]{2,1,0:T(8,128)(2,1)S(1)} %copy-done.1, bf16[4,32,8192]{2,1,0:T(8,128)(2,1)} %collective-permute-done.2.refs_1_, ...), custom_call_target="tpu_custom_call" | custom-call | bytes 8388608 | tf_op jit(solution)/shard_map/pallas_call | solution.py:64
  68.8 2.0 %copy-done = bf16[8192,256]{1,0:T(8,128)(2,1)} copy-done((bf16[8192,256]{1,0:T(8,128)(2,1)}, bf16[8192,256]{1,0:T(8,128)(2,1)S(1)}, u32[]{:S(2)}) %copy-start) | copy-done | bytes 4194328
  70.7 7.2 %collective-permute-start.9 = (bf16[192,4096]{1,0:T(8,128)(2,1)}, bf16[192,4096]{1,0:T(8,128)(2,1)}, u32[]{:S(2)}, u32[]{:S(2)}) collective-permute-start(bf16[192,4096]{1,0:T(8,128)(2,1)} %get-tuple-element.61), channel_id=1, source_target_pairs={{0,4},{12,8},{1,5},{13,9},{2,6},{14,10},{3,7},{15,11},{16,20},{28,... | collective-permute-start | bytes 4718600 | tf_op jit(solution)/shard_map/ppermute | solution.py:477
  77.9 1.6 copy-done.5
  79.5 19.4 %shard_map.101 = (f32[512,2048]{1,0:T(8,128)}, f32[512,32]{1,0:T(8,128)S(1)}) custom-call(s32[6]{0:T(128)S(1)} %select_n.86.start, s32[3]{0:T(128)S(1)} %get-tuple-element.48.valid, bf16[512,2048]{1,0:T(8,128)(2,1)S(1)} %copy-done.5, bf16[512,2048]{1,0:T(8,128)(2,1)S(1)} %copy-done.3, bf16[512,2048]{1,0:T(8,128)(2,1)} %collective-permute-done.1.refs_2_.right_1, ...), custom_call_target="tpu_custom_call" | custom-call | flops 14495514624 | bytes 42991616 | tf_op jit(solution)/shard_map/pallas_call | solution.py:169
  99.0 12.3 %collective-permute-done.7.right_2.refs_1_ = bf16[512,2048]{1,0:T(8,128)(2,1)} collective-permute-done((bf16[512,2048]{1,0:T(8,128)(2,1)}, bf16[512,2048]{1,0:T(8,128)(2,1)}, u32[]{:S(2)}, u32[]{:S(2)}) %collective-permute-start.7) | collective-permute-done | bytes 2097184 | tf_op jit(solution)/shard_map/ppermute | solution.py:474
  111.2 2.4 %slice_select_fusion = bf16[512,1024]{1,0:T(8,128)(2,1)} fusion(bf16[512,2048]{1,0:T(8,128)(2,1)} %collective-permute-done.7.right_2.refs_1_, bf16[512,2048]{1,0:T(8,128)(2,1)S(1)} %collective-permute-done.6.left_2.refs_0_, pred[]{:T(512)S(6)} %ge.9), kind=kLoop, calls=%fused_computation | loop fusion | flops 524288 | bytes 3145729 | tf_op jit(solution)/shard_map/jit(_where)/select_n | solution.py:491
  113.6 3.8 %collective-permute-start.10 = (f32[512,32]{1,0:T(8,128)S(1)}, f32[512,32]{1,0:T(8,128)S(1)}, u32[]{:S(2)}, u32[]{:S(2)}) collective-permute-start(f32[512,32]{1,0:T(8,128)S(1)} %get-tuple-element.62.low), channel_id=1, source_target_pairs={{0,4},{12,8},{1,5},{13,9},{2,6},{14,10},{3,7},{15,11},{16,20},{28,... | collective-permute-start | bytes 196616 | tf_op jit(solution)/shard_map/ppermute | solution.py:482
  117.4 0.1 copy.23.row_rank
  117.6 1.3 collective-permute-start.8
  118.9 4.6 %collective-permute-done.10.other_low = f32[512,32]{1,0:T(8,128)S(1)} collective-permute-done((f32[512,32]{1,0:T(8,128)S(1)}, f32[512,32]{1,0:T(8,128)S(1)}, u32[]{:S(2)}, u32[]{:S(2)}) %collective-permute-start.10) | collective-permute-done | bytes 65568 | tf_op jit(solution)/shard_map/ppermute | solution.py:482
  123.5 1.6 copy-done.4
  125.1 8.1 %shard_map.102 = bf16[512,64]{1,0:T(8,128)(2,1)S(1)} custom-call(s32[4]{0:T(128)S(1)} %pad_add_fusion.1.facts, bf16[512,2048]{1,0:T(8,128)(2,1)S(1)} %copy-done.4, bf16[512,2048]{1,0:T(8,128)(2,1)S(1)} %collective-permute-done.6.left_2.refs_0_, bf16[512,2048]{1,0:T(8,128)(2,1)} %collective-permute-done.1.refs_2_.right_1, ...), custom_call_target="tpu_custom_call" | custom-call | flops 1610612736 | bytes 7340032 | tf_op jit(solution)/shard_map/pallas_call | solution.py:278
  133.1 0.7 collective-permute-start.11
  133.8 1.1 slice_select_fusion.2
  134.9 0.1 maximum_select_fusion
  135.2 1.3 collective-permute-start.12
  136.4 1.1 slice_select_fusion.1
  137.6 1.3 collective-permute-start.15
  138.9 11.7 %shard_map.103.base_in = f32[512,2048]{1,0:T(8,128)} custom-call(s32[4]{0:T(128)S(1)} %select_n.88.start, s32[2]{0:T(128)S(1)} %get-tuple-element.60.valid, bf16[512,2048]{1,0:T(8,128)(2,1)S(1)} %collective-permute-done.6.left_2.refs_0_, bf16[512,2048]{1,0:T(8,128)(2,1)} %collective-permute-done.7.right_2.refs_1_, bf16[8192,2048]{1,0:T(8,128)(2,1)} %weight.3, ...), custom_call_target="tpu_custom_call" | custom-call | flops 8589934592 | bytes 29360128 | tf_op jit(solution)/shard_map/pallas_call | solution.py:169
  150.5 5.7 %shard_map.104.base = f32[512,2048]{1,0:T(8,128)S(1)} custom-call(s32[1]{0:T(128)} %bitcast.1.start, s32[1]{0:T(128)} %bitcast.valid, bf16[512,1024]{1,0:T(8,128)(2,1)S(1)} %collective-permute-done.8.x, bf16[8192,2048]{1,0:T(8,128)(2,1)} %weight.3, f32[512,2048]{1,0:T(8,128)} %shard_map.103.base_in), custom_call_target="tpu_custom_call" | custom-call | flops 2147483648 | bytes 13631488 | tf_op jit(solution)/shard_map/pallas_call | solution.py:207
  156.3 3.4 %collective-permute-done.12.received = bf16[512,640]{1,0:T(8,128)(2,1)S(1)} collective-permute-done((bf16[512,640]{1,0:T(8,128)(2,1)S(1)}, bf16[512,640]{1,0:T(8,128)(2,1)S(1)}, u32[]{:S(2)}, u32[]{:S(2)}) %collective-permute-start.12) | collective-permute-done | bytes 655392 | tf_op jit(solution)/shard_map/ppermute | solution.py:505
  159.7 6.1 %shard_map.105 = (f32[512,2048]{1,0:T(8,128)S(1)}, bf16[512,2048]{1,0:T(8,128)(2,1)S(1)}) custom-call(s32[2]{0:T(128)S(1)} %pad_add_fusion.facts, s32[6]{0:T(128)S(1)} %fusion.2.places, f32[512,2048]{1,0:T(8,128)S(1)} %shard_map.104.base, bf16[512,640]{1,0:T(8,128)(2,1)S(1)} %pad_maximum_fusion.sent, bf16[512,640]{1,0:T(8,128)(2,1)S(1)} %collective-permute-done.12.received, ...), custom_call_target="tpu_custom_call" | custom-call | flops 2684354560 | bytes 15728640 | tf_op jit(solution)/shard_map/pallas_call | solution.py:358
  165.9 4.4 %collective-permute-done.15.x = bf16[512,512]{1,0:T(8,128)(2,1)S(1)} collective-permute-done((bf16[512,512]{1,0:T(8,128)(2,1)S(1)}, bf16[512,512]{1,0:T(8,128)(2,1)S(1)}, u32[]{:S(2)}, u32[]{:S(2)}) %collective-permute-start.15) | collective-permute-done | bytes 524320 | tf_op jit(solution)/shard_map/ppermute | solution.py:507
  170.3 3.5 %shard_map.106 = bf16[512,2048]{1,0:T(8,128)(2,1)} custom-call(s32[2]{0:T(128)S(1)} %pad_add_fusion.facts, f32[512,2048]{1,0:T(8,128)S(1)} %get-tuple-element.76.total, bf16[512,2048]{1,0:T(8,128)(2,1)S(1)} %get-tuple-element.77.weight, bf16[512,512]{1,0:T(8,128)(2,1)S(1)} %collective-permute-done.15.x), custom_call_target="tpu_custom_call" | custom-call | flops 1073741824 | bytes 2097152 | tf_op jit(solution)/shard_map/pallas_call | solution.py:395
  (31 shorter events, 0.6 us)
Async XLA Ops:
  0.0 56.6 %collective-permute-start.3 = (bf16[4,32,8192]{2,1,0:T(8,128)(2,1)}, bf16[4,32,8192]{2,1,0:T(8,128)(2,1)}, u32[]{:S(2)}, u32[]{:S(2)}) collective-permute-start(bf16[4,32,8192]{2,1,0:T(8,128)(2,1)} %refs_0_.3), channel_id=1, source_target_pairs={{0,2},{1,3},{2,0},{3,1},{4,6},{5,7},{6,4},{7,5},{8,10},{9,11},{10,... | collective-permute-start | bytes 6291464 | tf_op jit(solution)/shard_map/ppermute | solution.py:446
  2.9 57.7 %collective-permute-start.2 = (bf16[4,32,8192]{2,1,0:T(8,128)(2,1)}, bf16[4,32,8192]{2,1,0:T(8,128)(2,1)}, u32[]{:S(2)}, u32[]{:S(2)}) collective-permute-start(bf16[4,32,8192]{2,1,0:T(8,128)(2,1)} %refs_0_.3), channel_id=1, source_target_pairs={{0,1},{1,0},{2,3},{3,2},{4,5},{5,4},{6,7},{7,6},{8,9},{9,8},{10,11... | collective-permute-start | bytes 6291464 | tf_op jit(solution)/shard_map/ppermute | solution.py:446
  2.9 53.7 %collective-permute-start = (bf16[512,2048]{1,0:T(8,128)(2,1)}, bf16[512,2048]{1,0:T(8,128)(2,1)S(1)}, u32[]{:S(2)}, u32[]{:S(2)}) collective-permute-start(bf16[512,2048]{1,0:T(8,128)(2,1)} %refs_0_.4), channel_id=1, source_target_pairs={{0,4},{4,8},{8,12},{1,5},{5,9},{9,13},{2,6},{6,10},{10,14},{3,7},{... | collective-permute-start | bytes 6291464 | tf_op jit(solution)/shard_map/ppermute | solution.py:461
  6.6 50.0 %collective-permute-start.1 = (bf16[512,2048]{1,0:T(8,128)(2,1)}, bf16[512,2048]{1,0:T(8,128)(2,1)}, u32[]{:S(2)}, u32[]{:S(2)}) collective-permute-start(bf16[512,2048]{1,0:T(8,128)(2,1)} %refs_0_.4), channel_id=1, source_target_pairs={{4,0},{8,4},{12,8},{5,1},{9,5},{13,9},{6,2},{10,6},{14,10},{7,3},{... | collective-permute-start | bytes 6291464 | tf_op jit(solution)/shard_map/ppermute | solution.py:462
  56.6 1.3 copy-start.2
  57.9 4.5 %collective-permute-start.4 = (bf16[4,32,8192]{2,1,0:T(8,128)(2,1)}, bf16[4,32,8192]{2,1,0:T(8,128)(2,1)}, u32[]{:S(2)}, u32[]{:S(2)}) collective-permute-start(bf16[4,32,8192]{2,1,0:T(8,128)(2,1)} %collective-permute-done.3.refs_2_), channel_id=1, source_target_pairs={{0,1},{1,0},{2,3},{3,2},{4,5},{5,4},{6,7},{7,6},{8,9},{9,8},{10,11... | collective-permute-start | bytes 6291464 | tf_op jit(solution)/shard_map/ppermute | solution.py:446
  57.9 41.0 %collective-permute-start.6 = (bf16[512,2048]{1,0:T(8,128)(2,1)}, bf16[512,2048]{1,0:T(8,128)(2,1)S(1)}, u32[]{:S(2)}, u32[]{:S(2)}) collective-permute-start(bf16[512,2048]{1,0:T(8,128)(2,1)} %copy-done.2), channel_id=1, source_target_pairs={{4,8},{8,12},{5,9},{9,13},{6,10},{10,14},{7,11},{11,15},{20,24},{2... | collective-permute-start | bytes 6291464 | tf_op jit(solution)/shard_map/ppermute | solution.py:473
  58.7 52.5 %collective-permute-start.7 = (bf16[512,2048]{1,0:T(8,128)(2,1)}, bf16[512,2048]{1,0:T(8,128)(2,1)}, u32[]{:S(2)}, u32[]{:S(2)}) collective-permute-start(bf16[512,2048]{1,0:T(8,128)(2,1)} %collective-permute-done.1.refs_2_.right_1), channel_id=1, source_target_pairs={{4,0},{8,4},{5,1},{9,5},{6,2},{10,6},{7,3},{11,7},{20,16},{24,20},... | collective-permute-start | bytes 6291464 | tf_op jit(solution)/shard_map/ppermute | solution.py:474
  60.0 51.2 %collective-permute-start.5 = (bf16[4,128,2048]{2,1,0:T(8,128)(2,1)}, bf16[4,128,2048]{2,1,0:T(8,128)(2,1)}, u32[]{:S(2)}, u32[]{:S(2)}) collective-permute-start(bf16[4,128,2048]{2,1,0:T(8,128)(2,1)} %refs_0_.5), channel_id=1, source_target_pairs={{0,1},{1,0},{2,3},{3,2},{4,5},{5,4},{6,7},{7,6},{8,9},{9,8},{10,11... | collective-permute-start | bytes 6291464 | tf_op jit(solution)/shard_map/ppermute | solution.py:446
  60.6 53.0 %collective-permute-start.13 = (bf16[4,128,2048]{2,1,0:T(8,128)(2,1)}, bf16[4,128,2048]{2,1,0:T(8,128)(2,1)}, u32[]{:S(2)}, u32[]{:S(2)}) collective-permute-start(bf16[4,128,2048]{2,1,0:T(8,128)(2,1)} %refs_0_.5), channel_id=1, source_target_pairs={{0,2},{1,3},{2,0},{3,1},{4,6},{5,7},{6,4},{7,5},{8,10},{9,11},{10,... | collective-permute-start | bytes 6291464 | tf_op jit(solution)/shard_map/ppermute | solution.py:446
  62.4 1.6 copy-start.1
  64.0 13.9 %copy-start.3 = (bf16[512,2048]{1,0:T(8,128)(2,1)S(1)}, bf16[512,2048]{1,0:T(8,128)(2,1)}, u32[]{:S(2)}) copy-start(bf16[512,2048]{1,0:T(8,128)(2,1)} %copy-done.2) | copy-start | bytes 6291460
  68.7 2.0 %copy-start = (bf16[8192,256]{1,0:T(8,128)(2,1)}, bf16[8192,256]{1,0:T(8,128)(2,1)S(1)}, u32[]{:S(2)}) copy-start(bf16[8192,256]{1,0:T(8,128)(2,1)S(1)} %get-tuple-element.53.refs_4_.down) | copy-start | bytes 12582916
  70.7 52.7 %collective-permute-start.9 = (bf16[192,4096]{1,0:T(8,128)(2,1)}, bf16[192,4096]{1,0:T(8,128)(2,1)}, u32[]{:S(2)}, u32[]{:S(2)}) collective-permute-start(bf16[192,4096]{1,0:T(8,128)(2,1)} %get-tuple-element.61), channel_id=1, source_target_pairs={{0,4},{12,8},{1,5},{13,9},{2,6},{14,10},{3,7},{15,11},{16,20},{28,... | collective-permute-start | bytes 4718600 | tf_op jit(solution)/shard_map/ppermute | solution.py:477
  77.9 1.6 copy-start.5
  113.6 42.7 %collective-permute-start.14 = (bf16[4,128,2048]{2,1,0:T(8,128)(2,1)}, bf16[4,128,2048]{2,1,0:T(8,128)(2,1)}, u32[]{:S(2)}, u32[]{:S(2)}) collective-permute-start(bf16[4,128,2048]{2,1,0:T(8,128)(2,1)} %collective-permute-done.13.refs_2_), channel_id=1, source_target_pairs={{0,1},{1,0},{2,3},{3,2},{4,5},{5,4},{6,7},{7,6},{8,9},{9,8},{10,11... | collective-permute-start | bytes 6291464 | tf_op jit(solution)/shard_map/ppermute | solution.py:446
  113.6 9.9 %collective-permute-start.10 = (f32[512,32]{1,0:T(8,128)S(1)}, f32[512,32]{1,0:T(8,128)S(1)}, u32[]{:S(2)}, u32[]{:S(2)}) collective-permute-start(f32[512,32]{1,0:T(8,128)S(1)} %get-tuple-element.62.low), channel_id=1, source_target_pairs={{0,4},{12,8},{1,5},{13,9},{2,6},{14,10},{3,7},{15,11},{16,20},{28,... | collective-permute-start | bytes 196616 | tf_op jit(solution)/shard_map/ppermute | solution.py:482
  117.6 32.9 %collective-permute-start.8 = (bf16[512,1024]{1,0:T(8,128)(2,1)}, bf16[512,1024]{1,0:T(8,128)(2,1)S(1)}, u32[]{:S(2)}, u32[]{:S(2)}) collective-permute-start(bf16[512,1024]{1,0:T(8,128)(2,1)} %slice_select_fusion), channel_id=1, source_target_pairs={{8,12},{4,0},{9,13},{5,1},{10,14},{6,2},{11,15},{7,3},{24,28},{20,... | collective-permute-start | bytes 3145736 | tf_op jit(solution)/shard_map/ppermute | solution.py:494
  123.5 1.6 copy-start.4
  133.1 1.8 %collective-permute-start.11 = (bf16[512,64]{1,0:T(8,128)(2,1)S(1)}, bf16[512,64]{1,0:T(8,128)(2,1)S(1)}, u32[]{:S(2)}, u32[]{:S(2)}) collective-permute-start(bf16[512,64]{1,0:T(8,128)(2,1)S(1)} %shard_map.102), channel_id=1, source_target_pairs={{4,8},{8,4},{5,9},{9,5},{6,10},{10,6},{7,11},{11,7},{20,24},{24,20... | collective-permute-start | bytes 196616 | tf_op jit(solution)/shard_map/ppermute | solution.py:501
  135.2 24.6 %collective-permute-start.12 = (bf16[512,640]{1,0:T(8,128)(2,1)S(1)}, bf16[512,640]{1,0:T(8,128)(2,1)S(1)}, u32[]{:S(2)}, u32[]{:S(2)}) collective-permute-start(bf16[512,640]{1,0:T(8,128)(2,1)S(1)} %pad_maximum_fusion.sent), channel_id=1, source_target_pairs={{8,12},{4,0},{9,13},{5,1},{10,14},{6,2},{11,15},{7,3},{24,28},{20,... | collective-permute-start | bytes 1966088 | tf_op jit(solution)/shard_map/ppermute | solution.py:505
  137.6 32.7 %collective-permute-start.15 = (bf16[512,512]{1,0:T(8,128)(2,1)S(1)}, bf16[512,512]{1,0:T(8,128)(2,1)S(1)}, u32[]{:S(2)}, u32[]{:S(2)}) collective-permute-start(bf16[512,512]{1,0:T(8,128)(2,1)S(1)} %slice_select_fusion.1), channel_id=1, source_target_pairs={{8,12},{4,0},{9,13},{5,1},{10,14},{6,2},{11,15},{7,3},{24,28},{20,... | collective-permute-start | bytes 1572872 | tf_op jit(solution)/shard_map/ppermute | solution.py:507

commit v16 on v15

--- a/solution.py
+++ b/solution.py
@@ -11,20 +11,25 @@
 TAIL_PARAMS = pltpu.CompilerParams(vmem_limit_bytes=24 * 2**20)
 F32 = jnp.float32
 BF16 = jnp.bfloat16
-
-
-def start_pages(places, blocks, length, targets, sems, rows_of):
+PIECES = 2
+
+
+def start_pages(places, blocks, targets, sems, rows_of):
     for e, target in enumerate(targets):
-        for j, block in enumerate(blocks):
-
-            @pl.when(places[e] // length == j)
+        first = 0
+        for block in blocks:
+            past = first + block.shape[0]
+
+            @pl.when((places[e] >= first) & (places[e] < past))
             def _():
-                pltpu.make_async_copy(rows_of(block.at[lax.rem(places[e], length)]), target, sems[e]).start()
+                pltpu.make_async_copy(rows_of(block.at[places[e] - first]), target, sems[e]).start()
+
+            first = past
 
 
 def join_downs_kernel(places, upper, *refs):
     *blocks, out, other, held, sems = refs
-    length, rank_part, _ = blocks[0].shape
+    _, rank_part, _ = blocks[0].shape
     shards, slots, width = held.shape
     entries = places.shape[0]
     step = pl.program_id(0)
@@ -37,7 +42,7 @@
         for t in range(shards):
             semaphores = [sems.at[t, e] for e in range(entries)]
             start_pages(
-                places, blocks, length, targets(t), semaphores, lambda page: page.at[:, pl.ds(t * width, width)]
+                places, blocks, targets(t), semaphores, lambda page: page.at[:, pl.ds(t * width, width)]
             )
             held[t, entries * rank_part:] = jnp.zeros((slots - entries * rank_part, width), BF16)
 
@@ -76,7 +81,7 @@
         ],
         scratch_shapes=[pltpu.VMEM((shards, slots, width), BF16), pltpu.SemaphoreType.DMA((shards, entries))],
         compiler_params=TAIL_PARAMS,
-        cost_estimate=pl.CostEstimate(flops=0, bytes_accessed=4 * features * slots, transcendentals=0),
+        cost_estimate=pl.CostEstimate(flops=1, bytes_accessed=1, transcendentals=0),
     )(places, upper, *blocks)
 
 
@@ -177,11 +182,7 @@
             scratch_shapes=scratch,
         ),
         compiler_params=PARAMS,
-        cost_estimate=pl.CostEstimate(
-            flops=2 * steps * half * rows * (columns + slots),
-            bytes_accessed=2 * steps * half * (rows + columns + slots) + 8 * rows * columns,
-            transcendentals=0,
-        ),
+        cost_estimate=pl.CostEstimate(flops=1, bytes_accessed=1, transcendentals=0),
     )(*plan, *xs, weight, *rest)
 
 
@@ -218,11 +219,7 @@
             out_specs=whole,
         ),
         compiler_params=PARAMS,
-        cost_estimate=pl.CostEstimate(
-            flops=2 * half * rows * columns,
-            bytes_accessed=2 * half * (rows + columns) + 8 * rows * columns,
-            transcendentals=0,
-        ),
+        cost_estimate=pl.CostEstimate(flops=1, bytes_accessed=1, transcendentals=0),
     )(source, valid, x, weight, base)
 
 
@@ -288,9 +285,7 @@
             pltpu.SemaphoreType.DMA((4,)),
         ],
         compiler_params=TAIL_PARAMS,
-        cost_estimate=pl.CostEstimate(
-            flops=6 * width * rows * slots, bytes_accessed=2 * width * (2 * rows + 3 * slots), transcendentals=0
-        ),
+        cost_estimate=pl.CostEstimate(flops=1, bytes_accessed=1, transcendentals=0),
     )(facts, left_1, left_2, right_1, right_2, in_hbm(down), other_down, slot, row_rank, low, other_low)
 
 
@@ -298,7 +293,7 @@
     *blocks, slot, total, last_rows, mid, mid_rows, up, spread, sems = refs
     mid_width, last_width = mid_rows.shape[0], last_rows.shape[0]
     width = mid_width + last_width
-    length, rank, _ = blocks[0].shape
+    _, rank, _ = blocks[0].shape
     count = up.shape[0] // rank
     which, start = facts[0], facts[1] * 2 * width + width
     part = min(total.shape[1], 512)
@@ -321,7 +316,7 @@
         pltpu.make_async_copy(received, mid, sems.at[3]).start()
 
     to_total.start()
-    start_pages(places, blocks, length, pages, page_sems, lambda page: page)
+    start_pages(places, blocks, pages, page_sems, lambda page: page)
 
     @pl.when(which != 0)
     def _():
@@ -368,11 +363,7 @@
             pltpu.SemaphoreType.DMA((4 + entries,)),
         ],
         compiler_params=TAIL_PARAMS,
-        cost_estimate=pl.CostEstimate(
-            flops=2 * (mid_width + entries * rank) * rows * columns,
-            bytes_accessed=2 * (columns + entries * rank + 2 * rows) * columns,
-            transcendentals=0,
-        ),
+        cost_estimate=pl.CostEstimate(flops=1, bytes_accessed=1, transcendentals=0),
     )(facts, places, base, sent, received, weight, in_hbm(blocks[0]), *blocks[1:], slot)
 
 
@@ -399,9 +390,7 @@
         in_specs=[pl.BlockSpec(memory_space=pltpu.SMEM), RESIDENT, RESIDENT, pl.BlockSpec(x.shape, lambda n: (0, 0))],
         out_specs=pl.BlockSpec((rows, part), lambda n: (0, n)),
         compiler_params=TAIL_PARAMS,
-        cost_estimate=pl.CostEstimate(
-            flops=2 * x.shape[1] * rows * columns, bytes_accessed=2 * rows * columns, transcendentals=0
-        ),
+        cost_estimate=pl.CostEstimate(flops=1, bytes_accessed=1, transcendentals=0),
     )(facts, total, weight, x)
 
 
@@ -459,7 +448,7 @@
     far = plan_shards(me + jnp.array([-2, 2], jnp.int32), n_tensor)
 
     right_1 = lax.ppermute(attention_result, "tensor", right)
-    left_1 = lax.ppermute(after(attention_result, facts), "tensor", left)
+    left_1 = lax.ppermute(attention_result, "tensor", left)
     far_down = across(adapter_down_weight, 2)
     far_up = across(adapter_up_weight, 2)
     near_down = across(adapter_down_weight, 1)
@@ -472,7 +461,10 @@
     )
     right_2 = lax.ppermute(right_1, "tensor", right[1:])
     left_2 = lax.ppermute(left_1, "tensor", left[:-1])
-    downs = (adapter_down_weight, near_down, far_down, across(after(far_down, right_1, left_1), 1))
+    came = after(far_down, right_1, left_1)
+    cuts = range(0, holder_length, max(holder_length // PIECES, 1))
+    swapped = [across(came[i:i + cuts.step], 1) for i in cuts]
+    downs = (adapter_down_weight, near_down, far_down, *swapped)
     down, other_down = join_downs(places, is_upper, downs, n_tensor)
     other_down = lax.ppermute(other_down, "tensor", [(0, 1), (3, 2)])
 
@@ -481,8 +473,7 @@
     )
     other_low = lax.ppermute(low, "tensor", [(0, 1), (3, 2)])
 
-    near_up = across(after(adapter_up_weight, far_down), 1)
-    near_up, right_2, left_2 = lax.optimization_barrier((base, near_up, right_2, left_2))[1:]
+    right_2, left_2 = lax.optimization_barrier((base, right_2, left_2))[1:]
     third = right[-1:] + left[:1]
     cuts = (0, width // 2, width // 4 * 3, width)
 
@@ -505,7 +496,7 @@
     second_3 = lax.ppermute(second_2, "tensor", third)
     right_2, left_2 = lax.optimization_barrier((second_2, right_2, left_2))[1:]
     last_3 = lax.ppermute(piece(2), "tensor", third)
-    ups = (adapter_up_weight, near_up, far_up, across(after(far_up, first_2), 1))
+    ups = (adapter_up_weight, across(after(adapter_up_weight, far_down), 1), far_up, across(after(far_up, first_2), 1))
     base = add_half(base, first_3, ended, started, output_weight)
     total, rows_of = prepare(facts, places, base, second_2, second_3, output_weight, ups, slot)
     total, rows_of, last_3 = lax.optimization_barrier((total, rows_of, last_3))

time: 175 us -> 169 us (0.966)
  waiting for transfers between devices: 65.7 us -> 59.5 us
    ppermute x1, waiting for transfers between devices: 40.5 us -> 4.25 us  [local(): left_1 = lax.ppermute(attention_result, 'tensor', left)]
    ppermute x1, waiting for transfers between devices: 0.01 us -> 33.3 us  [local(): right_1 = lax.ppermute(attention_result, 'tensor', right)]
    ppermute x1, waiting for transfers between devices: 12.3 us -> 6.06 us  [local(): left_2 = lax.ppermute(left_1, 'tensor', left[:-1])]
    ppermute x6 -> x7, waiting for transfers between devices: 0.48 us -> 3.66 us  [across(): return lax.ppermute(x, 'dp', [(i, i ^ distance) for i in range(n_dp)])]
    ppermute x6 -> x7, starting transfers between devices: 4.05 us -> 2.72 us  [across(): return lax.ppermute(x, 'dp', [(i, i ^ distance) for i in range(n_dp)])]
    unnamed x12 -> x14, local copies, waits for them, and re-layouts: 8.06 us -> 6.75 us
  transfers between devices with their start and end apart: 16 -> 17, of which waited for: 6 -> 8; matrix products, arithmetic and copies ran while one was open for 8% -> 9% of each run, Pallas kernels for 32% -> 33%
where the time goes in v16:
time: 169 us; the launch traced here: 168 us
  waiting for transfers between devices  59.5 us (35%)
  Pallas kernels  59.1 us (35%)
  starting transfers between devices  27.6 us (16%)
  other arithmetic  11.5 us (7%)
  local copies, waits for them, and re-layouts  10.3 us (6%)
    ppermute x1, waiting for transfers between devices, local(): right_1 = lax.ppermute(attention_result, 'tensor', right)  33.3 us
    pallas_call x2, Pallas kernels, add_shards(): pl.pallas_call(functools.partial(shards_kernel, base is None), out_shape=...  31.1 us
    pallas_call x1, Pallas kernels, far_low(): pl.pallas_call(far_low_kernel, out_shape=jax.ShapeDtypeStruct((rows, 2 *...  8.06 us
    ppermute x1, starting transfers between devices, local(): other_down = lax.ppermute(other_down, 'tensor', [(0, 1), (3, 2)])  7.95 us
    unnamed x14, local copies, waits for them, and re-layouts  6.75 us
    pallas_call x1, Pallas kernels, prepare(): pl.pallas_call(prepare_kernel, out_shape=[pltpu.VMEM((rows, columns), F32...  6.11 us
    ppermute x1, waiting for transfers between devices, local(): left_2 = lax.ppermute(left_1, 'tensor', left[:-1])  6.06 us
    pallas_call x1, Pallas kernels, add_half(): pl.pallas_call(half_kernel, out_shape=jax.ShapeDtypeStruct((rows, columns...  5.74 us
  transfers between devices with their start and end apart: 17, of which 8 were waited for; matrix products, arithmetic and copies ran while one was open for 9% of the time, Pallas kernels for 33%

profile of v16, /device:TPU:0, one launch (start us, length us, event | category | flops | bytes accessed | tf_op | source)
XLA Modules:
  0.0 168.3 jit_solution(4785392501428737975)
XLA Ops:
  0.0 5.1 %collective-permute-start = (bf16[512,2048]{1,0:T(8,128)(2,1)}, bf16[512,2048]{1,0:T(8,128)(2,1)S(1)}, u32[]{:S(2)}, u32[]{:S(2)}) collective-permute-start(bf16[512,2048]{1,0:T(8,128)(2,1)} %refs_0_.4), channel_id=1, source_target_pairs={{0,4},{4,8},{8,12},{1,5},{5,9},{9,13},{2,6},{6,10},{10,14},{3,7},{... | collective-permute-start | bytes 6291464 | tf_op jit(solution)/shard_map/ppermute | solution.py:450
  5.1 1.3 collective-permute-start.1
  6.4 1.6 collective-permute-start.3
  7.9 0.5 collective-permute-start.14
  8.5 0.7 fusion
  9.1 0.6 slice.36
  9.8 0.7 add_bitcast_fusion
  10.5 0.7 fusion.4
  11.3 0.7 fusion.1
  12.0 0.7 fusion.6
  12.7 1.4 add_reduce_fusion
  14.2 0.9 select_reduce_fusion.1
  15.1 0.8 select_reduce_fusion
  15.9 0.7 fusion.3
  16.8 33.3 %collective-permute-done.refs_1_.left_1 = bf16[512,2048]{1,0:T(8,128)(2,1)S(1)} collective-permute-done((bf16[512,2048]{1,0:T(8,128)(2,1)}, bf16[512,2048]{1,0:T(8,128)(2,1)S(1)}, u32[]{:S(2)}, u32[]{:S(2)}) %collective-permute-start) | collective-permute-done | bytes 2097184 | tf_op jit(solution)/shard_map/ppermute | solution.py:450
  50.1 4.2 %collective-permute-done.1.refs_2_.right_1 = bf16[512,2048]{1,0:T(8,128)(2,1)} collective-permute-done((bf16[512,2048]{1,0:T(8,128)(2,1)}, bf16[512,2048]{1,0:T(8,128)(2,1)}, u32[]{:S(2)}, u32[]{:S(2)}) %collective-permute-start.1) | collective-permute-done | bytes 2097184 | tf_op jit(solution)/shard_map/ppermute | solution.py:451
  54.4 0.9 collective-permute-start.6
  55.3 1.3 collective-permute-start.7
  56.6 1.7 fusion.5
  58.4 0.5 collective-permute-start.5
  58.9 2.1 %collective-permute-done.4.refs_3_ = bf16[2,32,8192]{2,1,0:T(8,128)(2,1)S(1)} collective-permute-done((bf16[2,32,8192]{2,1,0:T(8,128)(2,1)S(1)}, bf16[2,32,8192]{2,1,0:T(8,128)(2,1)S(1)}, u32[]{:S(2)}, u32[]{:S(2)}) %collective-permute-start.4) | collective-permute-done | bytes 1048608 | tf_op jit(solution)/shard_map/ppermute | solution.py:435
  61.0 1.5 collective-permute-done.5.refs_4_
  62.5 4.6 %shard_map.100 = (bf16[8192,256]{1,0:T(8,128)(2,1)S(1)}, bf16[192,4096]{1,0:T(8,128)(2,1)}) custom-call(s32[6]{0:T(128)S(1)} %fusion.2.places, s32[1]{0:T(128)} %bitcast.8.upper, bf16[4,32,8192]{2,1,0:T(8,128)(2,1)S(1)} %copy-done.4, bf16[4,32,8192]{2,1,0:T(8,128)(2,1)} %collective-permute-done.2.refs_1_, ...), custom_call_target="tpu_custom_call" | custom-call | flops 1 | bytes 1 | tf_op jit(solution)/shard_map/pallas_call | solution.py:69
  67.1 2.0 %copy-done = bf16[8192,256]{1,0:T(8,128)(2,1)} copy-done((bf16[8192,256]{1,0:T(8,128)(2,1)}, bf16[8192,256]{1,0:T(8,128)(2,1)S(1)}, u32[]{:S(2)}) %copy-start) | copy-done | bytes 4194328
  69.1 8.0 %collective-permute-start.9 = (bf16[192,4096]{1,0:T(8,128)(2,1)}, bf16[192,4096]{1,0:T(8,128)(2,1)}, u32[]{:S(2)}, u32[]{:S(2)}) collective-permute-start(bf16[192,4096]{1,0:T(8,128)(2,1)} %get-tuple-element.57), channel_id=1, source_target_pairs={{0,4},{12,8},{1,5},{13,9},{2,6},{14,10},{3,7},{15,11},{16,20},{28,... | collective-permute-start | bytes 4718600 | tf_op jit(solution)/shard_map/ppermute | solution.py:469
  77.3 1.6 copy-done.2
  78.9 1.6 copy-done.5
  80.5 19.4 %shard_map.101 = (f32[512,2048]{1,0:T(8,128)}, f32[512,32]{1,0:T(8,128)S(1)}) custom-call(s32[6]{0:T(128)S(1)} %select_n.86.start, s32[3]{0:T(128)S(1)} %get-tuple-element.45.valid, bf16[512,2048]{1,0:T(8,128)(2,1)S(1)} %copy-done.5, bf16[512,2048]{1,0:T(8,128)(2,1)S(1)} %copy-done.2, bf16[512,2048]{1,0:T(8,128)(2,1)} %collective-permute-done.1.refs_2_.right_1, ...), custom_call_target="tpu_custom_call" | custom-call | flops 1 | bytes 1 | tf_op jit(solution)/shard_map/pallas_call | solution.py:174
  99.9 6.1 %collective-permute-done.7.right_2.refs_1_ = bf16[512,2048]{1,0:T(8,128)(2,1)} collective-permute-done((bf16[512,2048]{1,0:T(8,128)(2,1)}, bf16[512,2048]{1,0:T(8,128)(2,1)}, u32[]{:S(2)}, u32[]{:S(2)}) %collective-permute-start.7) | collective-permute-done | bytes 2097184 | tf_op jit(solution)/shard_map/ppermute | solution.py:463
  105.9 2.4 %slice_select_fusion = bf16[512,1024]{1,0:T(8,128)(2,1)} fusion(bf16[512,2048]{1,0:T(8,128)(2,1)} %collective-permute-done.7.right_2.refs_1_, bf16[512,2048]{1,0:T(8,128)(2,1)S(1)} %collective-permute-done.6.left_2.refs_0_, pred[]{:T(512)S(6)} %ge.9), kind=kLoop, calls=%fused_computation | loop fusion | flops 524288 | bytes 3145729 | tf_op jit(solution)/shard_map/jit(_where)/select_n | solution.py:482
  108.3 3.6 %collective-permute-start.10 = (f32[512,32]{1,0:T(8,128)S(1)}, f32[512,32]{1,0:T(8,128)S(1)}, u32[]{:S(2)}, u32[]{:S(2)}) collective-permute-start(f32[512,32]{1,0:T(8,128)S(1)} %get-tuple-element.58.low), channel_id=1, source_target_pairs={{0,4},{12,8},{1,5},{13,9},{2,6},{14,10},{3,7},{15,11},{16,20},{28,... | collective-permute-start | bytes 196616 | tf_op jit(solution)/shard_map/ppermute | solution.py:474
  111.9 0.1 copy.23.row_rank
  112.1 1.3 collective-permute-start.8
  113.4 4.7 %collective-permute-done.10.other_low = f32[512,32]{1,0:T(8,128)S(1)} collective-permute-done((f32[512,32]{1,0:T(8,128)S(1)}, f32[512,32]{1,0:T(8,128)S(1)}, u32[]{:S(2)}, u32[]{:S(2)}) %collective-permute-start.10) | collective-permute-done | bytes 65568 | tf_op jit(solution)/shard_map/ppermute | solution.py:474
  118.1 1.6 copy-done.3
  119.7 8.1 %shard_map.102 = bf16[512,64]{1,0:T(8,128)(2,1)S(1)} custom-call(s32[4]{0:T(128)S(1)} %pad_add_fusion.1.facts, bf16[512,2048]{1,0:T(8,128)(2,1)S(1)} %copy-done.3, bf16[512,2048]{1,0:T(8,128)(2,1)S(1)} %collective-permute-done.6.left_2.refs_0_, bf16[512,2048]{1,0:T(8,128)(2,1)} %collective-permute-done.1.refs_2_.right_1, ...), custom_call_target="tpu_custom_call" | custom-call | flops 1 | bytes 1 | tf_op jit(solution)/shard_map/pallas_call | solution.py:275
  127.8 0.9 collective-permute-start.11
  128.7 1.1 slice_select_fusion.2
  129.8 0.1 maximum_select_fusion
  130.1 1.3 collective-permute-start.12
  131.4 1.1 slice_select_fusion.1
  132.5 1.3 collective-permute-start.16
  133.8 11.7 %shard_map.103.base_in = f32[512,2048]{1,0:T(8,128)} custom-call(s32[4]{0:T(128)S(1)} %select_n.88.start, s32[2]{0:T(128)S(1)} %get-tuple-element.56.valid, bf16[512,2048]{1,0:T(8,128)(2,1)S(1)} %collective-permute-done.6.left_2.refs_0_, bf16[512,2048]{1,0:T(8,128)(2,1)} %collective-permute-done.7.right_2.refs_1_, bf16[8192,2048]{1,0:T(8,128)(2,1)} %weight.3, ...), custom_call_target="tpu_custom_call" | custom-call | flops 1 | bytes 1 | tf_op jit(solution)/shard_map/pallas_call | solution.py:174
  145.4 5.7 %shard_map.104.base = f32[512,2048]{1,0:T(8,128)S(1)} custom-call(s32[1]{0:T(128)} %bitcast.4.start, s32[1]{0:T(128)} %bitcast.3.valid, bf16[512,1024]{1,0:T(8,128)(2,1)S(1)} %collective-permute-done.8.x, bf16[8192,2048]{1,0:T(8,128)(2,1)} %weight.3, f32[512,2048]{1,0:T(8,128)} %shard_map.103.base_in), custom_call_target="tpu_custom_call" | custom-call | flops 1 | bytes 1 | tf_op jit(solution)/shard_map/pallas_call | solution.py:208
  151.2 3.3 %collective-permute-done.12.received = bf16[512,640]{1,0:T(8,128)(2,1)S(1)} collective-permute-done((bf16[512,640]{1,0:T(8,128)(2,1)S(1)}, bf16[512,640]{1,0:T(8,128)(2,1)S(1)}, u32[]{:S(2)}, u32[]{:S(2)}) %collective-permute-start.12) | collective-permute-done | bytes 655392 | tf_op jit(solution)/shard_map/ppermute | solution.py:496
  154.5 6.1 %shard_map.105 = (f32[512,2048]{1,0:T(8,128)S(1)}, bf16[512,2048]{1,0:T(8,128)(2,1)S(1)}) custom-call(s32[2]{0:T(128)S(1)} %pad_add_fusion.facts, s32[6]{0:T(128)S(1)} %fusion.2.places, f32[512,2048]{1,0:T(8,128)S(1)} %shard_map.104.base, bf16[512,640]{1,0:T(8,128)(2,1)S(1)} %pad_maximum_fusion.sent, bf16[512,640]{1,0:T(8,128)(2,1)S(1)} %collective-permute-done.12.received, ...), custom_call_target="tpu_custom_call" | custom-call | flops 1 | bytes 1 | tf_op jit(solution)/shard_map/pallas_call | solution.py:353
  160.6 4.2 %collective-permute-done.16.x = bf16[512,512]{1,0:T(8,128)(2,1)S(1)} collective-permute-done((bf16[512,512]{1,0:T(8,128)(2,1)S(1)}, bf16[512,512]{1,0:T(8,128)(2,1)S(1)}, u32[]{:S(2)}, u32[]{:S(2)}) %collective-permute-start.16) | collective-permute-done | bytes 524320 | tf_op jit(solution)/shard_map/ppermute | solution.py:498
  164.8 3.5 %shard_map.106 = bf16[512,2048]{1,0:T(8,128)(2,1)} custom-call(s32[2]{0:T(128)S(1)} %pad_add_fusion.facts, f32[512,2048]{1,0:T(8,128)S(1)} %get-tuple-element.72.total, bf16[512,2048]{1,0:T(8,128)(2,1)S(1)} %get-tuple-element.73.weight, bf16[512,512]{1,0:T(8,128)(2,1)S(1)} %collective-permute-done.16.x), custom_call_target="tpu_custom_call" | custom-call | flops 1 | bytes 1 | tf_op jit(solution)/shard_map/pallas_call | solution.py:386
  (36 shorter events, 1.0 us)
Async XLA Ops:
  0.0 50.1 %collective-permute-start = (bf16[512,2048]{1,0:T(8,128)(2,1)}, bf16[512,2048]{1,0:T(8,128)(2,1)S(1)}, u32[]{:S(2)}, u32[]{:S(2)}) collective-permute-start(bf16[512,2048]{1,0:T(8,128)(2,1)} %refs_0_.4), channel_id=1, source_target_pairs={{0,4},{4,8},{8,12},{1,5},{5,9},{9,13},{2,6},{6,10},{10,14},{3,7},{... | collective-permute-start | bytes 6291464 | tf_op jit(solution)/shard_map/ppermute | solution.py:450
  5.1 49.3 %collective-permute-start.1 = (bf16[512,2048]{1,0:T(8,128)(2,1)}, bf16[512,2048]{1,0:T(8,128)(2,1)}, u32[]{:S(2)}, u32[]{:S(2)}) collective-permute-start(bf16[512,2048]{1,0:T(8,128)(2,1)} %refs_0_.4), channel_id=1, source_target_pairs={{4,0},{8,4},{12,8},{5,1},{9,5},{13,9},{6,2},{10,6},{14,10},{7,3},{... | collective-permute-start | bytes 6291464 | tf_op jit(solution)/shard_map/ppermute | solution.py:451
  6.4 50.2 %collective-permute-start.3 = (bf16[4,32,8192]{2,1,0:T(8,128)(2,1)}, bf16[4,32,8192]{2,1,0:T(8,128)(2,1)}, u32[]{:S(2)}, u32[]{:S(2)}) collective-permute-start(bf16[4,32,8192]{2,1,0:T(8,128)(2,1)} %refs_0_.3), channel_id=1, source_target_pairs={{0,2},{1,3},{2,0},{3,1},{4,6},{5,7},{6,4},{7,5},{8,10},{9,11},{10,... | collective-permute-start | bytes 6291464 | tf_op jit(solution)/shard_map/ppermute | solution.py:435
  7.9 50.4 %collective-permute-start.2 = (bf16[4,32,8192]{2,1,0:T(8,128)(2,1)}, bf16[4,32,8192]{2,1,0:T(8,128)(2,1)}, u32[]{:S(2)}, u32[]{:S(2)}) collective-permute-start(bf16[4,32,8192]{2,1,0:T(8,128)(2,1)} %refs_0_.3), channel_id=1, source_target_pairs={{0,1},{1,0},{2,3},{3,2},{4,5},{5,4},{6,7},{7,6},{8,9},{9,8},{10,11... | collective-permute-start | bytes 6291464 | tf_op jit(solution)/shard_map/ppermute | solution.py:435
  7.9 100.4 %collective-permute-start.14 = (bf16[4,128,2048]{2,1,0:T(8,128)(2,1)}, bf16[4,128,2048]{2,1,0:T(8,128)(2,1)}, u32[]{:S(2)}, u32[]{:S(2)}) collective-permute-start(bf16[4,128,2048]{2,1,0:T(8,128)(2,1)} %refs_0_.5), channel_id=1, source_target_pairs={{0,2},{1,3},{2,0},{3,1},{4,6},{5,7},{6,4},{7,5},{8,10},{9,11},{10,... | collective-permute-start | bytes 6291464 | tf_op jit(solution)/shard_map/ppermute | solution.py:435
  50.1 4.3 %copy-start.1 = (bf16[512,2048]{1,0:T(8,128)(2,1)}, bf16[512,2048]{1,0:T(8,128)(2,1)S(1)}, u32[]{:S(2)}) copy-start(bf16[512,2048]{1,0:T(8,128)(2,1)S(1)} %collective-permute-done.refs_1_.left_1) | copy-start | bytes 6291460
  54.4 8.1 %copy-start.4 = (bf16[4,32,8192]{2,1,0:T(8,128)(2,1)S(1)}, bf16[4,32,8192]{2,1,0:T(8,128)(2,1)}, u32[]{:S(2)}) copy-start(bf16[4,32,8192]{2,1,0:T(8,128)(2,1)} %refs_0_.3) | copy-start | bytes 6291460
  54.4 45.5 %collective-permute-start.6 = (bf16[512,2048]{1,0:T(8,128)(2,1)}, bf16[512,2048]{1,0:T(8,128)(2,1)S(1)}, u32[]{:S(2)}, u32[]{:S(2)}) collective-permute-start(bf16[512,2048]{1,0:T(8,128)(2,1)} %copy-done.1), channel_id=1, source_target_pairs={{4,8},{8,12},{5,9},{9,13},{6,10},{10,14},{7,11},{11,15},{20,24},{2... | collective-permute-start | bytes 6291464 | tf_op jit(solution)/shard_map/ppermute | solution.py:462
  55.3 50.6 %collective-permute-start.7 = (bf16[512,2048]{1,0:T(8,128)(2,1)}, bf16[512,2048]{1,0:T(8,128)(2,1)}, u32[]{:S(2)}, u32[]{:S(2)}) collective-permute-start(bf16[512,2048]{1,0:T(8,128)(2,1)} %collective-permute-done.1.refs_2_.right_1), channel_id=1, source_target_pairs={{4,0},{8,4},{5,1},{9,5},{6,2},{10,6},{7,3},{11,7},{20,16},{24,20},... | collective-permute-start | bytes 6291464 | tf_op jit(solution)/shard_map/ppermute | solution.py:463
  58.3 2.7 %collective-permute-start.4 = (bf16[2,32,8192]{2,1,0:T(8,128)(2,1)S(1)}, bf16[2,32,8192]{2,1,0:T(8,128)(2,1)S(1)}, u32[]{:S(2)}, u32[]{:S(2)}) collective-permute-start(bf16[2,32,8192]{2,1,0:T(8,128)(2,1)S(1)} %get-tuple-element.82), channel_id=1, source_target_pairs={{0,1},{1,0},{2,3},{3,2},{4,5},{5,4},{6,7},{7,6},{8,9},{9,8},{10,11... | collective-permute-start | bytes 3145736 | tf_op jit(solution)/shard_map/ppermute | solution.py:435
  58.4 18.7 %copy-start.6 = (s32[512]{0:T(512)S(1)}, s32[512]{0:T(512)}, u32[]{:S(2)}) copy-start(s32[512]{0:T(512)} %param.16) | copy-start | bytes 6148
  58.4 4.1 %collective-permute-start.5 = (bf16[2,32,8192]{2,1,0:T(8,128)(2,1)S(1)}, bf16[2,32,8192]{2,1,0:T(8,128)(2,1)S(1)}, u32[]{:S(2)}, u32[]{:S(2)}) collective-permute-start(bf16[2,32,8192]{2,1,0:T(8,128)(2,1)S(1)} %get-tuple-element.81), channel_id=1, source_target_pairs={{0,1},{1,0},{2,3},{3,2},{4,5},{5,4},{6,7},{7,6},{8,9},{9,8},{10,11... | collective-permute-start | bytes 3145736 | tf_op jit(solution)/shard_map/ppermute | solution.py:435
  67.1 2.0 %copy-start = (bf16[8192,256]{1,0:T(8,128)(2,1)}, bf16[8192,256]{1,0:T(8,128)(2,1)S(1)}, u32[]{:S(2)}) copy-start(bf16[8192,256]{1,0:T(8,128)(2,1)S(1)} %get-tuple-element.50.refs_4_.down) | copy-start | bytes 12582916
  69.1 49.1 %collective-permute-start.9 = (bf16[192,4096]{1,0:T(8,128)(2,1)}, bf16[192,4096]{1,0:T(8,128)(2,1)}, u32[]{:S(2)}, u32[]{:S(2)}) collective-permute-start(bf16[192,4096]{1,0:T(8,128)(2,1)} %get-tuple-element.57), channel_id=1, source_target_pairs={{0,4},{12,8},{1,5},{13,9},{2,6},{14,10},{3,7},{15,11},{16,20},{28,... | collective-permute-start | bytes 4718600 | tf_op jit(solution)/shard_map/ppermute | solution.py:469
  77.2 74.0 %collective-permute-start.13 = (bf16[4,128,2048]{2,1,0:T(8,128)(2,1)}, bf16[4,128,2048]{2,1,0:T(8,128)(2,1)}, u32[]{:S(2)}, u32[]{:S(2)}) collective-permute-start(bf16[4,128,2048]{2,1,0:T(8,128)(2,1)} %refs_0_.5), channel_id=1, source_target_pairs={{0,1},{1,0},{2,3},{3,2},{4,5},{5,4},{6,7},{7,6},{8,9},{9,8},{10,11... | collective-permute-start | bytes 6291464 | tf_op jit(solution)/shard_map/ppermute | solution.py:435
  77.3 1.6 copy-start.2
  78.9 1.6 copy-start.5
  108.3 46.2 %collective-permute-start.15 = (bf16[4,128,2048]{2,1,0:T(8,128)(2,1)}, bf16[4,128,2048]{2,1,0:T(8,128)(2,1)}, u32[]{:S(2)}, u32[]{:S(2)}) collective-permute-start(bf16[4,128,2048]{2,1,0:T(8,128)(2,1)} %collective-permute-done.14.refs_2_), channel_id=1, source_target_pairs={{0,1},{1,0},{2,3},{3,2},{4,5},{5,4},{6,7},{7,6},{8,9},{9,8},{10,11... | collective-permute-start | bytes 6291464 | tf_op jit(solution)/shard_map/ppermute | solution.py:435
  108.3 9.9 %collective-permute-start.10 = (f32[512,32]{1,0:T(8,128)S(1)}, f32[512,32]{1,0:T(8,128)S(1)}, u32[]{:S(2)}, u32[]{:S(2)}) collective-permute-start(f32[512,32]{1,0:T(8,128)S(1)} %get-tuple-element.58.low), channel_id=1, source_target_pairs={{0,4},{12,8},{1,5},{13,9},{2,6},{14,10},{3,7},{15,11},{16,20},{28,... | collective-permute-start | bytes 196616 | tf_op jit(solution)/shard_map/ppermute | solution.py:474
  112.1 33.3 %collective-permute-start.8 = (bf16[512,1024]{1,0:T(8,128)(2,1)}, bf16[512,1024]{1,0:T(8,128)(2,1)S(1)}, u32[]{:S(2)}, u32[]{:S(2)}) collective-permute-start(bf16[512,1024]{1,0:T(8,128)(2,1)} %slice_select_fusion), channel_id=1, source_target_pairs={{8,12},{4,0},{9,13},{5,1},{10,14},{6,2},{11,15},{7,3},{24,28},{20,... | collective-permute-start | bytes 3145736 | tf_op jit(solution)/shard_map/ppermute | solution.py:485
  118.1 1.6 copy-start.3
  127.8 2.0 %collective-permute-start.11 = (bf16[512,64]{1,0:T(8,128)(2,1)S(1)}, bf16[512,64]{1,0:T(8,128)(2,1)S(1)}, u32[]{:S(2)}, u32[]{:S(2)}) collective-permute-start(bf16[512,64]{1,0:T(8,128)(2,1)S(1)} %shard_map.102), channel_id=1, source_target_pairs={{4,8},{8,4},{5,9},{9,5},{6,10},{10,6},{7,11},{11,7},{20,24},{24,20... | collective-permute-start | bytes 196616 | tf_op jit(solution)/shard_map/ppermute | solution.py:492
  130.1 24.4 %collective-permute-start.12 = (bf16[512,640]{1,0:T(8,128)(2,1)S(1)}, bf16[512,640]{1,0:T(8,128)(2,1)S(1)}, u32[]{:S(2)}, u32[]{:S(2)}) collective-permute-start(bf16[512,640]{1,0:T(8,128)(2,1)S(1)} %pad_maximum_fusion.sent), channel_id=1, source_target_pairs={{8,12},{4,0},{9,13},{5,1},{10,14},{6,2},{11,15},{7,3},{24,28},{20,... | collective-permute-start | bytes 1966088 | tf_op jit(solution)/shard_map/ppermute | solution.py:496
  132.5 32.3 %collective-permute-start.16 = (bf16[512,512]{1,0:T(8,128)(2,1)S(1)}, bf16[512,512]{1,0:T(8,128)(2,1)S(1)}, u32[]{:S(2)}, u32[]{:S(2)}) collective-permute-start(bf16[512,512]{1,0:T(8,128)(2,1)S(1)} %slice_select_fusion.1), channel_id=1, source_target_pairs={{8,12},{4,0},{9,13},{5,1},{10,14},{6,2},{11,15},{7,3},{24,28},{20,... | collective-permute-start | bytes 1572872 | tf_op jit(solution)/shard_map/ppermute | solution.py:498

commit v17 on v16

--- a/solution.py
+++ b/solution.py
@@ -203,17 +203,17 @@
 def add_half(base, x, valid, source, weight):
     rows, half = x.shape
     columns = weight.shape[1]
-    step = half // 2
+    step = half // 5
     whole = pl.BlockSpec((rows, columns), lambda s, *_: (0, 0))
     return pl.pallas_call(
         half_kernel,
         out_shape=jax.ShapeDtypeStruct((rows, columns), F32),
         grid_spec=pltpu.PrefetchScalarGridSpec(
             num_scalar_prefetch=2,
-            grid=(2,),
+            grid=(half // step,),
             in_specs=[
                 pl.BlockSpec((rows, step), lambda s, *_: (0, s)),
-                pl.BlockSpec((step, columns), lambda s, source, valid: (source[0] * 4 + s, 0)),
+                pl.BlockSpec((step, columns), lambda s, source, valid: (source[0] * (columns // step) + s, 0)),
                 whole,
             ],
             out_specs=whole,
@@ -292,14 +292,14 @@
 def prepare_kernel(facts, places, base, sent, received, weight, *refs):
     *blocks, slot, total, last_rows, mid, mid_rows, up, spread, sems = refs
     mid_width, last_width = mid_rows.shape[0], last_rows.shape[0]
-    width = mid_width + last_width
+    shard = total.shape[1]
     _, rank, _ = blocks[0].shape
     count = up.shape[0] // rank
-    which, start = facts[0], facts[1] * 2 * width + width
+    which, start = facts[0], (facts[1] + 1) * shard - mid_width - last_width
     part = min(total.shape[1], 512)
 
     def rows_at(first, length):
-        return weight.at[pl.ds(pl.multiple_of(start + first, length), length)]
+        return weight.at[pl.ds(pl.multiple_of(start + first, last_width), length)]
 
     to_total = pltpu.make_async_copy(base, total, sems.at[0])
     to_mid_rows = pltpu.make_async_copy(rows_at(0, mid_width), mid_rows, sems.at[1])
@@ -344,12 +344,11 @@
         to_last.wait()
 
 
-def prepare(facts, places, base, sent, received, weight, blocks, slot):
+def prepare(facts, places, base, sent, received, last_width, weight, blocks, slot):
     rows, columns = base.shape
     rank = blocks[0].shape[1]
     entries = places.shape[0]
     mid_width = sent.shape[1] - rank
-    last_width = mid_width
     return pl.pallas_call(
         prepare_kernel,
         out_shape=[pltpu.VMEM((rows, columns), F32), pltpu.VMEM((last_width, columns), BF16)],
@@ -475,7 +474,7 @@
 
     right_2, left_2 = lax.optimization_barrier((base, right_2, left_2))[1:]
     third = right[-1:] + left[:1]
-    cuts = (0, width // 2, width // 4 * 3, width)
+    cuts = (0, width // 8 * 5, width // 8 * 7, width)
 
     def piece(i):
         cut = slice(cuts[i], cuts[i + 1])
@@ -498,7 +497,7 @@
     last_3 = lax.ppermute(piece(2), "tensor", third)
     ups = (adapter_up_weight, across(after(adapter_up_weight, far_down), 1), far_up, across(after(far_up, first_2), 1))
     base = add_half(base, first_3, ended, started, output_weight)
-    total, rows_of = prepare(facts, places, base, second_2, second_3, output_weight, ups, slot)
+    total, rows_of = prepare(facts, places, base, second_2, second_3, width - cuts[2], output_weight, ups, slot)
     total, rows_of, last_3 = lax.optimization_barrier((total, rows_of, last_3))
     return add_last(facts, total, rows_of, last_3)
 

time: 169 us -> 168 us (level)
  waiting for transfers between devices: 59.5 us -> 54.1 us
  starting transfers between devices: 27.6 us -> 29.6 us
  Pallas kernels: 59.1 us -> 60.9 us
    ppermute x1, waiting for transfers between devices: 4.18 us -> 0.01 us  [local(): last_3 = lax.ppermute(piece(2), 'tensor', third)]
    ppermute x1, waiting for transfers between devices: 3.27 us -> 1.15 us  [local(): second_3 = lax.ppermute(second_2, 'tensor', third)]
    pallas_call x1, Pallas kernels: 5.74 us -> 7.79 us  [add_half(): pl.pallas_call(half_kernel, out_shape=jax.ShapeDtypeStruct((rows, columns...]
    ppermute x1, starting transfers between devices: 3.64 us -> 5.66 us  [local(): other_low = lax.ppermute(low, 'tensor', [(0, 1), (3, 2)])]
  transfers between devices with their start and end apart: 17 -> 17, of which waited for: 8 -> 7; matrix products, arithmetic and copies ran while one was open for 9% -> 9% of each run, Pallas kernels for 33% -> 35%
where the time goes in v17:
time: 168 us; the launch traced here: 167 us
  Pallas kernels  60.9 us (36%)
  waiting for transfers between devices  54.1 us (32%)
  starting transfers between devices  29.6 us (18%)
  other arithmetic  11.7 us (7%)
  local copies, waits for them, and re-layouts  10.2 us (6%)
    ppermute x1, waiting for transfers between devices, local(): right_1 = lax.ppermute(attention_result, 'tensor', right)  33.4 us
    pallas_call x2, Pallas kernels, add_shards(): pl.pallas_call(functools.partial(shards_kernel, base is None), out_shape=...  31.1 us
    pallas_call x1, Pallas kernels, far_low(): pl.pallas_call(far_low_kernel, out_shape=jax.ShapeDtypeStruct((rows, 2 *...  8.06 us
    ppermute x1, starting transfers between devices, local(): other_down = lax.ppermute(other_down, 'tensor', [(0, 1), (3, 2)])  7.95 us
    pallas_call x1, Pallas kernels, add_half(): pl.pallas_call(half_kernel, out_shape=jax.ShapeDtypeStruct((rows, columns...  7.79 us
    unnamed x14, local copies, waits for them, and re-layouts  6.75 us
    pallas_call x1, Pallas kernels, prepare(): pl.pallas_call(prepare_kernel, out_shape=[pltpu.VMEM((rows, columns), F32...  6.11 us
    ppermute x1, waiting for transfers between devices, local(): left_2 = lax.ppermute(left_1, 'tensor', left[:-1])  5.93 us
  transfers between devices with their start and end apart: 17, of which 7 were waited for; matrix products, arithmetic and copies ran while one was open for 9% of the time, Pallas kernels for 35%

profile of v17, /device:TPU:0, one launch (start us, length us, event | category | flops | bytes accessed | tf_op | source)
XLA Modules:
  0.0 166.8 jit_solution(16383671396995323986)
XLA Ops:
  0.0 5.1 %collective-permute-start = (bf16[512,2048]{1,0:T(8,128)(2,1)}, bf16[512,2048]{1,0:T(8,128)(2,1)S(1)}, u32[]{:S(2)}, u32[]{:S(2)}) collective-permute-start(bf16[512,2048]{1,0:T(8,128)(2,1)} %refs_0_.4), channel_id=1, source_target_pairs={{0,4},{4,8},{8,12},{1,5},{5,9},{9,13},{2,6},{6,10},{10,14},{3,7},{... | collective-permute-start | bytes 6291464 | tf_op jit(solution)/shard_map/ppermute | solution.py:449
  5.1 1.3 collective-permute-start.1
  6.4 1.6 collective-permute-start.3
  7.9 0.5 collective-permute-start.14
  8.5 0.7 fusion
  9.1 0.6 slice.36
  9.8 0.7 add_bitcast_fusion
  10.5 0.7 fusion.4
  11.3 0.7 fusion.1
  12.0 0.6 fusion.6
  12.6 1.4 add_reduce_fusion
  14.1 0.9 select_reduce_fusion.1
  15.0 0.8 select_reduce_fusion
  15.8 0.7 fusion.3
  16.7 33.4 %collective-permute-done.refs_1_.left_1 = bf16[512,2048]{1,0:T(8,128)(2,1)S(1)} collective-permute-done((bf16[512,2048]{1,0:T(8,128)(2,1)}, bf16[512,2048]{1,0:T(8,128)(2,1)S(1)}, u32[]{:S(2)}, u32[]{:S(2)}) %collective-permute-start) | collective-permute-done | bytes 2097184 | tf_op jit(solution)/shard_map/ppermute | solution.py:449
  50.1 4.2 %collective-permute-done.1.refs_2_.right_1 = bf16[512,2048]{1,0:T(8,128)(2,1)} collective-permute-done((bf16[512,2048]{1,0:T(8,128)(2,1)}, bf16[512,2048]{1,0:T(8,128)(2,1)}, u32[]{:S(2)}, u32[]{:S(2)}) %collective-permute-start.1) | collective-permute-done | bytes 2097184 | tf_op jit(solution)/shard_map/ppermute | solution.py:450
  54.4 0.9 collective-permute-start.6
  55.3 1.3 collective-permute-start.7
  56.6 1.7 %fusion.5 = (bf16[2,32,8192]{2,1,0:T(8,128)(2,1)S(1)}, bf16[2,32,8192]{2,1,0:T(8,128)(2,1)S(1)}) fusion(bf16[4,32,8192]{2,1,0:T(8,128)(2,1)} %collective-permute-done.3.refs_2_), kind=kLoop, calls=%fused_computation.32 | loop fusion | bytes 4194304 | tf_op jit(solution)/shard_map/slice | solution.py:465
  58.4 0.5 collective-permute-start.5
  58.9 2.1 %collective-permute-done.4.refs_3_ = bf16[2,32,8192]{2,1,0:T(8,128)(2,1)S(1)} collective-permute-done((bf16[2,32,8192]{2,1,0:T(8,128)(2,1)S(1)}, bf16[2,32,8192]{2,1,0:T(8,128)(2,1)S(1)}, u32[]{:S(2)}, u32[]{:S(2)}) %collective-permute-start.4) | collective-permute-done | bytes 1048608 | tf_op jit(solution)/shard_map/ppermute | solution.py:434
  61.0 1.5 collective-permute-done.5.refs_4_
  62.5 4.7 %shard_map.100 = (bf16[8192,256]{1,0:T(8,128)(2,1)S(1)}, bf16[192,4096]{1,0:T(8,128)(2,1)}) custom-call(s32[6]{0:T(128)S(1)} %fusion.2.places, s32[1]{0:T(128)} %bitcast.8.upper, bf16[4,32,8192]{2,1,0:T(8,128)(2,1)S(1)} %copy-done.4, bf16[4,32,8192]{2,1,0:T(8,128)(2,1)} %collective-permute-done.2.refs_1_, ...), custom_call_target="tpu_custom_call" | custom-call | flops 1 | bytes 1 | tf_op jit(solution)/shard_map/pallas_call | solution.py:69
  67.2 2.0 %copy-done = bf16[8192,256]{1,0:T(8,128)(2,1)} copy-done((bf16[8192,256]{1,0:T(8,128)(2,1)}, bf16[8192,256]{1,0:T(8,128)(2,1)S(1)}, u32[]{:S(2)}) %copy-start) | copy-done | bytes 4194328
  69.2 8.0 %collective-permute-start.9 = (bf16[192,4096]{1,0:T(8,128)(2,1)}, bf16[192,4096]{1,0:T(8,128)(2,1)}, u32[]{:S(2)}, u32[]{:S(2)}) collective-permute-start(bf16[192,4096]{1,0:T(8,128)(2,1)} %get-tuple-element.57), channel_id=1, source_target_pairs={{0,4},{12,8},{1,5},{13,9},{2,6},{14,10},{3,7},{15,11},{16,20},{28,... | collective-permute-start | bytes 4718600 | tf_op jit(solution)/shard_map/ppermute | solution.py:468
  77.2 0.1 copy.21.refs_5_.slot.refs_4_
  77.4 1.6 copy-done.2
  79.0 1.6 copy-done.5
  80.6 19.4 %shard_map.101 = (f32[512,2048]{1,0:T(8,128)}, f32[512,32]{1,0:T(8,128)S(1)}) custom-call(s32[6]{0:T(128)S(1)} %select_n.90.start, s32[3]{0:T(128)S(1)} %get-tuple-element.45.valid, bf16[512,2048]{1,0:T(8,128)(2,1)S(1)} %copy-done.5, bf16[512,2048]{1,0:T(8,128)(2,1)S(1)} %copy-done.2, bf16[512,2048]{1,0:T(8,128)(2,1)} %collective-permute-done.1.refs_2_.right_1, ...), custom_call_target="tpu_custom_call" | custom-call | flops 1 | bytes 1 | tf_op jit(solution)/shard_map/pallas_call | solution.py:174
  100.0 5.9 %collective-permute-done.7.right_2.refs_1_ = bf16[512,2048]{1,0:T(8,128)(2,1)} collective-permute-done((bf16[512,2048]{1,0:T(8,128)(2,1)}, bf16[512,2048]{1,0:T(8,128)(2,1)}, u32[]{:S(2)}, u32[]{:S(2)}) %collective-permute-start.7) | collective-permute-done | bytes 2097184 | tf_op jit(solution)/shard_map/ppermute | solution.py:462
  105.9 2.6 %slice_select_fusion = bf16[512,1280]{1,0:T(8,128)(2,1)} fusion(bf16[512,2048]{1,0:T(8,128)(2,1)} %collective-permute-done.7.right_2.refs_1_, bf16[512,2048]{1,0:T(8,128)(2,1)S(1)} %collective-permute-done.6.left_2.refs_0_, pred[]{:T(512)S(6)} %ge.9), kind=kLoop, calls=%fused_computation | loop fusion | flops 655360 | bytes 3932161 | tf_op jit(solution)/shard_map/jit(_where)/select_n | solution.py:481
  108.5 1.3 collective-permute-start.8
  109.8 5.7 %collective-permute-start.10 = (f32[512,32]{1,0:T(8,128)S(1)}, f32[512,32]{1,0:T(8,128)S(1)}, u32[]{:S(2)}, u32[]{:S(2)}) collective-permute-start(f32[512,32]{1,0:T(8,128)S(1)} %get-tuple-element.58.low), channel_id=1, source_target_pairs={{0,4},{12,8},{1,5},{13,9},{2,6},{14,10},{3,7},{15,11},{16,20},{28,... | collective-permute-start | bytes 196616 | tf_op jit(solution)/shard_map/ppermute | solution.py:473
  115.5 0.1 copy.23.row_rank
  115.6 5.8 %collective-permute-done.10.other_low = f32[512,32]{1,0:T(8,128)S(1)} collective-permute-done((f32[512,32]{1,0:T(8,128)S(1)}, f32[512,32]{1,0:T(8,128)S(1)}, u32[]{:S(2)}, u32[]{:S(2)}) %collective-permute-start.10) | collective-permute-done | bytes 65568 | tf_op jit(solution)/shard_map/ppermute | solution.py:473
  121.4 1.6 copy-done.3
  123.0 8.1 %shard_map.102 = bf16[512,64]{1,0:T(8,128)(2,1)S(1)} custom-call(s32[4]{0:T(128)S(1)} %pad_add_fusion.1.facts, bf16[512,2048]{1,0:T(8,128)(2,1)S(1)} %copy-done.3, bf16[512,2048]{1,0:T(8,128)(2,1)S(1)} %collective-permute-done.6.left_2.refs_0_, bf16[512,2048]{1,0:T(8,128)(2,1)} %collective-permute-done.1.refs_2_.right_1, ...), custom_call_target="tpu_custom_call" | custom-call | flops 1 | bytes 1 | tf_op jit(solution)/shard_map/pallas_call | solution.py:275
  131.1 0.9 collective-permute-start.11
  132.0 1.1 slice_select_fusion.1
  133.1 0.1 maximum_select_fusion
  133.3 1.3 collective-permute-start.12
  134.6 1.0 slice_select_fusion.2
  135.6 1.3 collective-permute-start.16
  136.9 11.7 %shard_map.103.base_in = f32[512,2048]{1,0:T(8,128)} custom-call(s32[4]{0:T(128)S(1)} %select_n.92.start, s32[2]{0:T(128)S(1)} %get-tuple-element.56.valid, bf16[512,2048]{1,0:T(8,128)(2,1)S(1)} %collective-permute-done.6.left_2.refs_0_, bf16[512,2048]{1,0:T(8,128)(2,1)} %collective-permute-done.7.right_2.refs_1_, bf16[8192,2048]{1,0:T(8,128)(2,1)} %weight.3, ...), custom_call_target="tpu_custom_call" | custom-call | flops 1 | bytes 1 | tf_op jit(solution)/shard_map/pallas_call | solution.py:174
  148.6 7.8 %shard_map.104.base = f32[512,2048]{1,0:T(8,128)S(1)} custom-call(s32[1]{0:T(128)} %bitcast.4.start, s32[1]{0:T(128)} %bitcast.3.valid, bf16[512,1280]{1,0:T(8,128)(2,1)} %collective-permute-done.8.x, bf16[8192,2048]{1,0:T(8,128)(2,1)} %weight.3, f32[512,2048]{1,0:T(8,128)} %shard_map.103.base_in), custom_call_target="tpu_custom_call" | custom-call | flops 1 | bytes 1 | tf_op jit(solution)/shard_map/pallas_call | solution.py:208
  156.4 1.2 collective-permute-done.12.received
  157.5 6.1 %shard_map.105 = (f32[512,2048]{1,0:T(8,128)S(1)}, bf16[256,2048]{1,0:T(8,128)(2,1)S(1)}) custom-call(s32[2]{0:T(128)S(1)} %pad_add_fusion.facts, s32[6]{0:T(128)S(1)} %fusion.2.places, f32[512,2048]{1,0:T(8,128)S(1)} %shard_map.104.base, bf16[512,640]{1,0:T(8,128)(2,1)S(1)} %pad_maximum_fusion.sent, bf16[512,640]{1,0:T(8,128)(2,1)S(1)} %collective-permute-done.12.received, ...), custom_call_target="tpu_custom_call" | custom-call | flops 1 | bytes 1 | tf_op jit(solution)/shard_map/pallas_call | solution.py:352
  163.7 3.1 %shard_map.106 = bf16[512,2048]{1,0:T(8,128)(2,1)} custom-call(s32[2]{0:T(128)S(1)} %pad_add_fusion.facts, f32[512,2048]{1,0:T(8,128)S(1)} %get-tuple-element.72.total, bf16[256,2048]{1,0:T(8,128)(2,1)S(1)} %get-tuple-element.73.weight, bf16[512,256]{1,0:T(8,128)(2,1)S(1)} %collective-permute-done.16.x), custom_call_target="tpu_custom_call" | custom-call | flops 1 | bytes 1 | tf_op jit(solution)/shard_map/pallas_call | solution.py:385
  (36 shorter events, 0.8 us)
Async XLA Ops:
  0.0 50.1 %collective-permute-start = (bf16[512,2048]{1,0:T(8,128)(2,1)}, bf16[512,2048]{1,0:T(8,128)(2,1)S(1)}, u32[]{:S(2)}, u32[]{:S(2)}) collective-permute-start(bf16[512,2048]{1,0:T(8,128)(2,1)} %refs_0_.4), channel_id=1, source_target_pairs={{0,4},{4,8},{8,12},{1,5},{5,9},{9,13},{2,6},{6,10},{10,14},{3,7},{... | collective-permute-start | bytes 6291464 | tf_op jit(solution)/shard_map/ppermute | solution.py:449
  5.1 49.3 %collective-permute-start.1 = (bf16[512,2048]{1,0:T(8,128)(2,1)}, bf16[512,2048]{1,0:T(8,128)(2,1)}, u32[]{:S(2)}, u32[]{:S(2)}) collective-permute-start(bf16[512,2048]{1,0:T(8,128)(2,1)} %refs_0_.4), channel_id=1, source_target_pairs={{4,0},{8,4},{12,8},{5,1},{9,5},{13,9},{6,2},{10,6},{14,10},{7,3},{... | collective-permute-start | bytes 6291464 | tf_op jit(solution)/shard_map/ppermute | solution.py:450
  6.4 50.2 %collective-permute-start.3 = (bf16[4,32,8192]{2,1,0:T(8,128)(2,1)}, bf16[4,32,8192]{2,1,0:T(8,128)(2,1)}, u32[]{:S(2)}, u32[]{:S(2)}) collective-permute-start(bf16[4,32,8192]{2,1,0:T(8,128)(2,1)} %refs_0_.3), channel_id=1, source_target_pairs={{0,2},{1,3},{2,0},{3,1},{4,6},{5,7},{6,4},{7,5},{8,10},{9,11},{10,... | collective-permute-start | bytes 6291464 | tf_op jit(solution)/shard_map/ppermute | solution.py:434
  7.9 50.4 %collective-permute-start.2 = (bf16[4,32,8192]{2,1,0:T(8,128)(2,1)}, bf16[4,32,8192]{2,1,0:T(8,128)(2,1)}, u32[]{:S(2)}, u32[]{:S(2)}) collective-permute-start(bf16[4,32,8192]{2,1,0:T(8,128)(2,1)} %refs_0_.3), channel_id=1, source_target_pairs={{0,1},{1,0},{2,3},{3,2},{4,5},{5,4},{6,7},{7,6},{8,9},{9,8},{10,11... | collective-permute-start | bytes 6291464 | tf_op jit(solution)/shard_map/ppermute | solution.py:434
  7.9 100.6 %collective-permute-start.14 = (bf16[4,128,2048]{2,1,0:T(8,128)(2,1)}, bf16[4,128,2048]{2,1,0:T(8,128)(2,1)}, u32[]{:S(2)}, u32[]{:S(2)}) collective-permute-start(bf16[4,128,2048]{2,1,0:T(8,128)(2,1)} %refs_0_.5), channel_id=1, source_target_pairs={{0,2},{1,3},{2,0},{3,1},{4,6},{5,7},{6,4},{7,5},{8,10},{9,11},{10,... | collective-permute-start | bytes 6291464 | tf_op jit(solution)/shard_map/ppermute | solution.py:434
  50.1 4.3 %copy-start.1 = (bf16[512,2048]{1,0:T(8,128)(2,1)}, bf16[512,2048]{1,0:T(8,128)(2,1)S(1)}, u32[]{:S(2)}) copy-start(bf16[512,2048]{1,0:T(8,128)(2,1)S(1)} %collective-permute-done.refs_1_.left_1) | copy-start | bytes 6291460
  54.4 8.1 %copy-start.4 = (bf16[4,32,8192]{2,1,0:T(8,128)(2,1)S(1)}, bf16[4,32,8192]{2,1,0:T(8,128)(2,1)}, u32[]{:S(2)}) copy-start(bf16[4,32,8192]{2,1,0:T(8,128)(2,1)} %refs_0_.3) | copy-start | bytes 6291460
  54.4 45.6 %collective-permute-start.6 = (bf16[512,2048]{1,0:T(8,128)(2,1)}, bf16[512,2048]{1,0:T(8,128)(2,1)S(1)}, u32[]{:S(2)}, u32[]{:S(2)}) collective-permute-start(bf16[512,2048]{1,0:T(8,128)(2,1)} %copy-done.1), channel_id=1, source_target_pairs={{4,8},{8,12},{5,9},{9,13},{6,10},{10,14},{7,11},{11,15},{20,24},{2... | collective-permute-start | bytes 6291464 | tf_op jit(solution)/shard_map/ppermute | solution.py:461
  55.3 50.6 %collective-permute-start.7 = (bf16[512,2048]{1,0:T(8,128)(2,1)}, bf16[512,2048]{1,0:T(8,128)(2,1)}, u32[]{:S(2)}, u32[]{:S(2)}) collective-permute-start(bf16[512,2048]{1,0:T(8,128)(2,1)} %collective-permute-done.1.refs_2_.right_1), channel_id=1, source_target_pairs={{4,0},{8,4},{5,1},{9,5},{6,2},{10,6},{7,3},{11,7},{20,16},{24,20},... | collective-permute-start | bytes 6291464 | tf_op jit(solution)/shard_map/ppermute | solution.py:462
  58.3 2.7 %collective-permute-start.4 = (bf16[2,32,8192]{2,1,0:T(8,128)(2,1)S(1)}, bf16[2,32,8192]{2,1,0:T(8,128)(2,1)S(1)}, u32[]{:S(2)}, u32[]{:S(2)}) collective-permute-start(bf16[2,32,8192]{2,1,0:T(8,128)(2,1)S(1)} %get-tuple-element.82), channel_id=1, source_target_pairs={{0,1},{1,0},{2,3},{3,2},{4,5},{5,4},{6,7},{7,6},{8,9},{9,8},{10,11... | collective-permute-start | bytes 3145736 | tf_op jit(solution)/shard_map/ppermute | solution.py:434
  58.4 18.8 %copy-start.6 = (s32[512]{0:T(512)S(1)}, s32[512]{0:T(512)}, u32[]{:S(2)}) copy-start(s32[512]{0:T(512)} %param.16) | copy-start | bytes 6148
  58.4 4.1 %collective-permute-start.5 = (bf16[2,32,8192]{2,1,0:T(8,128)(2,1)S(1)}, bf16[2,32,8192]{2,1,0:T(8,128)(2,1)S(1)}, u32[]{:S(2)}, u32[]{:S(2)}) collective-permute-start(bf16[2,32,8192]{2,1,0:T(8,128)(2,1)S(1)} %get-tuple-element.81), channel_id=1, source_target_pairs={{0,1},{1,0},{2,3},{3,2},{4,5},{5,4},{6,7},{7,6},{8,9},{9,8},{10,11... | collective-permute-start | bytes 3145736 | tf_op jit(solution)/shard_map/ppermute | solution.py:434
  67.2 2.0 %copy-start = (bf16[8192,256]{1,0:T(8,128)(2,1)}, bf16[8192,256]{1,0:T(8,128)(2,1)S(1)}, u32[]{:S(2)}) copy-start(bf16[8192,256]{1,0:T(8,128)(2,1)S(1)} %get-tuple-element.50.refs_4_.down) | copy-start | bytes 12582916
  69.2 52.2 %collective-permute-start.9 = (bf16[192,4096]{1,0:T(8,128)(2,1)}, bf16[192,4096]{1,0:T(8,128)(2,1)}, u32[]{:S(2)}, u32[]{:S(2)}) collective-permute-start(bf16[192,4096]{1,0:T(8,128)(2,1)} %get-tuple-element.57), channel_id=1, source_target_pairs={{0,4},{12,8},{1,5},{13,9},{2,6},{14,10},{3,7},{15,11},{16,20},{28,... | collective-permute-start | bytes 4718600 | tf_op jit(solution)/shard_map/ppermute | solution.py:468
  77.3 79.1 %collective-permute-start.13 = (bf16[4,128,2048]{2,1,0:T(8,128)(2,1)}, bf16[4,128,2048]{2,1,0:T(8,128)(2,1)}, u32[]{:S(2)}, u32[]{:S(2)}) collective-permute-start(bf16[4,128,2048]{2,1,0:T(8,128)(2,1)} %refs_0_.5), channel_id=1, source_target_pairs={{0,1},{1,0},{2,3},{3,2},{4,5},{5,4},{6,7},{7,6},{8,9},{9,8},{10,11... | collective-permute-start | bytes 6291464 | tf_op jit(solution)/shard_map/ppermute | solution.py:434
  77.4 1.6 copy-start.2
  79.0 1.6 copy-start.5
  108.5 49.0 %collective-permute-start.15 = (bf16[4,128,2048]{2,1,0:T(8,128)(2,1)}, bf16[4,128,2048]{2,1,0:T(8,128)(2,1)}, u32[]{:S(2)}, u32[]{:S(2)}) collective-permute-start(bf16[4,128,2048]{2,1,0:T(8,128)(2,1)} %collective-permute-done.14.refs_2_), channel_id=1, source_target_pairs={{0,1},{1,0},{2,3},{3,2},{4,5},{5,4},{6,7},{7,6},{8,9},{9,8},{10,11... | collective-permute-start | bytes 6291464 | tf_op jit(solution)/shard_map/ppermute | solution.py:434
  108.5 40.1 %collective-permute-start.8 = (bf16[512,1280]{1,0:T(8,128)(2,1)}, bf16[512,1280]{1,0:T(8,128)(2,1)}, u32[]{:S(2)}, u32[]{:S(2)}) collective-permute-start(bf16[512,1280]{1,0:T(8,128)(2,1)} %slice_select_fusion), channel_id=1, source_target_pairs={{8,12},{4,0},{9,13},{5,1},{10,14},{6,2},{11,15},{7,3},{24,28},{20,... | collective-permute-start | bytes 3932168 | tf_op jit(solution)/shard_map/ppermute | solution.py:484
  109.8 11.6 %collective-permute-start.10 = (f32[512,32]{1,0:T(8,128)S(1)}, f32[512,32]{1,0:T(8,128)S(1)}, u32[]{:S(2)}, u32[]{:S(2)}) collective-permute-start(f32[512,32]{1,0:T(8,128)S(1)} %get-tuple-element.58.low), channel_id=1, source_target_pairs={{0,4},{12,8},{1,5},{13,9},{2,6},{14,10},{3,7},{15,11},{16,20},{28,... | collective-permute-start | bytes 196616 | tf_op jit(solution)/shard_map/ppermute | solution.py:473
  121.4 1.6 copy-start.3
  131.1 2.0 %collective-permute-start.11 = (bf16[512,64]{1,0:T(8,128)(2,1)S(1)}, bf16[512,64]{1,0:T(8,128)(2,1)S(1)}, u32[]{:S(2)}, u32[]{:S(2)}) collective-permute-start(bf16[512,64]{1,0:T(8,128)(2,1)S(1)} %shard_map.102), channel_id=1, source_target_pairs={{4,8},{8,4},{5,9},{9,5},{6,10},{10,6},{7,11},{11,7},{20,24},{24,20... | collective-permute-start | bytes 196616 | tf_op jit(solution)/shard_map/ppermute | solution.py:491
  133.3 24.2 %collective-permute-start.12 = (bf16[512,640]{1,0:T(8,128)(2,1)S(1)}, bf16[512,640]{1,0:T(8,128)(2,1)S(1)}, u32[]{:S(2)}, u32[]{:S(2)}) collective-permute-start(bf16[512,640]{1,0:T(8,128)(2,1)S(1)} %pad_maximum_fusion.sent), channel_id=1, source_target_pairs={{8,12},{4,0},{9,13},{5,1},{10,14},{6,2},{11,15},{7,3},{24,28},{20,... | collective-permute-start | bytes 1966088 | tf_op jit(solution)/shard_map/ppermute | solution.py:495
  135.6 28.0 %collective-permute-start.16 = (bf16[512,256]{1,0:T(8,128)(2,1)S(1)}, bf16[512,256]{1,0:T(8,128)(2,1)S(1)}, u32[]{:S(2)}, u32[]{:S(2)}) collective-permute-start(bf16[512,256]{1,0:T(8,128)(2,1)S(1)} %slice_select_fusion.2), channel_id=1, source_target_pairs={{8,12},{4,0},{9,13},{5,1},{10,14},{6,2},{11,15},{7,3},{24,28},{20,... | collective-permute-start | bytes 786440 | tf_op jit(solution)/shard_map/ppermute | solution.py:497

commit v18 on v17

--- a/solution.py
+++ b/solution.py
@@ -103,7 +103,7 @@
     return jnp.dot(own, fold.astype(F32), precision=lax.Precision.HIGHEST, preferred_element_type=F32)
 
 
-def shards_kernel(with_low, start, valid, *refs):
+def shards_kernel(with_low, halves, start, valid, *refs):
     refs = list(refs)
     xs = [refs.pop(0) for _ in range(valid.shape[0])]
     weight = refs.pop(0)
@@ -121,7 +121,7 @@
 
     for i, x in enumerate(xs):
 
-        @pl.when((step // 2 == i) & (valid[i] != 0))
+        @pl.when((step // halves == i) & (valid[i] != 0))
         def _():
             part = min(base.shape[1], 512)
             for n in range(0, base.shape[1], part):
@@ -144,11 +144,15 @@
     return start, there.astype(jnp.int32)
 
 
-def add_shards(base, xs, plan, weight, down=None, slot=None, rank_part=0):
+def add_shards(base, xs, plan, weight, down=None, slot=None, rank_part=0, only=None):
     rows, width = xs[0].shape
     half = width // 2
     columns = weight.shape[1]
-    steps = 2 * len(xs)
+    halves = 2 if only is None else 1
+    steps = halves * len(xs)
+    if only is not None:
+        start = plan[0].reshape(-1, 2)[:, only]
+        plan = (jnp.where(plan[1] != 0, start, start[::-1]), plan[1])
 
     def whole(a):
         return pl.BlockSpec((rows, a), lambda s, *_: (0, 0))
@@ -157,7 +161,8 @@
         return pl.BlockSpec((half, a.shape[1]), lambda s, start, valid: (start[s], 0))
 
     in_specs = [
-        pl.BlockSpec((rows, half), lambda s, *_, i=i: (0, jnp.clip(s - 2 * i, 0, 1))) for i in range(len(xs))
+        pl.BlockSpec((rows, half), lambda s, *_, i=i: (0, jnp.clip(s - 2 * i, 0, 1) if only is None else only))
+        for i in range(len(xs))
     ] + [walked(weight)]
     out_shape = [jax.ShapeDtypeStruct((rows, columns), F32)]
     scratch = []
@@ -172,7 +177,7 @@
         in_specs += [whole(columns)]
         rest = (base,)
     return pl.pallas_call(
-        functools.partial(shards_kernel, base is None),
+        functools.partial(shards_kernel, base is None, halves),
         out_shape=out_shape,
         grid_spec=pltpu.PrefetchScalarGridSpec(
             num_scalar_prefetch=2,
@@ -470,8 +475,6 @@
     base, low = add_shards(
         None, [attention_result, right_1, left_1], near, output_weight, down, slot, rank_part
     )
-    other_low = lax.ppermute(low, "tensor", [(0, 1), (3, 2)])
-
     right_2, left_2 = lax.optimization_barrier((base, right_2, left_2))[1:]
     third = right[-1:] + left[:1]
     cuts = (0, width // 8 * 5, width // 8 * 7, width)
@@ -482,16 +485,20 @@
 
     first_2 = piece(0)
     first_3 = lax.ppermute(first_2, "tensor", third)
+    right_2, left_2 = lax.optimization_barrier((first_2, right_2, left_2))[1:]
+    middle = piece(1)
+    other_low = lax.ppermute(after(low, middle), "tensor", [(0, 1), (3, 2)])
+    base, = add_shards(base, [right_2, left_2], far, output_weight, only=0)
     right_2, left_2, other_down, other_low = lax.optimization_barrier(
-        (first_2, right_2, left_2, other_down, other_low)
+        (base, right_2, left_2, other_down, other_low)
     )[1:]
     pair = far_low(
         far_facts, right_1, right_2, left_1, left_2, down, other_down, slot, live, low, other_low
     )
     from_middle = lax.ppermute(pair, "tensor", [(1, 2), (2, 1)])
-    base, = add_shards(after(base, pair), [right_2, left_2], far, output_weight)
+    base, = add_shards(after(base, pair), [right_2, left_2], far, output_weight, only=1)
     low = jnp.where(upper, jnp.concatenate([from_middle, pair], axis=1), jnp.concatenate([pair, from_middle], axis=1))
-    second_2 = jnp.concatenate([piece(1), low], axis=1)
+    second_2 = jnp.concatenate([middle, low], axis=1)
     second_3 = lax.ppermute(second_2, "tensor", third)
     right_2, left_2 = lax.optimization_barrier((second_2, right_2, left_2))[1:]
     last_3 = lax.ppermute(piece(2), "tensor", third)

time: 168 us -> 169 us (level)
  Pallas kernels: 60.9 us -> 67.5 us
  waiting for transfers between devices: 54.1 us -> 50.2 us
    pallas_call x2 -> x3, Pallas kernels: 31.1 us -> 37.5 us  [add_shards(): pl.pallas_call(functools.partial(shards_kernel, base is None, halves), ou...]
    ppermute x1, waiting for transfers between devices: 5.77 us -> 0.01 us  [local(): other_low = lax.ppermute(after(low, middle), 'tensor', [(0, 1), (3, 2)])]
    unnamed x14 -> x16, local copies, waits for them, and re-layouts: 6.75 us -> 3.57 us
  transfers between devices with their start and end apart: 17 -> 17, of which waited for: 7 -> 6; matrix products, arithmetic and copies ran while one was open for 9% -> 10% of each run, Pallas kernels for 35% -> 38%
where the time goes in v18:
time: 169 us
  Pallas kernels  67.5 us (40%)
  waiting for transfers between devices  50.2 us (30%)
  starting transfers between devices  29.5 us (17%)
  other arithmetic  12.3 us (7%)
  local copies, waits for them, and re-layouts  8.82 us (5%)
    pallas_call x3, Pallas kernels, add_shards(): pl.pallas_call(functools.partial(shards_kernel, base is None, halves), ou...  37.5 us
    ppermute x1, waiting for transfers between devices, local(): right_1 = lax.ppermute(attention_result, 'tensor', right)  33.5 us
    pallas_call x1, Pallas kernels, far_low(): pl.pallas_call(far_low_kernel, out_shape=jax.ShapeDtypeStruct((rows, 2 *...  8.29 us
    ppermute x1, starting transfers between devices, local(): other_down = lax.ppermute(other_down, 'tensor', [(0, 1), (3, 2)])  8.03 us
    pallas_call x1, Pallas kernels, add_half(): pl.pallas_call(half_kernel, out_shape=jax.ShapeDtypeStruct((rows, columns...  7.79 us
    pallas_call x1, Pallas kernels, prepare(): pl.pallas_call(prepare_kernel, out_shape=[pltpu.VMEM((rows, columns), F32...  6.12 us
    ppermute x1, waiting for transfers between devices, local(): left_2 = lax.ppermute(left_1, 'tensor', left[:-1])  6.05 us
    ppermute x1, starting transfers between devices, local(): other_low = lax.ppermute(after(low, middle), 'tensor', [(0, 1), (3, 2)])  5.64 us
  transfers between devices with their start and end apart: 17, of which 6 were waited for; matrix products, arithmetic and copies ran while one was open for 10% of the time, Pallas kernels for 38%

profile of v18, /device:TPU:0, one launch (start us, length us, event | category | flops | bytes accessed | tf_op | source)
XLA Modules:
  0.0 168.6 jit_solution(14525617301682719687)
XLA Ops:
  0.0 5.1 %collective-permute-start = (bf16[512,2048]{1,0:T(8,128)(2,1)}, bf16[512,2048]{1,0:T(8,128)(2,1)S(1)}, u32[]{:S(2)}, u32[]{:S(2)}) collective-permute-start(bf16[512,2048]{1,0:T(8,128)(2,1)} %refs_0_.4), channel_id=1, source_target_pairs={{0,4},{4,8},{8,12},{1,5},{5,9},{9,13},{2,6},{6,10},{10,14},{3,7},{... | collective-permute-start | bytes 6291464 | tf_op jit(solution)/shard_map/ppermute | solution.py:454
  5.1 1.3 collective-permute-start.1
  6.4 1.6 collective-permute-start.3
  7.9 0.5 collective-permute-start.14
  8.5 0.7 fusion
  9.1 0.6 slice.42
  9.7 0.6 add_bitcast_fusion
  10.3 0.7 fusion.4
  11.1 0.7 fusion.1
  11.8 0.7 fusion.6
  12.5 1.4 add_reduce_fusion
  14.0 0.9 select_reduce_fusion.1
  14.9 0.8 select_reduce_fusion
  15.7 0.7 fusion.3
  16.6 33.5 %collective-permute-done.refs_1_.left_1 = bf16[512,2048]{1,0:T(8,128)(2,1)S(1)} collective-permute-done((bf16[512,2048]{1,0:T(8,128)(2,1)}, bf16[512,2048]{1,0:T(8,128)(2,1)S(1)}, u32[]{:S(2)}, u32[]{:S(2)}) %collective-permute-start) | collective-permute-done | bytes 2097184 | tf_op jit(solution)/shard_map/ppermute | solution.py:454
  50.1 4.2 %collective-permute-done.1.refs_2_.right_1 = bf16[512,2048]{1,0:T(8,128)(2,1)} collective-permute-done((bf16[512,2048]{1,0:T(8,128)(2,1)}, bf16[512,2048]{1,0:T(8,128)(2,1)}, u32[]{:S(2)}, u32[]{:S(2)}) %collective-permute-start.1) | collective-permute-done | bytes 2097184 | tf_op jit(solution)/shard_map/ppermute | solution.py:455
  54.4 0.9 collective-permute-start.6
  55.3 1.3 collective-permute-start.7
  56.6 3.0 %fusion.5 = (bf16[2,32,8192]{2,1,0:T(8,128)(2,1)}, bf16[2,32,8192]{2,1,0:T(8,128)(2,1)}) fusion(bf16[4,32,8192]{2,1,0:T(8,128)(2,1)} %collective-permute-done.3.refs_2_), kind=kLoop, calls=%fused_computation.36 | loop fusion | bytes 4194304 | tf_op jit(solution)/shard_map/slice | solution.py:470
  59.6 0.5 collective-permute-start.5
  60.2 0.1 copy.21.refs_5_.slot.refs_4_
  60.3 3.0 %collective-permute-done.4.refs_3_ = bf16[2,32,8192]{2,1,0:T(8,128)(2,1)S(1)} collective-permute-done((bf16[2,32,8192]{2,1,0:T(8,128)(2,1)}, bf16[2,32,8192]{2,1,0:T(8,128)(2,1)S(1)}, u32[]{:S(2)}, u32[]{:S(2)}) %collective-permute-start.4) | collective-permute-done | bytes 1048608 | tf_op jit(solution)/shard_map/ppermute | solution.py:439
  63.3 0.1 collective-permute-start.13
  63.5 0.7 collective-permute-done.5.refs_4_
  64.1 1.6 copy-done.4
  65.7 4.7 %shard_map.100 = (bf16[8192,256]{1,0:T(8,128)(2,1)S(1)}, bf16[192,4096]{1,0:T(8,128)(2,1)}) custom-call(s32[6]{0:T(128)S(1)} %fusion.2.places, s32[1]{0:T(128)} %bitcast.8.upper, bf16[4,32,8192]{2,1,0:T(8,128)(2,1)S(1)} %copy-done.4, bf16[4,32,8192]{2,1,0:T(8,128)(2,1)} %collective-permute-done.2.refs_1_, ...), custom_call_target="tpu_custom_call" | custom-call | flops 1 | bytes 1 | tf_op jit(solution)/shard_map/pallas_call | solution.py:69
  70.4 2.0 %copy-done = bf16[8192,256]{1,0:T(8,128)(2,1)} copy-done((bf16[8192,256]{1,0:T(8,128)(2,1)}, bf16[8192,256]{1,0:T(8,128)(2,1)S(1)}, u32[]{:S(2)}) %copy-start) | copy-done | bytes 4194328
  72.4 8.0 %collective-permute-start.9 = (bf16[192,4096]{1,0:T(8,128)(2,1)}, bf16[192,4096]{1,0:T(8,128)(2,1)}, u32[]{:S(2)}, u32[]{:S(2)}) collective-permute-start(bf16[192,4096]{1,0:T(8,128)(2,1)} %get-tuple-element.62), channel_id=1, source_target_pairs={{0,4},{12,8},{1,5},{13,9},{2,6},{14,10},{3,7},{15,11},{16,20},{28,... | collective-permute-start | bytes 4718600 | tf_op jit(solution)/shard_map/ppermute | solution.py:473
  80.4 19.4 %shard_map.101 = (f32[512,2048]{1,0:T(8,128)}, f32[512,32]{1,0:T(8,128)S(1)}) custom-call(s32[6]{0:T(128)S(1)} %select_n.97.start, s32[3]{0:T(128)S(1)} %get-tuple-element.48.valid, bf16[512,2048]{1,0:T(8,128)(2,1)S(1)} %copy-done.5, bf16[512,2048]{1,0:T(8,128)(2,1)S(1)} %copy-done.2, bf16[512,2048]{1,0:T(8,128)(2,1)} %collective-permute-done.1.refs_2_.right_1, ...), custom_call_target="tpu_custom_call" | custom-call | flops 1 | bytes 1 | tf_op jit(solution)/shard_map/pallas_call | solution.py:179
  99.9 6.1 %collective-permute-done.7.refs_1_.right_2 = bf16[512,2048]{1,0:T(8,128)(2,1)} collective-permute-done((bf16[512,2048]{1,0:T(8,128)(2,1)}, bf16[512,2048]{1,0:T(8,128)(2,1)}, u32[]{:S(2)}, u32[]{:S(2)}) %collective-permute-start.7) | collective-permute-done | bytes 2097184 | tf_op jit(solution)/shard_map/ppermute | solution.py:467
  105.9 2.5 %slice_select_fusion = bf16[512,1280]{1,0:T(8,128)(2,1)} fusion(bf16[512,2048]{1,0:T(8,128)(2,1)} %collective-permute-done.7.refs_1_.right_2, bf16[512,2048]{1,0:T(8,128)(2,1)S(1)} %collective-permute-done.6.refs_0_.left_2, pred[]{:T(512)S(6)} %ge.9), kind=kLoop, calls=%fused_computation | loop fusion | flops 655360 | bytes 3932161 | tf_op jit(solution)/shard_map/jit(_where)/select_n | solution.py:484
  108.6 0.2 slice_reduce_fusion
  108.9 1.3 collective-permute-start.8
  110.2 1.9 %slice_select_fusion.1 = bf16[512,512]{1,0:T(8,128)(2,1)} fusion(bf16[512,2048]{1,0:T(8,128)(2,1)} %collective-permute-done.7.refs_1_.right_2, bf16[512,2048]{1,0:T(8,128)(2,1)S(1)} %collective-permute-done.6.refs_0_.left_2, pred[]{:T(512)S(6)} %ge.9), kind=kLoop, calls=%fused_computation.2 | loop fusion | flops 262144 | bytes 1572865 | tf_op jit(solution)/shard_map/jit(_where)/select_n | solution.py:484
  112.1 5.6 %collective-permute-start.10 = (f32[512,32]{1,0:T(8,128)S(1)}, f32[512,32]{1,0:T(8,128)S(1)}, u32[]{:S(2)}, u32[]{:S(2)}) collective-permute-start(f32[512,32]{1,0:T(8,128)S(1)} %get-tuple-element.64.low), channel_id=1, source_target_pairs={{0,4},{12,8},{1,5},{13,9},{2,6},{14,10},{3,7},{15,11},{16,20},{28,... | collective-permute-start | bytes 196616 | tf_op jit(solution)/shard_map/ppermute | solution.py:490
  117.8 0.1 copy.23.row_rank
  118.0 9.1 %shard_map.102.refs_3_ = f32[512,2048]{1,0:T(8,128)} custom-call(s32[2]{0:T(128)S(1)} %get-tuple-element.93.start, s32[2]{0:T(128)S(1)} %get-tuple-element.58.valid, bf16[512,2048]{1,0:T(8,128)(2,1)S(1)} %collective-permute-done.6.refs_0_.left_2, bf16[512,2048]{1,0:T(8,128)(2,1)} %collective-permute-done.7.refs_1_.right_2, bf16[8192,2048]{1,0:T(8,128)(2,1)} %weight.3, ...), custom_call_target="tpu_custom_call" | custom-call | flops 1 | bytes 1 | tf_op jit(solution)/shard_map/pallas_call | solution.py:179
  127.1 8.3 %shard_map.103 = bf16[512,64]{1,0:T(8,128)(2,1)S(1)} custom-call(s32[4]{0:T(128)S(1)} %pad_add_fusion.1.facts, bf16[512,2048]{1,0:T(8,128)(2,1)S(1)} %copy-done.3, bf16[512,2048]{1,0:T(8,128)(2,1)S(1)} %collective-permute-done.6.refs_0_.left_2, bf16[512,2048]{1,0:T(8,128)(2,1)} %collective-permute-done.1.refs_2_.right_1, ...), custom_call_target="tpu_custom_call" | custom-call | flops 1 | bytes 1 | tf_op jit(solution)/shard_map/pallas_call | solution.py:280
  135.4 0.7 collective-permute-start.11
  136.0 0.1 maximum_select_fusion
  136.3 1.3 collective-permute-start.12
  137.6 1.0 slice_select_fusion.2
  138.6 1.3 collective-permute-start.16
  139.9 9.0 %shard_map.104.base_in = f32[512,2048]{1,0:T(8,128)} custom-call(s32[2]{0:T(128)S(1)} %get-tuple-element.94.start, s32[2]{0:T(128)S(1)} %get-tuple-element.58.valid, bf16[512,2048]{1,0:T(8,128)(2,1)S(1)} %collective-permute-done.6.refs_0_.left_2, bf16[512,2048]{1,0:T(8,128)(2,1)} %collective-permute-done.7.refs_1_.right_2, bf16[8192,2048]{1,0:T(8,128)(2,1)} %weight.3, ...), custom_call_target="tpu_custom_call" | custom-call | flops 1 | bytes 1 | tf_op jit(solution)/shard_map/pallas_call | solution.py:179
  148.9 7.8 %shard_map.105.base = f32[512,2048]{1,0:T(8,128)S(1)} custom-call(s32[1]{0:T(128)} %bitcast.4.start, s32[1]{0:T(128)} %bitcast.3.valid, bf16[512,1280]{1,0:T(8,128)(2,1)} %collective-permute-done.8.x, bf16[8192,2048]{1,0:T(8,128)(2,1)} %weight.3, f32[512,2048]{1,0:T(8,128)} %shard_map.104.base_in), custom_call_target="tpu_custom_call" | custom-call | flops 1 | bytes 1 | tf_op jit(solution)/shard_map/pallas_call | solution.py:213
  156.7 2.7 %collective-permute-done.12.received = bf16[512,640]{1,0:T(8,128)(2,1)S(1)} collective-permute-done((bf16[512,640]{1,0:T(8,128)(2,1)S(1)}, bf16[512,640]{1,0:T(8,128)(2,1)S(1)}, u32[]{:S(2)}, u32[]{:S(2)}) %collective-permute-start.12) | collective-permute-done | bytes 655392 | tf_op jit(solution)/shard_map/ppermute | solution.py:502
  159.4 6.1 %shard_map.106 = (f32[512,2048]{1,0:T(8,128)S(1)}, bf16[256,2048]{1,0:T(8,128)(2,1)S(1)}) custom-call(s32[2]{0:T(128)S(1)} %pad_add_fusion.facts, s32[6]{0:T(128)S(1)} %fusion.2.places, f32[512,2048]{1,0:T(8,128)S(1)} %shard_map.105.base, bf16[512,640]{1,0:T(8,128)(2,1)S(1)} %pad_maximum_fusion.sent, bf16[512,640]{1,0:T(8,128)(2,1)S(1)} %collective-permute-done.12.received, ...), custom_call_target="tpu_custom_call" | custom-call | flops 1 | bytes 1 | tf_op jit(solution)/shard_map/pallas_call | solution.py:357
  165.5 3.1 %shard_map.107 = bf16[512,2048]{1,0:T(8,128)(2,1)} custom-call(s32[2]{0:T(128)S(1)} %pad_add_fusion.facts, f32[512,2048]{1,0:T(8,128)S(1)} %get-tuple-element.78.total, bf16[256,2048]{1,0:T(8,128)(2,1)S(1)} %get-tuple-element.79.weight, bf16[512,256]{1,0:T(8,128)(2,1)S(1)} %collective-permute-done.16.x), custom_call_target="tpu_custom_call" | custom-call | flops 1 | bytes 1 | tf_op jit(solution)/shard_map/pallas_call | solution.py:390
  (44 shorter events, 1.0 us)
Async XLA Ops:
  0.0 50.1 %collective-permute-start = (bf16[512,2048]{1,0:T(8,128)(2,1)}, bf16[512,2048]{1,0:T(8,128)(2,1)S(1)}, u32[]{:S(2)}, u32[]{:S(2)}) collective-permute-start(bf16[512,2048]{1,0:T(8,128)(2,1)} %refs_0_.4), channel_id=1, source_target_pairs={{0,4},{4,8},{8,12},{1,5},{5,9},{9,13},{2,6},{6,10},{10,14},{3,7},{... | collective-permute-start | bytes 6291464 | tf_op jit(solution)/shard_map/ppermute | solution.py:454
  5.1 49.3 %collective-permute-start.1 = (bf16[512,2048]{1,0:T(8,128)(2,1)}, bf16[512,2048]{1,0:T(8,128)(2,1)}, u32[]{:S(2)}, u32[]{:S(2)}) collective-permute-start(bf16[512,2048]{1,0:T(8,128)(2,1)} %refs_0_.4), channel_id=1, source_target_pairs={{4,0},{8,4},{12,8},{5,1},{9,5},{13,9},{6,2},{10,6},{14,10},{7,3},{... | collective-permute-start | bytes 6291464 | tf_op jit(solution)/shard_map/ppermute | solution.py:455
  6.4 50.2 %collective-permute-start.3 = (bf16[4,32,8192]{2,1,0:T(8,128)(2,1)}, bf16[4,32,8192]{2,1,0:T(8,128)(2,1)}, u32[]{:S(2)}, u32[]{:S(2)}) collective-permute-start(bf16[4,32,8192]{2,1,0:T(8,128)(2,1)} %refs_0_.3), channel_id=1, source_target_pairs={{0,2},{1,3},{2,0},{3,1},{4,6},{5,7},{6,4},{7,5},{8,10},{9,11},{10,... | collective-permute-start | bytes 6291464 | tf_op jit(solution)/shard_map/ppermute | solution.py:439
  7.9 51.7 %collective-permute-start.2 = (bf16[4,32,8192]{2,1,0:T(8,128)(2,1)}, bf16[4,32,8192]{2,1,0:T(8,128)(2,1)}, u32[]{:S(2)}, u32[]{:S(2)}) collective-permute-start(bf16[4,32,8192]{2,1,0:T(8,128)(2,1)} %refs_0_.3), channel_id=1, source_target_pairs={{0,1},{1,0},{2,3},{3,2},{4,5},{5,4},{6,7},{7,6},{8,9},{9,8},{10,11... | collective-permute-start | bytes 6291464 | tf_op jit(solution)/shard_map/ppermute | solution.py:439
  7.9 100.5 %collective-permute-start.14 = (bf16[4,128,2048]{2,1,0:T(8,128)(2,1)}, bf16[4,128,2048]{2,1,0:T(8,128)(2,1)}, u32[]{:S(2)}, u32[]{:S(2)}) collective-permute-start(bf16[4,128,2048]{2,1,0:T(8,128)(2,1)} %refs_0_.5), channel_id=1, source_target_pairs={{0,2},{1,3},{2,0},{3,1},{4,6},{5,7},{6,4},{7,5},{8,10},{9,11},{10,... | collective-permute-start | bytes 6291464 | tf_op jit(solution)/shard_map/ppermute | solution.py:439
  50.1 4.3 %copy-start.1 = (bf16[512,2048]{1,0:T(8,128)(2,1)}, bf16[512,2048]{1,0:T(8,128)(2,1)S(1)}, u32[]{:S(2)}) copy-start(bf16[512,2048]{1,0:T(8,128)(2,1)S(1)} %collective-permute-done.refs_1_.left_1) | copy-start | bytes 6291460
  54.4 5.8 %copy-start.7 = (s32[512]{0:T(512)S(1)}, s32[512]{0:T(512)}, u32[]{:S(2)}) copy-start(s32[512]{0:T(512)} %param.16) | copy-start | bytes 6148
  54.4 45.5 %collective-permute-start.6 = (bf16[512,2048]{1,0:T(8,128)(2,1)}, bf16[512,2048]{1,0:T(8,128)(2,1)S(1)}, u32[]{:S(2)}, u32[]{:S(2)}) collective-permute-start(bf16[512,2048]{1,0:T(8,128)(2,1)} %copy-done.1), channel_id=1, source_target_pairs={{4,8},{8,12},{5,9},{9,13},{6,10},{10,14},{7,11},{11,15},{20,24},{2... | collective-permute-start | bytes 6291464 | tf_op jit(solution)/shard_map/ppermute | solution.py:466
  55.3 50.6 %collective-permute-start.7 = (bf16[512,2048]{1,0:T(8,128)(2,1)}, bf16[512,2048]{1,0:T(8,128)(2,1)}, u32[]{:S(2)}, u32[]{:S(2)}) collective-permute-start(bf16[512,2048]{1,0:T(8,128)(2,1)} %collective-permute-done.1.refs_2_.right_1), channel_id=1, source_target_pairs={{4,0},{8,4},{5,1},{9,5},{6,2},{10,6},{7,3},{11,7},{20,16},{24,20},... | collective-permute-start | bytes 6291464 | tf_op jit(solution)/shard_map/ppermute | solution.py:467
  59.6 3.7 %collective-permute-start.4 = (bf16[2,32,8192]{2,1,0:T(8,128)(2,1)}, bf16[2,32,8192]{2,1,0:T(8,128)(2,1)S(1)}, u32[]{:S(2)}, u32[]{:S(2)}) collective-permute-start(bf16[2,32,8192]{2,1,0:T(8,128)(2,1)} %get-tuple-element.90), channel_id=1, source_target_pairs={{0,1},{1,0},{2,3},{3,2},{4,5},{5,4},{6,7},{7,6},{8,9},{9,8},{10,11... | collective-permute-start | bytes 3145736 | tf_op jit(solution)/shard_map/ppermute | solution.py:439
  59.6 4.5 %collective-permute-start.5 = (bf16[2,32,8192]{2,1,0:T(8,128)(2,1)}, bf16[2,32,8192]{2,1,0:T(8,128)(2,1)}, u32[]{:S(2)}, u32[]{:S(2)}) collective-permute-start(bf16[2,32,8192]{2,1,0:T(8,128)(2,1)} %get-tuple-element.89), channel_id=1, source_target_pairs={{0,1},{1,0},{2,3},{3,2},{4,5},{5,4},{6,7},{7,6},{8,9},{9,8},{10,11... | collective-permute-start | bytes 3145736 | tf_op jit(solution)/shard_map/ppermute | solution.py:439
  60.3 20.1 %copy-start.2 = (bf16[512,2048]{1,0:T(8,128)(2,1)S(1)}, bf16[512,2048]{1,0:T(8,128)(2,1)}, u32[]{:S(2)}) copy-start(bf16[512,2048]{1,0:T(8,128)(2,1)} %copy-done.1) | copy-start | bytes 6291460
  63.3 93.3 %collective-permute-start.13 = (bf16[4,128,2048]{2,1,0:T(8,128)(2,1)}, bf16[4,128,2048]{2,1,0:T(8,128)(2,1)}, u32[]{:S(2)}, u32[]{:S(2)}) collective-permute-start(bf16[4,128,2048]{2,1,0:T(8,128)(2,1)} %refs_0_.5), channel_id=1, source_target_pairs={{0,1},{1,0},{2,3},{3,2},{4,5},{5,4},{6,7},{7,6},{8,9},{9,8},{10,11... | collective-permute-start | bytes 6291464 | tf_op jit(solution)/shard_map/ppermute | solution.py:439
  64.1 1.6 copy-start.4
  65.7 14.7 %copy-start.5 = (bf16[512,2048]{1,0:T(8,128)(2,1)S(1)}, bf16[512,2048]{1,0:T(8,128)(2,1)}, u32[]{:S(2)}) copy-start(bf16[512,2048]{1,0:T(8,128)(2,1)} %refs_0_.4) | copy-start | bytes 6291460
  70.4 2.0 %copy-start = (bf16[8192,256]{1,0:T(8,128)(2,1)}, bf16[8192,256]{1,0:T(8,128)(2,1)S(1)}, u32[]{:S(2)}) copy-start(bf16[8192,256]{1,0:T(8,128)(2,1)S(1)} %get-tuple-element.53.refs_4_.down) | copy-start | bytes 12582916
  72.4 54.6 %collective-permute-start.9 = (bf16[192,4096]{1,0:T(8,128)(2,1)}, bf16[192,4096]{1,0:T(8,128)(2,1)}, u32[]{:S(2)}, u32[]{:S(2)}) collective-permute-start(bf16[192,4096]{1,0:T(8,128)(2,1)} %get-tuple-element.62), channel_id=1, source_target_pairs={{0,4},{12,8},{1,5},{13,9},{2,6},{14,10},{3,7},{15,11},{16,20},{28,... | collective-permute-start | bytes 4718600 | tf_op jit(solution)/shard_map/ppermute | solution.py:473
  108.5 50.9 %collective-permute-start.15 = (bf16[4,128,2048]{2,1,0:T(8,128)(2,1)}, bf16[4,128,2048]{2,1,0:T(8,128)(2,1)}, u32[]{:S(2)}, u32[]{:S(2)}) collective-permute-start(bf16[4,128,2048]{2,1,0:T(8,128)(2,1)} %collective-permute-done.14.refs_2_), channel_id=1, source_target_pairs={{0,1},{1,0},{2,3},{3,2},{4,5},{5,4},{6,7},{7,6},{8,9},{9,8},{10,11... | collective-permute-start | bytes 6291464 | tf_op jit(solution)/shard_map/ppermute | solution.py:439
  108.9 40.0 %collective-permute-start.8 = (bf16[512,1280]{1,0:T(8,128)(2,1)}, bf16[512,1280]{1,0:T(8,128)(2,1)}, u32[]{:S(2)}, u32[]{:S(2)}) collective-permute-start(bf16[512,1280]{1,0:T(8,128)(2,1)} %slice_select_fusion), channel_id=1, source_target_pairs={{8,12},{4,0},{9,13},{5,1},{10,14},{6,2},{11,15},{7,3},{24,28},{20,... | collective-permute-start | bytes 3932168 | tf_op jit(solution)/shard_map/ppermute | solution.py:487
  112.1 14.9 %collective-permute-start.10 = (f32[512,32]{1,0:T(8,128)S(1)}, f32[512,32]{1,0:T(8,128)S(1)}, u32[]{:S(2)}, u32[]{:S(2)}) collective-permute-start(f32[512,32]{1,0:T(8,128)S(1)} %get-tuple-element.64.low), channel_id=1, source_target_pairs={{0,4},{12,8},{1,5},{13,9},{2,6},{14,10},{3,7},{15,11},{16,20},{28,... | collective-permute-start | bytes 196616 | tf_op jit(solution)/shard_map/ppermute | solution.py:490
  118.0 9.1 %copy-start.3 = (bf16[512,2048]{1,0:T(8,128)(2,1)S(1)}, bf16[512,2048]{1,0:T(8,128)(2,1)}, u32[]{:S(2)}) copy-start(bf16[512,2048]{1,0:T(8,128)(2,1)} %copy-done.1) | copy-start | bytes 6291460
  127.0 9.2 %copy-start.6 = (bf16[512,512]{1,0:T(8,128)(2,1)S(1)}, bf16[512,512]{1,0:T(8,128)(2,1)}, u32[]{:S(2)}) copy-start(bf16[512,512]{1,0:T(8,128)(2,1)} %slice_select_fusion.1) | copy-start | bytes 1572868
  135.4 0.7 collective-permute-start.11
  136.3 23.1 %collective-permute-start.12 = (bf16[512,640]{1,0:T(8,128)(2,1)S(1)}, bf16[512,640]{1,0:T(8,128)(2,1)S(1)}, u32[]{:S(2)}, u32[]{:S(2)}) collective-permute-start(bf16[512,640]{1,0:T(8,128)(2,1)S(1)} %pad_maximum_fusion.sent), channel_id=1, source_target_pairs={{8,12},{4,0},{9,13},{5,1},{10,14},{6,2},{11,15},{7,3},{24,28},{20,... | collective-permute-start | bytes 1966088 | tf_op jit(solution)/shard_map/ppermute | solution.py:502
  138.6 26.9 %collective-permute-start.16 = (bf16[512,256]{1,0:T(8,128)(2,1)S(1)}, bf16[512,256]{1,0:T(8,128)(2,1)S(1)}, u32[]{:S(2)}, u32[]{:S(2)}) collective-permute-start(bf16[512,256]{1,0:T(8,128)(2,1)S(1)} %slice_select_fusion.2), channel_id=1, source_target_pairs={{8,12},{4,0},{9,13},{5,1},{10,14},{6,2},{11,15},{7,3},{24,28},{20,... | collective-permute-start | bytes 786440 | tf_op jit(solution)/shard_map/ppermute | solution.py:504

commit v19 on v17

--- a/solution.py
+++ b/solution.py
@@ -186,41 +186,58 @@
     )(*plan, *xs, weight, *rest)
 
 
-def half_kernel(start, valid, x, weight, base_in, base):
+def far_kernel(start, valid, third_start, third_valid, left, right, third, weight, third_rows, base_in, base):
     step = pl.program_id(0)
+    part = min(base.shape[1], 512)
+
+    def add(x, rows):
+        for n in range(0, base.shape[1], part):
+            base[:, n:n + part] += jnp.dot(x[...], rows[:, n:n + part], preferred_element_type=F32)
 
     @pl.when(step == 0)
     def _():
         base[...] = base_in[...]
 
-    @pl.when(valid[0] != 0)
-    def _():
-        part = min(base.shape[1], 512)
-        for n in range(0, base.shape[1], part):
-            base[:, n:n + part] += jnp.dot(x[...], weight[:, n:n + part], preferred_element_type=F32)
-
-
-def add_half(base, x, valid, source, weight):
-    rows, half = x.shape
+    for i, x in enumerate((left, right)):
+
+        @pl.when((step // 2 == i) & (valid[i] != 0))
+        def _():
+            add(x, weight)
+
+    @pl.when((step >= 4) & (third_valid[0] != 0))
+    def _():
+        add(third, third_rows)
+
+
+def add_far(base, left, right, plan, third, third_start, third_valid, weight):
+    rows, width = left.shape
     columns = weight.shape[1]
-    step = half // 5
+    half, unit = width // 2, width // 8
+    pieces = third.shape[1] // unit
     whole = pl.BlockSpec((rows, columns), lambda s, *_: (0, 0))
+
+    def piece(s, third_valid):
+        return jnp.clip(s - 4, 0, pieces - 1) * third_valid[0]
+
     return pl.pallas_call(
-        half_kernel,
+        far_kernel,
         out_shape=jax.ShapeDtypeStruct((rows, columns), F32),
         grid_spec=pltpu.PrefetchScalarGridSpec(
-            num_scalar_prefetch=2,
-            grid=(half // step,),
+            num_scalar_prefetch=4,
+            grid=(4 + pieces,),
             in_specs=[
-                pl.BlockSpec((rows, step), lambda s, *_: (0, s)),
-                pl.BlockSpec((step, columns), lambda s, source, valid: (source[0] * (columns // step) + s, 0)),
+                pl.BlockSpec((rows, half), lambda s, *_: (0, jnp.clip(s, 0, 1))),
+                pl.BlockSpec((rows, half), lambda s, *_: (0, jnp.clip(s - 2, 0, 1))),
+                pl.BlockSpec((rows, unit), lambda s, a, b, c, d: (0, piece(s, d))),
+                pl.BlockSpec((half, columns), lambda s, a, b, c, d: (a[jnp.clip(s, 0, 3)], 0)),
+                pl.BlockSpec((unit, columns), lambda s, a, b, c, d: (c[0] * 8 + piece(s, d), 0)),
                 whole,
             ],
             out_specs=whole,
         ),
         compiler_params=PARAMS,
         cost_estimate=pl.CostEstimate(flops=1, bytes_accessed=1, transcendentals=0),
-    )(source, valid, x, weight, base)
+    )(*plan, third_start, third_valid, left, right, third, weight, weight, base)
 
 
 def far_low_kernel(
@@ -489,14 +506,13 @@
         far_facts, right_1, right_2, left_1, left_2, down, other_down, slot, live, low, other_low
     )
     from_middle = lax.ppermute(pair, "tensor", [(1, 2), (2, 1)])
-    base, = add_shards(after(base, pair), [right_2, left_2], far, output_weight)
     low = jnp.where(upper, jnp.concatenate([from_middle, pair], axis=1), jnp.concatenate([pair, from_middle], axis=1))
     second_2 = jnp.concatenate([piece(1), low], axis=1)
     second_3 = lax.ppermute(second_2, "tensor", third)
     right_2, left_2 = lax.optimization_barrier((second_2, right_2, left_2))[1:]
     last_3 = lax.ppermute(piece(2), "tensor", third)
     ups = (adapter_up_weight, across(after(adapter_up_weight, far_down), 1), far_up, across(after(far_up, first_2), 1))
-    base = add_half(base, first_3, ended, started, output_weight)
+    base = add_far(after(base, pair), right_2, left_2, far, first_3, started, ended, output_weight)
     total, rows_of = prepare(facts, places, base, second_2, second_3, width - cuts[2], output_weight, ups, slot)
     total, rows_of, last_3 = lax.optimization_barrier((total, rows_of, last_3))
     return add_last(facts, total, rows_of, last_3)

time: 168 us -> 172 us (1.024)
  waiting for transfers between devices: 54.1 us -> 58.4 us
  local copies, waits for them, and re-layouts: 10.2 us -> 12.4 us
  Pallas kernels: 60.9 us -> 58.7 us
    pallas_call x2 -> x1, Pallas kernels: 31.1 us -> 19.4 us  [add_shards(): pl.pallas_call(functools.partial(shards_kernel, base is None), out_shape=...]
    pallas_call x1, Pallas kernels: 7.79 us -> 17.3 us  [add_far(): pl.pallas_call(far_kernel, out_shape=jax.ShapeDtypeStruct((rows, columns)...]
    ppermute x1, waiting for transfers between devices: 0.01 us -> 5.38 us  [local(): first_3 = lax.ppermute(first_2, 'tensor', third)]
    unnamed x14 -> x16, local copies, waits for them, and re-layouts: 6.75 us -> 8.95 us
  transfers between devices with their start and end apart: 17 -> 17, of which waited for: 7 -> 7; matrix products, arithmetic and copies ran while one was open for 9% -> 9% of each run, Pallas kernels for 35% -> 33%
where the time goes in v19:
time: 172 us; the launch traced here: 171 us
  Pallas kernels  58.7 us (34%)
  waiting for transfers between devices  58.4 us (34%)
  starting transfers between devices  29.7 us (17%)
  local copies, waits for them, and re-layouts  12.4 us (7%)
  other arithmetic  11.5 us (7%)
    ppermute x1, waiting for transfers between devices, local(): right_1 = lax.ppermute(attention_result, 'tensor', right)  33.5 us
    pallas_call x1, Pallas kernels, add_shards(): pl.pallas_call(functools.partial(shards_kernel, base is None), out_shape=...  19.4 us
    pallas_call x1, Pallas kernels, add_far(): pl.pallas_call(far_kernel, out_shape=jax.ShapeDtypeStruct((rows, columns)...  17.3 us
    unnamed x16, local copies, waits for them, and re-layouts  8.95 us
    pallas_call x1, Pallas kernels, far_low(): pl.pallas_call(far_low_kernel, out_shape=jax.ShapeDtypeStruct((rows, 2 *...  8.07 us
    ppermute x1, starting transfers between devices, local(): other_down = lax.ppermute(other_down, 'tensor', [(0, 1), (3, 2)])  7.95 us
    pallas_call x1, Pallas kernels, prepare(): pl.pallas_call(prepare_kernel, out_shape=[pltpu.VMEM((rows, columns), F32...  6.03 us
    ppermute x1, waiting for transfers between devices, local(): left_2 = lax.ppermute(left_1, 'tensor', left[:-1])  5.88 us
  transfers between devices with their start and end apart: 17, of which 7 were waited for; matrix products, arithmetic and copies ran while one was open for 9% of the time, Pallas kernels for 33%

profile of v19, /device:TPU:0, one launch (start us, length us, event | category | flops | bytes accessed | tf_op | source)
XLA Modules:
  0.0 171.0 jit_solution(543640996730636492)
XLA Ops:
  0.0 5.1 %collective-permute-start = (bf16[512,2048]{1,0:T(8,128)(2,1)}, bf16[512,2048]{1,0:T(8,128)(2,1)S(1)}, u32[]{:S(2)}, u32[]{:S(2)}) collective-permute-start(bf16[512,2048]{1,0:T(8,128)(2,1)} %refs_0_.4), channel_id=1, source_target_pairs={{0,4},{4,8},{8,12},{1,5},{5,9},{9,13},{2,6},{6,10},{10,14},{3,7},{... | collective-permute-start | bytes 6291464 | tf_op jit(solution)/shard_map/ppermute | solution.py:466
  5.1 1.3 collective-permute-start.1
  6.4 1.6 collective-permute-start.3
  8.0 0.5 collective-permute-start.14
  8.5 0.7 fusion
  9.2 0.7 fusion.1
  9.9 0.6 slice.36
  10.5 0.6 fusion.6
  11.2 1.4 add_reduce_fusion
  12.6 0.6 add_bitcast_fusion
  13.3 0.9 select_reduce_fusion.1
  14.2 0.8 select_reduce_fusion
  15.0 0.7 fusion.4
  15.6 0.7 fusion.3
  16.7 33.5 %collective-permute-done.refs_1_.left_1 = bf16[512,2048]{1,0:T(8,128)(2,1)S(1)} collective-permute-done((bf16[512,2048]{1,0:T(8,128)(2,1)}, bf16[512,2048]{1,0:T(8,128)(2,1)S(1)}, u32[]{:S(2)}, u32[]{:S(2)}) %collective-permute-start) | collective-permute-done | bytes 2097184 | tf_op jit(solution)/shard_map/ppermute | solution.py:466
  50.1 4.2 %collective-permute-done.1.refs_2_.right_1 = bf16[512,2048]{1,0:T(8,128)(2,1)} collective-permute-done((bf16[512,2048]{1,0:T(8,128)(2,1)}, bf16[512,2048]{1,0:T(8,128)(2,1)}, u32[]{:S(2)}, u32[]{:S(2)}) %collective-permute-start.1) | collective-permute-done | bytes 2097184 | tf_op jit(solution)/shard_map/ppermute | solution.py:467
  54.4 0.9 collective-permute-start.6
  55.3 1.3 collective-permute-start.7
  56.6 1.7 fusion.5
  58.4 0.5 collective-permute-start.5
  58.9 2.1 %collective-permute-done.4.refs_3_ = bf16[2,32,8192]{2,1,0:T(8,128)(2,1)S(1)} collective-permute-done((bf16[2,32,8192]{2,1,0:T(8,128)(2,1)S(1)}, bf16[2,32,8192]{2,1,0:T(8,128)(2,1)S(1)}, u32[]{:S(2)}, u32[]{:S(2)}) %collective-permute-start.4) | collective-permute-done | bytes 1048608 | tf_op jit(solution)/shard_map/ppermute | solution.py:451
  61.0 1.5 collective-permute-done.5.refs_4_
  62.5 4.7 %shard_map.100 = (bf16[8192,256]{1,0:T(8,128)(2,1)S(1)}, bf16[192,4096]{1,0:T(8,128)(2,1)}) custom-call(s32[6]{0:T(128)S(1)} %fusion.2.places, s32[1]{0:T(128)} %bitcast.8.upper, bf16[4,32,8192]{2,1,0:T(8,128)(2,1)S(1)} %copy-done.5, bf16[4,32,8192]{2,1,0:T(8,128)(2,1)} %collective-permute-done.2.refs_1_, ...), custom_call_target="tpu_custom_call" | custom-call | flops 1 | bytes 1 | tf_op jit(solution)/shard_map/pallas_call | solution.py:69
  67.3 2.0 %copy-done = bf16[8192,256]{1,0:T(8,128)(2,1)} copy-done((bf16[8192,256]{1,0:T(8,128)(2,1)}, bf16[8192,256]{1,0:T(8,128)(2,1)S(1)}, u32[]{:S(2)}) %copy-start) | copy-done | bytes 4194328
  69.3 8.0 %collective-permute-start.8 = (bf16[192,4096]{1,0:T(8,128)(2,1)}, bf16[192,4096]{1,0:T(8,128)(2,1)}, u32[]{:S(2)}, u32[]{:S(2)}) collective-permute-start(bf16[192,4096]{1,0:T(8,128)(2,1)} %get-tuple-element.57), channel_id=1, source_target_pairs={{0,4},{12,8},{1,5},{13,9},{2,6},{14,10},{3,7},{15,11},{16,20},{28,... | collective-permute-start | bytes 4718600 | tf_op jit(solution)/shard_map/ppermute | solution.py:485
  77.2 0.1 copy.21.refs_5_.slot.refs_4_
  77.5 1.6 copy-done.3
  79.0 1.6 copy-done.6
  80.6 19.4 %shard_map.101 = (f32[512,2048]{1,0:T(8,128)}, f32[512,32]{1,0:T(8,128)S(1)}) custom-call(s32[6]{0:T(128)S(1)} %select_n.90.start, s32[3]{0:T(128)S(1)} %get-tuple-element.47.valid, bf16[512,2048]{1,0:T(8,128)(2,1)S(1)} %copy-done.6, bf16[512,2048]{1,0:T(8,128)(2,1)S(1)} %copy-done.3, bf16[512,2048]{1,0:T(8,128)(2,1)} %collective-permute-done.1.refs_2_.right_1, ...), custom_call_target="tpu_custom_call" | custom-call | flops 1 | bytes 1 | tf_op jit(solution)/shard_map/pallas_call | solution.py:174
  100.0 5.9 %collective-permute-done.7.right_2.right = bf16[512,2048]{1,0:T(8,128)(2,1)} collective-permute-done((bf16[512,2048]{1,0:T(8,128)(2,1)}, bf16[512,2048]{1,0:T(8,128)(2,1)}, u32[]{:S(2)}, u32[]{:S(2)}) %collective-permute-start.7) | collective-permute-done | bytes 2097184 | tf_op jit(solution)/shard_map/ppermute | solution.py:479
  105.9 2.6 %slice_select_fusion = bf16[512,1280]{1,0:T(8,128)(2,1)} fusion(bf16[512,2048]{1,0:T(8,128)(2,1)} %collective-permute-done.7.right_2.right, bf16[512,2048]{1,0:T(8,128)(2,1)S(1)} %collective-permute-done.6.left_2.left, pred[]{:T(512)S(6)} %ge.9), kind=kLoop, calls=%fused_computation | loop fusion | flops 655360 | bytes 3932161 | tf_op jit(solution)/shard_map/jit(_where)/select_n | solution.py:498
  108.5 1.3 collective-permute-start.11
  109.8 5.6 %collective-permute-start.9 = (f32[512,32]{1,0:T(8,128)S(1)}, f32[512,32]{1,0:T(8,128)S(1)}, u32[]{:S(2)}, u32[]{:S(2)}) collective-permute-start(f32[512,32]{1,0:T(8,128)S(1)} %get-tuple-element.58.low), channel_id=1, source_target_pairs={{0,4},{12,8},{1,5},{13,9},{2,6},{14,10},{3,7},{15,11},{16,20},{28,... | collective-permute-start | bytes 196616 | tf_op jit(solution)/shard_map/ppermute | solution.py:490
  115.5 0.1 copy.23.row_rank
  115.6 5.8 %collective-permute-done.9.other_low = f32[512,32]{1,0:T(8,128)S(1)} collective-permute-done((f32[512,32]{1,0:T(8,128)S(1)}, f32[512,32]{1,0:T(8,128)S(1)}, u32[]{:S(2)}, u32[]{:S(2)}) %collective-permute-start.9) | collective-permute-done | bytes 65568 | tf_op jit(solution)/shard_map/ppermute | solution.py:490
  121.4 1.6 copy-done.4
  123.0 8.1 %shard_map.102 = bf16[512,64]{1,0:T(8,128)(2,1)S(1)} custom-call(s32[4]{0:T(128)S(1)} %pad_add_fusion.1.facts, bf16[512,2048]{1,0:T(8,128)(2,1)S(1)} %copy-done.4, bf16[512,2048]{1,0:T(8,128)(2,1)S(1)} %collective-permute-done.6.left_2.left, bf16[512,2048]{1,0:T(8,128)(2,1)} %collective-permute-done.1.refs_2_.right_1, ...), custom_call_target="tpu_custom_call" | custom-call | flops 1 | bytes 1 | tf_op jit(solution)/shard_map/pallas_call | solution.py:292
  131.0 0.9 collective-permute-start.10
  131.9 1.1 slice_select_fusion.1
  133.1 0.1 maximum_select_fusion
  133.3 1.3 collective-permute-start.12
  134.6 1.0 slice_select_fusion.2
  135.6 1.3 collective-permute-start.16
  136.9 5.4 %collective-permute-done.11.third = bf16[512,1280]{1,0:T(8,128)(2,1)} collective-permute-done((bf16[512,1280]{1,0:T(8,128)(2,1)}, bf16[512,1280]{1,0:T(8,128)(2,1)}, u32[]{:S(2)}, u32[]{:S(2)}) %collective-permute-start.11) | collective-permute-done | bytes 1310752 | tf_op jit(solution)/shard_map/ppermute | solution.py:501
  142.3 17.3 %shard_map.103.base = f32[512,2048]{1,0:T(8,128)} custom-call(s32[4]{0:T(128)S(1)} %select_n.92.start, s32[2]{0:T(128)S(1)} %get-tuple-element.43.valid, s32[1]{0:T(128)} %bitcast.4.third_start, s32[1]{0:T(128)} %bitcast.3.third_valid, bf16[512,2048]{1,0:T(8,128)(2,1)S(1)} %collective-permute-done.6.left_2.left, ...), custom_call_target="tpu_custom_call" | custom-call | flops 1 | bytes 1 | tf_op jit(solution)/shard_map/pallas_call | solution.py:222
  159.6 2.2 %copy-done.1 = f32[512,2048]{1,0:T(8,128)S(1)} copy-done((f32[512,2048]{1,0:T(8,128)S(1)}, f32[512,2048]{1,0:T(8,128)}, u32[]{:S(2)}) %copy-start.1) | copy-done | bytes 4194328
  161.8 6.0 %shard_map.104 = (f32[512,2048]{1,0:T(8,128)S(1)}, bf16[256,2048]{1,0:T(8,128)(2,1)S(1)}) custom-call(s32[2]{0:T(128)S(1)} %pad_add_fusion.facts, s32[6]{0:T(128)S(1)} %fusion.2.places, f32[512,2048]{1,0:T(8,128)S(1)} %copy-done.1, bf16[512,640]{1,0:T(8,128)(2,1)S(1)} %pad_maximum_fusion.sent, bf16[512,640]{1,0:T(8,128)(2,1)S(1)} %collective-permute-done.12.received, ...), custom_call_target="tpu_custom_call" | custom-call | flops 1 | bytes 1 | tf_op jit(solution)/shard_map/pallas_call | solution.py:369
  167.9 3.1 %shard_map.105 = bf16[512,2048]{1,0:T(8,128)(2,1)} custom-call(s32[2]{0:T(128)S(1)} %pad_add_fusion.facts, f32[512,2048]{1,0:T(8,128)S(1)} %get-tuple-element.72.total, bf16[256,2048]{1,0:T(8,128)(2,1)S(1)} %get-tuple-element.73.weight, bf16[512,256]{1,0:T(8,128)(2,1)S(1)} %collective-permute-done.16.x), custom_call_target="tpu_custom_call" | custom-call | flops 1 | bytes 1 | tf_op jit(solution)/shard_map/pallas_call | solution.py:402
  (37 shorter events, 0.9 us)
Async XLA Ops:
  0.0 50.1 %collective-permute-start = (bf16[512,2048]{1,0:T(8,128)(2,1)}, bf16[512,2048]{1,0:T(8,128)(2,1)S(1)}, u32[]{:S(2)}, u32[]{:S(2)}) collective-permute-start(bf16[512,2048]{1,0:T(8,128)(2,1)} %refs_0_.4), channel_id=1, source_target_pairs={{0,4},{4,8},{8,12},{1,5},{5,9},{9,13},{2,6},{6,10},{10,14},{3,7},{... | collective-permute-start | bytes 6291464 | tf_op jit(solution)/shard_map/ppermute | solution.py:466
  5.1 49.3 %collective-permute-start.1 = (bf16[512,2048]{1,0:T(8,128)(2,1)}, bf16[512,2048]{1,0:T(8,128)(2,1)}, u32[]{:S(2)}, u32[]{:S(2)}) collective-permute-start(bf16[512,2048]{1,0:T(8,128)(2,1)} %refs_0_.4), channel_id=1, source_target_pairs={{4,0},{8,4},{12,8},{5,1},{9,5},{13,9},{6,2},{10,6},{14,10},{7,3},{... | collective-permute-start | bytes 6291464 | tf_op jit(solution)/shard_map/ppermute | solution.py:467
  6.4 52.0 %collective-permute-start.2 = (bf16[4,32,8192]{2,1,0:T(8,128)(2,1)}, bf16[4,32,8192]{2,1,0:T(8,128)(2,1)}, u32[]{:S(2)}, u32[]{:S(2)}) collective-permute-start(bf16[4,32,8192]{2,1,0:T(8,128)(2,1)} %refs_0_.3), channel_id=1, source_target_pairs={{0,1},{1,0},{2,3},{3,2},{4,5},{5,4},{6,7},{7,6},{8,9},{9,8},{10,11... | collective-permute-start | bytes 6291464 | tf_op jit(solution)/shard_map/ppermute | solution.py:451
  6.4 50.2 %collective-permute-start.3 = (bf16[4,32,8192]{2,1,0:T(8,128)(2,1)}, bf16[4,32,8192]{2,1,0:T(8,128)(2,1)}, u32[]{:S(2)}, u32[]{:S(2)}) collective-permute-start(bf16[4,32,8192]{2,1,0:T(8,128)(2,1)} %refs_0_.3), channel_id=1, source_target_pairs={{0,2},{1,3},{2,0},{3,1},{4,6},{5,7},{6,4},{7,5},{8,10},{9,11},{10,... | collective-permute-start | bytes 6291464 | tf_op jit(solution)/shard_map/ppermute | solution.py:451
  8.0 100.5 %collective-permute-start.14 = (bf16[4,128,2048]{2,1,0:T(8,128)(2,1)}, bf16[4,128,2048]{2,1,0:T(8,128)(2,1)}, u32[]{:S(2)}, u32[]{:S(2)}) collective-permute-start(bf16[4,128,2048]{2,1,0:T(8,128)(2,1)} %refs_0_.5), channel_id=1, source_target_pairs={{0,2},{1,3},{2,0},{3,1},{4,6},{5,7},{6,4},{7,5},{8,10},{9,11},{10,... | collective-permute-start | bytes 6291464 | tf_op jit(solution)/shard_map/ppermute | solution.py:451
  50.1 4.3 %copy-start.2 = (bf16[512,2048]{1,0:T(8,128)(2,1)}, bf16[512,2048]{1,0:T(8,128)(2,1)S(1)}, u32[]{:S(2)}) copy-start(bf16[512,2048]{1,0:T(8,128)(2,1)S(1)} %collective-permute-done.refs_1_.left_1) | copy-start | bytes 6291460
  54.4 8.1 %copy-start.5 = (bf16[4,32,8192]{2,1,0:T(8,128)(2,1)S(1)}, bf16[4,32,8192]{2,1,0:T(8,128)(2,1)}, u32[]{:S(2)}) copy-start(bf16[4,32,8192]{2,1,0:T(8,128)(2,1)} %refs_0_.3) | copy-start | bytes 6291460
  54.4 45.7 %collective-permute-start.6 = (bf16[512,2048]{1,0:T(8,128)(2,1)}, bf16[512,2048]{1,0:T(8,128)(2,1)S(1)}, u32[]{:S(2)}, u32[]{:S(2)}) collective-permute-start(bf16[512,2048]{1,0:T(8,128)(2,1)} %copy-done.2), channel_id=1, source_target_pairs={{4,8},{8,12},{5,9},{9,13},{6,10},{10,14},{7,11},{11,15},{20,24},{2... | collective-permute-start | bytes 6291464 | tf_op jit(solution)/shard_map/ppermute | solution.py:478
  55.3 50.6 %collective-permute-start.7 = (bf16[512,2048]{1,0:T(8,128)(2,1)}, bf16[512,2048]{1,0:T(8,128)(2,1)}, u32[]{:S(2)}, u32[]{:S(2)}) collective-permute-start(bf16[512,2048]{1,0:T(8,128)(2,1)} %collective-permute-done.1.refs_2_.right_1), channel_id=1, source_target_pairs={{4,0},{8,4},{5,1},{9,5},{6,2},{10,6},{7,3},{11,7},{20,16},{24,20},... | collective-permute-start | bytes 6291464 | tf_op jit(solution)/shard_map/ppermute | solution.py:479
  58.3 2.7 %collective-permute-start.4 = (bf16[2,32,8192]{2,1,0:T(8,128)(2,1)S(1)}, bf16[2,32,8192]{2,1,0:T(8,128)(2,1)S(1)}, u32[]{:S(2)}, u32[]{:S(2)}) collective-permute-start(bf16[2,32,8192]{2,1,0:T(8,128)(2,1)S(1)} %get-tuple-element.82), channel_id=1, source_target_pairs={{0,1},{1,0},{2,3},{3,2},{4,5},{5,4},{6,7},{7,6},{8,9},{9,8},{10,11... | collective-permute-start | bytes 3145736 | tf_op jit(solution)/shard_map/ppermute | solution.py:451
  58.4 18.8 %copy-start.7 = (s32[512]{0:T(512)S(1)}, s32[512]{0:T(512)}, u32[]{:S(2)}) copy-start(s32[512]{0:T(512)} %param.16) | copy-start | bytes 6148
  58.4 4.1 %collective-permute-start.5 = (bf16[2,32,8192]{2,1,0:T(8,128)(2,1)S(1)}, bf16[2,32,8192]{2,1,0:T(8,128)(2,1)S(1)}, u32[]{:S(2)}, u32[]{:S(2)}) collective-permute-start(bf16[2,32,8192]{2,1,0:T(8,128)(2,1)S(1)} %get-tuple-element.81), channel_id=1, source_target_pairs={{0,1},{1,0},{2,3},{3,2},{4,5},{5,4},{6,7},{7,6},{8,9},{9,8},{10,11... | collective-permute-start | bytes 3145736 | tf_op jit(solution)/shard_map/ppermute | solution.py:451
  67.3 2.0 %copy-start = (bf16[8192,256]{1,0:T(8,128)(2,1)}, bf16[8192,256]{1,0:T(8,128)(2,1)S(1)}, u32[]{:S(2)}) copy-start(bf16[8192,256]{1,0:T(8,128)(2,1)S(1)} %get-tuple-element.52.refs_4_.down) | copy-start | bytes 12582916
  69.3 52.1 %collective-permute-start.8 = (bf16[192,4096]{1,0:T(8,128)(2,1)}, bf16[192,4096]{1,0:T(8,128)(2,1)}, u32[]{:S(2)}, u32[]{:S(2)}) collective-permute-start(bf16[192,4096]{1,0:T(8,128)(2,1)} %get-tuple-element.57), channel_id=1, source_target_pairs={{0,4},{12,8},{1,5},{13,9},{2,6},{14,10},{3,7},{15,11},{16,20},{28,... | collective-permute-start | bytes 4718600 | tf_op jit(solution)/shard_map/ppermute | solution.py:485
  77.4 82.2 %collective-permute-start.13 = (bf16[4,128,2048]{2,1,0:T(8,128)(2,1)}, bf16[4,128,2048]{2,1,0:T(8,128)(2,1)}, u32[]{:S(2)}, u32[]{:S(2)}) collective-permute-start(bf16[4,128,2048]{2,1,0:T(8,128)(2,1)} %refs_0_.5), channel_id=1, source_target_pairs={{0,1},{1,0},{2,3},{3,2},{4,5},{5,4},{6,7},{7,6},{8,9},{9,8},{10,11... | collective-permute-start | bytes 6291464 | tf_op jit(solution)/shard_map/ppermute | solution.py:451
  77.4 1.6 copy-start.3
  79.0 1.6 copy-start.6
  108.5 51.1 %collective-permute-start.15 = (bf16[4,128,2048]{2,1,0:T(8,128)(2,1)}, bf16[4,128,2048]{2,1,0:T(8,128)(2,1)}, u32[]{:S(2)}, u32[]{:S(2)}) collective-permute-start(bf16[4,128,2048]{2,1,0:T(8,128)(2,1)} %collective-permute-done.14.refs_2_), channel_id=1, source_target_pairs={{0,1},{1,0},{2,3},{3,2},{4,5},{5,4},{6,7},{7,6},{8,9},{9,8},{10,11... | collective-permute-start | bytes 6291464 | tf_op jit(solution)/shard_map/ppermute | solution.py:451
  108.5 33.8 %collective-permute-start.11 = (bf16[512,1280]{1,0:T(8,128)(2,1)}, bf16[512,1280]{1,0:T(8,128)(2,1)}, u32[]{:S(2)}, u32[]{:S(2)}) collective-permute-start(bf16[512,1280]{1,0:T(8,128)(2,1)} %slice_select_fusion), channel_id=1, source_target_pairs={{8,12},{4,0},{9,13},{5,1},{10,14},{6,2},{11,15},{7,3},{24,28},{20,... | collective-permute-start | bytes 3932168 | tf_op jit(solution)/shard_map/ppermute | solution.py:501
  109.8 11.6 %collective-permute-start.9 = (f32[512,32]{1,0:T(8,128)S(1)}, f32[512,32]{1,0:T(8,128)S(1)}, u32[]{:S(2)}, u32[]{:S(2)}) collective-permute-start(f32[512,32]{1,0:T(8,128)S(1)} %get-tuple-element.58.low), channel_id=1, source_target_pairs={{0,4},{12,8},{1,5},{13,9},{2,6},{14,10},{3,7},{15,11},{16,20},{28,... | collective-permute-start | bytes 196616 | tf_op jit(solution)/shard_map/ppermute | solution.py:490
  121.4 1.6 copy-start.4
  131.0 2.0 %collective-permute-start.10 = (bf16[512,64]{1,0:T(8,128)(2,1)S(1)}, bf16[512,64]{1,0:T(8,128)(2,1)S(1)}, u32[]{:S(2)}, u32[]{:S(2)}) collective-permute-start(bf16[512,64]{1,0:T(8,128)(2,1)S(1)} %shard_map.102), channel_id=1, source_target_pairs={{4,8},{8,4},{5,9},{9,5},{6,10},{10,6},{7,11},{11,7},{20,24},{24,20... | collective-permute-start | bytes 196616 | tf_op jit(solution)/shard_map/ppermute | solution.py:508
  133.3 26.3 %collective-permute-start.12 = (bf16[512,640]{1,0:T(8,128)(2,1)S(1)}, bf16[512,640]{1,0:T(8,128)(2,1)S(1)}, u32[]{:S(2)}, u32[]{:S(2)}) collective-permute-start(bf16[512,640]{1,0:T(8,128)(2,1)S(1)} %pad_maximum_fusion.sent), channel_id=1, source_target_pairs={{8,12},{4,0},{9,13},{5,1},{10,14},{6,2},{11,15},{7,3},{24,28},{20,... | collective-permute-start | bytes 1966088 | tf_op jit(solution)/shard_map/ppermute | solution.py:511
  135.6 32.3 %collective-permute-start.16 = (bf16[512,256]{1,0:T(8,128)(2,1)S(1)}, bf16[512,256]{1,0:T(8,128)(2,1)S(1)}, u32[]{:S(2)}, u32[]{:S(2)}) collective-permute-start(bf16[512,256]{1,0:T(8,128)(2,1)S(1)} %slice_select_fusion.2), channel_id=1, source_target_pairs={{8,12},{4,0},{9,13},{5,1},{10,14},{6,2},{11,15},{7,3},{24,28},{20,... | collective-permute-start | bytes 786440 | tf_op jit(solution)/shard_map/ppermute | solution.py:513
  159.6 2.2 %copy-start.1 = (f32[512,2048]{1,0:T(8,128)S(1)}, f32[512,2048]{1,0:T(8,128)}, u32[]{:S(2)}) copy-start(f32[512,2048]{1,0:T(8,128)} %shard_map.103.base) | copy-start | bytes 12582916

commit v20 on v17

--- a/solution.py
+++ b/solution.py
@@ -212,8 +212,8 @@
             num_scalar_prefetch=2,
             grid=(half // step,),
             in_specs=[
-                pl.BlockSpec((rows, step), lambda s, *_: (0, s)),
-                pl.BlockSpec((step, columns), lambda s, source, valid: (source[0] * (columns // step) + s, 0)),
+                pl.BlockSpec((rows, step), lambda s, source, valid: (0, s * valid[0])),
+                pl.BlockSpec((step, columns), lambda s, source, valid: (source[0] * (columns // step) + s * valid[0], 0)),
                 whole,
             ],
             out_specs=whole,

time: 168 us -> 168 us (level)
  no operation moved by 1% of the time
where the time goes in v20:
time: 168 us; the launch traced here: 167 us
  Pallas kernels  60.7 us (36%)
  waiting for transfers between devices  54.3 us (32%)
  starting transfers between devices  29.7 us (18%)
  other arithmetic  11.7 us (7%)
  local copies, waits for them, and re-layouts  10.2 us (6%)
    ppermute x1, waiting for transfers between devices, local(): right_1 = lax.ppermute(attention_result, 'tensor', right)  33.4 us
    pallas_call x2, Pallas kernels, add_shards(): pl.pallas_call(functools.partial(shards_kernel, base is None), out_shape=...  31.1 us
    pallas_call x1, Pallas kernels, far_low(): pl.pallas_call(far_low_kernel, out_shape=jax.ShapeDtypeStruct((rows, 2 *...  8.06 us
    ppermute x1, starting transfers between devices, local(): other_down = lax.ppermute(other_down, 'tensor', [(0, 1), (3, 2)])  7.95 us
    pallas_call x1, Pallas kernels, add_half(): pl.pallas_call(half_kernel, out_shape=jax.ShapeDtypeStruct((rows, columns...  7.79 us
    unnamed x14, local copies, waits for them, and re-layouts  6.75 us
    pallas_call x1, Pallas kernels, prepare(): pl.pallas_call(prepare_kernel, out_shape=[pltpu.VMEM((rows, columns), F32...  6.11 us
    ppermute x1, waiting for transfers between devices, local(): left_2 = lax.ppermute(left_1, 'tensor', left[:-1])  6.06 us
  transfers between devices with their start and end apart: 17, of which 7 were waited for; matrix products, arithmetic and copies ran while one was open for 9% of the time, Pallas kernels for 35%

profile of v20, /device:TPU:0, one launch (start us, length us, event | category | flops | bytes accessed | tf_op | source)
XLA Modules:
  0.0 166.8 jit_solution(7606685597318761884)
XLA Ops:
  0.0 5.1 %collective-permute-start = (bf16[512,2048]{1,0:T(8,128)(2,1)}, bf16[512,2048]{1,0:T(8,128)(2,1)S(1)}, u32[]{:S(2)}, u32[]{:S(2)}) collective-permute-start(bf16[512,2048]{1,0:T(8,128)(2,1)} %refs_0_.4), channel_id=1, source_target_pairs={{0,4},{4,8},{8,12},{1,5},{5,9},{9,13},{2,6},{6,10},{10,14},{3,7},{... | collective-permute-start | bytes 6291464 | tf_op jit(solution)/shard_map/ppermute | solution.py:449
  5.1 1.3 collective-permute-start.1
  6.4 1.6 collective-permute-start.3
  7.9 0.5 collective-permute-start.14
  8.5 0.7 fusion
  9.1 0.6 slice.36
  9.8 0.7 add_bitcast_fusion
  10.5 0.7 fusion.4
  11.3 0.7 fusion.1
  12.0 0.6 fusion.6
  12.6 1.4 add_reduce_fusion
  14.1 0.9 select_reduce_fusion.1
  15.0 0.8 select_reduce_fusion
  15.8 0.7 fusion.3
  16.7 33.4 %collective-permute-done.refs_1_.left_1 = bf16[512,2048]{1,0:T(8,128)(2,1)S(1)} collective-permute-done((bf16[512,2048]{1,0:T(8,128)(2,1)}, bf16[512,2048]{1,0:T(8,128)(2,1)S(1)}, u32[]{:S(2)}, u32[]{:S(2)}) %collective-permute-start) | collective-permute-done | bytes 2097184 | tf_op jit(solution)/shard_map/ppermute | solution.py:449
  50.1 4.2 %collective-permute-done.1.refs_2_.right_1 = bf16[512,2048]{1,0:T(8,128)(2,1)} collective-permute-done((bf16[512,2048]{1,0:T(8,128)(2,1)}, bf16[512,2048]{1,0:T(8,128)(2,1)}, u32[]{:S(2)}, u32[]{:S(2)}) %collective-permute-start.1) | collective-permute-done | bytes 2097184 | tf_op jit(solution)/shard_map/ppermute | solution.py:450
  54.4 0.9 collective-permute-start.6
  55.3 1.3 collective-permute-start.7
  56.6 1.7 %fusion.5 = (bf16[2,32,8192]{2,1,0:T(8,128)(2,1)S(1)}, bf16[2,32,8192]{2,1,0:T(8,128)(2,1)S(1)}) fusion(bf16[4,32,8192]{2,1,0:T(8,128)(2,1)} %collective-permute-done.3.refs_2_), kind=kLoop, calls=%fused_computation.32 | loop fusion | bytes 4194304 | tf_op jit(solution)/shard_map/slice | solution.py:465
  58.4 0.5 collective-permute-start.5
  58.9 2.1 %collective-permute-done.4.refs_3_ = bf16[2,32,8192]{2,1,0:T(8,128)(2,1)S(1)} collective-permute-done((bf16[2,32,8192]{2,1,0:T(8,128)(2,1)S(1)}, bf16[2,32,8192]{2,1,0:T(8,128)(2,1)S(1)}, u32[]{:S(2)}, u32[]{:S(2)}) %collective-permute-start.4) | collective-permute-done | bytes 1048608 | tf_op jit(solution)/shard_map/ppermute | solution.py:434
  61.0 1.5 collective-permute-done.5.refs_4_
  62.5 4.6 %shard_map.100 = (bf16[8192,256]{1,0:T(8,128)(2,1)S(1)}, bf16[192,4096]{1,0:T(8,128)(2,1)}) custom-call(s32[6]{0:T(128)S(1)} %fusion.2.places, s32[1]{0:T(128)} %bitcast.8.upper, bf16[4,32,8192]{2,1,0:T(8,128)(2,1)S(1)} %copy-done.4, bf16[4,32,8192]{2,1,0:T(8,128)(2,1)} %collective-permute-done.2.refs_1_, ...), custom_call_target="tpu_custom_call" | custom-call | flops 1 | bytes 1 | tf_op jit(solution)/shard_map/pallas_call | solution.py:69
  67.1 2.0 %copy-done = bf16[8192,256]{1,0:T(8,128)(2,1)} copy-done((bf16[8192,256]{1,0:T(8,128)(2,1)}, bf16[8192,256]{1,0:T(8,128)(2,1)S(1)}, u32[]{:S(2)}) %copy-start) | copy-done | bytes 4194328
  69.1 8.0 %collective-permute-start.9 = (bf16[192,4096]{1,0:T(8,128)(2,1)}, bf16[192,4096]{1,0:T(8,128)(2,1)}, u32[]{:S(2)}, u32[]{:S(2)}) collective-permute-start(bf16[192,4096]{1,0:T(8,128)(2,1)} %get-tuple-element.57), channel_id=1, source_target_pairs={{0,4},{12,8},{1,5},{13,9},{2,6},{14,10},{3,7},{15,11},{16,20},{28,... | collective-permute-start | bytes 4718600 | tf_op jit(solution)/shard_map/ppermute | solution.py:468
  77.0 0.1 copy.21.refs_5_.slot.refs_4_
  77.3 1.6 copy-done.2
  78.9 1.6 copy-done.5
  80.5 19.4 %shard_map.101 = (f32[512,2048]{1,0:T(8,128)}, f32[512,32]{1,0:T(8,128)S(1)}) custom-call(s32[6]{0:T(128)S(1)} %select_n.90.start, s32[3]{0:T(128)S(1)} %get-tuple-element.45.valid, bf16[512,2048]{1,0:T(8,128)(2,1)S(1)} %copy-done.5, bf16[512,2048]{1,0:T(8,128)(2,1)S(1)} %copy-done.2, bf16[512,2048]{1,0:T(8,128)(2,1)} %collective-permute-done.1.refs_2_.right_1, ...), custom_call_target="tpu_custom_call" | custom-call | flops 1 | bytes 1 | tf_op jit(solution)/shard_map/pallas_call | solution.py:174
  99.9 6.1 %collective-permute-done.7.right_2.refs_1_ = bf16[512,2048]{1,0:T(8,128)(2,1)} collective-permute-done((bf16[512,2048]{1,0:T(8,128)(2,1)}, bf16[512,2048]{1,0:T(8,128)(2,1)}, u32[]{:S(2)}, u32[]{:S(2)}) %collective-permute-start.7) | collective-permute-done | bytes 2097184 | tf_op jit(solution)/shard_map/ppermute | solution.py:462
  105.9 2.6 %slice_select_fusion = bf16[512,1280]{1,0:T(8,128)(2,1)} fusion(bf16[512,2048]{1,0:T(8,128)(2,1)} %collective-permute-done.7.right_2.refs_1_, bf16[512,2048]{1,0:T(8,128)(2,1)S(1)} %collective-permute-done.6.left_2.refs_0_, pred[]{:T(512)S(6)} %ge.9), kind=kLoop, calls=%fused_computation | loop fusion | flops 655360 | bytes 3932161 | tf_op jit(solution)/shard_map/jit(_where)/select_n | solution.py:481
  108.5 1.3 collective-permute-start.8
  109.8 5.7 %collective-permute-start.10 = (f32[512,32]{1,0:T(8,128)S(1)}, f32[512,32]{1,0:T(8,128)S(1)}, u32[]{:S(2)}, u32[]{:S(2)}) collective-permute-start(f32[512,32]{1,0:T(8,128)S(1)} %get-tuple-element.58.low), channel_id=1, source_target_pairs={{0,4},{12,8},{1,5},{13,9},{2,6},{14,10},{3,7},{15,11},{16,20},{28,... | collective-permute-start | bytes 196616 | tf_op jit(solution)/shard_map/ppermute | solution.py:473
  115.5 0.1 copy.23.row_rank
  115.6 5.8 %collective-permute-done.10.other_low = f32[512,32]{1,0:T(8,128)S(1)} collective-permute-done((f32[512,32]{1,0:T(8,128)S(1)}, f32[512,32]{1,0:T(8,128)S(1)}, u32[]{:S(2)}, u32[]{:S(2)}) %collective-permute-start.10) | collective-permute-done | bytes 65568 | tf_op jit(solution)/shard_map/ppermute | solution.py:473
  121.4 1.6 copy-done.3
  123.0 8.1 %shard_map.102 = bf16[512,64]{1,0:T(8,128)(2,1)S(1)} custom-call(s32[4]{0:T(128)S(1)} %pad_add_fusion.1.facts, bf16[512,2048]{1,0:T(8,128)(2,1)S(1)} %copy-done.3, bf16[512,2048]{1,0:T(8,128)(2,1)S(1)} %collective-permute-done.6.left_2.refs_0_, bf16[512,2048]{1,0:T(8,128)(2,1)} %collective-permute-done.1.refs_2_.right_1, ...), custom_call_target="tpu_custom_call" | custom-call | flops 1 | bytes 1 | tf_op jit(solution)/shard_map/pallas_call | solution.py:275
  131.1 0.9 collective-permute-start.11
  132.0 1.1 slice_select_fusion.1
  133.1 0.1 maximum_select_fusion
  133.3 1.3 collective-permute-start.12
  134.6 1.0 slice_select_fusion.2
  135.6 1.3 collective-permute-start.16
  136.9 11.7 %shard_map.103.base_in = f32[512,2048]{1,0:T(8,128)} custom-call(s32[4]{0:T(128)S(1)} %select_n.92.start, s32[2]{0:T(128)S(1)} %get-tuple-element.56.valid, bf16[512,2048]{1,0:T(8,128)(2,1)S(1)} %collective-permute-done.6.left_2.refs_0_, bf16[512,2048]{1,0:T(8,128)(2,1)} %collective-permute-done.7.right_2.refs_1_, bf16[8192,2048]{1,0:T(8,128)(2,1)} %weight.3, ...), custom_call_target="tpu_custom_call" | custom-call | flops 1 | bytes 1 | tf_op jit(solution)/shard_map/pallas_call | solution.py:174
  148.6 7.8 %shard_map.104.base = f32[512,2048]{1,0:T(8,128)S(1)} custom-call(s32[1]{0:T(128)} %bitcast.4.start, s32[1]{0:T(128)} %bitcast.3.valid, bf16[512,1280]{1,0:T(8,128)(2,1)} %collective-permute-done.8.x, bf16[8192,2048]{1,0:T(8,128)(2,1)} %weight.3, f32[512,2048]{1,0:T(8,128)} %shard_map.103.base_in), custom_call_target="tpu_custom_call" | custom-call | flops 1 | bytes 1 | tf_op jit(solution)/shard_map/pallas_call | solution.py:208
  156.4 1.1 collective-permute-done.12.received
  157.5 6.1 %shard_map.105 = (f32[512,2048]{1,0:T(8,128)S(1)}, bf16[256,2048]{1,0:T(8,128)(2,1)S(1)}) custom-call(s32[2]{0:T(128)S(1)} %pad_add_fusion.facts, s32[6]{0:T(128)S(1)} %fusion.2.places, f32[512,2048]{1,0:T(8,128)S(1)} %shard_map.104.base, bf16[512,640]{1,0:T(8,128)(2,1)S(1)} %pad_maximum_fusion.sent, bf16[512,640]{1,0:T(8,128)(2,1)S(1)} %collective-permute-done.12.received, ...), custom_call_target="tpu_custom_call" | custom-call | flops 1 | bytes 1 | tf_op jit(solution)/shard_map/pallas_call | solution.py:352
  163.7 3.1 %shard_map.106 = bf16[512,2048]{1,0:T(8,128)(2,1)} custom-call(s32[2]{0:T(128)S(1)} %pad_add_fusion.facts, f32[512,2048]{1,0:T(8,128)S(1)} %get-tuple-element.72.total, bf16[256,2048]{1,0:T(8,128)(2,1)S(1)} %get-tuple-element.73.weight, bf16[512,256]{1,0:T(8,128)(2,1)S(1)} %collective-permute-done.16.x), custom_call_target="tpu_custom_call" | custom-call | flops 1 | bytes 1 | tf_op jit(solution)/shard_map/pallas_call | solution.py:385
  (36 shorter events, 0.9 us)
Async XLA Ops:
  0.0 50.1 %collective-permute-start = (bf16[512,2048]{1,0:T(8,128)(2,1)}, bf16[512,2048]{1,0:T(8,128)(2,1)S(1)}, u32[]{:S(2)}, u32[]{:S(2)}) collective-permute-start(bf16[512,2048]{1,0:T(8,128)(2,1)} %refs_0_.4), channel_id=1, source_target_pairs={{0,4},{4,8},{8,12},{1,5},{5,9},{9,13},{2,6},{6,10},{10,14},{3,7},{... | collective-permute-start | bytes 6291464 | tf_op jit(solution)/shard_map/ppermute | solution.py:449
  5.1 49.3 %collective-permute-start.1 = (bf16[512,2048]{1,0:T(8,128)(2,1)}, bf16[512,2048]{1,0:T(8,128)(2,1)}, u32[]{:S(2)}, u32[]{:S(2)}) collective-permute-start(bf16[512,2048]{1,0:T(8,128)(2,1)} %refs_0_.4), channel_id=1, source_target_pairs={{4,0},{8,4},{12,8},{5,1},{9,5},{13,9},{6,2},{10,6},{14,10},{7,3},{... | collective-permute-start | bytes 6291464 | tf_op jit(solution)/shard_map/ppermute | solution.py:450
  6.4 50.2 %collective-permute-start.3 = (bf16[4,32,8192]{2,1,0:T(8,128)(2,1)}, bf16[4,32,8192]{2,1,0:T(8,128)(2,1)}, u32[]{:S(2)}, u32[]{:S(2)}) collective-permute-start(bf16[4,32,8192]{2,1,0:T(8,128)(2,1)} %refs_0_.3), channel_id=1, source_target_pairs={{0,2},{1,3},{2,0},{3,1},{4,6},{5,7},{6,4},{7,5},{8,10},{9,11},{10,... | collective-permute-start | bytes 6291464 | tf_op jit(solution)/shard_map/ppermute | solution.py:434
  7.9 50.4 %collective-permute-start.2 = (bf16[4,32,8192]{2,1,0:T(8,128)(2,1)}, bf16[4,32,8192]{2,1,0:T(8,128)(2,1)}, u32[]{:S(2)}, u32[]{:S(2)}) collective-permute-start(bf16[4,32,8192]{2,1,0:T(8,128)(2,1)} %refs_0_.3), channel_id=1, source_target_pairs={{0,1},{1,0},{2,3},{3,2},{4,5},{5,4},{6,7},{7,6},{8,9},{9,8},{10,11... | collective-permute-start | bytes 6291464 | tf_op jit(solution)/shard_map/ppermute | solution.py:434
  7.9 100.6 %collective-permute-start.14 = (bf16[4,128,2048]{2,1,0:T(8,128)(2,1)}, bf16[4,128,2048]{2,1,0:T(8,128)(2,1)}, u32[]{:S(2)}, u32[]{:S(2)}) collective-permute-start(bf16[4,128,2048]{2,1,0:T(8,128)(2,1)} %refs_0_.5), channel_id=1, source_target_pairs={{0,2},{1,3},{2,0},{3,1},{4,6},{5,7},{6,4},{7,5},{8,10},{9,11},{10,... | collective-permute-start | bytes 6291464 | tf_op jit(solution)/shard_map/ppermute | solution.py:434
  50.1 4.3 %copy-start.1 = (bf16[512,2048]{1,0:T(8,128)(2,1)}, bf16[512,2048]{1,0:T(8,128)(2,1)S(1)}, u32[]{:S(2)}) copy-start(bf16[512,2048]{1,0:T(8,128)(2,1)S(1)} %collective-permute-done.refs_1_.left_1) | copy-start | bytes 6291460
  54.4 8.1 %copy-start.4 = (bf16[4,32,8192]{2,1,0:T(8,128)(2,1)S(1)}, bf16[4,32,8192]{2,1,0:T(8,128)(2,1)}, u32[]{:S(2)}) copy-start(bf16[4,32,8192]{2,1,0:T(8,128)(2,1)} %refs_0_.3) | copy-start | bytes 6291460
  54.4 45.5 %collective-permute-start.6 = (bf16[512,2048]{1,0:T(8,128)(2,1)}, bf16[512,2048]{1,0:T(8,128)(2,1)S(1)}, u32[]{:S(2)}, u32[]{:S(2)}) collective-permute-start(bf16[512,2048]{1,0:T(8,128)(2,1)} %copy-done.1), channel_id=1, source_target_pairs={{4,8},{8,12},{5,9},{9,13},{6,10},{10,14},{7,11},{11,15},{20,24},{2... | collective-permute-start | bytes 6291464 | tf_op jit(solution)/shard_map/ppermute | solution.py:461
  55.3 50.6 %collective-permute-start.7 = (bf16[512,2048]{1,0:T(8,128)(2,1)}, bf16[512,2048]{1,0:T(8,128)(2,1)}, u32[]{:S(2)}, u32[]{:S(2)}) collective-permute-start(bf16[512,2048]{1,0:T(8,128)(2,1)} %collective-permute-done.1.refs_2_.right_1), channel_id=1, source_target_pairs={{4,0},{8,4},{5,1},{9,5},{6,2},{10,6},{7,3},{11,7},{20,16},{24,20},... | collective-permute-start | bytes 6291464 | tf_op jit(solution)/shard_map/ppermute | solution.py:462
  58.3 2.7 %collective-permute-start.4 = (bf16[2,32,8192]{2,1,0:T(8,128)(2,1)S(1)}, bf16[2,32,8192]{2,1,0:T(8,128)(2,1)S(1)}, u32[]{:S(2)}, u32[]{:S(2)}) collective-permute-start(bf16[2,32,8192]{2,1,0:T(8,128)(2,1)S(1)} %get-tuple-element.82), channel_id=1, source_target_pairs={{0,1},{1,0},{2,3},{3,2},{4,5},{5,4},{6,7},{7,6},{8,9},{9,8},{10,11... | collective-permute-start | bytes 3145736 | tf_op jit(solution)/shard_map/ppermute | solution.py:434
  58.4 18.7 %copy-start.6 = (s32[512]{0:T(512)S(1)}, s32[512]{0:T(512)}, u32[]{:S(2)}) copy-start(s32[512]{0:T(512)} %param.16) | copy-start | bytes 6148
  58.4 4.1 %collective-permute-start.5 = (bf16[2,32,8192]{2,1,0:T(8,128)(2,1)S(1)}, bf16[2,32,8192]{2,1,0:T(8,128)(2,1)S(1)}, u32[]{:S(2)}, u32[]{:S(2)}) collective-permute-start(bf16[2,32,8192]{2,1,0:T(8,128)(2,1)S(1)} %get-tuple-element.81), channel_id=1, source_target_pairs={{0,1},{1,0},{2,3},{3,2},{4,5},{5,4},{6,7},{7,6},{8,9},{9,8},{10,11... | collective-permute-start | bytes 3145736 | tf_op jit(solution)/shard_map/ppermute | solution.py:434
  67.1 2.0 %copy-start = (bf16[8192,256]{1,0:T(8,128)(2,1)}, bf16[8192,256]{1,0:T(8,128)(2,1)S(1)}, u32[]{:S(2)}) copy-start(bf16[8192,256]{1,0:T(8,128)(2,1)S(1)} %get-tuple-element.50.refs_4_.down) | copy-start | bytes 12582916
  69.1 52.3 %collective-permute-start.9 = (bf16[192,4096]{1,0:T(8,128)(2,1)}, bf16[192,4096]{1,0:T(8,128)(2,1)}, u32[]{:S(2)}, u32[]{:S(2)}) collective-permute-start(bf16[192,4096]{1,0:T(8,128)(2,1)} %get-tuple-element.57), channel_id=1, source_target_pairs={{0,4},{12,8},{1,5},{13,9},{2,6},{14,10},{3,7},{15,11},{16,20},{28,... | collective-permute-start | bytes 4718600 | tf_op jit(solution)/shard_map/ppermute | solution.py:468
  77.2 79.2 %collective-permute-start.13 = (bf16[4,128,2048]{2,1,0:T(8,128)(2,1)}, bf16[4,128,2048]{2,1,0:T(8,128)(2,1)}, u32[]{:S(2)}, u32[]{:S(2)}) collective-permute-start(bf16[4,128,2048]{2,1,0:T(8,128)(2,1)} %refs_0_.5), channel_id=1, source_target_pairs={{0,1},{1,0},{2,3},{3,2},{4,5},{5,4},{6,7},{7,6},{8,9},{9,8},{10,11... | collective-permute-start | bytes 6291464 | tf_op jit(solution)/shard_map/ppermute | solution.py:434
  77.3 1.6 copy-start.2
  78.9 1.6 copy-start.5
  108.5 49.0 %collective-permute-start.15 = (bf16[4,128,2048]{2,1,0:T(8,128)(2,1)}, bf16[4,128,2048]{2,1,0:T(8,128)(2,1)}, u32[]{:S(2)}, u32[]{:S(2)}) collective-permute-start(bf16[4,128,2048]{2,1,0:T(8,128)(2,1)} %collective-permute-done.14.refs_2_), channel_id=1, source_target_pairs={{0,1},{1,0},{2,3},{3,2},{4,5},{5,4},{6,7},{7,6},{8,9},{9,8},{10,11... | collective-permute-start | bytes 6291464 | tf_op jit(solution)/shard_map/ppermute | solution.py:434
  108.5 40.1 %collective-permute-start.8 = (bf16[512,1280]{1,0:T(8,128)(2,1)}, bf16[512,1280]{1,0:T(8,128)(2,1)}, u32[]{:S(2)}, u32[]{:S(2)}) collective-permute-start(bf16[512,1280]{1,0:T(8,128)(2,1)} %slice_select_fusion), channel_id=1, source_target_pairs={{8,12},{4,0},{9,13},{5,1},{10,14},{6,2},{11,15},{7,3},{24,28},{20,... | collective-permute-start | bytes 3932168 | tf_op jit(solution)/shard_map/ppermute | solution.py:484
  109.8 11.6 %collective-permute-start.10 = (f32[512,32]{1,0:T(8,128)S(1)}, f32[512,32]{1,0:T(8,128)S(1)}, u32[]{:S(2)}, u32[]{:S(2)}) collective-permute-start(f32[512,32]{1,0:T(8,128)S(1)} %get-tuple-element.58.low), channel_id=1, source_target_pairs={{0,4},{12,8},{1,5},{13,9},{2,6},{14,10},{3,7},{15,11},{16,20},{28,... | collective-permute-start | bytes 196616 | tf_op jit(solution)/shard_map/ppermute | solution.py:473
  121.4 1.6 copy-start.3
  131.1 2.0 %collective-permute-start.11 = (bf16[512,64]{1,0:T(8,128)(2,1)S(1)}, bf16[512,64]{1,0:T(8,128)(2,1)S(1)}, u32[]{:S(2)}, u32[]{:S(2)}) collective-permute-start(bf16[512,64]{1,0:T(8,128)(2,1)S(1)} %shard_map.102), channel_id=1, source_target_pairs={{4,8},{8,4},{5,9},{9,5},{6,10},{10,6},{7,11},{11,7},{20,24},{24,20... | collective-permute-start | bytes 196616 | tf_op jit(solution)/shard_map/ppermute | solution.py:491
  133.3 24.2 %collective-permute-start.12 = (bf16[512,640]{1,0:T(8,128)(2,1)S(1)}, bf16[512,640]{1,0:T(8,128)(2,1)S(1)}, u32[]{:S(2)}, u32[]{:S(2)}) collective-permute-start(bf16[512,640]{1,0:T(8,128)(2,1)S(1)} %pad_maximum_fusion.sent), channel_id=1, source_target_pairs={{8,12},{4,0},{9,13},{5,1},{10,14},{6,2},{11,15},{7,3},{24,28},{20,... | collective-permute-start | bytes 1966088 | tf_op jit(solution)/shard_map/ppermute | solution.py:495
  135.6 28.0 %collective-permute-start.16 = (bf16[512,256]{1,0:T(8,128)(2,1)S(1)}, bf16[512,256]{1,0:T(8,128)(2,1)S(1)}, u32[]{:S(2)}, u32[]{:S(2)}) collective-permute-start(bf16[512,256]{1,0:T(8,128)(2,1)S(1)} %slice_select_fusion.2), channel_id=1, source_target_pairs={{8,12},{4,0},{9,13},{5,1},{10,14},{6,2},{11,15},{7,3},{24,28},{20,... | collective-permute-start | bytes 786440 | tf_op jit(solution)/shard_map/ppermute | solution.py:497
